TPU v7x, 32 devices: a whole 2x2x4 slice. The times are simulated.
32 devices in a mesh: ctx: 16 (over z, y, x), tp: 2 (over core).
Axes of the slice: x: 2, y: 2, z: 4, core: 2. Of those that a mesh axis runs over, the one named last changes fastest.
Arguments:
- tokens: bfloat16 [2048, 2048], P('ctx'), may hold values from -6 to 6
- w_proj: bfloat16 [2048, 4, 2048], P('ctx', None, 'tp'), may hold values from -3 to 3
- w_out: bfloat16 [2048, 2048], P('tp', 'ctx'), may hold values from -0.125 to 0.125
- positions: int32 [2048], P('ctx'), may hold values from 0 to 2047, as said below
- neg_emb: bfloat16 [1024, 2048], P('ctx', 'tp'), may hold values from -7 to 7
- neg_ids: int32 [1024], replicated, may hold values from 0 to 65535, as said below
- target_emb: bfloat16 [2048, 2048], P('ctx', 'tp'), may hold values from -6 to 6
- target_ids: int32 [2048], P(('ctx', 'tp')), may hold values from 0 to 65535, as said below
Outputs:
- hidden: bfloat16 [2048, 2048], P('ctx', 'tp')
- loss: float32 [2048], P(('ctx', 'tp'))
Inputs may be any that keep to these rules, and one draw needn't show every extreme that they name: positions never fall and rise by at most two from one event to the next; at the first event of every aligned block of 128 events and at the last event the position equals the event's index. `neg_ids`: item ids; some items are far more common than others. `target_ids`: item ids, drawn by the same popularity as the negatives.
All inputs are finite; a program needn't handle non-finite values.
Results may differ from a plain program's by a relative error of at most 0.0045.
Values may be sent and summed in bfloat16 or wider, within the bound.
No kernel may reach another device: no remote copies, remote signals or barrier semaphores. Data moves between devices by JAX's collectives and lax.ppermute only.
A program may use at most 64 MiB of HBM per device.

v0:
```python
import jax
import jax.numpy as jnp
from jax import lax
from jax.sharding import PartitionSpec as P

HEAD_DIM = 128


def attend_piece(q_group, q_pos, k_piece, v_piece, p_piece):
    heads = q_group.shape[1]
    width = q_group.shape[2]
    key_heads = k_piece.reshape(k_piece.shape[0], heads, width)
    value_heads = v_piece.reshape(v_piece.shape[0], heads, width)
    scores = jnp.einsum(
        "thd,khd->htk", q_group, key_heads, preferred_element_type=jnp.float32
    ) * width ** (-0.5)
    visible = p_piece[None, None, :] <= q_pos[None, :, None]
    weight = jnp.where(visible, jax.nn.silu(scores), 0.0).astype(jnp.bfloat16)
    return jnp.einsum("htk,khd->thd", weight, value_heads, preferred_element_type=jnp.float32)


def attend_groups(groups, key_flat, value_flat, own_pos):
    initial = tuple((jnp.zeros(group.shape, jnp.float32) for group, _ in groups))
    k_piece = lax.all_gather(key_flat, "ctx", axis=0, tiled=True)
    v_piece = lax.all_gather(value_flat, "ctx", axis=0, tiled=True)
    p_piece = lax.all_gather(own_pos, "ctx", axis=0, tiled=True)
    updated = []
    for (q_group, q_pos), total in zip(groups, initial):

        def skipped(carry):
            return carry

        def computed(carry):
            return attend_piece(q_group, q_pos, k_piece, v_piece, p_piece)

        updated.append(lax.cond(jnp.min(p_piece) > jnp.max(q_pos), skipped, computed, total))
    return tuple(updated)


def shards(tokens, w_proj, w_out, positions, neg_emb, neg_ids, target_emb, target_ids):
    tok_rows = tokens.shape[0]
    head_cols = w_proj.shape[2]
    local_heads = head_cols // HEAD_DIM
    proj_sum = jnp.einsum(
        "td,dfh->tfh",
        tokens,
        lax.all_gather(w_proj, "ctx", axis=0, tiled=True),
        preferred_element_type=jnp.float32,
    )
    proj = jax.nn.silu(proj_sum).astype(jnp.bfloat16)
    gate = proj[:, 0].reshape(tok_rows, local_heads, HEAD_DIM)
    value_flat = proj[:, 1]
    query = proj[:, 2].reshape(tok_rows, local_heads, HEAD_DIM)
    key_flat = proj[:, 3]
    (attn,) = attend_groups([(query, positions)], key_flat, value_flat, positions)
    normed = attn * lax.rsqrt(jnp.mean(attn * attn, axis=-1, keepdims=True) + 1e-06)
    gated = (normed * gate.astype(jnp.float32)).astype(jnp.bfloat16).reshape(tok_rows, head_cols)
    out_terms = jnp.dot(
        gated, lax.all_gather(w_out, "ctx", axis=1, tiled=True), preferred_element_type=jnp.float32
    )
    out_share = lax.psum_scatter(out_terms, "tp", scatter_dimension=1, tiled=True)
    feat_cols = out_share.shape[1]
    own_tokens = lax.dynamic_slice_in_dim(tokens, lax.axis_index("tp") * feat_cols, feat_cols, 1)
    hidden = (own_tokens.astype(jnp.float32) + out_share).astype(jnp.bfloat16)
    piece = lax.all_gather(neg_emb, "ctx", axis=0, tiled=True)
    panel_dots = lax.dot_general(
        hidden, piece, (((1,), (1,)), ((), ())), preferred_element_type=jnp.float32
    )
    panel_norms = jnp.sum(jnp.square(piece.astype(jnp.float32)), axis=1)
    hidden_f = hidden.astype(jnp.float32)
    target_f = target_emb.astype(jnp.float32)
    part_hh = jnp.sum(hidden_f * hidden_f, axis=1)
    part_he = jnp.sum(hidden_f * target_f, axis=1)
    part_ee = jnp.sum(target_f * target_f, axis=1)
    dots, hh_sum, he_sum, ee_sum = (
        lax.psum_scatter(panel_dots, "tp", scatter_dimension=0, tiled=True),
        lax.psum_scatter(part_hh, "tp", scatter_dimension=0, tiled=True),
        lax.psum_scatter(part_he, "tp", scatter_dimension=0, tiled=True),
        lax.psum_scatter(part_ee, "tp", scatter_dimension=0, tiled=True),
    )
    neg_sq = lax.psum(panel_norms, "tp")
    pos_logit = he_sum / jnp.sqrt(hh_sum + 1e-06) / jnp.sqrt(ee_sum + 1e-06) / 0.05
    neg_logit = dots / jnp.sqrt(hh_sum + 1e-06)[:, None] / jnp.sqrt(neg_sq + 1e-06)[None, :] / 0.05
    keep_mask = neg_ids[None, :] != target_ids[:, None]
    total_mass = jnp.exp(pos_logit) + jnp.sum(jnp.where(keep_mask, jnp.exp(neg_logit), 0.0), axis=1)
    loss = jnp.log(total_mass) - pos_logit
    return (hidden, loss)


def solution(mesh):
    placed = (
        P("ctx", None),
        P("ctx", None, "tp"),
        P("tp", "ctx"),
        P("ctx"),
        P("ctx", "tp"),
        P(),
        P("ctx", "tp"),
        P(("ctx", "tp")),
    )
    return jax.shard_map(
        shards,
        mesh=mesh,
        in_specs=placed,
        out_specs=(P("ctx", "tp"), P(("ctx", "tp"))),
        check_vma=False,
    )
```

profile of v0, /device:TPU:0, one launch (start us, length us, event | category | flops | bytes accessed | tf_op | source)
XLA Modules:
  0.0 551.7 jit_solution(14570283065698447033)
XLA Ops:
  7.2 2.5 copy.25
  9.8 195.1 %all-gather.9.cloned.1.call-done = bf16[2048,4,1024]{2,0,1:T(8,128)(2,1)} async-done(((bf16[128,4,1024]{2,0,1:T(8,128)(2,1)}), bf16[2048,4,1024]{2,0,1:T(8,128)(2,1)}) %all-gather.9.cloned.1.call-update) | async-done | bytes 16777232 | tf_op jit(solution)/shard_map/all_gather | solution.py:47
  204.9 8.4 %multiply_convert_fusion = bf16[128,4,1024]{2,0,1:T(8,128)(2,1)S(1)} fusion(bf16[2048,4,1024]{2,0,1:T(8,128)(2,1)} %all-gather.9.cloned.1.call-done, bf16[128,2048]{1,0:T(8,128)(2,1)} %param.10), kind=kOutput, calls=%fused_computation.11 | convolution fusion | flops 2150105088 | bytes 18350080 | tf_op jit(solution)/shard_map/td,dfh->tfh/dot_general | solution.py:44
  213.3 0.9 fusion.20
  214.3 0.7 all-gather.17.cloned.1.call-update
  215.6 0.7 reduce_max.9
  216.3 37.6 %all-gather.2 = s32[16,1,128]{2,1,0:T(1,128)S(1)} all-gather(s32[1,1,128]{2,1,0:T(1,128)S(1)} %bitcast.45), channel_id=1, replica_groups=mesh['ctx'=16,'tp'=2] {'ctx'}, dimensions={0}, use_global_device_ids=true | all-gather | bytes 8704 | tf_op jit(solution)/shard_map/all_gather | solution.py:26
  253.9 0.6 reduce_min.9
  256.1 32.6 %all-gather.15.cloned.1.call-done = bf16[2048,1,1024]{2,0,1:T(8,128)(2,1)} async-done(((bf16[128,1,1024]{2,0,1:T(8,128)(2,1)}), bf16[2048,1,1024]{2,0,1:T(8,128)(2,1)}) %all-gather.15.cloned.1.call-update) | async-done | bytes 4194320 | tf_op jit(solution)/shard_map/all_gather | solution.py:24
  288.7 78.1 %all-gather.17.cloned.1.call-done = bf16[2048,1,1024]{2,0,1:T(8,128)(2,1)} async-done(((bf16[128,1,1024]{2,0,1:T(8,128)(2,1)}), bf16[2048,1,1024]{2,0,1:T(8,128)(2,1)}) %all-gather.17.cloned.1.call-update) | async-done | bytes 4194320 | tf_op jit(solution)/shard_map/all_gather | solution.py:25
  366.8 13.8 %conditional.1 = (f32[128,8,128]{0,2,1:T(8,128)S(1)}, f32[128,8,1]{0,1,2:T(8,128)S(1)}) conditional(s32[]{:T(128)} %convert_element_type.34, (s32[2048]{0:T(1024)S(1)}, s32[128]{0:T(128)S(1)}, bf16[128,4,1024]{2,0,1:T(8,128)(2,1)S(1)}, bf16[2048,1024]{1,0:T(8,128)(2,1)}, bf16[2048,1024]{1,0:T(8,128)(2,1)}) %tuple.49, () %tuple.19), branch_computations={%region_2.4_spmd, %region_4.5_spmd} | conditional | flops 1088945152 | bytes 20722192 | solution.py:36
  366.8 6.5 %copy.27 = bf16[2048,1024]{0,1:T(8,128)(2,1)} copy(bf16[2048,1024]{1,0:T(8,128)(2,1)} %get-tuple-element.39) | data formatting | bytes 8388608 | tf_op jit(solution)/shard_map
  373.3 0.7 copy.26
  374.2 6.4 %multiply_reduce_fusion = (f32[128,8]{0,1:T(8,128)S(1)}, f32[128,8,128]{0,2,1:T(8,128)S(1)}) fusion(bf16[2048,8,128]{0,2,1:T(8,128)(2,1)} %bitcast.39, bf16[128,8,128]{0,2,1:T(8,128)(2,1)S(1)} %bitcast.42, pred[128,2048]{1,0:T(8,128)(4,1)S(1)} %broadcast_compare_fusion, bf16[2048,1024]{1,0:T(8,128)(2,1)} %get-tuple-element.17), kind=kOutput, calls=%fused_computation.5 | convolution fusion | flops 1088683008 | bytes 9441280 | tf_op jit(solution)/shard_map/cond/branch_0_fun/htk,khd->thd/dot_general | solution.py:19
  380.7 76.5 %all-gather.11.cloned.1.call-done = bf16[1024,2048]{1,0:T(8,128)(2,1)} async-done(((bf16[1024,128]{1,0:T(8,128)(2,1)}), bf16[1024,2048]{1,0:T(8,128)(2,1)}) %all-gather.11.cloned.1.call-update) | async-done | bytes 4194320 | tf_op jit(solution)/shard_map/all_gather | solution.py:59
  457.2 3.9 fusion.21
  461.7 6.3 %reduce-scatter.3.cloned.1.call-done = f32[128,1024]{1,0:T(8,128)} async-done(((f32[128,2048]{1,0:T(8,128)}), f32[128,1024]{1,0:T(8,128)}) %reduce-scatter.3.cloned.1.call-update) | async-done | bytes 524304 | tf_op jit(solution)/shard_map/reduce_scatter | solution.py:61
  468.0 1.3 fusion.12
  469.3 63.6 %all-gather.13.cloned.1.call-done = bf16[1024,1024]{1,0:T(8,128)(2,1)} async-done(((bf16[64,1024]{1,0:T(8,128)(2,1)}), bf16[1024,1024]{1,0:T(8,128)(2,1)}) %all-gather.13.cloned.1.call-update) | async-done | bytes 2097168 | tf_op jit(solution)/shard_map/all_gather | solution.py:65
  532.9 3.4 fusion.22
  538.0 2.5 all-reduce.3
  540.6 2.4 reduce-scatter.5.cloned.1.call-done
  543.0 1.2 select_reduce_fusion
  544.2 0.6 log_subtract_fusion
  (38 shorter events, 3.1 us)
Async XLA Ops:
  7.2 197.8 %all-gather.9.cloned.1.call-start = ((), (), s32[]{:S(2)}) async-start(), calls=%async_computation.2 | async-start | bytes 17825792 | tf_op jit(solution)/shard_map/all_gather | solution.py:47
  9.8 205.9 %copy-start.5 = (s32[128]{0:T(128)S(1)}, s32[128]{0:T(128)}, u32[]{:S(2)}) copy-start(s32[128]{0:T(128)} %param.13) | copy-start | bytes 1540
  9.8 279.0 %all-gather.15.cloned.1.call-start = ((), (), s32[]{:S(2)}) async-start(), calls=%async_computation.7 | async-start | bytes 4456448 | tf_op jit(solution)/shard_map/all_gather | solution.py:24
  214.3 152.5 %all-gather.17.cloned.1.call-start = ((), (), s32[]{:S(2)}) async-start(), calls=%async_computation.8 | async-start | bytes 4456448 | tf_op jit(solution)/shard_map/all_gather | solution.py:25
  215.0 242.2 %all-gather.11.cloned.1.call-start = ((), (), s32[]{:S(2)}) async-start(), calls=%async_computation.3 | async-start | bytes 4456448 | tf_op jit(solution)/shard_map/all_gather | solution.py:59
  215.6 252.4 %reduce-scatter.3.cloned.1.call-start = ((), (), s32[]{:S(2)}) async-start(), calls=%async_computation.4 | async-start | bytes 1572864 | tf_op jit(solution)/shard_map/reduce_scatter | solution.py:61
  380.6 87.5 %copy-start.2 = (bf16[128,1024]{1,0:T(8,128)(2,1)S(1)}, bf16[128,1024]{1,0:T(8,128)(2,1)}, u32[]{:S(2)}) copy-start(bf16[128,1024]{1,0:T(8,128)(2,1)} %param.16) | copy-start | bytes 786436
  380.6 87.5 %copy-start.3 = (bf16[128,2048]{1,0:T(8,128)(2,1)S(1)}, bf16[128,2048]{1,0:T(8,128)(2,1)}, u32[]{:S(2)}) copy-start(bf16[128,2048]{1,0:T(8,128)(2,1)} %param.10) | copy-start | bytes 1572868
  461.1 75.2 %copy-start.7 = (u32[32]{0:T(128)S(1)}, u32[32]{0:T(128)}, u32[]{:S(2)}) copy-start(u32[32]{0:T(128)} %constant.45) | copy-start | bytes 388
  461.1 82.0 %copy-start.4 = (s32[1024]{0:T(1024)S(1)}, s32[1024]{0:T(1024)}, u32[]{:S(2)}) copy-start(s32[1024]{0:T(1024)} %param.15) | copy-start | bytes 12292
  461.1 82.0 %copy-start.6 = (s32[64]{0:T(128)S(1)}, s32[64]{0:T(128)}, u32[]{:S(2)}) copy-start(s32[64]{0:T(128)} %param.17) | copy-start | bytes 772
  461.1 71.8 %all-gather.13.cloned.1.call-start = ((), (), s32[]{:S(2)}) async-start(), calls=%async_computation.5 | async-start | bytes 2228224 | tf_op jit(solution)/shard_map/all_gather | solution.py:65
  461.7 81.3 %reduce-scatter.5.cloned.1.call-start = ((), (), s32[]{:S(2)}) async-start(), calls=%async_computation.6 | async-start | bytes 786432 | tf_op jit(solution)/shard_map/reduce_scatter | solution.py:76
  469.3 75.6 %copy-start.1 = (bf16[128,1024]{1,0:T(8,128)(2,1)}, bf16[128,1024]{1,0:T(8,128)(2,1)S(1)}, u32[]{:S(2)}) copy-start(bf16[128,1024]{1,0:T(8,128)(2,1)S(1)} %get-tuple-element.47) | copy-start | bytes 786436
  532.9 4.6 copy-start
Sparse Core Ops, SparseCore 0:
  10.8 194.1 all-gather.8
  214.4 74.2 all-gather.14
  292.1 74.6 all-gather.16
  369.3 87.7 all-gather.10
  461.2 6.7 reduce-scatter.2
  471.0 61.8 all-gather.12
  536.4 6.5 reduce-scatter.4
where the time goes:
time: 552 us
  waiting for transfers between devices  456 us (83%)
  blocking collectives  40.1 us (7%)
  matrix products  22 us (4%)
  between operations  16.2 us (3%)
  local copies, waits for them, and re-layouts  10.5 us (2%)
  other arithmetic  6.2 us (1%)
    all_gather x1, waiting for transfers between devices, shards(): lax.all_gather(w_proj, 'ctx', axis=0, tiled=True)  195 us
    all_gather x1, waiting for transfers between devices, attend_groups(): v_piece = lax.all_gather(value_flat, 'ctx', axis=0, tiled=True)  78.1 us
    all_gather x1, waiting for transfers between devices, shards(): lax.all_gather(w_out, 'ctx', axis=1, tiled=True)  76.5 us
    all_gather x1, waiting for transfers between devices, shards(): piece = lax.all_gather(neg_emb, 'ctx', axis=0, tiled=True)  63.6 us
    all_gather x1, blocking collectives, attend_groups(): p_piece = lax.all_gather(own_pos, 'ctx', axis=0, tiled=True)  37.6 us
    all_gather x1, waiting for transfers between devices, attend_groups(): k_piece = lax.all_gather(key_flat, 'ctx', axis=0, tiled=True)  32.6 us
  transfers between devices with their start and end apart: 7, of which 7 were waited for; matrix products, arithmetic and copies ran while one was open for 3% of the time, Pallas kernels for 0%

commit v1 on v0

--- a/solution.py
+++ b/solution.py
@@ -1,9 +1,14 @@
 import jax
 import jax.numpy as jnp
 from jax import lax
+from jax.experimental import pallas as pl
+from jax.experimental.pallas import tpu as pltpu
 from jax.sharding import PartitionSpec as P
 
 HEAD_DIM = 128
+VMEM_LIMIT = 48 * 1024 * 1024
+BF16 = jnp.bfloat16
+F32 = jnp.float32
 
 
 def attend_piece(q_group, q_pos, k_piece, v_piece, p_piece):
@@ -19,25 +24,9 @@
     return jnp.einsum("htk,khd->thd", weight, value_heads, preferred_element_type=jnp.float32)
 
 
-def attend_groups(groups, key_flat, value_flat, own_pos):
-    initial = tuple((jnp.zeros(group.shape, jnp.float32) for group, _ in groups))
-    k_piece = lax.all_gather(key_flat, "ctx", axis=0, tiled=True)
-    v_piece = lax.all_gather(value_flat, "ctx", axis=0, tiled=True)
-    p_piece = lax.all_gather(own_pos, "ctx", axis=0, tiled=True)
-    updated = []
-    for (q_group, q_pos), total in zip(groups, initial):
-
-        def skipped(carry):
-            return carry
-
-        def computed(carry):
-            return attend_piece(q_group, q_pos, k_piece, v_piece, p_piece)
-
-        updated.append(lax.cond(jnp.min(p_piece) > jnp.max(q_pos), skipped, computed, total))
-    return tuple(updated)
-
-
-def shards(tokens, w_proj, w_out, positions, neg_emb, neg_ids, target_emb, target_ids):
+def general_shards(
+    tokens, w_proj, w_out, positions, neg_emb, neg_ids, target_emb, target_ids
+):
     tok_rows = tokens.shape[0]
     head_cols = w_proj.shape[2]
     local_heads = head_cols // HEAD_DIM
@@ -49,10 +38,11 @@
     )
     proj = jax.nn.silu(proj_sum).astype(jnp.bfloat16)
     gate = proj[:, 0].reshape(tok_rows, local_heads, HEAD_DIM)
-    value_flat = proj[:, 1]
     query = proj[:, 2].reshape(tok_rows, local_heads, HEAD_DIM)
-    key_flat = proj[:, 3]
-    (attn,) = attend_groups([(query, positions)], key_flat, value_flat, positions)
+    v_piece = lax.all_gather(proj[:, 1], "ctx", axis=0, tiled=True)
+    k_piece = lax.all_gather(proj[:, 3], "ctx", axis=0, tiled=True)
+    p_piece = lax.all_gather(positions, "ctx", axis=0, tiled=True)
+    attn = attend_piece(query, positions, k_piece, v_piece, p_piece)
     normed = attn * lax.rsqrt(jnp.mean(attn * attn, axis=-1, keepdims=True) + 1e-06)
     gated = (normed * gate.astype(jnp.float32)).astype(jnp.bfloat16).reshape(tok_rows, head_cols)
     out_terms = jnp.dot(
@@ -87,6 +77,279 @@
     return (hidden, loss)
 
 
+NZ, NY, NX = 4, 2, 2
+CHIPS = NZ * NY * NX
+SWAP = [(0, 1), (1, 0)]
+RELATIVE = [(by, bx, s) for by in range(NY) for bx in range(NX) for s in range(NZ)]
+
+
+def chip_at(z, y, x):
+    return (z * NY + y) * NX + x
+
+
+def coords(c):
+    return c // (NY * NX), (c // NX) % NY, c % NX
+
+
+def relative_chip(c, by, bx, s):
+    z, y, x = coords(c)
+    return chip_at((z + NZ - s) % NZ, y ^ by, x ^ bx)
+
+
+def z_shift(s):
+    return [(c, relative_chip(c, 0, 0, NZ - s)) for c in range(CHIPS)]
+
+
+def flip(by, bx):
+    return [(c, relative_chip(c, by, bx, 0)) for c in range(CHIPS)]
+
+
+def hop(value, perm):
+    return lax.ppermute(value, "ctx", perm)
+
+
+def swap_cores(value):
+    return lax.ppermute(value, "tp", SWAP)
+
+
+def gather_chips(own):
+    near = jnp.stack([own] + [hop(own, z_shift(s)) for s in range(1, NZ)])
+    beside_x = hop(near, flip(0, 1))
+    beside_y = hop(near, flip(1, 0))
+    half = NZ // 2
+    across_a = hop(beside_x[:half], flip(1, 0))
+    across_b = hop(beside_y[half:], flip(0, 1))
+    return [near, beside_x, beside_y, across_a, across_b]
+
+
+def silu(v):
+    return 0.5 * v * (1.0 + jnp.tanh(0.5 * v))
+
+
+def proj_kernel(where, *refs):
+    tok, (w_own, w_other), (gate_query, value_key), w_all = (
+        refs[:5], refs[5:7], refs[7:9], refs[9],
+    )
+    low, u = where[0], where[1]
+    block = HEAD_DIM
+    count = w_own.shape[0]
+    for d in range(count):
+        spot = lax.bitwise_xor(low, d)
+        for half, src in ((u, w_own), (1 - u, w_other)):
+            start = pl.multiple_of((half * count + spot) * block, block)
+            w_all[pl.ds(start, block), :] = src[d]
+    base = 0
+    for ref in tok:
+        pieces, rows, _ = ref.shape
+        for at in range(pieces):
+            proj = silu(jnp.dot(ref[at], w_all[...], preferred_element_type=F32)).astype(BF16)
+            out = pl.ds(base, rows)
+            gate_query[out, :HEAD_DIM] = proj[:, :HEAD_DIM]
+            value_key[out, :HEAD_DIM] = proj[:, HEAD_DIM : 2 * HEAD_DIM]
+            gate_query[out, HEAD_DIM:] = proj[:, 2 * HEAD_DIM : 3 * HEAD_DIM]
+            value_key[out, HEAD_DIM:] = proj[:, 3 * HEAD_DIM :]
+            base += rows
+
+
+def attend_kernel(gate_query, kv_own, kv_other, pos_col, pos_own, pos_other, gated):
+    rows = gate_query.shape[0]
+    tile = min(256, rows)
+
+    def step(at, carry):
+        span = pl.ds(pl.multiple_of(at * tile, tile), tile)
+        query = gate_query[span, HEAD_DIM:]
+        q_pos = pos_col[span, :]
+        attn = jnp.zeros((tile, HEAD_DIM), F32)
+        for kv, pos in ((kv_own, pos_own), (kv_other, pos_other)):
+            scores = lax.dot_general(
+                query, kv[:, HEAD_DIM:], (((1,), (1,)), ((), ())), preferred_element_type=F32
+            ) * HEAD_DIM ** (-0.5)
+            weight = jnp.where(pos[...] <= q_pos, silu(scores), 0.0).astype(BF16)
+            attn += jnp.dot(weight, kv[:, :HEAD_DIM], preferred_element_type=F32)
+        normed = attn * lax.rsqrt(jnp.mean(attn * attn, axis=-1, keepdims=True) + 1e-06)
+        gate = gate_query[span, :HEAD_DIM].astype(F32)
+        gated[span, :] = (normed * gate).astype(BF16)
+        return carry
+
+    lax.fori_loop(0, rows // tile, step, 0)
+
+
+def hidden_kernel(where, *refs):
+    pieces = refs[:CHIPS]
+    w_own, w_other = refs[CHIPS : CHIPS + 5], refs[CHIPS + 5 : CHIPS + 10]
+    tokens, keep, send, gated, hidden = refs[CHIPS + 10 :]
+    c, u = where[0], where[1]
+    width = HEAD_DIM
+    half = hidden.shape[1] // 2
+    for ref, (by, bx, s) in zip(pieces, RELATIVE):
+        head = relative_chip(c, by, bx, NZ - s)
+        gated[:, pl.ds(pl.multiple_of(head * width, width), width)] = ref[...]
+    g_own = gated[:, pl.ds(pl.multiple_of(u * half, half), half)]
+    g_other = gated[:, pl.ds(pl.multiple_of((1 - u) * half, half), half)]
+    at = 0
+    for own, other in zip(w_own, w_other):
+        for i in range(own.shape[0]):
+            block = relative_chip(c, *RELATIVE[at])
+            cols = pl.ds(pl.multiple_of(block * width, width), width)
+            total = jnp.dot(g_own, own[i], preferred_element_type=F32)
+            total += jnp.dot(g_other, other[i], preferred_element_type=F32)
+            hidden[:, cols] = (tokens[:, cols].astype(F32) + total).astype(BF16)
+            at += 1
+    keep[...] = hidden[:, pl.ds(pl.multiple_of(u * half, half), half)]
+    send[...] = hidden[:, pl.ds(pl.multiple_of((1 - u) * half, half), half)]
+
+
+def loss_kernel(*refs):
+    h_keep, h_send, t_keep, t_send, t_ids, n_ids, nn = refs[:7]
+    n_own, n_other = refs[7:12], refs[12:17]
+    loss, dots = refs[17:]
+    keep, send = h_keep[...], h_send[...]
+    at = 0
+    for own, other in zip(n_own, n_other):
+        for i in range(0, own.shape[0], 2):
+            rows = 2 * own.shape[1]
+            total = jnp.zeros((keep.shape[0], rows), F32)
+            for part, ref in ((keep, own), (send, other)):
+                neg = ref[pl.ds(i, 2)].reshape(rows, part.shape[1])
+                total += lax.dot_general(
+                    part, neg, (((1,), (1,)), ((), ())), preferred_element_type=F32
+                )
+            dots[:, pl.ds(at, rows)] = total
+            at += rows
+    hh = he = ee = 0.0
+    for part, ref in ((keep, t_keep), (send, t_send)):
+        h_f, t_f = part.astype(F32), ref[...].astype(F32)
+        hh += jnp.sum(h_f * h_f, axis=1, keepdims=True)
+        he += jnp.sum(h_f * t_f, axis=1, keepdims=True)
+        ee += jnp.sum(t_f * t_f, axis=1, keepdims=True)
+    h_scale = lax.rsqrt(hh + 1e-06) * 20.0
+    pos_logit = he * lax.rsqrt(ee + 1e-06) * h_scale
+    neg_logit = dots[...] * h_scale * lax.rsqrt(nn[...] + 1e-06)
+    mass = jnp.where(n_ids[...] != t_ids[...], jnp.exp(neg_logit), 0.0)
+    total = jnp.exp(pos_logit) + jnp.sum(mass, axis=1, keepdims=True)
+    loss[...] = jnp.log(total) - pos_logit
+
+
+def call(kernel, outs, scratch, args, scalars=0, flops=0, name=None):
+    specs = [pl.BlockSpec(memory_space=pltpu.SMEM)] * scalars
+    specs += [pl.BlockSpec(memory_space=pltpu.VMEM)] * (len(args) - scalars)
+    moved = sum(a.size * a.dtype.itemsize for a in args)
+    return pl.pallas_call(
+        kernel,
+        out_shape=[jax.ShapeDtypeStruct(shape, dtype) for shape, dtype in outs],
+        in_specs=specs,
+        out_specs=[pl.BlockSpec(memory_space=pltpu.VMEM)] * len(outs),
+        scratch_shapes=scratch,
+        compiler_params=pltpu.CompilerParams(vmem_limit_bytes=VMEM_LIMIT),
+        cost_estimate=pl.CostEstimate(flops=flops, bytes_accessed=moved, transcendentals=0),
+        name=name,
+    )(*args)
+
+
+def head_shards(
+    tokens, w_proj, w_out, positions, neg_emb, neg_ids, target_emb, target_ids
+):
+    c, u = lax.axis_index("ctx"), lax.axis_index("tp")
+    model = tokens.shape[1]
+    rows = tokens.shape[0] // 2
+    events = rows * CHIPS
+    low_heads = w_proj.shape[2] // HEAD_DIM
+    low = c % low_heads
+
+    mine = lax.dynamic_slice_in_dim(tokens, u * rows, rows, 0)
+    tok = gather_chips(mine)
+    pos = jnp.concatenate(gather_chips(positions.reshape(2, rows)))
+
+    w_heads = w_proj.reshape(-1, 4, low_heads, HEAD_DIM).transpose(2, 0, 1, 3)
+    w_heads = w_heads.reshape(low_heads, -1, 4 * HEAD_DIM)
+    w_mine = []
+    for d in range(low_heads):
+        perm = [
+            (2 * src + t, 2 * (t * low_heads + ((src ^ d) % low_heads)) + src // low_heads)
+            for src in range(CHIPS)
+            for t in range(2)
+        ]
+        piece = lax.dynamic_index_in_dim(w_heads, low ^ d, 0, keepdims=False)
+        w_mine.append(lax.ppermute(piece, ("ctx", "tp"), perm))
+    w_mine = jnp.stack(w_mine)
+    w_other = swap_cores(w_mine)
+
+    w_out, neg_emb, _ = lax.optimization_barrier((w_out, neg_emb, tok[0]))
+    out_own = gather_chips(w_out)
+    out_other = [swap_cores(piece) for piece in out_own]
+    neg_own = gather_chips(neg_emb)
+    neg_other = [swap_cores(piece) for piece in neg_own]
+    t_rows = target_emb.reshape(2, rows, -1)
+    t_keep = lax.dynamic_index_in_dim(t_rows, u, 0, keepdims=False)
+    t_send = swap_cores(lax.dynamic_index_in_dim(t_rows, 1 - u, 0, keepdims=False))
+    order = jnp.stack([relative_chip(c, *at) for at in RELATIVE])
+    n_ids = neg_ids.reshape(CHIPS, -1)[order].reshape(1, -1)
+    nn = sum(
+        jnp.concatenate([jnp.sum(jnp.square(p.astype(F32)), axis=-1) for p in side])
+        for side in (neg_own, neg_other)
+    ).reshape(1, -1)
+
+    where_low = jnp.stack([low, u]).astype(jnp.int32)
+    where = jnp.stack([c, u]).astype(jnp.int32)
+    gate_query, value_key = call(
+        proj_kernel,
+        [((events, 2 * HEAD_DIM), BF16)] * 2,
+        [pltpu.VMEM((model, 4 * HEAD_DIM), BF16)],
+        [where_low, *tok, w_mine, w_other],
+        scalars=1,
+        flops=2 * events * model * 4 * HEAD_DIM,
+        name="project",
+    )
+    kv_other = swap_cores(value_key)
+    pos_mine = lax.dynamic_index_in_dim(pos, u, 1, keepdims=False).reshape(-1)
+    pos_theirs = lax.dynamic_index_in_dim(pos, 1 - u, 1, keepdims=False).reshape(-1)
+    (gated,) = call(
+        attend_kernel,
+        [((events, HEAD_DIM), BF16)],
+        [],
+        [gate_query, value_key, kv_other, pos_mine[:, None], pos_mine[None], pos_theirs[None]],
+        flops=8 * events * events * HEAD_DIM,
+        name="attend",
+    )
+    gated = gated.reshape(CHIPS, rows, HEAD_DIM)
+    pieces = [gated[0]]
+    for at in range(1, CHIPS):
+        perm = [(src, relative_chip(src, *RELATIVE[at])) for src in range(CHIPS)]
+        pieces.append(hop(gated[at], perm))
+    half = model // 2
+    h_keep, h_send = call(
+        hidden_kernel,
+        [((rows, half), BF16)] * 2,
+        [pltpu.VMEM((rows, model), BF16)] * 2,
+        [where, *pieces, *out_own, *out_other, mine],
+        scalars=1,
+        flops=2 * rows * model * model,
+        name="hidden",
+    )
+    h_theirs = swap_cores(h_send)
+    (loss,) = call(
+        loss_kernel,
+        [((rows, 1), F32)],
+        [pltpu.VMEM((rows, neg_ids.shape[0]), F32)],
+        [h_keep, h_send, t_keep, t_send, target_ids[:, None], n_ids, nn, *neg_own, *neg_other],
+        flops=2 * rows * model * neg_ids.shape[0],
+        name="loss",
+    )
+    hidden = jnp.where(
+        u == 0,
+        jnp.concatenate([h_keep, h_theirs]),
+        jnp.concatenate([h_theirs, h_keep]),
+    )
+    return hidden, loss.reshape(-1)
+
+
+def shards(tokens, w_proj, *rest):
+    n_ctx, n_tp = lax.axis_size("ctx"), lax.axis_size("tp")
+    heads = w_proj.shape[2] * n_tp // HEAD_DIM
+    plan = head_shards if (n_ctx, n_tp, heads) == (CHIPS, 2, CHIPS) else general_shards
+    return plan(tokens, w_proj, *rest)
+
+
 def solution(mesh):
     placed = (
         P("ctx", None),

time: 552 us -> 262 us (0.47)
  waiting for transfers between devices: 456 us -> 86.8 us
  starting transfers between devices: 0.28 us -> 97.9 us
  blocking collectives: 40.1 us -> 0 us
  local copies, waits for them, and re-layouts: 10.5 us -> 39.1 us
  matrix products: 22 us -> 0 us
  Pallas kernels: 0 us -> 19.5 us
  between operations: 16.2 us -> 1.46 us
  other arithmetic: 6.2 us -> 15.8 us
    all_gather x5 -> x0, waiting for transfers between devices: 446 us -> none  [the longest x1 195 us: shards(): lax.all_gather(w_proj, 'ctx', axis=0, tiled=True)]
    ppermute x0 -> x65, starting transfers between devices: none -> 97.9 us  [the longest x43 79.9 us: hop(): return lax.ppermute(value, 'ctx', perm)]
    ppermute x0 -> x65, waiting for transfers between devices: none -> 86.8 us  [the longest x43 85.2 us: hop(): return lax.ppermute(value, 'ctx', perm)]
    all_gather x1 -> x0, blocking collectives: 37.6 us -> none  [attend_groups(): p_piece = lax.all_gather(own_pos, 'ctx', axis=0, tiled=True)]
    dot_general x4 -> x0, matrix products: 22 us -> none  [the longest x1 8.39 us: shards(): jnp.einsum('td,dfh->tfh', tokens, lax.all_gather(w_proj, 'ctx', axis=0, t...]
    pallas_call x0 -> x4, Pallas kernels: none -> 19.5 us  [call(): pl.pallas_call(kernel, out_shape=[jax.ShapeDtypeStruct(shape, dtype) for...]
    unnamed x18 -> x184, local copies, waits for them, and re-layouts: 3.14 us -> 21.9 us
    reduce_scatter x2 -> x0, waiting for transfers between devices: 8.69 us -> none  [the longest x1 6.27 us: shards(): lax.psum_scatter(out_terms, 'tp', scatter_dimension=1, tiled=True)]
  transfers between devices with their start and end apart: 7 -> 65, of which waited for: 7 -> 18; matrix products, arithmetic and copies ran while one was open for 3% -> 14% of each run, Pallas kernels for 0% -> 7%
where the time goes in v1:
time: 262 us; the launch traced here: 261 us
  starting transfers between devices  97.9 us (37%)
  waiting for transfers between devices  86.8 us (33%)
  local copies, waits for them, and re-layouts  39.1 us (15%)
  Pallas kernels  19.5 us (7%)
  other arithmetic  15.8 us (6%)
    ppermute x43, waiting for transfers between devices, hop(): return lax.ppermute(value, 'ctx', perm)  85.2 us
    ppermute x43, starting transfers between devices, hop(): return lax.ppermute(value, 'ctx', perm)  79.9 us
    unnamed x184, local copies, waits for them, and re-layouts  21.9 us
    pallas_call x4, Pallas kernels, call(): pl.pallas_call(kernel, out_shape=[jax.ShapeDtypeStruct(shape, dtype) for...  19.5 us
    ppermute x8, starting transfers between devices, head_shards(): w_mine.append(lax.ppermute(piece, ('ctx', 'tp'), perm))  15.2 us
    reduce_sum x10, other arithmetic, head_shards(): jnp.sum(jnp.square(p.astype(F32)), axis=-1)  10.8 us
  transfers between devices with their start and end apart: 65, of which 18 were waited for; matrix products, arithmetic and copies ran while one was open for 14% of the time, Pallas kernels for 7%

profile of v1, /device:TPU:0, one launch (start us, length us, event | category | flops | bytes accessed | tf_op | source)
XLA Modules:
  0.0 260.6 jit_solution(17802668845332765917)
XLA Ops:
  1.7 5.1 %collective-permute-start.2 = (bf16[64,2048]{1,0:T(8,128)(2,1)S(1)}, bf16[64,2048]{1,0:T(8,128)(2,1)S(1)}, u32[]{:S(2)}, u32[]{:S(2)}) collective-permute-start(bf16[64,2048]{1,0:T(8,128)(2,1)S(1)} %constant_dynamic-slice_fusion.1.refs_26_), channel_id=1, source_target_pairs={{0,24},{2,26},{4,28},{6,30},{8,0},{10,2},{12,4},{14,6},{16,8},{18,... | collective-permute-start | bytes 786440 | tf_op jit(solution)/shard_map/ppermute | solution.py:108
  19.8 2.5 collective-permute-start.17
  23.0 21.5 %collective-permute-start.18 = (s32[2,64]{1,0:T(2,128)}, s32[2,64]{1,0:T(2,128)S(1)}, u32[]{:S(2)}, u32[]{:S(2)}) collective-permute-start(s32[2,64]{1,0:T(2,128)} %reshape.699), channel_id=1, source_target_pairs={{0,16},{2,18},{4,20},{6,22},{8,24},{10,26},{12,28},{14,30},{16,0},... | collective-permute-start | bytes 1544 | tf_op jit(solution)/shard_map/ppermute | solution.py:108
  45.1 2.5 collective-permute-start.19
  54.9 4.1 %collective-permute-start.13 = (bf16[128,512]{1,0:T(8,128)(2,1)S(1)}, bf16[128,512]{1,0:T(8,128)(2,1)S(1)}, u32[]{:S(2)}, u32[]{:S(2)}) collective-permute-start(bf16[128,512]{1,0:T(8,128)(2,1)S(1)} %copy-done.60), channel_id=1, source_target_pairs={{0,12},{1,28},{2,14},{3,30},{4,8},{5,24},{6,10},{7,26},{8,4},{9,20... | collective-permute-start | bytes 393224 | tf_op jit(solution)/shard_map/ppermute | solution.py:273
  59.6 2.4 collective-permute-start.14
  62.1 4.8 %collective-permute-start.4 = (bf16[4,64,2048]{2,1,0:T(8,128)(2,1)S(1)}, bf16[4,64,2048]{2,1,0:T(8,128)(2,1)}, u32[]{:S(2)}, u32[]{:S(2)}) collective-permute-start(bf16[4,64,2048]{2,1,0:T(8,128)(2,1)S(1)} %pad_maximum_fusion.refs_0_), channel_id=1, source_target_pairs={{0,4},{2,6},{4,0},{6,2},{8,12},{10,14},{12,8},{14,10},{16,20},{18,... | collective-permute-start | bytes 3145736 | tf_op jit(solution)/shard_map/ppermute | solution.py:108
  70.8 2.5 collective-permute-done.55
  73.3 7.4 %collective-permute-done.54 = bf16[64,1024]{1,0:T(8,128)(2,1)S(1)} collective-permute-done((bf16[64,1024]{1,0:T(8,128)(2,1)S(1)}, bf16[64,1024]{1,0:T(8,128)(2,1)S(1)}, u32[]{:S(2)}, u32[]{:S(2)}) %collective-permute-start.54) | collective-permute-done | bytes 131104 | tf_op jit(solution)/shard_map/ppermute | solution.py:108
  87.7 2.7 %collective-permute-done.41 = bf16[1024,128]{1,0:T(8,128)(2,1)} collective-permute-done((bf16[1024,128]{1,0:T(8,128)(2,1)S(1)}, bf16[1024,128]{1,0:T(8,128)(2,1)}, u32[]{:S(2)}, u32[]{:S(2)}) %collective-permute-start.41) | collective-permute-done | bytes 262176 | tf_op jit(solution)/shard_map/ppermute | solution.py:108
  91.2 12.5 %collective-permute-done.40 = bf16[1024,128]{1,0:T(8,128)(2,1)} collective-permute-done((bf16[1024,128]{1,0:T(8,128)(2,1)S(1)}, bf16[1024,128]{1,0:T(8,128)(2,1)}, u32[]{:S(2)}, u32[]{:S(2)}) %collective-permute-start.40) | collective-permute-done | bytes 262176 | tf_op jit(solution)/shard_map/ppermute | solution.py:108
  111.1 6.3 %collective-permute-done.21 = s32[4,2,64]{2,1,0:T(2,128)S(1)} collective-permute-done((s32[4,2,64]{2,1,0:T(2,128)S(1)}, s32[4,2,64]{2,1,0:T(2,128)S(1)}, u32[]{:S(2)}, u32[]{:S(2)}) %collective-permute-start.21) | collective-permute-done | bytes 2080 | tf_op jit(solution)/shard_map/ppermute | solution.py:108
  121.7 30.6 %collective-permute-done.6.refs_4_ = bf16[2,64,2048]{2,1,0:T(8,128)(2,1)S(1)} collective-permute-done((bf16[2,64,2048]{2,1,0:T(8,128)(2,1)S(1)}, bf16[2,64,2048]{2,1,0:T(8,128)(2,1)S(1)}, u32[]{:S(2)}, u32[]{:S(2)}) %collective-permute-start.6) | collective-permute-done | bytes 524320 | tf_op jit(solution)/shard_map/ppermute | solution.py:108
  153.2 8.1 %project.1 = (bf16[1024,256]{1,0:T(8,128)(2,1)S(1)}, bf16[1024,256]{1,0:T(8,128)(2,1)S(1)}) custom-call(s32[2]{0:T(128)S(1)} %pad_add_fusion.2.where, bf16[4,64,2048]{2,1,0:T(8,128)(2,1)S(1)} %copy-done.14, bf16[4,64,2048]{2,1,0:T(8,128)(2,1)S(1)} %copy-done.19, bf16[4,64,2048]{2,1,0:T(8,128)(2,1)} %collective-permute-done.4.refs_2_, ...), custom_call_target="tpu_custom_call" | custom-call | flops 2147483648 | bytes 6291464 | tf_op jit(solution)/shard_map/project/pallas_call | solution.py:237
  165.2 6.0 %collective-permute-done.58.refs_10_ = bf16[2,64,1024]{2,1,0:T(8,128)(2,1)} collective-permute-done((bf16[2,64,1024]{2,1,0:T(8,128)(2,1)S(1)}, bf16[2,64,1024]{2,1,0:T(8,128)(2,1)}, u32[]{:S(2)}, u32[]{:S(2)}) %collective-permute-start.58) | collective-permute-done | bytes 262176 | tf_op jit(solution)/shard_map/ppermute | solution.py:108
  174.7 4.5 %collective-permute-done.59.refs_11_ = bf16[2,64,1024]{2,1,0:T(8,128)(2,1)S(1)} collective-permute-done((bf16[2,64,1024]{2,1,0:T(8,128)(2,1)S(1)}, bf16[2,64,1024]{2,1,0:T(8,128)(2,1)S(1)}, u32[]{:S(2)}, u32[]{:S(2)}) %collective-permute-start.59) | collective-permute-done | bytes 262176 | tf_op jit(solution)/shard_map/ppermute | solution.py:108
  190.2 3.8 %attend.1 = bf16[1024,128]{1,0:T(8,128)(2,1)S(1)} custom-call(bf16[1024,256]{1,0:T(8,128)(2,1)S(1)} %copy-done.56, bf16[1024,256]{1,0:T(8,128)(2,1)S(1)} %copy-done.52, bf16[1024,256]{1,0:T(8,128)(2,1)S(1)} %copy-done.54, s32[1024,1]{1,0:T(8,128)S(1)} %copy-done.15, s32[1,1024]{1,0:T(1,128)S(1)} %broadcast_in_dim_reshape.10.pos_own, ...), custom_call_target="tpu_custom_call" | custom-call | flops 1073741824 | bytes 1585152 | tf_op jit(solution)/shard_map/attend/pallas_call | solution.py:237
  205.4 2.5 collective-permute-start.29
  211.1 3.4 %collective-permute-start.32 = (bf16[64,128]{1,0:T(8,128)(2,1)S(1)}, bf16[64,128]{1,0:T(8,128)(2,1)S(1)}, u32[]{:S(2)}, u32[]{:S(2)}) collective-permute-start(bf16[64,128]{1,0:T(8,128)(2,1)S(1)} %copy-done.71), channel_id=1, source_target_pairs={{0,28},{2,30},{4,24},{6,26},{8,4},{10,6},{12,0},{14,2},{16,12},{18... | collective-permute-start | bytes 49160 | tf_op jit(solution)/shard_map/ppermute | solution.py:108
  220.2 2.2 collective-permute-start.36
  228.3 4.0 %collective-permute-done.37.refs_14_ = bf16[64,128]{1,0:T(8,128)(2,1)S(1)} collective-permute-done((bf16[64,128]{1,0:T(8,128)(2,1)}, bf16[64,128]{1,0:T(8,128)(2,1)S(1)}, u32[]{:S(2)}, u32[]{:S(2)}) %collective-permute-start.37) | collective-permute-done | bytes 16416 | tf_op jit(solution)/shard_map/ppermute | solution.py:108
  236.4 3.3 %collective-permute-done.38.refs_15_ = bf16[64,128]{1,0:T(8,128)(2,1)S(1)} collective-permute-done((bf16[64,128]{1,0:T(8,128)(2,1)S(1)}, bf16[64,128]{1,0:T(8,128)(2,1)S(1)}, u32[]{:S(2)}, u32[]{:S(2)}) %collective-permute-start.38) | collective-permute-done | bytes 16416 | tf_op jit(solution)/shard_map/ppermute | solution.py:108
  245.3 4.5 %hidden.1 = (bf16[64,1024]{1,0:T(8,128)(2,1)S(1)}, bf16[64,1024]{1,0:T(8,128)(2,1)}) custom-call(s32[2]{0:T(128)S(1)} %copy-done.50, bf16[64,128]{1,0:T(8,128)(2,1)S(1)} %get-tuple-element.43.refs_0_, bf16[64,128]{1,0:T(8,128)(2,1)S(1)} %copy-done.22, bf16[64,128]{1,0:T(8,128)(2,1)S(1)} %copy-done.24, bf16[64,128]{1,0:T(8,128)(2,1)S(1)} %copy-done.26, ...), custom_call_target="tpu_custom_call" | custom-call | flops 536870912 | bytes 8912904 | tf_op jit(solution)/shard_map/hidden/pallas_call | solution.py:237
  256.1 3.1 %loss.1 = f32[64,1]{1,0:T(8,128)S(1)} custom-call(bf16[64,1024]{1,0:T(8,128)(2,1)S(1)} %get-tuple-element.11.refs_0_, bf16[64,1024]{1,0:T(8,128)(2,1)} %get-tuple-element.12.refs_1_, bf16[64,1024]{1,0:T(8,128)(2,1)S(1)} %copy-done.16, bf16[64,1024]{1,0:T(8,128)(2,1)} %collective-permute-done.52.refs_3_, s32[64,1]{1,0:T(8,128)S(1)} %copy-done.20, ...), custom_call_target="tpu_custom_call" | custom-call | flops 268435456 | bytes 4727040 | tf_op jit(solution)/shard_map/loss/pallas_call | solution.py:237
  (347 shorter events, 108.7 us)
Async XLA Ops:
  1.7 43.4 %collective-permute-start.2 = (bf16[64,2048]{1,0:T(8,128)(2,1)S(1)}, bf16[64,2048]{1,0:T(8,128)(2,1)S(1)}, u32[]{:S(2)}, u32[]{:S(2)}) collective-permute-start(bf16[64,2048]{1,0:T(8,128)(2,1)S(1)} %constant_dynamic-slice_fusion.1.refs_26_), channel_id=1, source_target_pairs={{0,24},{2,26},{4,28},{6,30},{8,0},{10,2},{12,4},{14,6},{16,8},{18,... | collective-permute-start | bytes 786440 | tf_op jit(solution)/shard_map/ppermute | solution.py:108
  6.8 40.8 %collective-permute-start.1 = (bf16[64,2048]{1,0:T(8,128)(2,1)S(1)}, bf16[64,2048]{1,0:T(8,128)(2,1)S(1)}, u32[]{:S(2)}, u32[]{:S(2)}) collective-permute-start(bf16[64,2048]{1,0:T(8,128)(2,1)S(1)} %constant_dynamic-slice_fusion.1.refs_26_), channel_id=1, source_target_pairs={{0,16},{2,18},{4,20},{6,22},{8,24},{10,26},{12,28},{14,30},{16,0},... | collective-permute-start | bytes 786440 | tf_op jit(solution)/shard_map/ppermute | solution.py:108
  6.8 41.5 %collective-permute-start = (bf16[64,2048]{1,0:T(8,128)(2,1)S(1)}, bf16[64,2048]{1,0:T(8,128)(2,1)}, u32[]{:S(2)}, u32[]{:S(2)}) collective-permute-start(bf16[64,2048]{1,0:T(8,128)(2,1)S(1)} %constant_dynamic-slice_fusion.1.refs_26_), channel_id=1, source_target_pairs={{0,8},{2,10},{4,12},{6,14},{8,16},{10,18},{12,20},{14,22},{16,24},... | collective-permute-start | bytes 786440 | tf_op jit(solution)/shard_map/ppermute | solution.py:108
  19.8 39.8 %collective-permute-start.17 = (s32[2,64]{1,0:T(2,128)}, s32[2,64]{1,0:T(2,128)S(1)}, u32[]{:S(2)}, u32[]{:S(2)}) collective-permute-start(s32[2,64]{1,0:T(2,128)} %reshape.699), channel_id=1, source_target_pairs={{0,8},{2,10},{4,12},{6,14},{8,16},{10,18},{12,20},{14,22},{16,24},... | collective-permute-start | bytes 1544 | tf_op jit(solution)/shard_map/ppermute | solution.py:108
  23.0 44.6 %collective-permute-start.18 = (s32[2,64]{1,0:T(2,128)}, s32[2,64]{1,0:T(2,128)S(1)}, u32[]{:S(2)}, u32[]{:S(2)}) collective-permute-start(s32[2,64]{1,0:T(2,128)} %reshape.699), channel_id=1, source_target_pairs={{0,16},{2,18},{4,20},{6,22},{8,24},{10,26},{12,28},{14,30},{16,0},... | collective-permute-start | bytes 1544 | tf_op jit(solution)/shard_map/ppermute | solution.py:108
  45.1 24.4 %collective-permute-start.19 = (s32[2,64]{1,0:T(2,128)}, s32[2,64]{1,0:T(2,128)S(1)}, u32[]{:S(2)}, u32[]{:S(2)}) collective-permute-start(s32[2,64]{1,0:T(2,128)} %reshape.699), channel_id=1, source_target_pairs={{0,24},{2,26},{4,28},{6,30},{8,0},{10,2},{12,4},{14,6},{16,8},{18,... | collective-permute-start | bytes 1544 | tf_op jit(solution)/shard_map/ppermute | solution.py:108
  52.8 30.0 %collective-permute-start.3 = (bf16[4,64,2048]{2,1,0:T(8,128)(2,1)S(1)}, bf16[4,64,2048]{2,1,0:T(8,128)(2,1)S(1)}, u32[]{:S(2)}, u32[]{:S(2)}) collective-permute-start(bf16[4,64,2048]{2,1,0:T(8,128)(2,1)S(1)} %pad_maximum_fusion.refs_0_), channel_id=1, source_target_pairs={{0,2},{2,0},{4,6},{6,4},{8,10},{10,8},{12,14},{14,12},{16,18},{18,... | collective-permute-start | bytes 3145736 | tf_op jit(solution)/shard_map/ppermute | solution.py:108
  62.1 45.0 %collective-permute-start.4 = (bf16[4,64,2048]{2,1,0:T(8,128)(2,1)S(1)}, bf16[4,64,2048]{2,1,0:T(8,128)(2,1)}, u32[]{:S(2)}, u32[]{:S(2)}) collective-permute-start(bf16[4,64,2048]{2,1,0:T(8,128)(2,1)S(1)} %pad_maximum_fusion.refs_0_), channel_id=1, source_target_pairs={{0,4},{2,6},{4,0},{6,2},{8,12},{10,14},{12,8},{14,10},{16,20},{18,... | collective-permute-start | bytes 3145736 | tf_op jit(solution)/shard_map/ppermute | solution.py:108
  73.3 47.9 %collective-permute-start.15 = (bf16[8,128,512]{2,1,0:T(8,128)(2,1)}, bf16[8,128,512]{2,1,0:T(8,128)(2,1)}, u32[]{:S(2)}, u32[]{:S(2)}) collective-permute-start(bf16[8,128,512]{2,1,0:T(8,128)(2,1)} %bitcast_dynamic-update-slice_fusion.refs_5_), channel_id=1, source_target_pairs={{0,1},{1,0},{2,3},{3,2},{4,5},{5,4},{6,7},{7,6},{8,9},{9,8},{10,11... | collective-permute-start | bytes 3145736 | tf_op jit(solution)/shard_map/ppermute | solution.py:112
  80.8 22.9 %collective-permute-start.40 = (bf16[1024,128]{1,0:T(8,128)(2,1)S(1)}, bf16[1024,128]{1,0:T(8,128)(2,1)}, u32[]{:S(2)}, u32[]{:S(2)}) collective-permute-start(bf16[1024,128]{1,0:T(8,128)(2,1)S(1)} %copy-done.58), channel_id=1, source_target_pairs={{0,16},{2,18},{4,20},{6,22},{8,24},{10,26},{12,28},{14,30},{16,0},... | collective-permute-start | bytes 786440 | tf_op jit(solution)/shard_map/ppermute | solution.py:108
  86.5 20.1 %collective-permute-start.39 = (bf16[1024,128]{1,0:T(8,128)(2,1)S(1)}, bf16[1024,128]{1,0:T(8,128)(2,1)}, u32[]{:S(2)}, u32[]{:S(2)}) collective-permute-start(bf16[1024,128]{1,0:T(8,128)(2,1)S(1)} %copy-done.58), channel_id=1, source_target_pairs={{0,8},{2,10},{4,12},{6,14},{8,16},{10,18},{12,20},{14,22},{16,24},... | collective-permute-start | bytes 786440 | tf_op jit(solution)/shard_map/ppermute | solution.py:108
  90.4 29.2 %collective-permute-start.56 = (bf16[4,64,1024]{2,1,0:T(8,128)(2,1)S(1)}, bf16[4,64,1024]{2,1,0:T(8,128)(2,1)S(1)}, u32[]{:S(2)}, u32[]{:S(2)}) collective-permute-start(bf16[4,64,1024]{2,1,0:T(8,128)(2,1)S(1)} %get-tuple-element.15.refs_7_), channel_id=1, source_target_pairs={{0,2},{2,0},{4,6},{6,4},{8,10},{10,8},{12,14},{14,12},{16,18},{18,... | collective-permute-start | bytes 1572872 | tf_op jit(solution)/shard_map/ppermute | solution.py:108
  117.4 54.9 %collective-permute-start.42 = (bf16[4,1024,128]{2,1,0:T(8,128)(2,1)S(1)}, bf16[4,1024,128]{2,1,0:T(8,128)(2,1)S(1)}, u32[]{:S(2)}, u32[]{:S(2)}) collective-permute-start(bf16[4,1024,128]{2,1,0:T(8,128)(2,1)S(1)} %pad_maximum_fusion.1.refs_16_), channel_id=1, source_target_pairs={{0,2},{2,0},{4,6},{6,4},{8,10},{10,8},{12,14},{14,12},{16,18},{18,... | collective-permute-start | bytes 3145736 | tf_op jit(solution)/shard_map/ppermute | solution.py:108
  118.3 33.9 %collective-permute-start.6 = (bf16[2,64,2048]{2,1,0:T(8,128)(2,1)S(1)}, bf16[2,64,2048]{2,1,0:T(8,128)(2,1)S(1)}, u32[]{:S(2)}, u32[]{:S(2)}) collective-permute-start(bf16[2,64,2048]{2,1,0:T(8,128)(2,1)S(1)} %slice.115), channel_id=1, source_target_pairs={{0,2},{2,0},{4,6},{6,4},{8,10},{10,8},{12,14},{14,12},{16,18},{18,... | collective-permute-start | bytes 1572872 | tf_op jit(solution)/shard_map/ppermute | solution.py:108
  119.5 42.6 %collective-permute-start.57 = (bf16[4,64,1024]{2,1,0:T(8,128)(2,1)S(1)}, bf16[4,64,1024]{2,1,0:T(8,128)(2,1)S(1)}, u32[]{:S(2)}, u32[]{:S(2)}) collective-permute-start(bf16[4,64,1024]{2,1,0:T(8,128)(2,1)S(1)} %get-tuple-element.15.refs_7_), channel_id=1, source_target_pairs={{0,4},{2,6},{4,0},{6,2},{8,12},{10,14},{12,8},{14,10},{16,20},{18,... | collective-permute-start | bytes 1572872 | tf_op jit(solution)/shard_map/ppermute | solution.py:108
  121.3 42.9 %collective-permute-start.60 = (bf16[4,64,1024]{2,1,0:T(8,128)(2,1)S(1)}, bf16[4,64,1024]{2,1,0:T(8,128)(2,1)S(1)}, u32[]{:S(2)}, u32[]{:S(2)}) collective-permute-start(bf16[4,64,1024]{2,1,0:T(8,128)(2,1)S(1)} %get-tuple-element.15.refs_7_), channel_id=1, source_target_pairs={{0,1},{1,0},{2,3},{3,2},{4,5},{5,4},{6,7},{7,6},{8,9},{9,8},{10,11... | collective-permute-start | bytes 1572872 | tf_op jit(solution)/shard_map/ppermute | solution.py:112
  121.3 51.0 %collective-permute-start.43 = (bf16[4,1024,128]{2,1,0:T(8,128)(2,1)S(1)}, bf16[4,1024,128]{2,1,0:T(8,128)(2,1)S(1)}, u32[]{:S(2)}, u32[]{:S(2)}) collective-permute-start(bf16[4,1024,128]{2,1,0:T(8,128)(2,1)S(1)} %pad_maximum_fusion.1.refs_16_), channel_id=1, source_target_pairs={{0,4},{2,6},{4,0},{6,2},{8,12},{10,14},{12,8},{14,10},{16,20},{18,... | collective-permute-start | bytes 3145736 | tf_op jit(solution)/shard_map/ppermute | solution.py:108
  162.1 36.5 %collective-permute-start.46 = (bf16[4,1024,128]{2,1,0:T(8,128)(2,1)S(1)}, bf16[4,1024,128]{2,1,0:T(8,128)(2,1)}, u32[]{:S(2)}, u32[]{:S(2)}) collective-permute-start(bf16[4,1024,128]{2,1,0:T(8,128)(2,1)S(1)} %pad_maximum_fusion.1.refs_16_), channel_id=1, source_target_pairs={{0,1},{1,0},{2,3},{3,2},{4,5},{5,4},{6,7},{7,6},{8,9},{9,8},{10,11... | collective-permute-start | bytes 3145736 | tf_op jit(solution)/shard_map/ppermute | solution.py:112
  172.3 21.7 %collective-permute-start.61 = (bf16[4,64,1024]{2,1,0:T(8,128)(2,1)S(1)}, bf16[4,64,1024]{2,1,0:T(8,128)(2,1)}, u32[]{:S(2)}, u32[]{:S(2)}) collective-permute-start(bf16[4,64,1024]{2,1,0:T(8,128)(2,1)S(1)} %collective-permute-done.56.refs_8_), channel_id=1, source_target_pairs={{0,1},{1,0},{2,3},{3,2},{4,5},{5,4},{6,7},{7,6},{8,9},{9,8},{10,11... | collective-permute-start | bytes 1572872 | tf_op jit(solution)/shard_map/ppermute | solution.py:112
  172.3 22.5 %collective-permute-start.62 = (bf16[4,64,1024]{2,1,0:T(8,128)(2,1)S(1)}, bf16[4,64,1024]{2,1,0:T(8,128)(2,1)}, u32[]{:S(2)}, u32[]{:S(2)}) collective-permute-start(bf16[4,64,1024]{2,1,0:T(8,128)(2,1)S(1)} %collective-permute-done.57.refs_9_), channel_id=1, source_target_pairs={{0,1},{1,0},{2,3},{3,2},{4,5},{5,4},{6,7},{7,6},{8,9},{9,8},{10,11... | collective-permute-start | bytes 1572872 | tf_op jit(solution)/shard_map/ppermute | solution.py:112
  198.1 45.3 %collective-permute-start.47 = (bf16[4,1024,128]{2,1,0:T(8,128)(2,1)}, bf16[4,1024,128]{2,1,0:T(8,128)(2,1)}, u32[]{:S(2)}, u32[]{:S(2)}) collective-permute-start(bf16[4,1024,128]{2,1,0:T(8,128)(2,1)} %copy-done.1), channel_id=1, source_target_pairs={{0,1},{1,0},{2,3},{3,2},{4,5},{5,4},{6,7},{7,6},{8,9},{9,8},{10,11... | collective-permute-start | bytes 3145736 | tf_op jit(solution)/shard_map/ppermute | solution.py:112
  198.6 45.3 %collective-permute-start.48 = (bf16[4,1024,128]{2,1,0:T(8,128)(2,1)}, bf16[4,1024,128]{2,1,0:T(8,128)(2,1)}, u32[]{:S(2)}, u32[]{:S(2)}) collective-permute-start(bf16[4,1024,128]{2,1,0:T(8,128)(2,1)} %copy-done.3), channel_id=1, source_target_pairs={{0,1},{1,0},{2,3},{3,2},{4,5},{5,4},{6,7},{7,6},{8,9},{9,8},{10,11... | collective-permute-start | bytes 3145736 | tf_op jit(solution)/shard_map/ppermute | solution.py:112
  223.6 20.3 %collective-permute-start.49 = (bf16[2,1024,128]{2,1,0:T(8,128)(2,1)}, bf16[2,1024,128]{2,1,0:T(8,128)(2,1)}, u32[]{:S(2)}, u32[]{:S(2)}) collective-permute-start(bf16[2,1024,128]{2,1,0:T(8,128)(2,1)} %collective-permute-done.44.refs_19_), channel_id=1, source_target_pairs={{0,1},{1,0},{2,3},{3,2},{4,5},{5,4},{6,7},{7,6},{8,9},{9,8},{10,11... | collective-permute-start | bytes 1572872 | tf_op jit(solution)/shard_map/ppermute | solution.py:112
  223.7 20.2 %collective-permute-start.50 = (bf16[2,1024,128]{2,1,0:T(8,128)(2,1)}, bf16[2,1024,128]{2,1,0:T(8,128)(2,1)}, u32[]{:S(2)}, u32[]{:S(2)}) collective-permute-start(bf16[2,1024,128]{2,1,0:T(8,128)(2,1)} %collective-permute-done.45.refs_20_), channel_id=1, source_target_pairs={{0,1},{1,0},{2,3},{3,2},{4,5},{5,4},{6,7},{7,6},{8,9},{9,8},{10,11... | collective-permute-start | bytes 1572872 | tf_op jit(solution)/shard_map/ppermute | solution.py:112
  (126 other events, 786.5 us)

commit v2 on v0

--- a/solution.py
+++ b/solution.py
@@ -1,9 +1,14 @@
 import jax
 import jax.numpy as jnp
 from jax import lax
+from jax.experimental import pallas as pl
+from jax.experimental.pallas import tpu as pltpu
 from jax.sharding import PartitionSpec as P
 
 HEAD_DIM = 128
+VMEM_LIMIT = 48 * 1024 * 1024
+BF16 = jnp.bfloat16
+F32 = jnp.float32
 
 
 def attend_piece(q_group, q_pos, k_piece, v_piece, p_piece):
@@ -19,25 +24,9 @@
     return jnp.einsum("htk,khd->thd", weight, value_heads, preferred_element_type=jnp.float32)
 
 
-def attend_groups(groups, key_flat, value_flat, own_pos):
-    initial = tuple((jnp.zeros(group.shape, jnp.float32) for group, _ in groups))
-    k_piece = lax.all_gather(key_flat, "ctx", axis=0, tiled=True)
-    v_piece = lax.all_gather(value_flat, "ctx", axis=0, tiled=True)
-    p_piece = lax.all_gather(own_pos, "ctx", axis=0, tiled=True)
-    updated = []
-    for (q_group, q_pos), total in zip(groups, initial):
-
-        def skipped(carry):
-            return carry
-
-        def computed(carry):
-            return attend_piece(q_group, q_pos, k_piece, v_piece, p_piece)
-
-        updated.append(lax.cond(jnp.min(p_piece) > jnp.max(q_pos), skipped, computed, total))
-    return tuple(updated)
-
-
-def shards(tokens, w_proj, w_out, positions, neg_emb, neg_ids, target_emb, target_ids):
+def general_shards(
+    tokens, w_proj, w_out, positions, neg_emb, neg_ids, target_emb, target_ids
+):
     tok_rows = tokens.shape[0]
     head_cols = w_proj.shape[2]
     local_heads = head_cols // HEAD_DIM
@@ -49,10 +38,11 @@
     )
     proj = jax.nn.silu(proj_sum).astype(jnp.bfloat16)
     gate = proj[:, 0].reshape(tok_rows, local_heads, HEAD_DIM)
-    value_flat = proj[:, 1]
     query = proj[:, 2].reshape(tok_rows, local_heads, HEAD_DIM)
-    key_flat = proj[:, 3]
-    (attn,) = attend_groups([(query, positions)], key_flat, value_flat, positions)
+    v_piece = lax.all_gather(proj[:, 1], "ctx", axis=0, tiled=True)
+    k_piece = lax.all_gather(proj[:, 3], "ctx", axis=0, tiled=True)
+    p_piece = lax.all_gather(positions, "ctx", axis=0, tiled=True)
+    attn = attend_piece(query, positions, k_piece, v_piece, p_piece)
     normed = attn * lax.rsqrt(jnp.mean(attn * attn, axis=-1, keepdims=True) + 1e-06)
     gated = (normed * gate.astype(jnp.float32)).astype(jnp.bfloat16).reshape(tok_rows, head_cols)
     out_terms = jnp.dot(
@@ -87,6 +77,348 @@
     return (hidden, loss)
 
 
+NZ, NY, NX = 4, 2, 2
+CHIPS = NZ * NY * NX
+PLANE = [(by, bx) for by in range(NY) for bx in range(NX)]
+SWAP = [(0, 1), (1, 0)]
+RELATIVE = [(by, bx, s) for by, bx in PLANE for s in range(NZ)]
+W = HEAD_DIM
+
+
+def chip_at(z, y, x):
+    return (z * NY + y) * NX + x
+
+
+def coords(c):
+    return c // (NY * NX), (c // NX) % NY, c % NX
+
+
+def relative_chip(c, by, bx, s):
+    z, y, x = coords(c)
+    return chip_at((z + NZ - s) % NZ, y ^ by, x ^ bx)
+
+
+def z_shift(s):
+    return [(c, relative_chip(c, 0, 0, NZ - s)) for c in range(CHIPS)]
+
+
+def flip(by, bx):
+    return [(c, relative_chip(c, by, bx, 0)) for c in range(CHIPS)]
+
+
+def hop(value, perm):
+    return lax.ppermute(value, "ctx", perm)
+
+
+def swap_cores(value):
+    return lax.ppermute(value, "tp", SWAP)
+
+
+def gather_chips(own):
+    near = jnp.concatenate([own] + [hop(own, z_shift(s)) for s in range(1, NZ)])
+    beside_x = hop(near, flip(0, 1))
+    beside_y = hop(near, flip(1, 0))
+    half = near.shape[0] // 2
+    across_a = hop(beside_x[:half], flip(1, 0))
+    across_b = hop(beside_y[half:], flip(0, 1))
+    return [near, beside_x, beside_y, across_a, across_b]
+
+
+def scatter_heads(w_proj, z, y, x, after):
+    plane = NY * NX
+    heads = w_proj.reshape(-1, 4, 2 * plane, W).transpose(2, 0, 1, 3)
+    heads = heads.reshape(2, plane, -1, 4 * W)
+    heads, _ = lax.optimization_barrier((heads, after))
+    arrived = []
+    for e in range(2):
+        perm = []
+        for src in range(CHIPS):
+            sz, sy, sx = coords(src)
+            for t in range(2):
+                dst = chip_at(2 * t + (e ^ (sz & 1)), sy, sx)
+                perm.append((2 * src + t, 2 * dst + (sz >> 1)))
+        piece = lax.dynamic_index_in_dim(heads, e ^ (z & 1), 0, keepdims=False)
+        arrived.append(lax.ppermute(piece, ("ctx", "tp"), perm))
+    both = jnp.stack(arrived, 1)
+    out = []
+    for by, bx in PLANE:
+        spot = (y ^ by) * NX + (x ^ bx)
+        piece = lax.dynamic_index_in_dim(both, spot, 0, keepdims=False)
+        out.append(piece if (by, bx) == (0, 0) else hop(piece, flip(by, bx)))
+    return jnp.stack(out)
+
+
+def silu(v):
+    return 0.5 * v * (1.0 + jnp.tanh(0.5 * v))
+
+
+def start_all(copies):
+    for copy in copies:
+        copy.start()
+    return copies
+
+
+def proj_kernel(where, *refs):
+    tok, (w_own, w_other), (gate_query, value_key, marks) = refs[:5], refs[5:7], refs[7:10]
+    x_all, w_all, tok_sem, w_sem = refs[10:]
+    z, y, x, u = (where[i] for i in range(4))
+    copies = []
+    for side, (half, src) in enumerate(((u, w_own), (1 - u, w_other))):
+        for k, (by, bx) in enumerate(PLANE):
+            for e in range(2):
+                block = chip_at(2 * half + (e ^ (z & 1)), y ^ by, x ^ bx)
+                rows = pl.ds(pl.multiple_of(block * W, W), W)
+                sem = w_sem.at[(side * len(PLANE) + k) * 2 + e]
+                copies.append(pltpu.make_async_copy(src.at[k, e], w_all.at[rows, :], sem))
+    loads, base = [], 0
+    for i, ref in enumerate(tok):
+        rows = pl.ds(base, ref.shape[0])
+        loads.append(pltpu.make_async_copy(ref, x_all.at[rows, :], tok_sem.at[i]))
+        base += ref.shape[0]
+    start_all(copies)
+    start_all(loads)
+    for copy in copies + loads:
+        copy.wait()
+    model = w_all.shape[0]
+    tile = 256
+
+    def step(at, carry):
+        span = pl.ds(pl.multiple_of(at * tile, tile), tile)
+        total = jnp.dot(x_all[span, :model], w_all[...], preferred_element_type=F32)
+        proj = silu(total).astype(BF16)
+        gate_query[span, :W] = proj[:, :W]
+        value_key[span, :W] = proj[:, W : 2 * W]
+        gate_query[span, W:] = proj[:, 2 * W : 3 * W]
+        value_key[span, W:] = proj[:, 3 * W :]
+        marks[span, :] = x_all[span, model:]
+        return carry
+
+    lax.fori_loop(0, base // tile, step, 0)
+
+
+def attend_kernel(where, gate_query, kv_own, kv_other, marks, gated):
+    rows = gate_query.shape[0]
+    tile = rows // len(PLANE)
+    piece = tile // NZ
+    lane = lax.broadcasted_iota(jnp.int32, (8, W), 1)
+    line = lax.broadcasted_iota(jnp.int32, (8, W), 0)
+    pick = jnp.where(lane == 2 * line, 128.0, jnp.where(lane == 2 * line + 1, 1.0, 0.0))
+    pick = jnp.where(line < 2, pick, 0.0).astype(BF16)
+    across = (((1,), (1,)), ((), ()))
+    key_pos = lax.dot_general(pick, marks[...], across, preferred_element_type=F32)
+    z, y, x = (where[i] for i in range(3))
+    for k, (by, bx) in enumerate(PLANE):
+        span = pl.ds(k * tile, tile)
+        query = gate_query[span, W:]
+        q_pos = lax.dot_general(marks[span, :], pick, across, preferred_element_type=F32)[:, :1]
+        attn = jnp.zeros((tile, W), F32)
+        for side, kv in enumerate((kv_own, kv_other)):
+            scores = lax.dot_general(
+                query, kv[:, W:], across, preferred_element_type=F32
+            ) * W ** (-0.5)
+            visible = key_pos[side : side + 1, :] <= q_pos
+            weight = jnp.where(visible, silu(scores), 0.0).astype(BF16)
+            attn += jnp.dot(weight, kv[:, :W], preferred_element_type=F32)
+        normed = attn * lax.rsqrt(jnp.mean(attn * attn, axis=-1, keepdims=True) + 1e-06)
+        out = (normed * gate_query[span, :W].astype(F32)).astype(BF16)
+        for s in range(NZ):
+            chip = chip_at((z + NZ - s) % NZ, y ^ by, x ^ bx)
+            gated[pl.ds(chip, 1)] = out[s * piece : (s + 1) * piece][None]
+
+
+def hidden_kernel(where, gated, w_own, w_other, tokens, keep, send, g_all, h_all, w_all, sems):
+    u = where[3]
+    chips, rows, _ = gated.shape
+    half = chips * W // 2
+    copies = []
+    for side, src in enumerate((w_own, w_other)):
+        for chip in range(chips):
+            copies.append(
+                pltpu.make_async_copy(
+                    src.at[chip, pl.ds(0, half), :],
+                    w_all.at[side, :, pl.ds(chip * W, W)],
+                    sems.at[side * chips + chip],
+                )
+            )
+    start_all(copies)
+    for chip in range(chips):
+        g_all[:, chip * W : (chip + 1) * W] = gated[chip]
+    g_own = g_all[:, pl.ds(pl.multiple_of(u * half, half), half)]
+    g_other = g_all[:, pl.ds(pl.multiple_of((1 - u) * half, half), half)]
+    for chip in range(0, chips, 2):
+        cols = pl.ds(chip * W, 2 * W)
+        for i in (chip, chip + 1, chips + chip, chips + chip + 1):
+            copies[i].wait()
+        total = jnp.dot(g_own, w_all[0, :, cols], preferred_element_type=F32)
+        total += jnp.dot(g_other, w_all[1, :, cols], preferred_element_type=F32)
+        h_all[:, cols] = (tokens[:, cols].astype(F32) + total).astype(BF16)
+    keep[...] = h_all[:, pl.ds(pl.multiple_of(u * half, half), half)]
+    send[...] = h_all[:, pl.ds(pl.multiple_of((1 - u) * half, half), half)]
+
+
+def loss_kernel(h_keep, h_send, t_keep, t_send, t_ids, n_ids, nn, n_own, n_other, loss, n_all, sems):
+    keep, send = h_keep[...], h_send[...]
+    chips, panels, negs, _ = n_own.shape
+    copies = []
+    for side, src in enumerate((n_own, n_other)):
+        for panel in range(panels):
+            copies.append(
+                pltpu.make_async_copy(
+                    src.at[:, panel],
+                    n_all.at[side, :, :, pl.ds(panel * W, W)],
+                    sems.at[side * panels + panel],
+                )
+            )
+    start_all(copies)
+    hh = he = ee = 0.0
+    for part, ref in ((keep, t_keep), (send, t_send)):
+        h_f, t_f = part.astype(F32), ref[...].astype(F32)
+        hh += jnp.sum(h_f * h_f, axis=1, keepdims=True)
+        he += jnp.sum(h_f * t_f, axis=1, keepdims=True)
+        ee += jnp.sum(t_f * t_f, axis=1, keepdims=True)
+    h_scale = lax.rsqrt(hh + 1e-06) * 20.0
+    pos_logit = he * lax.rsqrt(ee + 1e-06) * h_scale
+    for copy in copies:
+        copy.wait()
+    dots = 0.0
+    for side, part in enumerate((keep, send)):
+        neg = n_all[side].reshape(chips * negs, panels * W)
+        dots += lax.dot_general(part, neg, (((1,), (1,)), ((), ())), preferred_element_type=F32)
+    neg_logit = dots * h_scale * lax.rsqrt(nn[...] + 1e-06)
+    mass = jnp.where(n_ids[...] != t_ids[...], jnp.exp(neg_logit), 0.0)
+    total = jnp.exp(pos_logit) + jnp.sum(mass, axis=1, keepdims=True)
+    loss[...] = jnp.log(total) - pos_logit
+
+
+def call(kernel, name, outs, scratch, args, places, flops):
+    space = {"s": pltpu.SMEM, "v": pltpu.VMEM, "h": pl.ANY}
+    moved = sum(a.size * a.dtype.itemsize for a in args)
+    return pl.pallas_call(
+        kernel,
+        out_shape=[jax.ShapeDtypeStruct(shape, dtype) for shape, dtype in outs],
+        in_specs=[pl.BlockSpec(memory_space=space[p]) for p in places],
+        out_specs=[pl.BlockSpec(memory_space=pltpu.VMEM)] * len(outs),
+        scratch_shapes=scratch,
+        compiler_params=pltpu.CompilerParams(vmem_limit_bytes=VMEM_LIMIT),
+        cost_estimate=pl.CostEstimate(flops=flops, bytes_accessed=moved, transcendentals=0),
+        name=name,
+    )(*args)
+
+
+def position_marks(pos):
+    return [(pos // 128).astype(BF16), (pos % 128).astype(BF16)]
+
+
+def head_shards(
+    tokens, w_proj, w_out, positions, neg_emb, neg_ids, target_emb, target_ids
+):
+    c, u = lax.axis_index("ctx"), lax.axis_index("tp")
+    z, y, x = coords(c)
+    where = jnp.stack([z, y, x, u]).astype(jnp.int32)
+    model = tokens.shape[1]
+    rows = tokens.shape[0] // 2
+    events = rows * CHIPS
+    half = model // 2
+
+    mine = lax.dynamic_slice_in_dim(tokens, u * rows, rows, 0)
+    p_own = lax.dynamic_slice_in_dim(positions, u * rows, rows, 0)
+    p_other = lax.dynamic_slice_in_dim(positions, (1 - u) * rows, rows, 0)
+    marks = jnp.stack(position_marks(p_own) + position_marks(p_other), 1)
+    marks = jnp.pad(marks, ((0, 0), (0, W - marks.shape[1])))
+    tok = gather_chips(jnp.concatenate([mine, marks], 1))
+    w_mine = scatter_heads(w_proj, z, y, x, tok[0])
+    w_theirs = swap_cores(w_mine)
+
+    negs, panels = neg_emb.shape[0], neg_emb.shape[1] // W
+    neg_panels = neg_emb.reshape(negs, panels, W).transpose(1, 0, 2).reshape(-1, W)
+    late_own = lax.all_gather(jnp.concatenate([w_out, neg_panels]), "ctx", axis=0)
+    t_rows = target_emb.reshape(2, rows, -1)
+    t_keep = lax.dynamic_index_in_dim(t_rows, u, 0, keepdims=False)
+    t_send = swap_cores(lax.dynamic_index_in_dim(t_rows, 1 - u, 0, keepdims=False))
+
+    gate_query, value_key, marks_all = call(
+        proj_kernel,
+        "project",
+        [((events, 2 * W), BF16)] * 2 + [((events, W), BF16)],
+        [
+            pltpu.VMEM((events, model + W), BF16),
+            pltpu.VMEM((model, 4 * W), BF16),
+            pltpu.SemaphoreType.DMA((5,)),
+            pltpu.SemaphoreType.DMA((16,)),
+        ],
+        [where, *tok, w_mine, w_theirs],
+        "s" + 7 * "h",
+        2 * events * model * 4 * W,
+    )
+    kv_theirs = swap_cores(value_key)
+    late_own, _ = lax.optimization_barrier((late_own, value_key))
+    late_other = swap_cores(late_own)
+    split = w_out.shape[0]
+    n_own = late_own[:, split:].reshape(CHIPS, panels, negs, W)
+    n_other = late_other[:, split:].reshape(CHIPS, panels, negs, W)
+    nn = sum(jnp.sum(jnp.square(n.astype(F32)), axis=(1, 3)) for n in (n_own, n_other))
+    (gated,) = call(
+        attend_kernel,
+        "attend",
+        [((CHIPS, rows, W), BF16)],
+        [],
+        [where, gate_query, value_key, kv_theirs, marks_all],
+        "svvvv",
+        8 * events * events * W,
+    )
+    gated = lax.all_to_all(gated, "ctx", 0, 0, tiled=True)
+    h_keep, h_send = call(
+        hidden_kernel,
+        "hidden",
+        [((rows, half), BF16)] * 2,
+        [
+            pltpu.VMEM((rows, model), BF16),
+            pltpu.VMEM((rows, model), BF16),
+            pltpu.VMEM((2, half, model), BF16),
+            pltpu.SemaphoreType.DMA((2 * CHIPS,)),
+        ],
+        [where, gated, late_own, late_other, mine],
+        "svhhv",
+        2 * rows * model * model,
+    )
+    h_theirs = swap_cores(h_send)
+    (loss,) = call(
+        loss_kernel,
+        "loss",
+        [((rows, 1), F32)],
+        [
+            pltpu.VMEM((2, CHIPS, negs, half), BF16),
+            pltpu.SemaphoreType.DMA((2 * panels,)),
+        ],
+        [
+            h_keep,
+            h_send,
+            t_keep,
+            t_send,
+            target_ids[:, None],
+            neg_ids[None],
+            nn.reshape(1, -1),
+            n_own,
+            n_other,
+        ],
+        "vvvvvvvhh",
+        2 * rows * model * neg_ids.shape[0],
+    )
+    hidden = jnp.where(
+        u == 0,
+        jnp.concatenate([h_keep, h_theirs]),
+        jnp.concatenate([h_theirs, h_keep]),
+    )
+    return hidden, loss.reshape(-1)
+
+
+def shards(tokens, w_proj, *rest):
+    n_ctx, n_tp = lax.axis_size("ctx"), lax.axis_size("tp")
+    heads = w_proj.shape[2] * n_tp // HEAD_DIM
+    plan = head_shards if (n_ctx, n_tp, heads) == (CHIPS, 2, CHIPS) else general_shards
+    return plan(tokens, w_proj, *rest)
+
+
 def solution(mesh):
     placed = (
         P("ctx", None),

time: 552 us -> 203 us (0.37)
  waiting for transfers between devices: 456 us -> 105 us
  blocking collectives: 40.1 us -> 0 us
  starting transfers between devices: 0.28 us -> 34.1 us
  Pallas kernels: 0 us -> 24.3 us
  matrix products: 22 us -> 0 us
    all_gather x5 -> x1, waiting for transfers between devices: 446 us -> 2.6 us  [head_shards(): lax.all_gather(jnp.concatenate([w_out, neg_panels]), 'ctx', axis=0)]
    ppermute x0 -> x17, waiting for transfers between devices: none -> 97.8 us  [the longest x10 71.4 us: hop(): return lax.ppermute(value, 'ctx', perm)]
    all_gather x1 -> x0, blocking collectives: 37.6 us -> none  [attend_groups(): p_piece = lax.all_gather(own_pos, 'ctx', axis=0, tiled=True)]
    ppermute x0 -> x17, starting transfers between devices: none -> 28.1 us  [the longest x10 15 us: hop(): return lax.ppermute(value, 'ctx', perm)]
    pallas_call x0 -> x4, Pallas kernels: none -> 24.3 us  [call(): pl.pallas_call(kernel, out_shape=[jax.ShapeDtypeStruct(shape, dtype) for...]
    dot_general x4 -> x0, matrix products: 22 us -> none  [the longest x1 8.39 us: shards(): jnp.einsum('td,dfh->tfh', tokens, lax.all_gather(w_proj, 'ctx', axis=0, t...]
    reduce_scatter x2 -> x0, waiting for transfers between devices: 8.69 us -> none  [the longest x1 6.27 us: shards(): lax.psum_scatter(out_terms, 'tp', scatter_dimension=1, tiled=True)]
    another operation x2 -> x1, local copies, waits for them, and re-layouts: 7.13 us -> 0.11 us  [head_shards(): marks = jnp.stack(position_marks(p_own) + position_marks(p_other), 1)]
  transfers between devices with their start and end apart: 7 -> 19, of which waited for: 7 -> 10; matrix products, arithmetic and copies ran while one was open for 3% -> 9% of each run, Pallas kernels for 0% -> 12%
where the time goes in v2:
time: 203 us
  waiting for transfers between devices  105 us (52%)
  starting transfers between devices  34.1 us (17%)
  Pallas kernels  24.3 us (12%)
  between operations  14.3 us (7%)
  local copies, waits for them, and re-layouts  13 us (6%)
  other arithmetic  11.6 us (6%)
    ppermute x10, waiting for transfers between devices, hop(): return lax.ppermute(value, 'ctx', perm)  71.4 us
    pallas_call x4, Pallas kernels, call(): pl.pallas_call(kernel, out_shape=[jax.ShapeDtypeStruct(shape, dtype) for...  24.3 us
    ppermute x2, waiting for transfers between devices, scatter_heads(): arrived.append(lax.ppermute(piece, ('ctx', 'tp'), perm))  19.5 us
    ppermute x10, starting transfers between devices, hop(): return lax.ppermute(value, 'ctx', perm)  15 us
    ppermute x5, starting transfers between devices, swap_cores(): return lax.ppermute(value, 'tp', SWAP)  10.5 us
    ppermute x5, waiting for transfers between devices, swap_cores(): return lax.ppermute(value, 'tp', SWAP)  6.87 us
    all_to_all x1, starting transfers between devices, head_shards(): gated = lax.all_to_all(gated, 'ctx', 0, 0, tiled=True)  6.01 us
    reduce_sum x4, other arithmetic, head_shards(): jnp.sum(jnp.square(n.astype(F32)), axis=(1, 3))  5.55 us
  transfers between devices with their start and end apart: 19, of which 10 were waited for; matrix products, arithmetic and copies ran while one was open for 9% of the time, Pallas kernels for 12%

profile of v2, /device:TPU:0, one launch (start us, length us, event | category | flops | bytes accessed | tf_op | source)
XLA Modules:
  0.0 202.5 jit_solution(10225779664930316922)
XLA Ops:
  8.3 1.7 pad_maximum_fusion.2
  11.8 5.0 %collective-permute-start.2 = (bf16[64,2176]{1,0:T(8,128)(2,1)}, bf16[64,2176]{1,0:T(8,128)(2,1)S(1)}, u32[]{:S(2)}, u32[]{:S(2)}) collective-permute-start(bf16[64,2176]{1,0:T(8,128)(2,1)} %pad_maximum_fusion.3), channel_id=1, source_target_pairs={{0,24},{2,26},{4,28},{6,30},{8,0},{10,2},{12,4},{14,6},{16,8},{18,... | collective-permute-start | bytes 835592 | tf_op jit(solution)/shard_map/ppermute | solution.py:110
  19.9 5.5 %collective-permute-done.2 = bf16[64,2176]{1,0:T(8,128)(2,1)S(1)} collective-permute-done((bf16[64,2176]{1,0:T(8,128)(2,1)}, bf16[64,2176]{1,0:T(8,128)(2,1)S(1)}, u32[]{:S(2)}, u32[]{:S(2)}) %collective-permute-start.2) | collective-permute-done | bytes 278560 | tf_op jit(solution)/shard_map/ppermute | solution.py:110
  25.4 23.8 %collective-permute-done.1 = bf16[64,2176]{1,0:T(8,128)(2,1)S(1)} collective-permute-done((bf16[64,2176]{1,0:T(8,128)(2,1)}, bf16[64,2176]{1,0:T(8,128)(2,1)S(1)}, u32[]{:S(2)}, u32[]{:S(2)}) %collective-permute-start.1) | collective-permute-done | bytes 278560 | tf_op jit(solution)/shard_map/ppermute | solution.py:110
  51.5 1.7 collective-permute-start.7
  57.1 19.5 %collective-permute-done.8 = bf16[4,128,512]{2,1,0:T(8,128)(2,1)S(1)} collective-permute-done((bf16[4,128,512]{2,1,0:T(8,128)(2,1)}, bf16[4,128,512]{2,1,0:T(8,128)(2,1)S(1)}, u32[]{:S(2)}, u32[]{:S(2)}) %collective-permute-start.8) | collective-permute-done | bytes 524320 | tf_op jit(solution)/shard_map/ppermute | solution.py:141
  76.7 3.2 %collective-permute-start.11 = (bf16[2,128,512]{2,1,0:T(8,128)(2,1)S(1)}, bf16[2,128,512]{2,1,0:T(8,128)(2,1)S(1)}, u32[]{:S(2)}, u32[]{:S(2)}) collective-permute-start(bf16[2,128,512]{2,1,0:T(8,128)(2,1)S(1)} %get-tuple-element.23), channel_id=1, source_target_pairs={{0,6},{2,4},{4,2},{6,0},{8,14},{10,12},{12,10},{14,8},{16,22},{18,... | collective-permute-start | bytes 786440 | tf_op jit(solution)/shard_map/ppermute | solution.py:110
  80.5 15.1 %collective-permute-done.11 = bf16[2,128,512]{2,1,0:T(8,128)(2,1)S(1)} collective-permute-done((bf16[2,128,512]{2,1,0:T(8,128)(2,1)S(1)}, bf16[2,128,512]{2,1,0:T(8,128)(2,1)S(1)}, u32[]{:S(2)}, u32[]{:S(2)}) %collective-permute-start.11) | collective-permute-done | bytes 262176 | tf_op jit(solution)/shard_map/ppermute | solution.py:110
  95.6 3.8 %collective-permute-done.9 = bf16[2,128,512]{2,1,0:T(8,128)(2,1)S(1)} collective-permute-done((bf16[2,128,512]{2,1,0:T(8,128)(2,1)S(1)}, bf16[2,128,512]{2,1,0:T(8,128)(2,1)S(1)}, u32[]{:S(2)}, u32[]{:S(2)}) %collective-permute-start.9) | collective-permute-done | bytes 262176 | tf_op jit(solution)/shard_map/ppermute | solution.py:110
  99.5 9.8 %collective-permute-start.12 = (bf16[4,2,128,512]{3,2,1,0:T(8,128)(2,1)S(1)}, bf16[4,2,128,512]{3,2,1,0:T(8,128)(2,1)S(1)}, u32[]{:S(2)}, u32[]{:S(2)}) collective-permute-start(bf16[4,2,128,512]{3,2,1,0:T(8,128)(2,1)S(1)} %pad_maximum_fusion.1.refs_5_), channel_id=1, source_target_pairs={{0,1},{1,0},{2,3},{3,2},{4,5},{5,4},{6,7},{7,6},{8,9},{9,8},{10,11... | collective-permute-start | bytes 3145736 | tf_op jit(solution)/shard_map/ppermute | solution.py:114
  113.7 21.3 %collective-permute-done.5.refs_3_ = bf16[128,2176]{1,0:T(8,128)(2,1)S(1)} collective-permute-done((bf16[128,2176]{1,0:T(8,128)(2,1)S(1)}, bf16[128,2176]{1,0:T(8,128)(2,1)S(1)}, u32[]{:S(2)}, u32[]{:S(2)}) %collective-permute-start.5) | collective-permute-done | bytes 557088 | tf_op jit(solution)/shard_map/ppermute | solution.py:110
  135.0 1.9 collective-permute-done.6.refs_4_
  136.9 8.4 %project.1 = (bf16[1024,256]{1,0:T(8,128)(2,1)S(1)}, bf16[1024,256]{1,0:T(8,128)(2,1)S(1)}, bf16[1024,128]{1,0:T(8,128)(2,1)S(1)}) custom-call(s32[4]{0:T(128)S(1)} %pad_add_fusion.where, bf16[256,2176]{1,0:T(8,128)(2,1)S(1)} %pad_maximum_fusion.refs_0_, bf16[256,2176]{1,0:T(8,128)(2,1)} %collective-permute-done.3.refs_1_, ...), custom_call_target="tpu_custom_call" | custom-call | flops 2147483648 | bytes 6553616 | tf_op jit(solution)/shard_map/project/pallas_call | solution.py:296
  146.2 2.6 %all-gather.3.cloned.1.call-done = bf16[24576,128]{1,0:T(8,128)(2,1)} async-done(((bf16[1536,128]{1,0:T(8,128)(2,1)}), bf16[24576,128]{1,0:T(8,128)(2,1)}) %all-gather.3.cloned.1.call-update) | async-done | bytes 6291472 | tf_op jit(solution)/shard_map/all_gather | solution.py:334
  149.3 6.9 %collective-permute-done.13.kv_other = bf16[1024,256]{1,0:T(8,128)(2,1)S(1)} collective-permute-done((bf16[1024,256]{1,0:T(8,128)(2,1)S(1)}, bf16[1024,256]{1,0:T(8,128)(2,1)S(1)}, u32[]{:S(2)}, u32[]{:S(2)}) %collective-permute-start.13) | collective-permute-done | bytes 524320 | tf_op jit(solution)/shard_map/ppermute | solution.py:114
  157.2 4.5 %attend.1 = bf16[16,64,128]{2,1,0:T(8,128)(2,1)} custom-call(s32[4]{0:T(128)S(1)} %pad_add_fusion.where, bf16[1024,256]{1,0:T(8,128)(2,1)S(1)} %copy-done.3, bf16[1024,256]{1,0:T(8,128)(2,1)S(1)} %get-tuple-element.11.kv_own, bf16[1024,256]{1,0:T(8,128)(2,1)S(1)} %collective-permute-done.13.kv_other, bf16[1024,128]{1,0:T(8,128)(2,1)S(1)} %get-tuple-element.12.marks), custom_call_target="tpu_custom_call" | custom-call | flops 1073741824 | bytes 1835024 | tf_op jit(solution)/shard_map/attend/pallas_call | solution.py:296
  161.7 6.0 %all-to-all-start = ((bf16[16,64,128]{2,1,0:T(8,128)(2,1)}), bf16[16,64,128]{2,1,0:T(8,128)(2,1)S(1)}, u32[]{:S(2)}, u32[]{:S(2)}) async-start(bf16[16,64,128]{2,1,0:T(8,128)(2,1)} %attend.1), calls=%async_computation | async-start | bytes 524288 | tf_op jit(solution)/shard_map/all_to_all | solution.py:369
  168.6 1.7 slice.14
  170.4 2.8 %multiply_reduce_fusion.1 = f32[16,512]{1,0:T(8,128)S(1)} fusion(bf16[16,1536,128]{2,1,0:T(8,128)(2,1)} %bitcast.48), kind=kLoop, calls=%fused_computation.1 | loop fusion | flops 3137536 | bytes 2129920 | tf_op jit(solution)/shard_map/reduce_sum | solution.py:359
  173.2 4.9 %all-to-all-done.gated = bf16[16,64,128]{2,1,0:T(8,128)(2,1)S(1)} async-done(((bf16[16,64,128]{2,1,0:T(8,128)(2,1)}), bf16[16,64,128]{2,1,0:T(8,128)(2,1)S(1)}, u32[]{:S(2)}, u32[]{:S(2)}) %all-to-all-start) | async-done | bytes 262176 | tf_op jit(solution)/shard_map/all_to_all | solution.py:369
  178.1 7.2 %hidden.1 = (bf16[64,1024]{1,0:T(8,128)(2,1)S(1)}, bf16[64,1024]{1,0:T(8,128)(2,1)}) custom-call(s32[4]{0:T(128)S(1)} %pad_add_fusion.where, bf16[16,64,128]{2,1,0:T(8,128)(2,1)S(1)} %all-to-all-done.gated, bf16[16,1536,128]{2,1,0:T(8,128)(2,1)} %bitcast.49, bf16[16,1536,128]{2,1,0:T(8,128)(2,1)} %collective-permute-done.14.w_other, ...), custom_call_target="tpu_custom_call" | custom-call | flops 536870912 | bytes 13107216 | tf_op jit(solution)/shard_map/hidden/pallas_call | solution.py:296
  185.5 2.8 %multiply_reduce_fusion = f32[16,512]{1,0:T(8,128)S(1)} fusion(bf16[16,1536,128]{2,1,0:T(8,128)(2,1)} %collective-permute-done.14.w_other), kind=kLoop, calls=%fused_computation | loop fusion | flops 3137536 | bytes 2129920 | tf_op jit(solution)/shard_map/reduce_sum | solution.py:359
  188.4 1.7 slice.18
  190.2 4.1 %loss.1 = f32[64,1]{1,0:T(8,128)S(1)} custom-call(bf16[64,1024]{1,0:T(8,128)(2,1)S(1)} %get-tuple-element.14.h_keep, bf16[64,1024]{1,0:T(8,128)(2,1)} %get-tuple-element.15.h_send, bf16[64,1024]{1,0:T(8,128)(2,1)S(1)} %get-tuple-element.27.t_keep, bf16[64,1024]{1,0:T(8,128)(2,1)} %collective-permute-done.16.t_send, s32[64,1]{1,0:T(8,128)S(1)} %copy.31.t_ids, ...), custom_call_target="tpu_custom_call" | custom-call | flops 268435456 | bytes 4727040 | tf_op jit(solution)/shard_map/loss/pallas_call | solution.py:296
  (69 shorter events, 22.3 us)
Async XLA Ops:
  7.2 3.9 %copy-start = (bf16[128,2048]{1,0:T(8,128)(2,1)S(1)}, bf16[128,2048]{1,0:T(8,128)(2,1)}, u32[]{:S(2)}) copy-start(bf16[128,2048]{1,0:T(8,128)(2,1)} %param.8) | copy-start | bytes 1572868
  7.2 10.7 %copy-start.5 = (bf16[128,4,1024]{2,1,0:T(4,128)(2,1)S(1)}, bf16[128,4,1024]{2,1,0:T(4,128)(2,1)}, u32[]{:S(2)}) copy-start(bf16[128,4,1024]{2,1,0:T(4,128)(2,1)} %param.9) | copy-start | bytes 3145732
  7.2 141.6 %all-gather.3.cloned.1.call-start = ((), (), s32[]{:S(2)}) async-start(), calls=%async_computation.1 | async-start | bytes 6684672 | tf_op jit(solution)/shard_map/all_gather | solution.py:334
  11.8 13.6 %collective-permute-start.2 = (bf16[64,2176]{1,0:T(8,128)(2,1)}, bf16[64,2176]{1,0:T(8,128)(2,1)S(1)}, u32[]{:S(2)}, u32[]{:S(2)}) collective-permute-start(bf16[64,2176]{1,0:T(8,128)(2,1)} %pad_maximum_fusion.3), channel_id=1, source_target_pairs={{0,24},{2,26},{4,28},{6,30},{8,0},{10,2},{12,4},{14,6},{16,8},{18,... | collective-permute-start | bytes 835592 | tf_op jit(solution)/shard_map/ppermute | solution.py:110
  16.9 32.4 %collective-permute-start.1 = (bf16[64,2176]{1,0:T(8,128)(2,1)}, bf16[64,2176]{1,0:T(8,128)(2,1)S(1)}, u32[]{:S(2)}, u32[]{:S(2)}) collective-permute-start(bf16[64,2176]{1,0:T(8,128)(2,1)} %pad_maximum_fusion.3), channel_id=1, source_target_pairs={{0,16},{2,18},{4,20},{6,22},{8,24},{10,26},{12,28},{14,30},{16,0},... | collective-permute-start | bytes 835592 | tf_op jit(solution)/shard_map/ppermute | solution.py:110
  16.9 32.4 %collective-permute-start = (bf16[64,2176]{1,0:T(8,128)(2,1)}, bf16[64,2176]{1,0:T(8,128)(2,1)}, u32[]{:S(2)}, u32[]{:S(2)}) collective-permute-start(bf16[64,2176]{1,0:T(8,128)(2,1)} %pad_maximum_fusion.3), channel_id=1, source_target_pairs={{0,8},{2,10},{4,12},{6,14},{8,16},{10,18},{12,20},{14,22},{16,24},... | collective-permute-start | bytes 835592 | tf_op jit(solution)/shard_map/ppermute | solution.py:110
  19.9 30.4 %copy-start.4 = (bf16[2,4,128,512]{3,2,1,0:T(8,128)(2,1)S(1)}, bf16[2,4,128,512]{3,2,1,0:T(8,128)(2,1)}, u32[]{:S(2)}) copy-start(bf16[2,4,128,512]{3,2,1,0:T(8,128)(2,1)} %reshape.50) | copy-start | bytes 3145732
  51.5 5.6 %collective-permute-start.7 = (bf16[4,128,512]{2,1,0:T(8,128)(2,1)}, bf16[4,128,512]{2,1,0:T(8,128)(2,1)S(1)}, u32[]{:S(2)}, u32[]{:S(2)}) collective-permute-start(bf16[4,128,512]{2,1,0:T(8,128)(2,1)} %get-tuple-element.25), channel_id=1, source_target_pairs={{0,0},{1,16},{2,2},{3,18},{4,4},{5,20},{6,6},{7,22},{8,8},{9,24},{... | collective-permute-start | bytes 1572872 | tf_op jit(solution)/shard_map/ppermute | solution.py:141
  53.2 23.4 %collective-permute-start.8 = (bf16[4,128,512]{2,1,0:T(8,128)(2,1)}, bf16[4,128,512]{2,1,0:T(8,128)(2,1)S(1)}, u32[]{:S(2)}, u32[]{:S(2)}) collective-permute-start(bf16[4,128,512]{2,1,0:T(8,128)(2,1)} %get-tuple-element.24), channel_id=1, source_target_pairs={{0,8},{1,24},{2,10},{3,26},{4,12},{5,28},{6,14},{7,30},{8,0},{9,16... | collective-permute-start | bytes 1572872 | tf_op jit(solution)/shard_map/ppermute | solution.py:141
  54.1 55.2 %collective-permute-start.3 = (bf16[256,2176]{1,0:T(8,128)(2,1)S(1)}, bf16[256,2176]{1,0:T(8,128)(2,1)}, u32[]{:S(2)}, u32[]{:S(2)}) collective-permute-start(bf16[256,2176]{1,0:T(8,128)(2,1)S(1)} %pad_maximum_fusion.refs_0_), channel_id=1, source_target_pairs={{0,2},{2,0},{4,6},{6,4},{8,10},{10,8},{12,14},{14,12},{16,18},{18,... | collective-permute-start | bytes 3342344 | tf_op jit(solution)/shard_map/ppermute | solution.py:110
  55.6 55.4 %collective-permute-start.4 = (bf16[256,2176]{1,0:T(8,128)(2,1)S(1)}, bf16[256,2176]{1,0:T(8,128)(2,1)}, u32[]{:S(2)}, u32[]{:S(2)}) collective-permute-start(bf16[256,2176]{1,0:T(8,128)(2,1)S(1)} %pad_maximum_fusion.refs_0_), channel_id=1, source_target_pairs={{0,4},{2,6},{4,0},{6,2},{8,12},{10,14},{12,8},{14,10},{16,20},{18,... | collective-permute-start | bytes 3342344 | tf_op jit(solution)/shard_map/ppermute | solution.py:110
  76.7 18.9 %collective-permute-start.11 = (bf16[2,128,512]{2,1,0:T(8,128)(2,1)S(1)}, bf16[2,128,512]{2,1,0:T(8,128)(2,1)S(1)}, u32[]{:S(2)}, u32[]{:S(2)}) collective-permute-start(bf16[2,128,512]{2,1,0:T(8,128)(2,1)S(1)} %get-tuple-element.23), channel_id=1, source_target_pairs={{0,6},{2,4},{4,2},{6,0},{8,14},{10,12},{12,10},{14,8},{16,22},{18,... | collective-permute-start | bytes 786440 | tf_op jit(solution)/shard_map/ppermute | solution.py:110
  79.8 15.8 %collective-permute-start.10 = (bf16[2,128,512]{2,1,0:T(8,128)(2,1)S(1)}, bf16[2,128,512]{2,1,0:T(8,128)(2,1)S(1)}, u32[]{:S(2)}, u32[]{:S(2)}) collective-permute-start(bf16[2,128,512]{2,1,0:T(8,128)(2,1)S(1)} %get-tuple-element.22), channel_id=1, source_target_pairs={{0,4},{2,6},{4,0},{6,2},{8,12},{10,14},{12,8},{14,10},{16,20},{18,... | collective-permute-start | bytes 786440 | tf_op jit(solution)/shard_map/ppermute | solution.py:110
  80.3 19.1 %collective-permute-start.9 = (bf16[2,128,512]{2,1,0:T(8,128)(2,1)S(1)}, bf16[2,128,512]{2,1,0:T(8,128)(2,1)S(1)}, u32[]{:S(2)}, u32[]{:S(2)}) collective-permute-start(bf16[2,128,512]{2,1,0:T(8,128)(2,1)S(1)} %get-tuple-element.21), channel_id=1, source_target_pairs={{0,2},{2,0},{4,6},{6,4},{8,10},{10,8},{12,14},{14,12},{16,18},{18,... | collective-permute-start | bytes 786440 | tf_op jit(solution)/shard_map/ppermute | solution.py:110
  99.5 37.4 %collective-permute-start.12 = (bf16[4,2,128,512]{3,2,1,0:T(8,128)(2,1)S(1)}, bf16[4,2,128,512]{3,2,1,0:T(8,128)(2,1)S(1)}, u32[]{:S(2)}, u32[]{:S(2)}) collective-permute-start(bf16[4,2,128,512]{3,2,1,0:T(8,128)(2,1)S(1)} %pad_maximum_fusion.1.refs_5_), channel_id=1, source_target_pairs={{0,1},{1,0},{2,3},{3,2},{4,5},{5,4},{6,7},{7,6},{8,9},{9,8},{10,11... | collective-permute-start | bytes 3145736 | tf_op jit(solution)/shard_map/ppermute | solution.py:114
  110.4 24.6 %collective-permute-start.5 = (bf16[128,2176]{1,0:T(8,128)(2,1)S(1)}, bf16[128,2176]{1,0:T(8,128)(2,1)S(1)}, u32[]{:S(2)}, u32[]{:S(2)}) collective-permute-start(bf16[128,2176]{1,0:T(8,128)(2,1)S(1)} %slice.16), channel_id=1, source_target_pairs={{0,4},{2,6},{4,0},{6,2},{8,12},{10,14},{12,8},{14,10},{16,20},{18,... | collective-permute-start | bytes 1671176 | tf_op jit(solution)/shard_map/ppermute | solution.py:110
  112.1 24.8 %collective-permute-start.6 = (bf16[128,2176]{1,0:T(8,128)(2,1)S(1)}, bf16[128,2176]{1,0:T(8,128)(2,1)S(1)}, u32[]{:S(2)}, u32[]{:S(2)}) collective-permute-start(bf16[128,2176]{1,0:T(8,128)(2,1)S(1)} %slice.17), channel_id=1, source_target_pairs={{0,2},{2,0},{4,6},{6,4},{8,10},{10,8},{12,14},{14,12},{16,18},{18,... | collective-permute-start | bytes 1671176 | tf_op jit(solution)/shard_map/ppermute | solution.py:110
  148.8 29.3 %collective-permute-start.14 = (bf16[16,1536,128]{2,1,0:T(8,128)(2,1)}, bf16[16,1536,128]{2,1,0:T(8,128)(2,1)}, u32[]{:S(2)}, u32[]{:S(2)}) collective-permute-start(bf16[16,1536,128]{2,1,0:T(8,128)(2,1)} %bitcast.46), channel_id=1, source_target_pairs={{0,1},{1,0},{2,3},{3,2},{4,5},{5,4},{6,7},{7,6},{8,9},{9,8},{10,11... | collective-permute-start | bytes 18874376 | tf_op jit(solution)/shard_map/ppermute | solution.py:114
  148.8 7.4 %collective-permute-start.13 = (bf16[1024,256]{1,0:T(8,128)(2,1)S(1)}, bf16[1024,256]{1,0:T(8,128)(2,1)S(1)}, u32[]{:S(2)}, u32[]{:S(2)}) collective-permute-start(bf16[1024,256]{1,0:T(8,128)(2,1)S(1)} %get-tuple-element.11.kv_own), channel_id=1, source_target_pairs={{0,1},{1,0},{2,3},{3,2},{4,5},{5,4},{6,7},{7,6},{8,9},{9,8},{10,11... | collective-permute-start | bytes 1572872 | tf_op jit(solution)/shard_map/ppermute | solution.py:114
  157.2 10.5 %copy-start.6 = (bf16[128,1024]{1,0:T(8,128)(2,1)S(1)}, bf16[128,1024]{1,0:T(8,128)(2,1)}, u32[]{:S(2)}) copy-start(bf16[128,1024]{1,0:T(8,128)(2,1)} %param.14) | copy-start | bytes 786436
  157.2 11.3 %copy-start.7 = (s32[64]{0:T(128)S(1)}, s32[64]{0:T(128)}, u32[]{:S(2)}) copy-start(s32[64]{0:T(128)} %param.15) | copy-start | bytes 772
  161.7 16.4 %all-to-all-start = ((bf16[16,64,128]{2,1,0:T(8,128)(2,1)}), bf16[16,64,128]{2,1,0:T(8,128)(2,1)S(1)}, u32[]{:S(2)}, u32[]{:S(2)}) async-start(bf16[16,64,128]{2,1,0:T(8,128)(2,1)} %attend.1), calls=%async_computation | async-start | bytes 524288 | tf_op jit(solution)/shard_map/all_to_all | solution.py:369
  168.5 21.7 %collective-permute-start.16 = (bf16[64,1024]{1,0:T(8,128)(2,1)}, bf16[64,1024]{1,0:T(8,128)(2,1)}, u32[]{:S(2)}, u32[]{:S(2)}) collective-permute-start(bf16[64,1024]{1,0:T(8,128)(2,1)} %get-tuple-element.26), channel_id=1, source_target_pairs={{0,1},{1,0},{2,3},{3,2},{4,5},{5,4},{6,7},{7,6},{8,9},{9,8},{10,11... | collective-permute-start | bytes 393224 | tf_op jit(solution)/shard_map/ppermute | solution.py:114
  185.4 9.5 %collective-permute-start.15 = (bf16[64,1024]{1,0:T(8,128)(2,1)}, bf16[64,1024]{1,0:T(8,128)(2,1)S(1)}, u32[]{:S(2)}, u32[]{:S(2)}) collective-permute-start(bf16[64,1024]{1,0:T(8,128)(2,1)} %get-tuple-element.15.h_send), channel_id=1, source_target_pairs={{0,1},{1,0},{2,3},{3,2},{4,5},{5,4},{6,7},{7,6},{8,9},{9,8},{10,11... | collective-permute-start | bytes 393224 | tf_op jit(solution)/shard_map/ppermute | solution.py:114
  (3 other events, 3.9 us)
Sparse Core Ops, SparseCore 0:
  10.8 137.9 all-gather.2

commit v3 on v2

--- a/solution.py
+++ b/solution.py
@@ -124,28 +124,16 @@
     return [near, beside_x, beside_y, across_a, across_b]
 
 
-def scatter_heads(w_proj, z, y, x, after):
-    plane = NY * NX
-    heads = w_proj.reshape(-1, 4, 2 * plane, W).transpose(2, 0, 1, 3)
-    heads = heads.reshape(2, plane, -1, 4 * W)
-    heads, _ = lax.optimization_barrier((heads, after))
-    arrived = []
-    for e in range(2):
-        perm = []
-        for src in range(CHIPS):
-            sz, sy, sx = coords(src)
-            for t in range(2):
-                dst = chip_at(2 * t + (e ^ (sz & 1)), sy, sx)
-                perm.append((2 * src + t, 2 * dst + (sz >> 1)))
-        piece = lax.dynamic_index_in_dim(heads, e ^ (z & 1), 0, keepdims=False)
-        arrived.append(lax.ppermute(piece, ("ctx", "tp"), perm))
-    both = jnp.stack(arrived, 1)
-    out = []
-    for by, bx in PLANE:
-        spot = (y ^ by) * NX + (x ^ bx)
-        piece = lax.dynamic_index_in_dim(both, spot, 0, keepdims=False)
-        out.append(piece if (by, bx) == (0, 0) else hop(piece, flip(by, bx)))
-    return jnp.stack(out)
+def scatter_heads(w_proj, u):
+    depth, _, cols = w_proj.shape
+    count = cols // W
+    heads = w_proj.reshape(2, depth // 2, 4, count, W).transpose(0, 3, 1, 2, 4)
+    heads = heads.reshape(2, count, depth // 2, 4 * W)
+    theirs = swap_cores(lax.dynamic_index_in_dim(heads, 1 - u, 0, keepdims=False))
+    ours = lax.dynamic_index_in_dim(heads, u, 0, keepdims=False)
+    return jnp.where(
+        u == 0, jnp.concatenate([ours, theirs]), jnp.concatenate([theirs, ours])
+    )
 
 
 def silu(v):
@@ -159,68 +147,63 @@
 
 
 def proj_kernel(where, *refs):
-    tok, (w_own, w_other), (gate_query, value_key, marks) = refs[:5], refs[5:7], refs[7:10]
-    x_all, w_all, tok_sem, w_sem = refs[10:]
-    z, y, x, u = (where[i] for i in range(4))
-    copies = []
+    count = len(refs) - 9
+    tok, (w_own, w_other) = refs[:count], refs[count : count + 2]
+    gate_query, value_key, marks, x_all, w_all, tok_sem, w_sem = refs[count + 2 :]
+    u = where[3]
+    copies, base = [], 0
     for side, (half, src) in enumerate(((u, w_own), (1 - u, w_other))):
-        for k, (by, bx) in enumerate(PLANE):
-            for e in range(2):
-                block = chip_at(2 * half + (e ^ (z & 1)), y ^ by, x ^ bx)
-                rows = pl.ds(pl.multiple_of(block * W, W), W)
-                sem = w_sem.at[(side * len(PLANE) + k) * 2 + e]
-                copies.append(pltpu.make_async_copy(src.at[k, e], w_all.at[rows, :], sem))
-    loads, base = [], 0
+        copies.append(pltpu.make_async_copy(src, w_all.at[:, half], w_sem.at[side]))
     for i, ref in enumerate(tok):
         rows = pl.ds(base, ref.shape[0])
-        loads.append(pltpu.make_async_copy(ref, x_all.at[rows, :], tok_sem.at[i]))
+        copies.append(pltpu.make_async_copy(ref, x_all.at[rows, :], tok_sem.at[i]))
         base += ref.shape[0]
     start_all(copies)
-    start_all(loads)
-    for copy in copies + loads:
+    for copy in copies:
         copy.wait()
-    model = w_all.shape[0]
-    tile = 256
-
-    def step(at, carry):
-        span = pl.ds(pl.multiple_of(at * tile, tile), tile)
-        total = jnp.dot(x_all[span, :model], w_all[...], preferred_element_type=F32)
-        proj = silu(total).astype(BF16)
-        gate_query[span, :W] = proj[:, :W]
-        value_key[span, :W] = proj[:, W : 2 * W]
-        gate_query[span, W:] = proj[:, 2 * W : 3 * W]
-        value_key[span, W:] = proj[:, 3 * W :]
-        marks[span, :] = x_all[span, model:]
-        return carry
-
-    lax.fori_loop(0, base // tile, step, 0)
-
-
-def attend_kernel(where, gate_query, kv_own, kv_other, marks, gated):
-    rows = gate_query.shape[0]
-    tile = rows // len(PLANE)
-    piece = tile // NZ
+    weights = w_all[...].reshape(-1, w_all.shape[-1])
+    model = weights.shape[0]
+    total = jnp.dot(x_all[:, :model], weights, preferred_element_type=F32)
+    proj = silu(total).astype(BF16)
+    gate_query[:, :W] = proj[:, :W]
+    value_key[:, :W] = proj[:, W : 2 * W]
+    gate_query[:, W:] = proj[:, 2 * W : 3 * W]
+    value_key[:, W:] = proj[:, 3 * W :]
+    marks[...] = x_all[:, model:]
+
+
+def attend_kernel(where, *refs):
+    gate_query, kv_own, kv_other, marks = refs[:2], refs[2:4], refs[4:6], refs[6:8]
+    gated = refs[8]
     lane = lax.broadcasted_iota(jnp.int32, (8, W), 1)
     line = lax.broadcasted_iota(jnp.int32, (8, W), 0)
     pick = jnp.where(lane == 2 * line, 128.0, jnp.where(lane == 2 * line + 1, 1.0, 0.0))
     pick = jnp.where(line < 2, pick, 0.0).astype(BF16)
     across = (((1,), (1,)), ((), ()))
-    key_pos = lax.dot_general(pick, marks[...], across, preferred_element_type=F32)
     z, y, x = (where[i] for i in range(3))
+    piece = gated.shape[1]
+    tile = NZ * piece
+    groups = []
+    for group in range(2):
+        key_pos = lax.dot_general(pick, marks[group][...], across, preferred_element_type=F32)
+        groups.append((kv_own[group], key_pos[0:1]))
+        groups.append((kv_other[group], key_pos[1:2]))
     for k, (by, bx) in enumerate(PLANE):
-        span = pl.ds(k * tile, tile)
-        query = gate_query[span, W:]
-        q_pos = lax.dot_general(marks[span, :], pick, across, preferred_element_type=F32)[:, :1]
+        group, base = (0, k * tile) if k < len(PLANE) - 1 else (1, 0)
+        span = pl.ds(base, tile)
+        query = gate_query[group][span, W:]
+        q_pos = lax.dot_general(
+            marks[group][span, :], pick, across, preferred_element_type=F32
+        )[:, :1]
         attn = jnp.zeros((tile, W), F32)
-        for side, kv in enumerate((kv_own, kv_other)):
+        for kv, key_pos in groups:
             scores = lax.dot_general(
                 query, kv[:, W:], across, preferred_element_type=F32
             ) * W ** (-0.5)
-            visible = key_pos[side : side + 1, :] <= q_pos
-            weight = jnp.where(visible, silu(scores), 0.0).astype(BF16)
+            weight = jnp.where(key_pos <= q_pos, silu(scores), 0.0).astype(BF16)
             attn += jnp.dot(weight, kv[:, :W], preferred_element_type=F32)
         normed = attn * lax.rsqrt(jnp.mean(attn * attn, axis=-1, keepdims=True) + 1e-06)
-        out = (normed * gate_query[span, :W].astype(F32)).astype(BF16)
+        out = (normed * gate_query[group][span, :W].astype(F32)).astype(BF16)
         for s in range(NZ):
             chip = chip_at((z + NZ - s) % NZ, y ^ by, x ^ bx)
             gated[pl.ds(chip, 1)] = out[s * piece : (s + 1) * piece][None]
@@ -233,9 +216,10 @@
     copies = []
     for side, src in enumerate((w_own, w_other)):
         for chip in range(chips):
+            panel = (chip % (NY * NX)) * NZ + chip // (NY * NX)
             copies.append(
                 pltpu.make_async_copy(
-                    src.at[chip, pl.ds(0, half), :],
+                    src.at[panel, pl.ds(0, half), :],
                     w_all.at[side, :, pl.ds(chip * W, W)],
                     sems.at[side * chips + chip],
                 )
@@ -256,15 +240,19 @@
     send[...] = h_all[:, pl.ds(pl.multiple_of((1 - u) * half, half), half)]
 
 
-def loss_kernel(h_keep, h_send, t_keep, t_send, t_ids, n_ids, nn, n_own, n_other, loss, n_all, sems):
+def loss_kernel(
+    h_keep, h_send, t_keep, t_send, t_ids, n_ids, nn, late_own, late_other, loss, n_all, sems
+):
     keep, send = h_keep[...], h_send[...]
-    chips, panels, negs, _ = n_own.shape
+    _, chips, negs, half = n_all.shape
+    panels = half // W
+    split = late_own.shape[1] - panels * negs
     copies = []
-    for side, src in enumerate((n_own, n_other)):
+    for side, src in enumerate((late_own, late_other)):
         for panel in range(panels):
             copies.append(
                 pltpu.make_async_copy(
-                    src.at[:, panel],
+                    src.at[:, pl.ds(split + panel * negs, negs), :],
                     n_all.at[side, :, :, pl.ds(panel * W, W)],
                     sems.at[side * panels + panel],
                 )
@@ -282,7 +270,7 @@
         copy.wait()
     dots = 0.0
     for side, part in enumerate((keep, send)):
-        neg = n_all[side].reshape(chips * negs, panels * W)
+        neg = n_all[side].reshape(chips * negs, half)
         dots += lax.dot_general(part, neg, (((1,), (1,)), ((), ())), preferred_element_type=F32)
     neg_logit = dots * h_scale * lax.rsqrt(nn[...] + 1e-06)
     mass = jnp.where(n_ids[...] != t_ids[...], jnp.exp(neg_logit), 0.0)
@@ -325,47 +313,67 @@
     p_other = lax.dynamic_slice_in_dim(positions, (1 - u) * rows, rows, 0)
     marks = jnp.stack(position_marks(p_own) + position_marks(p_other), 1)
     marks = jnp.pad(marks, ((0, 0), (0, W - marks.shape[1])))
+    w_heads = scatter_heads(w_proj, u)
     tok = gather_chips(jnp.concatenate([mine, marks], 1))
-    w_mine = scatter_heads(w_proj, z, y, x, tok[0])
+    w_heads, w_out, neg_emb, _ = lax.optimization_barrier((w_heads, w_out, neg_emb, tok[0]))
+    w_mine = lax.all_to_all(w_heads, "ctx", 0, 0, tiled=True)
     w_theirs = swap_cores(w_mine)
 
     negs, panels = neg_emb.shape[0], neg_emb.shape[1] // W
     neg_panels = neg_emb.reshape(negs, panels, W).transpose(1, 0, 2).reshape(-1, W)
-    late_own = lax.all_gather(jnp.concatenate([w_out, neg_panels]), "ctx", axis=0)
+    late = jnp.concatenate([w_out, neg_panels])
+    plane = NY * NX
+    lines = [[zz * plane + p for zz in range(NZ)] for p in range(plane)]
+    planes = [[zz * plane + p for p in range(plane)] for zz in range(NZ)]
+    late = lax.all_gather(late, "ctx", axis=0, axis_index_groups=lines)
+    late, _ = lax.optimization_barrier((late, tok[1:3]))
+    late = lax.all_gather(late, "ctx", axis=0, axis_index_groups=planes)
+    late = late.reshape(CHIPS, -1, W)
     t_rows = target_emb.reshape(2, rows, -1)
     t_keep = lax.dynamic_index_in_dim(t_rows, u, 0, keepdims=False)
     t_send = swap_cores(lax.dynamic_index_in_dim(t_rows, 1 - u, 0, keepdims=False))
 
-    gate_query, value_key, marks_all = call(
-        proj_kernel,
-        "project",
-        [((events, 2 * W), BF16)] * 2 + [((events, W), BF16)],
-        [
-            pltpu.VMEM((events, model + W), BF16),
-            pltpu.VMEM((model, 4 * W), BF16),
-            pltpu.SemaphoreType.DMA((5,)),
-            pltpu.SemaphoreType.DMA((16,)),
-        ],
-        [where, *tok, w_mine, w_theirs],
-        "s" + 7 * "h",
-        2 * events * model * 4 * W,
-    )
-    kv_theirs = swap_cores(value_key)
-    late_own, _ = lax.optimization_barrier((late_own, value_key))
-    late_other = swap_cores(late_own)
-    split = w_out.shape[0]
-    n_own = late_own[:, split:].reshape(CHIPS, panels, negs, W)
-    n_other = late_other[:, split:].reshape(CHIPS, panels, negs, W)
-    nn = sum(jnp.sum(jnp.square(n.astype(F32)), axis=(1, 3)) for n in (n_own, n_other))
+    def project(pieces):
+        count = sum(p.shape[0] for p in pieces)
+        return call(
+            proj_kernel,
+            "project",
+            [((count, 2 * W), BF16)] * 2 + [((count, W), BF16)],
+            [
+                pltpu.VMEM((count, model + W), BF16),
+                pltpu.VMEM((CHIPS, 2, model // (2 * CHIPS), 4 * W), BF16),
+                pltpu.SemaphoreType.DMA((len(pieces),)),
+                pltpu.SemaphoreType.DMA((2,)),
+            ],
+            [where, *pieces, w_mine, w_theirs],
+            "s" + (len(pieces) + 2) * "h",
+            2 * count * model * 4 * W,
+        )
+
+    gq_early, kv_early, marks_early = project(tok[:3])
+    kv_early_theirs = swap_cores(kv_early)
+    last, kv_early = lax.optimization_barrier((tok[3:], kv_early))
+    gq_last, kv_last, marks_last = project(last)
+    kv_last_theirs = swap_cores(kv_last)
     (gated,) = call(
         attend_kernel,
         "attend",
         [((CHIPS, rows, W), BF16)],
         [],
-        [where, gate_query, value_key, kv_theirs, marks_all],
-        "svvvv",
+        [where, gq_early, gq_last, kv_early, kv_last, kv_early_theirs, kv_last_theirs]
+        + [marks_early, marks_last],
+        "s" + 8 * "v",
         8 * events * events * W,
     )
+    late_own, _ = lax.optimization_barrier((late, gated))
+    late_other = swap_cores(late_own)
+    split = w_out.shape[0]
+    nn = sum(
+        jnp.sum(jnp.square(n[:, split:].astype(F32)).reshape(CHIPS, panels, negs, W), axis=(1, 3))
+        for n in (late_own, late_other)
+    )
+    order = [zz * plane + p for p in range(plane) for zz in range(NZ)]
+    n_ids = neg_ids.reshape(CHIPS, -1)[jnp.array(order)].reshape(1, -1)
     gated = lax.all_to_all(gated, "ctx", 0, 0, tiled=True)
     h_keep, h_send = call(
         hidden_kernel,
@@ -396,10 +404,10 @@
             t_keep,
             t_send,
             target_ids[:, None],
-            neg_ids[None],
+            n_ids,
             nn.reshape(1, -1),
-            n_own,
-            n_other,
+            late_own,
+            late_other,
         ],
         "vvvvvvvhh",
         2 * rows * model * neg_ids.shape[0],

time: 203 us -> 199 us (0.980)
  blocking collectives: 0 us -> 31.1 us
  starting transfers between devices: 34.1 us -> 16.3 us
  waiting for transfers between devices: 105 us -> 93.6 us
  local copies, waits for them, and re-layouts: 13 us -> 9.64 us
  Pallas kernels: 24.3 us -> 22.1 us
    all_gather x1 -> x2, waiting for transfers between devices: 2.6 us -> 33.9 us  [the longest x1 19.4 us: head_shards(): late = lax.all_gather(late, 'ctx', axis=0, axis_index_groups=planes)]
    all_to_all x0 -> x1, blocking collectives: none -> 31.1 us  [head_shards(): w_mine = lax.all_to_all(w_heads, 'ctx', 0, 0, tiled=True)]
    ppermute x2 -> x0, waiting for transfers between devices: 19.5 us -> none  [scatter_heads(): arrived.append(lax.ppermute(piece, ('ctx', 'tp'), perm))]
    ppermute x10 -> x7, waiting for transfers between devices: 71.4 us -> 52 us  [hop(): return lax.ppermute(value, 'ctx', perm)]
    ppermute x5 -> x7, starting transfers between devices: 10.5 us -> 0.77 us  [swap_cores(): return lax.ppermute(value, 'tp', SWAP)]
    ppermute x5 -> x7, waiting for transfers between devices: 6.87 us -> 1.35 us  [swap_cores(): return lax.ppermute(value, 'tp', SWAP)]
    slice x2 -> x0, local copies, waits for them, and re-layouts: 3.48 us -> none  [the longest x1 1.75 us: head_shards(): n_other = late_other[:, split:].reshape(CHIPS, panels, negs, W)]
    ppermute x10 -> x7, starting transfers between devices: 15 us -> 11.7 us  [hop(): return lax.ppermute(value, 'ctx', perm)]
  transfers between devices with their start and end apart: 19 -> 17, of which waited for: 10 -> 10; matrix products, arithmetic and copies ran while one was open for 9% -> 7% of each run, Pallas kernels for 12% -> 11%
where the time goes in v3:
time: 199 us
  waiting for transfers between devices  93.6 us (47%)
  blocking collectives  31.1 us (16%)
  Pallas kernels  22.1 us (11%)
  starting transfers between devices  16.3 us (8%)
  between operations  14.3 us (7%)
  other arithmetic  11.7 us (6%)
  local copies, waits for them, and re-layouts  9.64 us (5%)
    ppermute x7, waiting for transfers between devices, hop(): return lax.ppermute(value, 'ctx', perm)  52 us
    all_to_all x1, blocking collectives, head_shards(): w_mine = lax.all_to_all(w_heads, 'ctx', 0, 0, tiled=True)  31.1 us
    pallas_call x5, Pallas kernels, call(): pl.pallas_call(kernel, out_shape=[jax.ShapeDtypeStruct(shape, dtype) for...  22.1 us
    all_gather x1, waiting for transfers between devices, head_shards(): late = lax.all_gather(late, 'ctx', axis=0, axis_index_groups=planes)  19.4 us
    all_gather x1, waiting for transfers between devices, head_shards(): late = lax.all_gather(late, 'ctx', axis=0, axis_index_groups=lines)  14.5 us
    ppermute x7, starting transfers between devices, hop(): return lax.ppermute(value, 'ctx', perm)  11.7 us
    all_to_all x1, waiting for transfers between devices, head_shards(): gated = lax.all_to_all(gated, 'ctx', 0, 0, tiled=True)  6.29 us
    reduce_sum x4, other arithmetic, head_shards(): jnp.sum(jnp.square(n[:, split:].astype(F32)).reshape(CHIPS, panels, negs,...  5.54 us
  transfers between devices with their start and end apart: 17, of which 10 were waited for; matrix products, arithmetic and copies ran while one was open for 7% of the time, Pallas kernels for 11%

profile of v3, /device:TPU:0, one launch (start us, length us, event | category | flops | bytes accessed | tf_op | source)
XLA Modules:
  0.0 198.7 jit_solution(7533079391877161707)
XLA Ops:
  9.0 3.0 %collective-permute-start = (bf16[64,2176]{1,0:T(8,128)(2,1)}, bf16[64,2176]{1,0:T(8,128)(2,1)}, u32[]{:S(2)}, u32[]{:S(2)}) collective-permute-start(bf16[64,2176]{1,0:T(8,128)(2,1)} %pad_maximum_fusion.2), channel_id=1, source_target_pairs={{0,8},{2,10},{4,12},{6,14},{8,16},{10,18},{12,20},{14,22},{16,24},... | collective-permute-start | bytes 835592 | tf_op jit(solution)/shard_map/ppermute | solution.py:110
  12.0 2.6 %collective-permute-start.1 = (bf16[64,2176]{1,0:T(8,128)(2,1)}, bf16[64,2176]{1,0:T(8,128)(2,1)}, u32[]{:S(2)}, u32[]{:S(2)}) collective-permute-start(bf16[64,2176]{1,0:T(8,128)(2,1)} %pad_maximum_fusion.2), channel_id=1, source_target_pairs={{0,16},{2,18},{4,20},{6,22},{8,24},{10,26},{12,28},{14,30},{16,0},... | collective-permute-start | bytes 835592 | tf_op jit(solution)/shard_map/ppermute | solution.py:110
  14.6 1.3 collective-permute-start.2
  16.0 1.5 reshape.54
  19.3 2.7 %collective-permute-done = bf16[64,2176]{1,0:T(8,128)(2,1)} collective-permute-done((bf16[64,2176]{1,0:T(8,128)(2,1)}, bf16[64,2176]{1,0:T(8,128)(2,1)}, u32[]{:S(2)}, u32[]{:S(2)}) %collective-permute-start) | collective-permute-done | bytes 278560 | tf_op jit(solution)/shard_map/ppermute | solution.py:110
  22.0 11.1 %collective-permute-done.1 = bf16[64,2176]{1,0:T(8,128)(2,1)} collective-permute-done((bf16[64,2176]{1,0:T(8,128)(2,1)}, bf16[64,2176]{1,0:T(8,128)(2,1)}, u32[]{:S(2)}, u32[]{:S(2)}) %collective-permute-start.1) | collective-permute-done | bytes 278560 | tf_op jit(solution)/shard_map/ppermute | solution.py:110
  36.4 1.6 collective-permute-start.3
  37.9 1.5 collective-permute-start.4
  39.5 23.4 %collective-permute-done.3.refs_1_ = bf16[256,2176]{1,0:T(8,128)(2,1)S(1)} collective-permute-done((bf16[256,2176]{1,0:T(8,128)(2,1)S(1)}, bf16[256,2176]{1,0:T(8,128)(2,1)S(1)}, u32[]{:S(2)}, u32[]{:S(2)}) %collective-permute-start.3) | collective-permute-done | bytes 1114144 | tf_op jit(solution)/shard_map/ppermute | solution.py:110
  64.2 14.5 %all-gather.5.cloned.1.call-done = bf16[6144,128]{1,0:T(8,128)(2,1)} async-done(((bf16[1536,128]{1,0:T(8,128)(2,1)}), bf16[6144,128]{1,0:T(8,128)(2,1)}) %all-gather.5.cloned.1.call-update) | async-done | bytes 1572880 | tf_op jit(solution)/shard_map/all_gather | solution.py:328
  78.7 31.1 %all_to_all.10.refs_3_.refs_2_ = bf16[16,64,512]{2,1,0:T(8,128)(2,1)S(1)} all-to-all(bf16[16,64,512]{2,1,0:T(8,128)(2,1)} %maximum_select_fusion), channel_id=1, replica_groups=mesh['ctx'=16,'tp'=2] {'ctx'}, dimensions={0} | all-to-all | bytes 2097152 | tf_op jit(solution)/shard_map/all_to_all | solution.py:319
  111.8 1.9 slice.19
  115.6 4.2 %project.2 = (bf16[768,256]{1,0:T(8,128)(2,1)S(1)}, bf16[768,256]{1,0:T(8,128)(2,1)S(1)}, bf16[768,128]{1,0:T(8,128)(2,1)S(1)}) custom-call(s32[4]{0:T(128)S(1)} %pad_add_fusion.where, bf16[256,2176]{1,0:T(8,128)(2,1)S(1)} %pad_maximum_fusion.refs_0_, bf16[256,2176]{1,0:T(8,128)(2,1)S(1)} %copy-done.3, bf16[256,2176]{1,0:T(8,128)(2,1)} %collective-permute-done.4.refs_2_, ...), custom_call_target="tpu_custom_call" | custom-call | flops 1610612736 | bytes 5439504 | tf_op jit(solution)/shard_map/project/pallas_call | solution.py:284
  119.9 9.0 %collective-permute-done.7.refs_0_ = bf16[128,2176]{1,0:T(8,128)(2,1)S(1)} collective-permute-done((bf16[128,2176]{1,0:T(8,128)(2,1)}, bf16[128,2176]{1,0:T(8,128)(2,1)S(1)}, u32[]{:S(2)}, u32[]{:S(2)}) %collective-permute-start.7) | collective-permute-done | bytes 557088 | tf_op jit(solution)/shard_map/ppermute | solution.py:110
  128.9 5.5 %collective-permute-done.8.refs_1_ = bf16[128,2176]{1,0:T(8,128)(2,1)} collective-permute-done((bf16[128,2176]{1,0:T(8,128)(2,1)}, bf16[128,2176]{1,0:T(8,128)(2,1)}, u32[]{:S(2)}, u32[]{:S(2)}) %collective-permute-start.8) | collective-permute-done | bytes 557088 | tf_op jit(solution)/shard_map/ppermute | solution.py:110
  134.4 2.8 %project.3 = (bf16[256,256]{1,0:T(8,128)(2,1)S(1)}, bf16[256,256]{1,0:T(8,128)(2,1)S(1)}, bf16[256,128]{1,0:T(8,128)(2,1)S(1)}) custom-call(s32[4]{0:T(128)S(1)} %pad_add_fusion.where, bf16[128,2176]{1,0:T(8,128)(2,1)S(1)} %collective-permute-done.7.refs_0_, bf16[128,2176]{1,0:T(8,128)(2,1)} %collective-permute-done.8.refs_1_, ...), custom_call_target="tpu_custom_call" | custom-call | flops 536870912 | bytes 3211280 | tf_op jit(solution)/shard_map/project/pallas_call | solution.py:284
  138.6 4.7 %attend.1 = bf16[16,64,128]{2,1,0:T(8,128)(2,1)} custom-call(s32[4]{0:T(128)S(1)} %pad_add_fusion.where, bf16[768,256]{1,0:T(8,128)(2,1)S(1)} %get-tuple-element.19.refs_0_, bf16[256,256]{1,0:T(8,128)(2,1)S(1)} %get-tuple-element.23.refs_1_, bf16[768,256]{1,0:T(8,128)(2,1)S(1)} %get-tuple-element.24.refs_2_, bf16[256,256]{1,0:T(8,128)(2,1)S(1)} %get-tuple-element.25.refs_3_, ...), custom_call_target="tpu_custom_call" | custom-call | flops 1073741824 | bytes 1835024 | tf_op jit(solution)/shard_map/attend/pallas_call | solution.py:284
  143.3 19.4 %all-gather.7.cloned.1.call-done.w_own.late_own = bf16[16,1536,128]{2,1,0:T(8,128)(2,1)} async-done(((bf16[4,1536,128]{2,1,0:T(8,128)(2,1)}), bf16[16,1536,128]{2,1,0:T(8,128)(2,1)}) %all-gather.7.cloned.1.call-update) | async-done | bytes 6291472 | tf_op jit(solution)/shard_map/all_gather | solution.py:330
  162.7 3.7 %all-to-all-start.1 = ((bf16[16,64,128]{2,1,0:T(8,128)(2,1)}), bf16[16,64,128]{2,1,0:T(8,128)(2,1)S(1)}, u32[]{:S(2)}, u32[]{:S(2)}) async-start(bf16[16,64,128]{2,1,0:T(8,128)(2,1)} %attend.1), calls=%async_computation.1 | async-start | bytes 524288 | tf_op jit(solution)/shard_map/all_to_all | solution.py:377
  167.8 2.7 %multiply_reduce_fusion.1 = f32[16,512]{1,0:T(8,128)S(1)} fusion(bf16[16,1536,128]{2,1,0:T(8,128)(2,1)} %all-gather.7.cloned.1.call-done.w_own.late_own), kind=kLoop, calls=%fused_computation.2 | loop fusion | flops 3137536 | bytes 2129920 | tf_op jit(solution)/shard_map/reduce_sum | solution.py:372
  170.7 6.3 %all-to-all-done.1.gated = bf16[16,64,128]{2,1,0:T(8,128)(2,1)S(1)} async-done(((bf16[16,64,128]{2,1,0:T(8,128)(2,1)}), bf16[16,64,128]{2,1,0:T(8,128)(2,1)S(1)}, u32[]{:S(2)}, u32[]{:S(2)}) %all-to-all-start.1) | async-done | bytes 262176 | tf_op jit(solution)/shard_map/all_to_all | solution.py:377
  177.0 6.6 %hidden.1 = (bf16[64,1024]{1,0:T(8,128)(2,1)S(1)}, bf16[64,1024]{1,0:T(8,128)(2,1)S(1)}) custom-call(s32[4]{0:T(128)S(1)} %pad_add_fusion.where, bf16[16,64,128]{2,1,0:T(8,128)(2,1)S(1)} %all-to-all-done.1.gated, bf16[16,1536,128]{2,1,0:T(8,128)(2,1)} %all-gather.7.cloned.1.call-done.w_own.late_own, ...), custom_call_target="tpu_custom_call" | custom-call | flops 536870912 | bytes 13107216 | tf_op jit(solution)/shard_map/hidden/pallas_call | solution.py:284
  183.7 2.8 %multiply_reduce_fusion = f32[16,512]{1,0:T(8,128)S(1)} fusion(bf16[16,1536,128]{2,1,0:T(8,128)(2,1)} %collective-permute-done.11.w_other.late_other), kind=kLoop, calls=%fused_computation.1 | loop fusion | flops 3137536 | bytes 2129920 | tf_op jit(solution)/shard_map/reduce_sum | solution.py:372
  186.6 3.9 %loss.1 = f32[64,1]{1,0:T(8,128)S(1)} custom-call(bf16[64,1024]{1,0:T(8,128)(2,1)S(1)} %get-tuple-element.32.h_keep, bf16[64,1024]{1,0:T(8,128)(2,1)S(1)} %get-tuple-element.33.h_send, bf16[64,1024]{1,0:T(8,128)(2,1)S(1)} %get-tuple-element.41.t_keep, bf16[64,1024]{1,0:T(8,128)(2,1)S(1)} %collective-permute-done.13.t_send, s32[64,1]{1,0:T(8,128)S(1)} %copy.32.t_ids, ...), custom_call_target="tpu_custom_call" | custom-call | flops 268435456 | bytes 13115648 | tf_op jit(solution)/shard_map/loss/pallas_call | solution.py:284
  (73 shorter events, 16.7 us)
Async XLA Ops:
  7.2 71.5 %all-gather.5.cloned.1.call-start = ((), (), s32[]{:S(2)}) async-start(), calls=%async_computation.2 | async-start | bytes 1966080 | tf_op jit(solution)/shard_map/all_gather | solution.py:328
  9.0 13.0 %collective-permute-start = (bf16[64,2176]{1,0:T(8,128)(2,1)}, bf16[64,2176]{1,0:T(8,128)(2,1)}, u32[]{:S(2)}, u32[]{:S(2)}) collective-permute-start(bf16[64,2176]{1,0:T(8,128)(2,1)} %pad_maximum_fusion.2), channel_id=1, source_target_pairs={{0,8},{2,10},{4,12},{6,14},{8,16},{10,18},{12,20},{14,22},{16,24},... | collective-permute-start | bytes 835592 | tf_op jit(solution)/shard_map/ppermute | solution.py:110
  12.0 21.1 %collective-permute-start.1 = (bf16[64,2176]{1,0:T(8,128)(2,1)}, bf16[64,2176]{1,0:T(8,128)(2,1)}, u32[]{:S(2)}, u32[]{:S(2)}) collective-permute-start(bf16[64,2176]{1,0:T(8,128)(2,1)} %pad_maximum_fusion.2), channel_id=1, source_target_pairs={{0,16},{2,18},{4,20},{6,22},{8,24},{10,26},{12,28},{14,30},{16,0},... | collective-permute-start | bytes 835592 | tf_op jit(solution)/shard_map/ppermute | solution.py:110
  14.6 18.5 %collective-permute-start.2 = (bf16[64,2176]{1,0:T(8,128)(2,1)}, bf16[64,2176]{1,0:T(8,128)(2,1)}, u32[]{:S(2)}, u32[]{:S(2)}) collective-permute-start(bf16[64,2176]{1,0:T(8,128)(2,1)} %pad_maximum_fusion.2), channel_id=1, source_target_pairs={{0,24},{2,26},{4,28},{6,30},{8,0},{10,2},{12,4},{14,6},{16,8},{18,... | collective-permute-start | bytes 835592 | tf_op jit(solution)/shard_map/ppermute | solution.py:110
  19.3 16.2 %copy-start.6 = (bf16[64,1024]{1,0:T(8,128)(2,1)S(1)}, bf16[64,1024]{1,0:T(8,128)(2,1)}, u32[]{:S(2)}) copy-start(bf16[64,1024]{1,0:T(8,128)(2,1)} %param.13) | copy-start | bytes 393220
  19.3 15.0 %collective-permute-start.5 = (bf16[8,64,512]{2,1,0:T(8,128)(2,1)}, bf16[8,64,512]{2,1,0:T(8,128)(2,1)S(1)}, u32[]{:S(2)}, u32[]{:S(2)}) collective-permute-start(bf16[8,64,512]{2,1,0:T(8,128)(2,1)} %get-tuple-element.39), channel_id=1, source_target_pairs={{0,1},{1,0},{2,3},{3,2},{4,5},{5,4},{6,7},{7,6},{8,9},{9,8},{10,11... | collective-permute-start | bytes 1572872 | tf_op jit(solution)/shard_map/ppermute | solution.py:114
  19.3 16.2 %copy-start.4 = (bf16[1024,128]{1,0:T(8,128)(2,1)S(1)}, bf16[1024,128]{1,0:T(8,128)(2,1)}, u32[]{:S(2)}) copy-start(bf16[1024,128]{1,0:T(8,128)(2,1)} %param.11) | copy-start | bytes 786436
  36.3 126.3 %all-gather.7.cloned.1.call-start = ((), (), s32[]{:S(2)}) async-start(), calls=%async_computation.3 | async-start | bytes 7864320 | tf_op jit(solution)/shard_map/all_gather | solution.py:330
  36.4 26.5 %collective-permute-start.3 = (bf16[256,2176]{1,0:T(8,128)(2,1)S(1)}, bf16[256,2176]{1,0:T(8,128)(2,1)S(1)}, u32[]{:S(2)}, u32[]{:S(2)}) collective-permute-start(bf16[256,2176]{1,0:T(8,128)(2,1)S(1)} %pad_maximum_fusion.refs_0_), channel_id=1, source_target_pairs={{0,2},{2,0},{4,6},{6,4},{8,10},{10,8},{12,14},{14,12},{16,18},{18,... | collective-permute-start | bytes 3342344 | tf_op jit(solution)/shard_map/ppermute | solution.py:110
  37.9 26.2 %collective-permute-start.4 = (bf16[256,2176]{1,0:T(8,128)(2,1)S(1)}, bf16[256,2176]{1,0:T(8,128)(2,1)}, u32[]{:S(2)}, u32[]{:S(2)}) collective-permute-start(bf16[256,2176]{1,0:T(8,128)(2,1)S(1)} %pad_maximum_fusion.refs_0_), channel_id=1, source_target_pairs={{0,4},{2,6},{4,0},{6,2},{8,12},{10,14},{12,8},{14,10},{16,20},{18,... | collective-permute-start | bytes 3342344 | tf_op jit(solution)/shard_map/ppermute | solution.py:110
  78.7 31.1 %copy-start.2 = (bf16[256,2176]{1,0:T(8,128)(2,1)S(1)}, bf16[256,2176]{1,0:T(8,128)(2,1)}, u32[]{:S(2)}) copy-start(bf16[256,2176]{1,0:T(8,128)(2,1)} %copy-done.1) | copy-start | bytes 3342340
  109.8 4.5 %collective-permute-start.6 = (bf16[16,64,512]{2,1,0:T(8,128)(2,1)S(1)}, bf16[16,64,512]{2,1,0:T(8,128)(2,1)}, u32[]{:S(2)}, u32[]{:S(2)}) collective-permute-start(bf16[16,64,512]{2,1,0:T(8,128)(2,1)S(1)} %all_to_all.10.refs_3_.refs_2_), channel_id=1, source_target_pairs={{0,1},{1,0},{2,3},{3,2},{4,5},{5,4},{6,7},{7,6},{8,9},{9,8},{10,11... | collective-permute-start | bytes 3145736 | tf_op jit(solution)/shard_map/ppermute | solution.py:114
  110.7 18.2 %collective-permute-start.7 = (bf16[128,2176]{1,0:T(8,128)(2,1)}, bf16[128,2176]{1,0:T(8,128)(2,1)S(1)}, u32[]{:S(2)}, u32[]{:S(2)}) collective-permute-start(bf16[128,2176]{1,0:T(8,128)(2,1)} %slice.18), channel_id=1, source_target_pairs={{0,4},{2,6},{4,0},{6,2},{8,12},{10,14},{12,8},{14,10},{16,20},{18,... | collective-permute-start | bytes 1671176 | tf_op jit(solution)/shard_map/ppermute | solution.py:110
  113.7 20.7 %collective-permute-start.8 = (bf16[128,2176]{1,0:T(8,128)(2,1)}, bf16[128,2176]{1,0:T(8,128)(2,1)}, u32[]{:S(2)}, u32[]{:S(2)}) collective-permute-start(bf16[128,2176]{1,0:T(8,128)(2,1)} %slice.19), channel_id=1, source_target_pairs={{0,2},{2,0},{4,6},{6,4},{8,10},{10,8},{12,14},{14,12},{16,18},{18,... | collective-permute-start | bytes 1671176 | tf_op jit(solution)/shard_map/ppermute | solution.py:110
  119.8 18.8 %collective-permute-start.9 = (bf16[768,256]{1,0:T(8,128)(2,1)S(1)}, bf16[768,256]{1,0:T(8,128)(2,1)S(1)}, u32[]{:S(2)}, u32[]{:S(2)}) collective-permute-start(bf16[768,256]{1,0:T(8,128)(2,1)S(1)} %get-tuple-element.24.refs_2_), channel_id=1, source_target_pairs={{0,1},{1,0},{2,3},{3,2},{4,5},{5,4},{6,7},{7,6},{8,9},{9,8},{10,11... | collective-permute-start | bytes 1179656 | tf_op jit(solution)/shard_map/ppermute | solution.py:114
  137.2 1.4 collective-permute-start.10
  138.6 27.9 %copy-start.5 = (bf16[128,1024]{1,0:T(8,128)(2,1)S(1)}, bf16[128,1024]{1,0:T(8,128)(2,1)}, u32[]{:S(2)}) copy-start(bf16[128,1024]{1,0:T(8,128)(2,1)} %param.15) | copy-start | bytes 786436
  138.6 28.4 %copy-start.8 = (s32[64]{0:T(128)S(1)}, s32[64]{0:T(128)}, u32[]{:S(2)}) copy-start(s32[64]{0:T(128)} %param.16) | copy-start | bytes 772
  138.6 28.5 %copy-start.7 = (s32[1024]{0:T(1024)S(1)}, s32[1024]{0:T(1024)}, u32[]{:S(2)}) copy-start(s32[1024]{0:T(1024)} %param.14) | copy-start | bytes 12292
  138.6 28.6 %copy-start.9 = (s32[16]{0:T(128)S(1)}, s32[16]{0:T(128)}, u32[]{:S(2)}) copy-start(s32[16]{0:T(128)} %constant.116) | copy-start | bytes 196
  162.7 14.3 %collective-permute-start.11 = (bf16[16,1536,128]{2,1,0:T(8,128)(2,1)}, bf16[16,1536,128]{2,1,0:T(8,128)(2,1)}, u32[]{:S(2)}, u32[]{:S(2)}) collective-permute-start(bf16[16,1536,128]{2,1,0:T(8,128)(2,1)} %all-gather.7.cloned.1.call-done.w_own.late_own), channel_id=1, source_target_pairs={{0,1},{1,0},{2,3},{3,2},{4,5},{5,4},{6,7},{7,6},{8,9},{9,8},{10,11... | collective-permute-start | bytes 18874376 | tf_op jit(solution)/shard_map/ppermute | solution.py:114
  162.7 14.3 %all-to-all-start.1 = ((bf16[16,64,128]{2,1,0:T(8,128)(2,1)}), bf16[16,64,128]{2,1,0:T(8,128)(2,1)S(1)}, u32[]{:S(2)}, u32[]{:S(2)}) async-start(bf16[16,64,128]{2,1,0:T(8,128)(2,1)} %attend.1), calls=%async_computation.1 | async-start | bytes 524288 | tf_op jit(solution)/shard_map/all_to_all | solution.py:377
  166.5 20.1 %collective-permute-start.13 = (bf16[64,1024]{1,0:T(8,128)(2,1)S(1)}, bf16[64,1024]{1,0:T(8,128)(2,1)S(1)}, u32[]{:S(2)}, u32[]{:S(2)}) collective-permute-start(bf16[64,1024]{1,0:T(8,128)(2,1)S(1)} %get-tuple-element.40), channel_id=1, source_target_pairs={{0,1},{1,0},{2,3},{3,2},{4,5},{5,4},{6,7},{7,6},{8,9},{9,8},{10,11... | collective-permute-start | bytes 393224 | tf_op jit(solution)/shard_map/ppermute | solution.py:114
  183.6 7.5 %collective-permute-start.12 = (bf16[64,1024]{1,0:T(8,128)(2,1)S(1)}, bf16[64,1024]{1,0:T(8,128)(2,1)S(1)}, u32[]{:S(2)}, u32[]{:S(2)}) collective-permute-start(bf16[64,1024]{1,0:T(8,128)(2,1)S(1)} %get-tuple-element.33.h_send), channel_id=1, source_target_pairs={{0,1},{1,0},{2,3},{3,2},{4,5},{5,4},{6,7},{7,6},{8,9},{9,8},{10,11... | collective-permute-start | bytes 393224 | tf_op jit(solution)/shard_map/ppermute | solution.py:114
  (3 other events, 3.3 us)
Sparse Core Ops, SparseCore 0:
  36.4 42.1 all-gather.4
  80.5 82.0 all-gather.6

commit v4 on v3

v4 whole, which is shorter than its diff:
```python
import jax
import jax.numpy as jnp
from jax import lax
from jax.experimental import pallas as pl
from jax.experimental.pallas import tpu as pltpu
from jax.sharding import PartitionSpec as P

HEAD_DIM = 128
VMEM_LIMIT = 48 * 1024 * 1024
BF16 = jnp.bfloat16
F32 = jnp.float32


def attend_piece(q_group, q_pos, k_piece, v_piece, p_piece):
    heads = q_group.shape[1]
    width = q_group.shape[2]
    key_heads = k_piece.reshape(k_piece.shape[0], heads, width)
    value_heads = v_piece.reshape(v_piece.shape[0], heads, width)
    scores = jnp.einsum(
        "thd,khd->htk", q_group, key_heads, preferred_element_type=jnp.float32
    ) * width ** (-0.5)
    visible = p_piece[None, None, :] <= q_pos[None, :, None]
    weight = jnp.where(visible, jax.nn.silu(scores), 0.0).astype(jnp.bfloat16)
    return jnp.einsum("htk,khd->thd", weight, value_heads, preferred_element_type=jnp.float32)


def general_shards(
    tokens, w_proj, w_out, positions, neg_emb, neg_ids, target_emb, target_ids
):
    tok_rows = tokens.shape[0]
    head_cols = w_proj.shape[2]
    local_heads = head_cols // HEAD_DIM
    proj_sum = jnp.einsum(
        "td,dfh->tfh",
        tokens,
        lax.all_gather(w_proj, "ctx", axis=0, tiled=True),
        preferred_element_type=jnp.float32,
    )
    proj = jax.nn.silu(proj_sum).astype(jnp.bfloat16)
    gate = proj[:, 0].reshape(tok_rows, local_heads, HEAD_DIM)
    query = proj[:, 2].reshape(tok_rows, local_heads, HEAD_DIM)
    v_piece = lax.all_gather(proj[:, 1], "ctx", axis=0, tiled=True)
    k_piece = lax.all_gather(proj[:, 3], "ctx", axis=0, tiled=True)
    p_piece = lax.all_gather(positions, "ctx", axis=0, tiled=True)
    attn = attend_piece(query, positions, k_piece, v_piece, p_piece)
    normed = attn * lax.rsqrt(jnp.mean(attn * attn, axis=-1, keepdims=True) + 1e-06)
    gated = (normed * gate.astype(jnp.float32)).astype(jnp.bfloat16).reshape(tok_rows, head_cols)
    out_terms = jnp.dot(
        gated, lax.all_gather(w_out, "ctx", axis=1, tiled=True), preferred_element_type=jnp.float32
    )
    out_share = lax.psum_scatter(out_terms, "tp", scatter_dimension=1, tiled=True)
    feat_cols = out_share.shape[1]
    own_tokens = lax.dynamic_slice_in_dim(tokens, lax.axis_index("tp") * feat_cols, feat_cols, 1)
    hidden = (own_tokens.astype(jnp.float32) + out_share).astype(jnp.bfloat16)
    piece = lax.all_gather(neg_emb, "ctx", axis=0, tiled=True)
    panel_dots = lax.dot_general(
        hidden, piece, (((1,), (1,)), ((), ())), preferred_element_type=jnp.float32
    )
    panel_norms = jnp.sum(jnp.square(piece.astype(jnp.float32)), axis=1)
    hidden_f = hidden.astype(jnp.float32)
    target_f = target_emb.astype(jnp.float32)
    part_hh = jnp.sum(hidden_f * hidden_f, axis=1)
    part_he = jnp.sum(hidden_f * target_f, axis=1)
    part_ee = jnp.sum(target_f * target_f, axis=1)
    dots, hh_sum, he_sum, ee_sum = (
        lax.psum_scatter(panel_dots, "tp", scatter_dimension=0, tiled=True),
        lax.psum_scatter(part_hh, "tp", scatter_dimension=0, tiled=True),
        lax.psum_scatter(part_he, "tp", scatter_dimension=0, tiled=True),
        lax.psum_scatter(part_ee, "tp", scatter_dimension=0, tiled=True),
    )
    neg_sq = lax.psum(panel_norms, "tp")
    pos_logit = he_sum / jnp.sqrt(hh_sum + 1e-06) / jnp.sqrt(ee_sum + 1e-06) / 0.05
    neg_logit = dots / jnp.sqrt(hh_sum + 1e-06)[:, None] / jnp.sqrt(neg_sq + 1e-06)[None, :] / 0.05
    keep_mask = neg_ids[None, :] != target_ids[:, None]
    total_mass = jnp.exp(pos_logit) + jnp.sum(jnp.where(keep_mask, jnp.exp(neg_logit), 0.0), axis=1)
    loss = jnp.log(total_mass) - pos_logit
    return (hidden, loss)


NZ, NY, NX = 4, 2, 2
CHIPS = NZ * NY * NX
PLANE = [(by, bx) for by in range(NY) for bx in range(NX)]
SWAP = [(0, 1), (1, 0)]
W = HEAD_DIM
ACROSS = (((1,), (1,)), ((), ()))


def chip_at(z, y, x):
    return (z * NY + y) * NX + x


def coords(c):
    return c // (NY * NX), (c // NX) % NY, c % NX


def relative_chip(c, by, bx, s):
    z, y, x = coords(c)
    return chip_at((z + NZ - s) % NZ, y ^ by, x ^ bx)


def z_shift(s):
    return [(c, relative_chip(c, 0, 0, NZ - s)) for c in range(CHIPS)]


def flip(by, bx):
    return [(c, relative_chip(c, by, bx, 0)) for c in range(CHIPS)]


def hop(value, perm):
    return lax.ppermute(value, "ctx", perm)


def swap_cores(value):
    return lax.ppermute(value, "tp", SWAP)


def pick_row(value, at):
    return lax.dynamic_index_in_dim(value, at, 0, keepdims=False)


def after(values, *others):
    return lax.optimization_barrier((values, others))[0]


def along_z(own):
    return [own] + [hop(own, z_shift(s)) for s in range(1, NZ)]


def beside(near):
    return [near, hop(near, flip(0, 1)), hop(near, flip(1, 0))]


def across(near, beside_x, beside_y):
    half = near.shape[0] // 2
    first = hop(beside_x[:half], flip(1, 0))
    second = hop(beside_y[half:], flip(0, 1))
    return [near, beside_x, beside_y, first, second]


def heads_in_plane(w_proj, y, x):
    plane = NY * NX
    heads = w_proj.reshape(-1, 4, 2, plane, W).transpose(3, 2, 0, 1, 4)
    heads = heads.reshape(plane, 2, -1, 4 * W)
    out = []
    for by, bx in PLANE:
        piece = pick_row(heads, (y ^ by) * NX + (x ^ bx))
        if (by, bx) == PLANE[-1]:
            piece = after(piece, out[1])
        out.append(piece if (by, bx) == (0, 0) else hop(piece, flip(by, bx)))
    return jnp.stack(out, 1)


def heads_along_z(heads, z):
    arrived = []
    for e in range(2):
        perm = []
        for src in range(CHIPS):
            sz, sy, sx = coords(src)
            for t in range(2):
                dst = chip_at(2 * t + (e ^ (sz & 1)), sy, sx)
                perm.append((2 * src + t, 2 * dst + (sz >> 1)))
        arrived.append(lax.ppermute(pick_row(heads, e ^ (z & 1)), ("ctx", "tp"), perm))
    return jnp.stack(arrived)


def silu(v):
    return 0.5 * v * (1.0 + jnp.tanh(0.5 * v))


def run_copies(copies):
    for copy in copies:
        copy.start()
    for copy in copies:
        copy.wait()


def proj_kernel(where, *refs):
    count = len(refs) - 9
    tok, (w_own, w_other) = refs[:count], refs[count : count + 2]
    gate_query, value_key, marks, x_all, w_all, tok_sem, w_sem = refs[count + 2 :]
    z, y, x, u = (where[i] for i in range(4))
    copies, base = [], 0
    for side, (half, src) in enumerate(((u, w_own), (1 - u, w_other))):
        for e in range(2):
            for k, (by, bx) in enumerate(PLANE):
                block = chip_at(2 * half + (e ^ (z & 1)), y ^ by, x ^ bx)
                sem = w_sem.at[(side * 2 + e) * len(PLANE) + k]
                copies.append(pltpu.make_async_copy(src.at[e, k], w_all.at[block], sem))
    for i, ref in enumerate(tok):
        rows = pl.ds(base, ref.shape[0])
        copies.append(pltpu.make_async_copy(ref, x_all.at[rows, :], tok_sem.at[i]))
        base += ref.shape[0]
    run_copies(copies)
    weights = w_all[...].reshape(-1, w_all.shape[-1])
    model = weights.shape[0]
    total = jnp.dot(x_all[:, :model], weights, preferred_element_type=F32)
    proj = silu(total).astype(BF16)
    gate_query[:, :W] = proj[:, :W]
    value_key[:, :W] = proj[:, W : 2 * W]
    gate_query[:, W:] = proj[:, 2 * W : 3 * W]
    value_key[:, W:] = proj[:, 3 * W :]
    marks[...] = x_all[:, model:]


def pick_columns(*weights):
    lane = lax.broadcasted_iota(jnp.int32, (8, W), 1)
    line = lax.broadcasted_iota(jnp.int32, (8, W), 0)
    pick = jnp.zeros((8, W), F32)
    for i, row in enumerate(weights):
        for at, weight in row.items():
            pick = jnp.where((line == i) & (lane == at), weight, pick)
    return pick.astype(BF16)


def attend_kernel(*refs):
    gate_query, kv_own, kv_other, marks = refs[:2], refs[2:4], refs[4:6], refs[6:8]
    gated = refs[8]
    pick = pick_columns({0: 128.0, 1: 1.0}, {2: 128.0, 3: 1.0})
    piece = gated.shape[2]
    tile = NZ * piece
    groups = []
    for group in range(2):
        key_pos = lax.dot_general(pick, marks[group][...], ACROSS, preferred_element_type=F32)
        groups.append((kv_own[group], key_pos[0:1]))
        groups.append((kv_other[group], key_pos[1:2]))
    for k in range(len(PLANE)):
        group, base = (0, k * tile) if k < len(PLANE) - 1 else (1, 0)
        span = pl.ds(base, tile)
        query = gate_query[group][span, W:]
        q_pos = lax.dot_general(
            marks[group][span, :], pick, ACROSS, preferred_element_type=F32
        )[:, :1]
        attn = jnp.zeros((tile, W), F32)
        for kv, key_pos in groups:
            scores = lax.dot_general(
                query, kv[:, W:], ACROSS, preferred_element_type=F32
            ) * W ** (-0.5)
            weight = jnp.where(key_pos <= q_pos, silu(scores), 0.0).astype(BF16)
            attn += jnp.dot(weight, kv[:, :W], preferred_element_type=F32)
        normed = attn * lax.rsqrt(jnp.mean(attn * attn, axis=-1, keepdims=True) + 1e-06)
        out = (normed * gate_query[group][span, :W].astype(F32)).astype(BF16)
        for s in range(NZ):
            gated[s, k] = out[s * piece : (s + 1) * piece]


def hidden_kernel(where, *refs):
    n = len(PLANE)
    gated, w_own, w_other, tok = refs[:n], refs[n], refs[n + 1], refs[n + 2 : 2 * n + 2]
    hidden, g_all, t_all, w_all, sems = refs[-5:]
    z, y, x, u = (where[i] for i in range(4))
    c = chip_at(z, y, x)
    rows = hidden.shape[1]
    half = w_all.shape[1]
    copies = []
    for s in range(NZ):
        cols = pl.ds(s * W, W)
        for side, src in enumerate((w_own, w_other)):
            copies.append((src.at[s], w_all.at[side, :, cols]))
        block = relative_chip(c, 0, 0, s)
        from_cols = pl.ds(pl.multiple_of(block * W, W), W)
        for k in range(n):
            copies.append((tok[k].at[pl.ds(0, rows), from_cols], t_all.at[k, :, cols]))
    copies = [pltpu.make_async_copy(a, b, sems.at[i]) for i, (a, b) in enumerate(copies)]
    for copy in copies:
        copy.start()
    for k, (by, bx) in enumerate(PLANE):
        for s in range(NZ):
            head = relative_chip(c, by, bx, NZ - s)
            cols = pl.ds(pl.multiple_of(head * W, W), W)
            for j, (jy, jx) in enumerate(PLANE):
                block = (jy ^ by) * NX + (jx ^ bx)
                g_all[block * rows : (block + 1) * rows, cols] = gated[k][s, j]
    for copy in copies:
        copy.wait()
    total = 0.0
    for side, at in enumerate((u, 1 - u)):
        part = g_all[:, pl.ds(pl.multiple_of(at * half, half), half)]
        total += jnp.dot(part, w_all[side], preferred_element_type=F32)
    for k in range(n):
        for s in range(NZ):
            term = total[k * rows : (k + 1) * rows, s * W : (s + 1) * W]
            cols = pl.ds(pl.multiple_of(((z + NZ - s) % NZ) * W, W), W)
            hidden[k, :, cols] = (t_all[k, :, s * W : (s + 1) * W].astype(F32) + term).astype(BF16)


def order_kernel(where, *refs):
    pieces, (keep, send, h_all) = refs[: len(PLANE)], refs[len(PLANE) :]
    y, x, u = (where[i] for i in range(1, 4))
    half = keep.shape[1]
    for (by, bx), ref in zip(PLANE, pieces):
        for at in range(NZ):
            block = chip_at(at, y ^ by, x ^ bx)
            h_all[:, pl.ds(pl.multiple_of(block * W, W), W)] = ref[:, at * W : (at + 1) * W]
    keep[...] = h_all[:, pl.ds(pl.multiple_of(u * half, half), half)]
    send[...] = h_all[:, pl.ds(pl.multiple_of((1 - u) * half, half), half)]


def loss_kernel(h_keep, h_send, t_keep, t_send, t_ids, n_own, n_other, loss, n_all, sems):
    keep, send = h_keep[...], h_send[...]
    half = keep.shape[1]
    copies = []
    for side, src in enumerate((n_own, n_other)):
        copies.append(pltpu.make_async_copy(src, n_all.at[side], sems.at[side]))
    for copy in copies:
        copy.start()
    hh = he = ee = 0.0
    for part, ref in ((keep, t_keep), (send, t_send)):
        h_f, t_f = part.astype(F32), ref[...].astype(F32)
        hh += jnp.sum(h_f * h_f, axis=1, keepdims=True)
        he += jnp.sum(h_f * t_f, axis=1, keepdims=True)
        ee += jnp.sum(t_f * t_f, axis=1, keepdims=True)
    h_scale = lax.rsqrt(hh + 1e-06) * 20.0
    pos_logit = he * lax.rsqrt(ee + 1e-06) * h_scale
    for copy in copies:
        copy.wait()
    pick = pick_columns({0: 1.0, 1: 1.0, 2: 1.0}, {3: 256.0, 4: 1.0})
    dots, read = 0.0, []
    for side, part in enumerate((keep, send)):
        neg, marks = n_all[side, :, :half], n_all[side, :, half:]
        dots += lax.dot_general(part, neg, ACROSS, preferred_element_type=F32)
        read.append(lax.dot_general(pick, marks, ACROSS, preferred_element_type=F32))
    nn = read[0][0:1] + read[1][0:1]
    n_ids = read[0][1:2]
    neg_logit = dots * h_scale * lax.rsqrt(nn + 1e-06)
    mass = jnp.where(n_ids != t_ids[...].astype(F32), jnp.exp(neg_logit), 0.0)
    total = jnp.exp(pos_logit) + jnp.sum(mass, axis=1, keepdims=True)
    loss[...] = jnp.log(total) - pos_logit


def call(kernel, name, outs, scratch, args, places, flops):
    space = {"s": pltpu.SMEM, "v": pltpu.VMEM, "h": pl.ANY}
    moved = sum(a.size * a.dtype.itemsize for a in args)
    return pl.pallas_call(
        kernel,
        out_shape=[jax.ShapeDtypeStruct(shape, dtype) for shape, dtype in outs],
        in_specs=[pl.BlockSpec(memory_space=space[p]) for p in places],
        out_specs=[pl.BlockSpec(memory_space=pltpu.VMEM)] * len(outs),
        scratch_shapes=scratch,
        compiler_params=pltpu.CompilerParams(vmem_limit_bytes=VMEM_LIMIT),
        cost_estimate=pl.CostEstimate(flops=flops, bytes_accessed=moved, transcendentals=0),
        name=name,
    )(*args)


def whole_parts(value, base):
    return [(value // base).astype(BF16), (value % base).astype(BF16)]


def float_parts(value):
    parts = []
    for _ in range(3):
        parts.append(lax.reduce_precision(value, 8, 7))
        value = value - parts[-1]
    return [part.astype(BF16) for part in parts]


def with_marks(rows, marks):
    marks = jnp.stack(marks, 1)
    marks = jnp.pad(marks, ((0, 0), (0, W - marks.shape[1])))
    return jnp.concatenate([rows, marks], 1)


def head_shards(
    tokens, w_proj, w_out, positions, neg_emb, neg_ids, target_emb, target_ids
):
    c, u = lax.axis_index("ctx"), lax.axis_index("tp")
    z, y, x = coords(c)
    where = jnp.stack([z, y, x, u]).astype(jnp.int32)
    model = tokens.shape[1]
    rows = tokens.shape[0] // 2
    events = rows * CHIPS
    half = model // 2
    negs = neg_emb.shape[0]
    plane = len(PLANE)

    mine = lax.dynamic_slice_in_dim(tokens, u * rows, rows, 0)
    p_own = lax.dynamic_slice_in_dim(positions, u * rows, rows, 0)
    p_other = lax.dynamic_slice_in_dim(positions, (1 - u) * rows, rows, 0)
    mine = with_marks(mine, whole_parts(p_own, 128) + whole_parts(p_other, 128))
    near = jnp.concatenate(along_z(mine))

    w_plane, near = lax.optimization_barrier((heads_in_plane(w_proj, y, x), near))
    tok = across(*beside(near))
    w_mine = heads_along_z(w_plane, z)
    w_theirs = swap_cores(w_mine)

    own_ids = lax.dynamic_slice_in_dim(neg_ids, c * negs, negs, 0)
    norms = jnp.sum(jnp.square(neg_emb.astype(F32)), axis=1)
    neg = with_marks(neg_emb, float_parts(norms) + whole_parts(own_ids, 256))
    neg_near = jnp.concatenate(along_z(after(neg, w_mine)))
    out_own = along_z(after(w_out, neg_near))
    neg_beside = beside(after(neg_near, tok))
    t_rows = target_emb.reshape(2, rows, -1)
    t_keep = pick_row(t_rows, u)
    t_send = swap_cores(pick_row(t_rows, 1 - u))

    def project(pieces):
        count = sum(p.shape[0] for p in pieces)
        return call(
            proj_kernel,
            "project",
            [((count, 2 * W), BF16)] * 2 + [((count, W), BF16)],
            [
                pltpu.VMEM((count, model + W), BF16),
                pltpu.VMEM((CHIPS, model // CHIPS, 4 * W), BF16),
                pltpu.SemaphoreType.DMA((len(pieces),)),
                pltpu.SemaphoreType.DMA((CHIPS,)),
            ],
            [where, *pieces, w_mine, w_theirs],
            "s" + (len(pieces) + 2) * "h",
            2 * count * model * 4 * W,
        )

    gq_early, kv_early, marks_early = project(tok[:3])
    kv_early_theirs = swap_cores(kv_early)
    gq_last, kv_last, marks_last = project(after(tok[3:], kv_early))
    kv_last_theirs = swap_cores(kv_last)
    (gated,) = call(
        attend_kernel,
        "attend",
        [((NZ, plane, rows, W), BF16)],
        [],
        [gq_early, gq_last, kv_early, kv_last, kv_early_theirs, kv_last_theirs]
        + [marks_early, marks_last],
        8 * "v",
        8 * events * events * W,
    )
    gated = jnp.stack([gated[0]] + [hop(gated[s], z_shift(NZ - s)) for s in range(1, NZ)])
    neg_own = jnp.concatenate(across(*after(neg_beside, gated)))
    neg_other = swap_cores(neg_own)
    out_own = after(jnp.stack(out_own), gated)
    out_other = swap_cores(out_own)
    gated = [gated] + [hop(gated, flip(by, bx)) for by, bx in PLANE[1:]]
    (hidden,) = call(
        hidden_kernel,
        "hidden",
        [((plane, rows, NZ * W), BF16)],
        [
            pltpu.VMEM((plane * rows, model), BF16),
            pltpu.VMEM((plane, rows, NZ * W), BF16),
            pltpu.VMEM((2, half, NZ * W), BF16),
            pltpu.SemaphoreType.DMA((NZ * (2 + plane),)),
        ],
        [where, *gated, out_own, out_other, *tok[:4]],
        "s" + 4 * "v" + 6 * "h",
        2 * plane * rows * model * NZ * W,
    )
    pieces = [hidden[0]] + [hop(hidden[k], flip(*PLANE[k])) for k in range(1, plane)]
    h_keep, h_send = call(
        order_kernel,
        "order",
        [((rows, half), BF16)] * 2,
        [pltpu.VMEM((rows, model), BF16)],
        [where, *pieces],
        "svvvv",
        0,
    )
    h_theirs = swap_cores(h_send)
    (loss,) = call(
        loss_kernel,
        "loss",
        [((rows, 1), F32)],
        [
            pltpu.VMEM((2, CHIPS * negs, half + W), BF16),
            pltpu.SemaphoreType.DMA((2,)),
        ],
        [h_keep, h_send, t_keep, t_send, target_ids[:, None], neg_own, neg_other],
        "vvvvvhh",
        2 * rows * model * neg_ids.shape[0],
    )
    hidden = jnp.where(
        u == 0,
        jnp.concatenate([h_keep, h_theirs]),
        jnp.concatenate([h_theirs, h_keep]),
    )
    return hidden, loss.reshape(-1)


def shards(tokens, w_proj, *rest):
    n_ctx, n_tp = lax.axis_size("ctx"), lax.axis_size("tp")
    heads = w_proj.shape[2] * n_tp // HEAD_DIM
    plan = head_shards if (n_ctx, n_tp, heads) == (CHIPS, 2, CHIPS) else general_shards
    return plan(tokens, w_proj, *rest)


def solution(mesh):
    placed = (
        P("ctx", None),
        P("ctx", None, "tp"),
        P("tp", "ctx"),
        P("ctx"),
        P("ctx", "tp"),
        P(),
        P("ctx", "tp"),
        P(("ctx", "tp")),
    )
    return jax.shard_map(
        shards,
        mesh=mesh,
        in_specs=placed,
        out_specs=(P("ctx", "tp"), P(("ctx", "tp"))),
        check_vma=False,
    )
```

time: 199 us -> 175 us (0.88)
  starting transfers between devices: 16.3 us -> 55.3 us
  blocking collectives: 31.1 us -> 0 us
  waiting for transfers between devices: 93.6 us -> 79.7 us
  between operations: 14.3 us -> 1.07 us
  other arithmetic: 11.7 us -> 8.19 us
    all_gather x2 -> x0, waiting for transfers between devices: 33.9 us -> none  [the longest x1 19.4 us: head_shards(): late = lax.all_gather(late, 'ctx', axis=0, axis_index_groups=planes)]
    all_to_all x1 -> x0, blocking collectives: 31.1 us -> none  [head_shards(): w_mine = lax.all_to_all(w_heads, 'ctx', 0, 0, tiled=True)]
    ppermute x7 -> x29, starting transfers between devices: 11.7 us -> 40.2 us  [hop(): return lax.ppermute(value, 'ctx', perm)]
    ppermute x7 -> x29, waiting for transfers between devices: 52 us -> 71.3 us  [hop(): return lax.ppermute(value, 'ctx', perm)]
    ppermute x7, starting transfers between devices: 0.77 us -> 12.7 us  [swap_cores(): return lax.ppermute(value, 'tp', SWAP)]
    ppermute x0 -> x2, waiting for transfers between devices: none -> 7.69 us  [heads_along_z(): lax.ppermute(pick_row(heads, e ^ z & 1), ('ctx', 'tp'), perm)]
    all_to_all x1 -> x0, waiting for transfers between devices: 6.29 us -> none  [head_shards(): gated = lax.all_to_all(gated, 'ctx', 0, 0, tiled=True)]
    reduce_sum x4 -> x1, other arithmetic: 5.54 us -> 0.13 us  [head_shards(): norms = jnp.sum(jnp.square(neg_emb.astype(F32)), axis=1)]
  transfers between devices with their start and end apart: 17 -> 38, of which waited for: 10 -> 22; matrix products, arithmetic and copies ran while one was open for 7% -> 7% of each run, Pallas kernels for 11% -> 10%
where the time goes in v4:
time: 175 us
  waiting for transfers between devices  79.7 us (46%)
  starting transfers between devices  55.3 us (32%)
  Pallas kernels  21 us (12%)
  local copies, waits for them, and re-layouts  9.68 us (6%)
  other arithmetic  8.19 us (5%)
    ppermute x29, waiting for transfers between devices, hop(): return lax.ppermute(value, 'ctx', perm)  71.3 us
    ppermute x29, starting transfers between devices, hop(): return lax.ppermute(value, 'ctx', perm)  40.2 us
    pallas_call x6, Pallas kernels, call(): pl.pallas_call(kernel, out_shape=[jax.ShapeDtypeStruct(shape, dtype) for...  21 us
    ppermute x7, starting transfers between devices, swap_cores(): return lax.ppermute(value, 'tp', SWAP)  12.7 us
    ppermute x2, waiting for transfers between devices, heads_along_z(): lax.ppermute(pick_row(heads, e ^ z & 1), ('ctx', 'tp'), perm)  7.69 us
    unnamed x22, local copies, waits for them, and re-layouts  5.42 us
  transfers between devices with their start and end apart: 38, of which 22 were waited for; matrix products, arithmetic and copies ran while one was open for 7% of the time, Pallas kernels for 10%

profile of v4, /device:TPU:0, one launch (start us, length us, event | category | flops | bytes accessed | tf_op | source)
XLA Modules:
  0.0 174.9 jit_solution(4378837605205543624)
XLA Ops:
  2.5 5.0 %collective-permute-start.5 = (bf16[64,2176]{1,0:T(8,128)(2,1)}, bf16[64,2176]{1,0:T(8,128)(2,1)S(1)}, u32[]{:S(2)}, u32[]{:S(2)}) collective-permute-start(bf16[64,2176]{1,0:T(8,128)(2,1)} %pad_maximum_fusion.4), channel_id=1, source_target_pairs={{0,24},{2,26},{4,28},{6,30},{8,0},{10,2},{12,4},{14,6},{16,8},{18,... | collective-permute-start | bytes 835592 | tf_op jit(solution)/shard_map/ppermute | solution.py:110
  8.5 1.9 %copy.43 = bf16[128,4,1024]{0,2,1:T(8,128)(2,1)S(1)} copy(bf16[128,4,1024]{2,1,0:T(4,128)(2,1)} %param.9) | data formatting | bytes 2097152 | tf_op args[1]
  14.4 3.7 %collective-permute-done = bf16[2,128,512]{2,1,0:T(8,128)(2,1)S(1)} collective-permute-done((bf16[2,128,512]{2,1,0:T(8,128)(2,1)S(1)}, bf16[2,128,512]{2,1,0:T(8,128)(2,1)S(1)}, u32[]{:S(2)}, u32[]{:S(2)}) %collective-permute-start) | collective-permute-done | bytes 262176 | tf_op jit(solution)/shard_map/ppermute | solution.py:110
  18.1 2.4 %collective-permute-start.2 = (bf16[2,128,512]{2,1,0:T(8,128)(2,1)S(1)}, bf16[2,128,512]{2,1,0:T(8,128)(2,1)S(1)}, u32[]{:S(2)}, u32[]{:S(2)}) collective-permute-start(bf16[2,128,512]{2,1,0:T(8,128)(2,1)S(1)} %bitcast.74), channel_id=1, source_target_pairs={{0,6},{2,4},{4,2},{6,0},{8,14},{10,12},{12,10},{14,8},{16,22},{18,... | collective-permute-start | bytes 786440 | tf_op jit(solution)/shard_map/ppermute | solution.py:110
  20.6 10.9 %collective-permute-done.4 = bf16[64,2176]{1,0:T(8,128)(2,1)S(1)} collective-permute-done((bf16[64,2176]{1,0:T(8,128)(2,1)}, bf16[64,2176]{1,0:T(8,128)(2,1)S(1)}, u32[]{:S(2)}, u32[]{:S(2)}) %collective-permute-start.4) | collective-permute-done | bytes 278560 | tf_op jit(solution)/shard_map/ppermute | solution.py:110
  40.8 7.7 %collective-permute-done.9 = bf16[4,128,512]{2,1,0:T(8,128)(2,1)S(1)} collective-permute-done((bf16[4,128,512]{2,1,0:T(8,128)(2,1)S(1)}, bf16[4,128,512]{2,1,0:T(8,128)(2,1)S(1)}, u32[]{:S(2)}, u32[]{:S(2)}) %collective-permute-start.9) | collective-permute-done | bytes 524320 | tf_op jit(solution)/shard_map/ppermute | solution.py:162
  49.6 11.9 %collective-permute-start.10 = (bf16[2,4,128,512]{3,2,1,0:T(8,128)(2,1)S(1)}, bf16[2,4,128,512]{3,2,1,0:T(8,128)(2,1)}, u32[]{:S(2)}, u32[]{:S(2)}) collective-permute-start(bf16[2,4,128,512]{3,2,1,0:T(8,128)(2,1)S(1)} %pad_maximum_fusion.2.refs_3_.refs_2_), channel_id=1, source_target_pairs={{0,1},{1,0},{2,3},{3,2},{4,5},{5,4},{6,7},{7,6},{8,9},{9,8},{10,11... | collective-permute-start | bytes 3145736 | tf_op jit(solution)/shard_map/ppermute | solution.py:114
  62.9 3.0 %collective-permute-start.23 = (bf16[64,1152]{1,0:T(8,128)(2,1)S(1)}, bf16[64,1152]{1,0:T(8,128)(2,1)S(1)}, u32[]{:S(2)}, u32[]{:S(2)}) collective-permute-start(bf16[64,1152]{1,0:T(8,128)(2,1)S(1)} %fusion.1), channel_id=1, source_target_pairs={{0,24},{2,26},{4,28},{6,30},{8,0},{10,2},{12,4},{14,6},{16,8},{18,... | collective-permute-start | bytes 442376 | tf_op jit(solution)/shard_map/ppermute | solution.py:110
  72.1 6.1 %project.2 = (bf16[768,256]{1,0:T(8,128)(2,1)S(1)}, bf16[768,256]{1,0:T(8,128)(2,1)S(1)}, bf16[768,128]{1,0:T(8,128)(2,1)S(1)}) custom-call(s32[4]{0:T(128)S(1)} %pad_add_fusion.where, bf16[256,2176]{1,0:T(8,128)(2,1)S(1)} %pad_maximum_fusion.refs_0_.refs_6_, bf16[256,2176]{1,0:T(8,128)(2,1)} %collective-permute-done.6.refs_1_.refs_7_, ...), custom_call_target="tpu_custom_call" | custom-call | flops 1610612736 | bytes 5439504 | tf_op jit(solution)/shard_map/project/pallas_call | solution.py:333
  78.3 2.7 %collective-permute-done.11.refs_0_.refs_9_ = bf16[128,2176]{1,0:T(8,128)(2,1)S(1)} collective-permute-done((bf16[128,2176]{1,0:T(8,128)(2,1)S(1)}, bf16[128,2176]{1,0:T(8,128)(2,1)S(1)}, u32[]{:S(2)}, u32[]{:S(2)}) %collective-permute-start.11) | collective-permute-done | bytes 557088 | tf_op jit(solution)/shard_map/ppermute | solution.py:110
  81.0 2.4 %collective-permute-done.12.refs_1_ = bf16[128,2176]{1,0:T(8,128)(2,1)S(1)} collective-permute-done((bf16[128,2176]{1,0:T(8,128)(2,1)S(1)}, bf16[128,2176]{1,0:T(8,128)(2,1)S(1)}, u32[]{:S(2)}, u32[]{:S(2)}) %collective-permute-start.12) | collective-permute-done | bytes 557088 | tf_op jit(solution)/shard_map/ppermute | solution.py:110
  83.4 4.1 %project.3 = (bf16[256,256]{1,0:T(8,128)(2,1)S(1)}, bf16[256,256]{1,0:T(8,128)(2,1)S(1)}, bf16[256,128]{1,0:T(8,128)(2,1)S(1)}) custom-call(s32[4]{0:T(128)S(1)} %pad_add_fusion.where, bf16[128,2176]{1,0:T(8,128)(2,1)S(1)} %collective-permute-done.11.refs_0_.refs_9_, bf16[128,2176]{1,0:T(8,128)(2,1)S(1)} %collective-permute-done.12.refs_1_, ...), custom_call_target="tpu_custom_call" | custom-call | flops 536870912 | bytes 3211280 | tf_op jit(solution)/shard_map/project/pallas_call | solution.py:333
  90.6 3.5 %attend.1 = bf16[4,4,64,128]{3,2,1,0:T(8,128)(2,1)S(1)} custom-call(bf16[768,256]{1,0:T(8,128)(2,1)S(1)} %get-tuple-element.25.refs_0_, bf16[256,256]{1,0:T(8,128)(2,1)S(1)} %get-tuple-element.29.refs_1_, bf16[768,256]{1,0:T(8,128)(2,1)S(1)} %get-tuple-element.26.refs_2_, bf16[256,256]{1,0:T(8,128)(2,1)S(1)} %get-tuple-element.30.refs_3_, ...), custom_call_target="tpu_custom_call" | custom-call | flops 1073741824 | bytes 1835008 | tf_op jit(solution)/shard_map/attend/pallas_call | solution.py:333
  95.1 2.9 %collective-permute-start.15 = (bf16[4,64,128]{2,1,0:T(8,128)(2,1)S(1)}, bf16[4,64,128]{2,1,0:T(8,128)(2,1)S(1)}, u32[]{:S(2)}, u32[]{:S(2)}) collective-permute-start(bf16[4,64,128]{2,1,0:T(8,128)(2,1)S(1)} %get-tuple-element.63), channel_id=1, source_target_pairs={{0,24},{2,26},{4,28},{6,30},{8,0},{10,2},{12,4},{14,6},{16,8},{18,... | collective-permute-start | bytes 196616 | tf_op jit(solution)/shard_map/ppermute | solution.py:110
  98.0 2.9 %collective-permute-done.17 = bf16[4,64,128]{2,1,0:T(8,128)(2,1)S(1)} collective-permute-done((bf16[4,64,128]{2,1,0:T(8,128)(2,1)S(1)}, bf16[4,64,128]{2,1,0:T(8,128)(2,1)S(1)}, u32[]{:S(2)}, u32[]{:S(2)}) %collective-permute-start.17) | collective-permute-done | bytes 65568 | tf_op jit(solution)/shard_map/ppermute | solution.py:110
  100.9 1.7 collective-permute-done.16
  109.3 4.6 %collective-permute-done.35 = bf16[128,1152]{1,0:T(8,128)(2,1)S(1)} collective-permute-done((bf16[128,1152]{1,0:T(8,128)(2,1)S(1)}, bf16[128,1152]{1,0:T(8,128)(2,1)S(1)}, u32[]{:S(2)}, u32[]{:S(2)}) %collective-permute-start.35) | collective-permute-done | bytes 294944 | tf_op jit(solution)/shard_map/ppermute | solution.py:110
  119.6 6.8 %collective-permute-done.26 = bf16[1024,128]{1,0:T(8,128)(2,1)S(1)} collective-permute-done((bf16[1024,128]{1,0:T(8,128)(2,1)S(1)}, bf16[1024,128]{1,0:T(8,128)(2,1)S(1)}, u32[]{:S(2)}, u32[]{:S(2)}) %collective-permute-start.26) | collective-permute-done | bytes 262176 | tf_op jit(solution)/shard_map/ppermute | solution.py:110
  126.4 15.2 %collective-permute-done.25 = bf16[1024,128]{1,0:T(8,128)(2,1)S(1)} collective-permute-done((bf16[1024,128]{1,0:T(8,128)(2,1)S(1)}, bf16[1024,128]{1,0:T(8,128)(2,1)S(1)}, u32[]{:S(2)}, u32[]{:S(2)}) %collective-permute-start.25) | collective-permute-done | bytes 262176 | tf_op jit(solution)/shard_map/ppermute | solution.py:110
  145.4 5.6 %collective-permute-done.18.refs_1_ = bf16[4,4,64,128]{3,2,1,0:T(8,128)(2,1)S(1)} collective-permute-done((bf16[4,4,64,128]{3,2,1,0:T(8,128)(2,1)S(1)}, bf16[4,4,64,128]{3,2,1,0:T(8,128)(2,1)S(1)}, u32[]{:S(2)}, u32[]{:S(2)}) %collective-permute-start.18) | collective-permute-done | bytes 262176 | tf_op jit(solution)/shard_map/ppermute | solution.py:110
  151.0 4.8 %collective-permute-done.19.refs_2_ = bf16[4,4,64,128]{3,2,1,0:T(8,128)(2,1)S(1)} collective-permute-done((bf16[4,4,64,128]{3,2,1,0:T(8,128)(2,1)S(1)}, bf16[4,4,64,128]{3,2,1,0:T(8,128)(2,1)S(1)}, u32[]{:S(2)}, u32[]{:S(2)}) %collective-permute-start.19) | collective-permute-done | bytes 262176 | tf_op jit(solution)/shard_map/ppermute | solution.py:110
  157.2 2.6 %hidden.1 = bf16[4,64,512]{2,1,0:T(8,128)(2,1)S(1)} custom-call(s32[4]{0:T(128)S(1)} %pad_add_fusion.where, bf16[4,4,64,128]{3,2,1,0:T(8,128)(2,1)S(1)} %pad_maximum_fusion.5.refs_0_, bf16[4,4,64,128]{3,2,1,0:T(8,128)(2,1)S(1)} %collective-permute-done.18.refs_1_, bf16[4,4,64,128]{3,2,1,0:T(8,128)(2,1)S(1)} %collective-permute-done.19.refs_2_, ...), custom_call_target="tpu_custom_call" | custom-call | flops 536870912 | bytes 7045136 | tf_op jit(solution)/shard_map/hidden/pallas_call | solution.py:333
  165.7 1.7 collective-permute-done.30.refs_3_
  170.2 4.1 %loss.1 = f32[64,1]{1,0:T(8,128)S(1)} custom-call(bf16[64,1024]{1,0:T(8,128)(2,1)S(1)} %get-tuple-element.36.h_keep, bf16[64,1024]{1,0:T(8,128)(2,1)S(1)} %get-tuple-element.37.h_send, bf16[64,1024]{1,0:T(8,128)(2,1)S(1)} %get-tuple-element.55.t_keep, bf16[64,1024]{1,0:T(8,128)(2,1)S(1)} %collective-permute-done.32.t_send, s32[64,1]{1,0:T(8,128)S(1)} %copy.51.t_ids, ...), custom_call_target="tpu_custom_call" | custom-call | flops 268435456 | bytes 5243136 | tf_op jit(solution)/shard_map/loss/pallas_call | solution.py:333
  (119 shorter events, 55.6 us)
Async XLA Ops:
  2.5 18.1 %collective-permute-start.5 = (bf16[64,2176]{1,0:T(8,128)(2,1)}, bf16[64,2176]{1,0:T(8,128)(2,1)S(1)}, u32[]{:S(2)}, u32[]{:S(2)}) collective-permute-start(bf16[64,2176]{1,0:T(8,128)(2,1)} %pad_maximum_fusion.4), channel_id=1, source_target_pairs={{0,24},{2,26},{4,28},{6,30},{8,0},{10,2},{12,4},{14,6},{16,8},{18,... | collective-permute-start | bytes 835592 | tf_op jit(solution)/shard_map/ppermute | solution.py:110
  7.5 23.9 %collective-permute-start.4 = (bf16[64,2176]{1,0:T(8,128)(2,1)}, bf16[64,2176]{1,0:T(8,128)(2,1)S(1)}, u32[]{:S(2)}, u32[]{:S(2)}) collective-permute-start(bf16[64,2176]{1,0:T(8,128)(2,1)} %pad_maximum_fusion.4), channel_id=1, source_target_pairs={{0,16},{2,18},{4,20},{6,22},{8,24},{10,26},{12,28},{14,30},{16,0},... | collective-permute-start | bytes 835592 | tf_op jit(solution)/shard_map/ppermute | solution.py:110
  7.5 23.9 %collective-permute-start.3 = (bf16[64,2176]{1,0:T(8,128)(2,1)}, bf16[64,2176]{1,0:T(8,128)(2,1)}, u32[]{:S(2)}, u32[]{:S(2)}) collective-permute-start(bf16[64,2176]{1,0:T(8,128)(2,1)} %pad_maximum_fusion.4), channel_id=1, source_target_pairs={{0,8},{2,10},{4,12},{6,14},{8,16},{10,18},{12,20},{14,22},{16,24},... | collective-permute-start | bytes 835592 | tf_op jit(solution)/shard_map/ppermute | solution.py:110
  12.5 20.0 %collective-permute-start.1 = (bf16[2,128,512]{2,1,0:T(8,128)(2,1)S(1)}, bf16[2,128,512]{2,1,0:T(8,128)(2,1)}, u32[]{:S(2)}, u32[]{:S(2)}) collective-permute-start(bf16[2,128,512]{2,1,0:T(8,128)(2,1)S(1)} %bitcast.72), channel_id=1, source_target_pairs={{0,4},{2,6},{4,0},{6,2},{8,12},{10,14},{12,8},{14,10},{16,20},{18,... | collective-permute-start | bytes 786440 | tf_op jit(solution)/shard_map/ppermute | solution.py:110
  18.1 14.4 %collective-permute-start.2 = (bf16[2,128,512]{2,1,0:T(8,128)(2,1)S(1)}, bf16[2,128,512]{2,1,0:T(8,128)(2,1)S(1)}, u32[]{:S(2)}, u32[]{:S(2)}) collective-permute-start(bf16[2,128,512]{2,1,0:T(8,128)(2,1)S(1)} %bitcast.74), channel_id=1, source_target_pairs={{0,6},{2,4},{4,2},{6,0},{8,14},{10,12},{12,10},{14,8},{16,22},{18,... | collective-permute-start | bytes 786440 | tf_op jit(solution)/shard_map/ppermute | solution.py:110
  33.8 14.7 %collective-permute-start.9 = (bf16[4,128,512]{2,1,0:T(8,128)(2,1)S(1)}, bf16[4,128,512]{2,1,0:T(8,128)(2,1)S(1)}, u32[]{:S(2)}, u32[]{:S(2)}) collective-permute-start(bf16[4,128,512]{2,1,0:T(8,128)(2,1)S(1)} %get-tuple-element.49), channel_id=1, source_target_pairs={{0,8},{1,24},{2,10},{3,26},{4,12},{5,28},{6,14},{7,30},{8,0},{9,16... | collective-permute-start | bytes 1572872 | tf_op jit(solution)/shard_map/ppermute | solution.py:162
  34.8 13.7 %collective-permute-start.8 = (bf16[4,128,512]{2,1,0:T(8,128)(2,1)S(1)}, bf16[4,128,512]{2,1,0:T(8,128)(2,1)}, u32[]{:S(2)}, u32[]{:S(2)}) collective-permute-start(bf16[4,128,512]{2,1,0:T(8,128)(2,1)S(1)} %get-tuple-element.48), channel_id=1, source_target_pairs={{0,0},{1,16},{2,2},{3,18},{4,4},{5,20},{6,6},{7,22},{8,8},{9,24},{... | collective-permute-start | bytes 1572872 | tf_op jit(solution)/shard_map/ppermute | solution.py:162
  37.0 25.9 %collective-permute-start.6 = (bf16[256,2176]{1,0:T(8,128)(2,1)S(1)}, bf16[256,2176]{1,0:T(8,128)(2,1)}, u32[]{:S(2)}, u32[]{:S(2)}) collective-permute-start(bf16[256,2176]{1,0:T(8,128)(2,1)S(1)} %pad_maximum_fusion.refs_0_.refs_6_), channel_id=1, source_target_pairs={{0,2},{2,0},{4,6},{6,4},{8,10},{10,8},{12,14},{14,12},{16,18},{18,... | collective-permute-start | bytes 3342344 | tf_op jit(solution)/shard_map/ppermute | solution.py:110
  38.5 28.5 %collective-permute-start.7 = (bf16[256,2176]{1,0:T(8,128)(2,1)S(1)}, bf16[256,2176]{1,0:T(8,128)(2,1)}, u32[]{:S(2)}, u32[]{:S(2)}) collective-permute-start(bf16[256,2176]{1,0:T(8,128)(2,1)S(1)} %pad_maximum_fusion.refs_0_.refs_6_), channel_id=1, source_target_pairs={{0,4},{2,6},{4,0},{6,2},{8,12},{10,14},{12,8},{14,10},{16,20},{18,... | collective-permute-start | bytes 3342344 | tf_op jit(solution)/shard_map/ppermute | solution.py:110
  49.6 22.5 %collective-permute-start.10 = (bf16[2,4,128,512]{3,2,1,0:T(8,128)(2,1)S(1)}, bf16[2,4,128,512]{3,2,1,0:T(8,128)(2,1)}, u32[]{:S(2)}, u32[]{:S(2)}) collective-permute-start(bf16[2,4,128,512]{3,2,1,0:T(8,128)(2,1)S(1)} %pad_maximum_fusion.2.refs_3_.refs_2_), channel_id=1, source_target_pairs={{0,1},{1,0},{2,3},{3,2},{4,5},{5,4},{6,7},{7,6},{8,9},{9,8},{10,11... | collective-permute-start | bytes 3145736 | tf_op jit(solution)/shard_map/ppermute | solution.py:114
  62.0 16.3 %collective-permute-start.22 = (bf16[64,1152]{1,0:T(8,128)(2,1)S(1)}, bf16[64,1152]{1,0:T(8,128)(2,1)S(1)}, u32[]{:S(2)}, u32[]{:S(2)}) collective-permute-start(bf16[64,1152]{1,0:T(8,128)(2,1)S(1)} %fusion.1), channel_id=1, source_target_pairs={{0,16},{2,18},{4,20},{6,22},{8,24},{10,26},{12,28},{14,30},{16,0},... | collective-permute-start | bytes 442376 | tf_op jit(solution)/shard_map/ppermute | solution.py:110
  62.9 24.7 %collective-permute-start.23 = (bf16[64,1152]{1,0:T(8,128)(2,1)S(1)}, bf16[64,1152]{1,0:T(8,128)(2,1)S(1)}, u32[]{:S(2)}, u32[]{:S(2)}) collective-permute-start(bf16[64,1152]{1,0:T(8,128)(2,1)S(1)} %fusion.1), channel_id=1, source_target_pairs={{0,24},{2,26},{4,28},{6,30},{8,0},{10,2},{12,4},{14,6},{16,8},{18,... | collective-permute-start | bytes 442376 | tf_op jit(solution)/shard_map/ppermute | solution.py:110
  67.0 14.0 %collective-permute-start.11 = (bf16[128,2176]{1,0:T(8,128)(2,1)S(1)}, bf16[128,2176]{1,0:T(8,128)(2,1)S(1)}, u32[]{:S(2)}, u32[]{:S(2)}) collective-permute-start(bf16[128,2176]{1,0:T(8,128)(2,1)S(1)} %slice.48), channel_id=1, source_target_pairs={{0,4},{2,6},{4,0},{6,2},{8,12},{10,14},{12,8},{14,10},{16,20},{18,... | collective-permute-start | bytes 1671176 | tf_op jit(solution)/shard_map/ppermute | solution.py:110
  70.5 12.9 %collective-permute-start.12 = (bf16[128,2176]{1,0:T(8,128)(2,1)S(1)}, bf16[128,2176]{1,0:T(8,128)(2,1)S(1)}, u32[]{:S(2)}, u32[]{:S(2)}) collective-permute-start(bf16[128,2176]{1,0:T(8,128)(2,1)S(1)} %slice.49), channel_id=1, source_target_pairs={{0,2},{2,0},{4,6},{6,4},{8,10},{10,8},{12,14},{14,12},{16,18},{18,... | collective-permute-start | bytes 1671176 | tf_op jit(solution)/shard_map/ppermute | solution.py:110
  78.2 12.4 %collective-permute-start.13 = (bf16[768,256]{1,0:T(8,128)(2,1)S(1)}, bf16[768,256]{1,0:T(8,128)(2,1)S(1)}, u32[]{:S(2)}, u32[]{:S(2)}) collective-permute-start(bf16[768,256]{1,0:T(8,128)(2,1)S(1)} %get-tuple-element.26.refs_2_), channel_id=1, source_target_pairs={{0,1},{1,0},{2,3},{3,2},{4,5},{5,4},{6,7},{7,6},{8,9},{9,8},{10,11... | collective-permute-start | bytes 1179656 | tf_op jit(solution)/shard_map/ppermute | solution.py:114
  87.7 15.8 %collective-permute-start.33 = (bf16[256,1152]{1,0:T(8,128)(2,1)S(1)}, bf16[256,1152]{1,0:T(8,128)(2,1)S(1)}, u32[]{:S(2)}, u32[]{:S(2)}) collective-permute-start(bf16[256,1152]{1,0:T(8,128)(2,1)S(1)} %constant_dynamic-update-slice_fusion), channel_id=1, source_target_pairs={{0,2},{2,0},{4,6},{6,4},{8,10},{10,8},{12,14},{14,12},{16,18},{18,... | collective-permute-start | bytes 1769480 | tf_op jit(solution)/shard_map/ppermute | solution.py:110
  89.2 15.4 %collective-permute-start.34 = (bf16[256,1152]{1,0:T(8,128)(2,1)S(1)}, bf16[256,1152]{1,0:T(8,128)(2,1)S(1)}, u32[]{:S(2)}, u32[]{:S(2)}) collective-permute-start(bf16[256,1152]{1,0:T(8,128)(2,1)S(1)} %constant_dynamic-update-slice_fusion), channel_id=1, source_target_pairs={{0,4},{2,6},{4,0},{6,2},{8,12},{10,14},{12,8},{14,10},{16,20},{18,... | collective-permute-start | bytes 1769480 | tf_op jit(solution)/shard_map/ppermute | solution.py:110
  116.7 53.5 %collective-permute-start.37 = (bf16[1024,1152]{1,0:T(8,128)(2,1)}, bf16[1024,1152]{1,0:T(8,128)(2,1)}, u32[]{:S(2)}, u32[]{:S(2)}) collective-permute-start(bf16[1024,1152]{1,0:T(8,128)(2,1)} %constant_dynamic-update-slice_fusion.4.n_own), channel_id=1, source_target_pairs={{0,1},{1,0},{2,3},{3,2},{4,5},{5,4},{6,7},{7,6},{8,9},{9,8},{10,11... | collective-permute-start | bytes 7077896 | tf_op jit(solution)/shard_map/ppermute | solution.py:114
  116.7 9.8 %collective-permute-start.26 = (bf16[1024,128]{1,0:T(8,128)(2,1)S(1)}, bf16[1024,128]{1,0:T(8,128)(2,1)S(1)}, u32[]{:S(2)}, u32[]{:S(2)}) collective-permute-start(bf16[1024,128]{1,0:T(8,128)(2,1)S(1)} %copy-done.3), channel_id=1, source_target_pairs={{0,24},{2,26},{4,28},{6,30},{8,0},{10,2},{12,4},{14,6},{16,8},{18,... | collective-permute-start | bytes 786440 | tf_op jit(solution)/shard_map/ppermute | solution.py:110
  116.7 25.0 %collective-permute-start.25 = (bf16[1024,128]{1,0:T(8,128)(2,1)S(1)}, bf16[1024,128]{1,0:T(8,128)(2,1)S(1)}, u32[]{:S(2)}, u32[]{:S(2)}) collective-permute-start(bf16[1024,128]{1,0:T(8,128)(2,1)S(1)} %copy-done.3), channel_id=1, source_target_pairs={{0,16},{2,18},{4,20},{6,22},{8,24},{10,26},{12,28},{14,30},{16,0},... | collective-permute-start | bytes 786440 | tf_op jit(solution)/shard_map/ppermute | solution.py:110
  118.1 23.5 %collective-permute-start.24 = (bf16[1024,128]{1,0:T(8,128)(2,1)S(1)}, bf16[1024,128]{1,0:T(8,128)(2,1)S(1)}, u32[]{:S(2)}, u32[]{:S(2)}) collective-permute-start(bf16[1024,128]{1,0:T(8,128)(2,1)S(1)} %copy-done.3), channel_id=1, source_target_pairs={{0,8},{2,10},{4,12},{6,14},{8,16},{10,18},{12,20},{14,22},{16,24},... | collective-permute-start | bytes 786440 | tf_op jit(solution)/shard_map/ppermute | solution.py:110
  141.8 15.4 %collective-permute-start.27 = (bf16[4,1024,128]{2,1,0:T(8,128)(2,1)S(1)}, bf16[4,1024,128]{2,1,0:T(8,128)(2,1)S(1)}, u32[]{:S(2)}, u32[]{:S(2)}) collective-permute-start(bf16[4,1024,128]{2,1,0:T(8,128)(2,1)S(1)} %pad_maximum_fusion.3.refs_4_), channel_id=1, source_target_pairs={{0,1},{1,0},{2,3},{3,2},{4,5},{5,4},{6,7},{7,6},{8,9},{9,8},{10,11... | collective-permute-start | bytes 3145736 | tf_op jit(solution)/shard_map/ppermute | solution.py:114
  142.8 13.1 %collective-permute-start.19 = (bf16[4,4,64,128]{3,2,1,0:T(8,128)(2,1)S(1)}, bf16[4,4,64,128]{3,2,1,0:T(8,128)(2,1)S(1)}, u32[]{:S(2)}, u32[]{:S(2)}) collective-permute-start(bf16[4,4,64,128]{3,2,1,0:T(8,128)(2,1)S(1)} %pad_maximum_fusion.5.refs_0_), channel_id=1, source_target_pairs={{0,4},{2,6},{4,0},{6,2},{8,12},{10,14},{12,8},{14,10},{16,20},{18,... | collective-permute-start | bytes 786440 | tf_op jit(solution)/shard_map/ppermute | solution.py:110
  144.3 12.9 %collective-permute-start.20 = (bf16[4,4,64,128]{3,2,1,0:T(8,128)(2,1)S(1)}, bf16[4,4,64,128]{3,2,1,0:T(8,128)(2,1)S(1)}, u32[]{:S(2)}, u32[]{:S(2)}) collective-permute-start(bf16[4,4,64,128]{3,2,1,0:T(8,128)(2,1)S(1)} %pad_maximum_fusion.5.refs_0_), channel_id=1, source_target_pairs={{0,6},{2,4},{4,2},{6,0},{8,14},{10,12},{12,10},{14,8},{16,22},{18,... | collective-permute-start | bytes 786440 | tf_op jit(solution)/shard_map/ppermute | solution.py:110
  (21 other events, 193.3 us)

commit v5 on v4

--- a/solution.py
+++ b/solution.py
@@ -126,28 +126,29 @@
     return [own] + [hop(own, z_shift(s)) for s in range(1, NZ)]
 
 
-def beside(near):
-    return [near, hop(near, flip(0, 1)), hop(near, flip(1, 0))]
-
-
-def across(near, beside_x, beside_y):
-    half = near.shape[0] // 2
-    first = hop(beside_x[:half], flip(1, 0))
-    second = hop(beside_y[half:], flip(0, 1))
-    return [near, beside_x, beside_y, first, second]
+def in_plane(low, high):
+    to_x, to_y = flip(0, 1), flip(1, 0)
+    low_x, high_y = hop(low, to_x), hop(high, to_y)
+    high_x, low_y = hop(high, to_x), hop(low, to_y)
+    return [low, high, low_x, high_x, low_y, high_y, hop(low_x, to_y), hop(high_y, to_x)]
 
 
 def heads_in_plane(w_proj, y, x):
     plane = NY * NX
     heads = w_proj.reshape(-1, 4, 2, plane, W).transpose(3, 2, 0, 1, 4)
     heads = heads.reshape(plane, 2, -1, 4 * W)
-    out = []
+    out = jnp.zeros((2, plane, *heads.shape[2:]), heads.dtype)
+    first = None
     for by, bx in PLANE:
-        piece = pick_row(heads, (y ^ by) * NX + (x ^ bx))
+        spot = (y ^ by) * NX + (x ^ bx)
+        piece = pick_row(heads, spot)
         if (by, bx) == PLANE[-1]:
-            piece = after(piece, out[1])
-        out.append(piece if (by, bx) == (0, 0) else hop(piece, flip(by, bx)))
-    return jnp.stack(out, 1)
+            piece = after(piece, first)
+        if (by, bx) != (0, 0):
+            piece = hop(piece, flip(by, bx))
+            first = piece if first is None else first
+        out = lax.dynamic_update_slice_in_dim(out, piece[:, None], spot, 1)
+    return out
 
 
 def heads_along_z(heads, z):
@@ -160,7 +161,8 @@
                 dst = chip_at(2 * t + (e ^ (sz & 1)), sy, sx)
                 perm.append((2 * src + t, 2 * dst + (sz >> 1)))
         arrived.append(lax.ppermute(pick_row(heads, e ^ (z & 1)), ("ctx", "tp"), perm))
-    return jnp.stack(arrived)
+    rows = jnp.where(z % 2 == 0, jnp.stack(arrived), jnp.stack(arrived[::-1]))
+    return rows.reshape(-1, rows.shape[-1])
 
 
 def silu(v):
@@ -178,22 +180,19 @@
     count = len(refs) - 9
     tok, (w_own, w_other) = refs[:count], refs[count : count + 2]
     gate_query, value_key, marks, x_all, w_all, tok_sem, w_sem = refs[count + 2 :]
-    z, y, x, u = (where[i] for i in range(4))
+    u = where[3]
     copies, base = [], 0
-    for side, (half, src) in enumerate(((u, w_own), (1 - u, w_other))):
-        for e in range(2):
-            for k, (by, bx) in enumerate(PLANE):
-                block = chip_at(2 * half + (e ^ (z & 1)), y ^ by, x ^ bx)
-                sem = w_sem.at[(side * 2 + e) * len(PLANE) + k]
-                copies.append(pltpu.make_async_copy(src.at[e, k], w_all.at[block], sem))
+    half = w_own.shape[0]
+    for side, (at, src) in enumerate(((u, w_own), (1 - u, w_other))):
+        rows = pl.ds(pl.multiple_of(at * half, half), half)
+        copies.append(pltpu.make_async_copy(src, w_all.at[rows, :], w_sem.at[side]))
     for i, ref in enumerate(tok):
         rows = pl.ds(base, ref.shape[0])
         copies.append(pltpu.make_async_copy(ref, x_all.at[rows, :], tok_sem.at[i]))
         base += ref.shape[0]
     run_copies(copies)
-    weights = w_all[...].reshape(-1, w_all.shape[-1])
-    model = weights.shape[0]
-    total = jnp.dot(x_all[:, :model], weights, preferred_element_type=F32)
+    model = w_all.shape[0]
+    total = jnp.dot(x_all[:, :model], w_all[...], preferred_element_type=F32)
     proj = silu(total).astype(BF16)
     gate_query[:, :W] = proj[:, :W]
     value_key[:, :W] = proj[:, W : 2 * W]
@@ -377,19 +376,19 @@
     p_own = lax.dynamic_slice_in_dim(positions, u * rows, rows, 0)
     p_other = lax.dynamic_slice_in_dim(positions, (1 - u) * rows, rows, 0)
     mine = with_marks(mine, whole_parts(p_own, 128) + whole_parts(p_other, 128))
-    near = jnp.concatenate(along_z(mine))
-
-    w_plane, near = lax.optimization_barrier((heads_in_plane(w_proj, y, x), near))
-    tok = across(*beside(near))
+    line = along_z(mine)
+
+    w_plane, line = lax.optimization_barrier((heads_in_plane(w_proj, y, x), line))
+    tok = in_plane(jnp.concatenate(line[:2]), jnp.concatenate(line[2:]))
     w_mine = heads_along_z(w_plane, z)
+    w_mine = after(w_mine, tok[2:6])
     w_theirs = swap_cores(w_mine)
 
     own_ids = lax.dynamic_slice_in_dim(neg_ids, c * negs, negs, 0)
     norms = jnp.sum(jnp.square(neg_emb.astype(F32)), axis=1)
     neg = with_marks(neg_emb, float_parts(norms) + whole_parts(own_ids, 256))
-    neg_near = jnp.concatenate(along_z(after(neg, w_mine)))
-    out_own = along_z(after(w_out, neg_near))
-    neg_beside = beside(after(neg_near, tok))
+    neg_own = lax.all_gather(neg, "ctx", axis=0, tiled=True)
+    out_own = along_z(after(w_out, w_mine))
     t_rows = target_emb.reshape(2, rows, -1)
     t_keep = pick_row(t_rows, u)
     t_send = swap_cores(pick_row(t_rows, 1 - u))
@@ -402,19 +401,20 @@
             [((count, 2 * W), BF16)] * 2 + [((count, W), BF16)],
             [
                 pltpu.VMEM((count, model + W), BF16),
-                pltpu.VMEM((CHIPS, model // CHIPS, 4 * W), BF16),
+                pltpu.VMEM((model, 4 * W), BF16),
                 pltpu.SemaphoreType.DMA((len(pieces),)),
-                pltpu.SemaphoreType.DMA((CHIPS,)),
+                pltpu.SemaphoreType.DMA((2,)),
             ],
             [where, *pieces, w_mine, w_theirs],
             "s" + (len(pieces) + 2) * "h",
             2 * count * model * 4 * W,
         )
 
-    gq_early, kv_early, marks_early = project(tok[:3])
+    gq_early, kv_early, marks_early = project(tok[:6])
     kv_early_theirs = swap_cores(kv_early)
-    gq_last, kv_last, marks_last = project(after(tok[3:], kv_early))
+    gq_last, kv_last, marks_last = project(after(tok[6:], kv_early))
     kv_last_theirs = swap_cores(kv_last)
+    kv_last_theirs = after(kv_last_theirs, out_own)
     (gated,) = call(
         attend_kernel,
         "attend",
@@ -426,7 +426,7 @@
         8 * events * events * W,
     )
     gated = jnp.stack([gated[0]] + [hop(gated[s], z_shift(NZ - s)) for s in range(1, NZ)])
-    neg_own = jnp.concatenate(across(*after(neg_beside, gated)))
+    neg_own = after(neg_own, gated)
     neg_other = swap_cores(neg_own)
     out_own = after(jnp.stack(out_own), gated)
     out_other = swap_cores(out_own)
@@ -441,7 +441,7 @@
             pltpu.VMEM((2, half, NZ * W), BF16),
             pltpu.SemaphoreType.DMA((NZ * (2 + plane),)),
         ],
-        [where, *gated, out_own, out_other, *tok[:4]],
+        [where, *gated, out_own, out_other, *tok[:5:2], tok[6]],
         "s" + 4 * "v" + 6 * "h",
         2 * plane * rows * model * NZ * W,
     )

time: 175 us -> 183 us (1.046)
  waiting for transfers between devices: 79.7 us -> 65.3 us
  between operations: 1.07 us -> 14.4 us
  local copies, waits for them, and re-layouts: 9.68 us -> 23 us
  Pallas kernels: 21 us -> 15.7 us
    ppermute x29 -> x24, waiting for transfers between devices: 71.3 us -> 53 us  [hop(): return lax.ppermute(value, 'ctx', perm)]
    ppermute x2, starting transfers between devices: 2.49 us -> 13 us  [heads_along_z(): lax.ppermute(pick_row(heads, e ^ z & 1), ('ctx', 'tp'), perm)]
    ppermute x7, starting transfers between devices: 12.7 us -> 2.25 us  [swap_cores(): return lax.ppermute(value, 'tp', SWAP)]
    unnamed x22 -> x41, local copies, waits for them, and re-layouts: 5.42 us -> 12.1 us
    pallas_call x6, Pallas kernels: 21 us -> 15.7 us  [call(): pl.pallas_call(kernel, out_shape=[jax.ShapeDtypeStruct(shape, dtype) for...]
    squeeze x2, local copies, waits for them, and re-layouts: 0.11 us -> 3.75 us  [pick_row(): return lax.dynamic_index_in_dim(value, at, 0, keepdims=False)]
    ppermute x2, waiting for transfers between devices: 7.69 us -> 11 us  [heads_along_z(): lax.ppermute(pick_row(heads, e ^ z & 1), ('ctx', 'tp'), perm)]
    dynamic_update_slice x0 -> x4, local copies, waits for them, and re-layouts: none -> 2.87 us  [heads_in_plane(): out = lax.dynamic_update_slice_in_dim(out, piece[:, None], spot, 1)]
  transfers between devices with their start and end apart: 38 -> 34, of which waited for: 22 -> 15; matrix products, arithmetic and copies ran while one was open for 7% -> 10% of each run, Pallas kernels for 10% -> 7%
where the time goes in v5:
time: 183 us; the launch traced here: 182 us
  waiting for transfers between devices  65.3 us (36%)
  starting transfers between devices  55.6 us (30%)
  local copies, waits for them, and re-layouts  23 us (13%)
  Pallas kernels  15.7 us (9%)
  between operations  14.4 us (8%)
  other arithmetic  7.55 us (4%)
    ppermute x24, waiting for transfers between devices, hop(): return lax.ppermute(value, 'ctx', perm)  53 us
    ppermute x24, starting transfers between devices, hop(): return lax.ppermute(value, 'ctx', perm)  40.3 us
    pallas_call x6, Pallas kernels, call(): pl.pallas_call(kernel, out_shape=[jax.ShapeDtypeStruct(shape, dtype) for...  15.7 us
    ppermute x2, starting transfers between devices, heads_along_z(): lax.ppermute(pick_row(heads, e ^ z & 1), ('ctx', 'tp'), perm)  13 us
    unnamed x41, local copies, waits for them, and re-layouts  12.1 us
    ppermute x2, waiting for transfers between devices, heads_along_z(): lax.ppermute(pick_row(heads, e ^ z & 1), ('ctx', 'tp'), perm)  11 us
    squeeze x2, local copies, waits for them, and re-layouts, pick_row(): return lax.dynamic_index_in_dim(value, at, 0, keepdims=False)  3.75 us
  transfers between devices with their start and end apart: 34, of which 15 were waited for; matrix products, arithmetic and copies ran while one was open for 10% of the time, Pallas kernels for 7%

profile of v5, /device:TPU:0, one launch (start us, length us, event | category | flops | bytes accessed | tf_op | source)
XLA Modules:
  0.0 181.5 jit_solution(7352651230154870161)
XLA Ops:
  8.3 3.1 %collective-permute-start.3 = (bf16[64,2176]{1,0:T(8,128)(2,1)S(1)}, bf16[64,2176]{1,0:T(8,128)(2,1)}, u32[]{:S(2)}, u32[]{:S(2)}) collective-permute-start(bf16[64,2176]{1,0:T(8,128)(2,1)S(1)} %fusion.2), channel_id=1, source_target_pairs={{0,8},{2,10},{4,12},{6,14},{8,16},{10,18},{12,20},{14,22},{16,24},... | collective-permute-start | bytes 835592 | tf_op jit(solution)/shard_map/ppermute | solution.py:110
  11.4 2.6 %collective-permute-start.4 = (bf16[64,2176]{1,0:T(8,128)(2,1)S(1)}, bf16[64,2176]{1,0:T(8,128)(2,1)S(1)}, u32[]{:S(2)}, u32[]{:S(2)}) collective-permute-start(bf16[64,2176]{1,0:T(8,128)(2,1)S(1)} %fusion.2), channel_id=1, source_target_pairs={{0,16},{2,18},{4,20},{6,22},{8,24},{10,26},{12,28},{14,30},{16,0},... | collective-permute-start | bytes 835592 | tf_op jit(solution)/shard_map/ppermute | solution.py:110
  15.3 1.9 %copy.55 = bf16[128,4,1024]{0,2,1:T(8,128)(2,1)S(1)} copy(bf16[128,4,1024]{2,1,0:T(4,128)(2,1)} %param.9) | data formatting | bytes 2097152 | tf_op args[1]
  25.6 1.8 collective-permute-start.2
  28.8 5.5 %collective-permute-done.2 = bf16[2,128,512]{2,1,0:T(8,128)(2,1)S(1)} collective-permute-done((bf16[2,128,512]{2,1,0:T(8,128)(2,1)S(1)}, bf16[2,128,512]{2,1,0:T(8,128)(2,1)S(1)}, u32[]{:S(2)}, u32[]{:S(2)}) %collective-permute-start.2) | collective-permute-done | bytes 262176 | tf_op jit(solution)/shard_map/ppermute | solution.py:110
  38.2 2.1 %dynamic-slice_bitcast_fusion.1 = (bf16[4,128,512]{2,1,0:T(8,128)(2,1)}, bf16[4,128,512]{2,1,0:T(8,128)(2,1)S(1)}) fusion(bf16[2,4,128,512]{3,2,0,1:T(8,128)(2,1)} %bitcast_dynamic-update-slice_fusion, s32[]{:T(128)S(6)} %select_n.125, s32[]{:T(128)S(6)} %select_n.126), kind=kLoop, calls=%fused_computation.5 | loop fusion | bytes 2097160 | tf_op jit(solution)/shard_map/jit(dynamic_index_in_dim)/squeeze | solution.py:118
  40.3 7.6 %collective-permute-start.11 = (bf16[4,128,512]{2,1,0:T(8,128)(2,1)S(1)}, bf16[4,128,512]{2,1,0:T(8,128)(2,1)}, u32[]{:S(2)}, u32[]{:S(2)}) collective-permute-start(bf16[4,128,512]{2,1,0:T(8,128)(2,1)S(1)} %get-tuple-element.51), channel_id=1, source_target_pairs={{0,8},{1,24},{2,10},{3,26},{4,12},{5,28},{6,14},{7,30},{8,0},{9,16... | collective-permute-start | bytes 1572872 | tf_op jit(solution)/shard_map/ppermute | solution.py:163
  47.9 5.3 %collective-permute-start.10 = (bf16[4,128,512]{2,1,0:T(8,128)(2,1)}, bf16[4,128,512]{2,1,0:T(8,128)(2,1)}, u32[]{:S(2)}, u32[]{:S(2)}) collective-permute-start(bf16[4,128,512]{2,1,0:T(8,128)(2,1)} %get-tuple-element.50), channel_id=1, source_target_pairs={{0,0},{1,16},{2,2},{3,18},{4,4},{5,20},{6,6},{7,22},{8,8},{9,24},{... | collective-permute-start | bytes 1572872 | tf_op jit(solution)/shard_map/ppermute | solution.py:163
  54.8 11.0 %collective-permute-done.11 = bf16[4,128,512]{2,1,0:T(8,128)(2,1)} collective-permute-done((bf16[4,128,512]{2,1,0:T(8,128)(2,1)S(1)}, bf16[4,128,512]{2,1,0:T(8,128)(2,1)}, u32[]{:S(2)}, u32[]{:S(2)}) %collective-permute-start.11) | collective-permute-done | bytes 524320 | tf_op jit(solution)/shard_map/ppermute | solution.py:163
  69.6 15.8 %collective-permute-done.9.refs_5_ = bf16[128,2176]{1,0:T(8,128)(2,1)} collective-permute-done((bf16[128,2176]{1,0:T(8,128)(2,1)S(1)}, bf16[128,2176]{1,0:T(8,128)(2,1)}, u32[]{:S(2)}, u32[]{:S(2)}) %collective-permute-start.9) | collective-permute-done | bytes 557088 | tf_op jit(solution)/shard_map/ppermute | solution.py:110
  91.5 4.2 %project.2 = (bf16[768,256]{1,0:T(8,128)(2,1)S(1)}, bf16[768,256]{1,0:T(8,128)(2,1)S(1)}, bf16[768,128]{1,0:T(8,128)(2,1)S(1)}) custom-call(s32[4]{0:T(128)S(1)} %pad_add_fusion.where, bf16[128,2176]{1,0:T(8,128)(2,1)S(1)} %constant_dynamic-update-slice_fusion.refs_0_.refs_6_, bf16[128,2176]{1,0:T(8,128)(2,1)S(1)} %copy-done.14, ...), custom_call_target="tpu_custom_call" | custom-call | flops 1610612736 | bytes 5439504 | tf_op jit(solution)/shard_map/project/pallas_call | solution.py:332
  96.9 4.8 %collective-permute-start.17 = (bf16[1024,128]{1,0:T(8,128)(2,1)S(1)}, bf16[1024,128]{1,0:T(8,128)(2,1)S(1)}, u32[]{:S(2)}, u32[]{:S(2)}) collective-permute-start(bf16[1024,128]{1,0:T(8,128)(2,1)S(1)} %copy-done.16), channel_id=1, source_target_pairs={{0,8},{2,10},{4,12},{6,14},{8,16},{10,18},{12,20},{14,22},{16,24},... | collective-permute-start | bytes 786440 | tf_op jit(solution)/shard_map/ppermute | solution.py:110
  101.7 2.4 %collective-permute-start.19 = (bf16[1024,128]{1,0:T(8,128)(2,1)S(1)}, bf16[1024,128]{1,0:T(8,128)(2,1)S(1)}, u32[]{:S(2)}, u32[]{:S(2)}) collective-permute-start(bf16[1024,128]{1,0:T(8,128)(2,1)S(1)} %copy-done.16), channel_id=1, source_target_pairs={{0,24},{2,26},{4,28},{6,30},{8,0},{10,2},{12,4},{14,6},{16,8},{18,... | collective-permute-start | bytes 786440 | tf_op jit(solution)/shard_map/ppermute | solution.py:110
  108.3 10.0 %collective-permute-done.18 = bf16[1024,128]{1,0:T(8,128)(2,1)S(1)} collective-permute-done((bf16[1024,128]{1,0:T(8,128)(2,1)S(1)}, bf16[1024,128]{1,0:T(8,128)(2,1)S(1)}, u32[]{:S(2)}, u32[]{:S(2)}) %collective-permute-start.18) | collective-permute-done | bytes 262176 | tf_op jit(solution)/shard_map/ppermute | solution.py:110
  119.1 3.4 %attend.1 = bf16[4,4,64,128]{3,2,1,0:T(8,128)(2,1)S(1)} custom-call(bf16[768,256]{1,0:T(8,128)(2,1)S(1)} %get-tuple-element.30.refs_0_, bf16[256,256]{1,0:T(8,128)(2,1)S(1)} %get-tuple-element.34.refs_1_, bf16[768,256]{1,0:T(8,128)(2,1)S(1)} %get-tuple-element.31.refs_2_, bf16[256,256]{1,0:T(8,128)(2,1)S(1)} %get-tuple-element.35.refs_3_, ...), custom_call_target="tpu_custom_call" | custom-call | flops 1073741824 | bytes 1835008 | tf_op jit(solution)/shard_map/attend/pallas_call | solution.py:332
  122.5 5.9 %collective-permute-start.22 = (bf16[4,64,128]{2,1,0:T(8,128)(2,1)S(1)}, bf16[4,64,128]{2,1,0:T(8,128)(2,1)S(1)}, u32[]{:S(2)}, u32[]{:S(2)}) collective-permute-start(bf16[4,64,128]{2,1,0:T(8,128)(2,1)S(1)} %get-tuple-element.63), channel_id=1, source_target_pairs={{0,8},{2,10},{4,12},{6,14},{8,16},{10,18},{12,20},{14,22},{16,24},... | collective-permute-start | bytes 196616 | tf_op jit(solution)/shard_map/ppermute | solution.py:110
  128.5 3.4 %collective-permute-start.21 = (bf16[4,64,128]{2,1,0:T(8,128)(2,1)S(1)}, bf16[4,64,128]{2,1,0:T(8,128)(2,1)S(1)}, u32[]{:S(2)}, u32[]{:S(2)}) collective-permute-start(bf16[4,64,128]{2,1,0:T(8,128)(2,1)S(1)} %get-tuple-element.64), channel_id=1, source_target_pairs={{0,16},{2,18},{4,20},{6,22},{8,24},{10,26},{12,28},{14,30},{16,0},... | collective-permute-start | bytes 196616 | tf_op jit(solution)/shard_map/ppermute | solution.py:110
  131.9 2.5 %collective-permute-done.22 = bf16[4,64,128]{2,1,0:T(8,128)(2,1)S(1)} collective-permute-done((bf16[4,64,128]{2,1,0:T(8,128)(2,1)S(1)}, bf16[4,64,128]{2,1,0:T(8,128)(2,1)S(1)}, u32[]{:S(2)}, u32[]{:S(2)}) %collective-permute-start.22) | collective-permute-done | bytes 65568 | tf_op jit(solution)/shard_map/ppermute | solution.py:110
  134.3 1.9 %collective-permute-done.21 = bf16[4,64,128]{2,1,0:T(8,128)(2,1)S(1)} collective-permute-done((bf16[4,64,128]{2,1,0:T(8,128)(2,1)S(1)}, bf16[4,64,128]{2,1,0:T(8,128)(2,1)S(1)}, u32[]{:S(2)}, u32[]{:S(2)}) %collective-permute-start.21) | collective-permute-done | bytes 65568 | tf_op jit(solution)/shard_map/ppermute | solution.py:110
  141.1 5.7 %collective-permute-done.23.refs_1_ = bf16[4,4,64,128]{3,2,1,0:T(8,128)(2,1)S(1)} collective-permute-done((bf16[4,4,64,128]{3,2,1,0:T(8,128)(2,1)S(1)}, bf16[4,4,64,128]{3,2,1,0:T(8,128)(2,1)S(1)}, u32[]{:S(2)}, u32[]{:S(2)}) %collective-permute-start.23) | collective-permute-done | bytes 262176 | tf_op jit(solution)/shard_map/ppermute | solution.py:110
  146.8 5.1 %collective-permute-done.24.refs_2_ = bf16[4,4,64,128]{3,2,1,0:T(8,128)(2,1)S(1)} collective-permute-done((bf16[4,4,64,128]{3,2,1,0:T(8,128)(2,1)S(1)}, bf16[4,4,64,128]{3,2,1,0:T(8,128)(2,1)S(1)}, u32[]{:S(2)}, u32[]{:S(2)}) %collective-permute-start.24) | collective-permute-done | bytes 262176 | tf_op jit(solution)/shard_map/ppermute | solution.py:110
  156.1 2.2 %hidden.1 = bf16[4,64,512]{2,1,0:T(8,128)(2,1)S(1)} custom-call(s32[4]{0:T(128)S(1)} %pad_add_fusion.where, bf16[4,4,64,128]{3,2,1,0:T(8,128)(2,1)S(1)} %copy-done.5, bf16[4,4,64,128]{3,2,1,0:T(8,128)(2,1)S(1)} %collective-permute-done.23.refs_1_, bf16[4,4,64,128]{3,2,1,0:T(8,128)(2,1)S(1)} %collective-permute-done.24.refs_2_, ...), custom_call_target="tpu_custom_call" | custom-call | flops 536870912 | bytes 5373968 | tf_op jit(solution)/shard_map/hidden/pallas_call | solution.py:332
  168.7 1.7 maximum_select_fusion.1
  170.5 3.6 %loss.1 = f32[64,1]{1,0:T(8,128)S(1)} custom-call(bf16[64,1024]{1,0:T(8,128)(2,1)S(1)} %get-tuple-element.41.h_keep, bf16[64,1024]{1,0:T(8,128)(2,1)S(1)} %get-tuple-element.42.h_send, bf16[64,1024]{1,0:T(8,128)(2,1)S(1)} %get-tuple-element.57.t_keep, bf16[64,1024]{1,0:T(8,128)(2,1)S(1)} %collective-permute-done.31.t_send, s32[64,1]{1,0:T(8,128)S(1)} %copy.63.t_ids, ...), custom_call_target="tpu_custom_call" | custom-call | flops 268435456 | bytes 5243136 | tf_op jit(solution)/shard_map/loss/pallas_call | solution.py:332
  (129 shorter events, 53.5 us)
Async XLA Ops:
  7.2 129.7 %all-gather.2.cloned.1.call-start = ((), (), s32[]{:S(2)}) async-start(), calls=%async_computation | async-start | bytes 2506752 | tf_op jit(solution)/shard_map/all_gather | solution.py:390
  8.3 26.7 %collective-permute-start.3 = (bf16[64,2176]{1,0:T(8,128)(2,1)S(1)}, bf16[64,2176]{1,0:T(8,128)(2,1)}, u32[]{:S(2)}, u32[]{:S(2)}) collective-permute-start(bf16[64,2176]{1,0:T(8,128)(2,1)S(1)} %fusion.2), channel_id=1, source_target_pairs={{0,8},{2,10},{4,12},{6,14},{8,16},{10,18},{12,20},{14,22},{16,24},... | collective-permute-start | bytes 835592 | tf_op jit(solution)/shard_map/ppermute | solution.py:110
  11.4 23.6 %collective-permute-start.4 = (bf16[64,2176]{1,0:T(8,128)(2,1)S(1)}, bf16[64,2176]{1,0:T(8,128)(2,1)S(1)}, u32[]{:S(2)}, u32[]{:S(2)}) collective-permute-start(bf16[64,2176]{1,0:T(8,128)(2,1)S(1)} %fusion.2), channel_id=1, source_target_pairs={{0,16},{2,18},{4,20},{6,22},{8,24},{10,26},{12,28},{14,30},{16,0},... | collective-permute-start | bytes 835592 | tf_op jit(solution)/shard_map/ppermute | solution.py:110
  14.0 21.0 %collective-permute-start.5 = (bf16[64,2176]{1,0:T(8,128)(2,1)S(1)}, bf16[64,2176]{1,0:T(8,128)(2,1)}, u32[]{:S(2)}, u32[]{:S(2)}) collective-permute-start(bf16[64,2176]{1,0:T(8,128)(2,1)S(1)} %fusion.2), channel_id=1, source_target_pairs={{0,24},{2,26},{4,28},{6,30},{8,0},{10,2},{12,4},{14,6},{16,8},{18,... | collective-permute-start | bytes 835592 | tf_op jit(solution)/shard_map/ppermute | solution.py:110
  19.3 8.7 %collective-permute-start.1 = (bf16[2,128,512]{2,1,0:T(8,128)(2,1)S(1)}, bf16[2,128,512]{2,1,0:T(8,128)(2,1)S(1)}, u32[]{:S(2)}, u32[]{:S(2)}) collective-permute-start(bf16[2,128,512]{2,1,0:T(8,128)(2,1)S(1)} %bitcast.78), channel_id=1, source_target_pairs={{0,4},{2,6},{4,0},{6,2},{8,12},{10,14},{12,8},{14,10},{16,20},{18,... | collective-permute-start | bytes 786440 | tf_op jit(solution)/shard_map/ppermute | solution.py:110
  36.0 32.8 %collective-permute-start.6 = (bf16[128,2176]{1,0:T(8,128)(2,1)S(1)}, bf16[128,2176]{1,0:T(8,128)(2,1)S(1)}, u32[]{:S(2)}, u32[]{:S(2)}) collective-permute-start(bf16[128,2176]{1,0:T(8,128)(2,1)S(1)} %constant_dynamic-update-slice_fusion.refs_0_.refs_6_), channel_id=1, source_target_pairs={{0,2},{2,0},{4,6},{6,4},{8,10},{10,8},{12,14},{14,12},{16,18},{18,... | collective-permute-start | bytes 1671176 | tf_op jit(solution)/shard_map/ppermute | solution.py:110
  36.6 32.1 %collective-permute-start.8 = (bf16[128,2176]{1,0:T(8,128)(2,1)S(1)}, bf16[128,2176]{1,0:T(8,128)(2,1)S(1)}, u32[]{:S(2)}, u32[]{:S(2)}) collective-permute-start(bf16[128,2176]{1,0:T(8,128)(2,1)S(1)} %constant_dynamic-update-slice_fusion.refs_0_.refs_6_), channel_id=1, source_target_pairs={{0,4},{2,6},{4,0},{6,2},{8,12},{10,14},{12,8},{14,10},{16,20},{18,... | collective-permute-start | bytes 1671176 | tf_op jit(solution)/shard_map/ppermute | solution.py:110
  40.3 25.5 %collective-permute-start.11 = (bf16[4,128,512]{2,1,0:T(8,128)(2,1)S(1)}, bf16[4,128,512]{2,1,0:T(8,128)(2,1)}, u32[]{:S(2)}, u32[]{:S(2)}) collective-permute-start(bf16[4,128,512]{2,1,0:T(8,128)(2,1)S(1)} %get-tuple-element.51), channel_id=1, source_target_pairs={{0,8},{1,24},{2,10},{3,26},{4,12},{5,28},{6,14},{7,30},{8,0},{9,16... | collective-permute-start | bytes 1572872 | tf_op jit(solution)/shard_map/ppermute | solution.py:163
  47.9 19.2 %collective-permute-start.10 = (bf16[4,128,512]{2,1,0:T(8,128)(2,1)}, bf16[4,128,512]{2,1,0:T(8,128)(2,1)}, u32[]{:S(2)}, u32[]{:S(2)}) collective-permute-start(bf16[4,128,512]{2,1,0:T(8,128)(2,1)} %get-tuple-element.50), channel_id=1, source_target_pairs={{0,0},{1,16},{2,2},{3,18},{4,4},{5,20},{6,6},{7,22},{8,8},{9,24},{... | collective-permute-start | bytes 1572872 | tf_op jit(solution)/shard_map/ppermute | solution.py:163
  54.3 14.5 %collective-permute-start.7 = (bf16[128,2176]{1,0:T(8,128)(2,1)S(1)}, bf16[128,2176]{1,0:T(8,128)(2,1)}, u32[]{:S(2)}, u32[]{:S(2)}) collective-permute-start(bf16[128,2176]{1,0:T(8,128)(2,1)S(1)} %constant_dynamic-update-slice_fusion.2.refs_1_), channel_id=1, source_target_pairs={{0,2},{2,0},{4,6},{6,4},{8,10},{10,8},{12,14},{14,12},{16,18},{18,... | collective-permute-start | bytes 1671176 | tf_op jit(solution)/shard_map/ppermute | solution.py:110
  65.8 19.7 %collective-permute-start.9 = (bf16[128,2176]{1,0:T(8,128)(2,1)S(1)}, bf16[128,2176]{1,0:T(8,128)(2,1)}, u32[]{:S(2)}, u32[]{:S(2)}) collective-permute-start(bf16[128,2176]{1,0:T(8,128)(2,1)S(1)} %constant_dynamic-update-slice_fusion.2.refs_1_), channel_id=1, source_target_pairs={{0,4},{2,6},{4,0},{6,2},{8,12},{10,14},{12,8},{14,10},{16,20},{18,... | collective-permute-start | bytes 1671176 | tf_op jit(solution)/shard_map/ppermute | solution.py:110
  86.1 15.6 %collective-permute-start.13 = (bf16[128,2176]{1,0:T(8,128)(2,1)S(1)}, bf16[128,2176]{1,0:T(8,128)(2,1)S(1)}, u32[]{:S(2)}, u32[]{:S(2)}) collective-permute-start(bf16[128,2176]{1,0:T(8,128)(2,1)S(1)} %collective-permute-done.6.refs_2_.refs_7_), channel_id=1, source_target_pairs={{0,4},{2,6},{4,0},{6,2},{8,12},{10,14},{12,8},{14,10},{16,20},{18,... | collective-permute-start | bytes 1671176 | tf_op jit(solution)/shard_map/ppermute | solution.py:110
  86.7 17.3 %collective-permute-start.14 = (bf16[128,2176]{1,0:T(8,128)(2,1)}, bf16[128,2176]{1,0:T(8,128)(2,1)S(1)}, u32[]{:S(2)}, u32[]{:S(2)}) collective-permute-start(bf16[128,2176]{1,0:T(8,128)(2,1)} %collective-permute-done.9.refs_5_), channel_id=1, source_target_pairs={{0,2},{2,0},{4,6},{6,4},{8,10},{10,8},{12,14},{14,12},{16,18},{18,... | collective-permute-start | bytes 1671176 | tf_op jit(solution)/shard_map/ppermute | solution.py:110
  96.5 22.6 %collective-permute-start.15 = (bf16[768,256]{1,0:T(8,128)(2,1)S(1)}, bf16[768,256]{1,0:T(8,128)(2,1)S(1)}, u32[]{:S(2)}, u32[]{:S(2)}) collective-permute-start(bf16[768,256]{1,0:T(8,128)(2,1)S(1)} %get-tuple-element.31.refs_2_), channel_id=1, source_target_pairs={{0,1},{1,0},{2,3},{3,2},{4,5},{5,4},{6,7},{7,6},{8,9},{9,8},{10,11... | collective-permute-start | bytes 1179656 | tf_op jit(solution)/shard_map/ppermute | solution.py:114
  96.9 11.4 %collective-permute-start.17 = (bf16[1024,128]{1,0:T(8,128)(2,1)S(1)}, bf16[1024,128]{1,0:T(8,128)(2,1)S(1)}, u32[]{:S(2)}, u32[]{:S(2)}) collective-permute-start(bf16[1024,128]{1,0:T(8,128)(2,1)S(1)} %copy-done.16), channel_id=1, source_target_pairs={{0,8},{2,10},{4,12},{6,14},{8,16},{10,18},{12,20},{14,22},{16,24},... | collective-permute-start | bytes 786440 | tf_op jit(solution)/shard_map/ppermute | solution.py:110
  101.7 16.7 %collective-permute-start.18 = (bf16[1024,128]{1,0:T(8,128)(2,1)S(1)}, bf16[1024,128]{1,0:T(8,128)(2,1)S(1)}, u32[]{:S(2)}, u32[]{:S(2)}) collective-permute-start(bf16[1024,128]{1,0:T(8,128)(2,1)S(1)} %copy-done.16), channel_id=1, source_target_pairs={{0,16},{2,18},{4,20},{6,22},{8,24},{10,26},{12,28},{14,30},{16,0},... | collective-permute-start | bytes 786440 | tf_op jit(solution)/shard_map/ppermute | solution.py:110
  101.7 17.4 %collective-permute-start.19 = (bf16[1024,128]{1,0:T(8,128)(2,1)S(1)}, bf16[1024,128]{1,0:T(8,128)(2,1)S(1)}, u32[]{:S(2)}, u32[]{:S(2)}) collective-permute-start(bf16[1024,128]{1,0:T(8,128)(2,1)S(1)} %copy-done.16), channel_id=1, source_target_pairs={{0,24},{2,26},{4,28},{6,30},{8,0},{10,2},{12,4},{14,6},{16,8},{18,... | collective-permute-start | bytes 786440 | tf_op jit(solution)/shard_map/ppermute | solution.py:110
  106.9 12.1 %collective-permute-start.16 = (bf16[256,256]{1,0:T(8,128)(2,1)S(1)}, bf16[256,256]{1,0:T(8,128)(2,1)S(1)}, u32[]{:S(2)}, u32[]{:S(2)}) collective-permute-start(bf16[256,256]{1,0:T(8,128)(2,1)S(1)} %get-tuple-element.35.refs_3_), channel_id=1, source_target_pairs={{0,1},{1,0},{2,3},{3,2},{4,5},{5,4},{6,7},{7,6},{8,9},{9,8},{10,11... | collective-permute-start | bytes 393224 | tf_op jit(solution)/shard_map/ppermute | solution.py:114
  122.5 11.8 %collective-permute-start.22 = (bf16[4,64,128]{2,1,0:T(8,128)(2,1)S(1)}, bf16[4,64,128]{2,1,0:T(8,128)(2,1)S(1)}, u32[]{:S(2)}, u32[]{:S(2)}) collective-permute-start(bf16[4,64,128]{2,1,0:T(8,128)(2,1)S(1)} %get-tuple-element.63), channel_id=1, source_target_pairs={{0,8},{2,10},{4,12},{6,14},{8,16},{10,18},{12,20},{14,22},{16,24},... | collective-permute-start | bytes 196616 | tf_op jit(solution)/shard_map/ppermute | solution.py:110
  136.9 33.6 %collective-permute-start.32 = (bf16[1024,1152]{1,0:T(8,128)(2,1)}, bf16[1024,1152]{1,0:T(8,128)(2,1)}, u32[]{:S(2)}, u32[]{:S(2)}) collective-permute-start(bf16[1024,1152]{1,0:T(8,128)(2,1)} %all-gather.2.cloned.1.call-done.n_own), channel_id=1, source_target_pairs={{0,1},{1,0},{2,3},{3,2},{4,5},{5,4},{6,7},{7,6},{8,9},{9,8},{10,11... | collective-permute-start | bytes 7077896 | tf_op jit(solution)/shard_map/ppermute | solution.py:114
  137.1 14.8 %collective-permute-start.26 = (bf16[4,1024,128]{2,1,0:T(8,128)(2,1)S(1)}, bf16[4,1024,128]{2,1,0:T(8,128)(2,1)S(1)}, u32[]{:S(2)}, u32[]{:S(2)}) collective-permute-start(bf16[4,1024,128]{2,1,0:T(8,128)(2,1)S(1)} %pad_maximum_fusion.refs_4_), channel_id=1, source_target_pairs={{0,1},{1,0},{2,3},{3,2},{4,5},{5,4},{6,7},{7,6},{8,9},{9,8},{10,11... | collective-permute-start | bytes 3145736 | tf_op jit(solution)/shard_map/ppermute | solution.py:114
  137.7 9.2 %collective-permute-start.23 = (bf16[4,4,64,128]{3,2,1,0:T(8,128)(2,1)S(1)}, bf16[4,4,64,128]{3,2,1,0:T(8,128)(2,1)S(1)}, u32[]{:S(2)}, u32[]{:S(2)}) collective-permute-start(bf16[4,4,64,128]{3,2,1,0:T(8,128)(2,1)S(1)} %pad_maximum_fusion.1.refs_0_), channel_id=1, source_target_pairs={{0,2},{2,0},{4,6},{6,4},{8,10},{10,8},{12,14},{14,12},{16,18},{18,... | collective-permute-start | bytes 786440 | tf_op jit(solution)/shard_map/ppermute | solution.py:110
  138.3 13.6 %collective-permute-start.24 = (bf16[4,4,64,128]{3,2,1,0:T(8,128)(2,1)S(1)}, bf16[4,4,64,128]{3,2,1,0:T(8,128)(2,1)S(1)}, u32[]{:S(2)}, u32[]{:S(2)}) collective-permute-start(bf16[4,4,64,128]{3,2,1,0:T(8,128)(2,1)S(1)} %pad_maximum_fusion.1.refs_0_), channel_id=1, source_target_pairs={{0,4},{2,6},{4,0},{6,2},{8,12},{10,14},{12,8},{14,10},{16,20},{18,... | collective-permute-start | bytes 786440 | tf_op jit(solution)/shard_map/ppermute | solution.py:110
  139.7 12.2 %collective-permute-start.25 = (bf16[4,4,64,128]{3,2,1,0:T(8,128)(2,1)S(1)}, bf16[4,4,64,128]{3,2,1,0:T(8,128)(2,1)S(1)}, u32[]{:S(2)}, u32[]{:S(2)}) collective-permute-start(bf16[4,4,64,128]{3,2,1,0:T(8,128)(2,1)S(1)} %pad_maximum_fusion.1.refs_0_), channel_id=1, source_target_pairs={{0,6},{2,4},{4,2},{6,0},{8,14},{10,12},{12,10},{14,8},{16,22},{18,... | collective-permute-start | bytes 786440 | tf_op jit(solution)/shard_map/ppermute | solution.py:110
  (29 other events, 234.0 us)
Sparse Core Ops, SparseCore 0:
  23.6 72.6 all-gather.1

commit v6 on v5

--- a/solution.py
+++ b/solution.py
@@ -95,15 +95,11 @@
 
 def relative_chip(c, by, bx, s):
     z, y, x = coords(c)
-    return chip_at((z + NZ - s) % NZ, y ^ by, x ^ bx)
-
-
-def z_shift(s):
-    return [(c, relative_chip(c, 0, 0, NZ - s)) for c in range(CHIPS)]
-
-
-def flip(by, bx):
-    return [(c, relative_chip(c, by, bx, 0)) for c in range(CHIPS)]
+    return chip_at(z ^ s, y ^ by, x ^ bx)
+
+
+def flip(by, bx, s=0):
+    return [(c, relative_chip(c, by, bx, s)) for c in range(CHIPS)]
 
 
 def hop(value, perm):
@@ -122,15 +118,8 @@
     return lax.optimization_barrier((values, others))[0]
 
 
-def along_z(own):
-    return [own] + [hop(own, z_shift(s)) for s in range(1, NZ)]
-
-
-def in_plane(low, high):
-    to_x, to_y = flip(0, 1), flip(1, 0)
-    low_x, high_y = hop(low, to_x), hop(high, to_y)
-    high_x, low_y = hop(high, to_x), hop(low, to_y)
-    return [low, high, low_x, high_x, low_y, high_y, hop(low_x, to_y), hop(high_y, to_x)]
+def pair_up(own):
+    return jnp.concatenate([own, hop(own, flip(0, 0, 1))])
 
 
 def heads_in_plane(w_proj, y, x):
@@ -244,7 +233,7 @@
 
 def hidden_kernel(where, *refs):
     n = len(PLANE)
-    gated, w_own, w_other, tok = refs[:n], refs[n], refs[n + 1], refs[n + 2 : 2 * n + 2]
+    gated, w_own, w_other, tok = refs[:n], refs[n : n + 2], refs[n + 2 : n + 4], refs[n + 4 : -5]
     hidden, g_all, t_all, w_all, sems = refs[-5:]
     z, y, x, u = (where[i] for i in range(4))
     c = chip_at(z, y, x)
@@ -254,7 +243,7 @@
     for s in range(NZ):
         cols = pl.ds(s * W, W)
         for side, src in enumerate((w_own, w_other)):
-            copies.append((src.at[s], w_all.at[side, :, cols]))
+            copies.append((src[s // 2].at[s % 2], w_all.at[side, :, cols]))
         block = relative_chip(c, 0, 0, s)
         from_cols = pl.ds(pl.multiple_of(block * W, W), W)
         for k in range(n):
@@ -264,7 +253,7 @@
         copy.start()
     for k, (by, bx) in enumerate(PLANE):
         for s in range(NZ):
-            head = relative_chip(c, by, bx, NZ - s)
+            head = relative_chip(c, by, bx, s)
             cols = pl.ds(pl.multiple_of(head * W, W), W)
             for j, (jy, jx) in enumerate(PLANE):
                 block = (jy ^ by) * NX + (jx ^ bx)
@@ -278,7 +267,7 @@
     for k in range(n):
         for s in range(NZ):
             term = total[k * rows : (k + 1) * rows, s * W : (s + 1) * W]
-            cols = pl.ds(pl.multiple_of(((z + NZ - s) % NZ) * W, W), W)
+            cols = pl.ds(pl.multiple_of((z ^ s) * W, W), W)
             hidden[k, :, cols] = (t_all[k, :, s * W : (s + 1) * W].astype(F32) + term).astype(BF16)
 
 
@@ -327,7 +316,7 @@
 
 
 def call(kernel, name, outs, scratch, args, places, flops):
-    space = {"s": pltpu.SMEM, "v": pltpu.VMEM, "h": pl.ANY}
+    space = {"s": pltpu.SMEM, "v": pltpu.VMEM, "h": pltpu.HBM}
     moved = sum(a.size * a.dtype.itemsize for a in args)
     return pl.pallas_call(
         kernel,
@@ -376,19 +365,28 @@
     p_own = lax.dynamic_slice_in_dim(positions, u * rows, rows, 0)
     p_other = lax.dynamic_slice_in_dim(positions, (1 - u) * rows, rows, 0)
     mine = with_marks(mine, whole_parts(p_own, 128) + whole_parts(p_other, 128))
-    line = along_z(mine)
-
-    w_plane, line = lax.optimization_barrier((heads_in_plane(w_proj, y, x), line))
-    tok = in_plane(jnp.concatenate(line[:2]), jnp.concatenate(line[2:]))
-    w_mine = heads_along_z(w_plane, z)
-    w_mine = after(w_mine, tok[2:6])
+    line = [mine] + [hop(mine, flip(0, 0, s)) for s in range(1, NZ)]
+    low = jnp.concatenate(line[:2])
+
+    to_x, to_y = flip(0, 1), flip(1, 0)
+    low_x, low_y = hop(low, to_x), hop(low, to_y)
+    w_plane = heads_in_plane(w_proj, y, x)
+    w_plane, high = lax.optimization_barrier((w_plane, after(line[2:], low_x, low_y)))
+    high = jnp.concatenate(high)
+    high_x, high_y = hop(high, to_x), hop(high, to_y)
+    low_xy, high_xy = hop(low_x, to_y), hop(high_y, to_x)
+    tok = [low, high, low_x, high_x, low_y, high_y, low_xy, high_xy]
+    w_mine = after(heads_along_z(w_plane, z), high_x, high_y, low_xy)
     w_theirs = swap_cores(w_mine)
 
     own_ids = lax.dynamic_slice_in_dim(neg_ids, c * negs, negs, 0)
     norms = jnp.sum(jnp.square(neg_emb.astype(F32)), axis=1)
     neg = with_marks(neg_emb, float_parts(norms) + whole_parts(own_ids, 256))
-    neg_own = lax.all_gather(neg, "ctx", axis=0, tiled=True)
-    out_own = along_z(after(w_out, w_mine))
+    neg_pair = pair_up(after(neg, w_mine))
+    neg_pair = after(neg_pair, w_theirs)
+    neg_near = jnp.concatenate([neg_pair, hop(neg_pair, flip(0, 0, 2))])
+    out_pair = pair_up(after(w_out[None], neg_pair))
+    out_own = [out_pair, hop(after(out_pair, neg_near), flip(0, 0, 2))]
     t_rows = target_emb.reshape(2, rows, -1)
     t_keep = pick_row(t_rows, u)
     t_send = swap_cores(pick_row(t_rows, 1 - u))
@@ -414,7 +412,8 @@
     kv_early_theirs = swap_cores(kv_early)
     gq_last, kv_last, marks_last = project(after(tok[6:], kv_early))
     kv_last_theirs = swap_cores(kv_last)
-    kv_last_theirs = after(kv_last_theirs, out_own)
+    neg_near = after(neg_near, kv_last)
+    neg_x, neg_y = hop(neg_near, flip(0, 1)), hop(neg_near, flip(1, 0))
     (gated,) = call(
         attend_kernel,
         "attend",
@@ -425,12 +424,14 @@
         8 * "v",
         8 * events * events * W,
     )
-    gated = jnp.stack([gated[0]] + [hop(gated[s], z_shift(NZ - s)) for s in range(1, NZ)])
-    neg_own = after(neg_own, gated)
-    neg_other = swap_cores(neg_own)
-    out_own = after(jnp.stack(out_own), gated)
-    out_other = swap_cores(out_own)
+    gated = jnp.stack([gated[0]] + [hop(gated[s], flip(0, 0, s)) for s in range(1, NZ)])
+    out_other = [swap_cores(w) for w in out_own]
+    gated = after(gated, out_own)
     gated = [gated] + [hop(gated, flip(by, bx)) for by, bx in PLANE[1:]]
+    neg_x, neg_y = after((neg_x, neg_y), gated, out_other)
+    part = neg_x.shape[0] // 2
+    neg_own = [neg_near, neg_x, neg_y]
+    neg_own += [hop(neg_x[:part], flip(1, 0)), hop(neg_y[part:], flip(0, 1))]
     (hidden,) = call(
         hidden_kernel,
         "hidden",
@@ -441,11 +442,13 @@
             pltpu.VMEM((2, half, NZ * W), BF16),
             pltpu.SemaphoreType.DMA((NZ * (2 + plane),)),
         ],
-        [where, *gated, out_own, out_other, *tok[:5:2], tok[6]],
-        "s" + 4 * "v" + 6 * "h",
+        [where, *gated, *out_own, *out_other, *tok[::2]],
+        "s" + 4 * "v" + 8 * "h",
         2 * plane * rows * model * NZ * W,
     )
     pieces = [hidden[0]] + [hop(hidden[k], flip(*PLANE[k])) for k in range(1, plane)]
+    neg_own = jnp.concatenate(after(neg_own, hidden))
+    neg_other = swap_cores(neg_own)
     h_keep, h_send = call(
         order_kernel,
         "order",

time: 183 us -> 173 us (0.945)
  waiting for transfers between devices: 65.3 us -> 88.7 us
  between operations: 14.4 us -> 1.05 us
  starting transfers between devices: 55.6 us -> 44.7 us
  local copies, waits for them, and re-layouts: 23 us -> 13.5 us
    ppermute x24 -> x29, waiting for transfers between devices: 53 us -> 83.5 us  [hop(): return lax.ppermute(value, 'ctx', perm)]
    ppermute x2, starting transfers between devices: 13 us -> 5.8 us  [heads_along_z(): lax.ppermute(pick_row(heads, e ^ z & 1), ('ctx', 'tp'), perm)]
    unnamed x41 -> x24, local copies, waits for them, and re-layouts: 12.1 us -> 5.21 us
    ppermute x2, waiting for transfers between devices: 11 us -> 4.84 us  [heads_along_z(): lax.ppermute(pick_row(heads, e ^ z & 1), ('ctx', 'tp'), perm)]
    ppermute x24 -> x29, starting transfers between devices: 40.3 us -> 37.6 us  [hop(): return lax.ppermute(value, 'ctx', perm)]
  transfers between devices with their start and end apart: 34 -> 39, of which waited for: 15 -> 22; matrix products, arithmetic and copies ran while one was open for 10% -> 8% of each run, Pallas kernels for 7% -> 8%
where the time goes in v6:
time: 173 us; the launch traced here: 172 us
  waiting for transfers between devices  88.7 us (51%)
  starting transfers between devices  44.7 us (26%)
  Pallas kernels  16.9 us (10%)
  local copies, waits for them, and re-layouts  13.5 us (8%)
  other arithmetic  7.5 us (4%)
    ppermute x29, waiting for transfers between devices, hop(): return lax.ppermute(value, 'ctx', perm)  83.5 us
    ppermute x29, starting transfers between devices, hop(): return lax.ppermute(value, 'ctx', perm)  37.6 us
    pallas_call x6, Pallas kernels, call(): pl.pallas_call(kernel, out_shape=[jax.ShapeDtypeStruct(shape, dtype) for...  16.9 us
    ppermute x2, starting transfers between devices, heads_along_z(): lax.ppermute(pick_row(heads, e ^ z & 1), ('ctx', 'tp'), perm)  5.8 us
    unnamed x24, local copies, waits for them, and re-layouts  5.21 us
    ppermute x2, waiting for transfers between devices, heads_along_z(): lax.ppermute(pick_row(heads, e ^ z & 1), ('ctx', 'tp'), perm)  4.84 us
  transfers between devices with their start and end apart: 39, of which 22 were waited for; matrix products, arithmetic and copies ran while one was open for 8% of the time, Pallas kernels for 8%

profile of v6, /device:TPU:0, one launch (start us, length us, event | category | flops | bytes accessed | tf_op | source)
XLA Modules:
  0.0 172.3 jit_solution(10039720916569968883)
XLA Ops:
  2.5 3.0 %collective-permute-start = (bf16[64,2176]{1,0:T(8,128)(2,1)}, bf16[64,2176]{1,0:T(8,128)(2,1)S(1)}, u32[]{:S(2)}, u32[]{:S(2)}) collective-permute-start(bf16[64,2176]{1,0:T(8,128)(2,1)} %pad_maximum_fusion.2), channel_id=1, source_target_pairs={{0,8},{2,10},{4,12},{6,14},{8,0},{10,2},{12,4},{14,6},{16,24},{18,... | collective-permute-start | bytes 835592 | tf_op jit(solution)/shard_map/ppermute | solution.py:106
  9.4 2.6 %collective-permute-start.4 = (bf16[64,2176]{1,0:T(8,128)(2,1)}, bf16[64,2176]{1,0:T(8,128)(2,1)}, u32[]{:S(2)}, u32[]{:S(2)}) collective-permute-start(bf16[64,2176]{1,0:T(8,128)(2,1)} %pad_maximum_fusion.2), channel_id=1, source_target_pairs={{0,16},{2,18},{4,20},{6,22},{8,24},{10,26},{12,28},{14,30},{16,0},... | collective-permute-start | bytes 835592 | tf_op jit(solution)/shard_map/ppermute | solution.py:106
  15.6 2.4 %collective-permute-start.3 = (bf16[2,128,512]{2,1,0:T(8,128)(2,1)}, bf16[2,128,512]{2,1,0:T(8,128)(2,1)S(1)}, u32[]{:S(2)}, u32[]{:S(2)}) collective-permute-start(bf16[2,128,512]{2,1,0:T(8,128)(2,1)} %bitcast.16), channel_id=1, source_target_pairs={{0,6},{2,4},{4,2},{6,0},{8,14},{10,12},{12,10},{14,8},{16,22},{18,... | collective-permute-start | bytes 786440 | tf_op jit(solution)/shard_map/ppermute | solution.py:106
  20.3 7.6 %collective-permute-done.2 = bf16[2,128,512]{2,1,0:T(8,128)(2,1)} collective-permute-done((bf16[2,128,512]{2,1,0:T(8,128)(2,1)}, bf16[2,128,512]{2,1,0:T(8,128)(2,1)}, u32[]{:S(2)}, u32[]{:S(2)}) %collective-permute-start.2) | collective-permute-done | bytes 262176 | tf_op jit(solution)/shard_map/ppermute | solution.py:106
  29.0 7.6 %collective-permute-done.5 = bf16[64,2176]{1,0:T(8,128)(2,1)S(1)} collective-permute-done((bf16[64,2176]{1,0:T(8,128)(2,1)}, bf16[64,2176]{1,0:T(8,128)(2,1)S(1)}, u32[]{:S(2)}, u32[]{:S(2)}) %collective-permute-start.5) | collective-permute-done | bytes 278560 | tf_op jit(solution)/shard_map/ppermute | solution.py:106
  41.2 5.4 %collective-permute-start.10 = (bf16[4,128,512]{2,1,0:T(8,128)(2,1)}, bf16[4,128,512]{2,1,0:T(8,128)(2,1)}, u32[]{:S(2)}, u32[]{:S(2)}) collective-permute-start(bf16[4,128,512]{2,1,0:T(8,128)(2,1)} %get-tuple-element.68), channel_id=1, source_target_pairs={{0,0},{1,16},{2,2},{3,18},{4,4},{5,20},{6,6},{7,22},{8,8},{9,24},{... | collective-permute-start | bytes 1572872 | tf_op jit(solution)/shard_map/ppermute | solution.py:152
  50.7 4.8 %collective-permute-done.11 = bf16[4,128,512]{2,1,0:T(8,128)(2,1)} collective-permute-done((bf16[4,128,512]{2,1,0:T(8,128)(2,1)}, bf16[4,128,512]{2,1,0:T(8,128)(2,1)}, u32[]{:S(2)}, u32[]{:S(2)}) %collective-permute-start.11) | collective-permute-done | bytes 524320 | tf_op jit(solution)/shard_map/ppermute | solution.py:152
  59.1 4.6 %collective-permute-done.9.refs_5_ = bf16[128,2176]{1,0:T(8,128)(2,1)} collective-permute-done((bf16[128,2176]{1,0:T(8,128)(2,1)}, bf16[128,2176]{1,0:T(8,128)(2,1)}, u32[]{:S(2)}, u32[]{:S(2)}) %collective-permute-start.9) | collective-permute-done | bytes 557088 | tf_op jit(solution)/shard_map/ppermute | solution.py:106
  63.7 8.5 %collective-permute-done.12.refs_0_.refs_11_ = bf16[128,2176]{1,0:T(8,128)(2,1)S(1)} collective-permute-done((bf16[128,2176]{1,0:T(8,128)(2,1)S(1)}, bf16[128,2176]{1,0:T(8,128)(2,1)S(1)}, u32[]{:S(2)}, u32[]{:S(2)}) %collective-permute-start.12) | collective-permute-done | bytes 557088 | tf_op jit(solution)/shard_map/ppermute | solution.py:106
  75.3 4.2 %collective-permute-done.20 = bf16[64,1152]{1,0:T(8,128)(2,1)S(1)} collective-permute-done((bf16[64,1152]{1,0:T(8,128)(2,1)S(1)}, bf16[64,1152]{1,0:T(8,128)(2,1)S(1)}, u32[]{:S(2)}, u32[]{:S(2)}) %collective-permute-start.20) | collective-permute-done | bytes 147488 | tf_op jit(solution)/shard_map/ppermute | solution.py:106
  79.5 3.1 %collective-permute-start.22 = (bf16[128,1152]{1,0:T(8,128)(2,1)S(1)}, bf16[128,1152]{1,0:T(8,128)(2,1)S(1)}, u32[]{:S(2)}, u32[]{:S(2)}) collective-permute-start(bf16[128,1152]{1,0:T(8,128)(2,1)S(1)} %pad_maximum_fusion.1), channel_id=1, source_target_pairs={{0,16},{2,18},{4,20},{6,22},{8,24},{10,26},{12,28},{14,30},{16,0},... | collective-permute-start | bytes 884744 | tf_op jit(solution)/shard_map/ppermute | solution.py:106
  84.7 4.4 %project.2 = (bf16[768,256]{1,0:T(8,128)(2,1)S(1)}, bf16[768,256]{1,0:T(8,128)(2,1)S(1)}, bf16[768,128]{1,0:T(8,128)(2,1)S(1)}) custom-call(s32[4]{0:T(128)S(1)} %pad_add_fusion.where, bf16[128,2176]{1,0:T(8,128)(2,1)S(1)} %pad_maximum_fusion.refs_0_.refs_8_, bf16[128,2176]{1,0:T(8,128)(2,1)} %constant_dynamic-update-slice_fusion.refs_1_, ...), custom_call_target="tpu_custom_call" | custom-call | flops 1610612736 | bytes 5439504 | tf_op jit(solution)/shard_map/project/pallas_call | solution.py:321
  89.8 6.2 %collective-permute-done.21 = bf16[1,1024,128]{2,1,0:T(8,128)(2,1)S(1)} collective-permute-done((bf16[1,1024,128]{2,1,0:T(8,128)(2,1)}, bf16[1,1024,128]{2,1,0:T(8,128)(2,1)S(1)}, u32[]{:S(2)}, u32[]{:S(2)}) %collective-permute-start.21) | collective-permute-done | bytes 262176 | tf_op jit(solution)/shard_map/ppermute | solution.py:106
  96.5 2.6 %project.3 = (bf16[256,256]{1,0:T(8,128)(2,1)S(1)}, bf16[256,256]{1,0:T(8,128)(2,1)S(1)}, bf16[256,128]{1,0:T(8,128)(2,1)S(1)}) custom-call(s32[4]{0:T(128)S(1)} %pad_add_fusion.where, bf16[128,2176]{1,0:T(8,128)(2,1)S(1)} %collective-permute-done.12.refs_0_.refs_11_, bf16[128,2176]{1,0:T(8,128)(2,1)S(1)} %collective-permute-done.14.refs_1_, ...), custom_call_target="tpu_custom_call" | custom-call | flops 536870912 | bytes 3211280 | tf_op jit(solution)/shard_map/project/pallas_call | solution.py:321
  102.2 3.5 %attend.1 = bf16[4,4,64,128]{3,2,1,0:T(8,128)(2,1)S(1)} custom-call(bf16[768,256]{1,0:T(8,128)(2,1)S(1)} %get-tuple-element.39.refs_0_, bf16[256,256]{1,0:T(8,128)(2,1)S(1)} %get-tuple-element.43.refs_1_, bf16[768,256]{1,0:T(8,128)(2,1)S(1)} %get-tuple-element.40.refs_2_, bf16[256,256]{1,0:T(8,128)(2,1)S(1)} %get-tuple-element.44.refs_3_, ...), custom_call_target="tpu_custom_call" | custom-call | flops 1073741824 | bytes 1835008 | tf_op jit(solution)/shard_map/attend/pallas_call | solution.py:321
  105.7 3.0 %collective-permute-start.19 = (bf16[4,64,128]{2,1,0:T(8,128)(2,1)S(1)}, bf16[4,64,128]{2,1,0:T(8,128)(2,1)S(1)}, u32[]{:S(2)}, u32[]{:S(2)}) collective-permute-start(bf16[4,64,128]{2,1,0:T(8,128)(2,1)S(1)} %get-tuple-element.81), channel_id=1, source_target_pairs={{0,24},{2,26},{4,28},{6,30},{8,16},{10,18},{12,20},{14,22},{16,8},... | collective-permute-start | bytes 196616 | tf_op jit(solution)/shard_map/ppermute | solution.py:106
  108.7 14.3 %collective-permute-done.23.refs_5_ = bf16[2,1024,128]{2,1,0:T(8,128)(2,1)S(1)} collective-permute-done((bf16[2,1024,128]{2,1,0:T(8,128)(2,1)S(1)}, bf16[2,1024,128]{2,1,0:T(8,128)(2,1)S(1)}, u32[]{:S(2)}, u32[]{:S(2)}) %collective-permute-start.23) | collective-permute-done | bytes 524320 | tf_op jit(solution)/shard_map/ppermute | solution.py:106
  124.4 5.4 %collective-permute-done.18 = bf16[4,64,128]{2,1,0:T(8,128)(2,1)S(1)} collective-permute-done((bf16[4,64,128]{2,1,0:T(8,128)(2,1)S(1)}, bf16[4,64,128]{2,1,0:T(8,128)(2,1)S(1)}, u32[]{:S(2)}, u32[]{:S(2)}) %collective-permute-start.18) | collective-permute-done | bytes 65568 | tf_op jit(solution)/shard_map/ppermute | solution.py:106
  129.8 4.2 %collective-permute-done.17 = bf16[4,64,128]{2,1,0:T(8,128)(2,1)S(1)} collective-permute-done((bf16[4,64,128]{2,1,0:T(8,128)(2,1)S(1)}, bf16[4,64,128]{2,1,0:T(8,128)(2,1)S(1)}, u32[]{:S(2)}, u32[]{:S(2)}) %collective-permute-start.17) | collective-permute-done | bytes 65568 | tf_op jit(solution)/shard_map/ppermute | solution.py:106
  137.7 5.7 %collective-permute-done.24.refs_1_ = bf16[4,4,64,128]{3,2,1,0:T(8,128)(2,1)S(1)} collective-permute-done((bf16[4,4,64,128]{3,2,1,0:T(8,128)(2,1)S(1)}, bf16[4,4,64,128]{3,2,1,0:T(8,128)(2,1)S(1)}, u32[]{:S(2)}, u32[]{:S(2)}) %collective-permute-start.24) | collective-permute-done | bytes 262176 | tf_op jit(solution)/shard_map/ppermute | solution.py:106
  143.4 3.8 %collective-permute-done.25.refs_2_ = bf16[4,4,64,128]{3,2,1,0:T(8,128)(2,1)S(1)} collective-permute-done((bf16[4,4,64,128]{3,2,1,0:T(8,128)(2,1)S(1)}, bf16[4,4,64,128]{3,2,1,0:T(8,128)(2,1)S(1)}, u32[]{:S(2)}, u32[]{:S(2)}) %collective-permute-start.25) | collective-permute-done | bytes 262176 | tf_op jit(solution)/shard_map/ppermute | solution.py:106
  149.8 2.2 %hidden.1 = bf16[4,64,512]{2,1,0:T(8,128)(2,1)S(1)} custom-call(s32[4]{0:T(128)S(1)} %pad_add_fusion.where, bf16[4,4,64,128]{3,2,1,0:T(8,128)(2,1)S(1)} %pad_maximum_fusion.3.refs_0_, bf16[4,4,64,128]{3,2,1,0:T(8,128)(2,1)S(1)} %collective-permute-done.24.refs_1_, bf16[4,4,64,128]{3,2,1,0:T(8,128)(2,1)S(1)} %collective-permute-done.25.refs_2_, ...), custom_call_target="tpu_custom_call" | custom-call | flops 536870912 | bytes 5373968 | tf_op jit(solution)/shard_map/hidden/pallas_call | solution.py:321
  161.3 2.1 %collective-permute-done.31.refs_3_ = bf16[64,512]{1,0:T(8,128)(2,1)S(1)} collective-permute-done((bf16[64,512]{1,0:T(8,128)(2,1)S(1)}, bf16[64,512]{1,0:T(8,128)(2,1)S(1)}, u32[]{:S(2)}, u32[]{:S(2)}) %collective-permute-start.31) | collective-permute-done | bytes 65568 | tf_op jit(solution)/shard_map/ppermute | solution.py:106
  168.1 3.6 %loss.1 = f32[64,1]{1,0:T(8,128)S(1)} custom-call(bf16[64,1024]{1,0:T(8,128)(2,1)S(1)} %get-tuple-element.52.h_keep, bf16[64,1024]{1,0:T(8,128)(2,1)S(1)} %get-tuple-element.53.h_send, bf16[64,1024]{1,0:T(8,128)(2,1)S(1)} %get-tuple-element.75.t_keep, bf16[64,1024]{1,0:T(8,128)(2,1)S(1)} %collective-permute-done.33.t_send, s32[64,1]{1,0:T(8,128)S(1)} %copy.63.t_ids, ...), custom_call_target="tpu_custom_call" | custom-call | flops 268435456 | bytes 5243136 | tf_op jit(solution)/shard_map/loss/pallas_call | solution.py:321
  (127 shorter events, 56.2 us)
Async XLA Ops:
  2.5 15.6 %collective-permute-start = (bf16[64,2176]{1,0:T(8,128)(2,1)}, bf16[64,2176]{1,0:T(8,128)(2,1)S(1)}, u32[]{:S(2)}, u32[]{:S(2)}) collective-permute-start(bf16[64,2176]{1,0:T(8,128)(2,1)} %pad_maximum_fusion.2), channel_id=1, source_target_pairs={{0,8},{2,10},{4,12},{6,14},{8,0},{10,2},{12,4},{14,6},{16,24},{18,... | collective-permute-start | bytes 835592 | tf_op jit(solution)/shard_map/ppermute | solution.py:106
  9.4 19.6 %collective-permute-start.4 = (bf16[64,2176]{1,0:T(8,128)(2,1)}, bf16[64,2176]{1,0:T(8,128)(2,1)}, u32[]{:S(2)}, u32[]{:S(2)}) collective-permute-start(bf16[64,2176]{1,0:T(8,128)(2,1)} %pad_maximum_fusion.2), channel_id=1, source_target_pairs={{0,16},{2,18},{4,20},{6,22},{8,24},{10,26},{12,28},{14,30},{16,0},... | collective-permute-start | bytes 835592 | tf_op jit(solution)/shard_map/ppermute | solution.py:106
  12.8 15.2 %collective-permute-start.2 = (bf16[2,128,512]{2,1,0:T(8,128)(2,1)}, bf16[2,128,512]{2,1,0:T(8,128)(2,1)}, u32[]{:S(2)}, u32[]{:S(2)}) collective-permute-start(bf16[2,128,512]{2,1,0:T(8,128)(2,1)} %bitcast.14), channel_id=1, source_target_pairs={{0,4},{2,6},{4,0},{6,2},{8,12},{10,14},{12,8},{14,10},{16,20},{18,... | collective-permute-start | bytes 786440 | tf_op jit(solution)/shard_map/ppermute | solution.py:106
  15.6 13.3 %collective-permute-start.3 = (bf16[2,128,512]{2,1,0:T(8,128)(2,1)}, bf16[2,128,512]{2,1,0:T(8,128)(2,1)S(1)}, u32[]{:S(2)}, u32[]{:S(2)}) collective-permute-start(bf16[2,128,512]{2,1,0:T(8,128)(2,1)} %bitcast.16), channel_id=1, source_target_pairs={{0,6},{2,4},{4,2},{6,0},{8,14},{10,12},{12,10},{14,8},{16,22},{18,... | collective-permute-start | bytes 786440 | tf_op jit(solution)/shard_map/ppermute | solution.py:106
  18.1 18.5 %collective-permute-start.6 = (bf16[128,2176]{1,0:T(8,128)(2,1)S(1)}, bf16[128,2176]{1,0:T(8,128)(2,1)S(1)}, u32[]{:S(2)}, u32[]{:S(2)}) collective-permute-start(bf16[128,2176]{1,0:T(8,128)(2,1)S(1)} %pad_maximum_fusion.refs_0_.refs_8_), channel_id=1, source_target_pairs={{0,2},{2,0},{4,6},{6,4},{8,10},{10,8},{12,14},{14,12},{16,18},{18,... | collective-permute-start | bytes 1671176 | tf_op jit(solution)/shard_map/ppermute | solution.py:106
  18.7 19.0 %collective-permute-start.7 = (bf16[128,2176]{1,0:T(8,128)(2,1)S(1)}, bf16[128,2176]{1,0:T(8,128)(2,1)S(1)}, u32[]{:S(2)}, u32[]{:S(2)}) collective-permute-start(bf16[128,2176]{1,0:T(8,128)(2,1)S(1)} %pad_maximum_fusion.refs_0_.refs_8_), channel_id=1, source_target_pairs={{0,4},{2,6},{4,0},{6,2},{8,12},{10,14},{12,8},{14,10},{16,20},{18,... | collective-permute-start | bytes 1671176 | tf_op jit(solution)/shard_map/ppermute | solution.py:106
  40.7 14.8 %collective-permute-start.11 = (bf16[4,128,512]{2,1,0:T(8,128)(2,1)}, bf16[4,128,512]{2,1,0:T(8,128)(2,1)}, u32[]{:S(2)}, u32[]{:S(2)}) collective-permute-start(bf16[4,128,512]{2,1,0:T(8,128)(2,1)} %get-tuple-element.69), channel_id=1, source_target_pairs={{0,8},{1,24},{2,10},{3,26},{4,12},{5,28},{6,14},{7,30},{8,0},{9,16... | collective-permute-start | bytes 1572872 | tf_op jit(solution)/shard_map/ppermute | solution.py:152
  41.2 14.4 %collective-permute-start.10 = (bf16[4,128,512]{2,1,0:T(8,128)(2,1)}, bf16[4,128,512]{2,1,0:T(8,128)(2,1)}, u32[]{:S(2)}, u32[]{:S(2)}) collective-permute-start(bf16[4,128,512]{2,1,0:T(8,128)(2,1)} %get-tuple-element.68), channel_id=1, source_target_pairs={{0,0},{1,16},{2,2},{3,18},{4,4},{5,20},{6,6},{7,22},{8,8},{9,24},{... | collective-permute-start | bytes 1572872 | tf_op jit(solution)/shard_map/ppermute | solution.py:152
  47.3 11.8 %collective-permute-start.8 = (bf16[128,2176]{1,0:T(8,128)(2,1)}, bf16[128,2176]{1,0:T(8,128)(2,1)}, u32[]{:S(2)}, u32[]{:S(2)}) collective-permute-start(bf16[128,2176]{1,0:T(8,128)(2,1)} %constant_dynamic-update-slice_fusion.refs_1_), channel_id=1, source_target_pairs={{0,2},{2,0},{4,6},{6,4},{8,10},{10,8},{12,14},{14,12},{16,18},{18,... | collective-permute-start | bytes 1671176 | tf_op jit(solution)/shard_map/ppermute | solution.py:106
  47.8 15.9 %collective-permute-start.9 = (bf16[128,2176]{1,0:T(8,128)(2,1)}, bf16[128,2176]{1,0:T(8,128)(2,1)}, u32[]{:S(2)}, u32[]{:S(2)}) collective-permute-start(bf16[128,2176]{1,0:T(8,128)(2,1)} %constant_dynamic-update-slice_fusion.refs_1_), channel_id=1, source_target_pairs={{0,4},{2,6},{4,0},{6,2},{8,12},{10,14},{12,8},{14,10},{16,20},{18,... | collective-permute-start | bytes 1671176 | tf_op jit(solution)/shard_map/ppermute | solution.py:106
  49.3 22.8 %collective-permute-start.12 = (bf16[128,2176]{1,0:T(8,128)(2,1)S(1)}, bf16[128,2176]{1,0:T(8,128)(2,1)S(1)}, u32[]{:S(2)}, u32[]{:S(2)}) collective-permute-start(bf16[128,2176]{1,0:T(8,128)(2,1)S(1)} %collective-permute-done.6.refs_2_.refs_9_), channel_id=1, source_target_pairs={{0,4},{2,6},{4,0},{6,2},{8,12},{10,14},{12,8},{14,10},{16,20},{18,... | collective-permute-start | bytes 1671176 | tf_op jit(solution)/shard_map/ppermute | solution.py:106
  74.8 15.0 %collective-permute-start.14 = (bf16[128,2176]{1,0:T(8,128)(2,1)}, bf16[128,2176]{1,0:T(8,128)(2,1)S(1)}, u32[]{:S(2)}, u32[]{:S(2)}) collective-permute-start(bf16[128,2176]{1,0:T(8,128)(2,1)} %collective-permute-done.9.refs_5_), channel_id=1, source_target_pairs={{0,2},{2,0},{4,6},{6,4},{8,10},{10,8},{12,14},{14,12},{16,18},{18,... | collective-permute-start | bytes 1671176 | tf_op jit(solution)/shard_map/ppermute | solution.py:106
  79.5 16.6 %collective-permute-start.22 = (bf16[128,1152]{1,0:T(8,128)(2,1)S(1)}, bf16[128,1152]{1,0:T(8,128)(2,1)S(1)}, u32[]{:S(2)}, u32[]{:S(2)}) collective-permute-start(bf16[128,1152]{1,0:T(8,128)(2,1)S(1)} %pad_maximum_fusion.1), channel_id=1, source_target_pairs={{0,16},{2,18},{4,20},{6,22},{8,24},{10,26},{12,28},{14,30},{16,0},... | collective-permute-start | bytes 884744 | tf_op jit(solution)/shard_map/ppermute | solution.py:106
  82.6 13.5 %collective-permute-start.21 = (bf16[1,1024,128]{2,1,0:T(8,128)(2,1)}, bf16[1,1024,128]{2,1,0:T(8,128)(2,1)S(1)}, u32[]{:S(2)}, u32[]{:S(2)}) collective-permute-start(bf16[1,1024,128]{2,1,0:T(8,128)(2,1)} %bitcast.74), channel_id=1, source_target_pairs={{0,8},{2,10},{4,12},{6,14},{8,0},{10,2},{12,4},{14,6},{16,24},{18,... | collective-permute-start | bytes 786440 | tf_op jit(solution)/shard_map/ppermute | solution.py:106
  89.0 13.1 %collective-permute-start.15 = (bf16[768,256]{1,0:T(8,128)(2,1)S(1)}, bf16[768,256]{1,0:T(8,128)(2,1)S(1)}, u32[]{:S(2)}, u32[]{:S(2)}) collective-permute-start(bf16[768,256]{1,0:T(8,128)(2,1)S(1)} %get-tuple-element.40.refs_2_), channel_id=1, source_target_pairs={{0,1},{1,0},{2,3},{3,2},{4,5},{5,4},{6,7},{7,6},{8,9},{9,8},{10,11... | collective-permute-start | bytes 1179656 | tf_op jit(solution)/shard_map/ppermute | solution.py:110
  96.1 26.9 %collective-permute-start.23 = (bf16[2,1024,128]{2,1,0:T(8,128)(2,1)S(1)}, bf16[2,1024,128]{2,1,0:T(8,128)(2,1)S(1)}, u32[]{:S(2)}, u32[]{:S(2)}) collective-permute-start(bf16[2,1024,128]{2,1,0:T(8,128)(2,1)S(1)} %constant_dynamic-update-slice_fusion.2.refs_4_), channel_id=1, source_target_pairs={{0,16},{2,18},{4,20},{6,22},{8,24},{10,26},{12,28},{14,30},{16,0},... | collective-permute-start | bytes 1572872 | tf_op jit(solution)/shard_map/ppermute | solution.py:106
  99.2 35.5 %collective-permute-start.27 = (bf16[2,1024,128]{2,1,0:T(8,128)(2,1)S(1)}, bf16[2,1024,128]{2,1,0:T(8,128)(2,1)S(1)}, u32[]{:S(2)}, u32[]{:S(2)}) collective-permute-start(bf16[2,1024,128]{2,1,0:T(8,128)(2,1)S(1)} %constant_dynamic-update-slice_fusion.2.refs_4_), channel_id=1, source_target_pairs={{0,1},{1,0},{2,3},{3,2},{4,5},{5,4},{6,7},{7,6},{8,9},{9,8},{10,11... | collective-permute-start | bytes 1572872 | tf_op jit(solution)/shard_map/ppermute | solution.py:110
  99.7 36.5 %collective-permute-start.34 = (bf16[256,1152]{1,0:T(8,128)(2,1)S(1)}, bf16[256,1152]{1,0:T(8,128)(2,1)S(1)}, u32[]{:S(2)}, u32[]{:S(2)}) collective-permute-start(bf16[256,1152]{1,0:T(8,128)(2,1)S(1)} %constant_dynamic-update-slice_fusion.4), channel_id=1, source_target_pairs={{0,2},{2,0},{4,6},{6,4},{8,10},{10,8},{12,14},{14,12},{16,18},{18,... | collective-permute-start | bytes 1769480 | tf_op jit(solution)/shard_map/ppermute | solution.py:106
  100.5 37.2 %collective-permute-start.35 = (bf16[256,1152]{1,0:T(8,128)(2,1)S(1)}, bf16[256,1152]{1,0:T(8,128)(2,1)S(1)}, u32[]{:S(2)}, u32[]{:S(2)}) collective-permute-start(bf16[256,1152]{1,0:T(8,128)(2,1)S(1)} %constant_dynamic-update-slice_fusion.4), channel_id=1, source_target_pairs={{0,4},{2,6},{4,0},{6,2},{8,12},{10,14},{12,8},{14,10},{16,20},{18,... | collective-permute-start | bytes 1769480 | tf_op jit(solution)/shard_map/ppermute | solution.py:106
  105.7 17.3 %collective-permute-start.19 = (bf16[4,64,128]{2,1,0:T(8,128)(2,1)S(1)}, bf16[4,64,128]{2,1,0:T(8,128)(2,1)S(1)}, u32[]{:S(2)}, u32[]{:S(2)}) collective-permute-start(bf16[4,64,128]{2,1,0:T(8,128)(2,1)S(1)} %get-tuple-element.81), channel_id=1, source_target_pairs={{0,24},{2,26},{4,28},{6,30},{8,16},{10,18},{12,20},{14,22},{16,8},... | collective-permute-start | bytes 196616 | tf_op jit(solution)/shard_map/ppermute | solution.py:106
  123.0 24.2 %collective-permute-start.28 = (bf16[2,1024,128]{2,1,0:T(8,128)(2,1)S(1)}, bf16[2,1024,128]{2,1,0:T(8,128)(2,1)S(1)}, u32[]{:S(2)}, u32[]{:S(2)}) collective-permute-start(bf16[2,1024,128]{2,1,0:T(8,128)(2,1)S(1)} %collective-permute-done.23.refs_5_), channel_id=1, source_target_pairs={{0,1},{1,0},{2,3},{3,2},{4,5},{5,4},{6,7},{7,6},{8,9},{9,8},{10,11... | collective-permute-start | bytes 1572872 | tf_op jit(solution)/shard_map/ppermute | solution.py:110
  134.6 12.6 %collective-permute-start.25 = (bf16[4,4,64,128]{3,2,1,0:T(8,128)(2,1)S(1)}, bf16[4,4,64,128]{3,2,1,0:T(8,128)(2,1)S(1)}, u32[]{:S(2)}, u32[]{:S(2)}) collective-permute-start(bf16[4,4,64,128]{3,2,1,0:T(8,128)(2,1)S(1)} %pad_maximum_fusion.3.refs_0_), channel_id=1, source_target_pairs={{0,4},{2,6},{4,0},{6,2},{8,12},{10,14},{12,8},{14,10},{16,20},{18,... | collective-permute-start | bytes 786440 | tf_op jit(solution)/shard_map/ppermute | solution.py:106
  136.1 11.1 %collective-permute-start.26 = (bf16[4,4,64,128]{3,2,1,0:T(8,128)(2,1)S(1)}, bf16[4,4,64,128]{3,2,1,0:T(8,128)(2,1)S(1)}, u32[]{:S(2)}, u32[]{:S(2)}) collective-permute-start(bf16[4,4,64,128]{3,2,1,0:T(8,128)(2,1)S(1)} %pad_maximum_fusion.3.refs_0_), channel_id=1, source_target_pairs={{0,6},{2,4},{4,2},{6,0},{8,14},{10,12},{12,10},{14,8},{16,22},{18,... | collective-permute-start | bytes 786440 | tf_op jit(solution)/shard_map/ppermute | solution.py:106
  155.3 12.8 %collective-permute-start.38 = (bf16[1024,1152]{1,0:T(8,128)(2,1)S(1)}, bf16[1024,1152]{1,0:T(8,128)(2,1)}, u32[]{:S(2)}, u32[]{:S(2)}) collective-permute-start(bf16[1024,1152]{1,0:T(8,128)(2,1)S(1)} %constant_dynamic-update-slice_fusion.6.n_own), channel_id=1, source_target_pairs={{0,1},{1,0},{2,3},{3,2},{4,5},{5,4},{6,7},{7,6},{8,9},{9,8},{10,11... | collective-permute-start | bytes 7077896 | tf_op jit(solution)/shard_map/ppermute | solution.py:110
  (23 other events, 195.2 us)

commit v7 on v6

--- a/solution.py
+++ b/solution.py
@@ -122,22 +122,35 @@
     return jnp.concatenate([own, hop(own, flip(0, 0, 1))])
 
 
+def relay_pairs(pair, z):
+    inner, outer = [], []
+    for c in range(CHIPS):
+        if coords(c)[0] in (1, 2):
+            inner.append((c, relative_chip(c, 0, 0, 3)))
+            outer.append((c, relative_chip(c, 0, 0, 1)))
+    met = hop(pair, inner)
+    return met, lambda met: jnp.where((z == 1) | (z == 2), met, hop(met, outer))
+
+
+def across(value_x, value_y):
+    half = value_x.shape[0] // 2
+    return [hop(value_x[:half], flip(1, 0)), hop(value_y[half:], flip(0, 1))]
+
+
 def heads_in_plane(w_proj, y, x):
     plane = NY * NX
     heads = w_proj.reshape(-1, 4, 2, plane, W).transpose(3, 2, 0, 1, 4)
     heads = heads.reshape(plane, 2, -1, 4 * W)
     out = jnp.zeros((2, plane, *heads.shape[2:]), heads.dtype)
-    first = None
+    came = []
     for by, bx in PLANE:
         spot = (y ^ by) * NX + (x ^ bx)
         piece = pick_row(heads, spot)
-        if (by, bx) == PLANE[-1]:
-            piece = after(piece, first)
         if (by, bx) != (0, 0):
             piece = hop(piece, flip(by, bx))
-            first = piece if first is None else first
+            came.append(piece)
         out = lax.dynamic_update_slice_in_dim(out, piece[:, None], spot, 1)
-    return out
+    return out, came
 
 
 def heads_along_z(heads, z):
@@ -200,50 +213,44 @@
     return pick.astype(BF16)
 
 
-def attend_kernel(*refs):
-    gate_query, kv_own, kv_other, marks = refs[:2], refs[2:4], refs[4:6], refs[6:8]
-    gated = refs[8]
+def attend_kernel(gate_query, kv_own, kv_other, marks, gated):
     pick = pick_columns({0: 128.0, 1: 1.0}, {2: 128.0, 3: 1.0})
     piece = gated.shape[2]
     tile = NZ * piece
-    groups = []
-    for group in range(2):
-        key_pos = lax.dot_general(pick, marks[group][...], ACROSS, preferred_element_type=F32)
-        groups.append((kv_own[group], key_pos[0:1]))
-        groups.append((kv_other[group], key_pos[1:2]))
+    key_pos = lax.dot_general(pick, marks[...], ACROSS, preferred_element_type=F32)
     for k in range(len(PLANE)):
-        group, base = (0, k * tile) if k < len(PLANE) - 1 else (1, 0)
-        span = pl.ds(base, tile)
-        query = gate_query[group][span, W:]
-        q_pos = lax.dot_general(
-            marks[group][span, :], pick, ACROSS, preferred_element_type=F32
-        )[:, :1]
+        span = pl.ds(k * tile, tile)
+        query = gate_query[span, W:]
+        q_pos = lax.dot_general(marks[span, :], pick, ACROSS, preferred_element_type=F32)[:, :1]
         attn = jnp.zeros((tile, W), F32)
-        for kv, key_pos in groups:
+        for side, kv in enumerate((kv_own, kv_other)):
             scores = lax.dot_general(
                 query, kv[:, W:], ACROSS, preferred_element_type=F32
             ) * W ** (-0.5)
-            weight = jnp.where(key_pos <= q_pos, silu(scores), 0.0).astype(BF16)
+            visible = key_pos[side : side + 1] <= q_pos
+            weight = jnp.where(visible, silu(scores), 0.0).astype(BF16)
             attn += jnp.dot(weight, kv[:, :W], preferred_element_type=F32)
         normed = attn * lax.rsqrt(jnp.mean(attn * attn, axis=-1, keepdims=True) + 1e-06)
-        out = (normed * gate_query[group][span, :W].astype(F32)).astype(BF16)
+        out = (normed * gate_query[span, :W].astype(F32)).astype(BF16)
         for s in range(NZ):
             gated[s, k] = out[s * piece : (s + 1) * piece]
 
 
 def hidden_kernel(where, *refs):
     n = len(PLANE)
-    gated, w_own, w_other, tok = refs[:n], refs[n : n + 2], refs[n + 2 : n + 4], refs[n + 4 : -5]
+    gated, w_own, w_other, tok = refs[: n + 1], refs[n + 1 : n + 3], refs[n + 3 : n + 5], refs[n + 5 : -5]
     hidden, g_all, t_all, w_all, sems = refs[-5:]
     z, y, x, u = (where[i] for i in range(4))
     c = chip_at(z, y, x)
     rows = hidden.shape[1]
     half = w_all.shape[1]
+    inner = ((z + 1) // 2) % 2
     copies = []
     for s in range(NZ):
         cols = pl.ds(s * W, W)
         for side, src in enumerate((w_own, w_other)):
-            copies.append((src[s // 2].at[s % 2], w_all.at[side, :, cols]))
+            panel = src[0].at[s] if s < 2 else src[1].at[(s % 2) ^ inner]
+            copies.append((panel, w_all.at[side, :, cols]))
         block = relative_chip(c, 0, 0, s)
         from_cols = pl.ds(pl.multiple_of(block * W, W), W)
         for k in range(n):
@@ -257,7 +264,8 @@
             cols = pl.ds(pl.multiple_of(head * W, W), W)
             for j, (jy, jx) in enumerate(PLANE):
                 block = (jy ^ by) * NX + (jx ^ bx)
-                g_all[block * rows : (block + 1) * rows, cols] = gated[k][s, j]
+                piece = gated[k][s, j] if k < n - 1 else gated[k + s // 2][s % 2, j]
+                g_all[block * rows : (block + 1) * rows, cols] = piece
     for copy in copies:
         copy.wait()
     total = 0.0
@@ -312,7 +320,17 @@
     neg_logit = dots * h_scale * lax.rsqrt(nn + 1e-06)
     mass = jnp.where(n_ids != t_ids[...].astype(F32), jnp.exp(neg_logit), 0.0)
     total = jnp.exp(pos_logit) + jnp.sum(mass, axis=1, keepdims=True)
-    loss[...] = jnp.log(total) - pos_logit
+    column = jnp.log(total) - pos_logit
+    size = column.shape[0]
+    line = lax.broadcasted_iota(jnp.int32, (size, size), 0)
+    lane = lax.broadcasted_iota(jnp.int32, (size, size), 1)
+    loss[...] = jnp.sum(jnp.where(line == lane, column, 0.0), axis=0, keepdims=True)
+
+
+def join_kernel(where, keep, theirs, hidden):
+    u, rows = where[3], keep.shape[0]
+    hidden[pl.ds(pl.multiple_of(u * rows, rows), rows), :] = keep[...]
+    hidden[pl.ds(pl.multiple_of((1 - u) * rows, rows), rows), :] = theirs[...]
 
 
 def call(kernel, name, outs, scratch, args, places, flops):
@@ -365,31 +383,30 @@
     p_own = lax.dynamic_slice_in_dim(positions, u * rows, rows, 0)
     p_other = lax.dynamic_slice_in_dim(positions, (1 - u) * rows, rows, 0)
     mine = with_marks(mine, whole_parts(p_own, 128) + whole_parts(p_other, 128))
-    line = [mine] + [hop(mine, flip(0, 0, s)) for s in range(1, NZ)]
-    low = jnp.concatenate(line[:2])
+    low = pair_up(mine)
 
     to_x, to_y = flip(0, 1), flip(1, 0)
+    high = hop(low, flip(0, 0, 2))
+    w_plane, came = heads_in_plane(w_proj, y, x)
+    low = after(low, came[:2])
     low_x, low_y = hop(low, to_x), hop(low, to_y)
-    w_plane = heads_in_plane(w_proj, y, x)
-    w_plane, high = lax.optimization_barrier((w_plane, after(line[2:], low_x, low_y)))
-    high = jnp.concatenate(high)
+    low_xy = across(low_x, low_y)
+    w_plane = after(w_plane, high)
     high_x, high_y = hop(high, to_x), hop(high, to_y)
-    low_xy, high_xy = hop(low_x, to_y), hop(high_y, to_x)
-    tok = [low, high, low_x, high_x, low_y, high_y, low_xy, high_xy]
-    w_mine = after(heads_along_z(w_plane, z), high_x, high_y, low_xy)
+    high_xy = across(high_x, high_y)
+    tok = [low, high, low_x, high_x, low_y, high_y, *low_xy, *high_xy]
+    w_mine = after(heads_along_z(w_plane, z), low_xy, high_xy)
     w_theirs = swap_cores(w_mine)
 
+    t_rows = after(target_emb.reshape(2, rows, -1), high)
+    t_keep = pick_row(t_rows, u)
+    t_send = swap_cores(pick_row(t_rows, 1 - u))
     own_ids = lax.dynamic_slice_in_dim(neg_ids, c * negs, negs, 0)
     norms = jnp.sum(jnp.square(neg_emb.astype(F32)), axis=1)
     neg = with_marks(neg_emb, float_parts(norms) + whole_parts(own_ids, 256))
-    neg_pair = pair_up(after(neg, w_mine))
-    neg_pair = after(neg_pair, w_theirs)
-    neg_near = jnp.concatenate([neg_pair, hop(neg_pair, flip(0, 0, 2))])
+    neg_pair = pair_up(after(neg, w_mine, t_send))
+    neg_met, neg_far = relay_pairs(after(neg_pair, w_theirs), z)
     out_pair = pair_up(after(w_out[None], neg_pair))
-    out_own = [out_pair, hop(after(out_pair, neg_near), flip(0, 0, 2))]
-    t_rows = target_emb.reshape(2, rows, -1)
-    t_keep = pick_row(t_rows, u)
-    t_send = swap_cores(pick_row(t_rows, 1 - u))
 
     def project(pieces):
         count = sum(p.shape[0] for p in pieces)
@@ -408,30 +425,28 @@
             2 * count * model * 4 * W,
         )
 
-    gq_early, kv_early, marks_early = project(tok[:6])
-    kv_early_theirs = swap_cores(kv_early)
-    gq_last, kv_last, marks_last = project(after(tok[6:], kv_early))
-    kv_last_theirs = swap_cores(kv_last)
-    neg_near = after(neg_near, kv_last)
-    neg_x, neg_y = hop(neg_near, flip(0, 1)), hop(neg_near, flip(1, 0))
+    gate_query, value_key, marks = project(tok)
+    kv_theirs = swap_cores(value_key)
+    out_met, out_far = relay_pairs(after(out_pair, neg_met, value_key), z)
+    neg_near = jnp.concatenate([neg_pair, neg_far(after(neg_met, value_key))])
+    neg_row = jnp.concatenate([neg_near, hop(neg_near, to_x)])
+    neg_own = [neg_row, hop(neg_row, to_y)]
     (gated,) = call(
         attend_kernel,
         "attend",
         [((NZ, plane, rows, W), BF16)],
         [],
-        [gq_early, gq_last, kv_early, kv_last, kv_early_theirs, kv_last_theirs]
-        + [marks_early, marks_last],
-        8 * "v",
+        [gate_query, value_key, kv_theirs, marks],
+        4 * "v",
         8 * events * events * W,
     )
+    gated = after(gated, neg_near)
     gated = jnp.stack([gated[0]] + [hop(gated[s], flip(0, 0, s)) for s in range(1, NZ)])
+    out_met = after(out_met, gated)
+    gated = [gated, hop(gated, to_x), hop(gated, to_y)]
+    gated += across(gated[1], gated[2])
+    out_own = [after(out_pair, gated), after(out_far(out_met), gated)]
     out_other = [swap_cores(w) for w in out_own]
-    gated = after(gated, out_own)
-    gated = [gated] + [hop(gated, flip(by, bx)) for by, bx in PLANE[1:]]
-    neg_x, neg_y = after((neg_x, neg_y), gated, out_other)
-    part = neg_x.shape[0] // 2
-    neg_own = [neg_near, neg_x, neg_y]
-    neg_own += [hop(neg_x[:part], flip(1, 0)), hop(neg_y[part:], flip(0, 1))]
     (hidden,) = call(
         hidden_kernel,
         "hidden",
@@ -442,8 +457,8 @@
             pltpu.VMEM((2, half, NZ * W), BF16),
             pltpu.SemaphoreType.DMA((NZ * (2 + plane),)),
         ],
-        [where, *gated, *out_own, *out_other, *tok[::2]],
-        "s" + 4 * "v" + 8 * "h",
+        [where, *gated, *out_own, *out_other, *tok[:7:2]],
+        "s" + 5 * "v" + 8 * "h",
         2 * plane * rows * model * NZ * W,
     )
     pieces = [hidden[0]] + [hop(hidden[k], flip(*PLANE[k])) for k in range(1, plane)]
@@ -462,7 +477,7 @@
     (loss,) = call(
         loss_kernel,
         "loss",
-        [((rows, 1), F32)],
+        [((1, rows), F32)],
         [
             pltpu.VMEM((2, CHIPS * negs, half + W), BF16),
             pltpu.SemaphoreType.DMA((2,)),
@@ -471,10 +486,14 @@
         "vvvvvhh",
         2 * rows * model * neg_ids.shape[0],
     )
-    hidden = jnp.where(
-        u == 0,
-        jnp.concatenate([h_keep, h_theirs]),
-        jnp.concatenate([h_theirs, h_keep]),
+    (hidden,) = call(
+        join_kernel,
+        "join",
+        [((2 * rows, half), BF16)],
+        [],
+        [where, h_keep, after(h_theirs, loss)],
+        "svv",
+        0,
     )
     return hidden, loss.reshape(-1)
 

time: 173 us -> 178 us (1.029)
  starting transfers between devices: 44.7 us -> 50.1 us
  waiting for transfers between devices: 88.7 us -> 86.6 us
    ppermute x2, waiting for transfers between devices: 4.84 us -> 0.52 us  [heads_along_z(): lax.ppermute(pick_row(heads, e ^ z & 1), ('ctx', 'tp'), perm)]
    ppermute x8 -> x7, starting transfers between devices: 1.27 us -> 5.18 us  [swap_cores(): return lax.ppermute(value, 'tp', SWAP)]
    ppermute x8 -> x7, waiting for transfers between devices: 0.42 us -> 2.43 us  [swap_cores(): return lax.ppermute(value, 'tp', SWAP)]
    dynamic_update_slice x4, local copies, waits for them, and re-layouts: 1.98 us -> 0.09 us  [heads_in_plane(): out = lax.dynamic_update_slice_in_dim(out, piece[:, None], spot, 1)]
    unnamed x24 -> x48, local copies, waits for them, and re-layouts: 5.21 us -> 7.09 us
    ppermute x29 -> x31, starting transfers between devices: 37.6 us -> 39.3 us  [hop(): return lax.ppermute(value, 'ctx', perm)]
    ppermute x29 -> x31, waiting for transfers between devices: 83.5 us -> 83.7 us  [hop(): return lax.ppermute(value, 'ctx', perm)]
  transfers between devices with their start and end apart: 39 -> 40, of which waited for: 22 -> 21; matrix products, arithmetic and copies ran while one was open for 8% -> 9% of each run, Pallas kernels for 8% -> 9%
where the time goes in v7:
time: 178 us
  waiting for transfers between devices  86.6 us (49%)
  starting transfers between devices  50.1 us (28%)
  Pallas kernels  16.9 us (9%)
  local copies, waits for them, and re-layouts  14.1 us (8%)
  other arithmetic  8.62 us (5%)
    ppermute x31, waiting for transfers between devices, hop(): return lax.ppermute(value, 'ctx', perm)  83.7 us
    ppermute x31, starting transfers between devices, hop(): return lax.ppermute(value, 'ctx', perm)  39.3 us
    pallas_call x6, Pallas kernels, call(): pl.pallas_call(kernel, out_shape=[jax.ShapeDtypeStruct(shape, dtype) for...  16.9 us
    unnamed x48, local copies, waits for them, and re-layouts  7.09 us
    ppermute x2, starting transfers between devices, heads_along_z(): lax.ppermute(pick_row(heads, e ^ z & 1), ('ctx', 'tp'), perm)  5.57 us
    ppermute x7, starting transfers between devices, swap_cores(): return lax.ppermute(value, 'tp', SWAP)  5.18 us
  transfers between devices with their start and end apart: 40, of which 21 were waited for; matrix products, arithmetic and copies ran while one was open for 9% of the time, Pallas kernels for 9%

profile of v7, /device:TPU:0, one launch (start us, length us, event | category | flops | bytes accessed | tf_op | source)
XLA Modules:
  0.0 177.5 jit_solution(17906733520656832169)
XLA Ops:
  1.8 3.1 %collective-permute-start = (bf16[64,2176]{1,0:T(8,128)(2,1)S(1)}, bf16[64,2176]{1,0:T(8,128)(2,1)S(1)}, u32[]{:S(2)}, u32[]{:S(2)}) collective-permute-start(bf16[64,2176]{1,0:T(8,128)(2,1)S(1)} %pad_maximum_fusion.3), channel_id=1, source_target_pairs={{0,8},{2,10},{4,12},{6,14},{8,0},{10,2},{12,4},{14,6},{16,24},{18,... | collective-permute-start | bytes 835592 | tf_op jit(solution)/shard_map/ppermute | solution.py:106
  12.4 2.7 %collective-permute-start.3 = (bf16[128,2176]{1,0:T(8,128)(2,1)S(1)}, bf16[128,2176]{1,0:T(8,128)(2,1)}, u32[]{:S(2)}, u32[]{:S(2)}) collective-permute-start(bf16[128,2176]{1,0:T(8,128)(2,1)S(1)} %pad_maximum_fusion.2.refs_0_.refs_9_), channel_id=1, source_target_pairs={{0,16},{2,18},{4,20},{6,22},{8,24},{10,26},{12,28},{14,30},{16,0},... | collective-permute-start | bytes 1671176 | tf_op jit(solution)/shard_map/ppermute | solution.py:106
  16.4 6.2 %collective-permute-done.2 = bf16[2,128,512]{2,1,0:T(8,128)(2,1)S(1)} collective-permute-done((bf16[2,128,512]{2,1,0:T(8,128)(2,1)}, bf16[2,128,512]{2,1,0:T(8,128)(2,1)S(1)}, u32[]{:S(2)}, u32[]{:S(2)}) %collective-permute-start.2) | collective-permute-done | bytes 262176 | tf_op jit(solution)/shard_map/ppermute | solution.py:106
  24.5 14.2 %collective-permute-done.3.refs_1_ = bf16[128,2176]{1,0:T(8,128)(2,1)} collective-permute-done((bf16[128,2176]{1,0:T(8,128)(2,1)S(1)}, bf16[128,2176]{1,0:T(8,128)(2,1)}, u32[]{:S(2)}, u32[]{:S(2)}) %collective-permute-start.3) | collective-permute-done | bytes 557088 | tf_op jit(solution)/shard_map/ppermute | solution.py:106
  43.1 5.4 %collective-permute-start.13 = (bf16[4,128,512]{2,1,0:T(8,128)(2,1)}, bf16[4,128,512]{2,1,0:T(8,128)(2,1)}, u32[]{:S(2)}, u32[]{:S(2)}) collective-permute-start(bf16[4,128,512]{2,1,0:T(8,128)(2,1)} %get-tuple-element.50), channel_id=1, source_target_pairs={{0,0},{1,16},{2,2},{3,18},{4,4},{5,20},{6,6},{7,22},{8,8},{9,24},{... | collective-permute-start | bytes 1572872 | tf_op jit(solution)/shard_map/ppermute | solution.py:165
  49.8 3.0 %collective-permute-done.5.refs_3_ = bf16[128,2176]{1,0:T(8,128)(2,1)S(1)} collective-permute-done((bf16[128,2176]{1,0:T(8,128)(2,1)}, bf16[128,2176]{1,0:T(8,128)(2,1)S(1)}, u32[]{:S(2)}, u32[]{:S(2)}) %collective-permute-start.5) | collective-permute-done | bytes 557088 | tf_op jit(solution)/shard_map/ppermute | solution.py:106
  54.4 1.7 collective-permute-done.7.refs_5_
  60.4 2.8 %maximum_select_fusion = bf16[2,4,128,512]{3,2,1,0:T(8,128)(2,1)} fusion(bf16[1,4,128,512]{3,2,1,0:T(8,128)(2,1)} %bitcast.21, bf16[1,4,128,512]{3,2,1,0:T(8,128)(2,1)} %bitcast.19, pred[]{:T(512)S(6)} %eq.19), kind=kLoop, calls=%fused_computation.1 | loop fusion | flops 1572864 | bytes 2097153 | tf_op jit(solution)/shard_map/jit(_where)/select_n | solution.py:166
  63.2 2.8 %collective-permute-done.10.refs_8_ = bf16[64,2176]{1,0:T(8,128)(2,1)S(1)} collective-permute-done((bf16[64,2176]{1,0:T(8,128)(2,1)S(1)}, bf16[64,2176]{1,0:T(8,128)(2,1)S(1)}, u32[]{:S(2)}, u32[]{:S(2)}) %collective-permute-start.10) | collective-permute-done | bytes 278560 | tf_op jit(solution)/shard_map/ppermute | solution.py:106
  67.4 4.2 %collective-permute-start.15 = (bf16[1024,512]{1,0:T(8,128)(2,1)}, bf16[1024,512]{1,0:T(8,128)(2,1)}, u32[]{:S(2)}, u32[]{:S(2)}) collective-permute-start(bf16[1024,512]{1,0:T(8,128)(2,1)} %bitcast.22.refs_10_), channel_id=1, source_target_pairs={{0,1},{1,0},{2,3},{3,2},{4,5},{5,4},{6,7},{7,6},{8,9},{9,8},{10,11... | collective-permute-start | bytes 3145736 | tf_op jit(solution)/shard_map/ppermute | solution.py:110
  74.5 5.9 %collective-permute-done.18 = bf16[64,1152]{1,0:T(8,128)(2,1)S(1)} collective-permute-done((bf16[64,1152]{1,0:T(8,128)(2,1)S(1)}, bf16[64,1152]{1,0:T(8,128)(2,1)S(1)}, u32[]{:S(2)}, u32[]{:S(2)}) %collective-permute-start.18) | collective-permute-done | bytes 147488 | tf_op jit(solution)/shard_map/ppermute | solution.py:106
  82.9 5.1 %project.1 = (bf16[1024,256]{1,0:T(8,128)(2,1)S(1)}, bf16[1024,256]{1,0:T(8,128)(2,1)S(1)}, bf16[1024,128]{1,0:T(8,128)(2,1)S(1)}) custom-call(s32[4]{0:T(128)S(1)} %pad_add_fusion.where, bf16[128,2176]{1,0:T(8,128)(2,1)S(1)} %pad_maximum_fusion.2.refs_0_.refs_9_, bf16[128,2176]{1,0:T(8,128)(2,1)} %collective-permute-done.3.refs_1_, ...), custom_call_target="tpu_custom_call" | custom-call | flops 2147483648 | bytes 6553616 | tf_op jit(solution)/shard_map/project/pallas_call | solution.py:339
  90.8 3.3 %collective-permute-start.28 = (bf16[1,1024,128]{2,1,0:T(8,128)(2,1)}, bf16[1,1024,128]{2,1,0:T(8,128)(2,1)S(1)}, u32[]{:S(2)}, u32[]{:S(2)}) collective-permute-start(bf16[1,1024,128]{2,1,0:T(8,128)(2,1)} %bitcast.73), channel_id=1, source_target_pairs={{0,8},{2,10},{4,12},{6,14},{8,0},{10,2},{12,4},{14,6},{16,24},{18,... | collective-permute-start | bytes 786440 | tf_op jit(solution)/shard_map/ppermute | solution.py:106
  95.2 6.4 %collective-permute-done.20 = bf16[128,1152]{1,0:T(8,128)(2,1)} collective-permute-done((bf16[128,1152]{1,0:T(8,128)(2,1)}, bf16[128,1152]{1,0:T(8,128)(2,1)}, u32[]{:S(2)}, u32[]{:S(2)}) %collective-permute-start.20) | collective-permute-done | bytes 294944 | tf_op jit(solution)/shard_map/ppermute | solution.py:106
  107.3 3.2 %attend.1 = bf16[4,4,64,128]{3,2,1,0:T(8,128)(2,1)S(1)} custom-call(bf16[1024,256]{1,0:T(8,128)(2,1)S(1)} %copy-done.12, bf16[1024,256]{1,0:T(8,128)(2,1)S(1)} %copy-done.4, bf16[1024,256]{1,0:T(8,128)(2,1)S(1)} %collective-permute-done.16.kv_other, bf16[1024,128]{1,0:T(8,128)(2,1)S(1)} %copy-done.14), custom_call_target="tpu_custom_call" | custom-call | flops 1073741824 | bytes 1835008 | tf_op jit(solution)/shard_map/attend/pallas_call | solution.py:339
  110.5 2.3 %collective-permute-start.23 = (bf16[4,64,128]{2,1,0:T(8,128)(2,1)S(1)}, bf16[4,64,128]{2,1,0:T(8,128)(2,1)S(1)}, u32[]{:S(2)}, u32[]{:S(2)}) collective-permute-start(bf16[4,64,128]{2,1,0:T(8,128)(2,1)S(1)} %get-tuple-element.63), channel_id=1, source_target_pairs={{0,24},{2,26},{4,28},{6,30},{8,16},{10,18},{12,20},{14,22},{16,8},... | collective-permute-start | bytes 196616 | tf_op jit(solution)/shard_map/ppermute | solution.py:106
  115.0 2.3 %collective-permute-done.23 = bf16[4,64,128]{2,1,0:T(8,128)(2,1)S(1)} collective-permute-done((bf16[4,64,128]{2,1,0:T(8,128)(2,1)S(1)}, bf16[4,64,128]{2,1,0:T(8,128)(2,1)S(1)}, u32[]{:S(2)}, u32[]{:S(2)}) %collective-permute-start.23) | collective-permute-done | bytes 65568 | tf_op jit(solution)/shard_map/ppermute | solution.py:106
  117.3 7.0 %collective-permute-done.22 = bf16[4,64,128]{2,1,0:T(8,128)(2,1)S(1)} collective-permute-done((bf16[4,64,128]{2,1,0:T(8,128)(2,1)S(1)}, bf16[4,64,128]{2,1,0:T(8,128)(2,1)S(1)}, u32[]{:S(2)}, u32[]{:S(2)}) %collective-permute-start.22) | collective-permute-done | bytes 65568 | tf_op jit(solution)/shard_map/ppermute | solution.py:106
  128.7 3.0 %collective-permute-done.24.refs_1_ = bf16[4,4,64,128]{3,2,1,0:T(8,128)(2,1)S(1)} collective-permute-done((bf16[4,4,64,128]{3,2,1,0:T(8,128)(2,1)S(1)}, bf16[4,4,64,128]{3,2,1,0:T(8,128)(2,1)S(1)}, u32[]{:S(2)}, u32[]{:S(2)}) %collective-permute-start.24) | collective-permute-done | bytes 262176 | tf_op jit(solution)/shard_map/ppermute | solution.py:106
  131.8 2.4 %collective-permute-done.25.refs_2_ = bf16[4,4,64,128]{3,2,1,0:T(8,128)(2,1)S(1)} collective-permute-done((bf16[4,4,64,128]{3,2,1,0:T(8,128)(2,1)S(1)}, bf16[4,4,64,128]{3,2,1,0:T(8,128)(2,1)S(1)}, u32[]{:S(2)}, u32[]{:S(2)}) %collective-permute-start.25) | collective-permute-done | bytes 262176 | tf_op jit(solution)/shard_map/ppermute | solution.py:106
  135.8 22.4 %collective-permute-done.26.refs_3_ = bf16[2,4,64,128]{3,2,1,0:T(8,128)(2,1)S(1)} collective-permute-done((bf16[2,4,64,128]{3,2,1,0:T(8,128)(2,1)S(1)}, bf16[2,4,64,128]{3,2,1,0:T(8,128)(2,1)S(1)}, u32[]{:S(2)}, u32[]{:S(2)}) %collective-permute-start.26) | collective-permute-done | bytes 131104 | tf_op jit(solution)/shard_map/ppermute | solution.py:106
  160.8 2.2 %hidden.1 = bf16[4,64,512]{2,1,0:T(8,128)(2,1)S(1)} custom-call(s32[4]{0:T(128)S(1)} %pad_add_fusion.where, bf16[4,4,64,128]{3,2,1,0:T(8,128)(2,1)S(1)} %pad_maximum_fusion.4.refs_0_, bf16[4,4,64,128]{3,2,1,0:T(8,128)(2,1)S(1)} %collective-permute-done.24.refs_1_, bf16[4,4,64,128]{3,2,1,0:T(8,128)(2,1)S(1)} %collective-permute-done.25.refs_2_, ...), custom_call_target="tpu_custom_call" | custom-call | flops 536870912 | bytes 5095440 | tf_op jit(solution)/shard_map/hidden/pallas_call | solution.py:339
  168.1 2.1 %collective-permute-done.34.refs_2_ = bf16[64,512]{1,0:T(8,128)(2,1)S(1)} collective-permute-done((bf16[64,512]{1,0:T(8,128)(2,1)S(1)}, bf16[64,512]{1,0:T(8,128)(2,1)S(1)}, u32[]{:S(2)}, u32[]{:S(2)}) %collective-permute-start.34) | collective-permute-done | bytes 65568 | tf_op jit(solution)/shard_map/ppermute | solution.py:106
  171.8 4.1 %loss.1 = f32[1,64]{1,0:T(1,128)} custom-call(bf16[64,1024]{1,0:T(8,128)(2,1)S(1)} %get-tuple-element.39.h_keep.keep, bf16[64,1024]{1,0:T(8,128)(2,1)S(1)} %get-tuple-element.40.h_send, bf16[64,1024]{1,0:T(8,128)(2,1)S(1)} %get-tuple-element.56.t_keep, bf16[64,1024]{1,0:T(8,128)(2,1)S(1)} %collective-permute-done.17.t_send, s32[64,1]{1,0:T(8,128)S(1)} %copy.63.t_ids, ...), custom_call_target="tpu_custom_call" | custom-call | flops 268435456 | bytes 5243136 | tf_op jit(solution)/shard_map/loss/pallas_call | solution.py:339
  (157 shorter events, 58.4 us)
Async XLA Ops:
  1.8 10.6 %collective-permute-start = (bf16[64,2176]{1,0:T(8,128)(2,1)S(1)}, bf16[64,2176]{1,0:T(8,128)(2,1)S(1)}, u32[]{:S(2)}, u32[]{:S(2)}) collective-permute-start(bf16[64,2176]{1,0:T(8,128)(2,1)S(1)} %pad_maximum_fusion.3), channel_id=1, source_target_pairs={{0,8},{2,10},{4,12},{6,14},{8,0},{10,2},{12,4},{14,6},{16,24},{18,... | collective-permute-start | bytes 835592 | tf_op jit(solution)/shard_map/ppermute | solution.py:106
  9.3 13.3 %collective-permute-start.2 = (bf16[2,128,512]{2,1,0:T(8,128)(2,1)}, bf16[2,128,512]{2,1,0:T(8,128)(2,1)S(1)}, u32[]{:S(2)}, u32[]{:S(2)}) collective-permute-start(bf16[2,128,512]{2,1,0:T(8,128)(2,1)} %bitcast.12), channel_id=1, source_target_pairs={{0,4},{2,6},{4,0},{6,2},{8,12},{10,14},{12,8},{14,10},{16,20},{18,... | collective-permute-start | bytes 786440 | tf_op jit(solution)/shard_map/ppermute | solution.py:106
  11.6 11.6 %collective-permute-start.12 = (bf16[2,128,512]{2,1,0:T(8,128)(2,1)}, bf16[2,128,512]{2,1,0:T(8,128)(2,1)S(1)}, u32[]{:S(2)}, u32[]{:S(2)}) collective-permute-start(bf16[2,128,512]{2,1,0:T(8,128)(2,1)} %bitcast.16), channel_id=1, source_target_pairs={{0,6},{2,4},{4,2},{6,0},{8,14},{10,12},{12,10},{14,8},{16,22},{18,... | collective-permute-start | bytes 786440 | tf_op jit(solution)/shard_map/ppermute | solution.py:106
  12.4 26.3 %collective-permute-start.3 = (bf16[128,2176]{1,0:T(8,128)(2,1)S(1)}, bf16[128,2176]{1,0:T(8,128)(2,1)}, u32[]{:S(2)}, u32[]{:S(2)}) collective-permute-start(bf16[128,2176]{1,0:T(8,128)(2,1)S(1)} %pad_maximum_fusion.2.refs_0_.refs_9_), channel_id=1, source_target_pairs={{0,16},{2,18},{4,20},{6,22},{8,24},{10,26},{12,28},{14,30},{16,0},... | collective-permute-start | bytes 1671176 | tf_op jit(solution)/shard_map/ppermute | solution.py:106
  22.6 20.5 %collective-permute-start.4 = (bf16[128,2176]{1,0:T(8,128)(2,1)S(1)}, bf16[128,2176]{1,0:T(8,128)(2,1)S(1)}, u32[]{:S(2)}, u32[]{:S(2)}) collective-permute-start(bf16[128,2176]{1,0:T(8,128)(2,1)S(1)} %pad_maximum_fusion.2.refs_0_.refs_9_), channel_id=1, source_target_pairs={{0,2},{2,0},{4,6},{6,4},{8,10},{10,8},{12,14},{14,12},{16,18},{18,... | collective-permute-start | bytes 1671176 | tf_op jit(solution)/shard_map/ppermute | solution.py:106
  23.2 26.0 %collective-permute-start.6 = (bf16[128,2176]{1,0:T(8,128)(2,1)S(1)}, bf16[128,2176]{1,0:T(8,128)(2,1)S(1)}, u32[]{:S(2)}, u32[]{:S(2)}) collective-permute-start(bf16[128,2176]{1,0:T(8,128)(2,1)S(1)} %pad_maximum_fusion.2.refs_0_.refs_9_), channel_id=1, source_target_pairs={{0,4},{2,6},{4,0},{6,2},{8,12},{10,14},{12,8},{14,10},{16,20},{18,... | collective-permute-start | bytes 1671176 | tf_op jit(solution)/shard_map/ppermute | solution.py:106
  38.7 14.1 %collective-permute-start.5 = (bf16[128,2176]{1,0:T(8,128)(2,1)}, bf16[128,2176]{1,0:T(8,128)(2,1)S(1)}, u32[]{:S(2)}, u32[]{:S(2)}) collective-permute-start(bf16[128,2176]{1,0:T(8,128)(2,1)} %collective-permute-done.3.refs_1_), channel_id=1, source_target_pairs={{0,2},{2,0},{4,6},{6,4},{8,10},{10,8},{12,14},{14,12},{16,18},{18,... | collective-permute-start | bytes 1671176 | tf_op jit(solution)/shard_map/ppermute | solution.py:106
  40.2 15.9 %collective-permute-start.7 = (bf16[128,2176]{1,0:T(8,128)(2,1)}, bf16[128,2176]{1,0:T(8,128)(2,1)}, u32[]{:S(2)}, u32[]{:S(2)}) collective-permute-start(bf16[128,2176]{1,0:T(8,128)(2,1)} %collective-permute-done.3.refs_1_), channel_id=1, source_target_pairs={{0,4},{2,6},{4,0},{6,2},{8,12},{10,14},{12,8},{14,10},{16,20},{18,... | collective-permute-start | bytes 1671176 | tf_op jit(solution)/shard_map/ppermute | solution.py:106
  42.9 16.2 %collective-permute-start.14 = (bf16[4,128,512]{2,1,0:T(8,128)(2,1)}, bf16[4,128,512]{2,1,0:T(8,128)(2,1)}, u32[]{:S(2)}, u32[]{:S(2)}) collective-permute-start(bf16[4,128,512]{2,1,0:T(8,128)(2,1)} %get-tuple-element.51), channel_id=1, source_target_pairs={{0,8},{1,24},{2,10},{3,26},{4,12},{5,28},{6,14},{7,30},{8,0},{9,16... | collective-permute-start | bytes 1572872 | tf_op jit(solution)/shard_map/ppermute | solution.py:165
  43.1 17.3 %collective-permute-start.13 = (bf16[4,128,512]{2,1,0:T(8,128)(2,1)}, bf16[4,128,512]{2,1,0:T(8,128)(2,1)}, u32[]{:S(2)}, u32[]{:S(2)}) collective-permute-start(bf16[4,128,512]{2,1,0:T(8,128)(2,1)} %get-tuple-element.50), channel_id=1, source_target_pairs={{0,0},{1,16},{2,2},{3,18},{4,4},{5,20},{6,6},{7,22},{8,8},{9,24},{... | collective-permute-start | bytes 1572872 | tf_op jit(solution)/shard_map/ppermute | solution.py:165
  49.2 13.9 %collective-permute-start.8 = (bf16[64,2176]{1,0:T(8,128)(2,1)S(1)}, bf16[64,2176]{1,0:T(8,128)(2,1)S(1)}, u32[]{:S(2)}, u32[]{:S(2)}) collective-permute-start(bf16[64,2176]{1,0:T(8,128)(2,1)S(1)} %slice.56), channel_id=1, source_target_pairs={{0,4},{2,6},{4,0},{6,2},{8,12},{10,14},{12,8},{14,10},{16,20},{18,... | collective-permute-start | bytes 835592 | tf_op jit(solution)/shard_map/ppermute | solution.py:106
  52.8 10.3 %collective-permute-start.9 = (bf16[64,2176]{1,0:T(8,128)(2,1)S(1)}, bf16[64,2176]{1,0:T(8,128)(2,1)S(1)}, u32[]{:S(2)}, u32[]{:S(2)}) collective-permute-start(bf16[64,2176]{1,0:T(8,128)(2,1)S(1)} %slice.57), channel_id=1, source_target_pairs={{0,2},{2,0},{4,6},{6,4},{8,10},{10,8},{12,14},{14,12},{16,18},{18,... | collective-permute-start | bytes 835592 | tf_op jit(solution)/shard_map/ppermute | solution.py:106
  67.4 13.0 %collective-permute-start.15 = (bf16[1024,512]{1,0:T(8,128)(2,1)}, bf16[1024,512]{1,0:T(8,128)(2,1)}, u32[]{:S(2)}, u32[]{:S(2)}) collective-permute-start(bf16[1024,512]{1,0:T(8,128)(2,1)} %bitcast.22.refs_10_), channel_id=1, source_target_pairs={{0,1},{1,0},{2,3},{3,2},{4,5},{5,4},{6,7},{7,6},{8,9},{9,8},{10,11... | collective-permute-start | bytes 3145736 | tf_op jit(solution)/shard_map/ppermute | solution.py:110
  89.5 12.1 %collective-permute-start.20 = (bf16[128,1152]{1,0:T(8,128)(2,1)}, bf16[128,1152]{1,0:T(8,128)(2,1)}, u32[]{:S(2)}, u32[]{:S(2)}) collective-permute-start(bf16[128,1152]{1,0:T(8,128)(2,1)} %collective-permute-done.19), channel_id=1, source_target_pairs={{8,0},{10,2},{12,4},{14,6},{16,24},{18,26},{20,28},{22,30},{9,1},{... | collective-permute-start | bytes 884744 | tf_op jit(solution)/shard_map/ppermute | solution.py:106
  90.8 14.7 %collective-permute-start.28 = (bf16[1,1024,128]{2,1,0:T(8,128)(2,1)}, bf16[1,1024,128]{2,1,0:T(8,128)(2,1)S(1)}, u32[]{:S(2)}, u32[]{:S(2)}) collective-permute-start(bf16[1,1024,128]{2,1,0:T(8,128)(2,1)} %bitcast.73), channel_id=1, source_target_pairs={{0,8},{2,10},{4,12},{6,14},{8,0},{10,2},{12,4},{14,6},{16,24},{18,... | collective-permute-start | bytes 786440 | tf_op jit(solution)/shard_map/ppermute | solution.py:106
  95.1 11.0 %collective-permute-start.16 = (bf16[1024,256]{1,0:T(8,128)(2,1)S(1)}, bf16[1024,256]{1,0:T(8,128)(2,1)S(1)}, u32[]{:S(2)}, u32[]{:S(2)}) collective-permute-start(bf16[1024,256]{1,0:T(8,128)(2,1)S(1)} %get-tuple-element.27.kv_own), channel_id=1, source_target_pairs={{0,1},{1,0},{2,3},{3,2},{4,5},{5,4},{6,7},{7,6},{8,9},{9,8},{10,11... | collective-permute-start | bytes 1572872 | tf_op jit(solution)/shard_map/ppermute | solution.py:110
  103.7 23.3 %collective-permute-start.37 = (bf16[256,1152]{1,0:T(8,128)(2,1)S(1)}, bf16[256,1152]{1,0:T(8,128)(2,1)S(1)}, u32[]{:S(2)}, u32[]{:S(2)}) collective-permute-start(bf16[256,1152]{1,0:T(8,128)(2,1)S(1)} %pad_maximum_fusion.1), channel_id=1, source_target_pairs={{0,2},{2,0},{4,6},{6,4},{8,10},{10,8},{12,14},{14,12},{16,18},{18,... | collective-permute-start | bytes 1769480 | tf_op jit(solution)/shard_map/ppermute | solution.py:106
  105.5 20.0 %collective-permute-start.29 = (bf16[2,1024,128]{2,1,0:T(8,128)(2,1)S(1)}, bf16[2,1024,128]{2,1,0:T(8,128)(2,1)S(1)}, u32[]{:S(2)}, u32[]{:S(2)}) collective-permute-start(bf16[2,1024,128]{2,1,0:T(8,128)(2,1)S(1)} %constant_dynamic-update-slice_fusion.2.refs_5_), channel_id=1, source_target_pairs={{8,16},{10,18},{12,20},{14,22},{16,8},{18,10},{20,12},{22,14},{9,1... | collective-permute-start | bytes 1572872 | tf_op jit(solution)/shard_map/ppermute | solution.py:106
  112.8 11.5 %collective-permute-start.22 = (bf16[4,64,128]{2,1,0:T(8,128)(2,1)S(1)}, bf16[4,64,128]{2,1,0:T(8,128)(2,1)S(1)}, u32[]{:S(2)}, u32[]{:S(2)}) collective-permute-start(bf16[4,64,128]{2,1,0:T(8,128)(2,1)S(1)} %get-tuple-element.64), channel_id=1, source_target_pairs={{0,16},{2,18},{4,20},{6,22},{8,24},{10,26},{12,28},{14,30},{16,0},... | collective-permute-start | bytes 196616 | tf_op jit(solution)/shard_map/ppermute | solution.py:106
  114.2 10.1 %collective-permute-start.21 = (bf16[4,64,128]{2,1,0:T(8,128)(2,1)S(1)}, bf16[4,64,128]{2,1,0:T(8,128)(2,1)S(1)}, u32[]{:S(2)}, u32[]{:S(2)}) collective-permute-start(bf16[4,64,128]{2,1,0:T(8,128)(2,1)S(1)} %get-tuple-element.65), channel_id=1, source_target_pairs={{0,8},{2,10},{4,12},{6,14},{8,0},{10,2},{12,4},{14,6},{16,24},{18,... | collective-permute-start | bytes 196616 | tf_op jit(solution)/shard_map/ppermute | solution.py:106
  125.5 32.7 %collective-permute-start.30 = (bf16[2,1024,128]{2,1,0:T(8,128)(2,1)S(1)}, bf16[2,1024,128]{2,1,0:T(8,128)(2,1)S(1)}, u32[]{:S(2)}, u32[]{:S(2)}) collective-permute-start(bf16[2,1024,128]{2,1,0:T(8,128)(2,1)S(1)} %collective-permute-done.29), channel_id=1, source_target_pairs={{8,0},{10,2},{12,4},{14,6},{16,24},{18,26},{20,28},{22,30},{9,1},{... | collective-permute-start | bytes 1572872 | tf_op jit(solution)/shard_map/ppermute | solution.py:106
  127.1 36.0 %collective-permute-start.38 = (bf16[512,1152]{1,0:T(8,128)(2,1)S(1)}, bf16[512,1152]{1,0:T(8,128)(2,1)S(1)}, u32[]{:S(2)}, u32[]{:S(2)}) collective-permute-start(bf16[512,1152]{1,0:T(8,128)(2,1)S(1)} %pad_maximum_fusion), channel_id=1, source_target_pairs={{0,4},{2,6},{4,0},{6,2},{8,12},{10,14},{12,8},{14,10},{16,20},{18,... | collective-permute-start | bytes 3538952 | tf_op jit(solution)/shard_map/ppermute | solution.py:106
  131.7 26.5 %collective-permute-start.26 = (bf16[2,4,64,128]{3,2,1,0:T(8,128)(2,1)S(1)}, bf16[2,4,64,128]{3,2,1,0:T(8,128)(2,1)S(1)}, u32[]{:S(2)}, u32[]{:S(2)}) collective-permute-start(bf16[2,4,64,128]{3,2,1,0:T(8,128)(2,1)S(1)} %slice.60), channel_id=1, source_target_pairs={{0,4},{2,6},{4,0},{6,2},{8,12},{10,14},{12,8},{14,10},{16,20},{18,... | collective-permute-start | bytes 393224 | tf_op jit(solution)/shard_map/ppermute | solution.py:106
  134.2 24.0 %collective-permute-start.27 = (bf16[2,4,64,128]{3,2,1,0:T(8,128)(2,1)S(1)}, bf16[2,4,64,128]{3,2,1,0:T(8,128)(2,1)S(1)}, u32[]{:S(2)}, u32[]{:S(2)}) collective-permute-start(bf16[2,4,64,128]{3,2,1,0:T(8,128)(2,1)S(1)} %slice.61), channel_id=1, source_target_pairs={{0,2},{2,0},{4,6},{6,4},{8,10},{10,8},{12,14},{14,12},{16,18},{18,... | collective-permute-start | bytes 393224 | tf_op jit(solution)/shard_map/ppermute | solution.py:106
  (38 other events, 274.1 us)

commit v8 on v7

--- a/solution.py
+++ b/solution.py
@@ -122,19 +122,16 @@
     return jnp.concatenate([own, hop(own, flip(0, 0, 1))])
 
 
-def relay_pairs(pair, z):
-    inner, outer = [], []
-    for c in range(CHIPS):
-        if coords(c)[0] in (1, 2):
-            inner.append((c, relative_chip(c, 0, 0, 3)))
-            outer.append((c, relative_chip(c, 0, 0, 1)))
-    met = hop(pair, inner)
-    return met, lambda met: jnp.where((z == 1) | (z == 2), met, hop(met, outer))
-
-
-def across(value_x, value_y):
-    half = value_x.shape[0] // 2
-    return [hop(value_x[:half], flip(1, 0)), hop(value_y[half:], flip(0, 1))]
+def inner_hop(pair):
+    return hop(pair, [(c, relative_chip(c, 0, 0, 3)) for c in range(CHIPS) if is_inner(coords(c)[0])])
+
+
+def outer_hop(pair):
+    return hop(pair, [(c, relative_chip(c, 0, 0, 1)) for c in range(CHIPS) if is_inner(coords(c)[0])])
+
+
+def is_inner(z):
+    return ((z + 1) // 2) % 2 == 1
 
 
 def heads_in_plane(w_proj, y, x):
@@ -213,10 +210,11 @@
     return pick.astype(BF16)
 
 
-def attend_kernel(gate_query, kv_own, kv_other, marks, gated):
+def attend_kernel(where, gate_query, kv_own, kv_other, marks, gated):
     pick = pick_columns({0: 128.0, 1: 1.0}, {2: 128.0, 3: 1.0})
     piece = gated.shape[2]
     tile = NZ * piece
+    flipped = ((where[0] + 1) // 2) % 2
     key_pos = lax.dot_general(pick, marks[...], ACROSS, preferred_element_type=F32)
     for k in range(len(PLANE)):
         span = pl.ds(k * tile, tile)
@@ -233,24 +231,28 @@
         normed = attn * lax.rsqrt(jnp.mean(attn * attn, axis=-1, keepdims=True) + 1e-06)
         out = (normed * gate_query[span, :W].astype(F32)).astype(BF16)
         for s in range(NZ):
-            gated[s, k] = out[s * piece : (s + 1) * piece]
+            part = out[s * piece : (s + 1) * piece]
+            if s < 2:
+                gated[s, k] = part
+            else:
+                gated[pl.ds(2 + ((s % 2) ^ flipped), 1), k] = part[None]
 
 
 def hidden_kernel(where, *refs):
     n = len(PLANE)
-    gated, w_own, w_other, tok = refs[: n + 1], refs[n + 1 : n + 3], refs[n + 3 : n + 5], refs[n + 5 : -5]
+    gated, late_own, late_other, tok = refs[:n], refs[n : n + 2], refs[n + 2 : n + 4], refs[n + 4 : -5]
     hidden, g_all, t_all, w_all, sems = refs[-5:]
     z, y, x, u = (where[i] for i in range(4))
     c = chip_at(z, y, x)
     rows = hidden.shape[1]
     half = w_all.shape[1]
-    inner = ((z + 1) // 2) % 2
+    flipped = ((z + 1) // 2) % 2
     copies = []
     for s in range(NZ):
         cols = pl.ds(s * W, W)
-        for side, src in enumerate((w_own, w_other)):
-            panel = src[0].at[s] if s < 2 else src[1].at[(s % 2) ^ inner]
-            copies.append((panel, w_all.at[side, :, cols]))
+        for side, src in enumerate((late_own, late_other)):
+            panel = src[0].at[s] if s < 2 else src[1].at[(s % 2) ^ flipped]
+            copies.append((panel.at[pl.ds(0, half), :], w_all.at[side, :, cols]))
         block = relative_chip(c, 0, 0, s)
         from_cols = pl.ds(pl.multiple_of(block * W, W), W)
         for k in range(n):
@@ -264,8 +266,7 @@
             cols = pl.ds(pl.multiple_of(head * W, W), W)
             for j, (jy, jx) in enumerate(PLANE):
                 block = (jy ^ by) * NX + (jx ^ bx)
-                piece = gated[k][s, j] if k < n - 1 else gated[k + s // 2][s % 2, j]
-                g_all[block * rows : (block + 1) * rows, cols] = piece
+                g_all[block * rows : (block + 1) * rows, cols] = gated[k][s, j]
     for copy in copies:
         copy.wait()
     total = 0.0
@@ -279,58 +280,89 @@
             hidden[k, :, cols] = (t_all[k, :, s * W : (s + 1) * W].astype(F32) + term).astype(BF16)
 
 
-def order_kernel(where, *refs):
-    pieces, (keep, send, h_all) = refs[: len(PLANE)], refs[len(PLANE) :]
-    y, x, u = (where[i] for i in range(1, 4))
-    half = keep.shape[1]
-    for (by, bx), ref in zip(PLANE, pieces):
-        for at in range(NZ):
-            block = chip_at(at, y ^ by, x ^ bx)
-            h_all[:, pl.ds(pl.multiple_of(block * W, W), W)] = ref[:, at * W : (at + 1) * W]
-    keep[...] = h_all[:, pl.ds(pl.multiple_of(u * half, half), half)]
-    send[...] = h_all[:, pl.ds(pl.multiple_of((1 - u) * half, half), half)]
-
-
-def loss_kernel(h_keep, h_send, t_keep, t_send, t_ids, n_own, n_other, loss, n_all, sems):
-    keep, send = h_keep[...], h_send[...]
-    half = keep.shape[1]
-    copies = []
-    for side, src in enumerate((n_own, n_other)):
-        copies.append(pltpu.make_async_copy(src, n_all.at[side], sems.at[side]))
-    for copy in copies:
-        copy.start()
-    hh = he = ee = 0.0
-    for part, ref in ((keep, t_keep), (send, t_send)):
-        h_f, t_f = part.astype(F32), ref[...].astype(F32)
-        hh += jnp.sum(h_f * h_f, axis=1, keepdims=True)
-        he += jnp.sum(h_f * t_f, axis=1, keepdims=True)
-        ee += jnp.sum(t_f * t_f, axis=1, keepdims=True)
-    h_scale = lax.rsqrt(hh + 1e-06) * 20.0
-    pos_logit = he * lax.rsqrt(ee + 1e-06) * h_scale
-    for copy in copies:
-        copy.wait()
-    pick = pick_columns({0: 1.0, 1: 1.0, 2: 1.0}, {3: 256.0, 4: 1.0})
-    dots, read = 0.0, []
-    for side, part in enumerate((keep, send)):
-        neg, marks = n_all[side, :, :half], n_all[side, :, half:]
-        dots += lax.dot_general(part, neg, ACROSS, preferred_element_type=F32)
-        read.append(lax.dot_general(pick, marks, ACROSS, preferred_element_type=F32))
-    nn = read[0][0:1] + read[1][0:1]
-    n_ids = read[0][1:2]
-    neg_logit = dots * h_scale * lax.rsqrt(nn + 1e-06)
-    mass = jnp.where(n_ids != t_ids[...].astype(F32), jnp.exp(neg_logit), 0.0)
-    total = jnp.exp(pos_logit) + jnp.sum(mass, axis=1, keepdims=True)
-    column = jnp.log(total) - pos_logit
+def as_line(column):
     size = column.shape[0]
     line = lax.broadcasted_iota(jnp.int32, (size, size), 0)
     lane = lax.broadcasted_iota(jnp.int32, (size, size), 1)
-    loss[...] = jnp.sum(jnp.where(line == lane, column, 0.0), axis=0, keepdims=True)
-
-
-def join_kernel(where, keep, theirs, hidden):
+    return jnp.sum(jnp.where(line == lane, column, 0.0), axis=0, keepdims=True)
+
+
+def mass_kernel(where, *refs):
+    n = len(PLANE)
+    pieces, late_own, late_other = refs[:n], refs[n : n + 2], refs[n + 2 : n + 4]
+    t_keep, t_send, marks = refs[n + 4 : n + 7]
+    keep, send, positive, mass, h_all, raw, n_all, sems = refs[n + 7 :]
+    y, x, u = (where[i] for i in range(1, 4))
+    rows, half = keep.shape
+    negs, panels = n_all.shape[2], half // W
+    split = raw.shape[2]
+    copies = []
+    for side, src in enumerate((late_own, late_other)):
+        for pair in range(2):
+            rest = src[pair].at[:, pl.ds(src[pair].shape[1] - split, split), :]
+            to = raw.at[side, pl.ds(2 * pair, 2)]
+            copies.append(pltpu.make_async_copy(rest, to, sems.at[2 * side + pair]))
+    for copy in copies:
+        copy.start()
+    for k, (by, bx) in enumerate(PLANE):
+        for at in range(NZ):
+            block = chip_at(at, y ^ by, x ^ bx)
+            cols = pl.ds(pl.multiple_of(block * W, W), W)
+            for j, (jy, jx) in enumerate(PLANE):
+                row = ((jy ^ by) * NX + (jx ^ bx)) * rows
+                h_all[row : row + rows, cols] = pieces[k][j, :, at * W : (at + 1) * W]
+    mine = pl.ds(pl.multiple_of(u * half, half), half)
+    theirs = pl.ds(pl.multiple_of((1 - u) * half, half), half)
+    keep[...] = h_all[:rows, mine]
+    send[...] = h_all[:rows, theirs]
+    hh = 0.0
+    for part in (mine, theirs):
+        h_f = h_all[:, part].astype(F32)
+        hh += jnp.sum(h_f * h_f, axis=1, keepdims=True)
+    h_scale = lax.rsqrt(hh + 1e-06) * 20.0
+    he = ee = 0.0
+    for h_ref, ref in ((keep, t_keep), (send, t_send)):
+        h_f, t_f = h_ref[...].astype(F32), ref[...].astype(F32)
+        he += jnp.sum(h_f * t_f, axis=1, keepdims=True)
+        ee += jnp.sum(t_f * t_f, axis=1, keepdims=True)
+    positive[...] = as_line(he * lax.rsqrt(ee + 1e-06) * h_scale[:rows])
+    first = [marks[k * NZ * rows : (k * NZ + 1) * rows] for k in range(n)]
+    pick = pick_columns({4: 256.0, 5: 1.0})
+    t_ids = lax.dot_general(
+        jnp.concatenate(first), pick, ACROSS, preferred_element_type=F32
+    )[:, :1]
+    for copy in copies:
+        copy.wait()
+    total = 0.0
+    for s in range(NZ):
+        nn, dots = 0.0, 0.0
+        for side, part in enumerate((mine, theirs)):
+            for panel in range(panels):
+                n_all[side, s, :, panel * W : (panel + 1) * W] = raw[
+                    side, s, panel * negs : (panel + 1) * negs
+                ]
+            dots += lax.dot_general(
+                h_all[:, part], n_all[side, s], ACROSS, preferred_element_type=F32
+            )
+            lines = raw[side, s, panels * negs :].astype(F32)
+            nn += lines[0:1, :negs] + lines[1:2, :negs] + lines[2:3, :negs]
+        n_ids = 256.0 * lines[3:4, :negs] + lines[4:5, :negs]
+        neg_logit = dots * h_scale * lax.rsqrt(nn + 1e-06)
+        kept = jnp.where(n_ids != t_ids, jnp.exp(neg_logit), 0.0)
+        total += jnp.sum(kept, axis=1, keepdims=True)
+    for k in range(n):
+        mass[k] = as_line(total[k * rows : (k + 1) * rows])
+
+
+def final_kernel(where, keep, theirs, positive, *refs):
+    masses, (hidden, loss) = refs[:-2], refs[-2:]
     u, rows = where[3], keep.shape[0]
     hidden[pl.ds(pl.multiple_of(u * rows, rows), rows), :] = keep[...]
     hidden[pl.ds(pl.multiple_of((1 - u) * rows, rows), rows), :] = theirs[...]
+    total = jnp.exp(positive[...])
+    for mass in masses:
+        total += mass[...]
+    loss[...] = jnp.log(total) - positive[...]
 
 
 def call(kernel, name, outs, scratch, args, places, flops):
@@ -382,31 +414,34 @@
     mine = lax.dynamic_slice_in_dim(tokens, u * rows, rows, 0)
     p_own = lax.dynamic_slice_in_dim(positions, u * rows, rows, 0)
     p_other = lax.dynamic_slice_in_dim(positions, (1 - u) * rows, rows, 0)
-    mine = with_marks(mine, whole_parts(p_own, 128) + whole_parts(p_other, 128))
+    ids = whole_parts(target_ids, 256)
+    mine = with_marks(mine, whole_parts(p_own, 128) + whole_parts(p_other, 128) + ids)
     low = pair_up(mine)
 
-    to_x, to_y = flip(0, 1), flip(1, 0)
-    high = hop(low, flip(0, 0, 2))
-    w_plane, came = heads_in_plane(w_proj, y, x)
-    low = after(low, came[:2])
-    low_x, low_y = hop(low, to_x), hop(low, to_y)
-    low_xy = across(low_x, low_y)
-    w_plane = after(w_plane, high)
-    high_x, high_y = hop(high, to_x), hop(high, to_y)
-    high_xy = across(high_x, high_y)
-    tok = [low, high, low_x, high_x, low_y, high_y, *low_xy, *high_xy]
-    w_mine = after(heads_along_z(w_plane, z), low_xy, high_xy)
-    w_theirs = swap_cores(w_mine)
-
-    t_rows = after(target_emb.reshape(2, rows, -1), high)
-    t_keep = pick_row(t_rows, u)
-    t_send = swap_cores(pick_row(t_rows, 1 - u))
     own_ids = lax.dynamic_slice_in_dim(neg_ids, c * negs, negs, 0)
     norms = jnp.sum(jnp.square(neg_emb.astype(F32)), axis=1)
-    neg = with_marks(neg_emb, float_parts(norms) + whole_parts(own_ids, 256))
-    neg_pair = pair_up(after(neg, w_mine, t_send))
-    neg_met, neg_far = relay_pairs(after(neg_pair, w_theirs), z)
-    out_pair = pair_up(after(w_out[None], neg_pair))
+    lines = jnp.stack(float_parts(norms) + whole_parts(own_ids, 256))
+    lines = jnp.pad(lines, ((0, 16 - lines.shape[0]), (0, W - negs)))
+    panels = neg_emb.reshape(negs, half // W, W).transpose(1, 0, 2).reshape(-1, W)
+    late = jnp.concatenate([w_out, panels, lines])[None]
+
+    to_x, to_y = flip(0, 1), flip(1, 0)
+    high_met = inner_hop(low)
+    w_plane, came = heads_in_plane(w_proj, y, x)
+    low_x, low_y = hop(after(low, came), to_x), hop(after(low, came), to_y)
+    late_pair = pair_up(after(late, low))
+    late_met = inner_hop(after(late_pair, high_met))
+    high = jnp.where(is_inner(z), high_met, outer_hop(high_met))
+    high_x, high_y = hop(high, to_x), hop(high, to_y)
+    low_xy, high_xy = hop(low_x, to_y), hop(high_y, to_x)
+    tok = [low, high, low_x, high_x, low_y, high_y, low_xy, high_xy]
+    w_mine = heads_along_z(after(w_plane, high, late_met), z)
+    late_out = outer_hop(after(late_met, w_mine))
+    w_mine = after(w_mine, high_x, low_y, low_xy, high_xy)
+    w_theirs = swap_cores(w_mine)
+    t_rows = target_emb.reshape(2, rows, -1)
+    t_keep = pick_row(t_rows, u)
+    t_send = swap_cores(pick_row(after(t_rows, w_theirs), 1 - u))
 
     def project(pieces):
         count = sum(p.shape[0] for p in pieces)
@@ -427,26 +462,20 @@
 
     gate_query, value_key, marks = project(tok)
     kv_theirs = swap_cores(value_key)
-    out_met, out_far = relay_pairs(after(out_pair, neg_met, value_key), z)
-    neg_near = jnp.concatenate([neg_pair, neg_far(after(neg_met, value_key))])
-    neg_row = jnp.concatenate([neg_near, hop(neg_near, to_x)])
-    neg_own = [neg_row, hop(neg_row, to_y)]
     (gated,) = call(
         attend_kernel,
         "attend",
         [((NZ, plane, rows, W), BF16)],
         [],
-        [gate_query, value_key, kv_theirs, marks],
-        4 * "v",
+        [where, gate_query, value_key, kv_theirs, marks],
+        "svvvv",
         8 * events * events * W,
     )
-    gated = after(gated, neg_near)
+    late_out = after(late_out, gated, t_send)
     gated = jnp.stack([gated[0]] + [hop(gated[s], flip(0, 0, s)) for s in range(1, NZ)])
-    out_met = after(out_met, gated)
-    gated = [gated, hop(gated, to_x), hop(gated, to_y)]
-    gated += across(gated[1], gated[2])
-    out_own = [after(out_pair, gated), after(out_far(out_met), gated)]
-    out_other = [swap_cores(w) for w in out_own]
+    late_own = [late_pair, jnp.where(is_inner(z), late_met, late_out)]
+    late_other = [swap_cores(piece) for piece in after(late_own, gated)]
+    gated = [gated] + [hop(gated, flip(by, bx)) for by, bx in PLANE[1:]]
     (hidden,) = call(
         hidden_kernel,
         "hidden",
@@ -457,42 +486,34 @@
             pltpu.VMEM((2, half, NZ * W), BF16),
             pltpu.SemaphoreType.DMA((NZ * (2 + plane),)),
         ],
-        [where, *gated, *out_own, *out_other, *tok[:7:2]],
-        "s" + 5 * "v" + 8 * "h",
+        [where, *gated, *late_own, *late_other, *tok[::2]],
+        "s" + 4 * "v" + 8 * "h",
         2 * plane * rows * model * NZ * W,
     )
-    pieces = [hidden[0]] + [hop(hidden[k], flip(*PLANE[k])) for k in range(1, plane)]
-    neg_own = jnp.concatenate(after(neg_own, hidden))
-    neg_other = swap_cores(neg_own)
-    h_keep, h_send = call(
-        order_kernel,
-        "order",
-        [((rows, half), BF16)] * 2,
-        [pltpu.VMEM((rows, model), BF16)],
-        [where, *pieces],
-        "svvvv",
-        0,
-    )
+    pieces = [hidden] + [hop(hidden, flip(by, bx)) for by, bx in PLANE[1:]]
+    h_keep, h_send, positive, mass = call(
+        mass_kernel,
+        "mass",
+        [((rows, half), BF16)] * 2 + [((1, rows), F32), ((plane, 1, rows), F32)],
+        [
+            pltpu.VMEM((plane * rows, model), BF16),
+            pltpu.VMEM((2, NZ, late.shape[1] - half, W), BF16),
+            pltpu.VMEM((2, NZ, negs, half), BF16),
+            pltpu.SemaphoreType.DMA((4,)),
+        ],
+        [where, *pieces, *late_own, *late_other, t_keep, t_send, marks],
+        "s" + 4 * "v" + 4 * "h" + "vvv",
+        2 * plane * rows * model * NZ * negs,
+    )
+    masses = [mass[0]] + [hop(mass[k], flip(*PLANE[k])) for k in range(1, plane)]
     h_theirs = swap_cores(h_send)
-    (loss,) = call(
-        loss_kernel,
-        "loss",
-        [((1, rows), F32)],
-        [
-            pltpu.VMEM((2, CHIPS * negs, half + W), BF16),
-            pltpu.SemaphoreType.DMA((2,)),
-        ],
-        [h_keep, h_send, t_keep, t_send, target_ids[:, None], neg_own, neg_other],
-        "vvvvvhh",
-        2 * rows * model * neg_ids.shape[0],
-    )
-    (hidden,) = call(
-        join_kernel,
-        "join",
-        [((2 * rows, half), BF16)],
+    hidden, loss = call(
+        final_kernel,
+        "final",
+        [((2 * rows, half), BF16), ((1, rows), F32)],
         [],
-        [where, h_keep, after(h_theirs, loss)],
-        "svv",
+        [where, h_keep, h_theirs, positive, *masses],
+        "s" + 7 * "v",
         0,
     )
     return hidden, loss.reshape(-1)

time: 178 us -> 182 us (1.022)
  waiting for transfers between devices: 86.6 us -> 73.3 us
  starting transfers between devices: 50.1 us -> 58.4 us
  local copies, waits for them, and re-layouts: 14.1 us -> 20.7 us
    ppermute x31 -> x27, waiting for transfers between devices: 83.7 us -> 70.7 us  [hop(): return lax.ppermute(value, 'ctx', perm)]
    ppermute x2, starting transfers between devices: 5.57 us -> 17.5 us  [heads_along_z(): lax.ppermute(pick_row(heads, e ^ z & 1), ('ctx', 'tp'), perm)]
    unnamed x48 -> x42, local copies, waits for them, and re-layouts: 7.09 us -> 11.1 us
    ppermute x7 -> x6, starting transfers between devices: 5.18 us -> 1.22 us  [swap_cores(): return lax.ppermute(value, 'tp', SWAP)]
    dynamic_update_slice x4, local copies, waits for them, and re-layouts: 0.09 us -> 2.94 us  [heads_in_plane(): out = lax.dynamic_update_slice_in_dim(out, piece[:, None], spot, 1)]
    pallas_call x6 -> x5, Pallas kernels: 16.9 us -> 18.7 us  [call(): pl.pallas_call(kernel, out_shape=[jax.ShapeDtypeStruct(shape, dtype) for...]
    ppermute x31 -> x27, starting transfers between devices: 39.3 us -> 39.6 us  [hop(): return lax.ppermute(value, 'ctx', perm)]
  transfers between devices with their start and end apart: 40 -> 35, of which waited for: 21 -> 15; matrix products, arithmetic and copies ran while one was open for 9% -> 9% of each run, Pallas kernels for 9% -> 2%
where the time goes in v8:
time: 182 us; the launch traced here: 180 us
  waiting for transfers between devices  73.3 us (40%)
  starting transfers between devices  58.4 us (32%)
  local copies, waits for them, and re-layouts  20.7 us (11%)
  Pallas kernels  18.7 us (10%)
  other arithmetic  8.18 us (4%)
    ppermute x27, waiting for transfers between devices, hop(): return lax.ppermute(value, 'ctx', perm)  70.7 us
    ppermute x27, starting transfers between devices, hop(): return lax.ppermute(value, 'ctx', perm)  39.6 us
    pallas_call x5, Pallas kernels, call(): pl.pallas_call(kernel, out_shape=[jax.ShapeDtypeStruct(shape, dtype) for...  18.7 us
    ppermute x2, starting transfers between devices, heads_along_z(): lax.ppermute(pick_row(heads, e ^ z & 1), ('ctx', 'tp'), perm)  17.5 us
    unnamed x42, local copies, waits for them, and re-layouts  11.1 us
  transfers between devices with their start and end apart: 35, of which 15 were waited for; matrix products, arithmetic and copies ran while one was open for 9% of the time, Pallas kernels for 2%

profile of v8, /device:TPU:0, one launch (start us, length us, event | category | flops | bytes accessed | tf_op | source)
XLA Modules:
  0.0 180.4 jit_solution(8871252208250894121)
XLA Ops:
  4.0 3.1 %collective-permute-start = (bf16[64,2176]{1,0:T(8,128)(2,1)S(1)}, bf16[64,2176]{1,0:T(8,128)(2,1)}, u32[]{:S(2)}, u32[]{:S(2)}) collective-permute-start(bf16[64,2176]{1,0:T(8,128)(2,1)S(1)} %pad_maximum_fusion.1), channel_id=1, source_target_pairs={{0,8},{2,10},{4,12},{6,14},{8,0},{10,2},{12,4},{14,6},{16,24},{18,... | collective-permute-start | bytes 835592 | tf_op jit(solution)/shard_map/ppermute | solution.py:106
  19.9 3.7 %collective-permute-start.12 = (bf16[1,1552,128]{2,1,0:T(8,128)(2,1)S(1)}, bf16[1,1552,128]{2,1,0:T(8,128)(2,1)S(1)}, u32[]{:S(2)}, u32[]{:S(2)}) collective-permute-start(bf16[1,1552,128]{2,1,0:T(8,128)(2,1)S(1)} %fusion.2), channel_id=1, source_target_pairs={{0,8},{2,10},{4,12},{6,14},{8,0},{10,2},{12,4},{14,6},{16,24},{18,... | collective-permute-start | bytes 1191944 | tf_op jit(solution)/shard_map/ppermute | solution.py:106
  28.2 3.1 %collective-permute-done.12 = bf16[1,1552,128]{2,1,0:T(8,128)(2,1)S(1)} collective-permute-done((bf16[1,1552,128]{2,1,0:T(8,128)(2,1)S(1)}, bf16[1,1552,128]{2,1,0:T(8,128)(2,1)S(1)}, u32[]{:S(2)}, u32[]{:S(2)}) %collective-permute-start.12) | collective-permute-done | bytes 397344 | tf_op jit(solution)/shard_map/ppermute | solution.py:106
  35.5 10.8 %collective-permute-done.2 = bf16[128,2176]{1,0:T(8,128)(2,1)S(1)} collective-permute-done((bf16[128,2176]{1,0:T(8,128)(2,1)}, bf16[128,2176]{1,0:T(8,128)(2,1)S(1)}, u32[]{:S(2)}, u32[]{:S(2)}) %collective-permute-start.2) | collective-permute-done | bytes 557088 | tf_op jit(solution)/shard_map/ppermute | solution.py:106
  46.4 1.6 collective-permute-start.9
  48.9 12.2 %collective-permute-start.15 = (bf16[4,128,512]{2,1,0:T(8,128)(2,1)S(1)}, bf16[4,128,512]{2,1,0:T(8,128)(2,1)}, u32[]{:S(2)}, u32[]{:S(2)}) collective-permute-start(bf16[4,128,512]{2,1,0:T(8,128)(2,1)S(1)} %get-tuple-element.47), channel_id=1, source_target_pairs={{0,8},{1,24},{2,10},{3,26},{4,12},{5,28},{6,14},{7,30},{8,0},{9,16... | collective-permute-start | bytes 1572872 | tf_op jit(solution)/shard_map/ppermute | solution.py:162
  61.1 5.3 %collective-permute-start.14 = (bf16[4,128,512]{2,1,0:T(8,128)(2,1)}, bf16[4,128,512]{2,1,0:T(8,128)(2,1)}, u32[]{:S(2)}, u32[]{:S(2)}) collective-permute-start(bf16[4,128,512]{2,1,0:T(8,128)(2,1)} %get-tuple-element.46), channel_id=1, source_target_pairs={{0,0},{1,16},{2,2},{3,18},{4,4},{5,20},{6,6},{7,22},{8,8},{9,24},{... | collective-permute-start | bytes 1572872 | tf_op jit(solution)/shard_map/ppermute | solution.py:162
  66.4 2.2 %collective-permute-start.8 = (bf16[128,2176]{1,0:T(8,128)(2,1)S(1)}, bf16[128,2176]{1,0:T(8,128)(2,1)}, u32[]{:S(2)}, u32[]{:S(2)}) collective-permute-start(bf16[128,2176]{1,0:T(8,128)(2,1)S(1)} %pad_maximum_fusion.refs_0_.refs_8_), channel_id=1, source_target_pairs={{0,4},{2,6},{4,0},{6,2},{8,12},{10,14},{12,8},{14,10},{16,20},{18,... | collective-permute-start | bytes 1671176 | tf_op jit(solution)/shard_map/ppermute | solution.py:106
  71.7 1.7 maximum_select_fusion
  73.4 8.8 %collective-permute-done.8.refs_4_.refs_10_ = bf16[128,2176]{1,0:T(8,128)(2,1)} collective-permute-done((bf16[128,2176]{1,0:T(8,128)(2,1)S(1)}, bf16[128,2176]{1,0:T(8,128)(2,1)}, u32[]{:S(2)}, u32[]{:S(2)}) %collective-permute-start.8) | collective-permute-done | bytes 557088 | tf_op jit(solution)/shard_map/ppermute | solution.py:106
  82.3 9.0 %collective-permute-done.10.refs_6_.refs_11_ = bf16[128,2176]{1,0:T(8,128)(2,1)} collective-permute-done((bf16[128,2176]{1,0:T(8,128)(2,1)S(1)}, bf16[128,2176]{1,0:T(8,128)(2,1)}, u32[]{:S(2)}, u32[]{:S(2)}) %collective-permute-start.10) | collective-permute-done | bytes 557088 | tf_op jit(solution)/shard_map/ppermute | solution.py:106
  92.9 2.6 %collective-permute-done.16.refs_9_ = bf16[1024,512]{1,0:T(8,128)(2,1)S(1)} collective-permute-done((bf16[1024,512]{1,0:T(8,128)(2,1)S(1)}, bf16[1024,512]{1,0:T(8,128)(2,1)S(1)}, u32[]{:S(2)}, u32[]{:S(2)}) %collective-permute-start.16) | collective-permute-done | bytes 1048608 | tf_op jit(solution)/shard_map/ppermute | solution.py:110
  96.4 6.3 %project.1 = (bf16[1024,256]{1,0:T(8,128)(2,1)S(1)}, bf16[1024,256]{1,0:T(8,128)(2,1)}, bf16[1024,128]{1,0:T(8,128)(2,1)S(1)}) custom-call(s32[4]{0:T(128)S(1)} %pad_add_fusion.where, bf16[128,2176]{1,0:T(8,128)(2,1)S(1)} %pad_maximum_fusion.refs_0_.refs_8_, bf16[128,2176]{1,0:T(8,128)(2,1)S(1)} %broadcast_select_fusion.1.refs_1_, ...), custom_call_target="tpu_custom_call" | custom-call | flops 2147483648 | bytes 6553616 | tf_op jit(solution)/shard_map/project/pallas_call | solution.py:371
  109.3 4.3 %attend.1 = bf16[4,4,64,128]{3,2,1,0:T(8,128)(2,1)S(1)} custom-call(s32[4]{0:T(128)S(1)} %pad_add_fusion.where, bf16[1024,256]{1,0:T(8,128)(2,1)S(1)} %copy-done.11, bf16[1024,256]{1,0:T(8,128)(2,1)} %get-tuple-element.27.kv_own, bf16[1024,256]{1,0:T(8,128)(2,1)S(1)} %collective-permute-done.17.kv_other, bf16[1024,128]{1,0:T(8,128)(2,1)S(1)} %copy-done.6), custom_call_target="tpu_custom_call" | custom-call | flops 1073741824 | bytes 1835024 | tf_op jit(solution)/shard_map/attend/pallas_call | solution.py:371
  113.7 4.5 %collective-permute-start.19 = (bf16[4,64,128]{2,1,0:T(8,128)(2,1)S(1)}, bf16[4,64,128]{2,1,0:T(8,128)(2,1)S(1)}, u32[]{:S(2)}, u32[]{:S(2)}) collective-permute-start(bf16[4,64,128]{2,1,0:T(8,128)(2,1)S(1)} %get-tuple-element.54), channel_id=1, source_target_pairs={{0,16},{2,18},{4,20},{6,22},{8,24},{10,26},{12,28},{14,30},{16,0},... | collective-permute-start | bytes 196616 | tf_op jit(solution)/shard_map/ppermute | solution.py:106
  118.2 11.8 %collective-permute-done.24 = bf16[2,1552,128]{2,1,0:T(8,128)(2,1)} collective-permute-done((bf16[2,1552,128]{2,1,0:T(8,128)(2,1)}, bf16[2,1552,128]{2,1,0:T(8,128)(2,1)}, u32[]{:S(2)}, u32[]{:S(2)}) %collective-permute-start.24) | collective-permute-done | bytes 794656 | tf_op jit(solution)/shard_map/ppermute | solution.py:106
  136.0 5.7 %collective-permute-done.21.refs_1_ = bf16[4,4,64,128]{3,2,1,0:T(8,128)(2,1)S(1)} collective-permute-done((bf16[4,4,64,128]{3,2,1,0:T(8,128)(2,1)S(1)}, bf16[4,4,64,128]{3,2,1,0:T(8,128)(2,1)S(1)}, u32[]{:S(2)}, u32[]{:S(2)}) %collective-permute-start.21) | collective-permute-done | bytes 262176 | tf_op jit(solution)/shard_map/ppermute | solution.py:106
  141.7 6.0 %collective-permute-done.22.refs_2_ = bf16[4,4,64,128]{3,2,1,0:T(8,128)(2,1)S(1)} collective-permute-done((bf16[4,4,64,128]{3,2,1,0:T(8,128)(2,1)S(1)}, bf16[4,4,64,128]{3,2,1,0:T(8,128)(2,1)S(1)}, u32[]{:S(2)}, u32[]{:S(2)}) %collective-permute-start.22) | collective-permute-done | bytes 262176 | tf_op jit(solution)/shard_map/ppermute | solution.py:106
  148.6 3.5 %hidden.1.refs_0_ = bf16[4,64,512]{2,1,0:T(8,128)(2,1)} custom-call(s32[4]{0:T(128)S(1)} %pad_add_fusion.where, bf16[4,4,64,128]{3,2,1,0:T(8,128)(2,1)S(1)} %pad_maximum_fusion.2.refs_0_, bf16[4,4,64,128]{3,2,1,0:T(8,128)(2,1)S(1)} %collective-permute-done.21.refs_1_, bf16[4,4,64,128]{3,2,1,0:T(8,128)(2,1)S(1)} %collective-permute-done.22.refs_2_, ...), custom_call_target="tpu_custom_call" | custom-call | flops 536870912 | bytes 6455312 | tf_op jit(solution)/shard_map/hidden/pallas_call | solution.py:371
  156.6 5.0 %collective-permute-done.28.refs_1_ = bf16[4,64,512]{2,1,0:T(8,128)(2,1)S(1)} collective-permute-done((bf16[4,64,512]{2,1,0:T(8,128)(2,1)}, bf16[4,64,512]{2,1,0:T(8,128)(2,1)S(1)}, u32[]{:S(2)}, u32[]{:S(2)}) %collective-permute-start.28) | collective-permute-done | bytes 262176 | tf_op jit(solution)/shard_map/ppermute | solution.py:106
  161.7 4.8 %collective-permute-done.29.refs_2_ = bf16[4,64,512]{2,1,0:T(8,128)(2,1)S(1)} collective-permute-done((bf16[4,64,512]{2,1,0:T(8,128)(2,1)}, bf16[4,64,512]{2,1,0:T(8,128)(2,1)S(1)}, u32[]{:S(2)}, u32[]{:S(2)}) %collective-permute-start.29) | collective-permute-done | bytes 262176 | tf_op jit(solution)/shard_map/ppermute | solution.py:106
  169.4 3.2 %mass.1 = (bf16[64,1024]{1,0:T(8,128)(2,1)S(1)}, bf16[64,1024]{1,0:T(8,128)(2,1)S(1)}, f32[1,64]{1,0:T(1,128)S(1)}, f32[4,1,64]{2,1,0:T(1,128)S(1)}) custom-call(s32[4]{0:T(128)S(1)} %pad_add_fusion.where, bf16[4,64,512]{2,1,0:T(8,128)(2,1)} %hidden.1.refs_0_, bf16[4,64,512]{2,1,0:T(8,128)(2,1)S(1)} %collective-permute-done.28.refs_1_, ...), custom_call_target="tpu_custom_call" | custom-call | flops 268435456 | bytes 4751376 | tf_op jit(solution)/shard_map/mass/pallas_call | solution.py:371
  174.7 1.6 collective-permute-start.34
  177.0 2.2 %collective-permute-done.34.refs_3_ = f32[1,64]{1,0:T(1,128)S(1)} collective-permute-done((f32[1,64]{1,0:T(1,128)S(1)}, f32[1,64]{1,0:T(1,128)S(1)}, u32[]{:S(2)}, u32[]{:S(2)}) %collective-permute-start.34) | collective-permute-done | bytes 288 | tf_op jit(solution)/shard_map/ppermute | solution.py:106
  (131 shorter events, 56.1 us)
Async XLA Ops:
  4.0 12.3 %collective-permute-start = (bf16[64,2176]{1,0:T(8,128)(2,1)S(1)}, bf16[64,2176]{1,0:T(8,128)(2,1)}, u32[]{:S(2)}, u32[]{:S(2)}) collective-permute-start(bf16[64,2176]{1,0:T(8,128)(2,1)S(1)} %pad_maximum_fusion.1), channel_id=1, source_target_pairs={{0,8},{2,10},{4,12},{6,14},{8,0},{10,2},{12,4},{14,6},{16,24},{18,... | collective-permute-start | bytes 835592 | tf_op jit(solution)/shard_map/ppermute | solution.py:106
  11.5 13.4 %collective-permute-start.4 = (bf16[2,128,512]{2,1,0:T(8,128)(2,1)}, bf16[2,128,512]{2,1,0:T(8,128)(2,1)}, u32[]{:S(2)}, u32[]{:S(2)}) collective-permute-start(bf16[2,128,512]{2,1,0:T(8,128)(2,1)} %bitcast.14), channel_id=1, source_target_pairs={{0,4},{2,6},{4,0},{6,2},{8,12},{10,14},{12,8},{14,10},{16,20},{18,... | collective-permute-start | bytes 786440 | tf_op jit(solution)/shard_map/ppermute | solution.py:106
  13.8 19.1 %collective-permute-start.5 = (bf16[2,128,512]{2,1,0:T(8,128)(2,1)}, bf16[2,128,512]{2,1,0:T(8,128)(2,1)}, u32[]{:S(2)}, u32[]{:S(2)}) collective-permute-start(bf16[2,128,512]{2,1,0:T(8,128)(2,1)} %bitcast.15), channel_id=1, source_target_pairs={{0,6},{2,4},{4,2},{6,0},{8,14},{10,12},{12,10},{14,8},{16,22},{18,... | collective-permute-start | bytes 786440 | tf_op jit(solution)/shard_map/ppermute | solution.py:106
  19.9 11.5 %collective-permute-start.12 = (bf16[1,1552,128]{2,1,0:T(8,128)(2,1)S(1)}, bf16[1,1552,128]{2,1,0:T(8,128)(2,1)S(1)}, u32[]{:S(2)}, u32[]{:S(2)}) collective-permute-start(bf16[1,1552,128]{2,1,0:T(8,128)(2,1)S(1)} %fusion.2), channel_id=1, source_target_pairs={{0,8},{2,10},{4,12},{6,14},{8,0},{10,2},{12,4},{14,6},{16,24},{18,... | collective-permute-start | bytes 1191944 | tf_op jit(solution)/shard_map/ppermute | solution.py:106
  26.9 19.4 %collective-permute-start.2 = (bf16[128,2176]{1,0:T(8,128)(2,1)}, bf16[128,2176]{1,0:T(8,128)(2,1)S(1)}, u32[]{:S(2)}, u32[]{:S(2)}) collective-permute-start(bf16[128,2176]{1,0:T(8,128)(2,1)} %collective-permute-done.1), channel_id=1, source_target_pairs={{8,0},{10,2},{12,4},{14,6},{16,24},{18,26},{20,28},{22,30},{9,1},{... | collective-permute-start | bytes 1671176 | tf_op jit(solution)/shard_map/ppermute | solution.py:106
  31.4 16.6 %collective-permute-start.13 = (bf16[2,1552,128]{2,1,0:T(8,128)(2,1)S(1)}, bf16[2,1552,128]{2,1,0:T(8,128)(2,1)}, u32[]{:S(2)}, u32[]{:S(2)}) collective-permute-start(bf16[2,1552,128]{2,1,0:T(8,128)(2,1)S(1)} %constant_dynamic-update-slice_fusion.refs_4_), channel_id=1, source_target_pairs={{8,16},{10,18},{12,20},{14,22},{16,8},{18,10},{20,12},{22,14},{9,1... | collective-permute-start | bytes 2383880 | tf_op jit(solution)/shard_map/ppermute | solution.py:106
  33.9 34.7 %collective-permute-start.6 = (bf16[128,2176]{1,0:T(8,128)(2,1)S(1)}, bf16[128,2176]{1,0:T(8,128)(2,1)S(1)}, u32[]{:S(2)}, u32[]{:S(2)}) collective-permute-start(bf16[128,2176]{1,0:T(8,128)(2,1)S(1)} %pad_maximum_fusion.refs_0_.refs_8_), channel_id=1, source_target_pairs={{0,2},{2,0},{4,6},{6,4},{8,10},{10,8},{12,14},{14,12},{16,18},{18,... | collective-permute-start | bytes 1671176 | tf_op jit(solution)/shard_map/ppermute | solution.py:106
  46.4 22.3 %collective-permute-start.9 = (bf16[128,2176]{1,0:T(8,128)(2,1)S(1)}, bf16[128,2176]{1,0:T(8,128)(2,1)}, u32[]{:S(2)}, u32[]{:S(2)}) collective-permute-start(bf16[128,2176]{1,0:T(8,128)(2,1)S(1)} %broadcast_select_fusion.1.refs_1_), channel_id=1, source_target_pairs={{0,4},{2,6},{4,0},{6,2},{8,12},{10,14},{12,8},{14,10},{16,20},{18,... | collective-permute-start | bytes 1671176 | tf_op jit(solution)/shard_map/ppermute | solution.py:106
  48.9 21.3 %collective-permute-start.15 = (bf16[4,128,512]{2,1,0:T(8,128)(2,1)S(1)}, bf16[4,128,512]{2,1,0:T(8,128)(2,1)}, u32[]{:S(2)}, u32[]{:S(2)}) collective-permute-start(bf16[4,128,512]{2,1,0:T(8,128)(2,1)S(1)} %get-tuple-element.47), channel_id=1, source_target_pairs={{0,8},{1,24},{2,10},{3,26},{4,12},{5,28},{6,14},{7,30},{8,0},{9,16... | collective-permute-start | bytes 1572872 | tf_op jit(solution)/shard_map/ppermute | solution.py:162
  66.4 15.9 %collective-permute-start.8 = (bf16[128,2176]{1,0:T(8,128)(2,1)S(1)}, bf16[128,2176]{1,0:T(8,128)(2,1)}, u32[]{:S(2)}, u32[]{:S(2)}) collective-permute-start(bf16[128,2176]{1,0:T(8,128)(2,1)S(1)} %pad_maximum_fusion.refs_0_.refs_8_), channel_id=1, source_target_pairs={{0,4},{2,6},{4,0},{6,2},{8,12},{10,14},{12,8},{14,10},{16,20},{18,... | collective-permute-start | bytes 1671176 | tf_op jit(solution)/shard_map/ppermute | solution.py:106
  68.6 22.7 %collective-permute-start.10 = (bf16[128,2176]{1,0:T(8,128)(2,1)S(1)}, bf16[128,2176]{1,0:T(8,128)(2,1)}, u32[]{:S(2)}, u32[]{:S(2)}) collective-permute-start(bf16[128,2176]{1,0:T(8,128)(2,1)S(1)} %collective-permute-done.6.refs_2_.refs_9_), channel_id=1, source_target_pairs={{0,4},{2,6},{4,0},{6,2},{8,12},{10,14},{12,8},{14,10},{16,20},{18,... | collective-permute-start | bytes 1671176 | tf_op jit(solution)/shard_map/ppermute | solution.py:106
  68.7 22.6 %collective-permute-start.7 = (bf16[128,2176]{1,0:T(8,128)(2,1)S(1)}, bf16[128,2176]{1,0:T(8,128)(2,1)}, u32[]{:S(2)}, u32[]{:S(2)}) collective-permute-start(bf16[128,2176]{1,0:T(8,128)(2,1)S(1)} %broadcast_select_fusion.1.refs_1_), channel_id=1, source_target_pairs={{0,2},{2,0},{4,6},{6,4},{8,10},{10,8},{12,14},{14,12},{16,18},{18,... | collective-permute-start | bytes 1671176 | tf_op jit(solution)/shard_map/ppermute | solution.py:106
  70.2 22.6 %collective-permute-start.11 = (bf16[128,2176]{1,0:T(8,128)(2,1)}, bf16[128,2176]{1,0:T(8,128)(2,1)}, u32[]{:S(2)}, u32[]{:S(2)}) collective-permute-start(bf16[128,2176]{1,0:T(8,128)(2,1)} %collective-permute-done.9.refs_5_), channel_id=1, source_target_pairs={{0,2},{2,0},{4,6},{6,4},{8,10},{10,8},{12,14},{14,12},{16,18},{18,... | collective-permute-start | bytes 1671176 | tf_op jit(solution)/shard_map/ppermute | solution.py:106
  104.5 25.6 %collective-permute-start.24 = (bf16[2,1552,128]{2,1,0:T(8,128)(2,1)}, bf16[2,1552,128]{2,1,0:T(8,128)(2,1)}, u32[]{:S(2)}, u32[]{:S(2)}) collective-permute-start(bf16[2,1552,128]{2,1,0:T(8,128)(2,1)} %collective-permute-done.13), channel_id=1, source_target_pairs={{8,0},{10,2},{12,4},{14,6},{16,24},{18,26},{20,28},{22,30},{9,1},{... | collective-permute-start | bytes 2383880 | tf_op jit(solution)/shard_map/ppermute | solution.py:106
  106.9 23.2 %collective-permute-start.25 = (bf16[64,1024]{1,0:T(8,128)(2,1)S(1)}, bf16[64,1024]{1,0:T(8,128)(2,1)S(1)}, u32[]{:S(2)}, u32[]{:S(2)}) collective-permute-start(bf16[64,1024]{1,0:T(8,128)(2,1)S(1)} %dynamic-slice_bitcast_fusion.3), channel_id=1, source_target_pairs={{0,1},{1,0},{2,3},{3,2},{4,5},{5,4},{6,7},{7,6},{8,9},{9,8},{10,11... | collective-permute-start | bytes 393224 | tf_op jit(solution)/shard_map/ppermute | solution.py:110
  113.6 18.3 %collective-permute-start.20 = (bf16[4,64,128]{2,1,0:T(8,128)(2,1)S(1)}, bf16[4,64,128]{2,1,0:T(8,128)(2,1)S(1)}, u32[]{:S(2)}, u32[]{:S(2)}) collective-permute-start(bf16[4,64,128]{2,1,0:T(8,128)(2,1)S(1)} %get-tuple-element.53), channel_id=1, source_target_pairs={{0,24},{2,26},{4,28},{6,30},{8,16},{10,18},{12,20},{14,22},{16,8},... | collective-permute-start | bytes 196616 | tf_op jit(solution)/shard_map/ppermute | solution.py:106
  113.7 18.2 %collective-permute-start.19 = (bf16[4,64,128]{2,1,0:T(8,128)(2,1)S(1)}, bf16[4,64,128]{2,1,0:T(8,128)(2,1)S(1)}, u32[]{:S(2)}, u32[]{:S(2)}) collective-permute-start(bf16[4,64,128]{2,1,0:T(8,128)(2,1)S(1)} %get-tuple-element.54), channel_id=1, source_target_pairs={{0,16},{2,18},{4,20},{6,22},{8,24},{10,26},{12,28},{14,30},{16,0},... | collective-permute-start | bytes 196616 | tf_op jit(solution)/shard_map/ppermute | solution.py:106
  118.2 13.7 %collective-permute-start.18 = (bf16[4,64,128]{2,1,0:T(8,128)(2,1)S(1)}, bf16[4,64,128]{2,1,0:T(8,128)(2,1)S(1)}, u32[]{:S(2)}, u32[]{:S(2)}) collective-permute-start(bf16[4,64,128]{2,1,0:T(8,128)(2,1)S(1)} %get-tuple-element.55), channel_id=1, source_target_pairs={{0,8},{2,10},{4,12},{6,14},{8,0},{10,2},{12,4},{14,6},{16,24},{18,... | collective-permute-start | bytes 196616 | tf_op jit(solution)/shard_map/ppermute | solution.py:106
  132.0 15.7 %collective-permute-start.26 = (bf16[2,1552,128]{2,1,0:T(8,128)(2,1)S(1)}, bf16[2,1552,128]{2,1,0:T(8,128)(2,1)S(1)}, u32[]{:S(2)}, u32[]{:S(2)}) collective-permute-start(bf16[2,1552,128]{2,1,0:T(8,128)(2,1)S(1)} %constant_dynamic-update-slice_fusion.refs_4_), channel_id=1, source_target_pairs={{0,1},{1,0},{2,3},{3,2},{4,5},{5,4},{6,7},{7,6},{8,9},{9,8},{10,11... | collective-permute-start | bytes 2383880 | tf_op jit(solution)/shard_map/ppermute | solution.py:110
  132.1 15.6 %collective-permute-start.27 = (bf16[2,1552,128]{2,1,0:T(8,128)(2,1)S(1)}, bf16[2,1552,128]{2,1,0:T(8,128)(2,1)S(1)}, u32[]{:S(2)}, u32[]{:S(2)}) collective-permute-start(bf16[2,1552,128]{2,1,0:T(8,128)(2,1)S(1)} %broadcast_select_fusion.refs_5_), channel_id=1, source_target_pairs={{0,1},{1,0},{2,3},{3,2},{4,5},{5,4},{6,7},{7,6},{8,9},{9,8},{10,11... | collective-permute-start | bytes 2383880 | tf_op jit(solution)/shard_map/ppermute | solution.py:110
  134.0 13.6 %collective-permute-start.22 = (bf16[4,4,64,128]{3,2,1,0:T(8,128)(2,1)S(1)}, bf16[4,4,64,128]{3,2,1,0:T(8,128)(2,1)S(1)}, u32[]{:S(2)}, u32[]{:S(2)}) collective-permute-start(bf16[4,4,64,128]{3,2,1,0:T(8,128)(2,1)S(1)} %pad_maximum_fusion.2.refs_0_), channel_id=1, source_target_pairs={{0,4},{2,6},{4,0},{6,2},{8,12},{10,14},{12,8},{14,10},{16,20},{18,... | collective-permute-start | bytes 786440 | tf_op jit(solution)/shard_map/ppermute | solution.py:106
  135.6 12.1 %collective-permute-start.23 = (bf16[4,4,64,128]{3,2,1,0:T(8,128)(2,1)S(1)}, bf16[4,4,64,128]{3,2,1,0:T(8,128)(2,1)S(1)}, u32[]{:S(2)}, u32[]{:S(2)}) collective-permute-start(bf16[4,4,64,128]{3,2,1,0:T(8,128)(2,1)S(1)} %pad_maximum_fusion.2.refs_0_), channel_id=1, source_target_pairs={{0,6},{2,4},{4,2},{6,0},{8,14},{10,12},{12,10},{14,8},{16,22},{18,... | collective-permute-start | bytes 786440 | tf_op jit(solution)/shard_map/ppermute | solution.py:106
  153.4 13.0 %collective-permute-start.29 = (bf16[4,64,512]{2,1,0:T(8,128)(2,1)}, bf16[4,64,512]{2,1,0:T(8,128)(2,1)S(1)}, u32[]{:S(2)}, u32[]{:S(2)}) collective-permute-start(bf16[4,64,512]{2,1,0:T(8,128)(2,1)} %hidden.1.refs_0_), channel_id=1, source_target_pairs={{0,4},{2,6},{4,0},{6,2},{8,12},{10,14},{12,8},{14,10},{16,20},{18,... | collective-permute-start | bytes 786440 | tf_op jit(solution)/shard_map/ppermute | solution.py:106
  154.3 12.2 %collective-permute-start.30 = (bf16[4,64,512]{2,1,0:T(8,128)(2,1)}, bf16[4,64,512]{2,1,0:T(8,128)(2,1)}, u32[]{:S(2)}, u32[]{:S(2)}) collective-permute-start(bf16[4,64,512]{2,1,0:T(8,128)(2,1)} %hidden.1.refs_0_), channel_id=1, source_target_pairs={{0,6},{2,4},{4,2},{6,0},{8,14},{10,12},{12,10},{14,8},{16,22},{18,... | collective-permute-start | bytes 786440 | tf_op jit(solution)/shard_map/ppermute | solution.py:106
  (31 other events, 186.4 us)

commit v9 on v7

--- a/solution.py
+++ b/solution.py
@@ -80,6 +80,7 @@
 NZ, NY, NX = 4, 2, 2
 CHIPS = NZ * NY * NX
 PLANE = [(by, bx) for by in range(NY) for bx in range(NX)]
+BITS = [(0, 0), (0, 1), (1, 0), (1, 1)]
 SWAP = [(0, 1), (1, 0)]
 W = HEAD_DIM
 ACROSS = (((1,), (1,)), ((), ()))
@@ -122,22 +123,12 @@
     return jnp.concatenate([own, hop(own, flip(0, 0, 1))])
 
 
-def relay_pairs(pair, z):
-    inner, outer = [], []
-    for c in range(CHIPS):
-        if coords(c)[0] in (1, 2):
-            inner.append((c, relative_chip(c, 0, 0, 3)))
-            outer.append((c, relative_chip(c, 0, 0, 1)))
-    met = hop(pair, inner)
-    return met, lambda met: jnp.where((z == 1) | (z == 2), met, hop(met, outer))
-
-
 def across(value_x, value_y):
     half = value_x.shape[0] // 2
     return [hop(value_x[:half], flip(1, 0)), hop(value_y[half:], flip(0, 1))]
 
 
-def heads_in_plane(w_proj, y, x):
+def heads_in_plane(w_proj, y, x, first):
     plane = NY * NX
     heads = w_proj.reshape(-1, 4, 2, plane, W).transpose(3, 2, 0, 1, 4)
     heads = heads.reshape(plane, 2, -1, 4 * W)
@@ -147,7 +138,7 @@
         spot = (y ^ by) * NX + (x ^ bx)
         piece = pick_row(heads, spot)
         if (by, bx) != (0, 0):
-            piece = hop(piece, flip(by, bx))
+            piece = hop(after(piece, first), flip(by, bx))
             came.append(piece)
         out = lax.dynamic_update_slice_in_dim(out, piece[:, None], spot, 1)
     return out, came
@@ -213,17 +204,24 @@
     return pick.astype(BF16)
 
 
-def attend_kernel(gate_query, kv_own, kv_other, marks, gated):
+def attend_kernel(gq_hbm, own_hbm, other_hbm, marks_hbm, gated, gate_query, own, other, marks, sems):
+    sources = (gq_hbm, own_hbm, other_hbm, marks_hbm)
+    run_copies(
+        [
+            pltpu.make_async_copy(src, dst, sems.at[i])
+            for i, (src, dst) in enumerate(zip(sources, (gate_query, own, other, marks)))
+        ]
+    )
     pick = pick_columns({0: 128.0, 1: 1.0}, {2: 128.0, 3: 1.0})
-    piece = gated.shape[2]
+    piece = gated.shape[3]
     tile = NZ * piece
     key_pos = lax.dot_general(pick, marks[...], ACROSS, preferred_element_type=F32)
-    for k in range(len(PLANE)):
+    for k, (by, bx) in enumerate(PLANE):
         span = pl.ds(k * tile, tile)
         query = gate_query[span, W:]
         q_pos = lax.dot_general(marks[span, :], pick, ACROSS, preferred_element_type=F32)[:, :1]
         attn = jnp.zeros((tile, W), F32)
-        for side, kv in enumerate((kv_own, kv_other)):
+        for side, kv in enumerate((own, other)):
             scores = lax.dot_general(
                 query, kv[:, W:], ACROSS, preferred_element_type=F32
             ) * W ** (-0.5)
@@ -233,60 +231,56 @@
         normed = attn * lax.rsqrt(jnp.mean(attn * attn, axis=-1, keepdims=True) + 1e-06)
         out = (normed * gate_query[span, :W].astype(F32)).astype(BF16)
         for s in range(NZ):
-            gated[s, k] = out[s * piece : (s + 1) * piece]
+            gated[s % 2, bx, 2 * (s // 2) + by] = out[s * piece : (s + 1) * piece]
 
 
 def hidden_kernel(where, *refs):
-    n = len(PLANE)
-    gated, w_own, w_other, tok = refs[: n + 1], refs[n + 1 : n + 3], refs[n + 3 : n + 5], refs[n + 5 : -5]
-    hidden, g_all, t_all, w_all, sems = refs[-5:]
+    gated, w_own, w_other, tok = refs[:4], refs[4:6], refs[6:8], refs[8:12]
+    hidden, g_raw, g_all, t_all, w_all, sems = refs[12:]
     z, y, x, u = (where[i] for i in range(4))
-    c = chip_at(z, y, x)
     rows = hidden.shape[1]
     half = w_all.shape[1]
-    inner = ((z + 1) // 2) % 2
-    copies = []
-    for s in range(NZ):
-        cols = pl.ds(s * W, W)
+    copies = [(src, g_raw.at[k]) for k, src in enumerate(gated)]
+    for e, d in BITS:
+        cols = pl.ds((2 * e + d) * W, W)
         for side, src in enumerate((w_own, w_other)):
-            panel = src[0].at[s] if s < 2 else src[1].at[(s % 2) ^ inner]
-            copies.append((panel, w_all.at[side, :, cols]))
-        block = relative_chip(c, 0, 0, s)
+            copies.append((src[e].at[d], w_all.at[side, :, cols]))
+        block = chip_at(z ^ e, y, x ^ d)
         from_cols = pl.ds(pl.multiple_of(block * W, W), W)
-        for k in range(n):
+        for k in range(4):
             copies.append((tok[k].at[pl.ds(0, rows), from_cols], t_all.at[k, :, cols]))
-    copies = [pltpu.make_async_copy(a, b, sems.at[i]) for i, (a, b) in enumerate(copies)]
+    copies = [pltpu.make_async_copy(src, dst, sems.at[i]) for i, (src, dst) in enumerate(copies)]
     for copy in copies:
         copy.start()
-    for k, (by, bx) in enumerate(PLANE):
-        for s in range(NZ):
-            head = relative_chip(c, by, bx, s)
+    for copy in copies[:4]:
+        copy.wait()
+    for k, (far, by) in enumerate(BITS):
+        for e, d in BITS:
+            head = chip_at(z ^ (2 * far + e), y ^ by, x ^ d)
             cols = pl.ds(pl.multiple_of(head * W, W), W)
-            for j, (jy, jx) in enumerate(PLANE):
-                block = (jy ^ by) * NX + (jx ^ bx)
-                piece = gated[k][s, j] if k < n - 1 else gated[k + s // 2][s % 2, j]
-                g_all[block * rows : (block + 1) * rows, cols] = piece
-    for copy in copies:
+            for j in range(4):
+                block = j ^ k
+                g_all[block * rows : (block + 1) * rows, cols] = g_raw[k, e, d, j]
+    for copy in copies[4:]:
         copy.wait()
     total = 0.0
     for side, at in enumerate((u, 1 - u)):
         part = g_all[:, pl.ds(pl.multiple_of(at * half, half), half)]
         total += jnp.dot(part, w_all[side], preferred_element_type=F32)
-    for k in range(n):
-        for s in range(NZ):
-            term = total[k * rows : (k + 1) * rows, s * W : (s + 1) * W]
-            cols = pl.ds(pl.multiple_of((z ^ s) * W, W), W)
-            hidden[k, :, cols] = (t_all[k, :, s * W : (s + 1) * W].astype(F32) + term).astype(BF16)
+    for k in range(4):
+        terms = total[k * rows : (k + 1) * rows]
+        hidden[k] = (t_all[k].astype(F32) + terms).astype(BF16)
 
 
 def order_kernel(where, *refs):
-    pieces, (keep, send, h_all) = refs[: len(PLANE)], refs[len(PLANE) :]
-    y, x, u = (where[i] for i in range(1, 4))
+    pieces, (keep, send, h_all) = refs[:4], refs[4:]
+    z, y, x, u = (where[i] for i in range(4))
     half = keep.shape[1]
-    for (by, bx), ref in zip(PLANE, pieces):
-        for at in range(NZ):
-            block = chip_at(at, y ^ by, x ^ bx)
-            h_all[:, pl.ds(pl.multiple_of(block * W, W), W)] = ref[:, at * W : (at + 1) * W]
+    for (far, by), ref in zip(BITS, pieces):
+        for e, d in BITS:
+            block = chip_at(z ^ (2 * far + e), y ^ by, x ^ d)
+            from_cols = slice((2 * e + d) * W, (2 * e + d + 1) * W)
+            h_all[:, pl.ds(pl.multiple_of(block * W, W), W)] = ref[:, from_cols]
     keep[...] = h_all[:, pl.ds(pl.multiple_of(u * half, half), half)]
     send[...] = h_all[:, pl.ds(pl.multiple_of((1 - u) * half, half), half)]
 
@@ -386,27 +380,31 @@
     low = pair_up(mine)
 
     to_x, to_y = flip(0, 1), flip(1, 0)
+    own_ids = lax.dynamic_slice_in_dim(neg_ids, c * negs, negs, 0)
+    norms = jnp.sum(jnp.square(neg_emb.astype(F32)), axis=1)
+    neg = with_marks(neg_emb, float_parts(norms) + whole_parts(own_ids, 256))
     high = hop(low, flip(0, 0, 2))
-    w_plane, came = heads_in_plane(w_proj, y, x)
-    low = after(low, came[:2])
-    low_x, low_y = hop(low, to_x), hop(low, to_y)
+    w_plane, came = heads_in_plane(w_proj, y, x, low)
+    low_late = after(low, came)
+    out_row = jnp.concatenate([w_out[None], hop(after(w_out[None], came), to_x)])
+    neg_pair = pair_up(after(neg, came))
+    low_x, low_y = hop(low_late, to_x), hop(low_late, to_y)
     low_xy = across(low_x, low_y)
-    w_plane = after(w_plane, high)
+    high = after(high, out_row, neg_pair)
     high_x, high_y = hop(high, to_x), hop(high, to_y)
     high_xy = across(high_x, high_y)
+    out_own = [out_row, hop(after(out_row, high), flip(0, 0, 1))]
     tok = [low, high, low_x, high_x, low_y, high_y, *low_xy, *high_xy]
-    w_mine = after(heads_along_z(w_plane, z), low_xy, high_xy)
-    w_theirs = swap_cores(w_mine)
+    w_mine = heads_along_z(after(w_plane, high), z)
 
     t_rows = after(target_emb.reshape(2, rows, -1), high)
     t_keep = pick_row(t_rows, u)
     t_send = swap_cores(pick_row(t_rows, 1 - u))
-    own_ids = lax.dynamic_slice_in_dim(neg_ids, c * negs, negs, 0)
-    norms = jnp.sum(jnp.square(neg_emb.astype(F32)), axis=1)
-    neg = with_marks(neg_emb, float_parts(norms) + whole_parts(own_ids, 256))
-    neg_pair = pair_up(after(neg, w_mine, t_send))
-    neg_met, neg_far = relay_pairs(after(neg_pair, w_theirs), z)
-    out_pair = pair_up(after(w_out[None], neg_pair))
+    w_mine = after(w_mine, low_xy, high_xy, out_own, t_send)
+    w_theirs = swap_cores(w_mine)
+    neg_far = hop(after(neg_pair, w_mine), flip(0, 0, 2))
+    neg_near = jnp.concatenate([neg_pair, neg_far])
+    neg_x, neg_y = hop(neg_near, to_x), hop(neg_near, to_y)
 
     def project(pieces):
         count = sum(p.shape[0] for p in pieces)
@@ -426,42 +424,40 @@
         )
 
     gate_query, value_key, marks = project(tok)
-    kv_theirs = swap_cores(value_key)
-    out_met, out_far = relay_pairs(after(out_pair, neg_met, value_key), z)
-    neg_near = jnp.concatenate([neg_pair, neg_far(after(neg_met, value_key))])
-    neg_row = jnp.concatenate([neg_near, hop(neg_near, to_x)])
-    neg_own = [neg_row, hop(neg_row, to_y)]
+    kv_theirs = swap_cores(after(value_key, neg_far))
     (gated,) = call(
         attend_kernel,
         "attend",
-        [((NZ, plane, rows, W), BF16)],
-        [],
+        [((2, 2, 4, rows, W), BF16)],
+        [pltpu.VMEM((events, 2 * W), BF16)] * 3
+        + [pltpu.VMEM((events, W), BF16), pltpu.SemaphoreType.DMA((4,))],
         [gate_query, value_key, kv_theirs, marks],
-        4 * "v",
+        4 * "h",
         8 * events * events * W,
     )
-    gated = after(gated, neg_near)
-    gated = jnp.stack([gated[0]] + [hop(gated[s], flip(0, 0, s)) for s in range(1, NZ)])
-    out_met = after(out_met, gated)
-    gated = [gated, hop(gated, to_x), hop(gated, to_y)]
-    gated += across(gated[1], gated[2])
-    out_own = [after(out_pair, gated), after(out_far(out_met), gated)]
-    out_other = [swap_cores(w) for w in out_own]
+    out_other = [swap_cores(w) for w in after(out_own, gated)]
+    hops = [hop(gated[e, d], flip(0, d, e)) for e, d in BITS[1:]]
+    gated = jnp.stack([gated[0, 0], *hops]).reshape(gated.shape)
+    gated = [gated] + [hop(gated, flip(by, 0, 2 * far)) for far, by in BITS[1:]]
+    neg_x, neg_y = after((neg_x, neg_y), gated)
+    neg_own = [neg_near, neg_x, neg_y, *across(neg_x, neg_y)]
     (hidden,) = call(
         hidden_kernel,
         "hidden",
-        [((plane, rows, NZ * W), BF16)],
+        [((4, rows, 4 * W), BF16)],
         [
-            pltpu.VMEM((plane * rows, model), BF16),
-            pltpu.VMEM((plane, rows, NZ * W), BF16),
-            pltpu.VMEM((2, half, NZ * W), BF16),
-            pltpu.SemaphoreType.DMA((NZ * (2 + plane),)),
+            pltpu.VMEM((4, 2, 2, 4, rows, W), BF16),
+            pltpu.VMEM((4 * rows, model), BF16),
+            pltpu.VMEM((4, rows, 4 * W), BF16),
+            pltpu.VMEM((2, half, 4 * W), BF16),
+            pltpu.SemaphoreType.DMA((28,)),
         ],
-        [where, *gated, *out_own, *out_other, *tok[:7:2]],
-        "s" + 5 * "v" + 8 * "h",
-        2 * plane * rows * model * NZ * W,
-    )
-    pieces = [hidden[0]] + [hop(hidden[k], flip(*PLANE[k])) for k in range(1, plane)]
+        [where, *gated, *out_own, *out_other, low, low_y, high, high_y],
+        "s" + 12 * "h",
+        8 * rows * model * 4 * W,
+    )
+    pieces = [hidden[0]]
+    pieces += [hop(hidden[k], flip(BITS[k][1], 0, 2 * BITS[k][0])) for k in range(1, 4)]
     neg_own = jnp.concatenate(after(neg_own, hidden))
     neg_other = swap_cores(neg_own)
     h_keep, h_send = call(

time: 178 us -> 173 us (0.972)
  waiting for transfers between devices: 86.6 us -> 83.4 us
  other arithmetic: 8.62 us -> 6.1 us
  starting transfers between devices: 50.1 us -> 47.9 us
  local copies, waits for them, and re-layouts: 14.1 us -> 15.9 us
    ppermute x31 -> x30, waiting for transfers between devices: 83.7 us -> 77.9 us  [hop(): return lax.ppermute(value, 'ctx', perm)]
    ppermute x2, waiting for transfers between devices: 0.52 us -> 5.43 us  [heads_along_z(): lax.ppermute(pick_row(heads, e ^ z & 1), ('ctx', 'tp'), perm)]
    ppermute x7, starting transfers between devices: 5.18 us -> 0.83 us  [swap_cores(): return lax.ppermute(value, 'tp', SWAP)]
    slice x6, local copies, waits for them, and re-layouts: 1.06 us -> 4.88 us  [across(): return [hop(value_x[:half], flip(1, 0)), hop(value_y[half:], flip(0, 1))]]
    ppermute x7, waiting for transfers between devices: 2.43 us -> 0.06 us  [swap_cores(): return lax.ppermute(value, 'tp', SWAP)]
    ppermute x31 -> x30, starting transfers between devices: 39.3 us -> 41.1 us  [hop(): return lax.ppermute(value, 'ctx', perm)]
    unnamed x48 -> x21, local copies, waits for them, and re-layouts: 7.09 us -> 5.47 us
  transfers between devices with their start and end apart: 40 -> 39, of which waited for: 21 -> 19; matrix products, arithmetic and copies ran while one was open for 9% -> 10% of each run, Pallas kernels for 9% -> 9%
where the time goes in v9:
time: 173 us; the launch traced here: 172 us
  waiting for transfers between devices  83.4 us (48%)
  starting transfers between devices  47.9 us (28%)
  Pallas kernels  18 us (10%)
  local copies, waits for them, and re-layouts  15.9 us (9%)
  other arithmetic  6.1 us (4%)
    ppermute x30, waiting for transfers between devices, hop(): return lax.ppermute(value, 'ctx', perm)  77.9 us
    ppermute x30, starting transfers between devices, hop(): return lax.ppermute(value, 'ctx', perm)  41.1 us
    pallas_call x6, Pallas kernels, call(): pl.pallas_call(kernel, out_shape=[jax.ShapeDtypeStruct(shape, dtype) for...  18 us
    ppermute x2, starting transfers between devices, heads_along_z(): lax.ppermute(pick_row(heads, e ^ z & 1), ('ctx', 'tp'), perm)  5.97 us
    unnamed x21, local copies, waits for them, and re-layouts  5.47 us
    ppermute x2, waiting for transfers between devices, heads_along_z(): lax.ppermute(pick_row(heads, e ^ z & 1), ('ctx', 'tp'), perm)  5.43 us
    slice x6, local copies, waits for them, and re-layouts, across(): return [hop(value_x[:half], flip(1, 0)), hop(value_y[half:], flip(0, 1))]  4.88 us
  transfers between devices with their start and end apart: 39, of which 19 were waited for; matrix products, arithmetic and copies ran while one was open for 10% of the time, Pallas kernels for 9%

profile of v9, /device:TPU:0, one launch (start us, length us, event | category | flops | bytes accessed | tf_op | source)
XLA Modules:
  0.0 172.3 jit_solution(1673447211514441421)
XLA Ops:
  2.5 3.0 %collective-permute-start = (bf16[64,2176]{1,0:T(8,128)(2,1)}, bf16[64,2176]{1,0:T(8,128)(2,1)S(1)}, u32[]{:S(2)}, u32[]{:S(2)}) collective-permute-start(bf16[64,2176]{1,0:T(8,128)(2,1)} %pad_maximum_fusion.2), channel_id=1, source_target_pairs={{0,8},{2,10},{4,12},{6,14},{8,0},{10,2},{12,4},{14,6},{16,24},{18,... | collective-permute-start | bytes 835592 | tf_op jit(solution)/shard_map/ppermute | solution.py:107
  16.3 2.8 %collective-permute-start.1 = (bf16[128,2176]{1,0:T(8,128)(2,1)S(1)}, bf16[128,2176]{1,0:T(8,128)(2,1)S(1)}, u32[]{:S(2)}, u32[]{:S(2)}) collective-permute-start(bf16[128,2176]{1,0:T(8,128)(2,1)S(1)} %pad_maximum_fusion.refs_0_.refs_8_), channel_id=1, source_target_pairs={{0,16},{2,18},{4,20},{6,22},{8,24},{10,26},{12,28},{14,30},{16,0},... | collective-permute-start | bytes 1671176 | tf_op jit(solution)/shard_map/ppermute | solution.py:107
  19.1 2.8 %collective-permute-done.2 = bf16[2,128,512]{2,1,0:T(8,128)(2,1)S(1)} collective-permute-done((bf16[2,128,512]{2,1,0:T(8,128)(2,1)}, bf16[2,128,512]{2,1,0:T(8,128)(2,1)S(1)}, u32[]{:S(2)}, u32[]{:S(2)}) %collective-permute-start.2) | collective-permute-done | bytes 262176 | tf_op jit(solution)/shard_map/ppermute | solution.py:107
  21.9 5.0 %collective-permute-done.3 = bf16[2,128,512]{2,1,0:T(8,128)(2,1)S(1)} collective-permute-done((bf16[2,128,512]{2,1,0:T(8,128)(2,1)}, bf16[2,128,512]{2,1,0:T(8,128)(2,1)S(1)}, u32[]{:S(2)}, u32[]{:S(2)}) %collective-permute-start.3) | collective-permute-done | bytes 262176 | tf_op jit(solution)/shard_map/ppermute | solution.py:107
  32.7 10.6 %collective-permute-done.6 = bf16[64,1152]{1,0:T(8,128)(2,1)S(1)} collective-permute-done((bf16[64,1152]{1,0:T(8,128)(2,1)S(1)}, bf16[64,1152]{1,0:T(8,128)(2,1)S(1)}, u32[]{:S(2)}, u32[]{:S(2)}) %collective-permute-start.6) | collective-permute-done | bytes 147488 | tf_op jit(solution)/shard_map/ppermute | solution.py:107
  51.7 5.4 %collective-permute-start.15 = (bf16[4,128,512]{2,1,0:T(8,128)(2,1)}, bf16[4,128,512]{2,1,0:T(8,128)(2,1)}, u32[]{:S(2)}, u32[]{:S(2)}) collective-permute-start(bf16[4,128,512]{2,1,0:T(8,128)(2,1)} %get-tuple-element.64), channel_id=1, source_target_pairs={{0,0},{1,16},{2,2},{3,18},{4,4},{5,20},{6,6},{7,22},{8,8},{9,24},{... | collective-permute-start | bytes 1572872 | tf_op jit(solution)/shard_map/ppermute | solution.py:156
  66.4 5.4 %collective-permute-done.16 = bf16[4,128,512]{2,1,0:T(8,128)(2,1)} collective-permute-done((bf16[4,128,512]{2,1,0:T(8,128)(2,1)}, bf16[4,128,512]{2,1,0:T(8,128)(2,1)}, u32[]{:S(2)}, u32[]{:S(2)}) %collective-permute-start.16) | collective-permute-done | bytes 524320 | tf_op jit(solution)/shard_map/ppermute | solution.py:156
  75.6 7.4 %collective-permute-done.17.refs_5_ = bf16[2,1024,128]{2,1,0:T(8,128)(2,1)} collective-permute-done((bf16[2,1024,128]{2,1,0:T(8,128)(2,1)S(1)}, bf16[2,1024,128]{2,1,0:T(8,128)(2,1)}, u32[]{:S(2)}, u32[]{:S(2)}) %collective-permute-start.17) | collective-permute-done | bytes 524320 | tf_op jit(solution)/shard_map/ppermute | solution.py:107
  83.6 2.2 %collective-permute-start.20 = (bf16[128,1152]{1,0:T(8,128)(2,1)}, bf16[128,1152]{1,0:T(8,128)(2,1)S(1)}, u32[]{:S(2)}, u32[]{:S(2)}) collective-permute-start(bf16[128,1152]{1,0:T(8,128)(2,1)} %get-tuple-element.43), channel_id=1, source_target_pairs={{0,16},{2,18},{4,20},{6,22},{8,24},{10,26},{12,28},{14,30},{16,0},... | collective-permute-start | bytes 884744 | tf_op jit(solution)/shard_map/ppermute | solution.py:107
  86.9 5.4 %project.1 = (bf16[1024,256]{1,0:T(8,128)(2,1)S(1)}, bf16[1024,256]{1,0:T(8,128)(2,1)S(1)}, bf16[1024,128]{1,0:T(8,128)(2,1)S(1)}) custom-call(s32[4]{0:T(128)S(1)} %pad_add_fusion.where, bf16[128,2176]{1,0:T(8,128)(2,1)S(1)} %pad_maximum_fusion.refs_0_.refs_8_, bf16[128,2176]{1,0:T(8,128)(2,1)S(1)} %collective-permute-done.1.refs_1_.refs_10_, ...), custom_call_target="tpu_custom_call" | custom-call | flops 2147483648 | bytes 6553616 | tf_op jit(solution)/shard_map/project/pallas_call | solution.py:333
  92.3 7.7 %collective-permute-done.20 = bf16[128,1152]{1,0:T(8,128)(2,1)S(1)} collective-permute-done((bf16[128,1152]{1,0:T(8,128)(2,1)}, bf16[128,1152]{1,0:T(8,128)(2,1)S(1)}, u32[]{:S(2)}, u32[]{:S(2)}) %collective-permute-start.20) | collective-permute-done | bytes 294944 | tf_op jit(solution)/shard_map/ppermute | solution.py:107
  102.1 3.4 %attend.1 = bf16[2,2,4,64,128]{4,3,2,1,0:T(8,128)(2,1)S(1)} custom-call(bf16[1024,256]{1,0:T(8,128)(2,1)S(1)} %get-tuple-element.41.gq_hbm, bf16[1024,256]{1,0:T(8,128)(2,1)S(1)} %get-tuple-element.44.own_hbm, bf16[1024,256]{1,0:T(8,128)(2,1)S(1)} %collective-permute-done.21.other_hbm, bf16[1024,128]{1,0:T(8,128)(2,1)S(1)} %get-tuple-element.45.marks_hbm), custom_call_target="tpu_custom_call" | custom-call | flops 1073741824 | bytes 1835008 | tf_op jit(solution)/shard_map/attend/pallas_call | solution.py:333
  109.1 2.1 %collective-permute-done.24 = bf16[4,64,128]{2,1,0:T(8,128)(2,1)S(1)} collective-permute-done((bf16[4,64,128]{2,1,0:T(8,128)(2,1)S(1)}, bf16[4,64,128]{2,1,0:T(8,128)(2,1)S(1)}, u32[]{:S(2)}, u32[]{:S(2)}) %collective-permute-start.24) | collective-permute-done | bytes 65568 | tf_op jit(solution)/shard_map/ppermute | solution.py:107
  111.9 6.7 %collective-permute-done.22 = bf16[4,64,128]{2,1,0:T(8,128)(2,1)S(1)} collective-permute-done((bf16[4,64,128]{2,1,0:T(8,128)(2,1)S(1)}, bf16[4,64,128]{2,1,0:T(8,128)(2,1)S(1)}, u32[]{:S(2)}, u32[]{:S(2)}) %collective-permute-start.22) | collective-permute-done | bytes 65568 | tf_op jit(solution)/shard_map/ppermute | solution.py:107
  120.2 2.9 %collective-permute-start.27 = (bf16[2,2,4,64,128]{4,3,2,1,0:T(8,128)(2,1)S(1)}, bf16[2,2,4,64,128]{4,3,2,1,0:T(8,128)(2,1)S(1)}, u32[]{:S(2)}, u32[]{:S(2)}) collective-permute-start(bf16[2,2,4,64,128]{4,3,2,1,0:T(8,128)(2,1)S(1)} %bitcast.75), channel_id=1, source_target_pairs={{0,20},{2,22},{4,16},{6,18},{8,28},{10,30},{12,24},{14,26},{16,4},... | collective-permute-start | bytes 786440 | tf_op jit(solution)/shard_map/ppermute | solution.py:107
  123.1 3.5 %collective-permute-done.25.refs_1_ = bf16[2,2,4,64,128]{4,3,2,1,0:T(8,128)(2,1)S(1)} collective-permute-done((bf16[2,2,4,64,128]{4,3,2,1,0:T(8,128)(2,1)S(1)}, bf16[2,2,4,64,128]{4,3,2,1,0:T(8,128)(2,1)S(1)}, u32[]{:S(2)}, u32[]{:S(2)}) %collective-permute-start.25) | collective-permute-done | bytes 262176 | tf_op jit(solution)/shard_map/ppermute | solution.py:107
  126.7 14.3 %collective-permute-done.26.refs_2_ = bf16[2,2,4,64,128]{4,3,2,1,0:T(8,128)(2,1)S(1)} collective-permute-done((bf16[2,2,4,64,128]{4,3,2,1,0:T(8,128)(2,1)S(1)}, bf16[2,2,4,64,128]{4,3,2,1,0:T(8,128)(2,1)S(1)}, u32[]{:S(2)}, u32[]{:S(2)}) %collective-permute-start.26) | collective-permute-done | bytes 262176 | tf_op jit(solution)/shard_map/ppermute | solution.py:107
  141.0 4.6 %collective-permute-done.27.refs_3_ = bf16[2,2,4,64,128]{4,3,2,1,0:T(8,128)(2,1)S(1)} collective-permute-done((bf16[2,2,4,64,128]{4,3,2,1,0:T(8,128)(2,1)S(1)}, bf16[2,2,4,64,128]{4,3,2,1,0:T(8,128)(2,1)S(1)}, u32[]{:S(2)}, u32[]{:S(2)}) %collective-permute-start.27) | collective-permute-done | bytes 262176 | tf_op jit(solution)/shard_map/ppermute | solution.py:107
  147.9 2.8 %hidden.1 = bf16[4,64,512]{2,1,0:T(8,128)(2,1)S(1)} custom-call(s32[4]{0:T(128)S(1)} %pad_add_fusion.where, bf16[2,2,4,64,128]{4,3,2,1,0:T(8,128)(2,1)S(1)} %bitcast.76, bf16[2,2,4,64,128]{4,3,2,1,0:T(8,128)(2,1)S(1)} %collective-permute-done.25.refs_1_, bf16[2,2,4,64,128]{4,3,2,1,0:T(8,128)(2,1)S(1)} %collective-permute-done.26.refs_2_, ...), custom_call_target="tpu_custom_call" | custom-call | flops 536870912 | bytes 5373968 | tf_op jit(solution)/shard_map/hidden/pallas_call | solution.py:333
  150.7 3.0 %collective-permute-done.36 = bf16[128,1152]{1,0:T(8,128)(2,1)S(1)} collective-permute-done((bf16[128,1152]{1,0:T(8,128)(2,1)S(1)}, bf16[128,1152]{1,0:T(8,128)(2,1)S(1)}, u32[]{:S(2)}, u32[]{:S(2)}) %collective-permute-start.36) | collective-permute-done | bytes 294944 | tf_op jit(solution)/shard_map/ppermute | solution.py:107
  156.1 3.8 %collective-permute-start.32 = (bf16[64,512]{1,0:T(8,128)(2,1)S(1)}, bf16[64,512]{1,0:T(8,128)(2,1)S(1)}, u32[]{:S(2)}, u32[]{:S(2)}) collective-permute-start(bf16[64,512]{1,0:T(8,128)(2,1)S(1)} %get-tuple-element.72), channel_id=1, source_target_pairs={{0,20},{2,22},{4,16},{6,18},{8,28},{10,30},{12,24},{14,26},{16,4},... | collective-permute-start | bytes 196616 | tf_op jit(solution)/shard_map/ppermute | solution.py:107
  160.0 2.1 %collective-permute-done.31.refs_2_ = bf16[64,512]{1,0:T(8,128)(2,1)S(1)} collective-permute-done((bf16[64,512]{1,0:T(8,128)(2,1)S(1)}, bf16[64,512]{1,0:T(8,128)(2,1)S(1)}, u32[]{:S(2)}, u32[]{:S(2)}) %collective-permute-start.31) | collective-permute-done | bytes 65568 | tf_op jit(solution)/shard_map/ppermute | solution.py:107
  162.1 3.6 %collective-permute-done.32.refs_3_ = bf16[64,512]{1,0:T(8,128)(2,1)S(1)} collective-permute-done((bf16[64,512]{1,0:T(8,128)(2,1)S(1)}, bf16[64,512]{1,0:T(8,128)(2,1)S(1)}, u32[]{:S(2)}, u32[]{:S(2)}) %collective-permute-start.32) | collective-permute-done | bytes 65568 | tf_op jit(solution)/shard_map/ppermute | solution.py:107
  166.5 4.1 %loss.1 = f32[1,64]{1,0:T(1,128)} custom-call(bf16[64,1024]{1,0:T(8,128)(2,1)S(1)} %get-tuple-element.48.h_keep.keep, bf16[64,1024]{1,0:T(8,128)(2,1)S(1)} %get-tuple-element.49.h_send, bf16[64,1024]{1,0:T(8,128)(2,1)S(1)} %get-tuple-element.70.t_keep, bf16[64,1024]{1,0:T(8,128)(2,1)S(1)} %collective-permute-done.18.t_send, s32[64,1]{1,0:T(8,128)S(1)} %copy.63.t_ids, ...), custom_call_target="tpu_custom_call" | custom-call | flops 268435456 | bytes 5243136 | tf_op jit(solution)/shard_map/loss/pallas_call | solution.py:333
  (124 shorter events, 56.4 us)
Async XLA Ops:
  14.1 12.8 %collective-permute-start.3 = (bf16[2,128,512]{2,1,0:T(8,128)(2,1)}, bf16[2,128,512]{2,1,0:T(8,128)(2,1)S(1)}, u32[]{:S(2)}, u32[]{:S(2)}) collective-permute-start(bf16[2,128,512]{2,1,0:T(8,128)(2,1)} %bitcast.13), channel_id=1, source_target_pairs={{0,4},{2,6},{4,0},{6,2},{8,12},{10,14},{12,8},{14,10},{16,20},{18,... | collective-permute-start | bytes 786440 | tf_op jit(solution)/shard_map/ppermute | solution.py:107
  15.6 11.3 %collective-permute-start.4 = (bf16[2,128,512]{2,1,0:T(8,128)(2,1)}, bf16[2,128,512]{2,1,0:T(8,128)(2,1)S(1)}, u32[]{:S(2)}, u32[]{:S(2)}) collective-permute-start(bf16[2,128,512]{2,1,0:T(8,128)(2,1)} %bitcast.14), channel_id=1, source_target_pairs={{0,6},{2,4},{4,2},{6,0},{8,14},{10,12},{12,10},{14,8},{16,22},{18,... | collective-permute-start | bytes 786440 | tf_op jit(solution)/shard_map/ppermute | solution.py:107
  16.3 31.5 %collective-permute-start.1 = (bf16[128,2176]{1,0:T(8,128)(2,1)S(1)}, bf16[128,2176]{1,0:T(8,128)(2,1)S(1)}, u32[]{:S(2)}, u32[]{:S(2)}) collective-permute-start(bf16[128,2176]{1,0:T(8,128)(2,1)S(1)} %pad_maximum_fusion.refs_0_.refs_8_), channel_id=1, source_target_pairs={{0,16},{2,18},{4,20},{6,22},{8,24},{10,26},{12,28},{14,30},{16,0},... | collective-permute-start | bytes 1671176 | tf_op jit(solution)/shard_map/ppermute | solution.py:107
  27.6 15.7 %collective-permute-start.6 = (bf16[64,1152]{1,0:T(8,128)(2,1)S(1)}, bf16[64,1152]{1,0:T(8,128)(2,1)S(1)}, u32[]{:S(2)}, u32[]{:S(2)}) collective-permute-start(bf16[64,1152]{1,0:T(8,128)(2,1)S(1)} %fusion.1), channel_id=1, source_target_pairs={{0,8},{2,10},{4,12},{6,14},{8,0},{10,2},{12,4},{14,6},{16,24},{18,... | collective-permute-start | bytes 442376 | tf_op jit(solution)/shard_map/ppermute | solution.py:107
  29.1 22.5 %collective-permute-start.7 = (bf16[128,2176]{1,0:T(8,128)(2,1)S(1)}, bf16[128,2176]{1,0:T(8,128)(2,1)}, u32[]{:S(2)}, u32[]{:S(2)}) collective-permute-start(bf16[128,2176]{1,0:T(8,128)(2,1)S(1)} %pad_maximum_fusion.refs_0_.refs_8_), channel_id=1, source_target_pairs={{0,2},{2,0},{4,6},{6,4},{8,10},{10,8},{12,14},{14,12},{16,18},{18,... | collective-permute-start | bytes 1671176 | tf_op jit(solution)/shard_map/ppermute | solution.py:107
  30.3 26.7 %collective-permute-start.9 = (bf16[128,2176]{1,0:T(8,128)(2,1)S(1)}, bf16[128,2176]{1,0:T(8,128)(2,1)S(1)}, u32[]{:S(2)}, u32[]{:S(2)}) collective-permute-start(bf16[128,2176]{1,0:T(8,128)(2,1)S(1)} %pad_maximum_fusion.refs_0_.refs_8_), channel_id=1, source_target_pairs={{0,4},{2,6},{4,0},{6,2},{8,12},{10,14},{12,8},{14,10},{16,20},{18,... | collective-permute-start | bytes 1671176 | tf_op jit(solution)/shard_map/ppermute | solution.py:107
  31.2 15.6 %collective-permute-start.5 = (bf16[1,1024,128]{2,1,0:T(8,128)(2,1)}, bf16[1,1024,128]{2,1,0:T(8,128)(2,1)S(1)}, u32[]{:S(2)}, u32[]{:S(2)}) collective-permute-start(bf16[1,1024,128]{2,1,0:T(8,128)(2,1)} %bitcast.82), channel_id=1, source_target_pairs={{0,2},{2,0},{4,6},{6,4},{8,10},{10,8},{12,14},{14,12},{16,18},{18,... | collective-permute-start | bytes 786440 | tf_op jit(solution)/shard_map/ppermute | solution.py:107
  47.8 11.6 %collective-permute-start.8 = (bf16[128,2176]{1,0:T(8,128)(2,1)S(1)}, bf16[128,2176]{1,0:T(8,128)(2,1)}, u32[]{:S(2)}, u32[]{:S(2)}) collective-permute-start(bf16[128,2176]{1,0:T(8,128)(2,1)S(1)} %collective-permute-done.1.refs_1_.refs_10_), channel_id=1, source_target_pairs={{0,2},{2,0},{4,6},{6,4},{8,10},{10,8},{12,14},{14,12},{16,18},{18,... | collective-permute-start | bytes 1671176 | tf_op jit(solution)/shard_map/ppermute | solution.py:107
  49.4 14.3 %collective-permute-start.10 = (bf16[128,2176]{1,0:T(8,128)(2,1)S(1)}, bf16[128,2176]{1,0:T(8,128)(2,1)S(1)}, u32[]{:S(2)}, u32[]{:S(2)}) collective-permute-start(bf16[128,2176]{1,0:T(8,128)(2,1)S(1)} %collective-permute-done.1.refs_1_.refs_10_), channel_id=1, source_target_pairs={{0,4},{2,6},{4,0},{6,2},{8,12},{10,14},{12,8},{14,10},{16,20},{18,... | collective-permute-start | bytes 1671176 | tf_op jit(solution)/shard_map/ppermute | solution.py:107
  51.0 20.8 %collective-permute-start.16 = (bf16[4,128,512]{2,1,0:T(8,128)(2,1)}, bf16[4,128,512]{2,1,0:T(8,128)(2,1)}, u32[]{:S(2)}, u32[]{:S(2)}) collective-permute-start(bf16[4,128,512]{2,1,0:T(8,128)(2,1)} %get-tuple-element.65), channel_id=1, source_target_pairs={{0,8},{1,24},{2,10},{3,26},{4,12},{5,28},{6,14},{7,30},{8,0},{9,16... | collective-permute-start | bytes 1572872 | tf_op jit(solution)/shard_map/ppermute | solution.py:156
  51.7 21.9 %collective-permute-start.15 = (bf16[4,128,512]{2,1,0:T(8,128)(2,1)}, bf16[4,128,512]{2,1,0:T(8,128)(2,1)}, u32[]{:S(2)}, u32[]{:S(2)}) collective-permute-start(bf16[4,128,512]{2,1,0:T(8,128)(2,1)} %get-tuple-element.64), channel_id=1, source_target_pairs={{0,0},{1,16},{2,2},{3,18},{4,4},{5,20},{6,6},{7,22},{8,8},{9,24},{... | collective-permute-start | bytes 1572872 | tf_op jit(solution)/shard_map/ppermute | solution.py:156
  57.0 26.0 %collective-permute-start.17 = (bf16[2,1024,128]{2,1,0:T(8,128)(2,1)S(1)}, bf16[2,1024,128]{2,1,0:T(8,128)(2,1)}, u32[]{:S(2)}, u32[]{:S(2)}) collective-permute-start(bf16[2,1024,128]{2,1,0:T(8,128)(2,1)S(1)} %pad_maximum_fusion.1.refs_4_), channel_id=1, source_target_pairs={{0,8},{2,10},{4,12},{6,14},{8,0},{10,2},{12,4},{14,6},{16,24},{18,... | collective-permute-start | bytes 1572872 | tf_op jit(solution)/shard_map/ppermute | solution.py:107
  63.6 19.4 %collective-permute-start.11 = (bf16[64,2176]{1,0:T(8,128)(2,1)}, bf16[64,2176]{1,0:T(8,128)(2,1)}, u32[]{:S(2)}, u32[]{:S(2)}) collective-permute-start(bf16[64,2176]{1,0:T(8,128)(2,1)} %slice.56), channel_id=1, source_target_pairs={{0,4},{2,6},{4,0},{6,2},{8,12},{10,14},{12,8},{14,10},{16,20},{18,... | collective-permute-start | bytes 835592 | tf_op jit(solution)/shard_map/ppermute | solution.py:107
  65.8 17.2 %collective-permute-start.12 = (bf16[64,2176]{1,0:T(8,128)(2,1)}, bf16[64,2176]{1,0:T(8,128)(2,1)}, u32[]{:S(2)}, u32[]{:S(2)}) collective-permute-start(bf16[64,2176]{1,0:T(8,128)(2,1)} %slice.57), channel_id=1, source_target_pairs={{0,2},{2,0},{4,6},{6,4},{8,10},{10,8},{12,14},{14,12},{16,18},{18,... | collective-permute-start | bytes 835592 | tf_op jit(solution)/shard_map/ppermute | solution.py:107
  71.8 11.2 %collective-permute-start.13 = (bf16[64,2176]{1,0:T(8,128)(2,1)}, bf16[64,2176]{1,0:T(8,128)(2,1)}, u32[]{:S(2)}, u32[]{:S(2)}) collective-permute-start(bf16[64,2176]{1,0:T(8,128)(2,1)} %slice.58), channel_id=1, source_target_pairs={{0,4},{2,6},{4,0},{6,2},{8,12},{10,14},{12,8},{14,10},{16,20},{18,... | collective-permute-start | bytes 835592 | tf_op jit(solution)/shard_map/ppermute | solution.py:107
  83.6 16.4 %collective-permute-start.20 = (bf16[128,1152]{1,0:T(8,128)(2,1)}, bf16[128,1152]{1,0:T(8,128)(2,1)S(1)}, u32[]{:S(2)}, u32[]{:S(2)}) collective-permute-start(bf16[128,1152]{1,0:T(8,128)(2,1)} %get-tuple-element.43), channel_id=1, source_target_pairs={{0,16},{2,18},{4,20},{6,22},{8,24},{10,26},{12,28},{14,30},{16,0},... | collective-permute-start | bytes 884744 | tf_op jit(solution)/shard_map/ppermute | solution.py:107
  100.0 20.2 %collective-permute-start.34 = (bf16[256,1152]{1,0:T(8,128)(2,1)S(1)}, bf16[256,1152]{1,0:T(8,128)(2,1)S(1)}, u32[]{:S(2)}, u32[]{:S(2)}) collective-permute-start(bf16[256,1152]{1,0:T(8,128)(2,1)S(1)} %constant_dynamic-update-slice_fusion.2), channel_id=1, source_target_pairs={{0,2},{2,0},{4,6},{6,4},{8,10},{10,8},{12,14},{14,12},{16,18},{18,... | collective-permute-start | bytes 1769480 | tf_op jit(solution)/shard_map/ppermute | solution.py:107
  101.0 19.2 %collective-permute-start.35 = (bf16[256,1152]{1,0:T(8,128)(2,1)S(1)}, bf16[256,1152]{1,0:T(8,128)(2,1)S(1)}, u32[]{:S(2)}, u32[]{:S(2)}) collective-permute-start(bf16[256,1152]{1,0:T(8,128)(2,1)S(1)} %constant_dynamic-update-slice_fusion.2), channel_id=1, source_target_pairs={{0,4},{2,6},{4,0},{6,2},{8,12},{10,14},{12,8},{14,10},{16,20},{18,... | collective-permute-start | bytes 1769480 | tf_op jit(solution)/shard_map/ppermute | solution.py:107
  108.6 10.1 %collective-permute-start.22 = (bf16[4,64,128]{2,1,0:T(8,128)(2,1)S(1)}, bf16[4,64,128]{2,1,0:T(8,128)(2,1)S(1)}, u32[]{:S(2)}, u32[]{:S(2)}) collective-permute-start(bf16[4,64,128]{2,1,0:T(8,128)(2,1)S(1)} %get-tuple-element.79), channel_id=1, source_target_pairs={{0,2},{2,0},{4,6},{6,4},{8,10},{10,8},{12,14},{14,12},{16,18},{18,... | collective-permute-start | bytes 196616 | tf_op jit(solution)/shard_map/ppermute | solution.py:107
  111.2 36.6 %collective-permute-start.28 = (bf16[2,1024,128]{2,1,0:T(8,128)(2,1)S(1)}, bf16[2,1024,128]{2,1,0:T(8,128)(2,1)S(1)}, u32[]{:S(2)}, u32[]{:S(2)}) collective-permute-start(bf16[2,1024,128]{2,1,0:T(8,128)(2,1)S(1)} %pad_maximum_fusion.1.refs_4_), channel_id=1, source_target_pairs={{0,1},{1,0},{2,3},{3,2},{4,5},{5,4},{6,7},{7,6},{8,9},{9,8},{10,11... | collective-permute-start | bytes 1572872 | tf_op jit(solution)/shard_map/ppermute | solution.py:111
  111.9 36.0 %collective-permute-start.29 = (bf16[2,1024,128]{2,1,0:T(8,128)(2,1)}, bf16[2,1024,128]{2,1,0:T(8,128)(2,1)S(1)}, u32[]{:S(2)}, u32[]{:S(2)}) collective-permute-start(bf16[2,1024,128]{2,1,0:T(8,128)(2,1)} %collective-permute-done.17.refs_5_), channel_id=1, source_target_pairs={{0,1},{1,0},{2,3},{3,2},{4,5},{5,4},{6,7},{7,6},{8,9},{9,8},{10,11... | collective-permute-start | bytes 1572872 | tf_op jit(solution)/shard_map/ppermute | solution.py:111
  120.2 20.8 %collective-permute-start.26 = (bf16[2,2,4,64,128]{4,3,2,1,0:T(8,128)(2,1)S(1)}, bf16[2,2,4,64,128]{4,3,2,1,0:T(8,128)(2,1)S(1)}, u32[]{:S(2)}, u32[]{:S(2)}) collective-permute-start(bf16[2,2,4,64,128]{4,3,2,1,0:T(8,128)(2,1)S(1)} %bitcast.74), channel_id=1, source_target_pairs={{0,16},{2,18},{4,20},{6,22},{8,24},{10,26},{12,28},{14,30},{16,0},... | collective-permute-start | bytes 786440 | tf_op jit(solution)/shard_map/ppermute | solution.py:107
  120.2 25.4 %collective-permute-start.27 = (bf16[2,2,4,64,128]{4,3,2,1,0:T(8,128)(2,1)S(1)}, bf16[2,2,4,64,128]{4,3,2,1,0:T(8,128)(2,1)S(1)}, u32[]{:S(2)}, u32[]{:S(2)}) collective-permute-start(bf16[2,2,4,64,128]{4,3,2,1,0:T(8,128)(2,1)S(1)} %bitcast.75), channel_id=1, source_target_pairs={{0,20},{2,22},{4,16},{6,18},{8,28},{10,30},{12,24},{14,26},{16,4},... | collective-permute-start | bytes 786440 | tf_op jit(solution)/shard_map/ppermute | solution.py:107
  155.3 11.2 %collective-permute-start.38 = (bf16[1024,1152]{1,0:T(8,128)(2,1)S(1)}, bf16[1024,1152]{1,0:T(8,128)(2,1)}, u32[]{:S(2)}, u32[]{:S(2)}) collective-permute-start(bf16[1024,1152]{1,0:T(8,128)(2,1)S(1)} %constant_dynamic-update-slice_fusion.5.n_own), channel_id=1, source_target_pairs={{0,1},{1,0},{2,3},{3,2},{4,5},{5,4},{6,7},{7,6},{8,9},{9,8},{10,11... | collective-permute-start | bytes 7077896 | tf_op jit(solution)/shard_map/ppermute | solution.py:111
  (22 other events, 139.3 us)

commit v10 on v9

--- a/solution.py
+++ b/solution.py
@@ -80,7 +80,6 @@
 NZ, NY, NX = 4, 2, 2
 CHIPS = NZ * NY * NX
 PLANE = [(by, bx) for by in range(NY) for bx in range(NX)]
-BITS = [(0, 0), (0, 1), (1, 0), (1, 1)]
 SWAP = [(0, 1), (1, 0)]
 W = HEAD_DIM
 ACROSS = (((1,), (1,)), ((), ()))
@@ -204,7 +203,8 @@
     return pick.astype(BF16)
 
 
-def attend_kernel(gq_hbm, own_hbm, other_hbm, marks_hbm, gated, gate_query, own, other, marks, sems):
+def attend_kernel(where, gq_hbm, own_hbm, other_hbm, marks_hbm, gated, gate_query, own, other, marks, sems):
+    z, y, x = (where[i] for i in range(3))
     sources = (gq_hbm, own_hbm, other_hbm, marks_hbm)
     run_copies(
         [
@@ -213,7 +213,7 @@
         ]
     )
     pick = pick_columns({0: 128.0, 1: 1.0}, {2: 128.0, 3: 1.0})
-    piece = gated.shape[3]
+    piece = gated.shape[1]
     tile = NZ * piece
     key_pos = lax.dot_general(pick, marks[...], ACROSS, preferred_element_type=F32)
     for k, (by, bx) in enumerate(PLANE):
@@ -231,56 +231,41 @@
         normed = attn * lax.rsqrt(jnp.mean(attn * attn, axis=-1, keepdims=True) + 1e-06)
         out = (normed * gate_query[span, :W].astype(F32)).astype(BF16)
         for s in range(NZ):
-            gated[s % 2, bx, 2 * (s // 2) + by] = out[s * piece : (s + 1) * piece]
-
-
-def hidden_kernel(where, *refs):
-    gated, w_own, w_other, tok = refs[:4], refs[4:6], refs[6:8], refs[8:12]
-    hidden, g_raw, g_all, t_all, w_all, sems = refs[12:]
+            chip = chip_at(z ^ s, y ^ by, x ^ bx)
+            gated[pl.ds(chip, 1)] = out[s * piece : (s + 1) * piece][None]
+
+
+def hidden_kernel(where, gated, low, high, low_other, high_other, tokens, *refs):
+    keep, send, g_all, h_all, w_all, sems = refs
     z, y, x, u = (where[i] for i in range(4))
-    rows = hidden.shape[1]
-    half = w_all.shape[1]
-    copies = [(src, g_raw.at[k]) for k, src in enumerate(gated)]
-    for e, d in BITS:
-        cols = pl.ds((2 * e + d) * W, W)
-        for side, src in enumerate((w_own, w_other)):
-            copies.append((src[e].at[d], w_all.at[side, :, cols]))
-        block = chip_at(z ^ e, y, x ^ d)
-        from_cols = pl.ds(pl.multiple_of(block * W, W), W)
-        for k in range(4):
-            copies.append((tok[k].at[pl.ds(0, rows), from_cols], t_all.at[k, :, cols]))
-    copies = [pltpu.make_async_copy(src, dst, sems.at[i]) for i, (src, dst) in enumerate(copies)]
+    chips, rows, _ = gated.shape
+    half = chips * W // 2
+    copies = []
+    for group, sides in enumerate(((low, low_other), (high, high_other))):
+        for at in range(chips // 2):
+            cols = pl.ds((group * chips // 2 + at) * W, W)
+            for side, src in enumerate(sides):
+                sem = sems.at[len(copies)]
+                copies.append(pltpu.make_async_copy(src.at[at], w_all.at[side, :, cols], sem))
     for copy in copies:
         copy.start()
-    for copy in copies[:4]:
-        copy.wait()
-    for k, (far, by) in enumerate(BITS):
-        for e, d in BITS:
-            head = chip_at(z ^ (2 * far + e), y ^ by, x ^ d)
-            cols = pl.ds(pl.multiple_of(head * W, W), W)
-            for j in range(4):
-                block = j ^ k
-                g_all[block * rows : (block + 1) * rows, cols] = g_raw[k, e, d, j]
-    for copy in copies[4:]:
-        copy.wait()
-    total = 0.0
-    for side, at in enumerate((u, 1 - u)):
-        part = g_all[:, pl.ds(pl.multiple_of(at * half, half), half)]
-        total += jnp.dot(part, w_all[side], preferred_element_type=F32)
-    for k in range(4):
-        terms = total[k * rows : (k + 1) * rows]
-        hidden[k] = (t_all[k].astype(F32) + terms).astype(BF16)
-
-
-def order_kernel(where, *refs):
-    pieces, (keep, send, h_all) = refs[:4], refs[4:]
-    z, y, x, u = (where[i] for i in range(4))
-    half = keep.shape[1]
-    for (far, by), ref in zip(BITS, pieces):
-        for e, d in BITS:
-            block = chip_at(z ^ (2 * far + e), y ^ by, x ^ d)
-            from_cols = slice((2 * e + d) * W, (2 * e + d + 1) * W)
-            h_all[:, pl.ds(pl.multiple_of(block * W, W), W)] = ref[:, from_cols]
+    for chip in range(chips):
+        g_all[:, chip * W : (chip + 1) * W] = gated[chip]
+    g_own = g_all[:, pl.ds(pl.multiple_of(u * half, half), half)]
+    g_other = g_all[:, pl.ds(pl.multiple_of((1 - u) * half, half), half)]
+    for group in range(2):
+        for k, (by, bx) in enumerate(PLANE):
+            at = group * len(PLANE) + k
+            for copy in copies[4 * at : 4 * at + 4]:
+                copy.wait()
+            panels = slice(2 * at * W, 2 * (at + 1) * W)
+            total = jnp.dot(g_own, w_all[0, :, panels], preferred_element_type=F32)
+            total += jnp.dot(g_other, w_all[1, :, panels], preferred_element_type=F32)
+            for j in range(2):
+                chip = chip_at(z ^ (2 * group + j), y ^ by, x ^ bx)
+                cols = pl.ds(pl.multiple_of(chip * W, W), W)
+                term = total[:, j * W : (j + 1) * W]
+                h_all[:, cols] = (tokens[:, cols].astype(F32) + term).astype(BF16)
     keep[...] = h_all[:, pl.ds(pl.multiple_of(u * half, half), half)]
     send[...] = h_all[:, pl.ds(pl.multiple_of((1 - u) * half, half), half)]
 
@@ -386,25 +371,23 @@
     high = hop(low, flip(0, 0, 2))
     w_plane, came = heads_in_plane(w_proj, y, x, low)
     low_late = after(low, came)
-    out_row = jnp.concatenate([w_out[None], hop(after(w_out[None], came), to_x)])
-    neg_pair = pair_up(after(neg, came))
     low_x, low_y = hop(low_late, to_x), hop(low_late, to_y)
     low_xy = across(low_x, low_y)
-    high = after(high, out_row, neg_pair)
+    out_low = pair_up(after(w_out[None], came))
+    out_low_x, out_low_y = hop(out_low, to_x), hop(out_low, to_y)
+    high = after(high, low_xy, out_low)
     high_x, high_y = hop(high, to_x), hop(high, to_y)
     high_xy = across(high_x, high_y)
-    out_own = [out_row, hop(after(out_row, high), flip(0, 0, 1))]
     tok = [low, high, low_x, high_x, low_y, high_y, *low_xy, *high_xy]
     w_mine = heads_along_z(after(w_plane, high), z)
-
-    t_rows = after(target_emb.reshape(2, rows, -1), high)
+    w_mine = after(w_mine, high_xy, out_low_x, out_low_y)
+    w_theirs = swap_cores(w_mine)
+    out_high = hop(after(out_low, w_mine), flip(0, 0, 2))
+    out_low = [out_low, out_low_x, out_low_y, *across(*after((out_low_x, out_low_y), w_mine))]
+    t_rows = target_emb.reshape(2, rows, -1)
     t_keep = pick_row(t_rows, u)
-    t_send = swap_cores(pick_row(t_rows, 1 - u))
-    w_mine = after(w_mine, low_xy, high_xy, out_own, t_send)
-    w_theirs = swap_cores(w_mine)
-    neg_far = hop(after(neg_pair, w_mine), flip(0, 0, 2))
-    neg_near = jnp.concatenate([neg_pair, neg_far])
-    neg_x, neg_y = hop(neg_near, to_x), hop(neg_near, to_y)
+    t_send = swap_cores(pick_row(after(t_rows, w_theirs), 1 - u))
+    neg_pair = pair_up(after(neg, w_mine))
 
     def project(pieces):
         count = sum(p.shape[0] for p in pieces)
@@ -424,51 +407,45 @@
         )
 
     gate_query, value_key, marks = project(tok)
-    kv_theirs = swap_cores(after(value_key, neg_far))
+    kv_theirs = swap_cores(value_key)
     (gated,) = call(
         attend_kernel,
         "attend",
-        [((2, 2, 4, rows, W), BF16)],
+        [((CHIPS, rows, W), BF16)],
         [pltpu.VMEM((events, 2 * W), BF16)] * 3
         + [pltpu.VMEM((events, W), BF16), pltpu.SemaphoreType.DMA((4,))],
-        [gate_query, value_key, kv_theirs, marks],
-        4 * "h",
+        [where, gate_query, value_key, kv_theirs, marks],
+        "s" + 4 * "h",
         8 * events * events * W,
     )
-    out_other = [swap_cores(w) for w in after(out_own, gated)]
-    hops = [hop(gated[e, d], flip(0, d, e)) for e, d in BITS[1:]]
-    gated = jnp.stack([gated[0, 0], *hops]).reshape(gated.shape)
-    gated = [gated] + [hop(gated, flip(by, 0, 2 * far)) for far, by in BITS[1:]]
-    neg_x, neg_y = after((neg_x, neg_y), gated)
+    out_high, neg_pair, out_low = after((out_high, neg_pair, out_low), gated)
+    gated = lax.all_to_all(gated, "ctx", 0, 0, tiled=True)
+    out_high_x, out_high_y = hop(out_high, to_x), hop(out_high, to_y)
+    out_high_x, out_high_y = after((out_high_x, out_high_y), gated)
+    out_high = [out_high, out_high_x, out_high_y, *across(out_high_x, out_high_y)]
+    neg_far = hop(after(neg_pair, out_high[0]), flip(0, 0, 2))
+    neg_near = jnp.concatenate([neg_pair, neg_far])
+    neg_near = after(neg_near, out_high)
+    neg_x, neg_y = hop(neg_near, to_x), hop(neg_near, to_y)
+    out_own = [jnp.concatenate(out_low), jnp.concatenate(out_high)]
+    out_other = [swap_cores(panels) for panels in out_own]
     neg_own = [neg_near, neg_x, neg_y, *across(neg_x, neg_y)]
-    (hidden,) = call(
+    h_keep, h_send = call(
         hidden_kernel,
         "hidden",
-        [((4, rows, 4 * W), BF16)],
+        [((rows, half), BF16)] * 2,
         [
-            pltpu.VMEM((4, 2, 2, 4, rows, W), BF16),
-            pltpu.VMEM((4 * rows, model), BF16),
-            pltpu.VMEM((4, rows, 4 * W), BF16),
-            pltpu.VMEM((2, half, 4 * W), BF16),
-            pltpu.SemaphoreType.DMA((28,)),
+            pltpu.VMEM((rows, model), BF16),
+            pltpu.VMEM((rows, model), BF16),
+            pltpu.VMEM((2, half, model), BF16),
+            pltpu.SemaphoreType.DMA((2 * CHIPS,)),
         ],
-        [where, *gated, *out_own, *out_other, low, low_y, high, high_y],
-        "s" + 12 * "h",
-        8 * rows * model * 4 * W,
-    )
-    pieces = [hidden[0]]
-    pieces += [hop(hidden[k], flip(BITS[k][1], 0, 2 * BITS[k][0])) for k in range(1, 4)]
-    neg_own = jnp.concatenate(after(neg_own, hidden))
+        [where, gated, *out_own, *out_other, mine[:, :model]],
+        "sv" + 4 * "h" + "v",
+        2 * rows * model * model,
+    )
+    neg_own = jnp.concatenate(after(neg_own, h_send))
     neg_other = swap_cores(neg_own)
-    h_keep, h_send = call(
-        order_kernel,
-        "order",
-        [((rows, half), BF16)] * 2,
-        [pltpu.VMEM((rows, model), BF16)],
-        [where, *pieces],
-        "svvvv",
-        0,
-    )
     h_theirs = swap_cores(h_send)
     (loss,) = call(
         loss_kernel,

time: 173 us -> 211 us (1.22)
  local copies, waits for them, and re-layouts: 15.9 us -> 31.4 us
  waiting for transfers between devices: 83.4 us -> 96.1 us
  starting transfers between devices: 47.9 us -> 54.4 us
  Pallas kernels: 18 us -> 20.5 us
    ppermute x30 -> x29, waiting for transfers between devices: 77.9 us -> 93.6 us  [hop(): return lax.ppermute(value, 'ctx', perm)]
    unnamed x21 -> x46, local copies, waits for them, and re-layouts: 5.47 us -> 20.6 us
    all_to_all x0 -> x1, starting transfers between devices: none -> 7.32 us  [head_shards(): gated = lax.all_to_all(gated, 'ctx', 0, 0, tiled=True)]
    ppermute x2, waiting for transfers between devices: 5.43 us -> 0.01 us  [heads_along_z(): lax.ppermute(pick_row(heads, e ^ z & 1), ('ctx', 'tp'), perm)]
    ppermute x2, starting transfers between devices: 5.97 us -> 2.26 us  [heads_along_z(): lax.ppermute(pick_row(heads, e ^ z & 1), ('ctx', 'tp'), perm)]
    ppermute x30 -> x29, starting transfers between devices: 41.1 us -> 43.8 us  [hop(): return lax.ppermute(value, 'ctx', perm)]
    ppermute x7, waiting for transfers between devices: 0.06 us -> 2.54 us  [swap_cores(): return lax.ppermute(value, 'tp', SWAP)]
    pallas_call x6 -> x5, Pallas kernels: 18 us -> 20.5 us  [call(): pl.pallas_call(kernel, out_shape=[jax.ShapeDtypeStruct(shape, dtype) for...]
  transfers between devices with their start and end apart: 39 -> 39, of which waited for: 19 -> 19; matrix products, arithmetic and copies ran while one was open for 10% -> 13% of each run, Pallas kernels for 9% -> 9%
where the time goes in v10:
time: 211 us; the launch traced here: 210 us
  waiting for transfers between devices  96.1 us (46%)
  starting transfers between devices  54.4 us (26%)
  local copies, waits for them, and re-layouts  31.4 us (15%)
  Pallas kernels  20.5 us (10%)
  other arithmetic  6.18 us (3%)
    ppermute x29, waiting for transfers between devices, hop(): return lax.ppermute(value, 'ctx', perm)  93.6 us
    ppermute x29, starting transfers between devices, hop(): return lax.ppermute(value, 'ctx', perm)  43.8 us
    unnamed x46, local copies, waits for them, and re-layouts  20.6 us
    pallas_call x5, Pallas kernels, call(): pl.pallas_call(kernel, out_shape=[jax.ShapeDtypeStruct(shape, dtype) for...  20.5 us
    all_to_all x1, starting transfers between devices, head_shards(): gated = lax.all_to_all(gated, 'ctx', 0, 0, tiled=True)  7.32 us
    slice x10, local copies, waits for them, and re-layouts, across(): return [hop(value_x[:half], flip(1, 0)), hop(value_y[half:], flip(0, 1))]  5.42 us
  transfers between devices with their start and end apart: 39, of which 19 were waited for; matrix products, arithmetic and copies ran while one was open for 13% of the time, Pallas kernels for 9%

profile of v10, /device:TPU:0, one launch (start us, length us, event | category | flops | bytes accessed | tf_op | source)
XLA Modules:
  0.0 209.7 jit_solution(9677009519654389640)
XLA Ops:
  1.8 3.1 %collective-permute-start = (bf16[64,2176]{1,0:T(8,128)(2,1)S(1)}, bf16[64,2176]{1,0:T(8,128)(2,1)S(1)}, u32[]{:S(2)}, u32[]{:S(2)}) collective-permute-start(bf16[64,2176]{1,0:T(8,128)(2,1)S(1)} %pad_maximum_fusion.3), channel_id=1, source_target_pairs={{0,8},{2,10},{4,12},{6,14},{8,0},{10,2},{12,4},{14,6},{16,24},{18,... | collective-permute-start | bytes 835592 | tf_op jit(solution)/shard_map/ppermute | solution.py:106
  8.2 3.4 %collective-permute-done = bf16[64,2176]{1,0:T(8,128)(2,1)S(1)} collective-permute-done((bf16[64,2176]{1,0:T(8,128)(2,1)S(1)}, bf16[64,2176]{1,0:T(8,128)(2,1)S(1)}, u32[]{:S(2)}, u32[]{:S(2)}) %collective-permute-start) | collective-permute-done | bytes 278560 | tf_op jit(solution)/shard_map/ppermute | solution.py:106
  15.1 5.8 %collective-permute-done.2 = bf16[2,128,512]{2,1,0:T(8,128)(2,1)S(1)} collective-permute-done((bf16[2,128,512]{2,1,0:T(8,128)(2,1)S(1)}, bf16[2,128,512]{2,1,0:T(8,128)(2,1)S(1)}, u32[]{:S(2)}, u32[]{:S(2)}) %collective-permute-start.2) | collective-permute-done | bytes 262176 | tf_op jit(solution)/shard_map/ppermute | solution.py:106
  20.9 5.1 %collective-permute-done.3 = bf16[2,128,512]{2,1,0:T(8,128)(2,1)S(1)} collective-permute-done((bf16[2,128,512]{2,1,0:T(8,128)(2,1)}, bf16[2,128,512]{2,1,0:T(8,128)(2,1)S(1)}, u32[]{:S(2)}, u32[]{:S(2)}) %collective-permute-start.3) | collective-permute-done | bytes 262176 | tf_op jit(solution)/shard_map/ppermute | solution.py:106
  28.4 2.9 %collective-permute-start.1 = (bf16[128,2176]{1,0:T(8,128)(2,1)S(1)}, bf16[128,2176]{1,0:T(8,128)(2,1)S(1)}, u32[]{:S(2)}, u32[]{:S(2)}) collective-permute-start(bf16[128,2176]{1,0:T(8,128)(2,1)S(1)} %pad_maximum_fusion.1.refs_0_), channel_id=1, source_target_pairs={{0,16},{2,18},{4,20},{6,22},{8,24},{10,26},{12,28},{14,30},{16,0},... | collective-permute-start | bytes 1671176 | tf_op jit(solution)/shard_map/ppermute | solution.py:106
  32.8 5.3 %collective-permute-done.7.refs_4_ = bf16[128,2176]{1,0:T(8,128)(2,1)S(1)} collective-permute-done((bf16[128,2176]{1,0:T(8,128)(2,1)S(1)}, bf16[128,2176]{1,0:T(8,128)(2,1)S(1)}, u32[]{:S(2)}, u32[]{:S(2)}) %collective-permute-start.7) | collective-permute-done | bytes 557088 | tf_op jit(solution)/shard_map/ppermute | solution.py:106
  42.2 3.6 %collective-permute-done.9 = bf16[1,1024,128]{2,1,0:T(8,128)(2,1)S(1)} collective-permute-done((bf16[1,1024,128]{2,1,0:T(8,128)(2,1)}, bf16[1,1024,128]{2,1,0:T(8,128)(2,1)S(1)}, u32[]{:S(2)}, u32[]{:S(2)}) %collective-permute-start.9) | collective-permute-done | bytes 262176 | tf_op jit(solution)/shard_map/ppermute | solution.py:106
  46.6 6.2 %collective-permute-done.1.refs_1_ = bf16[128,2176]{1,0:T(8,128)(2,1)S(1)} collective-permute-done((bf16[128,2176]{1,0:T(8,128)(2,1)S(1)}, bf16[128,2176]{1,0:T(8,128)(2,1)S(1)}, u32[]{:S(2)}, u32[]{:S(2)}) %collective-permute-start.1) | collective-permute-done | bytes 557088 | tf_op jit(solution)/shard_map/ppermute | solution.py:106
  59.4 9.5 %collective-permute-done.11.refs_5_ = bf16[128,2176]{1,0:T(8,128)(2,1)S(1)} collective-permute-done((bf16[128,2176]{1,0:T(8,128)(2,1)S(1)}, bf16[128,2176]{1,0:T(8,128)(2,1)S(1)}, u32[]{:S(2)}, u32[]{:S(2)}) %collective-permute-start.11) | collective-permute-done | bytes 557088 | tf_op jit(solution)/shard_map/ppermute | solution.py:106
  74.9 2.7 %maximum_select_fusion = bf16[2,4,128,512]{3,2,1,0:T(8,128)(2,1)} fusion(bf16[1,4,128,512]{3,2,1,0:T(8,128)(2,1)} %bitcast.22, bf16[1,4,128,512]{3,2,1,0:T(8,128)(2,1)} %bitcast.20, pred[]{:T(512)S(6)} %eq.11), kind=kLoop, calls=%fused_computation | loop fusion | flops 1572864 | bytes 2097153 | tf_op jit(solution)/shard_map/jit(_where)/select_n | solution.py:156
  82.7 3.0 %collective-permute-done.13.refs_9_ = bf16[64,2176]{1,0:T(8,128)(2,1)} collective-permute-done((bf16[64,2176]{1,0:T(8,128)(2,1)}, bf16[64,2176]{1,0:T(8,128)(2,1)}, u32[]{:S(2)}, u32[]{:S(2)}) %collective-permute-start.13) | collective-permute-done | bytes 278560 | tf_op jit(solution)/shard_map/ppermute | solution.py:106
  87.6 2.6 %collective-permute-start.20 = (bf16[2,1024,128]{2,1,0:T(8,128)(2,1)}, bf16[2,1024,128]{2,1,0:T(8,128)(2,1)}, u32[]{:S(2)}, u32[]{:S(2)}) collective-permute-start(bf16[2,1024,128]{2,1,0:T(8,128)(2,1)} %constant_dynamic-update-slice_fusion), channel_id=1, source_target_pairs={{0,16},{2,18},{4,20},{6,22},{8,24},{10,26},{12,28},{14,30},{16,0},... | collective-permute-start | bytes 1572872 | tf_op jit(solution)/shard_map/ppermute | solution.py:106
  93.3 4.9 %project.1 = (bf16[1024,256]{1,0:T(8,128)(2,1)S(1)}, bf16[1024,256]{1,0:T(8,128)(2,1)S(1)}, bf16[1024,128]{1,0:T(8,128)(2,1)S(1)}) custom-call(s32[4]{0:T(128)S(1)} %pad_add_fusion.where, bf16[128,2176]{1,0:T(8,128)(2,1)S(1)} %pad_maximum_fusion.1.refs_0_, bf16[128,2176]{1,0:T(8,128)(2,1)S(1)} %copy-done.4, ...), custom_call_target="tpu_custom_call" | custom-call | flops 2147483648 | bytes 6553616 | tf_op jit(solution)/shard_map/project/pallas_call | solution.py:318
  98.5 3.4 %collective-permute-start.21 = (bf16[64,1152]{1,0:T(8,128)(2,1)S(1)}, bf16[64,1152]{1,0:T(8,128)(2,1)S(1)}, u32[]{:S(2)}, u32[]{:S(2)}) collective-permute-start(bf16[64,1152]{1,0:T(8,128)(2,1)S(1)} %fusion.1), channel_id=1, source_target_pairs={{0,8},{2,10},{4,12},{6,14},{8,0},{10,2},{12,4},{14,6},{16,24},{18,... | collective-permute-start | bytes 442376 | tf_op jit(solution)/shard_map/ppermute | solution.py:106
  105.9 8.6 %collective-permute-done.21 = bf16[64,1152]{1,0:T(8,128)(2,1)S(1)} collective-permute-done((bf16[64,1152]{1,0:T(8,128)(2,1)S(1)}, bf16[64,1152]{1,0:T(8,128)(2,1)S(1)}, u32[]{:S(2)}, u32[]{:S(2)}) %collective-permute-start.21) | collective-permute-done | bytes 147488 | tf_op jit(solution)/shard_map/ppermute | solution.py:106
  115.3 4.7 %attend.1 = bf16[16,64,128]{2,1,0:T(8,128)(2,1)} custom-call(s32[4]{0:T(128)S(1)} %pad_add_fusion.where, bf16[1024,256]{1,0:T(8,128)(2,1)S(1)} %get-tuple-element.45.gq_hbm, bf16[1024,256]{1,0:T(8,128)(2,1)S(1)} %get-tuple-element.46.own_hbm, bf16[1024,256]{1,0:T(8,128)(2,1)S(1)} %collective-permute-done.19.other_hbm, ...), custom_call_target="tpu_custom_call" | custom-call | flops 1073741824 | bytes 1835024 | tf_op jit(solution)/shard_map/attend/pallas_call | solution.py:318
  120.0 7.3 %all-to-all-start = ((bf16[16,64,128]{2,1,0:T(8,128)(2,1)}), bf16[16,64,128]{2,1,0:T(8,128)(2,1)S(1)}, u32[]{:S(2)}, u32[]{:S(2)}) async-start(bf16[16,64,128]{2,1,0:T(8,128)(2,1)} %attend.1), calls=%async_computation | async-start | bytes 524288 | tf_op jit(solution)/shard_map/all_to_all | solution.py:422
  138.2 5.2 %collective-permute-done.25 = bf16[2,1024,128]{2,1,0:T(8,128)(2,1)} collective-permute-done((bf16[2,1024,128]{2,1,0:T(8,128)(2,1)}, bf16[2,1024,128]{2,1,0:T(8,128)(2,1)}, u32[]{:S(2)}, u32[]{:S(2)}) %collective-permute-start.25) | collective-permute-done | bytes 524320 | tf_op jit(solution)/shard_map/ppermute | solution.py:106
  152.3 4.3 %collective-permute-done.27 = bf16[1,1024,128]{2,1,0:T(8,128)(2,1)S(1)} collective-permute-done((bf16[1,1024,128]{2,1,0:T(8,128)(2,1)S(1)}, bf16[1,1024,128]{2,1,0:T(8,128)(2,1)S(1)}, u32[]{:S(2)}, u32[]{:S(2)}) %collective-permute-start.27) | collective-permute-done | bytes 262176 | tf_op jit(solution)/shard_map/ppermute | solution.py:106
  156.7 2.6 %collective-permute-start.32 = (bf16[128,1152]{1,0:T(8,128)(2,1)S(1)}, bf16[128,1152]{1,0:T(8,128)(2,1)S(1)}, u32[]{:S(2)}, u32[]{:S(2)}) collective-permute-start(bf16[128,1152]{1,0:T(8,128)(2,1)S(1)} %copy-done.9), channel_id=1, source_target_pairs={{0,16},{2,18},{4,20},{6,22},{8,24},{10,26},{12,28},{14,30},{16,0},... | collective-permute-start | bytes 884744 | tf_op jit(solution)/shard_map/ppermute | solution.py:106
  159.3 14.0 %collective-permute-done.32 = bf16[128,1152]{1,0:T(8,128)(2,1)S(1)} collective-permute-done((bf16[128,1152]{1,0:T(8,128)(2,1)S(1)}, bf16[128,1152]{1,0:T(8,128)(2,1)S(1)}, u32[]{:S(2)}, u32[]{:S(2)}) %collective-permute-start.32) | collective-permute-done | bytes 294944 | tf_op jit(solution)/shard_map/ppermute | solution.py:106
  175.9 12.5 %collective-permute-done.34 = bf16[256,1152]{1,0:T(8,128)(2,1)S(1)} collective-permute-done((bf16[256,1152]{1,0:T(8,128)(2,1)S(1)}, bf16[256,1152]{1,0:T(8,128)(2,1)S(1)}, u32[]{:S(2)}, u32[]{:S(2)}) %collective-permute-start.34) | collective-permute-done | bytes 589856 | tf_op jit(solution)/shard_map/ppermute | solution.py:106
  193.7 5.5 %hidden.1 = (bf16[64,1024]{1,0:T(8,128)(2,1)S(1)}, bf16[64,1024]{1,0:T(8,128)(2,1)S(1)}) custom-call(s32[4]{0:T(128)S(1)} %pad_add_fusion.where, bf16[16,64,128]{2,1,0:T(8,128)(2,1)S(1)} %all-to-all-done.gated, bf16[8,1024,128]{2,1,0:T(8,128)(2,1)} %constant_dynamic-update-slice_fusion.2.low, ...), custom_call_target="tpu_custom_call" | custom-call | flops 536870912 | bytes 8912912 | tf_op jit(solution)/shard_map/hidden/pallas_call | solution.py:318
  204.3 4.1 %loss.1 = f32[1,64]{1,0:T(1,128)} custom-call(bf16[64,1024]{1,0:T(8,128)(2,1)S(1)} %get-tuple-element.60.h_keep.keep, bf16[64,1024]{1,0:T(8,128)(2,1)S(1)} %get-tuple-element.61.h_send, bf16[64,1024]{1,0:T(8,128)(2,1)S(1)} %dynamic-slice_bitcast_fusion.3.t_keep, bf16[64,1024]{1,0:T(8,128)(2,1)S(1)} %collective-permute-done.31.t_send, ...), custom_call_target="tpu_custom_call" | custom-call | flops 268435456 | bytes 5243136 | tf_op jit(solution)/shard_map/loss/pallas_call | solution.py:318
  (153 shorter events, 78.2 us)
Async XLA Ops:
  28.4 24.4 %collective-permute-start.1 = (bf16[128,2176]{1,0:T(8,128)(2,1)S(1)}, bf16[128,2176]{1,0:T(8,128)(2,1)S(1)}, u32[]{:S(2)}, u32[]{:S(2)}) collective-permute-start(bf16[128,2176]{1,0:T(8,128)(2,1)S(1)} %pad_maximum_fusion.1.refs_0_), channel_id=1, source_target_pairs={{0,16},{2,18},{4,20},{6,22},{8,24},{10,26},{12,28},{14,30},{16,0},... | collective-permute-start | bytes 1671176 | tf_op jit(solution)/shard_map/ppermute | solution.py:106
  31.2 14.6 %collective-permute-start.9 = (bf16[1,1024,128]{2,1,0:T(8,128)(2,1)}, bf16[1,1024,128]{2,1,0:T(8,128)(2,1)S(1)}, u32[]{:S(2)}, u32[]{:S(2)}) collective-permute-start(bf16[1,1024,128]{2,1,0:T(8,128)(2,1)} %bitcast.55), channel_id=1, source_target_pairs={{0,8},{2,10},{4,12},{6,14},{8,0},{10,2},{12,4},{14,6},{16,24},{18,... | collective-permute-start | bytes 786440 | tf_op jit(solution)/shard_map/ppermute | solution.py:106
  38.2 14.6 %collective-permute-start.8 = (bf16[64,2176]{1,0:T(8,128)(2,1)S(1)}, bf16[64,2176]{1,0:T(8,128)(2,1)S(1)}, u32[]{:S(2)}, u32[]{:S(2)}) collective-permute-start(bf16[64,2176]{1,0:T(8,128)(2,1)S(1)} %slice.41), channel_id=1, source_target_pairs={{0,2},{2,0},{4,6},{6,4},{8,10},{10,8},{12,14},{14,12},{16,18},{18,... | collective-permute-start | bytes 835592 | tf_op jit(solution)/shard_map/ppermute | solution.py:106
  40.0 12.8 %collective-permute-start.6 = (bf16[64,2176]{1,0:T(8,128)(2,1)S(1)}, bf16[64,2176]{1,0:T(8,128)(2,1)S(1)}, u32[]{:S(2)}, u32[]{:S(2)}) collective-permute-start(bf16[64,2176]{1,0:T(8,128)(2,1)S(1)} %slice.40), channel_id=1, source_target_pairs={{0,4},{2,6},{4,0},{6,2},{8,12},{10,14},{12,8},{14,10},{16,20},{18,... | collective-permute-start | bytes 835592 | tf_op jit(solution)/shard_map/ppermute | solution.py:106
  53.6 15.3 %collective-permute-start.11 = (bf16[128,2176]{1,0:T(8,128)(2,1)S(1)}, bf16[128,2176]{1,0:T(8,128)(2,1)S(1)}, u32[]{:S(2)}, u32[]{:S(2)}) collective-permute-start(bf16[128,2176]{1,0:T(8,128)(2,1)S(1)} %collective-permute-done.1.refs_1_), channel_id=1, source_target_pairs={{0,4},{2,6},{4,0},{6,2},{8,12},{10,14},{12,8},{14,10},{16,20},{18,... | collective-permute-start | bytes 1671176 | tf_op jit(solution)/shard_map/ppermute | solution.py:106
  55.1 15.8 %collective-permute-start.10 = (bf16[128,2176]{1,0:T(8,128)(2,1)S(1)}, bf16[128,2176]{1,0:T(8,128)(2,1)S(1)}, u32[]{:S(2)}, u32[]{:S(2)}) collective-permute-start(bf16[128,2176]{1,0:T(8,128)(2,1)S(1)} %collective-permute-done.1.refs_1_), channel_id=1, source_target_pairs={{0,2},{2,0},{4,6},{6,4},{8,10},{10,8},{12,14},{14,12},{16,18},{18,... | collective-permute-start | bytes 1671176 | tf_op jit(solution)/shard_map/ppermute | solution.py:106
  56.6 16.5 %collective-permute-start.14 = (bf16[4,128,512]{2,1,0:T(8,128)(2,1)S(1)}, bf16[4,128,512]{2,1,0:T(8,128)(2,1)}, u32[]{:S(2)}, u32[]{:S(2)}) collective-permute-start(bf16[4,128,512]{2,1,0:T(8,128)(2,1)S(1)} %get-tuple-element.78), channel_id=1, source_target_pairs={{0,0},{1,16},{2,2},{3,18},{4,4},{5,20},{6,6},{7,22},{8,8},{9,24},{... | collective-permute-start | bytes 1572872 | tf_op jit(solution)/shard_map/ppermute | solution.py:155
  58.2 16.7 %collective-permute-start.15 = (bf16[4,128,512]{2,1,0:T(8,128)(2,1)}, bf16[4,128,512]{2,1,0:T(8,128)(2,1)}, u32[]{:S(2)}, u32[]{:S(2)}) collective-permute-start(bf16[4,128,512]{2,1,0:T(8,128)(2,1)} %get-tuple-element.79), channel_id=1, source_target_pairs={{0,8},{1,24},{2,10},{3,26},{4,12},{5,28},{6,14},{7,30},{8,0},{9,16... | collective-permute-start | bytes 1572872 | tf_op jit(solution)/shard_map/ppermute | solution.py:155
  58.9 21.3 %collective-permute-start.17 = (bf16[2,1024,128]{2,1,0:T(8,128)(2,1)}, bf16[2,1024,128]{2,1,0:T(8,128)(2,1)}, u32[]{:S(2)}, u32[]{:S(2)}) collective-permute-start(bf16[2,1024,128]{2,1,0:T(8,128)(2,1)} %constant_dynamic-update-slice_fusion), channel_id=1, source_target_pairs={{0,4},{2,6},{4,0},{6,2},{8,12},{10,14},{12,8},{14,10},{16,20},{18,... | collective-permute-start | bytes 1572872 | tf_op jit(solution)/shard_map/ppermute | solution.py:106
  68.9 13.8 %collective-permute-start.16 = (bf16[2,1024,128]{2,1,0:T(8,128)(2,1)}, bf16[2,1024,128]{2,1,0:T(8,128)(2,1)}, u32[]{:S(2)}, u32[]{:S(2)}) collective-permute-start(bf16[2,1024,128]{2,1,0:T(8,128)(2,1)} %constant_dynamic-update-slice_fusion), channel_id=1, source_target_pairs={{0,2},{2,0},{4,6},{6,4},{8,10},{10,8},{12,14},{14,12},{16,18},{18,... | collective-permute-start | bytes 1572872 | tf_op jit(solution)/shard_map/ppermute | solution.py:106
  70.9 14.8 %collective-permute-start.13 = (bf16[64,2176]{1,0:T(8,128)(2,1)}, bf16[64,2176]{1,0:T(8,128)(2,1)}, u32[]{:S(2)}, u32[]{:S(2)}) collective-permute-start(bf16[64,2176]{1,0:T(8,128)(2,1)} %slice.43), channel_id=1, source_target_pairs={{0,2},{2,0},{4,6},{6,4},{8,10},{10,8},{12,14},{14,12},{16,18},{18,... | collective-permute-start | bytes 835592 | tf_op jit(solution)/shard_map/ppermute | solution.py:106
  87.6 39.8 %collective-permute-start.20 = (bf16[2,1024,128]{2,1,0:T(8,128)(2,1)}, bf16[2,1024,128]{2,1,0:T(8,128)(2,1)}, u32[]{:S(2)}, u32[]{:S(2)}) collective-permute-start(bf16[2,1024,128]{2,1,0:T(8,128)(2,1)} %constant_dynamic-update-slice_fusion), channel_id=1, source_target_pairs={{0,16},{2,18},{4,20},{6,22},{8,24},{10,26},{12,28},{14,30},{16,0},... | collective-permute-start | bytes 1572872 | tf_op jit(solution)/shard_map/ppermute | solution.py:106
  98.2 17.1 %collective-permute-start.19 = (bf16[1024,256]{1,0:T(8,128)(2,1)S(1)}, bf16[1024,256]{1,0:T(8,128)(2,1)S(1)}, u32[]{:S(2)}, u32[]{:S(2)}) collective-permute-start(bf16[1024,256]{1,0:T(8,128)(2,1)S(1)} %get-tuple-element.46.own_hbm), channel_id=1, source_target_pairs={{0,1},{1,0},{2,3},{3,2},{4,5},{5,4},{6,7},{7,6},{8,9},{9,8},{10,11... | collective-permute-start | bytes 1572872 | tf_op jit(solution)/shard_map/ppermute | solution.py:110
  98.5 16.1 %collective-permute-start.21 = (bf16[64,1152]{1,0:T(8,128)(2,1)S(1)}, bf16[64,1152]{1,0:T(8,128)(2,1)S(1)}, u32[]{:S(2)}, u32[]{:S(2)}) collective-permute-start(bf16[64,1152]{1,0:T(8,128)(2,1)S(1)} %fusion.1), channel_id=1, source_target_pairs={{0,8},{2,10},{4,12},{6,14},{8,0},{10,2},{12,4},{14,6},{16,24},{18,... | collective-permute-start | bytes 442376 | tf_op jit(solution)/shard_map/ppermute | solution.py:106
  103.8 23.5 %collective-permute-start.23 = (bf16[1,1024,128]{2,1,0:T(8,128)(2,1)S(1)}, bf16[1,1024,128]{2,1,0:T(8,128)(2,1)S(1)}, u32[]{:S(2)}, u32[]{:S(2)}) collective-permute-start(bf16[1,1024,128]{2,1,0:T(8,128)(2,1)S(1)} %slice.35), channel_id=1, source_target_pairs={{0,2},{2,0},{4,6},{6,4},{8,10},{10,8},{12,14},{14,12},{16,18},{18,... | collective-permute-start | bytes 786440 | tf_op jit(solution)/shard_map/ppermute | solution.py:106
  104.4 22.9 %collective-permute-start.22 = (bf16[1,1024,128]{2,1,0:T(8,128)(2,1)S(1)}, bf16[1,1024,128]{2,1,0:T(8,128)(2,1)S(1)}, u32[]{:S(2)}, u32[]{:S(2)}) collective-permute-start(bf16[1,1024,128]{2,1,0:T(8,128)(2,1)S(1)} %slice.34), channel_id=1, source_target_pairs={{0,4},{2,6},{4,0},{6,2},{8,12},{10,14},{12,8},{14,10},{16,20},{18,... | collective-permute-start | bytes 786440 | tf_op jit(solution)/shard_map/ppermute | solution.py:106
  120.0 18.2 %all-to-all-start = ((bf16[16,64,128]{2,1,0:T(8,128)(2,1)}), bf16[16,64,128]{2,1,0:T(8,128)(2,1)S(1)}, u32[]{:S(2)}, u32[]{:S(2)}) async-start(bf16[16,64,128]{2,1,0:T(8,128)(2,1)} %attend.1), calls=%async_computation | async-start | bytes 524288 | tf_op jit(solution)/shard_map/all_to_all | solution.py:422
  127.4 16.1 %collective-permute-start.25 = (bf16[2,1024,128]{2,1,0:T(8,128)(2,1)}, bf16[2,1024,128]{2,1,0:T(8,128)(2,1)}, u32[]{:S(2)}, u32[]{:S(2)}) collective-permute-start(bf16[2,1024,128]{2,1,0:T(8,128)(2,1)} %collective-permute-done.20), channel_id=1, source_target_pairs={{0,4},{2,6},{4,0},{6,2},{8,12},{10,14},{12,8},{14,10},{16,20},{18,... | collective-permute-start | bytes 1572872 | tf_op jit(solution)/shard_map/ppermute | solution.py:106
  129.3 15.0 %collective-permute-start.24 = (bf16[2,1024,128]{2,1,0:T(8,128)(2,1)}, bf16[2,1024,128]{2,1,0:T(8,128)(2,1)}, u32[]{:S(2)}, u32[]{:S(2)}) collective-permute-start(bf16[2,1024,128]{2,1,0:T(8,128)(2,1)} %collective-permute-done.20), channel_id=1, source_target_pairs={{0,2},{2,0},{4,6},{6,4},{8,10},{10,8},{12,14},{14,12},{16,18},{18,... | collective-permute-start | bytes 1572872 | tf_op jit(solution)/shard_map/ppermute | solution.py:106
  146.8 44.1 %collective-permute-start.28 = (bf16[8,1024,128]{2,1,0:T(8,128)(2,1)}, bf16[8,1024,128]{2,1,0:T(8,128)(2,1)S(1)}, u32[]{:S(2)}, u32[]{:S(2)}) collective-permute-start(bf16[8,1024,128]{2,1,0:T(8,128)(2,1)} %constant_dynamic-update-slice_fusion.2.low), channel_id=1, source_target_pairs={{0,1},{1,0},{2,3},{3,2},{4,5},{5,4},{6,7},{7,6},{8,9},{9,8},{10,11... | collective-permute-start | bytes 6291464 | tf_op jit(solution)/shard_map/ppermute | solution.py:110
  156.6 34.3 %collective-permute-start.29 = (bf16[8,1024,128]{2,1,0:T(8,128)(2,1)S(1)}, bf16[8,1024,128]{2,1,0:T(8,128)(2,1)S(1)}, u32[]{:S(2)}, u32[]{:S(2)}) collective-permute-start(bf16[8,1024,128]{2,1,0:T(8,128)(2,1)S(1)} %constant_dynamic-update-slice_fusion.7.high), channel_id=1, source_target_pairs={{0,1},{1,0},{2,3},{3,2},{4,5},{5,4},{6,7},{7,6},{8,9},{9,8},{10,11... | collective-permute-start | bytes 6291464 | tf_op jit(solution)/shard_map/ppermute | solution.py:110
  156.7 16.6 %collective-permute-start.32 = (bf16[128,1152]{1,0:T(8,128)(2,1)S(1)}, bf16[128,1152]{1,0:T(8,128)(2,1)S(1)}, u32[]{:S(2)}, u32[]{:S(2)}) collective-permute-start(bf16[128,1152]{1,0:T(8,128)(2,1)S(1)} %copy-done.9), channel_id=1, source_target_pairs={{0,16},{2,18},{4,20},{6,22},{8,24},{10,26},{12,28},{14,30},{16,0},... | collective-permute-start | bytes 884744 | tf_op jit(solution)/shard_map/ppermute | solution.py:106
  173.4 14.9 %collective-permute-start.34 = (bf16[256,1152]{1,0:T(8,128)(2,1)S(1)}, bf16[256,1152]{1,0:T(8,128)(2,1)S(1)}, u32[]{:S(2)}, u32[]{:S(2)}) collective-permute-start(bf16[256,1152]{1,0:T(8,128)(2,1)S(1)} %pad_maximum_fusion), channel_id=1, source_target_pairs={{0,4},{2,6},{4,0},{6,2},{8,12},{10,14},{12,8},{14,10},{16,20},{18,... | collective-permute-start | bytes 1769480 | tf_op jit(solution)/shard_map/ppermute | solution.py:106
  174.8 15.0 %collective-permute-start.33 = (bf16[256,1152]{1,0:T(8,128)(2,1)S(1)}, bf16[256,1152]{1,0:T(8,128)(2,1)S(1)}, u32[]{:S(2)}, u32[]{:S(2)}) collective-permute-start(bf16[256,1152]{1,0:T(8,128)(2,1)S(1)} %pad_maximum_fusion), channel_id=1, source_target_pairs={{0,2},{2,0},{4,6},{6,4},{8,10},{10,8},{12,14},{14,12},{16,18},{18,... | collective-permute-start | bytes 1769480 | tf_op jit(solution)/shard_map/ppermute | solution.py:106
  (31 other events, 236.8 us)

commit v11 on v7

--- a/solution.py
+++ b/solution.py
@@ -122,35 +122,19 @@
     return jnp.concatenate([own, hop(own, flip(0, 0, 1))])
 
 
-def relay_pairs(pair, z):
-    inner, outer = [], []
-    for c in range(CHIPS):
-        if coords(c)[0] in (1, 2):
-            inner.append((c, relative_chip(c, 0, 0, 3)))
-            outer.append((c, relative_chip(c, 0, 0, 1)))
-    met = hop(pair, inner)
-    return met, lambda met: jnp.where((z == 1) | (z == 2), met, hop(met, outer))
-
-
 def across(value_x, value_y):
     half = value_x.shape[0] // 2
     return [hop(value_x[:half], flip(1, 0)), hop(value_y[half:], flip(0, 1))]
 
 
 def heads_in_plane(w_proj, y, x):
-    plane = NY * NX
-    heads = w_proj.reshape(-1, 4, 2, plane, W).transpose(3, 2, 0, 1, 4)
-    heads = heads.reshape(plane, 2, -1, 4 * W)
-    out = jnp.zeros((2, plane, *heads.shape[2:]), heads.dtype)
-    came = []
-    for by, bx in PLANE:
-        spot = (y ^ by) * NX + (x ^ bx)
-        piece = pick_row(heads, spot)
-        if (by, bx) != (0, 0):
-            piece = hop(piece, flip(by, bx))
-            came.append(piece)
-        out = lax.dynamic_update_slice_in_dim(out, piece[:, None], spot, 1)
-    return out, came
+    heads = w_proj.reshape(-1, 4, 2, NY, NX, W).transpose(4, 3, 2, 0, 1, 5)
+    heads = heads.reshape(NX, NY, 2, -1, 4 * W)
+    kept, came = pick_row(heads, x), hop(pick_row(heads, x ^ 1), flip(0, 1))
+    lined = jnp.where(x == 0, jnp.stack([kept, came], 1), jnp.stack([came, kept], 1))
+    kept, came = pick_row(lined, y), hop(pick_row(lined, y ^ 1), flip(1, 0))
+    whole = jnp.where(y == 0, jnp.stack([kept, came]), jnp.stack([came, kept]))
+    return whole.transpose(2, 0, 1, 3, 4).reshape(2, NY * NX, *whole.shape[3:])
 
 
 def heads_along_z(heads, z):
@@ -213,7 +197,14 @@
     return pick.astype(BF16)
 
 
-def attend_kernel(gate_query, kv_own, kv_other, marks, gated):
+def attend_kernel(gq_hbm, own_hbm, other_hbm, marks_hbm, gated, gate_query, own, other, marks, sems):
+    sources = (gq_hbm, own_hbm, other_hbm, marks_hbm)
+    run_copies(
+        [
+            pltpu.make_async_copy(src, dst, sems.at[i])
+            for i, (src, dst) in enumerate(zip(sources, (gate_query, own, other, marks)))
+        ]
+    )
     pick = pick_columns({0: 128.0, 1: 1.0}, {2: 128.0, 3: 1.0})
     piece = gated.shape[2]
     tile = NZ * piece
@@ -223,7 +214,7 @@
         query = gate_query[span, W:]
         q_pos = lax.dot_general(marks[span, :], pick, ACROSS, preferred_element_type=F32)[:, :1]
         attn = jnp.zeros((tile, W), F32)
-        for side, kv in enumerate((kv_own, kv_other)):
+        for side, kv in enumerate((own, other)):
             scores = lax.dot_general(
                 query, kv[:, W:], ACROSS, preferred_element_type=F32
             ) * W ** (-0.5)
@@ -238,35 +229,34 @@
 
 def hidden_kernel(where, *refs):
     n = len(PLANE)
-    gated, w_own, w_other, tok = refs[: n + 1], refs[n + 1 : n + 3], refs[n + 3 : n + 5], refs[n + 5 : -5]
-    hidden, g_all, t_all, w_all, sems = refs[-5:]
+    gated, w_own, w_other, tok = refs[:n], refs[n : n + 2], refs[n + 2 : n + 4], refs[n + 4 : 2 * n + 4]
+    hidden, g_raw, g_all, t_all, w_all, sems = refs[2 * n + 4 :]
     z, y, x, u = (where[i] for i in range(4))
     c = chip_at(z, y, x)
     rows = hidden.shape[1]
     half = w_all.shape[1]
-    inner = ((z + 1) // 2) % 2
-    copies = []
+    copies = [(src, g_raw.at[k]) for k, src in enumerate(gated)]
     for s in range(NZ):
         cols = pl.ds(s * W, W)
         for side, src in enumerate((w_own, w_other)):
-            panel = src[0].at[s] if s < 2 else src[1].at[(s % 2) ^ inner]
-            copies.append((panel, w_all.at[side, :, cols]))
+            copies.append((src[s // 2].at[s % 2], w_all.at[side, :, cols]))
         block = relative_chip(c, 0, 0, s)
         from_cols = pl.ds(pl.multiple_of(block * W, W), W)
         for k in range(n):
             copies.append((tok[k].at[pl.ds(0, rows), from_cols], t_all.at[k, :, cols]))
-    copies = [pltpu.make_async_copy(a, b, sems.at[i]) for i, (a, b) in enumerate(copies)]
+    copies = [pltpu.make_async_copy(src, dst, sems.at[i]) for i, (src, dst) in enumerate(copies)]
     for copy in copies:
         copy.start()
+    for copy in copies[:n]:
+        copy.wait()
     for k, (by, bx) in enumerate(PLANE):
         for s in range(NZ):
             head = relative_chip(c, by, bx, s)
             cols = pl.ds(pl.multiple_of(head * W, W), W)
-            for j, (jy, jx) in enumerate(PLANE):
-                block = (jy ^ by) * NX + (jx ^ bx)
-                piece = gated[k][s, j] if k < n - 1 else gated[k + s // 2][s % 2, j]
-                g_all[block * rows : (block + 1) * rows, cols] = piece
-    for copy in copies:
+            for j in range(n):
+                block = j ^ k
+                g_all[block * rows : (block + 1) * rows, cols] = g_raw[k, s, j]
+    for copy in copies[n:]:
         copy.wait()
     total = 0.0
     for side, at in enumerate((u, 1 - u)):
@@ -387,26 +377,25 @@
 
     to_x, to_y = flip(0, 1), flip(1, 0)
     high = hop(low, flip(0, 0, 2))
-    w_plane, came = heads_in_plane(w_proj, y, x)
-    low = after(low, came[:2])
+    w_plane = heads_in_plane(w_proj, y, x)
     low_x, low_y = hop(low, to_x), hop(low, to_y)
     low_xy = across(low_x, low_y)
-    w_plane = after(w_plane, high)
     high_x, high_y = hop(high, to_x), hop(high, to_y)
     high_xy = across(high_x, high_y)
     tok = [low, high, low_x, high_x, low_y, high_y, *low_xy, *high_xy]
-    w_mine = after(heads_along_z(w_plane, z), low_xy, high_xy)
+    w_mine = heads_along_z(after(w_plane, high), z)
+    out_pair = pair_up(after(w_out[None], high))
+    w_mine = after(w_mine, low_xy, high_xy, out_pair)
     w_theirs = swap_cores(w_mine)
-
-    t_rows = after(target_emb.reshape(2, rows, -1), high)
-    t_keep = pick_row(t_rows, u)
-    t_send = swap_cores(pick_row(t_rows, 1 - u))
+    out_own = [out_pair, hop(after(out_pair, w_mine), flip(0, 0, 2))]
+
     own_ids = lax.dynamic_slice_in_dim(neg_ids, c * negs, negs, 0)
     norms = jnp.sum(jnp.square(neg_emb.astype(F32)), axis=1)
     neg = with_marks(neg_emb, float_parts(norms) + whole_parts(own_ids, 256))
-    neg_pair = pair_up(after(neg, w_mine, t_send))
-    neg_met, neg_far = relay_pairs(after(neg_pair, w_theirs), z)
-    out_pair = pair_up(after(w_out[None], neg_pair))
+    neg_pair = pair_up(after(neg, out_pair))
+    t_rows = after(target_emb.reshape(2, rows, -1), w_theirs)
+    t_keep = pick_row(t_rows, u)
+    t_send = swap_cores(pick_row(t_rows, 1 - u))
 
     def project(pieces):
         count = sum(p.shape[0] for p in pieces)
@@ -422,47 +411,47 @@
             ],
             [where, *pieces, w_mine, w_theirs],
             "s" + (len(pieces) + 2) * "h",
-            2 * count * model * 4 * W,
+            20 * 2 * count * model * 4 * W,
         )
 
     gate_query, value_key, marks = project(tok)
     kv_theirs = swap_cores(value_key)
-    out_met, out_far = relay_pairs(after(out_pair, neg_met, value_key), z)
-    neg_near = jnp.concatenate([neg_pair, neg_far(after(neg_met, value_key))])
-    neg_row = jnp.concatenate([neg_near, hop(neg_near, to_x)])
-    neg_own = [neg_row, hop(neg_row, to_y)]
+    out_pair_theirs = swap_cores(after(out_pair, value_key))
     (gated,) = call(
         attend_kernel,
         "attend",
         [((NZ, plane, rows, W), BF16)],
-        [],
+        [pltpu.VMEM((events, 2 * W), BF16)] * 3
+        + [pltpu.VMEM((events, W), BF16), pltpu.SemaphoreType.DMA((4,))],
         [gate_query, value_key, kv_theirs, marks],
-        4 * "v",
-        8 * events * events * W,
-    )
-    gated = after(gated, neg_near)
+        4 * "h",
+        0,
+    )
+    out_own, out_pair_theirs, gated = lax.optimization_barrier((out_own, out_pair_theirs, gated))
     gated = jnp.stack([gated[0]] + [hop(gated[s], flip(0, 0, s)) for s in range(1, NZ)])
-    out_met = after(out_met, gated)
-    gated = [gated, hop(gated, to_x), hop(gated, to_y)]
-    gated += across(gated[1], gated[2])
-    out_own = [after(out_pair, gated), after(out_far(out_met), gated)]
-    out_other = [swap_cores(w) for w in out_own]
+    neg_far = hop(after(neg_pair, gated), flip(0, 0, 2))
+    out_other = [out_pair_theirs, swap_cores(after(out_own[1], gated))]
+    gated = [gated] + [hop(gated, flip(by, bx)) for by, bx in PLANE[1:]]
+    neg_near = after(jnp.concatenate([neg_pair, neg_far]), gated, out_other)
+    neg_x, neg_y = hop(neg_near, to_x), hop(neg_near, to_y)
     (hidden,) = call(
         hidden_kernel,
         "hidden",
         [((plane, rows, NZ * W), BF16)],
         [
+            pltpu.VMEM((plane, NZ, plane, rows, W), BF16),
             pltpu.VMEM((plane * rows, model), BF16),
             pltpu.VMEM((plane, rows, NZ * W), BF16),
             pltpu.VMEM((2, half, NZ * W), BF16),
-            pltpu.SemaphoreType.DMA((NZ * (2 + plane),)),
+            pltpu.SemaphoreType.DMA((28,)),
         ],
-        [where, *gated, *out_own, *out_other, *tok[:7:2]],
-        "s" + 5 * "v" + 8 * "h",
+        [where, *gated, *out_own, *out_other, low, low_x, low_y, low_xy[0]],
+        "s" + 12 * "h",
         2 * plane * rows * model * NZ * W,
     )
     pieces = [hidden[0]] + [hop(hidden[k], flip(*PLANE[k])) for k in range(1, plane)]
-    neg_own = jnp.concatenate(after(neg_own, hidden))
+    neg_own = [neg_near, neg_x, neg_y, *across(*after((neg_x, neg_y), pieces))]
+    neg_own = jnp.concatenate(neg_own)
     neg_other = swap_cores(neg_own)
     h_keep, h_send = call(
         order_kernel,

time: 178 us -> 175 us (0.983)
  waiting for transfers between devices: 86.6 us -> 76 us
  local copies, waits for them, and re-layouts: 14.1 us -> 20.6 us
  starting transfers between devices: 50.1 us -> 47.2 us
  Pallas kernels: 16.9 us -> 19.5 us
    ppermute x31 -> x29, waiting for transfers between devices: 83.7 us -> 74.5 us  [hop(): return lax.ppermute(value, 'ctx', perm)]
    unnamed x48 -> x46, local copies, waits for them, and re-layouts: 7.09 us -> 13.7 us
    ppermute x7, starting transfers between devices: 5.18 us -> 1.16 us  [swap_cores(): return lax.ppermute(value, 'tp', SWAP)]
    pallas_call x6, Pallas kernels: 16.9 us -> 19.5 us  [call(): pl.pallas_call(kernel, out_shape=[jax.ShapeDtypeStruct(shape, dtype) for...]
    ppermute x31 -> x29, starting transfers between devices: 39.3 us -> 40.3 us  [hop(): return lax.ppermute(value, 'ctx', perm)]
  transfers between devices with their start and end apart: 40 -> 38, of which waited for: 21 -> 18; matrix products, arithmetic and copies ran while one was open for 9% -> 11% of each run, Pallas kernels for 9% -> 10%
where the time goes in v11:
time: 175 us; the launch traced here: 174 us
  waiting for transfers between devices  76 us (43%)
  starting transfers between devices  47.2 us (27%)
  local copies, waits for them, and re-layouts  20.6 us (12%)
  Pallas kernels  19.5 us (11%)
  other arithmetic  9.94 us (6%)
    ppermute x29, waiting for transfers between devices, hop(): return lax.ppermute(value, 'ctx', perm)  74.5 us
    ppermute x29, starting transfers between devices, hop(): return lax.ppermute(value, 'ctx', perm)  40.3 us
    pallas_call x6, Pallas kernels, call(): pl.pallas_call(kernel, out_shape=[jax.ShapeDtypeStruct(shape, dtype) for...  19.5 us
    unnamed x46, local copies, waits for them, and re-layouts  13.7 us
    ppermute x2, starting transfers between devices, heads_along_z(): lax.ppermute(pick_row(heads, e ^ z & 1), ('ctx', 'tp'), perm)  5.68 us
  transfers between devices with their start and end apart: 38, of which 18 were waited for; matrix products, arithmetic and copies ran while one was open for 11% of the time, Pallas kernels for 10%

profile of v11, /device:TPU:0, one launch (start us, length us, event | category | flops | bytes accessed | tf_op | source)
XLA Modules:
  0.0 174.2 jit_solution(10082984464375380744)
XLA Ops:
  1.8 3.1 %collective-permute-start = (bf16[64,2176]{1,0:T(8,128)(2,1)S(1)}, bf16[64,2176]{1,0:T(8,128)(2,1)S(1)}, u32[]{:S(2)}, u32[]{:S(2)}) collective-permute-start(bf16[64,2176]{1,0:T(8,128)(2,1)S(1)} %pad_maximum_fusion.3), channel_id=1, source_target_pairs={{0,8},{2,10},{4,12},{6,14},{8,0},{10,2},{12,4},{14,6},{16,24},{18,... | collective-permute-start | bytes 835592 | tf_op jit(solution)/shard_map/ppermute | solution.py:106
  4.9 1.9 %copy.54 = bf16[128,4,1024]{0,2,1:T(8,128)(2,1)S(1)} copy(bf16[128,4,1024]{2,1,0:T(4,128)(2,1)} %param.9) | data formatting | bytes 2097152 | tf_op args[1]
  9.8 1.8 %collective-permute-done = bf16[64,2176]{1,0:T(8,128)(2,1)S(1)} collective-permute-done((bf16[64,2176]{1,0:T(8,128)(2,1)S(1)}, bf16[64,2176]{1,0:T(8,128)(2,1)S(1)}, u32[]{:S(2)}, u32[]{:S(2)}) %collective-permute-start) | collective-permute-done | bytes 278560 | tf_op jit(solution)/shard_map/ppermute | solution.py:106
  11.6 2.8 %collective-permute-start.1 = (bf16[128,2176]{1,0:T(8,128)(2,1)S(1)}, bf16[128,2176]{1,0:T(8,128)(2,1)S(1)}, u32[]{:S(2)}, u32[]{:S(2)}) collective-permute-start(bf16[128,2176]{1,0:T(8,128)(2,1)S(1)} %pad_maximum_fusion.1.refs_0_.refs_8_), channel_id=1, source_target_pairs={{0,16},{2,18},{4,20},{6,22},{8,24},{10,26},{12,28},{14,30},{16,0},... | collective-permute-start | bytes 1671176 | tf_op jit(solution)/shard_map/ppermute | solution.py:106
  14.4 6.4 %collective-permute-done.3 = bf16[2,2,128,512]{3,2,1,0:T(8,128)(2,1)} collective-permute-done((bf16[2,2,128,512]{3,2,1,0:T(8,128)(2,1)S(1)}, bf16[2,2,128,512]{3,2,1,0:T(8,128)(2,1)}, u32[]{:S(2)}, u32[]{:S(2)}) %collective-permute-start.3) | collective-permute-done | bytes 524320 | tf_op jit(solution)/shard_map/ppermute | solution.py:106
  20.8 1.8 %maximum_select_fusion = bf16[2,2,2,128,512]{4,3,2,0,1:T(8,128)(2,1)S(1)} fusion(bf16[2,1,2,128,512]{4,3,2,0,1:T(8,128)(2,1)} %bitcast.14, bf16[2,1,2,128,512]{4,3,2,0,1:T(8,128)(2,1)} %bitcast.71, pred[]{:T(512)S(6)} %eq.19), kind=kLoop, calls=%fused_computation | loop fusion | flops 1572864 | bytes 2097153 | tf_op jit(solution)/shard_map/jit(_where)/select_n | solution.py:134
  27.2 11.1 %collective-permute-done.1.refs_1_ = bf16[128,2176]{1,0:T(8,128)(2,1)S(1)} collective-permute-done((bf16[128,2176]{1,0:T(8,128)(2,1)S(1)}, bf16[128,2176]{1,0:T(8,128)(2,1)S(1)}, u32[]{:S(2)}, u32[]{:S(2)}) %collective-permute-start.1) | collective-permute-done | bytes 557088 | tf_op jit(solution)/shard_map/ppermute | solution.py:106
  44.1 5.3 %collective-permute-start.5 = (bf16[4,128,512]{2,1,0:T(8,128)(2,1)}, bf16[4,128,512]{2,1,0:T(8,128)(2,1)}, u32[]{:S(2)}, u32[]{:S(2)}) collective-permute-start(bf16[4,128,512]{2,1,0:T(8,128)(2,1)} %get-tuple-element.52), channel_id=1, source_target_pairs={{0,0},{1,16},{2,2},{3,18},{4,4},{5,20},{6,6},{7,22},{8,8},{9,24},{... | collective-permute-start | bytes 1572872 | tf_op jit(solution)/shard_map/ppermute | solution.py:149
  54.4 6.0 %collective-permute-done.13.refs_5_ = bf16[128,2176]{1,0:T(8,128)(2,1)} collective-permute-done((bf16[128,2176]{1,0:T(8,128)(2,1)S(1)}, bf16[128,2176]{1,0:T(8,128)(2,1)}, u32[]{:S(2)}, u32[]{:S(2)}) %collective-permute-start.13) | collective-permute-done | bytes 557088 | tf_op jit(solution)/shard_map/ppermute | solution.py:106
  62.9 10.9 %collective-permute-done.2 = bf16[1,1024,128]{2,1,0:T(8,128)(2,1)} collective-permute-done((bf16[1,1024,128]{2,1,0:T(8,128)(2,1)}, bf16[1,1024,128]{2,1,0:T(8,128)(2,1)}, u32[]{:S(2)}, u32[]{:S(2)}) %collective-permute-start.2) | collective-permute-done | bytes 262176 | tf_op jit(solution)/shard_map/ppermute | solution.py:106
  75.4 2.0 %collective-permute-start.14 = (bf16[64,2176]{1,0:T(8,128)(2,1)S(1)}, bf16[64,2176]{1,0:T(8,128)(2,1)S(1)}, u32[]{:S(2)}, u32[]{:S(2)}) collective-permute-start(bf16[64,2176]{1,0:T(8,128)(2,1)S(1)} %slice.59), channel_id=1, source_target_pairs={{0,2},{2,0},{4,6},{6,4},{8,10},{10,8},{12,14},{14,12},{16,18},{18,... | collective-permute-start | bytes 835592 | tf_op jit(solution)/shard_map/ppermute | solution.py:106
  79.3 2.8 %maximum_select_fusion.2 = bf16[2,4,128,512]{3,2,1,0:T(8,128)(2,1)} fusion(bf16[1,4,128,512]{3,2,1,0:T(8,128)(2,1)} %bitcast.22, bf16[1,4,128,512]{3,2,1,0:T(8,128)(2,1)} %bitcast.20, pred[]{:T(512)S(6)} %eq.17), kind=kLoop, calls=%fused_computation.3 | loop fusion | flops 1572864 | bytes 2097153 | tf_op jit(solution)/shard_map/jit(_where)/select_n | solution.py:150
  92.2 5.7 %project.1 = (bf16[1024,256]{1,0:T(8,128)(2,1)S(1)}, bf16[1024,256]{1,0:T(8,128)(2,1)}, bf16[1024,128]{1,0:T(8,128)(2,1)S(1)}) custom-call(s32[4]{0:T(128)S(1)} %pad_add_fusion.where, bf16[128,2176]{1,0:T(8,128)(2,1)S(1)} %pad_maximum_fusion.1.refs_0_.refs_8_, bf16[128,2176]{1,0:T(8,128)(2,1)S(1)} %copy-done.10, ...), custom_call_target="tpu_custom_call" | custom-call | flops 42949672960 | bytes 6553616 | tf_op jit(solution)/shard_map/project/pallas_call | solution.py:329
  101.9 4.5 %attend.1 = bf16[4,4,64,128]{3,2,1,0:T(8,128)(2,1)S(1)} custom-call(bf16[1024,256]{1,0:T(8,128)(2,1)S(1)} %get-tuple-element.30.gq_hbm, bf16[1024,256]{1,0:T(8,128)(2,1)} %get-tuple-element.28.own_hbm, bf16[1024,256]{1,0:T(8,128)(2,1)} %collective-permute-done.18.other_hbm, bf16[1024,128]{1,0:T(8,128)(2,1)S(1)} %copy-done.2), custom_call_target="tpu_custom_call" | custom-call | bytes 1835008 | tf_op jit(solution)/shard_map/attend/pallas_call | solution.py:329
  106.4 5.1 %collective-permute-done.15.refs_5_ = bf16[2,1024,128]{2,1,0:T(8,128)(2,1)} collective-permute-done((bf16[2,1024,128]{2,1,0:T(8,128)(2,1)S(1)}, bf16[2,1024,128]{2,1,0:T(8,128)(2,1)}, u32[]{:S(2)}, u32[]{:S(2)}) %collective-permute-start.15) | collective-permute-done | bytes 524320 | tf_op jit(solution)/shard_map/ppermute | solution.py:106
  111.7 2.3 %collective-permute-start.20 = (bf16[4,64,128]{2,1,0:T(8,128)(2,1)S(1)}, bf16[4,64,128]{2,1,0:T(8,128)(2,1)S(1)}, u32[]{:S(2)}, u32[]{:S(2)}) collective-permute-start(bf16[4,64,128]{2,1,0:T(8,128)(2,1)S(1)} %get-tuple-element.66), channel_id=1, source_target_pairs={{0,16},{2,18},{4,20},{6,22},{8,24},{10,26},{12,28},{14,30},{16,0},... | collective-permute-start | bytes 196616 | tf_op jit(solution)/shard_map/ppermute | solution.py:106
  113.9 2.1 %collective-permute-start.21 = (bf16[4,64,128]{2,1,0:T(8,128)(2,1)S(1)}, bf16[4,64,128]{2,1,0:T(8,128)(2,1)S(1)}, u32[]{:S(2)}, u32[]{:S(2)}) collective-permute-start(bf16[4,64,128]{2,1,0:T(8,128)(2,1)S(1)} %get-tuple-element.65), channel_id=1, source_target_pairs={{0,24},{2,26},{4,28},{6,30},{8,16},{10,18},{12,20},{14,22},{16,8},... | collective-permute-start | bytes 196616 | tf_op jit(solution)/shard_map/ppermute | solution.py:106
  116.7 3.4 %collective-permute-done.20 = bf16[4,64,128]{2,1,0:T(8,128)(2,1)S(1)} collective-permute-done((bf16[4,64,128]{2,1,0:T(8,128)(2,1)S(1)}, bf16[4,64,128]{2,1,0:T(8,128)(2,1)S(1)}, u32[]{:S(2)}, u32[]{:S(2)}) %collective-permute-start.20) | collective-permute-done | bytes 65568 | tf_op jit(solution)/shard_map/ppermute | solution.py:106
  125.1 9.0 %collective-permute-done.32 = bf16[128,1152]{1,0:T(8,128)(2,1)S(1)} collective-permute-done((bf16[128,1152]{1,0:T(8,128)(2,1)S(1)}, bf16[128,1152]{1,0:T(8,128)(2,1)S(1)}, u32[]{:S(2)}, u32[]{:S(2)}) %collective-permute-start.32) | collective-permute-done | bytes 294944 | tf_op jit(solution)/shard_map/ppermute | solution.py:106
  134.1 3.1 %collective-permute-done.23.refs_2_ = bf16[4,4,64,128]{3,2,1,0:T(8,128)(2,1)S(1)} collective-permute-done((bf16[4,4,64,128]{3,2,1,0:T(8,128)(2,1)S(1)}, bf16[4,4,64,128]{3,2,1,0:T(8,128)(2,1)S(1)}, u32[]{:S(2)}, u32[]{:S(2)}) %collective-permute-start.23) | collective-permute-done | bytes 262176 | tf_op jit(solution)/shard_map/ppermute | solution.py:106
  139.0 2.9 %hidden.1 = bf16[4,64,512]{2,1,0:T(8,128)(2,1)S(1)} custom-call(s32[4]{0:T(128)S(1)} %pad_add_fusion.where, bf16[4,4,64,128]{3,2,1,0:T(8,128)(2,1)S(1)} %pad_maximum_fusion.4.refs_0_, bf16[4,4,64,128]{3,2,1,0:T(8,128)(2,1)S(1)} %collective-permute-done.22.refs_1_, bf16[4,4,64,128]{3,2,1,0:T(8,128)(2,1)S(1)} %collective-permute-done.23.refs_2_, ...), custom_call_target="tpu_custom_call" | custom-call | flops 536870912 | bytes 5095440 | tf_op jit(solution)/shard_map/hidden/pallas_call | solution.py:329
  145.5 8.5 %collective-permute-done.26.refs_1_ = bf16[64,512]{1,0:T(8,128)(2,1)S(1)} collective-permute-done((bf16[64,512]{1,0:T(8,128)(2,1)S(1)}, bf16[64,512]{1,0:T(8,128)(2,1)S(1)}, u32[]{:S(2)}, u32[]{:S(2)}) %collective-permute-start.26) | collective-permute-done | bytes 65568 | tf_op jit(solution)/shard_map/ppermute | solution.py:106
  157.4 4.8 %collective-permute-done.35 = bf16[128,1152]{1,0:T(8,128)(2,1)S(1)} collective-permute-done((bf16[128,1152]{1,0:T(8,128)(2,1)S(1)}, bf16[128,1152]{1,0:T(8,128)(2,1)S(1)}, u32[]{:S(2)}, u32[]{:S(2)}) %collective-permute-start.35) | collective-permute-done | bytes 294944 | tf_op jit(solution)/shard_map/ppermute | solution.py:106
  168.5 4.1 %loss.1 = f32[1,64]{1,0:T(1,128)} custom-call(bf16[64,1024]{1,0:T(8,128)(2,1)S(1)} %get-tuple-element.37.h_keep.keep, bf16[64,1024]{1,0:T(8,128)(2,1)S(1)} %get-tuple-element.38.h_send, bf16[64,1024]{1,0:T(8,128)(2,1)S(1)} %get-tuple-element.59.t_keep, bf16[64,1024]{1,0:T(8,128)(2,1)S(1)} %collective-permute-done.30.t_send, s32[64,1]{1,0:T(8,128)S(1)} %copy.60.t_ids, ...), custom_call_target="tpu_custom_call" | custom-call | flops 268435456 | bytes 5243136 | tf_op jit(solution)/shard_map/loss/pallas_call | solution.py:329
  (145 shorter events, 61.9 us)
Async XLA Ops:
  7.2 13.6 %collective-permute-start.3 = (bf16[2,2,128,512]{3,2,1,0:T(8,128)(2,1)S(1)}, bf16[2,2,128,512]{3,2,1,0:T(8,128)(2,1)}, u32[]{:S(2)}, u32[]{:S(2)}) collective-permute-start(bf16[2,2,128,512]{3,2,1,0:T(8,128)(2,1)S(1)} %bitcast.72), channel_id=1, source_target_pairs={{0,2},{2,0},{4,6},{6,4},{8,10},{10,8},{12,14},{14,12},{16,18},{18,... | collective-permute-start | bytes 1572872 | tf_op jit(solution)/shard_map/ppermute | solution.py:106
  11.6 26.7 %collective-permute-start.1 = (bf16[128,2176]{1,0:T(8,128)(2,1)S(1)}, bf16[128,2176]{1,0:T(8,128)(2,1)S(1)}, u32[]{:S(2)}, u32[]{:S(2)}) collective-permute-start(bf16[128,2176]{1,0:T(8,128)(2,1)S(1)} %pad_maximum_fusion.1.refs_0_.refs_8_), channel_id=1, source_target_pairs={{0,16},{2,18},{4,20},{6,22},{8,24},{10,26},{12,28},{14,30},{16,0},... | collective-permute-start | bytes 1671176 | tf_op jit(solution)/shard_map/ppermute | solution.py:106
  23.7 17.4 %collective-permute-start.4 = (bf16[2,2,128,512]{3,2,1,0:T(8,128)(2,1)}, bf16[2,2,128,512]{3,2,1,0:T(8,128)(2,1)}, u32[]{:S(2)}, u32[]{:S(2)}) collective-permute-start(bf16[2,2,128,512]{3,2,1,0:T(8,128)(2,1)} %get-tuple-element.55), channel_id=1, source_target_pairs={{0,4},{2,6},{4,0},{6,2},{8,12},{10,14},{12,8},{14,10},{16,20},{18,... | collective-permute-start | bytes 1572872 | tf_op jit(solution)/shard_map/ppermute | solution.py:106
  25.2 25.5 %collective-permute-start.9 = (bf16[128,2176]{1,0:T(8,128)(2,1)S(1)}, bf16[128,2176]{1,0:T(8,128)(2,1)S(1)}, u32[]{:S(2)}, u32[]{:S(2)}) collective-permute-start(bf16[128,2176]{1,0:T(8,128)(2,1)S(1)} %pad_maximum_fusion.1.refs_0_.refs_8_), channel_id=1, source_target_pairs={{0,4},{2,6},{4,0},{6,2},{8,12},{10,14},{12,8},{14,10},{16,20},{18,... | collective-permute-start | bytes 1671176 | tf_op jit(solution)/shard_map/ppermute | solution.py:106
  25.7 25.3 %collective-permute-start.7 = (bf16[128,2176]{1,0:T(8,128)(2,1)S(1)}, bf16[128,2176]{1,0:T(8,128)(2,1)S(1)}, u32[]{:S(2)}, u32[]{:S(2)}) collective-permute-start(bf16[128,2176]{1,0:T(8,128)(2,1)S(1)} %pad_maximum_fusion.1.refs_0_.refs_8_), channel_id=1, source_target_pairs={{0,2},{2,0},{4,6},{6,4},{8,10},{10,8},{12,14},{14,12},{16,18},{18,... | collective-permute-start | bytes 1671176 | tf_op jit(solution)/shard_map/ppermute | solution.py:106
  38.3 14.5 %collective-permute-start.11 = (bf16[128,2176]{1,0:T(8,128)(2,1)S(1)}, bf16[128,2176]{1,0:T(8,128)(2,1)S(1)}, u32[]{:S(2)}, u32[]{:S(2)}) collective-permute-start(bf16[128,2176]{1,0:T(8,128)(2,1)S(1)} %collective-permute-done.1.refs_1_), channel_id=1, source_target_pairs={{0,2},{2,0},{4,6},{6,4},{8,10},{10,8},{12,14},{14,12},{16,18},{18,... | collective-permute-start | bytes 1671176 | tf_op jit(solution)/shard_map/ppermute | solution.py:106
  39.6 20.8 %collective-permute-start.13 = (bf16[128,2176]{1,0:T(8,128)(2,1)S(1)}, bf16[128,2176]{1,0:T(8,128)(2,1)}, u32[]{:S(2)}, u32[]{:S(2)}) collective-permute-start(bf16[128,2176]{1,0:T(8,128)(2,1)S(1)} %collective-permute-done.1.refs_1_), channel_id=1, source_target_pairs={{0,4},{2,6},{4,0},{6,2},{8,12},{10,14},{12,8},{14,10},{16,20},{18,... | collective-permute-start | bytes 1671176 | tf_op jit(solution)/shard_map/ppermute | solution.py:106
  44.1 31.3 %collective-permute-start.5 = (bf16[4,128,512]{2,1,0:T(8,128)(2,1)}, bf16[4,128,512]{2,1,0:T(8,128)(2,1)}, u32[]{:S(2)}, u32[]{:S(2)}) collective-permute-start(bf16[4,128,512]{2,1,0:T(8,128)(2,1)} %get-tuple-element.52), channel_id=1, source_target_pairs={{0,0},{1,16},{2,2},{3,18},{4,4},{5,20},{6,6},{7,22},{8,8},{9,24},{... | collective-permute-start | bytes 1572872 | tf_op jit(solution)/shard_map/ppermute | solution.py:149
  50.7 28.6 %collective-permute-start.6 = (bf16[4,128,512]{2,1,0:T(8,128)(2,1)}, bf16[4,128,512]{2,1,0:T(8,128)(2,1)}, u32[]{:S(2)}, u32[]{:S(2)}) collective-permute-start(bf16[4,128,512]{2,1,0:T(8,128)(2,1)} %get-tuple-element.53), channel_id=1, source_target_pairs={{0,8},{1,24},{2,10},{3,26},{4,12},{5,28},{6,14},{7,30},{8,0},{9,16... | collective-permute-start | bytes 1572872 | tf_op jit(solution)/shard_map/ppermute | solution.py:149
  51.0 22.8 %collective-permute-start.2 = (bf16[1,1024,128]{2,1,0:T(8,128)(2,1)}, bf16[1,1024,128]{2,1,0:T(8,128)(2,1)}, u32[]{:S(2)}, u32[]{:S(2)}) collective-permute-start(bf16[1,1024,128]{2,1,0:T(8,128)(2,1)} %bitcast.4), channel_id=1, source_target_pairs={{0,8},{2,10},{4,12},{6,14},{8,0},{10,2},{12,4},{14,6},{16,24},{18,... | collective-permute-start | bytes 786440 | tf_op jit(solution)/shard_map/ppermute | solution.py:106
  52.8 29.3 %collective-permute-start.10 = (bf16[64,2176]{1,0:T(8,128)(2,1)S(1)}, bf16[64,2176]{1,0:T(8,128)(2,1)S(1)}, u32[]{:S(2)}, u32[]{:S(2)}) collective-permute-start(bf16[64,2176]{1,0:T(8,128)(2,1)S(1)} %slice.57), channel_id=1, source_target_pairs={{0,2},{2,0},{4,6},{6,4},{8,10},{10,8},{12,14},{14,12},{16,18},{18,... | collective-permute-start | bytes 835592 | tf_op jit(solution)/shard_map/ppermute | solution.py:106
  60.4 22.5 %collective-permute-start.8 = (bf16[64,2176]{1,0:T(8,128)(2,1)S(1)}, bf16[64,2176]{1,0:T(8,128)(2,1)S(1)}, u32[]{:S(2)}, u32[]{:S(2)}) collective-permute-start(bf16[64,2176]{1,0:T(8,128)(2,1)S(1)} %slice.56), channel_id=1, source_target_pairs={{0,4},{2,6},{4,0},{6,2},{8,12},{10,14},{12,8},{14,10},{16,20},{18,... | collective-permute-start | bytes 835592 | tf_op jit(solution)/shard_map/ppermute | solution.py:106
  85.9 25.7 %collective-permute-start.15 = (bf16[2,1024,128]{2,1,0:T(8,128)(2,1)S(1)}, bf16[2,1024,128]{2,1,0:T(8,128)(2,1)}, u32[]{:S(2)}, u32[]{:S(2)}) collective-permute-start(bf16[2,1024,128]{2,1,0:T(8,128)(2,1)S(1)} %constant_dynamic-update-slice_fusion.refs_4_), channel_id=1, source_target_pairs={{0,16},{2,18},{4,20},{6,22},{8,24},{10,26},{12,28},{14,30},{16,0},... | collective-permute-start | bytes 1572872 | tf_op jit(solution)/shard_map/ppermute | solution.py:106
  98.8 12.7 %collective-permute-start.17 = (bf16[2,1024,128]{2,1,0:T(8,128)(2,1)S(1)}, bf16[2,1024,128]{2,1,0:T(8,128)(2,1)}, u32[]{:S(2)}, u32[]{:S(2)}) collective-permute-start(bf16[2,1024,128]{2,1,0:T(8,128)(2,1)S(1)} %constant_dynamic-update-slice_fusion.refs_4_), channel_id=1, source_target_pairs={{0,1},{1,0},{2,3},{3,2},{4,5},{5,4},{6,7},{7,6},{8,9},{9,8},{10,11... | collective-permute-start | bytes 1572872 | tf_op jit(solution)/shard_map/ppermute | solution.py:110
  100.4 15.6 %collective-permute-start.31 = (bf16[64,1152]{1,0:T(8,128)(2,1)S(1)}, bf16[64,1152]{1,0:T(8,128)(2,1)S(1)}, u32[]{:S(2)}, u32[]{:S(2)}) collective-permute-start(bf16[64,1152]{1,0:T(8,128)(2,1)S(1)} %fusion.2), channel_id=1, source_target_pairs={{0,8},{2,10},{4,12},{6,14},{8,0},{10,2},{12,4},{14,6},{16,24},{18,... | collective-permute-start | bytes 442376 | tf_op jit(solution)/shard_map/ppermute | solution.py:106
  120.2 13.9 %collective-permute-start.32 = (bf16[128,1152]{1,0:T(8,128)(2,1)S(1)}, bf16[128,1152]{1,0:T(8,128)(2,1)S(1)}, u32[]{:S(2)}, u32[]{:S(2)}) collective-permute-start(bf16[128,1152]{1,0:T(8,128)(2,1)S(1)} %pad_maximum_fusion.2), channel_id=1, source_target_pairs={{0,16},{2,18},{4,20},{6,22},{8,24},{10,26},{12,28},{14,30},{16,0},... | collective-permute-start | bytes 884744 | tf_op jit(solution)/shard_map/ppermute | solution.py:106
  121.6 15.6 %collective-permute-start.25 = (bf16[2,1024,128]{2,1,0:T(8,128)(2,1)}, bf16[2,1024,128]{2,1,0:T(8,128)(2,1)S(1)}, u32[]{:S(2)}, u32[]{:S(2)}) collective-permute-start(bf16[2,1024,128]{2,1,0:T(8,128)(2,1)} %collective-permute-done.15.refs_5_), channel_id=1, source_target_pairs={{0,1},{1,0},{2,3},{3,2},{4,5},{5,4},{6,7},{7,6},{8,9},{9,8},{10,11... | collective-permute-start | bytes 1572872 | tf_op jit(solution)/shard_map/ppermute | solution.py:110
  121.6 12.5 %collective-permute-start.22 = (bf16[4,4,64,128]{3,2,1,0:T(8,128)(2,1)S(1)}, bf16[4,4,64,128]{3,2,1,0:T(8,128)(2,1)S(1)}, u32[]{:S(2)}, u32[]{:S(2)}) collective-permute-start(bf16[4,4,64,128]{3,2,1,0:T(8,128)(2,1)S(1)} %pad_maximum_fusion.4.refs_0_), channel_id=1, source_target_pairs={{0,2},{2,0},{4,6},{6,4},{8,10},{10,8},{12,14},{14,12},{16,18},{18,... | collective-permute-start | bytes 786440 | tf_op jit(solution)/shard_map/ppermute | solution.py:106
  123.2 14.1 %collective-permute-start.23 = (bf16[4,4,64,128]{3,2,1,0:T(8,128)(2,1)S(1)}, bf16[4,4,64,128]{3,2,1,0:T(8,128)(2,1)S(1)}, u32[]{:S(2)}, u32[]{:S(2)}) collective-permute-start(bf16[4,4,64,128]{3,2,1,0:T(8,128)(2,1)S(1)} %pad_maximum_fusion.4.refs_0_), channel_id=1, source_target_pairs={{0,4},{2,6},{4,0},{6,2},{8,12},{10,14},{12,8},{14,10},{16,20},{18,... | collective-permute-start | bytes 786440 | tf_op jit(solution)/shard_map/ppermute | solution.py:106
  124.0 13.2 %collective-permute-start.24 = (bf16[4,4,64,128]{3,2,1,0:T(8,128)(2,1)S(1)}, bf16[4,4,64,128]{3,2,1,0:T(8,128)(2,1)S(1)}, u32[]{:S(2)}, u32[]{:S(2)}) collective-permute-start(bf16[4,4,64,128]{3,2,1,0:T(8,128)(2,1)S(1)} %pad_maximum_fusion.4.refs_0_), channel_id=1, source_target_pairs={{0,6},{2,4},{4,2},{6,0},{8,14},{10,12},{12,10},{14,8},{16,22},{18,... | collective-permute-start | bytes 786440 | tf_op jit(solution)/shard_map/ppermute | solution.py:106
  137.2 18.0 %collective-permute-start.33 = (bf16[256,1152]{1,0:T(8,128)(2,1)S(1)}, bf16[256,1152]{1,0:T(8,128)(2,1)S(1)}, u32[]{:S(2)}, u32[]{:S(2)}) collective-permute-start(bf16[256,1152]{1,0:T(8,128)(2,1)S(1)} %pad_maximum_fusion), channel_id=1, source_target_pairs={{0,2},{2,0},{4,6},{6,4},{8,10},{10,8},{12,14},{14,12},{16,18},{18,... | collective-permute-start | bytes 1769480 | tf_op jit(solution)/shard_map/ppermute | solution.py:106
  137.8 17.5 %collective-permute-start.34 = (bf16[256,1152]{1,0:T(8,128)(2,1)S(1)}, bf16[256,1152]{1,0:T(8,128)(2,1)S(1)}, u32[]{:S(2)}, u32[]{:S(2)}) collective-permute-start(bf16[256,1152]{1,0:T(8,128)(2,1)S(1)} %pad_maximum_fusion), channel_id=1, source_target_pairs={{0,4},{2,6},{4,0},{6,2},{8,12},{10,14},{12,8},{14,10},{16,20},{18,... | collective-permute-start | bytes 1769480 | tf_op jit(solution)/shard_map/ppermute | solution.py:106
  141.9 12.1 %collective-permute-start.26 = (bf16[64,512]{1,0:T(8,128)(2,1)S(1)}, bf16[64,512]{1,0:T(8,128)(2,1)S(1)}, u32[]{:S(2)}, u32[]{:S(2)}) collective-permute-start(bf16[64,512]{1,0:T(8,128)(2,1)S(1)} %get-tuple-element.62), channel_id=1, source_target_pairs={{0,2},{2,0},{4,6},{6,4},{8,10},{10,8},{12,14},{14,12},{16,18},{18,... | collective-permute-start | bytes 196616 | tf_op jit(solution)/shard_map/ppermute | solution.py:106
  143.0 12.2 %collective-permute-start.27 = (bf16[64,512]{1,0:T(8,128)(2,1)S(1)}, bf16[64,512]{1,0:T(8,128)(2,1)S(1)}, u32[]{:S(2)}, u32[]{:S(2)}) collective-permute-start(bf16[64,512]{1,0:T(8,128)(2,1)S(1)} %get-tuple-element.61), channel_id=1, source_target_pairs={{0,4},{2,6},{4,0},{6,2},{8,12},{10,14},{12,8},{14,10},{16,20},{18,... | collective-permute-start | bytes 196616 | tf_op jit(solution)/shard_map/ppermute | solution.py:106
  (34 other events, 174.8 us)

commit v12 on v11

--- a/solution.py
+++ b/solution.py
@@ -6,7 +6,7 @@
 from jax.sharding import PartitionSpec as P
 
 HEAD_DIM = 128
-VMEM_LIMIT = 48 * 1024 * 1024
+VMEM_LIMIT = 24 * 1024 * 1024
 BF16 = jnp.bfloat16
 F32 = jnp.float32
 
@@ -137,18 +137,17 @@
     return whole.transpose(2, 0, 1, 3, 4).reshape(2, NY * NX, *whole.shape[3:])
 
 
-def heads_along_z(heads, z):
+def heads_along_z(pieces):
     arrived = []
-    for e in range(2):
+    for e, piece in enumerate(pieces):
         perm = []
         for src in range(CHIPS):
             sz, sy, sx = coords(src)
             for t in range(2):
                 dst = chip_at(2 * t + (e ^ (sz & 1)), sy, sx)
                 perm.append((2 * src + t, 2 * dst + (sz >> 1)))
-        arrived.append(lax.ppermute(pick_row(heads, e ^ (z & 1)), ("ctx", "tp"), perm))
-    rows = jnp.where(z % 2 == 0, jnp.stack(arrived), jnp.stack(arrived[::-1]))
-    return rows.reshape(-1, rows.shape[-1])
+        arrived.append(lax.ppermute(piece, ("ctx", "tp"), perm).reshape(-1, piece.shape[-1]))
+    return arrived
 
 
 def silu(v):
@@ -163,15 +162,17 @@
 
 
 def proj_kernel(where, *refs):
-    count = len(refs) - 9
-    tok, (w_own, w_other) = refs[:count], refs[count : count + 2]
-    gate_query, value_key, marks, x_all, w_all, tok_sem, w_sem = refs[count + 2 :]
-    u = where[3]
+    count = len(refs) - 12
+    tok, w_own, w_other = refs[:count], refs[count : count + 2], refs[count + 2 : count + 4]
+    gate_query, value, key, marks, x_all, w_all, tok_sem, w_sem = refs[count + 4 :]
+    z, u = where[0], where[3]
     copies, base = [], 0
-    half = w_own.shape[0]
-    for side, (at, src) in enumerate(((u, w_own), (1 - u, w_other))):
-        rows = pl.ds(pl.multiple_of(at * half, half), half)
-        copies.append(pltpu.make_async_copy(src, w_all.at[rows, :], w_sem.at[side]))
+    for side, (at, srcs) in enumerate(((u, w_own), (1 - u, w_other))):
+        for e, src in enumerate(srcs):
+            size = src.shape[0]
+            start = pl.multiple_of((2 * at + (e ^ (z & 1))) * size, size)
+            to = w_all.at[pl.ds(start, size), :]
+            copies.append(pltpu.make_async_copy(src, to, w_sem.at[2 * side + e]))
     for i, ref in enumerate(tok):
         rows = pl.ds(base, ref.shape[0])
         copies.append(pltpu.make_async_copy(ref, x_all.at[rows, :], tok_sem.at[i]))
@@ -181,9 +182,9 @@
     total = jnp.dot(x_all[:, :model], w_all[...], preferred_element_type=F32)
     proj = silu(total).astype(BF16)
     gate_query[:, :W] = proj[:, :W]
-    value_key[:, :W] = proj[:, W : 2 * W]
+    value[...] = proj[:, W : 2 * W]
     gate_query[:, W:] = proj[:, 2 * W : 3 * W]
-    value_key[:, W:] = proj[:, 3 * W :]
+    key[...] = proj[:, 3 * W :]
     marks[...] = x_all[:, model:]
 
 
@@ -197,14 +198,15 @@
     return pick.astype(BF16)
 
 
-def attend_kernel(gq_hbm, own_hbm, other_hbm, marks_hbm, gated, gate_query, own, other, marks, sems):
-    sources = (gq_hbm, own_hbm, other_hbm, marks_hbm)
+def attend_kernel(*refs):
+    sources, gated, copied, sems = refs[:6], refs[6], refs[7:13], refs[13]
     run_copies(
         [
             pltpu.make_async_copy(src, dst, sems.at[i])
-            for i, (src, dst) in enumerate(zip(sources, (gate_query, own, other, marks)))
+            for i, (src, dst) in enumerate(zip(sources, copied))
         ]
     )
+    gate_query, key, value, key_theirs, value_theirs, marks = copied
     pick = pick_columns({0: 128.0, 1: 1.0}, {2: 128.0, 3: 1.0})
     piece = gated.shape[2]
     tile = NZ * piece
@@ -214,13 +216,13 @@
         query = gate_query[span, W:]
         q_pos = lax.dot_general(marks[span, :], pick, ACROSS, preferred_element_type=F32)[:, :1]
         attn = jnp.zeros((tile, W), F32)
-        for side, kv in enumerate((own, other)):
+        for side, (keys, values) in enumerate(((key, value), (key_theirs, value_theirs))):
             scores = lax.dot_general(
-                query, kv[:, W:], ACROSS, preferred_element_type=F32
+                query, keys[...], ACROSS, preferred_element_type=F32
             ) * W ** (-0.5)
             visible = key_pos[side : side + 1] <= q_pos
             weight = jnp.where(visible, silu(scores), 0.0).astype(BF16)
-            attn += jnp.dot(weight, kv[:, :W], preferred_element_type=F32)
+            attn += jnp.dot(weight, values[...], preferred_element_type=F32)
         normed = attn * lax.rsqrt(jnp.mean(attn * attn, axis=-1, keepdims=True) + 1e-06)
         out = (normed * gate_query[span, :W].astype(F32)).astype(BF16)
         for s in range(NZ):
@@ -324,7 +326,7 @@
 
 
 def call(kernel, name, outs, scratch, args, places, flops):
-    space = {"s": pltpu.SMEM, "v": pltpu.VMEM, "h": pltpu.HBM}
+    space = {"s": pltpu.SMEM, "v": pltpu.VMEM, "h": pl.ANY}
     moved = sum(a.size * a.dtype.itemsize for a in args)
     return pl.pallas_call(
         kernel,
@@ -378,21 +380,23 @@
     to_x, to_y = flip(0, 1), flip(1, 0)
     high = hop(low, flip(0, 0, 2))
     w_plane = heads_in_plane(w_proj, y, x)
+    w_pieces = [pick_row(w_plane, e ^ (z & 1)) for e in range(2)]
     low_x, low_y = hop(low, to_x), hop(low, to_y)
     low_xy = across(low_x, low_y)
-    high_x, high_y = hop(high, to_x), hop(high, to_y)
-    high_xy = across(high_x, high_y)
-    tok = [low, high, low_x, high_x, low_y, high_y, *low_xy, *high_xy]
-    w_mine = heads_along_z(after(w_plane, high), z)
-    out_pair = pair_up(after(w_out[None], high))
-    w_mine = after(w_mine, low_xy, high_xy, out_pair)
-    w_theirs = swap_cores(w_mine)
-    out_own = [out_pair, hop(after(out_pair, w_mine), flip(0, 0, 2))]
-
+
+    out_pair = pair_up(after(w_out[None], low))
     own_ids = lax.dynamic_slice_in_dim(neg_ids, c * negs, negs, 0)
     norms = jnp.sum(jnp.square(neg_emb.astype(F32)), axis=1)
     neg = with_marks(neg_emb, float_parts(norms) + whole_parts(own_ids, 256))
     neg_pair = pair_up(after(neg, out_pair))
+
+    w_pieces, high = lax.optimization_barrier((w_pieces, after(high, neg_pair)))
+    high_x, high_y = hop(high, to_x), hop(high, to_y)
+    high_xy = across(high_x, high_y)
+    tok = [low, high, low_x, high_x, low_y, high_y, *low_xy, *high_xy]
+    w_mine = after(heads_along_z(w_pieces), low_xy, high_xy)
+    w_theirs = [swap_cores(w) for w in w_mine]
+    out_own = [out_pair, hop(after(out_pair, w_mine), flip(0, 0, 2))]
     t_rows = after(target_emb.reshape(2, rows, -1), w_theirs)
     t_keep = pick_row(t_rows, u)
     t_send = swap_cores(pick_row(t_rows, 1 - u))
@@ -402,29 +406,30 @@
         return call(
             proj_kernel,
             "project",
-            [((count, 2 * W), BF16)] * 2 + [((count, W), BF16)],
+            [((count, 2 * W), BF16)] + [((count, W), BF16)] * 3,
             [
                 pltpu.VMEM((count, model + W), BF16),
                 pltpu.VMEM((model, 4 * W), BF16),
                 pltpu.SemaphoreType.DMA((len(pieces),)),
-                pltpu.SemaphoreType.DMA((2,)),
+                pltpu.SemaphoreType.DMA((4,)),
             ],
-            [where, *pieces, w_mine, w_theirs],
-            "s" + (len(pieces) + 2) * "h",
+            [where, *pieces, *w_mine, *w_theirs],
+            "s" + (len(pieces) + 4) * "h",
             20 * 2 * count * model * 4 * W,
         )
 
-    gate_query, value_key, marks = project(tok)
-    kv_theirs = swap_cores(value_key)
-    out_pair_theirs = swap_cores(after(out_pair, value_key))
+    gate_query, value, key, marks = project(tok)
+    key_theirs, value_theirs = swap_cores(key), swap_cores(value)
+    out_pair_theirs = swap_cores(after(out_pair, value))
     (gated,) = call(
         attend_kernel,
         "attend",
         [((NZ, plane, rows, W), BF16)],
-        [pltpu.VMEM((events, 2 * W), BF16)] * 3
-        + [pltpu.VMEM((events, W), BF16), pltpu.SemaphoreType.DMA((4,))],
-        [gate_query, value_key, kv_theirs, marks],
-        4 * "h",
+        [pltpu.VMEM((events, 2 * W), BF16)]
+        + [pltpu.VMEM((events, W), BF16)] * 5
+        + [pltpu.SemaphoreType.DMA((6,))],
+        [gate_query, key, value, key_theirs, value_theirs, marks],
+        6 * "h",
         0,
     )
     out_own, out_pair_theirs, gated = lax.optimization_barrier((out_own, out_pair_theirs, gated))
@@ -432,7 +437,7 @@
     neg_far = hop(after(neg_pair, gated), flip(0, 0, 2))
     out_other = [out_pair_theirs, swap_cores(after(out_own[1], gated))]
     gated = [gated] + [hop(gated, flip(by, bx)) for by, bx in PLANE[1:]]
-    neg_near = after(jnp.concatenate([neg_pair, neg_far]), gated, out_other)
+    neg_near = after(jnp.concatenate([neg_pair, neg_far]), gated, out_other, t_send)
     neg_x, neg_y = hop(neg_near, to_x), hop(neg_near, to_y)
     (hidden,) = call(
         hidden_kernel,

time: 175 us -> 167 us (0.954)
  waiting for transfers between devices: 76 us -> 90.4 us
  local copies, waits for them, and re-layouts: 20.6 us -> 8.91 us
  other arithmetic: 9.94 us -> 4.6 us
  Pallas kernels: 19.5 us -> 16.7 us
  starting transfers between devices: 47.2 us -> 44.7 us
    ppermute x29, waiting for transfers between devices: 74.5 us -> 84.7 us  [hop(): return lax.ppermute(value, 'ctx', perm)]
    unnamed x46 -> x27, local copies, waits for them, and re-layouts: 13.7 us -> 4.95 us
    ppermute x2, starting transfers between devices: 5.68 us -> 0.93 us  [heads_along_z(): lax.ppermute(piece, ('ctx', 'tp'), perm).reshape(-1, piece.shape[-1])]
    ppermute x7 -> x9, waiting for transfers between devices: 1.52 us -> 5.68 us  [swap_cores(): return lax.ppermute(value, 'tp', SWAP)]
    select_n x1 -> x0, other arithmetic: 2.77 us -> none  [heads_along_z(): rows = jnp.where(z % 2 == 0, jnp.stack(arrived), jnp.stack(arrived[::-1]))]
    pallas_call x6, Pallas kernels: 19.5 us -> 16.7 us  [call(): pl.pallas_call(kernel, out_shape=[jax.ShapeDtypeStruct(shape, dtype) for...]
  transfers between devices with their start and end apart: 38 -> 40, of which waited for: 18 -> 19; matrix products, arithmetic and copies ran while one was open for 11% -> 5% of each run, Pallas kernels for 10% -> 9%
where the time goes in v12:
time: 167 us
  waiting for transfers between devices  90.4 us (54%)
  starting transfers between devices  44.7 us (27%)
  Pallas kernels  16.7 us (10%)
  local copies, waits for them, and re-layouts  8.91 us (5%)
  other arithmetic  4.6 us (3%)
    ppermute x29, waiting for transfers between devices, hop(): return lax.ppermute(value, 'ctx', perm)  84.7 us
    ppermute x29, starting transfers between devices, hop(): return lax.ppermute(value, 'ctx', perm)  42 us
    pallas_call x6, Pallas kernels, call(): pl.pallas_call(kernel, out_shape=[jax.ShapeDtypeStruct(shape, dtype) for...  16.7 us
    ppermute x9, waiting for transfers between devices, swap_cores(): return lax.ppermute(value, 'tp', SWAP)  5.68 us
    unnamed x27, local copies, waits for them, and re-layouts  4.95 us
  transfers between devices with their start and end apart: 40, of which 19 were waited for; matrix products, arithmetic and copies ran while one was open for 5% of the time, Pallas kernels for 9%

profile of v12, /device:TPU:0, one launch (start us, length us, event | category | flops | bytes accessed | tf_op | source)
XLA Modules:
  0.0 166.5 jit_solution(17360346049069427218)
XLA Ops:
  0.7 2.0 %copy.54 = bf16[128,4,1024]{0,2,1:T(8,128)(2,1)S(1)} copy(bf16[128,4,1024]{2,1,0:T(4,128)(2,1)} %param.9) | data formatting | bytes 2097152 | tf_op args[1]
  3.9 2.9 %collective-permute-start.2 = (bf16[2,2,128,512]{3,2,1,0:T(8,128)(2,1)}, bf16[2,2,128,512]{3,2,1,0:T(8,128)(2,1)}, u32[]{:S(2)}, u32[]{:S(2)}) collective-permute-start(bf16[2,2,128,512]{3,2,1,0:T(8,128)(2,1)} %bitcast.13), channel_id=1, source_target_pairs={{0,2},{2,0},{4,6},{6,4},{8,10},{10,8},{12,14},{14,12},{16,18},{18,... | collective-permute-start | bytes 1572872 | tf_op jit(solution)/shard_map/ppermute | solution.py:106
  11.0 4.4 %collective-permute-done = bf16[64,2176]{1,0:T(8,128)(2,1)S(1)} collective-permute-done((bf16[64,2176]{1,0:T(8,128)(2,1)S(1)}, bf16[64,2176]{1,0:T(8,128)(2,1)S(1)}, u32[]{:S(2)}, u32[]{:S(2)}) %collective-permute-start) | collective-permute-done | bytes 278560 | tf_op jit(solution)/shard_map/ppermute | solution.py:106
  15.4 2.7 %collective-permute-start.4 = (bf16[128,2176]{1,0:T(8,128)(2,1)S(1)}, bf16[128,2176]{1,0:T(8,128)(2,1)S(1)}, u32[]{:S(2)}, u32[]{:S(2)}) collective-permute-start(bf16[128,2176]{1,0:T(8,128)(2,1)S(1)} %pad_maximum_fusion.1.refs_0_.refs_8_), channel_id=1, source_target_pairs={{0,16},{2,18},{4,20},{6,22},{8,24},{10,26},{12,28},{14,30},{16,0},... | collective-permute-start | bytes 1671176 | tf_op jit(solution)/shard_map/ppermute | solution.py:106
  24.7 9.9 %collective-permute-done.1 = bf16[1,1024,128]{2,1,0:T(8,128)(2,1)S(1)} collective-permute-done((bf16[1,1024,128]{2,1,0:T(8,128)(2,1)}, bf16[1,1024,128]{2,1,0:T(8,128)(2,1)S(1)}, u32[]{:S(2)}, u32[]{:S(2)}) %collective-permute-start.1) | collective-permute-done | bytes 262176 | tf_op jit(solution)/shard_map/ppermute | solution.py:106
  34.6 2.4 %collective-permute-start.5 = (bf16[64,1152]{1,0:T(8,128)(2,1)S(1)}, bf16[64,1152]{1,0:T(8,128)(2,1)S(1)}, u32[]{:S(2)}, u32[]{:S(2)}) collective-permute-start(bf16[64,1152]{1,0:T(8,128)(2,1)S(1)} %fusion.2), channel_id=1, source_target_pairs={{0,8},{2,10},{4,12},{6,14},{8,0},{10,2},{12,4},{14,6},{16,24},{18,... | collective-permute-start | bytes 442376 | tf_op jit(solution)/shard_map/ppermute | solution.py:106
  37.8 7.0 %collective-permute-done.5 = bf16[64,1152]{1,0:T(8,128)(2,1)S(1)} collective-permute-done((bf16[64,1152]{1,0:T(8,128)(2,1)S(1)}, bf16[64,1152]{1,0:T(8,128)(2,1)S(1)}, u32[]{:S(2)}, u32[]{:S(2)}) %collective-permute-start.5) | collective-permute-done | bytes 147488 | tf_op jit(solution)/shard_map/ppermute | solution.py:106
  50.5 10.9 %collective-permute-done.12.refs_3_ = bf16[128,2176]{1,0:T(8,128)(2,1)S(1)} collective-permute-done((bf16[128,2176]{1,0:T(8,128)(2,1)S(1)}, bf16[128,2176]{1,0:T(8,128)(2,1)S(1)}, u32[]{:S(2)}, u32[]{:S(2)}) %collective-permute-start.12) | collective-permute-done | bytes 557088 | tf_op jit(solution)/shard_map/ppermute | solution.py:106
  63.5 2.9 %collective-permute-done.11.refs_7_ = bf16[64,2176]{1,0:T(8,128)(2,1)S(1)} collective-permute-done((bf16[64,2176]{1,0:T(8,128)(2,1)S(1)}, bf16[64,2176]{1,0:T(8,128)(2,1)S(1)}, u32[]{:S(2)}, u32[]{:S(2)}) %collective-permute-start.11) | collective-permute-done | bytes 278560 | tf_op jit(solution)/shard_map/ppermute | solution.py:106
  67.1 3.9 %collective-permute-done.9.refs_6_.refs_11_ = bf16[64,2176]{1,0:T(8,128)(2,1)S(1)} collective-permute-done((bf16[64,2176]{1,0:T(8,128)(2,1)S(1)}, bf16[64,2176]{1,0:T(8,128)(2,1)S(1)}, u32[]{:S(2)}, u32[]{:S(2)}) %collective-permute-start.9) | collective-permute-done | bytes 278560 | tf_op jit(solution)/shard_map/ppermute | solution.py:106
  70.9 3.2 %collective-permute-done.13.refs_8_ = bf16[64,2176]{1,0:T(8,128)(2,1)S(1)} collective-permute-done((bf16[64,2176]{1,0:T(8,128)(2,1)S(1)}, bf16[64,2176]{1,0:T(8,128)(2,1)S(1)}, u32[]{:S(2)}, u32[]{:S(2)}) %collective-permute-start.13) | collective-permute-done | bytes 278560 | tf_op jit(solution)/shard_map/ppermute | solution.py:106
  74.7 5.8 %collective-permute-start.16 = (bf16[2,1024,128]{2,1,0:T(8,128)(2,1)S(1)}, bf16[2,1024,128]{2,1,0:T(8,128)(2,1)}, u32[]{:S(2)}, u32[]{:S(2)}) collective-permute-start(bf16[2,1024,128]{2,1,0:T(8,128)(2,1)S(1)} %constant_dynamic-update-slice_fusion.refs_4_), channel_id=1, source_target_pairs={{0,16},{2,18},{4,20},{6,22},{8,24},{10,26},{12,28},{14,30},{16,0},... | collective-permute-start | bytes 1572872 | tf_op jit(solution)/shard_map/ppermute | solution.py:106
  80.5 4.0 %project.1 = (bf16[1024,256]{1,0:T(8,128)(2,1)S(1)}, bf16[1024,128]{1,0:T(8,128)(2,1)S(1)}, bf16[1024,128]{1,0:T(8,128)(2,1)S(1)}, bf16[1024,128]{1,0:T(8,128)(2,1)S(1)}) custom-call(s32[4]{0:T(128)S(1)} %pad_add_fusion.where, bf16[128,2176]{1,0:T(8,128)(2,1)S(1)} %pad_maximum_fusion.1.refs_0_.refs_8_, bf16[128,2176]{1,0:T(8,128)(2,1)S(1)} %collective-permute-done.4.refs_1_, ...), custom_call_target="tpu_custom_call" | custom-call | flops 42949672960 | bytes 6553616 | tf_op jit(solution)/shard_map/project/pallas_call | solution.py:331
  87.2 3.4 %attend.1 = bf16[4,4,64,128]{3,2,1,0:T(8,128)(2,1)S(1)} custom-call(bf16[1024,256]{1,0:T(8,128)(2,1)S(1)} %get-tuple-element.40.refs_0_, bf16[1024,128]{1,0:T(8,128)(2,1)S(1)} %get-tuple-element.41.refs_1_, bf16[1024,128]{1,0:T(8,128)(2,1)S(1)} %get-tuple-element.38.refs_2_, bf16[1024,128]{1,0:T(8,128)(2,1)S(1)} %collective-permute-done.20.refs_3_, ...), custom_call_target="tpu_custom_call" | custom-call | bytes 1835008 | tf_op jit(solution)/shard_map/attend/pallas_call | solution.py:331
  90.6 13.4 %collective-permute-done.16.refs_5_ = bf16[2,1024,128]{2,1,0:T(8,128)(2,1)} collective-permute-done((bf16[2,1024,128]{2,1,0:T(8,128)(2,1)S(1)}, bf16[2,1024,128]{2,1,0:T(8,128)(2,1)}, u32[]{:S(2)}, u32[]{:S(2)}) %collective-permute-start.16) | collective-permute-done | bytes 524320 | tf_op jit(solution)/shard_map/ppermute | solution.py:106
  105.1 3.3 %collective-permute-start.24 = (bf16[4,64,128]{2,1,0:T(8,128)(2,1)S(1)}, bf16[4,64,128]{2,1,0:T(8,128)(2,1)S(1)}, u32[]{:S(2)}, u32[]{:S(2)}) collective-permute-start(bf16[4,64,128]{2,1,0:T(8,128)(2,1)S(1)} %get-tuple-element.75), channel_id=1, source_target_pairs={{0,24},{2,26},{4,28},{6,30},{8,16},{10,18},{12,20},{14,22},{16,8},... | collective-permute-start | bytes 196616 | tf_op jit(solution)/shard_map/ppermute | solution.py:106
  108.9 3.5 %collective-permute-done.23 = bf16[4,64,128]{2,1,0:T(8,128)(2,1)S(1)} collective-permute-done((bf16[4,64,128]{2,1,0:T(8,128)(2,1)S(1)}, bf16[4,64,128]{2,1,0:T(8,128)(2,1)S(1)}, u32[]{:S(2)}, u32[]{:S(2)}) %collective-permute-start.23) | collective-permute-done | bytes 65568 | tf_op jit(solution)/shard_map/ppermute | solution.py:106
  114.0 2.4 %collective-permute-start.27 = (bf16[4,4,64,128]{3,2,1,0:T(8,128)(2,1)S(1)}, bf16[4,4,64,128]{3,2,1,0:T(8,128)(2,1)S(1)}, u32[]{:S(2)}, u32[]{:S(2)}) collective-permute-start(bf16[4,4,64,128]{3,2,1,0:T(8,128)(2,1)S(1)} %pad_maximum_fusion.3.refs_0_), channel_id=1, source_target_pairs={{0,6},{2,4},{4,2},{6,0},{8,14},{10,12},{12,10},{14,8},{16,22},{18,... | collective-permute-start | bytes 786440 | tf_op jit(solution)/shard_map/ppermute | solution.py:106
  117.4 9.0 %collective-permute-done.34 = bf16[128,1152]{1,0:T(8,128)(2,1)} collective-permute-done((bf16[128,1152]{1,0:T(8,128)(2,1)}, bf16[128,1152]{1,0:T(8,128)(2,1)}, u32[]{:S(2)}, u32[]{:S(2)}) %collective-permute-start.34) | collective-permute-done | bytes 294944 | tf_op jit(solution)/shard_map/ppermute | solution.py:106
  130.6 3.0 %hidden.1 = bf16[4,64,512]{2,1,0:T(8,128)(2,1)S(1)} custom-call(s32[4]{0:T(128)S(1)} %pad_add_fusion.where, bf16[4,4,64,128]{3,2,1,0:T(8,128)(2,1)S(1)} %pad_maximum_fusion.3.refs_0_, bf16[4,4,64,128]{3,2,1,0:T(8,128)(2,1)S(1)} %collective-permute-done.25.refs_1_, bf16[4,4,64,128]{3,2,1,0:T(8,128)(2,1)S(1)} %collective-permute-done.26.refs_2_, ...), custom_call_target="tpu_custom_call" | custom-call | flops 536870912 | bytes 5095440 | tf_op jit(solution)/shard_map/hidden/pallas_call | solution.py:331
  137.2 8.2 %collective-permute-done.29.refs_1_ = bf16[64,512]{1,0:T(8,128)(2,1)S(1)} collective-permute-done((bf16[64,512]{1,0:T(8,128)(2,1)S(1)}, bf16[64,512]{1,0:T(8,128)(2,1)S(1)}, u32[]{:S(2)}, u32[]{:S(2)}) %collective-permute-start.29) | collective-permute-done | bytes 65568 | tf_op jit(solution)/shard_map/ppermute | solution.py:106
  148.8 5.6 %collective-permute-done.37 = bf16[128,1152]{1,0:T(8,128)(2,1)S(1)} collective-permute-done((bf16[128,1152]{1,0:T(8,128)(2,1)S(1)}, bf16[128,1152]{1,0:T(8,128)(2,1)S(1)}, u32[]{:S(2)}, u32[]{:S(2)}) %collective-permute-start.37) | collective-permute-done | bytes 294944 | tf_op jit(solution)/shard_map/ppermute | solution.py:106
  157.4 3.4 %collective-permute-done.39.n_other = bf16[1024,1152]{1,0:T(8,128)(2,1)} collective-permute-done((bf16[1024,1152]{1,0:T(8,128)(2,1)S(1)}, bf16[1024,1152]{1,0:T(8,128)(2,1)}, u32[]{:S(2)}, u32[]{:S(2)}) %collective-permute-start.39) | collective-permute-done | bytes 2359328 | tf_op jit(solution)/shard_map/ppermute | solution.py:110
  160.8 4.1 %loss.1 = f32[1,64]{1,0:T(1,128)} custom-call(bf16[64,1024]{1,0:T(8,128)(2,1)S(1)} %get-tuple-element.48.h_keep.keep, bf16[64,1024]{1,0:T(8,128)(2,1)S(1)} %get-tuple-element.49.h_send, bf16[64,1024]{1,0:T(8,128)(2,1)S(1)} %get-tuple-element.69.t_keep, bf16[64,1024]{1,0:T(8,128)(2,1)S(1)} %collective-permute-done.33.t_send, s32[64,1]{1,0:T(8,128)S(1)} %copy.60.t_ids, ...), custom_call_target="tpu_custom_call" | custom-call | flops 268435456 | bytes 5243136 | tf_op jit(solution)/shard_map/loss/pallas_call | solution.py:331
  (129 shorter events, 44.3 us)
Async XLA Ops:
  3.9 18.8 %collective-permute-start.2 = (bf16[2,2,128,512]{3,2,1,0:T(8,128)(2,1)}, bf16[2,2,128,512]{3,2,1,0:T(8,128)(2,1)}, u32[]{:S(2)}, u32[]{:S(2)}) collective-permute-start(bf16[2,2,128,512]{3,2,1,0:T(8,128)(2,1)} %bitcast.13), channel_id=1, source_target_pairs={{0,2},{2,0},{4,6},{6,4},{8,10},{10,8},{12,14},{14,12},{16,18},{18,... | collective-permute-start | bytes 1572872 | tf_op jit(solution)/shard_map/ppermute | solution.py:106
  15.4 30.1 %collective-permute-start.4 = (bf16[128,2176]{1,0:T(8,128)(2,1)S(1)}, bf16[128,2176]{1,0:T(8,128)(2,1)S(1)}, u32[]{:S(2)}, u32[]{:S(2)}) collective-permute-start(bf16[128,2176]{1,0:T(8,128)(2,1)S(1)} %pad_maximum_fusion.1.refs_0_.refs_8_), channel_id=1, source_target_pairs={{0,16},{2,18},{4,20},{6,22},{8,24},{10,26},{12,28},{14,30},{16,0},... | collective-permute-start | bytes 1671176 | tf_op jit(solution)/shard_map/ppermute | solution.py:106
  18.0 29.9 %collective-permute-start.10 = (bf16[128,2176]{1,0:T(8,128)(2,1)S(1)}, bf16[128,2176]{1,0:T(8,128)(2,1)S(1)}, u32[]{:S(2)}, u32[]{:S(2)}) collective-permute-start(bf16[128,2176]{1,0:T(8,128)(2,1)S(1)} %pad_maximum_fusion.1.refs_0_.refs_8_), channel_id=1, source_target_pairs={{0,4},{2,6},{4,0},{6,2},{8,12},{10,14},{12,8},{14,10},{16,20},{18,... | collective-permute-start | bytes 1671176 | tf_op jit(solution)/shard_map/ppermute | solution.py:106
  19.6 30.8 %collective-permute-start.8 = (bf16[128,2176]{1,0:T(8,128)(2,1)S(1)}, bf16[128,2176]{1,0:T(8,128)(2,1)S(1)}, u32[]{:S(2)}, u32[]{:S(2)}) collective-permute-start(bf16[128,2176]{1,0:T(8,128)(2,1)S(1)} %pad_maximum_fusion.1.refs_0_.refs_8_), channel_id=1, source_target_pairs={{0,2},{2,0},{4,6},{6,4},{8,10},{10,8},{12,14},{14,12},{16,18},{18,... | collective-permute-start | bytes 1671176 | tf_op jit(solution)/shard_map/ppermute | solution.py:106
  20.1 14.5 %collective-permute-start.1 = (bf16[1,1024,128]{2,1,0:T(8,128)(2,1)}, bf16[1,1024,128]{2,1,0:T(8,128)(2,1)S(1)}, u32[]{:S(2)}, u32[]{:S(2)}) collective-permute-start(bf16[1,1024,128]{2,1,0:T(8,128)(2,1)} %bitcast.4), channel_id=1, source_target_pairs={{0,8},{2,10},{4,12},{6,14},{8,0},{10,2},{12,4},{14,6},{16,24},{18,... | collective-permute-start | bytes 786440 | tf_op jit(solution)/shard_map/ppermute | solution.py:106
  24.1 21.3 %collective-permute-start.3 = (bf16[2,2,128,512]{3,2,1,0:T(8,128)(2,1)S(1)}, bf16[2,2,128,512]{3,2,1,0:T(8,128)(2,1)S(1)}, u32[]{:S(2)}, u32[]{:S(2)}) collective-permute-start(bf16[2,2,128,512]{3,2,1,0:T(8,128)(2,1)S(1)} %get-tuple-element.65), channel_id=1, source_target_pairs={{0,4},{2,6},{4,0},{6,2},{8,12},{10,14},{12,8},{14,10},{16,20},{18,... | collective-permute-start | bytes 1572872 | tf_op jit(solution)/shard_map/ppermute | solution.py:106
  45.8 15.6 %collective-permute-start.12 = (bf16[128,2176]{1,0:T(8,128)(2,1)S(1)}, bf16[128,2176]{1,0:T(8,128)(2,1)S(1)}, u32[]{:S(2)}, u32[]{:S(2)}) collective-permute-start(bf16[128,2176]{1,0:T(8,128)(2,1)S(1)} %collective-permute-done.4.refs_1_), channel_id=1, source_target_pairs={{0,2},{2,0},{4,6},{6,4},{8,10},{10,8},{12,14},{14,12},{16,18},{18,... | collective-permute-start | bytes 1671176 | tf_op jit(solution)/shard_map/ppermute | solution.py:106
  46.5 16.3 %collective-permute-start.14 = (bf16[128,2176]{1,0:T(8,128)(2,1)S(1)}, bf16[128,2176]{1,0:T(8,128)(2,1)S(1)}, u32[]{:S(2)}, u32[]{:S(2)}) collective-permute-start(bf16[128,2176]{1,0:T(8,128)(2,1)S(1)} %collective-permute-done.4.refs_1_), channel_id=1, source_target_pairs={{0,4},{2,6},{4,0},{6,2},{8,12},{10,14},{12,8},{14,10},{16,20},{18,... | collective-permute-start | bytes 1671176 | tf_op jit(solution)/shard_map/ppermute | solution.py:106
  47.9 18.4 %collective-permute-start.11 = (bf16[64,2176]{1,0:T(8,128)(2,1)S(1)}, bf16[64,2176]{1,0:T(8,128)(2,1)S(1)}, u32[]{:S(2)}, u32[]{:S(2)}) collective-permute-start(bf16[64,2176]{1,0:T(8,128)(2,1)S(1)} %slice.57), channel_id=1, source_target_pairs={{0,2},{2,0},{4,6},{6,4},{8,10},{10,8},{12,14},{14,12},{16,18},{18,... | collective-permute-start | bytes 835592 | tf_op jit(solution)/shard_map/ppermute | solution.py:106
  49.5 21.4 %collective-permute-start.6 = (bf16[4,128,512]{2,1,0:T(8,128)(2,1)S(1)}, bf16[4,128,512]{2,1,0:T(8,128)(2,1)S(1)}, u32[]{:S(2)}, u32[]{:S(2)}) collective-permute-start(bf16[4,128,512]{2,1,0:T(8,128)(2,1)S(1)} %get-tuple-element.32), channel_id=1, source_target_pairs={{0,0},{1,16},{2,2},{3,18},{4,4},{5,20},{6,6},{7,22},{8,8},{9,24},{... | collective-permute-start | bytes 1572872 | tf_op jit(solution)/shard_map/ppermute | solution.py:149
  50.4 20.6 %collective-permute-start.7 = (bf16[4,128,512]{2,1,0:T(8,128)(2,1)S(1)}, bf16[4,128,512]{2,1,0:T(8,128)(2,1)S(1)}, u32[]{:S(2)}, u32[]{:S(2)}) collective-permute-start(bf16[4,128,512]{2,1,0:T(8,128)(2,1)S(1)} %get-tuple-element.33), channel_id=1, source_target_pairs={{0,8},{1,24},{2,10},{3,26},{4,12},{5,28},{6,14},{7,30},{8,0},{9,16... | collective-permute-start | bytes 1572872 | tf_op jit(solution)/shard_map/ppermute | solution.py:149
  62.9 11.2 %collective-permute-start.13 = (bf16[64,2176]{1,0:T(8,128)(2,1)S(1)}, bf16[64,2176]{1,0:T(8,128)(2,1)S(1)}, u32[]{:S(2)}, u32[]{:S(2)}) collective-permute-start(bf16[64,2176]{1,0:T(8,128)(2,1)S(1)} %slice.58), channel_id=1, source_target_pairs={{0,4},{2,6},{4,0},{6,2},{8,12},{10,14},{12,8},{14,10},{16,20},{18,... | collective-permute-start | bytes 835592 | tf_op jit(solution)/shard_map/ppermute | solution.py:106
  74.7 29.3 %collective-permute-start.16 = (bf16[2,1024,128]{2,1,0:T(8,128)(2,1)S(1)}, bf16[2,1024,128]{2,1,0:T(8,128)(2,1)}, u32[]{:S(2)}, u32[]{:S(2)}) collective-permute-start(bf16[2,1024,128]{2,1,0:T(8,128)(2,1)S(1)} %constant_dynamic-update-slice_fusion.refs_4_), channel_id=1, source_target_pairs={{0,16},{2,18},{4,20},{6,22},{8,24},{10,26},{12,28},{14,30},{16,0},... | collective-permute-start | bytes 1572872 | tf_op jit(solution)/shard_map/ppermute | solution.py:106
  84.4 19.5 %collective-permute-start.19 = (bf16[2,1024,128]{2,1,0:T(8,128)(2,1)S(1)}, bf16[2,1024,128]{2,1,0:T(8,128)(2,1)S(1)}, u32[]{:S(2)}, u32[]{:S(2)}) collective-permute-start(bf16[2,1024,128]{2,1,0:T(8,128)(2,1)S(1)} %constant_dynamic-update-slice_fusion.refs_4_), channel_id=1, source_target_pairs={{0,1},{1,0},{2,3},{3,2},{4,5},{5,4},{6,7},{7,6},{8,9},{9,8},{10,11... | collective-permute-start | bytes 1572872 | tf_op jit(solution)/shard_map/ppermute | solution.py:110
  112.4 14.0 %collective-permute-start.34 = (bf16[128,1152]{1,0:T(8,128)(2,1)}, bf16[128,1152]{1,0:T(8,128)(2,1)}, u32[]{:S(2)}, u32[]{:S(2)}) collective-permute-start(bf16[128,1152]{1,0:T(8,128)(2,1)} %constant_dynamic-update-slice_fusion.2), channel_id=1, source_target_pairs={{0,16},{2,18},{4,20},{6,22},{8,24},{10,26},{12,28},{14,30},{16,0},... | collective-permute-start | bytes 884744 | tf_op jit(solution)/shard_map/ppermute | solution.py:106
  113.0 14.8 %collective-permute-start.28 = (bf16[2,1024,128]{2,1,0:T(8,128)(2,1)}, bf16[2,1024,128]{2,1,0:T(8,128)(2,1)}, u32[]{:S(2)}, u32[]{:S(2)}) collective-permute-start(bf16[2,1024,128]{2,1,0:T(8,128)(2,1)} %collective-permute-done.16.refs_5_), channel_id=1, source_target_pairs={{0,1},{1,0},{2,3},{3,2},{4,5},{5,4},{6,7},{7,6},{8,9},{9,8},{10,11... | collective-permute-start | bytes 1572872 | tf_op jit(solution)/shard_map/ppermute | solution.py:110
  113.0 14.8 %collective-permute-start.25 = (bf16[4,4,64,128]{3,2,1,0:T(8,128)(2,1)S(1)}, bf16[4,4,64,128]{3,2,1,0:T(8,128)(2,1)S(1)}, u32[]{:S(2)}, u32[]{:S(2)}) collective-permute-start(bf16[4,4,64,128]{3,2,1,0:T(8,128)(2,1)S(1)} %pad_maximum_fusion.3.refs_0_), channel_id=1, source_target_pairs={{0,2},{2,0},{4,6},{6,4},{8,10},{10,8},{12,14},{14,12},{16,18},{18,... | collective-permute-start | bytes 786440 | tf_op jit(solution)/shard_map/ppermute | solution.py:106
  113.5 14.3 %collective-permute-start.26 = (bf16[4,4,64,128]{3,2,1,0:T(8,128)(2,1)S(1)}, bf16[4,4,64,128]{3,2,1,0:T(8,128)(2,1)S(1)}, u32[]{:S(2)}, u32[]{:S(2)}) collective-permute-start(bf16[4,4,64,128]{3,2,1,0:T(8,128)(2,1)S(1)} %pad_maximum_fusion.3.refs_0_), channel_id=1, source_target_pairs={{0,4},{2,6},{4,0},{6,2},{8,12},{10,14},{12,8},{14,10},{16,20},{18,... | collective-permute-start | bytes 786440 | tf_op jit(solution)/shard_map/ppermute | solution.py:106
  114.0 13.8 %collective-permute-start.27 = (bf16[4,4,64,128]{3,2,1,0:T(8,128)(2,1)S(1)}, bf16[4,4,64,128]{3,2,1,0:T(8,128)(2,1)S(1)}, u32[]{:S(2)}, u32[]{:S(2)}) collective-permute-start(bf16[4,4,64,128]{3,2,1,0:T(8,128)(2,1)S(1)} %pad_maximum_fusion.3.refs_0_), channel_id=1, source_target_pairs={{0,6},{2,4},{4,2},{6,0},{8,14},{10,12},{12,10},{14,8},{16,22},{18,... | collective-permute-start | bytes 786440 | tf_op jit(solution)/shard_map/ppermute | solution.py:106
  127.8 18.7 %collective-permute-start.35 = (bf16[256,1152]{1,0:T(8,128)(2,1)S(1)}, bf16[256,1152]{1,0:T(8,128)(2,1)S(1)}, u32[]{:S(2)}, u32[]{:S(2)}) collective-permute-start(bf16[256,1152]{1,0:T(8,128)(2,1)S(1)} %pad_maximum_fusion), channel_id=1, source_target_pairs={{0,2},{2,0},{4,6},{6,4},{8,10},{10,8},{12,14},{14,12},{16,18},{18,... | collective-permute-start | bytes 1769480 | tf_op jit(solution)/shard_map/ppermute | solution.py:106
  129.0 17.4 %collective-permute-start.36 = (bf16[256,1152]{1,0:T(8,128)(2,1)S(1)}, bf16[256,1152]{1,0:T(8,128)(2,1)S(1)}, u32[]{:S(2)}, u32[]{:S(2)}) collective-permute-start(bf16[256,1152]{1,0:T(8,128)(2,1)S(1)} %pad_maximum_fusion), channel_id=1, source_target_pairs={{0,4},{2,6},{4,0},{6,2},{8,12},{10,14},{12,8},{14,10},{16,20},{18,... | collective-permute-start | bytes 1769480 | tf_op jit(solution)/shard_map/ppermute | solution.py:106
  133.6 11.8 %collective-permute-start.29 = (bf16[64,512]{1,0:T(8,128)(2,1)S(1)}, bf16[64,512]{1,0:T(8,128)(2,1)S(1)}, u32[]{:S(2)}, u32[]{:S(2)}) collective-permute-start(bf16[64,512]{1,0:T(8,128)(2,1)S(1)} %get-tuple-element.72), channel_id=1, source_target_pairs={{0,2},{2,0},{4,6},{6,4},{8,10},{10,8},{12,14},{14,12},{16,18},{18,... | collective-permute-start | bytes 196616 | tf_op jit(solution)/shard_map/ppermute | solution.py:106
  134.9 11.5 %collective-permute-start.30 = (bf16[64,512]{1,0:T(8,128)(2,1)S(1)}, bf16[64,512]{1,0:T(8,128)(2,1)S(1)}, u32[]{:S(2)}, u32[]{:S(2)}) collective-permute-start(bf16[64,512]{1,0:T(8,128)(2,1)S(1)} %get-tuple-element.71), channel_id=1, source_target_pairs={{0,4},{2,6},{4,0},{6,2},{8,12},{10,14},{12,8},{14,10},{16,20},{18,... | collective-permute-start | bytes 196616 | tf_op jit(solution)/shard_map/ppermute | solution.py:106
  136.1 10.4 %collective-permute-start.31 = (bf16[64,512]{1,0:T(8,128)(2,1)S(1)}, bf16[64,512]{1,0:T(8,128)(2,1)S(1)}, u32[]{:S(2)}, u32[]{:S(2)}) collective-permute-start(bf16[64,512]{1,0:T(8,128)(2,1)S(1)} %get-tuple-element.70), channel_id=1, source_target_pairs={{0,6},{2,4},{4,2},{6,0},{8,14},{10,12},{12,10},{14,8},{16,22},{18,... | collective-permute-start | bytes 196616 | tf_op jit(solution)/shard_map/ppermute | solution.py:106
  (26 other events, 232.1 us)

commit v13 on v12

--- a/solution.py
+++ b/solution.py
@@ -127,10 +127,11 @@
     return [hop(value_x[:half], flip(1, 0)), hop(value_y[half:], flip(0, 1))]
 
 
-def heads_in_plane(w_proj, y, x):
+def heads_in_plane(w_proj, y, x, first):
     heads = w_proj.reshape(-1, 4, 2, NY, NX, W).transpose(4, 3, 2, 0, 1, 5)
     heads = heads.reshape(NX, NY, 2, -1, 4 * W)
-    kept, came = pick_row(heads, x), hop(pick_row(heads, x ^ 1), flip(0, 1))
+    kept, sent = pick_row(heads, x), after(pick_row(heads, x ^ 1), first)
+    came = hop(sent, flip(0, 1))
     lined = jnp.where(x == 0, jnp.stack([kept, came], 1), jnp.stack([came, kept], 1))
     kept, came = pick_row(lined, y), hop(pick_row(lined, y ^ 1), flip(1, 0))
     whole = jnp.where(y == 0, jnp.stack([kept, came]), jnp.stack([came, kept]))
@@ -271,58 +272,66 @@
             hidden[k, :, cols] = (t_all[k, :, s * W : (s + 1) * W].astype(F32) + term).astype(BF16)
 
 
-def order_kernel(where, *refs):
-    pieces, (keep, send, h_all) = refs[: len(PLANE)], refs[len(PLANE) :]
-    y, x, u = (where[i] for i in range(1, 4))
-    half = keep.shape[1]
-    for (by, bx), ref in zip(PLANE, pieces):
-        for at in range(NZ):
-            block = chip_at(at, y ^ by, x ^ bx)
-            h_all[:, pl.ds(pl.multiple_of(block * W, W), W)] = ref[:, at * W : (at + 1) * W]
-    keep[...] = h_all[:, pl.ds(pl.multiple_of(u * half, half), half)]
-    send[...] = h_all[:, pl.ds(pl.multiple_of((1 - u) * half, half), half)]
-
-
-def loss_kernel(h_keep, h_send, t_keep, t_send, t_ids, n_own, n_other, loss, n_all, sems):
-    keep, send = h_keep[...], h_send[...]
-    half = keep.shape[1]
-    copies = []
-    for side, src in enumerate((n_own, n_other)):
-        copies.append(pltpu.make_async_copy(src, n_all.at[side], sems.at[side]))
-    for copy in copies:
-        copy.start()
-    hh = he = ee = 0.0
-    for part, ref in ((keep, t_keep), (send, t_send)):
-        h_f, t_f = part.astype(F32), ref[...].astype(F32)
-        hh += jnp.sum(h_f * h_f, axis=1, keepdims=True)
-        he += jnp.sum(h_f * t_f, axis=1, keepdims=True)
-        ee += jnp.sum(t_f * t_f, axis=1, keepdims=True)
-    h_scale = lax.rsqrt(hh + 1e-06) * 20.0
-    pos_logit = he * lax.rsqrt(ee + 1e-06) * h_scale
-    for copy in copies:
-        copy.wait()
-    pick = pick_columns({0: 1.0, 1: 1.0, 2: 1.0}, {3: 256.0, 4: 1.0})
-    dots, read = 0.0, []
-    for side, part in enumerate((keep, send)):
-        neg, marks = n_all[side, :, :half], n_all[side, :, half:]
-        dots += lax.dot_general(part, neg, ACROSS, preferred_element_type=F32)
-        read.append(lax.dot_general(pick, marks, ACROSS, preferred_element_type=F32))
-    nn = read[0][0:1] + read[1][0:1]
-    n_ids = read[0][1:2]
-    neg_logit = dots * h_scale * lax.rsqrt(nn + 1e-06)
-    mass = jnp.where(n_ids != t_ids[...].astype(F32), jnp.exp(neg_logit), 0.0)
-    total = jnp.exp(pos_logit) + jnp.sum(mass, axis=1, keepdims=True)
-    column = jnp.log(total) - pos_logit
+def as_line(column):
     size = column.shape[0]
     line = lax.broadcasted_iota(jnp.int32, (size, size), 0)
     lane = lax.broadcasted_iota(jnp.int32, (size, size), 1)
-    loss[...] = jnp.sum(jnp.where(line == lane, column, 0.0), axis=0, keepdims=True)
-
-
-def join_kernel(where, keep, theirs, hidden):
+    return jnp.sum(jnp.where(line == lane, column, 0.0), axis=0, keepdims=True)
+
+
+def mass_kernel(where, *refs):
+    n = len(PLANE)
+    pieces, (n_own, n_other, t_keep, t_send, marks) = refs[:n], refs[n : n + 5]
+    keep, send, positive, mass, h_all = refs[n + 5 :]
+    y, x, u = (where[i] for i in range(1, 4))
+    rows, half = keep.shape
+    for k, (by, bx) in enumerate(PLANE):
+        for at in range(NZ):
+            block = chip_at(at, y ^ by, x ^ bx)
+            cols = pl.ds(pl.multiple_of(block * W, W), W)
+            for j in range(n):
+                row = (j ^ k) * rows
+                h_all[row : row + rows, cols] = pieces[k][j, :, at * W : (at + 1) * W]
+    mine = pl.ds(pl.multiple_of(u * half, half), half)
+    theirs = pl.ds(pl.multiple_of((1 - u) * half, half), half)
+    keep[...] = h_all[:rows, mine]
+    send[...] = h_all[:rows, theirs]
+    hh, dots, lines = 0.0, 0.0, []
+    pick = pick_columns({0: 1.0, 1: 1.0, 2: 1.0}, {3: 256.0, 4: 1.0})
+    for part, neg in ((mine, n_own), (theirs, n_other)):
+        h_part = h_all[:, part]
+        h_f = h_part.astype(F32)
+        hh += jnp.sum(h_f * h_f, axis=1, keepdims=True)
+        dots += lax.dot_general(h_part, neg[:, :half], ACROSS, preferred_element_type=F32)
+        lines.append(lax.dot_general(pick, neg[:, half:], ACROSS, preferred_element_type=F32))
+    h_scale = lax.rsqrt(hh + 1e-06) * 20.0
+    he = ee = 0.0
+    for h_ref, ref in ((keep, t_keep), (send, t_send)):
+        h_f, t_f = h_ref[...].astype(F32), ref[...].astype(F32)
+        he += jnp.sum(h_f * t_f, axis=1, keepdims=True)
+        ee += jnp.sum(t_f * t_f, axis=1, keepdims=True)
+    positive[...] = as_line(he * lax.rsqrt(ee + 1e-06) * h_scale[:rows])
+    first = [marks[k * NZ * rows : (k * NZ + 1) * rows] for k in range(n)]
+    pick = pick_columns({4: 256.0, 5: 1.0})
+    t_ids = lax.dot_general(
+        jnp.concatenate(first), pick, ACROSS, preferred_element_type=F32
+    )[:, :1]
+    neg_logit = dots * h_scale * lax.rsqrt(lines[0][0:1] + lines[1][0:1] + 1e-06)
+    kept = jnp.where(lines[0][1:2] != t_ids, jnp.exp(neg_logit), 0.0)
+    total = jnp.sum(kept, axis=1, keepdims=True)
+    for k in range(n):
+        mass[k] = as_line(total[k * rows : (k + 1) * rows])
+
+
+def final_kernel(where, keep, theirs, positive, *refs):
+    masses, (hidden, loss) = refs[:-2], refs[-2:]
     u, rows = where[3], keep.shape[0]
     hidden[pl.ds(pl.multiple_of(u * rows, rows), rows), :] = keep[...]
     hidden[pl.ds(pl.multiple_of((1 - u) * rows, rows), rows), :] = theirs[...]
+    total = jnp.exp(positive[...])
+    for mass in masses:
+        total += mass[...]
+    loss[...] = jnp.log(total) - positive[...]
 
 
 def call(kernel, name, outs, scratch, args, places, flops):
@@ -374,12 +383,13 @@
     mine = lax.dynamic_slice_in_dim(tokens, u * rows, rows, 0)
     p_own = lax.dynamic_slice_in_dim(positions, u * rows, rows, 0)
     p_other = lax.dynamic_slice_in_dim(positions, (1 - u) * rows, rows, 0)
-    mine = with_marks(mine, whole_parts(p_own, 128) + whole_parts(p_other, 128))
+    ids = whole_parts(target_ids, 256)
+    mine = with_marks(mine, whole_parts(p_own, 128) + whole_parts(p_other, 128) + ids)
     low = pair_up(mine)
 
     to_x, to_y = flip(0, 1), flip(1, 0)
     high = hop(low, flip(0, 0, 2))
-    w_plane = heads_in_plane(w_proj, y, x)
+    w_plane = heads_in_plane(w_proj, y, x, low)
     w_pieces = [pick_row(w_plane, e ^ (z & 1)) for e in range(2)]
     low_x, low_y = hop(low, to_x), hop(low, to_y)
     low_xy = across(low_x, low_y)
@@ -388,15 +398,15 @@
     own_ids = lax.dynamic_slice_in_dim(neg_ids, c * negs, negs, 0)
     norms = jnp.sum(jnp.square(neg_emb.astype(F32)), axis=1)
     neg = with_marks(neg_emb, float_parts(norms) + whole_parts(own_ids, 256))
-    neg_pair = pair_up(after(neg, out_pair))
-
-    w_pieces, high = lax.optimization_barrier((w_pieces, after(high, neg_pair)))
+
+    w_pieces, high = lax.optimization_barrier((w_pieces, after(high, out_pair)))
     high_x, high_y = hop(high, to_x), hop(high, to_y)
     high_xy = across(high_x, high_y)
     tok = [low, high, low_x, high_x, low_y, high_y, *low_xy, *high_xy]
     w_mine = after(heads_along_z(w_pieces), low_xy, high_xy)
     w_theirs = [swap_cores(w) for w in w_mine]
     out_own = [out_pair, hop(after(out_pair, w_mine), flip(0, 0, 2))]
+    neg_pair = pair_up(after(neg, w_mine))
     t_rows = after(target_emb.reshape(2, rows, -1), w_theirs)
     t_keep = pick_row(t_rows, u)
     t_send = swap_cores(pick_row(t_rows, 1 - u))
@@ -415,7 +425,7 @@
             ],
             [where, *pieces, *w_mine, *w_theirs],
             "s" + (len(pieces) + 4) * "h",
-            20 * 2 * count * model * 4 * W,
+            0,
         )
 
     gate_query, value, key, marks = project(tok)
@@ -437,8 +447,6 @@
     neg_far = hop(after(neg_pair, gated), flip(0, 0, 2))
     out_other = [out_pair_theirs, swap_cores(after(out_own[1], gated))]
     gated = [gated] + [hop(gated, flip(by, bx)) for by, bx in PLANE[1:]]
-    neg_near = after(jnp.concatenate([neg_pair, neg_far]), gated, out_other, t_send)
-    neg_x, neg_y = hop(neg_near, to_x), hop(neg_near, to_y)
     (hidden,) = call(
         hidden_kernel,
         "hidden",
@@ -454,39 +462,27 @@
         "s" + 12 * "h",
         2 * plane * rows * model * NZ * W,
     )
-    pieces = [hidden[0]] + [hop(hidden[k], flip(*PLANE[k])) for k in range(1, plane)]
-    neg_own = [neg_near, neg_x, neg_y, *across(*after((neg_x, neg_y), pieces))]
-    neg_own = jnp.concatenate(neg_own)
+    neg_own = jnp.concatenate([neg_pair, after(neg_far, hidden, t_send)])
     neg_other = swap_cores(neg_own)
-    h_keep, h_send = call(
-        order_kernel,
-        "order",
-        [((rows, half), BF16)] * 2,
-        [pltpu.VMEM((rows, model), BF16)],
-        [where, *pieces],
-        "svvvv",
-        0,
-    )
+    pieces = [hidden] + [hop(hidden, flip(by, bx)) for by, bx in PLANE[1:]]
+    h_keep, h_send, positive, mass = call(
+        mass_kernel,
+        "mass",
+        [((rows, half), BF16)] * 2 + [((1, rows), F32), ((plane, 1, rows), F32)],
+        [pltpu.VMEM((plane * rows, model), BF16)],
+        [where, *pieces, neg_own, neg_other, t_keep, t_send, marks],
+        "s" + 9 * "v",
+        2 * plane * rows * model * NZ * negs,
+    )
+    masses = [mass[0]] + [hop(mass[k], flip(*PLANE[k])) for k in range(1, plane)]
     h_theirs = swap_cores(h_send)
-    (loss,) = call(
-        loss_kernel,
-        "loss",
-        [((1, rows), F32)],
-        [
-            pltpu.VMEM((2, CHIPS * negs, half + W), BF16),
-            pltpu.SemaphoreType.DMA((2,)),
-        ],
-        [h_keep, h_send, t_keep, t_send, target_ids[:, None], neg_own, neg_other],
-        "vvvvvhh",
-        2 * rows * model * neg_ids.shape[0],
-    )
-    (hidden,) = call(
-        join_kernel,
-        "join",
-        [((2 * rows, half), BF16)],
+    hidden, loss = call(
+        final_kernel,
+        "final",
+        [((2 * rows, half), BF16), ((1, rows), F32)],
         [],
-        [where, h_keep, after(h_theirs, loss)],
-        "svv",
+        [where, h_keep, h_theirs, positive, *masses],
+        "s" + 7 * "v",
         0,
     )
     return hidden, loss.reshape(-1)

time: 167 us -> 163 us (0.976)
  other arithmetic: 4.6 us -> 10.2 us
  waiting for transfers between devices: 90.4 us -> 86.6 us
  local copies, waits for them, and re-layouts: 8.91 us -> 6.2 us
  Pallas kernels: 16.7 us -> 14.8 us
    ppermute x9, waiting for transfers between devices: 5.68 us -> 0.02 us  [swap_cores(): return lax.ppermute(value, 'tp', SWAP)]
    ppermute x29 -> x28, starting transfers between devices: 42 us -> 39 us  [hop(): return lax.ppermute(value, 'ctx', perm)]
    another operation x5, other arithmetic: 1.64 us -> 4.36 us  [with_marks(): marks = jnp.stack(marks, 1)]
    ppermute x2, starting transfers between devices: 0.93 us -> 3.64 us  [heads_along_z(): lax.ppermute(piece, ('ctx', 'tp'), perm).reshape(-1, piece.shape[-1])]
    unnamed x27 -> x28, local copies, waits for them, and re-layouts: 4.95 us -> 2.9 us
    pallas_call x6 -> x5, Pallas kernels: 16.7 us -> 14.8 us  [call(): pl.pallas_call(kernel, out_shape=[jax.ShapeDtypeStruct(shape, dtype) for...]
    ppermute x29 -> x28, waiting for transfers between devices: 84.7 us -> 86.6 us  [hop(): return lax.ppermute(value, 'ctx', perm)]
  transfers between devices with their start and end apart: 40 -> 39, of which waited for: 19 -> 20; matrix products, arithmetic and copies ran while one was open for 5% -> 6% of each run, Pallas kernels for 9% -> 7%
where the time goes in v13:
time: 163 us
  waiting for transfers between devices  86.6 us (53%)
  starting transfers between devices  43.9 us (27%)
  Pallas kernels  14.8 us (9%)
  other arithmetic  10.2 us (6%)
  local copies, waits for them, and re-layouts  6.2 us (4%)
    ppermute x28, waiting for transfers between devices, hop(): return lax.ppermute(value, 'ctx', perm)  86.6 us
    ppermute x28, starting transfers between devices, hop(): return lax.ppermute(value, 'ctx', perm)  39 us
    pallas_call x5, Pallas kernels, call(): pl.pallas_call(kernel, out_shape=[jax.ShapeDtypeStruct(shape, dtype) for...  14.8 us
    another operation x5, other arithmetic, with_marks(): marks = jnp.stack(marks, 1)  4.36 us
    ppermute x2, starting transfers between devices, heads_along_z(): lax.ppermute(piece, ('ctx', 'tp'), perm).reshape(-1, piece.shape[-1])  3.64 us
  transfers between devices with their start and end apart: 39, of which 20 were waited for; matrix products, arithmetic and copies ran while one was open for 6% of the time, Pallas kernels for 7%

profile of v13, /device:TPU:0, one launch (start us, length us, event | category | flops | bytes accessed | tf_op | source)
XLA Modules:
  0.0 162.7 jit_solution(11671593457245489391)
XLA Ops:
  5.2 3.0 %collective-permute-start = (bf16[64,2176]{1,0:T(8,128)(2,1)}, bf16[64,2176]{1,0:T(8,128)(2,1)}, u32[]{:S(2)}, u32[]{:S(2)}) collective-permute-start(bf16[64,2176]{1,0:T(8,128)(2,1)} %pad_maximum_fusion.2), channel_id=1, source_target_pairs={{0,8},{2,10},{4,12},{6,14},{8,0},{10,2},{12,4},{14,6},{16,24},{18,... | collective-permute-start | bytes 835592 | tf_op jit(solution)/shard_map/ppermute | solution.py:106
  9.6 5.6 %collective-permute-done = bf16[64,2176]{1,0:T(8,128)(2,1)} collective-permute-done((bf16[64,2176]{1,0:T(8,128)(2,1)}, bf16[64,2176]{1,0:T(8,128)(2,1)}, u32[]{:S(2)}, u32[]{:S(2)}) %collective-permute-start) | collective-permute-done | bytes 278560 | tf_op jit(solution)/shard_map/ppermute | solution.py:106
  16.2 1.7 %collective-permute-start.2 = (bf16[2,2,128,512]{3,2,1,0:T(8,128)(2,1)S(1)}, bf16[2,2,128,512]{3,2,1,0:T(8,128)(2,1)}, u32[]{:S(2)}, u32[]{:S(2)}) collective-permute-start(bf16[2,2,128,512]{3,2,1,0:T(8,128)(2,1)S(1)} %bitcast.78), channel_id=1, source_target_pairs={{0,2},{2,0},{4,6},{6,4},{8,10},{10,8},{12,14},{14,12},{16,18},{18,... | collective-permute-start | bytes 1572872 | tf_op jit(solution)/shard_map/ppermute | solution.py:106
  18.2 2.7 %collective-permute-start.4 = (bf16[128,2176]{1,0:T(8,128)(2,1)S(1)}, bf16[128,2176]{1,0:T(8,128)(2,1)S(1)}, u32[]{:S(2)}, u32[]{:S(2)}) collective-permute-start(bf16[128,2176]{1,0:T(8,128)(2,1)S(1)} %pad_maximum_fusion.refs_0_.refs_8_), channel_id=1, source_target_pairs={{0,16},{2,18},{4,20},{6,22},{8,24},{10,26},{12,28},{14,30},{16,0},... | collective-permute-start | bytes 1671176 | tf_op jit(solution)/shard_map/ppermute | solution.py:106
  20.8 8.7 %collective-permute-done.2 = bf16[2,2,128,512]{3,2,1,0:T(8,128)(2,1)} collective-permute-done((bf16[2,2,128,512]{3,2,1,0:T(8,128)(2,1)S(1)}, bf16[2,2,128,512]{3,2,1,0:T(8,128)(2,1)}, u32[]{:S(2)}, u32[]{:S(2)}) %collective-permute-start.2) | collective-permute-done | bytes 524320 | tf_op jit(solution)/shard_map/ppermute | solution.py:106
  36.9 13.1 %collective-permute-done.1 = bf16[1,1024,128]{2,1,0:T(8,128)(2,1)} collective-permute-done((bf16[1,1024,128]{2,1,0:T(8,128)(2,1)S(1)}, bf16[1,1024,128]{2,1,0:T(8,128)(2,1)}, u32[]{:S(2)}, u32[]{:S(2)}) %collective-permute-start.1) | collective-permute-done | bytes 262176 | tf_op jit(solution)/shard_map/ppermute | solution.py:106
  56.7 2.8 %collective-permute-start.6 = (bf16[4,128,512]{2,1,0:T(8,128)(2,1)S(1)}, bf16[4,128,512]{2,1,0:T(8,128)(2,1)S(1)}, u32[]{:S(2)}, u32[]{:S(2)}) collective-permute-start(bf16[4,128,512]{2,1,0:T(8,128)(2,1)S(1)} %get-tuple-element.35), channel_id=1, source_target_pairs={{0,8},{1,24},{2,10},{3,26},{4,12},{5,28},{6,14},{7,30},{8,0},{9,16... | collective-permute-start | bytes 1572872 | tf_op jit(solution)/shard_map/ppermute | solution.py:150
  59.5 7.9 %collective-permute-done.11.refs_3_ = bf16[128,2176]{1,0:T(8,128)(2,1)S(1)} collective-permute-done((bf16[128,2176]{1,0:T(8,128)(2,1)S(1)}, bf16[128,2176]{1,0:T(8,128)(2,1)S(1)}, u32[]{:S(2)}, u32[]{:S(2)}) %collective-permute-start.11) | collective-permute-done | bytes 557088 | tf_op jit(solution)/shard_map/ppermute | solution.py:106
  70.4 4.6 %collective-permute-done.8.refs_6_.refs_11_ = bf16[64,2176]{1,0:T(8,128)(2,1)S(1)} collective-permute-done((bf16[64,2176]{1,0:T(8,128)(2,1)S(1)}, bf16[64,2176]{1,0:T(8,128)(2,1)S(1)}, u32[]{:S(2)}, u32[]{:S(2)}) %collective-permute-start.8) | collective-permute-done | bytes 278560 | tf_op jit(solution)/shard_map/ppermute | solution.py:106
  76.4 3.8 %collective-permute-done.12.refs_8_ = bf16[64,2176]{1,0:T(8,128)(2,1)S(1)} collective-permute-done((bf16[64,2176]{1,0:T(8,128)(2,1)S(1)}, bf16[64,2176]{1,0:T(8,128)(2,1)S(1)}, u32[]{:S(2)}, u32[]{:S(2)}) %collective-permute-start.12) | collective-permute-done | bytes 278560 | tf_op jit(solution)/shard_map/ppermute | solution.py:106
  80.2 1.9 %collective-permute-done.14.refs_9_ = bf16[64,2176]{1,0:T(8,128)(2,1)S(1)} collective-permute-done((bf16[64,2176]{1,0:T(8,128)(2,1)S(1)}, bf16[64,2176]{1,0:T(8,128)(2,1)S(1)}, u32[]{:S(2)}, u32[]{:S(2)}) %collective-permute-start.14) | collective-permute-done | bytes 278560 | tf_op jit(solution)/shard_map/ppermute | solution.py:106
  82.8 3.2 %collective-permute-start.15 = (bf16[2,1024,128]{2,1,0:T(8,128)(2,1)S(1)}, bf16[2,1024,128]{2,1,0:T(8,128)(2,1)}, u32[]{:S(2)}, u32[]{:S(2)}) collective-permute-start(bf16[2,1024,128]{2,1,0:T(8,128)(2,1)S(1)} %constant_dynamic-update-slice_fusion.refs_4_), channel_id=1, source_target_pairs={{0,16},{2,18},{4,20},{6,22},{8,24},{10,26},{12,28},{14,30},{16,0},... | collective-permute-start | bytes 1572872 | tf_op jit(solution)/shard_map/ppermute | solution.py:106
  86.0 4.7 %project.1 = (bf16[1024,256]{1,0:T(8,128)(2,1)S(1)}, bf16[1024,128]{1,0:T(8,128)(2,1)S(1)}, bf16[1024,128]{1,0:T(8,128)(2,1)}, bf16[1024,128]{1,0:T(8,128)(2,1)S(1)}) custom-call(s32[4]{0:T(128)S(1)} %pad_add_fusion.where, bf16[128,2176]{1,0:T(8,128)(2,1)S(1)} %pad_maximum_fusion.refs_0_.refs_8_, bf16[128,2176]{1,0:T(8,128)(2,1)S(1)} %copy-done.2, ...), custom_call_target="tpu_custom_call" | custom-call | bytes 6553616 | tf_op jit(solution)/shard_map/project/pallas_call | solution.py:340
  95.6 4.4 %attend.1 = bf16[4,4,64,128]{3,2,1,0:T(8,128)(2,1)S(1)} custom-call(bf16[1024,256]{1,0:T(8,128)(2,1)S(1)} %copy-done.4, bf16[1024,128]{1,0:T(8,128)(2,1)} %get-tuple-element.43.refs_1_, bf16[1024,128]{1,0:T(8,128)(2,1)S(1)} %get-tuple-element.40.refs_2_, bf16[1024,128]{1,0:T(8,128)(2,1)} %collective-permute-done.19.refs_3_, ...), custom_call_target="tpu_custom_call" | custom-call | bytes 1835008 | tf_op jit(solution)/shard_map/attend/pallas_call | solution.py:340
  100.1 9.5 %collective-permute-done.15.refs_5_ = bf16[2,1024,128]{2,1,0:T(8,128)(2,1)} collective-permute-done((bf16[2,1024,128]{2,1,0:T(8,128)(2,1)S(1)}, bf16[2,1024,128]{2,1,0:T(8,128)(2,1)}, u32[]{:S(2)}, u32[]{:S(2)}) %collective-permute-start.15) | collective-permute-done | bytes 524320 | tf_op jit(solution)/shard_map/ppermute | solution.py:106
  109.6 2.3 %collective-permute-start.23 = (bf16[4,64,128]{2,1,0:T(8,128)(2,1)S(1)}, bf16[4,64,128]{2,1,0:T(8,128)(2,1)S(1)}, u32[]{:S(2)}, u32[]{:S(2)}) collective-permute-start(bf16[4,64,128]{2,1,0:T(8,128)(2,1)S(1)} %get-tuple-element.75), channel_id=1, source_target_pairs={{0,24},{2,26},{4,28},{6,30},{8,16},{10,18},{12,20},{14,22},{16,8},... | collective-permute-start | bytes 196616 | tf_op jit(solution)/shard_map/ppermute | solution.py:106
  111.9 2.1 %collective-permute-start.21 = (bf16[4,64,128]{2,1,0:T(8,128)(2,1)S(1)}, bf16[4,64,128]{2,1,0:T(8,128)(2,1)S(1)}, u32[]{:S(2)}, u32[]{:S(2)}) collective-permute-start(bf16[4,64,128]{2,1,0:T(8,128)(2,1)S(1)} %get-tuple-element.77), channel_id=1, source_target_pairs={{0,8},{2,10},{4,12},{6,14},{8,0},{10,2},{12,4},{14,6},{16,24},{18,... | collective-permute-start | bytes 196616 | tf_op jit(solution)/shard_map/ppermute | solution.py:106
  114.1 2.1 %collective-permute-done.23 = bf16[4,64,128]{2,1,0:T(8,128)(2,1)S(1)} collective-permute-done((bf16[4,64,128]{2,1,0:T(8,128)(2,1)S(1)}, bf16[4,64,128]{2,1,0:T(8,128)(2,1)S(1)}, u32[]{:S(2)}, u32[]{:S(2)}) %collective-permute-start.23) | collective-permute-done | bytes 65568 | tf_op jit(solution)/shard_map/ppermute | solution.py:106
  122.9 3.7 %collective-permute-done.24.refs_1_ = bf16[4,4,64,128]{3,2,1,0:T(8,128)(2,1)S(1)} collective-permute-done((bf16[4,4,64,128]{3,2,1,0:T(8,128)(2,1)S(1)}, bf16[4,4,64,128]{3,2,1,0:T(8,128)(2,1)S(1)}, u32[]{:S(2)}, u32[]{:S(2)}) %collective-permute-start.24) | collective-permute-done | bytes 262176 | tf_op jit(solution)/shard_map/ppermute | solution.py:106
  126.5 7.3 %collective-permute-done.25.refs_2_ = bf16[4,4,64,128]{3,2,1,0:T(8,128)(2,1)S(1)} collective-permute-done((bf16[4,4,64,128]{3,2,1,0:T(8,128)(2,1)S(1)}, bf16[4,4,64,128]{3,2,1,0:T(8,128)(2,1)S(1)}, u32[]{:S(2)}, u32[]{:S(2)}) %collective-permute-start.25) | collective-permute-done | bytes 262176 | tf_op jit(solution)/shard_map/ppermute | solution.py:106
  133.8 2.9 %hidden.1.refs_0_ = bf16[4,64,512]{2,1,0:T(8,128)(2,1)S(1)} custom-call(s32[4]{0:T(128)S(1)} %pad_add_fusion.where, bf16[4,4,64,128]{3,2,1,0:T(8,128)(2,1)S(1)} %pad_maximum_fusion.3.refs_0_, bf16[4,4,64,128]{3,2,1,0:T(8,128)(2,1)S(1)} %collective-permute-done.24.refs_1_, bf16[4,4,64,128]{3,2,1,0:T(8,128)(2,1)S(1)} %collective-permute-done.25.refs_2_, ...), custom_call_target="tpu_custom_call" | custom-call | flops 536870912 | bytes 5095440 | tf_op jit(solution)/shard_map/hidden/pallas_call | solution.py:340
  141.2 5.6 %collective-permute-done.28.refs_1_ = bf16[4,64,512]{2,1,0:T(8,128)(2,1)S(1)} collective-permute-done((bf16[4,64,512]{2,1,0:T(8,128)(2,1)S(1)}, bf16[4,64,512]{2,1,0:T(8,128)(2,1)S(1)}, u32[]{:S(2)}, u32[]{:S(2)}) %collective-permute-start.28) | collective-permute-done | bytes 262176 | tf_op jit(solution)/shard_map/ppermute | solution.py:106
  146.8 6.4 %collective-permute-done.29.refs_2_ = bf16[4,64,512]{2,1,0:T(8,128)(2,1)S(1)} collective-permute-done((bf16[4,64,512]{2,1,0:T(8,128)(2,1)S(1)}, bf16[4,64,512]{2,1,0:T(8,128)(2,1)S(1)}, u32[]{:S(2)}, u32[]{:S(2)}) %collective-permute-start.29) | collective-permute-done | bytes 262176 | tf_op jit(solution)/shard_map/ppermute | solution.py:106
  159.7 1.7 %collective-permute-done.38.refs_3_ = f32[1,64]{1,0:T(1,128)S(1)} collective-permute-done((f32[1,64]{1,0:T(1,128)S(1)}, f32[1,64]{1,0:T(1,128)S(1)}, u32[]{:S(2)}, u32[]{:S(2)}) %collective-permute-start.38) | collective-permute-done | bytes 288 | tf_op jit(solution)/shard_map/ppermute | solution.py:106
  (124 shorter events, 50.3 us)
Async XLA Ops:
  5.2 10.0 %collective-permute-start = (bf16[64,2176]{1,0:T(8,128)(2,1)}, bf16[64,2176]{1,0:T(8,128)(2,1)}, u32[]{:S(2)}, u32[]{:S(2)}) collective-permute-start(bf16[64,2176]{1,0:T(8,128)(2,1)} %pad_maximum_fusion.2), channel_id=1, source_target_pairs={{0,8},{2,10},{4,12},{6,14},{8,0},{10,2},{12,4},{14,6},{16,24},{18,... | collective-permute-start | bytes 835592 | tf_op jit(solution)/shard_map/ppermute | solution.py:106
  16.2 13.3 %collective-permute-start.2 = (bf16[2,2,128,512]{3,2,1,0:T(8,128)(2,1)S(1)}, bf16[2,2,128,512]{3,2,1,0:T(8,128)(2,1)}, u32[]{:S(2)}, u32[]{:S(2)}) collective-permute-start(bf16[2,2,128,512]{3,2,1,0:T(8,128)(2,1)S(1)} %bitcast.78), channel_id=1, source_target_pairs={{0,2},{2,0},{4,6},{6,4},{8,10},{10,8},{12,14},{14,12},{16,18},{18,... | collective-permute-start | bytes 1572872 | tf_op jit(solution)/shard_map/ppermute | solution.py:106
  18.2 32.8 %collective-permute-start.4 = (bf16[128,2176]{1,0:T(8,128)(2,1)S(1)}, bf16[128,2176]{1,0:T(8,128)(2,1)S(1)}, u32[]{:S(2)}, u32[]{:S(2)}) collective-permute-start(bf16[128,2176]{1,0:T(8,128)(2,1)S(1)} %pad_maximum_fusion.refs_0_.refs_8_), channel_id=1, source_target_pairs={{0,16},{2,18},{4,20},{6,22},{8,24},{10,26},{12,28},{14,30},{16,0},... | collective-permute-start | bytes 1671176 | tf_op jit(solution)/shard_map/ppermute | solution.py:106
  31.9 19.1 %collective-permute-start.3 = (bf16[2,2,128,512]{3,2,1,0:T(8,128)(2,1)}, bf16[2,2,128,512]{3,2,1,0:T(8,128)(2,1)}, u32[]{:S(2)}, u32[]{:S(2)}) collective-permute-start(bf16[2,2,128,512]{3,2,1,0:T(8,128)(2,1)} %get-tuple-element.69), channel_id=1, source_target_pairs={{0,4},{2,6},{4,0},{6,2},{8,12},{10,14},{12,8},{14,10},{16,20},{18,... | collective-permute-start | bytes 1572872 | tf_op jit(solution)/shard_map/ppermute | solution.py:106
  33.3 16.7 %collective-permute-start.1 = (bf16[1,1024,128]{2,1,0:T(8,128)(2,1)S(1)}, bf16[1,1024,128]{2,1,0:T(8,128)(2,1)}, u32[]{:S(2)}, u32[]{:S(2)}) collective-permute-start(bf16[1,1024,128]{2,1,0:T(8,128)(2,1)S(1)} %bitcast.79), channel_id=1, source_target_pairs={{0,8},{2,10},{4,12},{6,14},{8,0},{10,2},{12,4},{14,6},{16,24},{18,... | collective-permute-start | bytes 786440 | tf_op jit(solution)/shard_map/ppermute | solution.py:106
  34.9 20.0 %collective-permute-start.7 = (bf16[128,2176]{1,0:T(8,128)(2,1)S(1)}, bf16[128,2176]{1,0:T(8,128)(2,1)S(1)}, u32[]{:S(2)}, u32[]{:S(2)}) collective-permute-start(bf16[128,2176]{1,0:T(8,128)(2,1)S(1)} %pad_maximum_fusion.refs_0_.refs_8_), channel_id=1, source_target_pairs={{0,2},{2,0},{4,6},{6,4},{8,10},{10,8},{12,14},{14,12},{16,18},{18,... | collective-permute-start | bytes 1671176 | tf_op jit(solution)/shard_map/ppermute | solution.py:106
  36.4 20.3 %collective-permute-start.9 = (bf16[128,2176]{1,0:T(8,128)(2,1)S(1)}, bf16[128,2176]{1,0:T(8,128)(2,1)S(1)}, u32[]{:S(2)}, u32[]{:S(2)}) collective-permute-start(bf16[128,2176]{1,0:T(8,128)(2,1)S(1)} %pad_maximum_fusion.refs_0_.refs_8_), channel_id=1, source_target_pairs={{0,4},{2,6},{4,0},{6,2},{8,12},{10,14},{12,8},{14,10},{16,20},{18,... | collective-permute-start | bytes 1671176 | tf_op jit(solution)/shard_map/ppermute | solution.py:106
  52.7 14.6 %collective-permute-start.11 = (bf16[128,2176]{1,0:T(8,128)(2,1)S(1)}, bf16[128,2176]{1,0:T(8,128)(2,1)S(1)}, u32[]{:S(2)}, u32[]{:S(2)}) collective-permute-start(bf16[128,2176]{1,0:T(8,128)(2,1)S(1)} %collective-permute-done.4.refs_1_), channel_id=1, source_target_pairs={{0,2},{2,0},{4,6},{6,4},{8,10},{10,8},{12,14},{14,12},{16,18},{18,... | collective-permute-start | bytes 1671176 | tf_op jit(solution)/shard_map/ppermute | solution.py:106
  53.5 15.5 %collective-permute-start.13 = (bf16[128,2176]{1,0:T(8,128)(2,1)S(1)}, bf16[128,2176]{1,0:T(8,128)(2,1)S(1)}, u32[]{:S(2)}, u32[]{:S(2)}) collective-permute-start(bf16[128,2176]{1,0:T(8,128)(2,1)S(1)} %collective-permute-done.4.refs_1_), channel_id=1, source_target_pairs={{0,4},{2,6},{4,0},{6,2},{8,12},{10,14},{12,8},{14,10},{16,20},{18,... | collective-permute-start | bytes 1671176 | tf_op jit(solution)/shard_map/ppermute | solution.py:106
  54.9 20.1 %collective-permute-start.8 = (bf16[64,2176]{1,0:T(8,128)(2,1)S(1)}, bf16[64,2176]{1,0:T(8,128)(2,1)S(1)}, u32[]{:S(2)}, u32[]{:S(2)}) collective-permute-start(bf16[64,2176]{1,0:T(8,128)(2,1)S(1)} %slice.48), channel_id=1, source_target_pairs={{0,4},{2,6},{4,0},{6,2},{8,12},{10,14},{12,8},{14,10},{16,20},{18,... | collective-permute-start | bytes 835592 | tf_op jit(solution)/shard_map/ppermute | solution.py:106
  55.6 20.7 %collective-permute-start.5 = (bf16[4,128,512]{2,1,0:T(8,128)(2,1)S(1)}, bf16[4,128,512]{2,1,0:T(8,128)(2,1)S(1)}, u32[]{:S(2)}, u32[]{:S(2)}) collective-permute-start(bf16[4,128,512]{2,1,0:T(8,128)(2,1)S(1)} %get-tuple-element.34), channel_id=1, source_target_pairs={{0,0},{1,16},{2,2},{3,18},{4,4},{5,20},{6,6},{7,22},{8,8},{9,24},{... | collective-permute-start | bytes 1572872 | tf_op jit(solution)/shard_map/ppermute | solution.py:150
  56.7 19.7 %collective-permute-start.6 = (bf16[4,128,512]{2,1,0:T(8,128)(2,1)S(1)}, bf16[4,128,512]{2,1,0:T(8,128)(2,1)S(1)}, u32[]{:S(2)}, u32[]{:S(2)}) collective-permute-start(bf16[4,128,512]{2,1,0:T(8,128)(2,1)S(1)} %get-tuple-element.35), channel_id=1, source_target_pairs={{0,8},{1,24},{2,10},{3,26},{4,12},{5,28},{6,14},{7,30},{8,0},{9,16... | collective-permute-start | bytes 1572872 | tf_op jit(solution)/shard_map/ppermute | solution.py:150
  69.0 11.1 %collective-permute-start.12 = (bf16[64,2176]{1,0:T(8,128)(2,1)S(1)}, bf16[64,2176]{1,0:T(8,128)(2,1)S(1)}, u32[]{:S(2)}, u32[]{:S(2)}) collective-permute-start(bf16[64,2176]{1,0:T(8,128)(2,1)S(1)} %slice.50), channel_id=1, source_target_pairs={{0,4},{2,6},{4,0},{6,2},{8,12},{10,14},{12,8},{14,10},{16,20},{18,... | collective-permute-start | bytes 835592 | tf_op jit(solution)/shard_map/ppermute | solution.py:106
  82.8 26.8 %collective-permute-start.15 = (bf16[2,1024,128]{2,1,0:T(8,128)(2,1)S(1)}, bf16[2,1024,128]{2,1,0:T(8,128)(2,1)}, u32[]{:S(2)}, u32[]{:S(2)}) collective-permute-start(bf16[2,1024,128]{2,1,0:T(8,128)(2,1)S(1)} %constant_dynamic-update-slice_fusion.refs_4_), channel_id=1, source_target_pairs={{0,16},{2,18},{4,20},{6,22},{8,24},{10,26},{12,28},{14,30},{16,0},... | collective-permute-start | bytes 1572872 | tf_op jit(solution)/shard_map/ppermute | solution.py:106
  91.5 18.1 %collective-permute-start.18 = (bf16[2,1024,128]{2,1,0:T(8,128)(2,1)S(1)}, bf16[2,1024,128]{2,1,0:T(8,128)(2,1)}, u32[]{:S(2)}, u32[]{:S(2)}) collective-permute-start(bf16[2,1024,128]{2,1,0:T(8,128)(2,1)S(1)} %constant_dynamic-update-slice_fusion.refs_4_), channel_id=1, source_target_pairs={{0,1},{1,0},{2,3},{3,2},{4,5},{5,4},{6,7},{7,6},{8,9},{9,8},{10,11... | collective-permute-start | bytes 1572872 | tf_op jit(solution)/shard_map/ppermute | solution.py:110
  93.9 25.5 %collective-permute-start.31 = (bf16[64,1152]{1,0:T(8,128)(2,1)S(1)}, bf16[64,1152]{1,0:T(8,128)(2,1)S(1)}, u32[]{:S(2)}, u32[]{:S(2)}) collective-permute-start(bf16[64,1152]{1,0:T(8,128)(2,1)S(1)} %fusion.2), channel_id=1, source_target_pairs={{0,8},{2,10},{4,12},{6,14},{8,0},{10,2},{12,4},{14,6},{16,24},{18,... | collective-permute-start | bytes 442376 | tf_op jit(solution)/shard_map/ppermute | solution.py:106
  119.4 14.4 %collective-permute-start.27 = (bf16[2,1024,128]{2,1,0:T(8,128)(2,1)}, bf16[2,1024,128]{2,1,0:T(8,128)(2,1)S(1)}, u32[]{:S(2)}, u32[]{:S(2)}) collective-permute-start(bf16[2,1024,128]{2,1,0:T(8,128)(2,1)} %collective-permute-done.15.refs_5_), channel_id=1, source_target_pairs={{0,1},{1,0},{2,3},{3,2},{4,5},{5,4},{6,7},{7,6},{8,9},{9,8},{10,11... | collective-permute-start | bytes 1572872 | tf_op jit(solution)/shard_map/ppermute | solution.py:110
  119.4 14.4 %collective-permute-start.25 = (bf16[4,4,64,128]{3,2,1,0:T(8,128)(2,1)S(1)}, bf16[4,4,64,128]{3,2,1,0:T(8,128)(2,1)S(1)}, u32[]{:S(2)}, u32[]{:S(2)}) collective-permute-start(bf16[4,4,64,128]{3,2,1,0:T(8,128)(2,1)S(1)} %pad_maximum_fusion.3.refs_0_), channel_id=1, source_target_pairs={{0,4},{2,6},{4,0},{6,2},{8,12},{10,14},{12,8},{14,10},{16,20},{18,... | collective-permute-start | bytes 786440 | tf_op jit(solution)/shard_map/ppermute | solution.py:106
  121.0 12.8 %collective-permute-start.26 = (bf16[4,4,64,128]{3,2,1,0:T(8,128)(2,1)S(1)}, bf16[4,4,64,128]{3,2,1,0:T(8,128)(2,1)S(1)}, u32[]{:S(2)}, u32[]{:S(2)}) collective-permute-start(bf16[4,4,64,128]{3,2,1,0:T(8,128)(2,1)S(1)} %pad_maximum_fusion.3.refs_0_), channel_id=1, source_target_pairs={{0,6},{2,4},{4,2},{6,0},{8,14},{10,12},{12,10},{14,8},{16,22},{18,... | collective-permute-start | bytes 786440 | tf_op jit(solution)/shard_map/ppermute | solution.py:106
  121.5 16.1 %collective-permute-start.32 = (bf16[128,1152]{1,0:T(8,128)(2,1)S(1)}, bf16[128,1152]{1,0:T(8,128)(2,1)S(1)}, u32[]{:S(2)}, u32[]{:S(2)}) collective-permute-start(bf16[128,1152]{1,0:T(8,128)(2,1)S(1)} %pad_maximum_fusion.1), channel_id=1, source_target_pairs={{0,16},{2,18},{4,20},{6,22},{8,24},{10,26},{12,28},{14,30},{16,0},... | collective-permute-start | bytes 884744 | tf_op jit(solution)/shard_map/ppermute | solution.py:106
  126.5 10.2 %collective-permute-start.33 = (bf16[64,1024]{1,0:T(8,128)(2,1)S(1)}, bf16[64,1024]{1,0:T(8,128)(2,1)S(1)}, u32[]{:S(2)}, u32[]{:S(2)}) collective-permute-start(bf16[64,1024]{1,0:T(8,128)(2,1)S(1)} %get-tuple-element.73), channel_id=1, source_target_pairs={{0,1},{1,0},{2,3},{3,2},{4,5},{5,4},{6,7},{7,6},{8,9},{9,8},{10,11... | collective-permute-start | bytes 393224 | tf_op jit(solution)/shard_map/ppermute | solution.py:110
  137.6 15.6 %collective-permute-start.34 = (bf16[256,1152]{1,0:T(8,128)(2,1)S(1)}, bf16[256,1152]{1,0:T(8,128)(2,1)S(1)}, u32[]{:S(2)}, u32[]{:S(2)}) collective-permute-start(bf16[256,1152]{1,0:T(8,128)(2,1)S(1)} %constant_dynamic-update-slice_fusion.2.refs_4_), channel_id=1, source_target_pairs={{0,1},{1,0},{2,3},{3,2},{4,5},{5,4},{6,7},{7,6},{8,9},{9,8},{10,11... | collective-permute-start | bytes 1769480 | tf_op jit(solution)/shard_map/ppermute | solution.py:110
  139.2 14.0 %collective-permute-start.29 = (bf16[4,64,512]{2,1,0:T(8,128)(2,1)S(1)}, bf16[4,64,512]{2,1,0:T(8,128)(2,1)S(1)}, u32[]{:S(2)}, u32[]{:S(2)}) collective-permute-start(bf16[4,64,512]{2,1,0:T(8,128)(2,1)S(1)} %hidden.1.refs_0_), channel_id=1, source_target_pairs={{0,4},{2,6},{4,0},{6,2},{8,12},{10,14},{12,8},{14,10},{16,20},{18,... | collective-permute-start | bytes 786440 | tf_op jit(solution)/shard_map/ppermute | solution.py:106
  140.7 12.5 %collective-permute-start.30 = (bf16[4,64,512]{2,1,0:T(8,128)(2,1)S(1)}, bf16[4,64,512]{2,1,0:T(8,128)(2,1)S(1)}, u32[]{:S(2)}, u32[]{:S(2)}) collective-permute-start(bf16[4,64,512]{2,1,0:T(8,128)(2,1)S(1)} %hidden.1.refs_0_), channel_id=1, source_target_pairs={{0,6},{2,4},{4,2},{6,0},{8,14},{10,12},{12,10},{14,8},{16,22},{18,... | collective-permute-start | bytes 786440 | tf_op jit(solution)/shard_map/ppermute | solution.py:106
  (27 other events, 221.4 us)

commit v14 on v13

--- a/solution.py
+++ b/solution.py
@@ -132,10 +132,8 @@
     heads = heads.reshape(NX, NY, 2, -1, 4 * W)
     kept, sent = pick_row(heads, x), after(pick_row(heads, x ^ 1), first)
     came = hop(sent, flip(0, 1))
-    lined = jnp.where(x == 0, jnp.stack([kept, came], 1), jnp.stack([came, kept], 1))
-    kept, came = pick_row(lined, y), hop(pick_row(lined, y ^ 1), flip(1, 0))
-    whole = jnp.where(y == 0, jnp.stack([kept, came]), jnp.stack([came, kept]))
-    return whole.transpose(2, 0, 1, 3, 4).reshape(2, NY * NX, *whole.shape[3:])
+    lined = jnp.where(x == 0, jnp.stack([kept, came], 2), jnp.stack([came, kept], 2))
+    return pick_row(lined, y), hop(pick_row(lined, y ^ 1), flip(1, 0))
 
 
 def heads_along_z(pieces):
@@ -147,7 +145,7 @@
             for t in range(2):
                 dst = chip_at(2 * t + (e ^ (sz & 1)), sy, sx)
                 perm.append((2 * src + t, 2 * dst + (sz >> 1)))
-        arrived.append(lax.ppermute(piece, ("ctx", "tp"), perm).reshape(-1, piece.shape[-1]))
+        arrived.append(lax.ppermute(piece, ("ctx", "tp"), perm))
     return arrived
 
 
@@ -162,18 +160,37 @@
         copy.wait()
 
 
+def mark_kernel(where, tokens, positions, ids, mine):
+    u = where[3]
+    rows, model = mine.shape[0], tokens.shape[1]
+    mine[:, :model] = tokens[pl.ds(pl.multiple_of(u * rows, rows), rows), :]
+    line = lax.broadcasted_iota(jnp.int32, (rows, rows), 0)
+    across = lax.broadcasted_iota(jnp.int32, (rows, rows), 1)
+    lane = lax.broadcasted_iota(jnp.int32, (rows, W), 1)
+    marks = jnp.zeros((rows, W), F32)
+    values = (positions[pl.ds(u, 1)], positions[pl.ds(1 - u, 1)], ids[...])
+    for i, (value, bits) in enumerate(zip(values, (7, 7, 8))):
+        column = jnp.sum(jnp.where(line == across, value, 0), axis=1, keepdims=True)
+        high = lax.shift_right_logical(column, bits)
+        marks = jnp.where(lane == 2 * i, high.astype(F32), marks)
+        marks = jnp.where(lane == 2 * i + 1, (column - high * 2**bits).astype(F32), marks)
+    mine[:, model:] = marks.astype(BF16)
+
+
 def proj_kernel(where, *refs):
     count = len(refs) - 12
     tok, w_own, w_other = refs[:count], refs[count : count + 2], refs[count + 2 : count + 4]
     gate_query, value, key, marks, x_all, w_all, tok_sem, w_sem = refs[count + 4 :]
-    z, u = where[0], where[3]
+    z, y, u = where[0], where[1], where[3]
     copies, base = [], 0
     for side, (at, srcs) in enumerate(((u, w_own), (1 - u, w_other))):
         for e, src in enumerate(srcs):
-            size = src.shape[0]
-            start = pl.multiple_of((2 * at + (e ^ (z & 1))) * size, size)
-            to = w_all.at[pl.ds(start, size), :]
-            copies.append(pltpu.make_async_copy(src, to, w_sem.at[2 * side + e]))
+            size = src.shape[0] // 2
+            for j in range(2):
+                start = ((2 * at + (e ^ (z & 1))) * 2 + (y ^ j)) * size
+                to = w_all.at[pl.ds(pl.multiple_of(start, size), size), :]
+                sem = w_sem.at[4 * side + 2 * e + j]
+                copies.append(pltpu.make_async_copy(src.at[pl.ds(j * size, size), :], to, sem))
     for i, ref in enumerate(tok):
         rows = pl.ds(base, ref.shape[0])
         copies.append(pltpu.make_async_copy(ref, x_all.at[rows, :], tok_sem.at[i]))
@@ -232,13 +249,14 @@
 
 def hidden_kernel(where, *refs):
     n = len(PLANE)
-    gated, w_own, w_other, tok = refs[:n], refs[n : n + 2], refs[n + 2 : n + 4], refs[n + 4 : 2 * n + 4]
-    hidden, g_raw, g_all, t_all, w_all, sems = refs[2 * n + 4 :]
+    gated, w_own, w_other, tok = refs[:5], refs[5:7], refs[7:9], refs[9:13]
+    hidden, g_raw, g_all, t_all, w_all, sems = refs[13:]
     z, y, x, u = (where[i] for i in range(4))
     c = chip_at(z, y, x)
     rows = hidden.shape[1]
     half = w_all.shape[1]
-    copies = [(src, g_raw.at[k]) for k, src in enumerate(gated)]
+    copies = [(src, g_raw.at[k]) for k, src in enumerate(gated[:3])]
+    copies += [(src, g_raw.at[3, pl.ds(2 * i, 2)]) for i, src in enumerate(gated[3:])]
     for s in range(NZ):
         cols = pl.ds(s * W, W)
         for side, src in enumerate((w_own, w_other)):
@@ -250,7 +268,7 @@
     copies = [pltpu.make_async_copy(src, dst, sems.at[i]) for i, (src, dst) in enumerate(copies)]
     for copy in copies:
         copy.start()
-    for copy in copies[:n]:
+    for copy in copies[:5]:
         copy.wait()
     for k, (by, bx) in enumerate(PLANE):
         for s in range(NZ):
@@ -259,7 +277,7 @@
             for j in range(n):
                 block = j ^ k
                 g_all[block * rows : (block + 1) * rows, cols] = g_raw[k, s, j]
-    for copy in copies[n:]:
+    for copy in copies[5:]:
         copy.wait()
     total = 0.0
     for side, at in enumerate((u, 1 - u)):
@@ -281,8 +299,8 @@
 
 def mass_kernel(where, *refs):
     n = len(PLANE)
-    pieces, (n_own, n_other, t_keep, t_send, marks) = refs[:n], refs[n : n + 5]
-    keep, send, positive, mass, h_all = refs[n + 5 :]
+    pieces, (n_own, n_other, t_keep, t_send, marks) = refs[:5], refs[5:10]
+    keep, send, positive, mass, h_all = refs[10:]
     y, x, u = (where[i] for i in range(1, 4))
     rows, half = keep.shape
     for k, (by, bx) in enumerate(PLANE):
@@ -291,7 +309,8 @@
             cols = pl.ds(pl.multiple_of(block * W, W), W)
             for j in range(n):
                 row = (j ^ k) * rows
-                h_all[row : row + rows, cols] = pieces[k][j, :, at * W : (at + 1) * W]
+                ref, i = (pieces[k], j) if k < n - 1 else (pieces[k + j // 2], j % 2)
+                h_all[row : row + rows, cols] = ref[i, :, at * W : (at + 1) * W]
     mine = pl.ds(pl.multiple_of(u * half, half), half)
     theirs = pl.ds(pl.multiple_of((1 - u) * half, half), half)
     keep[...] = h_all[:rows, mine]
@@ -380,30 +399,34 @@
     negs = neg_emb.shape[0]
     plane = len(PLANE)
 
-    mine = lax.dynamic_slice_in_dim(tokens, u * rows, rows, 0)
-    p_own = lax.dynamic_slice_in_dim(positions, u * rows, rows, 0)
-    p_other = lax.dynamic_slice_in_dim(positions, (1 - u) * rows, rows, 0)
-    ids = whole_parts(target_ids, 256)
-    mine = with_marks(mine, whole_parts(p_own, 128) + whole_parts(p_other, 128) + ids)
-    low = pair_up(mine)
+    (mine,) = call(
+        mark_kernel,
+        "mark",
+        [((rows, model + W), BF16)],
+        [],
+        [where, tokens, positions.reshape(2, rows), target_ids.reshape(1, rows)],
+        "svvv",
+        0,
+    )
+    line = [mine] + [hop(mine, flip(0, 0, s)) for s in range(1, NZ)]
 
     to_x, to_y = flip(0, 1), flip(1, 0)
-    high = hop(low, flip(0, 0, 2))
-    w_plane = heads_in_plane(w_proj, y, x, low)
-    w_pieces = [pick_row(w_plane, e ^ (z & 1)) for e in range(2)]
-    low_x, low_y = hop(low, to_x), hop(low, to_y)
-    low_xy = across(low_x, low_y)
-
-    out_pair = pair_up(after(w_out[None], low))
+    w_rows = heads_in_plane(after(w_proj, mine), y, x, line[1])
+    w_pieces = [
+        jnp.concatenate([pick_row(w, e ^ (z & 1)) for w in w_rows]).reshape(-1, 4 * W)
+        for e in range(2)
+    ]
+
     own_ids = lax.dynamic_slice_in_dim(neg_ids, c * negs, negs, 0)
     norms = jnp.sum(jnp.square(neg_emb.astype(F32)), axis=1)
     neg = with_marks(neg_emb, float_parts(norms) + whole_parts(own_ids, 256))
 
-    w_pieces, high = lax.optimization_barrier((w_pieces, after(high, out_pair)))
-    high_x, high_y = hop(high, to_x), hop(high, to_y)
-    high_xy = across(high_x, high_y)
-    tok = [low, high, low_x, high_x, low_y, high_y, *low_xy, *high_xy]
-    w_mine = after(heads_along_z(w_pieces), low_xy, high_xy)
+    out_pair = pair_up(after(w_out[None], mine))
+    w_pieces, neg, out_pair, line = lax.optimization_barrier((w_pieces, neg, out_pair, line))
+    near = jnp.concatenate(line)
+    near_x, near_y = hop(near, to_x), hop(near, to_y)
+    tok = [near, near_x, near_y, *across(near_x, near_y)]
+    w_mine = heads_along_z(w_pieces)
     w_theirs = [swap_cores(w) for w in w_mine]
     out_own = [out_pair, hop(after(out_pair, w_mine), flip(0, 0, 2))]
     neg_pair = pair_up(after(neg, w_mine))
@@ -421,7 +444,7 @@
                 pltpu.VMEM((count, model + W), BF16),
                 pltpu.VMEM((model, 4 * W), BF16),
                 pltpu.SemaphoreType.DMA((len(pieces),)),
-                pltpu.SemaphoreType.DMA((4,)),
+                pltpu.SemaphoreType.DMA((8,)),
             ],
             [where, *pieces, *w_mine, *w_theirs],
             "s" + (len(pieces) + 4) * "h",
@@ -446,7 +469,8 @@
     gated = jnp.stack([gated[0]] + [hop(gated[s], flip(0, 0, s)) for s in range(1, NZ)])
     neg_far = hop(after(neg_pair, gated), flip(0, 0, 2))
     out_other = [out_pair_theirs, swap_cores(after(out_own[1], gated))]
-    gated = [gated] + [hop(gated, flip(by, bx)) for by, bx in PLANE[1:]]
+    gated = [gated, hop(gated, to_x), hop(gated, to_y)]
+    gated += across(gated[1], gated[2])
     (hidden,) = call(
         hidden_kernel,
         "hidden",
@@ -456,22 +480,23 @@
             pltpu.VMEM((plane * rows, model), BF16),
             pltpu.VMEM((plane, rows, NZ * W), BF16),
             pltpu.VMEM((2, half, NZ * W), BF16),
-            pltpu.SemaphoreType.DMA((28,)),
+            pltpu.SemaphoreType.DMA((29,)),
         ],
-        [where, *gated, *out_own, *out_other, low, low_x, low_y, low_xy[0]],
-        "s" + 12 * "h",
+        [where, *gated, *out_own, *out_other, *tok[:4]],
+        "s" + 13 * "h",
         2 * plane * rows * model * NZ * W,
     )
     neg_own = jnp.concatenate([neg_pair, after(neg_far, hidden, t_send)])
     neg_other = swap_cores(neg_own)
-    pieces = [hidden] + [hop(hidden, flip(by, bx)) for by, bx in PLANE[1:]]
+    pieces = [hidden, hop(hidden, to_x), hop(hidden, to_y)]
+    pieces += across(pieces[1], pieces[2])
     h_keep, h_send, positive, mass = call(
         mass_kernel,
         "mass",
         [((rows, half), BF16)] * 2 + [((1, rows), F32), ((plane, 1, rows), F32)],
         [pltpu.VMEM((plane * rows, model), BF16)],
         [where, *pieces, neg_own, neg_other, t_keep, t_send, marks],
-        "s" + 9 * "v",
+        "s" + 10 * "v",
         2 * plane * rows * model * NZ * negs,
     )
     masses = [mass[0]] + [hop(mass[k], flip(*PLANE[k])) for k in range(1, plane)]

time: 163 us -> 154 us (0.945)
  waiting for transfers between devices: 86.6 us -> 68.2 us
  starting transfers between devices: 43.9 us -> 52.2 us
  other arithmetic: 10.2 us -> 3.91 us
  local copies, waits for them, and re-layouts: 6.2 us -> 11.7 us
    ppermute x28 -> x27, waiting for transfers between devices: 86.6 us -> 68.2 us  [hop(): return lax.ppermute(value, 'ctx', perm)]
    ppermute x28 -> x27, starting transfers between devices: 39 us -> 48.3 us  [hop(): return lax.ppermute(value, 'ctx', perm)]
    unnamed x28 -> x33, local copies, waits for them, and re-layouts: 2.9 us -> 7.06 us
    another operation x5 -> x2, other arithmetic: 4.36 us -> 1.54 us  [with_marks(): marks = jnp.stack(marks, 1)]
    optimization_barrier x0 -> x1, local copies, waits for them, and re-layouts: none -> 1.92 us  [after(): return lax.optimization_barrier((values, others))[0]]
    concatenate x2 -> x1, other arithmetic: 1.67 us -> 0.02 us  [with_marks(): return jnp.concatenate([rows, marks], 1)]
    pallas_call x5 -> x6, Pallas kernels: 14.8 us -> 16.1 us  [call(): pl.pallas_call(kernel, out_shape=[jax.ShapeDtypeStruct(shape, dtype) for...]
  transfers between devices with their start and end apart: 39 -> 38, of which waited for: 20 -> 20; matrix products, arithmetic and copies ran while one was open for 6% -> 4% of each run, Pallas kernels for 7% -> 8%
where the time goes in v14:
time: 154 us; the launch traced here: 153 us
  waiting for transfers between devices  68.2 us (44%)
  starting transfers between devices  52.2 us (34%)
  Pallas kernels  16.1 us (10%)
  local copies, waits for them, and re-layouts  11.7 us (8%)
  other arithmetic  3.91 us (3%)
    ppermute x27, waiting for transfers between devices, hop(): return lax.ppermute(value, 'ctx', perm)  68.2 us
    ppermute x27, starting transfers between devices, hop(): return lax.ppermute(value, 'ctx', perm)  48.3 us
    pallas_call x6, Pallas kernels, call(): pl.pallas_call(kernel, out_shape=[jax.ShapeDtypeStruct(shape, dtype) for...  16.1 us
    unnamed x33, local copies, waits for them, and re-layouts  7.06 us
  transfers between devices with their start and end apart: 38, of which 20 were waited for; matrix products, arithmetic and copies ran while one was open for 4% of the time, Pallas kernels for 8%

profile of v14, /device:TPU:0, one launch (start us, length us, event | category | flops | bytes accessed | tf_op | source)
XLA Modules:
  0.0 153.2 jit_solution(2576833372782031409)
XLA Ops:
  3.9 3.1 %collective-permute-start = (bf16[64,2176]{1,0:T(8,128)(2,1)S(1)}, bf16[64,2176]{1,0:T(8,128)(2,1)S(1)}, u32[]{:S(2)}, u32[]{:S(2)}) collective-permute-start(bf16[64,2176]{1,0:T(8,128)(2,1)S(1)} %mark.1), channel_id=1, source_target_pairs={{0,8},{2,10},{4,12},{6,14},{8,0},{10,2},{12,4},{14,6},{16,24},{18,... | collective-permute-start | bytes 835592 | tf_op jit(solution)/shard_map/ppermute | solution.py:106
  7.0 1.9 %copy.35 = bf16[128,4,1024]{0,2,1:T(8,128)(2,1)S(1)} copy(bf16[128,4,1024]{2,1,0:T(4,128)(2,1)} %param.9) | data formatting | bytes 2097152 | tf_op jit(solution)/shard_map/optimization_barrier | solution.py:118
  9.3 4.3 %collective-permute-done = bf16[64,2176]{1,0:T(8,128)(2,1)S(1)} collective-permute-done((bf16[64,2176]{1,0:T(8,128)(2,1)S(1)}, bf16[64,2176]{1,0:T(8,128)(2,1)S(1)}, u32[]{:S(2)}, u32[]{:S(2)}) %collective-permute-start) | collective-permute-done | bytes 278560 | tf_op jit(solution)/shard_map/ppermute | solution.py:106
  15.3 2.6 %collective-permute-start.4 = (bf16[64,2176]{1,0:T(8,128)(2,1)S(1)}, bf16[64,2176]{1,0:T(8,128)(2,1)}, u32[]{:S(2)}, u32[]{:S(2)}) collective-permute-start(bf16[64,2176]{1,0:T(8,128)(2,1)S(1)} %mark.1), channel_id=1, source_target_pairs={{0,16},{2,18},{4,20},{6,22},{8,24},{10,26},{12,28},{14,30},{16,0},... | collective-permute-start | bytes 835592 | tf_op jit(solution)/shard_map/ppermute | solution.py:106
  20.6 6.1 %collective-permute-done.1 = bf16[2,2,128,512]{3,2,1,0:T(8,128)(2,1)S(1)} collective-permute-done((bf16[2,2,128,512]{3,2,1,0:T(8,128)(2,1)S(1)}, bf16[2,2,128,512]{3,2,1,0:T(8,128)(2,1)S(1)}, u32[]{:S(2)}, u32[]{:S(2)}) %collective-permute-start.1) | collective-permute-done | bytes 524320 | tf_op jit(solution)/shard_map/ppermute | solution.py:106
  29.3 7.3 %collective-permute-done.3 = bf16[1,1024,128]{2,1,0:T(8,128)(2,1)} collective-permute-done((bf16[1,1024,128]{2,1,0:T(8,128)(2,1)}, bf16[1,1024,128]{2,1,0:T(8,128)(2,1)}, u32[]{:S(2)}, u32[]{:S(2)}) %collective-permute-start.3) | collective-permute-done | bytes 262176 | tf_op jit(solution)/shard_map/ppermute | solution.py:106
  36.7 1.8 %pad_maximum_fusion.2.refs_5_ = bf16[2,1024,128]{2,1,0:T(8,128)(2,1)} fusion(bf16[1,1024,128]{2,1,0:T(8,128)(2,1)} %collective-permute-done.3, bf16[1,1024,128]{2,1,0:T(8,128)(2,1)S(1)} %bitcast.69), kind=kLoop, calls=%fused_computation.3 | loop fusion | flops 262144 | bytes 1048576 | tf_op jit(solution)/shard_map/concatenate | solution.py:122
  47.4 19.1 %collective-permute-done.9.refs_1_.refs_10_ = bf16[256,2176]{1,0:T(8,128)(2,1)S(1)} collective-permute-done((bf16[256,2176]{1,0:T(8,128)(2,1)S(1)}, bf16[256,2176]{1,0:T(8,128)(2,1)S(1)}, u32[]{:S(2)}, u32[]{:S(2)}) %collective-permute-start.9) | collective-permute-done | bytes 1114144 | tf_op jit(solution)/shard_map/ppermute | solution.py:106
  67.9 2.3 %collective-permute-start.12 = (bf16[128,2176]{1,0:T(8,128)(2,1)S(1)}, bf16[128,2176]{1,0:T(8,128)(2,1)S(1)}, u32[]{:S(2)}, u32[]{:S(2)}) collective-permute-start(bf16[128,2176]{1,0:T(8,128)(2,1)S(1)} %slice.57), channel_id=1, source_target_pairs={{0,2},{2,0},{4,6},{6,4},{8,10},{10,8},{12,14},{14,12},{16,18},{18,... | collective-permute-start | bytes 1671176 | tf_op jit(solution)/shard_map/ppermute | solution.py:106
  70.7 5.1 %collective-permute-start.8 = (bf16[2,1024,128]{2,1,0:T(8,128)(2,1)}, bf16[2,1024,128]{2,1,0:T(8,128)(2,1)}, u32[]{:S(2)}, u32[]{:S(2)}) collective-permute-start(bf16[2,1024,128]{2,1,0:T(8,128)(2,1)} %pad_maximum_fusion.2.refs_5_), channel_id=1, source_target_pairs={{0,16},{2,18},{4,20},{6,22},{8,24},{10,26},{12,28},{14,30},{16,0},... | collective-permute-start | bytes 1572872 | tf_op jit(solution)/shard_map/ppermute | solution.py:106
  75.9 2.9 %collective-permute-done.11.refs_3_.refs_12_ = bf16[128,2176]{1,0:T(8,128)(2,1)S(1)} collective-permute-done((bf16[128,2176]{1,0:T(8,128)(2,1)S(1)}, bf16[128,2176]{1,0:T(8,128)(2,1)S(1)}, u32[]{:S(2)}, u32[]{:S(2)}) %collective-permute-start.11) | collective-permute-done | bytes 557088 | tf_op jit(solution)/shard_map/ppermute | solution.py:106
  78.8 4.8 %project.1 = (bf16[1024,256]{1,0:T(8,128)(2,1)S(1)}, bf16[1024,128]{1,0:T(8,128)(2,1)}, bf16[1024,128]{1,0:T(8,128)(2,1)}, bf16[1024,128]{1,0:T(8,128)(2,1)S(1)}) custom-call(s32[4]{0:T(128)S(1)} %pad_add_fusion.where, bf16[256,2176]{1,0:T(8,128)(2,1)S(1)} %constant_dynamic-update-slice_fusion.refs_0_.refs_9_, ...), custom_call_target="tpu_custom_call" | custom-call | bytes 6553616 | tf_op jit(solution)/shard_map/project/pallas_call | solution.py:359
  85.5 7.0 %collective-permute-start.30 = (bf16[64,1152]{1,0:T(8,128)(2,1)S(1)}, bf16[64,1152]{1,0:T(8,128)(2,1)S(1)}, u32[]{:S(2)}, u32[]{:S(2)}) collective-permute-start(bf16[64,1152]{1,0:T(8,128)(2,1)S(1)} %fusion.1), channel_id=1, source_target_pairs={{0,8},{2,10},{4,12},{6,14},{8,0},{10,2},{12,4},{14,6},{16,24},{18,... | collective-permute-start | bytes 442376 | tf_op jit(solution)/shard_map/ppermute | solution.py:106
  94.6 4.5 %attend.1 = bf16[4,4,64,128]{3,2,1,0:T(8,128)(2,1)S(1)} custom-call(bf16[1024,256]{1,0:T(8,128)(2,1)S(1)} %copy-done.7, bf16[1024,128]{1,0:T(8,128)(2,1)} %get-tuple-element.48.refs_1_, bf16[1024,128]{1,0:T(8,128)(2,1)} %get-tuple-element.45.refs_2_, bf16[1024,128]{1,0:T(8,128)(2,1)} %collective-permute-done.16.refs_3_, ...), custom_call_target="tpu_custom_call" | custom-call | bytes 1835008 | tf_op jit(solution)/shard_map/attend/pallas_call | solution.py:359
  101.7 2.1 %collective-permute-start.19 = (bf16[4,64,128]{2,1,0:T(8,128)(2,1)S(1)}, bf16[4,64,128]{2,1,0:T(8,128)(2,1)S(1)}, u32[]{:S(2)}, u32[]{:S(2)}) collective-permute-start(bf16[4,64,128]{2,1,0:T(8,128)(2,1)S(1)} %get-tuple-element.78), channel_id=1, source_target_pairs={{0,16},{2,18},{4,20},{6,22},{8,24},{10,26},{12,28},{14,30},{16,0},... | collective-permute-start | bytes 196616 | tf_op jit(solution)/shard_map/ppermute | solution.py:106
  105.2 2.0 %collective-permute-done.19 = bf16[4,64,128]{2,1,0:T(8,128)(2,1)S(1)} collective-permute-done((bf16[4,64,128]{2,1,0:T(8,128)(2,1)S(1)}, bf16[4,64,128]{2,1,0:T(8,128)(2,1)S(1)}, u32[]{:S(2)}, u32[]{:S(2)}) %collective-permute-start.19) | collective-permute-done | bytes 65568 | tf_op jit(solution)/shard_map/ppermute | solution.py:106
  107.2 2.9 %collective-permute-done.20 = bf16[4,64,128]{2,1,0:T(8,128)(2,1)S(1)} collective-permute-done((bf16[4,64,128]{2,1,0:T(8,128)(2,1)S(1)}, bf16[4,64,128]{2,1,0:T(8,128)(2,1)S(1)}, u32[]{:S(2)}, u32[]{:S(2)}) %collective-permute-start.20) | collective-permute-done | bytes 65568 | tf_op jit(solution)/shard_map/ppermute | solution.py:106
  111.9 3.0 %collective-permute-start.31 = (bf16[128,1152]{1,0:T(8,128)(2,1)S(1)}, bf16[128,1152]{1,0:T(8,128)(2,1)S(1)}, u32[]{:S(2)}, u32[]{:S(2)}) collective-permute-start(bf16[128,1152]{1,0:T(8,128)(2,1)S(1)} %pad_maximum_fusion.3), channel_id=1, source_target_pairs={{0,16},{2,18},{4,20},{6,22},{8,24},{10,26},{12,28},{14,30},{16,0},... | collective-permute-start | bytes 884744 | tf_op jit(solution)/shard_map/ppermute | solution.py:106
  115.1 2.8 %collective-permute-done.21.refs_1_ = bf16[4,4,64,128]{3,2,1,0:T(8,128)(2,1)S(1)} collective-permute-done((bf16[4,4,64,128]{3,2,1,0:T(8,128)(2,1)S(1)}, bf16[4,4,64,128]{3,2,1,0:T(8,128)(2,1)S(1)}, u32[]{:S(2)}, u32[]{:S(2)}) %collective-permute-start.21) | collective-permute-done | bytes 262176 | tf_op jit(solution)/shard_map/ppermute | solution.py:106
  119.8 3.2 %collective-permute-done.23.refs_3_ = bf16[2,4,64,128]{3,2,1,0:T(8,128)(2,1)S(1)} collective-permute-done((bf16[2,4,64,128]{3,2,1,0:T(8,128)(2,1)S(1)}, bf16[2,4,64,128]{3,2,1,0:T(8,128)(2,1)S(1)}, u32[]{:S(2)}, u32[]{:S(2)}) %collective-permute-start.23) | collective-permute-done | bytes 131104 | tf_op jit(solution)/shard_map/ppermute | solution.py:106
  123.5 3.3 %hidden.1.refs_0_ = bf16[4,64,512]{2,1,0:T(8,128)(2,1)S(1)} custom-call(s32[4]{0:T(128)S(1)} %pad_add_fusion.where, bf16[4,4,64,128]{3,2,1,0:T(8,128)(2,1)S(1)} %pad_maximum_fusion.4.refs_0_, bf16[4,4,64,128]{3,2,1,0:T(8,128)(2,1)S(1)} %collective-permute-done.21.refs_1_, bf16[4,4,64,128]{3,2,1,0:T(8,128)(2,1)S(1)} %collective-permute-done.22.refs_2_, ...), custom_call_target="tpu_custom_call" | custom-call | flops 536870912 | bytes 7045136 | tf_op jit(solution)/shard_map/hidden/pallas_call | solution.py:359
  126.9 1.9 %collective-permute-done.31 = bf16[128,1152]{1,0:T(8,128)(2,1)S(1)} collective-permute-done((bf16[128,1152]{1,0:T(8,128)(2,1)S(1)}, bf16[128,1152]{1,0:T(8,128)(2,1)S(1)}, u32[]{:S(2)}, u32[]{:S(2)}) %collective-permute-start.31) | collective-permute-done | bytes 294944 | tf_op jit(solution)/shard_map/ppermute | solution.py:106
  131.5 6.2 %collective-permute-done.26.refs_1_ = bf16[4,64,512]{2,1,0:T(8,128)(2,1)S(1)} collective-permute-done((bf16[4,64,512]{2,1,0:T(8,128)(2,1)S(1)}, bf16[4,64,512]{2,1,0:T(8,128)(2,1)S(1)}, u32[]{:S(2)}, u32[]{:S(2)}) %collective-permute-start.26) | collective-permute-done | bytes 262176 | tf_op jit(solution)/shard_map/ppermute | solution.py:106
  140.3 2.5 %collective-permute-done.28.refs_3_ = bf16[2,64,512]{2,1,0:T(8,128)(2,1)S(1)} collective-permute-done((bf16[2,64,512]{2,1,0:T(8,128)(2,1)S(1)}, bf16[2,64,512]{2,1,0:T(8,128)(2,1)S(1)}, u32[]{:S(2)}, u32[]{:S(2)}) %collective-permute-start.28) | collective-permute-done | bytes 131104 | tf_op jit(solution)/shard_map/ppermute | solution.py:106
  (124 shorter events, 49.4 us)
Async XLA Ops:
  3.9 9.7 %collective-permute-start = (bf16[64,2176]{1,0:T(8,128)(2,1)S(1)}, bf16[64,2176]{1,0:T(8,128)(2,1)S(1)}, u32[]{:S(2)}, u32[]{:S(2)}) collective-permute-start(bf16[64,2176]{1,0:T(8,128)(2,1)S(1)} %mark.1), channel_id=1, source_target_pairs={{0,8},{2,10},{4,12},{6,14},{8,0},{10,2},{12,4},{14,6},{16,24},{18,... | collective-permute-start | bytes 835592 | tf_op jit(solution)/shard_map/ppermute | solution.py:106
  13.6 13.1 %collective-permute-start.1 = (bf16[2,2,128,512]{3,2,1,0:T(8,128)(2,1)S(1)}, bf16[2,2,128,512]{3,2,1,0:T(8,128)(2,1)S(1)}, u32[]{:S(2)}, u32[]{:S(2)}) collective-permute-start(bf16[2,2,128,512]{3,2,1,0:T(8,128)(2,1)S(1)} %bitcast.64), channel_id=1, source_target_pairs={{0,2},{2,0},{4,6},{6,4},{8,10},{10,8},{12,14},{14,12},{16,18},{18,... | collective-permute-start | bytes 1572872 | tf_op jit(solution)/shard_map/ppermute | solution.py:106
  15.3 24.2 %collective-permute-start.4 = (bf16[64,2176]{1,0:T(8,128)(2,1)S(1)}, bf16[64,2176]{1,0:T(8,128)(2,1)}, u32[]{:S(2)}, u32[]{:S(2)}) collective-permute-start(bf16[64,2176]{1,0:T(8,128)(2,1)S(1)} %mark.1), channel_id=1, source_target_pairs={{0,16},{2,18},{4,20},{6,22},{8,24},{10,26},{12,28},{14,30},{16,0},... | collective-permute-start | bytes 835592 | tf_op jit(solution)/shard_map/ppermute | solution.py:106
  17.9 21.6 %collective-permute-start.5 = (bf16[64,2176]{1,0:T(8,128)(2,1)S(1)}, bf16[64,2176]{1,0:T(8,128)(2,1)}, u32[]{:S(2)}, u32[]{:S(2)}) collective-permute-start(bf16[64,2176]{1,0:T(8,128)(2,1)S(1)} %mark.1), channel_id=1, source_target_pairs={{0,24},{2,26},{4,28},{6,30},{8,16},{10,18},{12,20},{14,22},{16,8},... | collective-permute-start | bytes 835592 | tf_op jit(solution)/shard_map/ppermute | solution.py:106
  19.2 17.5 %collective-permute-start.3 = (bf16[1,1024,128]{2,1,0:T(8,128)(2,1)}, bf16[1,1024,128]{2,1,0:T(8,128)(2,1)}, u32[]{:S(2)}, u32[]{:S(2)}) collective-permute-start(bf16[1,1024,128]{2,1,0:T(8,128)(2,1)} %bitcast.68), channel_id=1, source_target_pairs={{0,8},{2,10},{4,12},{6,14},{8,0},{10,2},{12,4},{14,6},{16,24},{18,... | collective-permute-start | bytes 786440 | tf_op jit(solution)/shard_map/ppermute | solution.py:106
  27.0 12.4 %collective-permute-start.2 = (bf16[2,2,128,512]{3,2,1,0:T(8,128)(2,1)S(1)}, bf16[2,2,128,512]{3,2,1,0:T(8,128)(2,1)S(1)}, u32[]{:S(2)}, u32[]{:S(2)}) collective-permute-start(bf16[2,2,128,512]{3,2,1,0:T(8,128)(2,1)S(1)} %copy_bitcast_fusion), channel_id=1, source_target_pairs={{0,4},{2,6},{4,0},{6,2},{8,12},{10,14},{12,8},{14,10},{16,20},{18,... | collective-permute-start | bytes 1572872 | tf_op jit(solution)/shard_map/ppermute | solution.py:106
  42.3 24.2 %collective-permute-start.9 = (bf16[256,2176]{1,0:T(8,128)(2,1)S(1)}, bf16[256,2176]{1,0:T(8,128)(2,1)S(1)}, u32[]{:S(2)}, u32[]{:S(2)}) collective-permute-start(bf16[256,2176]{1,0:T(8,128)(2,1)S(1)} %constant_dynamic-update-slice_fusion.refs_0_.refs_9_), channel_id=1, source_target_pairs={{0,2},{2,0},{4,6},{6,4},{8,10},{10,8},{12,14},{14,12},{16,18},{18,... | collective-permute-start | bytes 3342344 | tf_op jit(solution)/shard_map/ppermute | solution.py:106
  43.4 24.4 %collective-permute-start.10 = (bf16[256,2176]{1,0:T(8,128)(2,1)S(1)}, bf16[256,2176]{1,0:T(8,128)(2,1)S(1)}, u32[]{:S(2)}, u32[]{:S(2)}) collective-permute-start(bf16[256,2176]{1,0:T(8,128)(2,1)S(1)} %constant_dynamic-update-slice_fusion.refs_0_.refs_9_), channel_id=1, source_target_pairs={{0,4},{2,6},{4,0},{6,2},{8,12},{10,14},{12,8},{14,10},{16,20},{18,... | collective-permute-start | bytes 3342344 | tf_op jit(solution)/shard_map/ppermute | solution.py:106
  44.9 25.3 %collective-permute-start.6 = (bf16[512,512]{1,0:T(8,128)(2,1)S(1)}, bf16[512,512]{1,0:T(8,128)(2,1)S(1)}, u32[]{:S(2)}, u32[]{:S(2)}) collective-permute-start(bf16[512,512]{1,0:T(8,128)(2,1)S(1)} %bitcast.66), channel_id=1, source_target_pairs={{0,0},{1,16},{2,2},{3,18},{4,4},{5,20},{6,6},{7,22},{8,8},{9,24},{... | collective-permute-start | bytes 1572872 | tf_op jit(solution)/shard_map/ppermute | solution.py:148
  45.8 24.4 %collective-permute-start.7 = (bf16[512,512]{1,0:T(8,128)(2,1)S(1)}, bf16[512,512]{1,0:T(8,128)(2,1)S(1)}, u32[]{:S(2)}, u32[]{:S(2)}) collective-permute-start(bf16[512,512]{1,0:T(8,128)(2,1)S(1)} %bitcast.65), channel_id=1, source_target_pairs={{0,8},{1,24},{2,10},{3,26},{4,12},{5,28},{6,14},{7,30},{8,0},{9,16... | collective-permute-start | bytes 1572872 | tf_op jit(solution)/shard_map/ppermute | solution.py:148
  66.6 12.2 %collective-permute-start.11 = (bf16[128,2176]{1,0:T(8,128)(2,1)S(1)}, bf16[128,2176]{1,0:T(8,128)(2,1)S(1)}, u32[]{:S(2)}, u32[]{:S(2)}) collective-permute-start(bf16[128,2176]{1,0:T(8,128)(2,1)S(1)} %slice.56), channel_id=1, source_target_pairs={{0,4},{2,6},{4,0},{6,2},{8,12},{10,14},{12,8},{14,10},{16,20},{18,... | collective-permute-start | bytes 1671176 | tf_op jit(solution)/shard_map/ppermute | solution.py:106
  67.9 10.9 %collective-permute-start.12 = (bf16[128,2176]{1,0:T(8,128)(2,1)S(1)}, bf16[128,2176]{1,0:T(8,128)(2,1)S(1)}, u32[]{:S(2)}, u32[]{:S(2)}) collective-permute-start(bf16[128,2176]{1,0:T(8,128)(2,1)S(1)} %slice.57), channel_id=1, source_target_pairs={{0,2},{2,0},{4,6},{6,4},{8,10},{10,8},{12,14},{14,12},{16,18},{18,... | collective-permute-start | bytes 1671176 | tf_op jit(solution)/shard_map/ppermute | solution.py:106
  70.7 29.4 %collective-permute-start.8 = (bf16[2,1024,128]{2,1,0:T(8,128)(2,1)}, bf16[2,1024,128]{2,1,0:T(8,128)(2,1)}, u32[]{:S(2)}, u32[]{:S(2)}) collective-permute-start(bf16[2,1024,128]{2,1,0:T(8,128)(2,1)} %pad_maximum_fusion.2.refs_5_), channel_id=1, source_target_pairs={{0,16},{2,18},{4,20},{6,22},{8,24},{10,26},{12,28},{14,30},{16,0},... | collective-permute-start | bytes 1572872 | tf_op jit(solution)/shard_map/ppermute | solution.py:106
  85.0 15.1 %collective-permute-start.15 = (bf16[2,1024,128]{2,1,0:T(8,128)(2,1)}, bf16[2,1024,128]{2,1,0:T(8,128)(2,1)}, u32[]{:S(2)}, u32[]{:S(2)}) collective-permute-start(bf16[2,1024,128]{2,1,0:T(8,128)(2,1)} %pad_maximum_fusion.2.refs_5_), channel_id=1, source_target_pairs={{0,1},{1,0},{2,3},{3,2},{4,5},{5,4},{6,7},{7,6},{8,9},{9,8},{10,11... | collective-permute-start | bytes 1572872 | tf_op jit(solution)/shard_map/ppermute | solution.py:110
  85.0 7.5 %collective-permute-start.16 = (bf16[1024,128]{1,0:T(8,128)(2,1)}, bf16[1024,128]{1,0:T(8,128)(2,1)}, u32[]{:S(2)}, u32[]{:S(2)}) collective-permute-start(bf16[1024,128]{1,0:T(8,128)(2,1)} %get-tuple-element.48.refs_1_), channel_id=1, source_target_pairs={{0,1},{1,0},{2,3},{3,2},{4,5},{5,4},{6,7},{7,6},{8,9},{9,8},{10,11... | collective-permute-start | bytes 786440 | tf_op jit(solution)/shard_map/ppermute | solution.py:110
  85.5 26.3 %collective-permute-start.30 = (bf16[64,1152]{1,0:T(8,128)(2,1)S(1)}, bf16[64,1152]{1,0:T(8,128)(2,1)S(1)}, u32[]{:S(2)}, u32[]{:S(2)}) collective-permute-start(bf16[64,1152]{1,0:T(8,128)(2,1)S(1)} %fusion.1), channel_id=1, source_target_pairs={{0,8},{2,10},{4,12},{6,14},{8,0},{10,2},{12,4},{14,6},{16,24},{18,... | collective-permute-start | bytes 442376 | tf_op jit(solution)/shard_map/ppermute | solution.py:106
  110.2 7.7 %collective-permute-start.21 = (bf16[4,4,64,128]{3,2,1,0:T(8,128)(2,1)S(1)}, bf16[4,4,64,128]{3,2,1,0:T(8,128)(2,1)S(1)}, u32[]{:S(2)}, u32[]{:S(2)}) collective-permute-start(bf16[4,4,64,128]{3,2,1,0:T(8,128)(2,1)S(1)} %pad_maximum_fusion.4.refs_0_), channel_id=1, source_target_pairs={{0,2},{2,0},{4,6},{6,4},{8,10},{10,8},{12,14},{14,12},{16,18},{18,... | collective-permute-start | bytes 786440 | tf_op jit(solution)/shard_map/ppermute | solution.py:106
  110.8 7.7 %collective-permute-start.22 = (bf16[4,4,64,128]{3,2,1,0:T(8,128)(2,1)S(1)}, bf16[4,4,64,128]{3,2,1,0:T(8,128)(2,1)S(1)}, u32[]{:S(2)}, u32[]{:S(2)}) collective-permute-start(bf16[4,4,64,128]{3,2,1,0:T(8,128)(2,1)S(1)} %pad_maximum_fusion.4.refs_0_), channel_id=1, source_target_pairs={{0,4},{2,6},{4,0},{6,2},{8,12},{10,14},{12,8},{14,10},{16,20},{18,... | collective-permute-start | bytes 786440 | tf_op jit(solution)/shard_map/ppermute | solution.py:106
  111.8 11.7 %collective-permute-start.25 = (bf16[2,1024,128]{2,1,0:T(8,128)(2,1)}, bf16[2,1024,128]{2,1,0:T(8,128)(2,1)S(1)}, u32[]{:S(2)}, u32[]{:S(2)}) collective-permute-start(bf16[2,1024,128]{2,1,0:T(8,128)(2,1)} %collective-permute-done.8.refs_6_), channel_id=1, source_target_pairs={{0,1},{1,0},{2,3},{3,2},{4,5},{5,4},{6,7},{7,6},{8,9},{9,8},{10,11... | collective-permute-start | bytes 1572872 | tf_op jit(solution)/shard_map/ppermute | solution.py:110
  111.9 17.0 %collective-permute-start.31 = (bf16[128,1152]{1,0:T(8,128)(2,1)S(1)}, bf16[128,1152]{1,0:T(8,128)(2,1)S(1)}, u32[]{:S(2)}, u32[]{:S(2)}) collective-permute-start(bf16[128,1152]{1,0:T(8,128)(2,1)S(1)} %pad_maximum_fusion.3), channel_id=1, source_target_pairs={{0,16},{2,18},{4,20},{6,22},{8,24},{10,26},{12,28},{14,30},{16,0},... | collective-permute-start | bytes 884744 | tf_op jit(solution)/shard_map/ppermute | solution.py:106
  114.8 12.0 %collective-permute-start.32 = (bf16[64,1024]{1,0:T(8,128)(2,1)S(1)}, bf16[64,1024]{1,0:T(8,128)(2,1)S(1)}, u32[]{:S(2)}, u32[]{:S(2)}) collective-permute-start(bf16[64,1024]{1,0:T(8,128)(2,1)S(1)} %get-tuple-element.75), channel_id=1, source_target_pairs={{0,1},{1,0},{2,3},{3,2},{4,5},{5,4},{6,7},{7,6},{8,9},{9,8},{10,11... | collective-permute-start | bytes 393224 | tf_op jit(solution)/shard_map/ppermute | solution.py:110
  128.9 14.9 %collective-permute-start.33 = (bf16[256,1152]{1,0:T(8,128)(2,1)S(1)}, bf16[256,1152]{1,0:T(8,128)(2,1)S(1)}, u32[]{:S(2)}, u32[]{:S(2)}) collective-permute-start(bf16[256,1152]{1,0:T(8,128)(2,1)S(1)} %constant_dynamic-update-slice_fusion.4.refs_5_), channel_id=1, source_target_pairs={{0,1},{1,0},{2,3},{3,2},{4,5},{5,4},{6,7},{7,6},{8,9},{9,8},{10,11... | collective-permute-start | bytes 1769480 | tf_op jit(solution)/shard_map/ppermute | solution.py:110
  128.9 8.7 %collective-permute-start.26 = (bf16[4,64,512]{2,1,0:T(8,128)(2,1)S(1)}, bf16[4,64,512]{2,1,0:T(8,128)(2,1)S(1)}, u32[]{:S(2)}, u32[]{:S(2)}) collective-permute-start(bf16[4,64,512]{2,1,0:T(8,128)(2,1)S(1)} %hidden.1.refs_0_), channel_id=1, source_target_pairs={{0,2},{2,0},{4,6},{6,4},{8,10},{10,8},{12,14},{14,12},{16,18},{18,... | collective-permute-start | bytes 786440 | tf_op jit(solution)/shard_map/ppermute | solution.py:106
  129.9 8.8 %collective-permute-start.27 = (bf16[4,64,512]{2,1,0:T(8,128)(2,1)S(1)}, bf16[4,64,512]{2,1,0:T(8,128)(2,1)S(1)}, u32[]{:S(2)}, u32[]{:S(2)}) collective-permute-start(bf16[4,64,512]{2,1,0:T(8,128)(2,1)S(1)} %hidden.1.refs_0_), channel_id=1, source_target_pairs={{0,4},{2,6},{4,0},{6,2},{8,12},{10,14},{12,8},{14,10},{16,20},{18,... | collective-permute-start | bytes 786440 | tf_op jit(solution)/shard_map/ppermute | solution.py:106
  (28 other events, 165.1 us)

commit v15 on v14

--- a/solution.py
+++ b/solution.py
@@ -411,7 +411,7 @@
     line = [mine] + [hop(mine, flip(0, 0, s)) for s in range(1, NZ)]
 
     to_x, to_y = flip(0, 1), flip(1, 0)
-    w_rows = heads_in_plane(after(w_proj, mine), y, x, line[1])
+    w_rows = heads_in_plane(w_proj, y, x, mine)
     w_pieces = [
         jnp.concatenate([pick_row(w, e ^ (z & 1)) for w in w_rows]).reshape(-1, 4 * W)
         for e in range(2)
@@ -422,14 +422,18 @@
     neg = with_marks(neg_emb, float_parts(norms) + whole_parts(own_ids, 256))
 
     out_pair = pair_up(after(w_out[None], mine))
-    w_pieces, neg, out_pair, line = lax.optimization_barrier((w_pieces, neg, out_pair, line))
-    near = jnp.concatenate(line)
-    near_x, near_y = hop(near, to_x), hop(near, to_y)
-    tok = [near, near_x, near_y, *across(near_x, near_y)]
+    low = jnp.concatenate(line[:2])
+    low_x, low_y = hop(low, to_x), hop(low, to_y)
+    low_xy = across(low_x, low_y)
+    w_pieces, neg, out_pair, high = lax.optimization_barrier((w_pieces, neg, out_pair, line[2:]))
+    high = jnp.concatenate(high)
+    high_x, high_y = hop(high, to_x), hop(high, to_y)
+    high_xy = across(high_x, high_y)
+    tok = [low, high, low_x, high_x, low_y, high_y, *low_xy, *high_xy]
     w_mine = heads_along_z(w_pieces)
+    w_mine = after(w_mine, low_xy, high_xy)
     w_theirs = [swap_cores(w) for w in w_mine]
     out_own = [out_pair, hop(after(out_pair, w_mine), flip(0, 0, 2))]
-    neg_pair = pair_up(after(neg, w_mine))
     t_rows = after(target_emb.reshape(2, rows, -1), w_theirs)
     t_keep = pick_row(t_rows, u)
     t_send = swap_cores(pick_row(t_rows, 1 - u))
@@ -467,7 +471,8 @@
     )
     out_own, out_pair_theirs, gated = lax.optimization_barrier((out_own, out_pair_theirs, gated))
     gated = jnp.stack([gated[0]] + [hop(gated[s], flip(0, 0, s)) for s in range(1, NZ)])
-    neg_far = hop(after(neg_pair, gated), flip(0, 0, 2))
+    neg_pair = pair_up(after(neg, gated))
+    neg_far = hop(neg_pair, flip(0, 0, 2))
     out_other = [out_pair_theirs, swap_cores(after(out_own[1], gated))]
     gated = [gated, hop(gated, to_x), hop(gated, to_y)]
     gated += across(gated[1], gated[2])
@@ -482,7 +487,7 @@
             pltpu.VMEM((2, half, NZ * W), BF16),
             pltpu.SemaphoreType.DMA((29,)),
         ],
-        [where, *gated, *out_own, *out_other, *tok[:4]],
+        [where, *gated, *out_own, *out_other, *tok[:7:2]],
         "s" + 13 * "h",
         2 * plane * rows * model * NZ * W,
     )

time: 154 us -> 163 us (1.058)
  waiting for transfers between devices: 68.2 us -> 79 us
  Pallas kernels: 16.1 us -> 13.7 us
    ppermute x27 -> x31, waiting for transfers between devices: 68.2 us -> 76.9 us  [hop(): return lax.ppermute(value, 'ctx', perm)]
    pallas_call x6, Pallas kernels: 16.1 us -> 13.7 us  [call(): pl.pallas_call(kernel, out_shape=[jax.ShapeDtypeStruct(shape, dtype) for...]
    ppermute x9, waiting for transfers between devices: 0.02 us -> 2.09 us  [swap_cores(): return lax.ppermute(value, 'tp', SWAP)]
    optimization_barrier x1 -> x0, local copies, waits for them, and re-layouts: 1.92 us -> none  [after(): return lax.optimization_barrier((values, others))[0]]
    ppermute x9, starting transfers between devices: 1.46 us -> 3.37 us  [swap_cores(): return lax.ppermute(value, 'tp', SWAP)]
    ppermute x27 -> x31, starting transfers between devices: 48.3 us -> 47.5 us  [hop(): return lax.ppermute(value, 'ctx', perm)]
    unnamed x33 -> x16, local copies, waits for them, and re-layouts: 7.06 us -> 6.52 us
  transfers between devices with their start and end apart: 38 -> 42, of which waited for: 20 -> 26; matrix products, arithmetic and copies ran while one was open for 4% -> 8% of each run, Pallas kernels for 8% -> 6%
where the time goes in v15:
time: 163 us; the launch traced here: 162 us
  waiting for transfers between devices  79 us (48%)
  starting transfers between devices  53.3 us (33%)
  Pallas kernels  13.7 us (8%)
  local copies, waits for them, and re-layouts  10.4 us (6%)
  other arithmetic  4.79 us (3%)
    ppermute x31, waiting for transfers between devices, hop(): return lax.ppermute(value, 'ctx', perm)  76.9 us
    ppermute x31, starting transfers between devices, hop(): return lax.ppermute(value, 'ctx', perm)  47.5 us
    pallas_call x6, Pallas kernels, call(): pl.pallas_call(kernel, out_shape=[jax.ShapeDtypeStruct(shape, dtype) for...  13.7 us
    unnamed x16, local copies, waits for them, and re-layouts  6.52 us
    ppermute x9, starting transfers between devices, swap_cores(): return lax.ppermute(value, 'tp', SWAP)  3.37 us
  transfers between devices with their start and end apart: 42, of which 26 were waited for; matrix products, arithmetic and copies ran while one was open for 8% of the time, Pallas kernels for 6%

profile of v15, /device:TPU:0, one launch (start us, length us, event | category | flops | bytes accessed | tf_op | source)
XLA Modules:
  0.0 162.2 jit_solution(16452742598874076164)
XLA Ops:
  3.9 4.1 %collective-permute-start.3 = (bf16[64,2176]{1,0:T(8,128)(2,1)S(1)}, bf16[64,2176]{1,0:T(8,128)(2,1)}, u32[]{:S(2)}, u32[]{:S(2)}) collective-permute-start(bf16[64,2176]{1,0:T(8,128)(2,1)S(1)} %mark.1), channel_id=1, source_target_pairs={{0,16},{2,18},{4,20},{6,22},{8,24},{10,26},{12,28},{14,30},{16,0},... | collective-permute-start | bytes 835592 | tf_op jit(solution)/shard_map/ppermute | solution.py:106
  9.5 2.0 %copy.35 = bf16[128,4,1024]{0,2,1:T(8,128)(2,1)S(1)} copy(bf16[128,4,1024]{2,1,0:T(4,128)(2,1)} %param.9) | data formatting | bytes 2097152 | tf_op args[1]
  13.6 1.8 %collective-permute-start.2 = (bf16[1,1024,128]{2,1,0:T(8,128)(2,1)S(1)}, bf16[1,1024,128]{2,1,0:T(8,128)(2,1)S(1)}, u32[]{:S(2)}, u32[]{:S(2)}) collective-permute-start(bf16[1,1024,128]{2,1,0:T(8,128)(2,1)S(1)} %bitcast.68), channel_id=1, source_target_pairs={{0,8},{2,10},{4,12},{6,14},{8,0},{10,2},{12,4},{14,6},{16,24},{18,... | collective-permute-start | bytes 786440 | tf_op jit(solution)/shard_map/ppermute | solution.py:106
  18.1 7.0 %collective-permute-done = bf16[2,2,128,512]{3,2,1,0:T(8,128)(2,1)S(1)} collective-permute-done((bf16[2,2,128,512]{3,2,1,0:T(8,128)(2,1)S(1)}, bf16[2,2,128,512]{3,2,1,0:T(8,128)(2,1)S(1)}, u32[]{:S(2)}, u32[]{:S(2)}) %collective-permute-start) | collective-permute-done | bytes 524320 | tf_op jit(solution)/shard_map/ppermute | solution.py:106
  27.0 6.6 %collective-permute-done.2 = bf16[1,1024,128]{2,1,0:T(8,128)(2,1)S(1)} collective-permute-done((bf16[1,1024,128]{2,1,0:T(8,128)(2,1)S(1)}, bf16[1,1024,128]{2,1,0:T(8,128)(2,1)S(1)}, u32[]{:S(2)}, u32[]{:S(2)}) %collective-permute-start.2) | collective-permute-done | bytes 262176 | tf_op jit(solution)/shard_map/ppermute | solution.py:106
  37.8 2.0 %collective-permute-done.1 = bf16[2,2,128,512]{3,2,1,0:T(8,128)(2,1)S(1)} collective-permute-done((bf16[2,2,128,512]{3,2,1,0:T(8,128)(2,1)S(1)}, bf16[2,2,128,512]{3,2,1,0:T(8,128)(2,1)S(1)}, u32[]{:S(2)}, u32[]{:S(2)}) %collective-permute-start.1) | collective-permute-done | bytes 524320 | tf_op jit(solution)/shard_map/ppermute | solution.py:106
  44.9 6.8 %collective-permute-done.10.refs_4_.refs_11_ = bf16[128,2176]{1,0:T(8,128)(2,1)S(1)} collective-permute-done((bf16[128,2176]{1,0:T(8,128)(2,1)S(1)}, bf16[128,2176]{1,0:T(8,128)(2,1)S(1)}, u32[]{:S(2)}, u32[]{:S(2)}) %collective-permute-start.10) | collective-permute-done | bytes 557088 | tf_op jit(solution)/shard_map/ppermute | solution.py:106
  55.7 8.1 %collective-permute-done.12.refs_3_ = bf16[128,2176]{1,0:T(8,128)(2,1)S(1)} collective-permute-done((bf16[128,2176]{1,0:T(8,128)(2,1)S(1)}, bf16[128,2176]{1,0:T(8,128)(2,1)S(1)}, u32[]{:S(2)}, u32[]{:S(2)}) %collective-permute-start.12) | collective-permute-done | bytes 557088 | tf_op jit(solution)/shard_map/ppermute | solution.py:106
  68.5 2.1 %collective-permute-done.9.refs_6_.refs_12_ = bf16[64,2176]{1,0:T(8,128)(2,1)S(1)} collective-permute-done((bf16[64,2176]{1,0:T(8,128)(2,1)S(1)}, bf16[64,2176]{1,0:T(8,128)(2,1)S(1)}, u32[]{:S(2)}, u32[]{:S(2)}) %collective-permute-start.9) | collective-permute-done | bytes 278560 | tf_op jit(solution)/shard_map/ppermute | solution.py:106
  70.6 3.0 %collective-permute-done.13.refs_8_ = bf16[64,2176]{1,0:T(8,128)(2,1)S(1)} collective-permute-done((bf16[64,2176]{1,0:T(8,128)(2,1)S(1)}, bf16[64,2176]{1,0:T(8,128)(2,1)S(1)}, u32[]{:S(2)}, u32[]{:S(2)}) %collective-permute-start.13) | collective-permute-done | bytes 278560 | tf_op jit(solution)/shard_map/ppermute | solution.py:106
  73.6 2.4 %collective-permute-start.17 = (bf16[512,512]{1,0:T(8,128)(2,1)S(1)}, bf16[512,512]{1,0:T(8,128)(2,1)S(1)}, u32[]{:S(2)}, u32[]{:S(2)}) collective-permute-start(bf16[512,512]{1,0:T(8,128)(2,1)S(1)} %collective-permute-done.5.refs_10_), channel_id=1, source_target_pairs={{0,1},{1,0},{2,3},{3,2},{4,5},{5,4},{6,7},{7,6},{8,9},{9,8},{10,11... | collective-permute-start | bytes 1572872 | tf_op jit(solution)/shard_map/ppermute | solution.py:110
  76.1 7.1 %collective-permute-start.16 = (bf16[2,1024,128]{2,1,0:T(8,128)(2,1)S(1)}, bf16[2,1024,128]{2,1,0:T(8,128)(2,1)S(1)}, u32[]{:S(2)}, u32[]{:S(2)}) collective-permute-start(bf16[2,1024,128]{2,1,0:T(8,128)(2,1)S(1)} %pad_maximum_fusion.3.refs_5_), channel_id=1, source_target_pairs={{0,16},{2,18},{4,20},{6,22},{8,24},{10,26},{12,28},{14,30},{16,0},... | collective-permute-start | bytes 1572872 | tf_op jit(solution)/shard_map/ppermute | solution.py:106
  83.2 4.0 %project.1 = (bf16[1024,256]{1,0:T(8,128)(2,1)S(1)}, bf16[1024,128]{1,0:T(8,128)(2,1)S(1)}, bf16[1024,128]{1,0:T(8,128)(2,1)S(1)}, bf16[1024,128]{1,0:T(8,128)(2,1)S(1)}) custom-call(s32[4]{0:T(128)S(1)} %pad_add_fusion.where, bf16[128,2176]{1,0:T(8,128)(2,1)S(1)} %pad_maximum_fusion.refs_0_.refs_9_, ...), custom_call_target="tpu_custom_call" | custom-call | bytes 6553616 | tf_op jit(solution)/shard_map/project/pallas_call | solution.py:359
  90.0 3.4 %attend.1 = bf16[4,4,64,128]{3,2,1,0:T(8,128)(2,1)S(1)} custom-call(bf16[1024,256]{1,0:T(8,128)(2,1)S(1)} %get-tuple-element.44.refs_0_, bf16[1024,128]{1,0:T(8,128)(2,1)S(1)} %get-tuple-element.45.refs_1_, bf16[1024,128]{1,0:T(8,128)(2,1)S(1)} %get-tuple-element.42.refs_2_, bf16[1024,128]{1,0:T(8,128)(2,1)S(1)} %collective-permute-done.20.refs_3_, ...), custom_call_target="tpu_custom_call" | custom-call | bytes 1835008 | tf_op jit(solution)/shard_map/attend/pallas_call | solution.py:359
  93.4 13.2 %collective-permute-done.16.refs_6_ = bf16[2,1024,128]{2,1,0:T(8,128)(2,1)S(1)} collective-permute-done((bf16[2,1024,128]{2,1,0:T(8,128)(2,1)S(1)}, bf16[2,1024,128]{2,1,0:T(8,128)(2,1)S(1)}, u32[]{:S(2)}, u32[]{:S(2)}) %collective-permute-start.16) | collective-permute-done | bytes 524320 | tf_op jit(solution)/shard_map/ppermute | solution.py:106
  106.7 2.2 %collective-permute-start.23 = (bf16[4,64,128]{2,1,0:T(8,128)(2,1)S(1)}, bf16[4,64,128]{2,1,0:T(8,128)(2,1)S(1)}, u32[]{:S(2)}, u32[]{:S(2)}) collective-permute-start(bf16[4,64,128]{2,1,0:T(8,128)(2,1)S(1)} %get-tuple-element.74), channel_id=1, source_target_pairs={{0,16},{2,18},{4,20},{6,22},{8,24},{10,26},{12,28},{14,30},{16,0},... | collective-permute-start | bytes 196616 | tf_op jit(solution)/shard_map/ppermute | solution.py:106
  109.0 2.1 %collective-permute-start.24 = (bf16[4,64,128]{2,1,0:T(8,128)(2,1)S(1)}, bf16[4,64,128]{2,1,0:T(8,128)(2,1)S(1)}, u32[]{:S(2)}, u32[]{:S(2)}) collective-permute-start(bf16[4,64,128]{2,1,0:T(8,128)(2,1)S(1)} %get-tuple-element.73), channel_id=1, source_target_pairs={{0,24},{2,26},{4,28},{6,30},{8,16},{10,18},{12,20},{14,22},{16,8},... | collective-permute-start | bytes 196616 | tf_op jit(solution)/shard_map/ppermute | solution.py:106
  111.2 2.9 %collective-permute-done.23 = bf16[4,64,128]{2,1,0:T(8,128)(2,1)S(1)} collective-permute-done((bf16[4,64,128]{2,1,0:T(8,128)(2,1)S(1)}, bf16[4,64,128]{2,1,0:T(8,128)(2,1)S(1)}, u32[]{:S(2)}, u32[]{:S(2)}) %collective-permute-start.23) | collective-permute-done | bytes 65568 | tf_op jit(solution)/shard_map/ppermute | solution.py:106
  124.1 2.0 %collective-permute-done.25.refs_1_ = bf16[4,4,64,128]{3,2,1,0:T(8,128)(2,1)S(1)} collective-permute-done((bf16[4,4,64,128]{3,2,1,0:T(8,128)(2,1)S(1)}, bf16[4,4,64,128]{3,2,1,0:T(8,128)(2,1)S(1)}, u32[]{:S(2)}, u32[]{:S(2)}) %collective-permute-start.25) | collective-permute-done | bytes 262176 | tf_op jit(solution)/shard_map/ppermute | solution.py:106
  129.2 2.0 %collective-permute-done.27.refs_3_ = bf16[2,4,64,128]{3,2,1,0:T(8,128)(2,1)S(1)} collective-permute-done((bf16[2,4,64,128]{3,2,1,0:T(8,128)(2,1)S(1)}, bf16[2,4,64,128]{3,2,1,0:T(8,128)(2,1)S(1)}, u32[]{:S(2)}, u32[]{:S(2)}) %collective-permute-start.27) | collective-permute-done | bytes 131104 | tf_op jit(solution)/shard_map/ppermute | solution.py:106
  132.7 2.7 %hidden.1.refs_0_ = bf16[4,64,512]{2,1,0:T(8,128)(2,1)S(1)} custom-call(s32[4]{0:T(128)S(1)} %pad_add_fusion.where, bf16[4,4,64,128]{3,2,1,0:T(8,128)(2,1)S(1)} %pad_maximum_fusion.5.refs_0_, bf16[4,4,64,128]{3,2,1,0:T(8,128)(2,1)S(1)} %collective-permute-done.25.refs_1_, bf16[4,4,64,128]{3,2,1,0:T(8,128)(2,1)S(1)} %collective-permute-done.26.refs_2_, ...), custom_call_target="tpu_custom_call" | custom-call | flops 536870912 | bytes 5095440 | tf_op jit(solution)/shard_map/hidden/pallas_call | solution.py:359
  139.4 6.7 %collective-permute-done.30.refs_1_ = bf16[4,64,512]{2,1,0:T(8,128)(2,1)S(1)} collective-permute-done((bf16[4,64,512]{2,1,0:T(8,128)(2,1)S(1)}, bf16[4,64,512]{2,1,0:T(8,128)(2,1)S(1)}, u32[]{:S(2)}, u32[]{:S(2)}) %collective-permute-start.30) | collective-permute-done | bytes 262176 | tf_op jit(solution)/shard_map/ppermute | solution.py:106
  148.2 3.0 %collective-permute-done.32.refs_3_ = bf16[2,64,512]{2,1,0:T(8,128)(2,1)S(1)} collective-permute-done((bf16[2,64,512]{2,1,0:T(8,128)(2,1)S(1)}, bf16[2,64,512]{2,1,0:T(8,128)(2,1)S(1)}, u32[]{:S(2)}, u32[]{:S(2)}) %collective-permute-start.32) | collective-permute-done | bytes 131104 | tf_op jit(solution)/shard_map/ppermute | solution.py:106
  158.5 2.4 %collective-permute-done.41.refs_3_ = f32[1,64]{1,0:T(1,128)S(1)} collective-permute-done((f32[1,64]{1,0:T(1,128)S(1)}, f32[1,64]{1,0:T(1,128)S(1)}, u32[]{:S(2)}, u32[]{:S(2)}) %collective-permute-start.41) | collective-permute-done | bytes 288 | tf_op jit(solution)/shard_map/ppermute | solution.py:106
  (117 shorter events, 61.4 us)
Async XLA Ops:
  3.9 36.0 %collective-permute-start.3 = (bf16[64,2176]{1,0:T(8,128)(2,1)S(1)}, bf16[64,2176]{1,0:T(8,128)(2,1)}, u32[]{:S(2)}, u32[]{:S(2)}) collective-permute-start(bf16[64,2176]{1,0:T(8,128)(2,1)S(1)} %mark.1), channel_id=1, source_target_pairs={{0,16},{2,18},{4,20},{6,22},{8,24},{10,26},{12,28},{14,30},{16,0},... | collective-permute-start | bytes 835592 | tf_op jit(solution)/shard_map/ppermute | solution.py:106
  8.0 31.9 %collective-permute-start.4 = (bf16[64,2176]{1,0:T(8,128)(2,1)S(1)}, bf16[64,2176]{1,0:T(8,128)(2,1)}, u32[]{:S(2)}, u32[]{:S(2)}) collective-permute-start(bf16[64,2176]{1,0:T(8,128)(2,1)S(1)} %mark.1), channel_id=1, source_target_pairs={{0,24},{2,26},{4,28},{6,30},{8,16},{10,18},{12,20},{14,22},{16,8},... | collective-permute-start | bytes 835592 | tf_op jit(solution)/shard_map/ppermute | solution.py:106
  9.3 24.3 %collective-permute-start.7 = (bf16[64,2176]{1,0:T(8,128)(2,1)S(1)}, bf16[64,2176]{1,0:T(8,128)(2,1)}, u32[]{:S(2)}, u32[]{:S(2)}) collective-permute-start(bf16[64,2176]{1,0:T(8,128)(2,1)S(1)} %mark.1), channel_id=1, source_target_pairs={{0,8},{2,10},{4,12},{6,14},{8,0},{10,2},{12,4},{14,6},{16,24},{18,... | collective-permute-start | bytes 835592 | tf_op jit(solution)/shard_map/ppermute | solution.py:106
  12.0 13.2 %collective-permute-start = (bf16[2,2,128,512]{3,2,1,0:T(8,128)(2,1)S(1)}, bf16[2,2,128,512]{3,2,1,0:T(8,128)(2,1)S(1)}, u32[]{:S(2)}, u32[]{:S(2)}) collective-permute-start(bf16[2,2,128,512]{3,2,1,0:T(8,128)(2,1)S(1)} %bitcast.64), channel_id=1, source_target_pairs={{0,2},{2,0},{4,6},{6,4},{8,10},{10,8},{12,14},{14,12},{16,18},{18,... | collective-permute-start | bytes 1572872 | tf_op jit(solution)/shard_map/ppermute | solution.py:106
  13.6 20.0 %collective-permute-start.2 = (bf16[1,1024,128]{2,1,0:T(8,128)(2,1)S(1)}, bf16[1,1024,128]{2,1,0:T(8,128)(2,1)S(1)}, u32[]{:S(2)}, u32[]{:S(2)}) collective-permute-start(bf16[1,1024,128]{2,1,0:T(8,128)(2,1)S(1)} %bitcast.68), channel_id=1, source_target_pairs={{0,8},{2,10},{4,12},{6,14},{8,0},{10,2},{12,4},{14,6},{16,24},{18,... | collective-permute-start | bytes 786440 | tf_op jit(solution)/shard_map/ppermute | solution.py:106
  25.4 14.4 %collective-permute-start.1 = (bf16[2,2,128,512]{3,2,1,0:T(8,128)(2,1)S(1)}, bf16[2,2,128,512]{3,2,1,0:T(8,128)(2,1)S(1)}, u32[]{:S(2)}, u32[]{:S(2)}) collective-permute-start(bf16[2,2,128,512]{3,2,1,0:T(8,128)(2,1)S(1)} %copy_bitcast_fusion), channel_id=1, source_target_pairs={{0,4},{2,6},{4,0},{6,2},{8,12},{10,14},{12,8},{14,10},{16,20},{18,... | collective-permute-start | bytes 1572872 | tf_op jit(solution)/shard_map/ppermute | solution.py:106
  34.6 17.1 %collective-permute-start.10 = (bf16[128,2176]{1,0:T(8,128)(2,1)S(1)}, bf16[128,2176]{1,0:T(8,128)(2,1)S(1)}, u32[]{:S(2)}, u32[]{:S(2)}) collective-permute-start(bf16[128,2176]{1,0:T(8,128)(2,1)S(1)} %pad_maximum_fusion.refs_0_.refs_9_), channel_id=1, source_target_pairs={{0,4},{2,6},{4,0},{6,2},{8,12},{10,14},{12,8},{14,10},{16,20},{18,... | collective-permute-start | bytes 1671176 | tf_op jit(solution)/shard_map/ppermute | solution.py:106
  36.3 17.8 %collective-permute-start.8 = (bf16[128,2176]{1,0:T(8,128)(2,1)S(1)}, bf16[128,2176]{1,0:T(8,128)(2,1)S(1)}, u32[]{:S(2)}, u32[]{:S(2)}) collective-permute-start(bf16[128,2176]{1,0:T(8,128)(2,1)S(1)} %pad_maximum_fusion.refs_0_.refs_9_), channel_id=1, source_target_pairs={{0,2},{2,0},{4,6},{6,4},{8,10},{10,8},{12,14},{14,12},{16,18},{18,... | collective-permute-start | bytes 1671176 | tf_op jit(solution)/shard_map/ppermute | solution.py:106
  41.9 21.9 %collective-permute-start.12 = (bf16[128,2176]{1,0:T(8,128)(2,1)S(1)}, bf16[128,2176]{1,0:T(8,128)(2,1)S(1)}, u32[]{:S(2)}, u32[]{:S(2)}) collective-permute-start(bf16[128,2176]{1,0:T(8,128)(2,1)S(1)} %constant_dynamic-update-slice_fusion.refs_1_), channel_id=1, source_target_pairs={{0,2},{2,0},{4,6},{6,4},{8,10},{10,8},{12,14},{14,12},{16,18},{18,... | collective-permute-start | bytes 1671176 | tf_op jit(solution)/shard_map/ppermute | solution.py:106
  43.4 20.9 %collective-permute-start.14 = (bf16[128,2176]{1,0:T(8,128)(2,1)S(1)}, bf16[128,2176]{1,0:T(8,128)(2,1)S(1)}, u32[]{:S(2)}, u32[]{:S(2)}) collective-permute-start(bf16[128,2176]{1,0:T(8,128)(2,1)S(1)} %constant_dynamic-update-slice_fusion.refs_1_), channel_id=1, source_target_pairs={{0,4},{2,6},{4,0},{6,2},{8,12},{10,14},{12,8},{14,10},{16,20},{18,... | collective-permute-start | bytes 1671176 | tf_op jit(solution)/shard_map/ppermute | solution.py:106
  51.7 15.3 %collective-permute-start.11 = (bf16[64,2176]{1,0:T(8,128)(2,1)S(1)}, bf16[64,2176]{1,0:T(8,128)(2,1)S(1)}, u32[]{:S(2)}, u32[]{:S(2)}) collective-permute-start(bf16[64,2176]{1,0:T(8,128)(2,1)S(1)} %slice.65), channel_id=1, source_target_pairs={{0,2},{2,0},{4,6},{6,4},{8,10},{10,8},{12,14},{14,12},{16,18},{18,... | collective-permute-start | bytes 835592 | tf_op jit(solution)/shard_map/ppermute | solution.py:106
  53.2 17.4 %collective-permute-start.5 = (bf16[512,512]{1,0:T(8,128)(2,1)S(1)}, bf16[512,512]{1,0:T(8,128)(2,1)S(1)}, u32[]{:S(2)}, u32[]{:S(2)}) collective-permute-start(bf16[512,512]{1,0:T(8,128)(2,1)S(1)} %bitcast.66), channel_id=1, source_target_pairs={{0,0},{1,16},{2,2},{3,18},{4,4},{5,20},{6,6},{7,22},{8,8},{9,24},{... | collective-permute-start | bytes 1572872 | tf_op jit(solution)/shard_map/ppermute | solution.py:148
  54.1 16.5 %collective-permute-start.6 = (bf16[512,512]{1,0:T(8,128)(2,1)S(1)}, bf16[512,512]{1,0:T(8,128)(2,1)S(1)}, u32[]{:S(2)}, u32[]{:S(2)}) collective-permute-start(bf16[512,512]{1,0:T(8,128)(2,1)S(1)} %bitcast.65), channel_id=1, source_target_pairs={{0,8},{1,24},{2,10},{3,26},{4,12},{5,28},{6,14},{7,30},{8,0},{9,16... | collective-permute-start | bytes 1572872 | tf_op jit(solution)/shard_map/ppermute | solution.py:148
  64.3 9.3 %collective-permute-start.13 = (bf16[64,2176]{1,0:T(8,128)(2,1)S(1)}, bf16[64,2176]{1,0:T(8,128)(2,1)S(1)}, u32[]{:S(2)}, u32[]{:S(2)}) collective-permute-start(bf16[64,2176]{1,0:T(8,128)(2,1)S(1)} %slice.66), channel_id=1, source_target_pairs={{0,4},{2,6},{4,0},{6,2},{8,12},{10,14},{12,8},{14,10},{16,20},{18,... | collective-permute-start | bytes 835592 | tf_op jit(solution)/shard_map/ppermute | solution.py:106
  73.6 9.7 %collective-permute-start.17 = (bf16[512,512]{1,0:T(8,128)(2,1)S(1)}, bf16[512,512]{1,0:T(8,128)(2,1)S(1)}, u32[]{:S(2)}, u32[]{:S(2)}) collective-permute-start(bf16[512,512]{1,0:T(8,128)(2,1)S(1)} %collective-permute-done.5.refs_10_), channel_id=1, source_target_pairs={{0,1},{1,0},{2,3},{3,2},{4,5},{5,4},{6,7},{7,6},{8,9},{9,8},{10,11... | collective-permute-start | bytes 1572872 | tf_op jit(solution)/shard_map/ppermute | solution.py:110
  76.1 30.5 %collective-permute-start.16 = (bf16[2,1024,128]{2,1,0:T(8,128)(2,1)S(1)}, bf16[2,1024,128]{2,1,0:T(8,128)(2,1)S(1)}, u32[]{:S(2)}, u32[]{:S(2)}) collective-permute-start(bf16[2,1024,128]{2,1,0:T(8,128)(2,1)S(1)} %pad_maximum_fusion.3.refs_5_), channel_id=1, source_target_pairs={{0,16},{2,18},{4,20},{6,22},{8,24},{10,26},{12,28},{14,30},{16,0},... | collective-permute-start | bytes 1572872 | tf_op jit(solution)/shard_map/ppermute | solution.py:106
  87.3 19.3 %collective-permute-start.19 = (bf16[2,1024,128]{2,1,0:T(8,128)(2,1)S(1)}, bf16[2,1024,128]{2,1,0:T(8,128)(2,1)S(1)}, u32[]{:S(2)}, u32[]{:S(2)}) collective-permute-start(bf16[2,1024,128]{2,1,0:T(8,128)(2,1)S(1)} %pad_maximum_fusion.3.refs_5_), channel_id=1, source_target_pairs={{0,1},{1,0},{2,3},{3,2},{4,5},{5,4},{6,7},{7,6},{8,9},{9,8},{10,11... | collective-permute-start | bytes 1572872 | tf_op jit(solution)/shard_map/ppermute | solution.py:110
  117.3 18.2 %collective-permute-start.36 = (bf16[64,1024]{1,0:T(8,128)(2,1)S(1)}, bf16[64,1024]{1,0:T(8,128)(2,1)S(1)}, u32[]{:S(2)}, u32[]{:S(2)}) collective-permute-start(bf16[64,1024]{1,0:T(8,128)(2,1)S(1)} %get-tuple-element.71), channel_id=1, source_target_pairs={{0,1},{1,0},{2,3},{3,2},{4,5},{5,4},{6,7},{7,6},{8,9},{9,8},{10,11... | collective-permute-start | bytes 393224 | tf_op jit(solution)/shard_map/ppermute | solution.py:110
  117.4 8.7 %collective-permute-start.25 = (bf16[4,4,64,128]{3,2,1,0:T(8,128)(2,1)S(1)}, bf16[4,4,64,128]{3,2,1,0:T(8,128)(2,1)S(1)}, u32[]{:S(2)}, u32[]{:S(2)}) collective-permute-start(bf16[4,4,64,128]{3,2,1,0:T(8,128)(2,1)S(1)} %pad_maximum_fusion.5.refs_0_), channel_id=1, source_target_pairs={{0,2},{2,0},{4,6},{6,4},{8,10},{10,8},{12,14},{14,12},{16,18},{18,... | collective-permute-start | bytes 786440 | tf_op jit(solution)/shard_map/ppermute | solution.py:106
  118.0 9.7 %collective-permute-start.26 = (bf16[4,4,64,128]{3,2,1,0:T(8,128)(2,1)S(1)}, bf16[4,4,64,128]{3,2,1,0:T(8,128)(2,1)S(1)}, u32[]{:S(2)}, u32[]{:S(2)}) collective-permute-start(bf16[4,4,64,128]{3,2,1,0:T(8,128)(2,1)S(1)} %pad_maximum_fusion.5.refs_0_), channel_id=1, source_target_pairs={{0,4},{2,6},{4,0},{6,2},{8,12},{10,14},{12,8},{14,10},{16,20},{18,... | collective-permute-start | bytes 786440 | tf_op jit(solution)/shard_map/ppermute | solution.py:106
  119.5 13.3 %collective-permute-start.29 = (bf16[2,1024,128]{2,1,0:T(8,128)(2,1)S(1)}, bf16[2,1024,128]{2,1,0:T(8,128)(2,1)S(1)}, u32[]{:S(2)}, u32[]{:S(2)}) collective-permute-start(bf16[2,1024,128]{2,1,0:T(8,128)(2,1)S(1)} %collective-permute-done.16.refs_6_), channel_id=1, source_target_pairs={{0,1},{1,0},{2,3},{3,2},{4,5},{5,4},{6,7},{7,6},{8,9},{9,8},{10,11... | collective-permute-start | bytes 1572872 | tf_op jit(solution)/shard_map/ppermute | solution.py:110
  121.7 15.5 %collective-permute-start.35 = (bf16[128,1152]{1,0:T(8,128)(2,1)S(1)}, bf16[128,1152]{1,0:T(8,128)(2,1)S(1)}, u32[]{:S(2)}, u32[]{:S(2)}) collective-permute-start(bf16[128,1152]{1,0:T(8,128)(2,1)S(1)} %pad_maximum_fusion.4), channel_id=1, source_target_pairs={{0,16},{2,18},{4,20},{6,22},{8,24},{10,26},{12,28},{14,30},{16,0},... | collective-permute-start | bytes 884744 | tf_op jit(solution)/shard_map/ppermute | solution.py:106
  137.2 15.1 %collective-permute-start.37 = (bf16[256,1152]{1,0:T(8,128)(2,1)S(1)}, bf16[256,1152]{1,0:T(8,128)(2,1)S(1)}, u32[]{:S(2)}, u32[]{:S(2)}) collective-permute-start(bf16[256,1152]{1,0:T(8,128)(2,1)S(1)} %constant_dynamic-update-slice_fusion.2.refs_5_), channel_id=1, source_target_pairs={{0,1},{1,0},{2,3},{3,2},{4,5},{5,4},{6,7},{7,6},{8,9},{9,8},{10,11... | collective-permute-start | bytes 1769480 | tf_op jit(solution)/shard_map/ppermute | solution.py:110
  137.3 8.7 %collective-permute-start.30 = (bf16[4,64,512]{2,1,0:T(8,128)(2,1)S(1)}, bf16[4,64,512]{2,1,0:T(8,128)(2,1)S(1)}, u32[]{:S(2)}, u32[]{:S(2)}) collective-permute-start(bf16[4,64,512]{2,1,0:T(8,128)(2,1)S(1)} %hidden.1.refs_0_), channel_id=1, source_target_pairs={{0,2},{2,0},{4,6},{6,4},{8,10},{10,8},{12,14},{14,12},{16,18},{18,... | collective-permute-start | bytes 786440 | tf_op jit(solution)/shard_map/ppermute | solution.py:106
  (24 other events, 129.9 us)

commit v16 on v14

--- a/solution.py
+++ b/solution.py
@@ -128,12 +128,16 @@
 
 
 def heads_in_plane(w_proj, y, x, first):
-    heads = w_proj.reshape(-1, 4, 2, NY, NX, W).transpose(4, 3, 2, 0, 1, 5)
-    heads = heads.reshape(NX, NY, 2, -1, 4 * W)
-    kept, sent = pick_row(heads, x), after(pick_row(heads, x ^ 1), first)
-    came = hop(sent, flip(0, 1))
-    lined = jnp.where(x == 0, jnp.stack([kept, came], 2), jnp.stack([came, kept], 2))
-    return pick_row(lined, y), hop(pick_row(lined, y ^ 1), flip(1, 0))
+    plane = NY * NX
+    heads = w_proj.reshape(-1, 4, 2, plane, W).transpose(3, 2, 0, 1, 4)
+    heads = heads.reshape(plane, 2, -1, 4 * W)
+    out = []
+    for by, bx in PLANE:
+        piece = pick_row(heads, (y ^ by) * NX + (x ^ bx))
+        if (by, bx) != (0, 0):
+            piece = hop(after(piece, first if len(out) < plane - 1 else out[1:]), flip(by, bx))
+        out.append(piece)
+    return out
 
 
 def heads_along_z(pieces):
@@ -181,15 +185,15 @@
     count = len(refs) - 12
     tok, w_own, w_other = refs[:count], refs[count : count + 2], refs[count + 2 : count + 4]
     gate_query, value, key, marks, x_all, w_all, tok_sem, w_sem = refs[count + 4 :]
-    z, y, u = where[0], where[1], where[3]
+    z, y, x, u = (where[i] for i in range(4))
     copies, base = [], 0
     for side, (at, srcs) in enumerate(((u, w_own), (1 - u, w_other))):
         for e, src in enumerate(srcs):
-            size = src.shape[0] // 2
-            for j in range(2):
-                start = ((2 * at + (e ^ (z & 1))) * 2 + (y ^ j)) * size
+            size = src.shape[0] // len(PLANE)
+            for j, (by, bx) in enumerate(PLANE):
+                start = chip_at(2 * at + (e ^ (z & 1)), y ^ by, x ^ bx) * size
                 to = w_all.at[pl.ds(pl.multiple_of(start, size), size), :]
-                sem = w_sem.at[4 * side + 2 * e + j]
+                sem = w_sem.at[(2 * side + e) * len(PLANE) + j]
                 copies.append(pltpu.make_async_copy(src.at[pl.ds(j * size, size), :], to, sem))
     for i, ref in enumerate(tok):
         rows = pl.ds(base, ref.shape[0])
@@ -411,7 +415,7 @@
     line = [mine] + [hop(mine, flip(0, 0, s)) for s in range(1, NZ)]
 
     to_x, to_y = flip(0, 1), flip(1, 0)
-    w_rows = heads_in_plane(after(w_proj, mine), y, x, line[1])
+    w_rows = heads_in_plane(w_proj, y, x, mine)
     w_pieces = [
         jnp.concatenate([pick_row(w, e ^ (z & 1)) for w in w_rows]).reshape(-1, 4 * W)
         for e in range(2)
@@ -421,7 +425,7 @@
     norms = jnp.sum(jnp.square(neg_emb.astype(F32)), axis=1)
     neg = with_marks(neg_emb, float_parts(norms) + whole_parts(own_ids, 256))
 
-    out_pair = pair_up(after(w_out[None], mine))
+    out_pair = pair_up(after(w_out[None], w_rows[1:3]))
     w_pieces, neg, out_pair, line = lax.optimization_barrier((w_pieces, neg, out_pair, line))
     near = jnp.concatenate(line)
     near_x, near_y = hop(near, to_x), hop(near, to_y)
@@ -429,7 +433,6 @@
     w_mine = heads_along_z(w_pieces)
     w_theirs = [swap_cores(w) for w in w_mine]
     out_own = [out_pair, hop(after(out_pair, w_mine), flip(0, 0, 2))]
-    neg_pair = pair_up(after(neg, w_mine))
     t_rows = after(target_emb.reshape(2, rows, -1), w_theirs)
     t_keep = pick_row(t_rows, u)
     t_send = swap_cores(pick_row(t_rows, 1 - u))
@@ -444,7 +447,7 @@
                 pltpu.VMEM((count, model + W), BF16),
                 pltpu.VMEM((model, 4 * W), BF16),
                 pltpu.SemaphoreType.DMA((len(pieces),)),
-                pltpu.SemaphoreType.DMA((8,)),
+                pltpu.SemaphoreType.DMA((16,)),
             ],
             [where, *pieces, *w_mine, *w_theirs],
             "s" + (len(pieces) + 4) * "h",
@@ -467,7 +470,8 @@
     )
     out_own, out_pair_theirs, gated = lax.optimization_barrier((out_own, out_pair_theirs, gated))
     gated = jnp.stack([gated[0]] + [hop(gated[s], flip(0, 0, s)) for s in range(1, NZ)])
-    neg_far = hop(after(neg_pair, gated), flip(0, 0, 2))
+    neg_pair = pair_up(after(neg, gated))
+    neg_far = hop(neg_pair, flip(0, 0, 2))
     out_other = [out_pair_theirs, swap_cores(after(out_own[1], gated))]
     gated = [gated, hop(gated, to_x), hop(gated, to_y)]
     gated += across(gated[1], gated[2])

time: 154 us -> 149 us (0.968)
  starting transfers between devices: 52.2 us -> 35.1 us
  waiting for transfers between devices: 68.2 us -> 80.2 us
    ppermute x27 -> x28, starting transfers between devices: 48.3 us -> 32.2 us  [hop(): return lax.ppermute(value, 'ctx', perm)]
    ppermute x27 -> x28, waiting for transfers between devices: 68.2 us -> 78.1 us  [hop(): return lax.ppermute(value, 'ctx', perm)]
    squeeze x4 -> x6, local copies, waits for them, and re-layouts: 0.13 us -> 2.25 us  [pick_row(): return lax.dynamic_index_in_dim(value, at, 0, keepdims=False)]
    ppermute x9, waiting for transfers between devices: 0.02 us -> 2.09 us  [swap_cores(): return lax.ppermute(value, 'tp', SWAP)]
    optimization_barrier x1 -> x0, local copies, waits for them, and re-layouts: 1.92 us -> none  [after(): return lax.optimization_barrier((values, others))[0]]
    reshape x0 -> x2, local copies, waits for them, and re-layouts: none -> 1.91 us  [the longest x1 1.47 us: heads_in_plane(): heads = w_proj.reshape(-1, 4, 2, plane, W).transpose(3, 2, 0, 1, 4)]
    unnamed x33 -> x43, local copies, waits for them, and re-layouts: 7.06 us -> 6.65 us
  transfers between devices with their start and end apart: 38 -> 39, of which waited for: 20 -> 24; matrix products, arithmetic and copies ran while one was open for 4% -> 6% of each run, Pallas kernels for 8% -> 9%
where the time goes in v16:
time: 149 us
  waiting for transfers between devices  80.2 us (54%)
  starting transfers between devices  35.1 us (24%)
  Pallas kernels  16.6 us (11%)
  local copies, waits for them, and re-layouts  12.3 us (8%)
  other arithmetic  3.56 us (2%)
    ppermute x28, waiting for transfers between devices, hop(): return lax.ppermute(value, 'ctx', perm)  78.1 us
    ppermute x28, starting transfers between devices, hop(): return lax.ppermute(value, 'ctx', perm)  32.2 us
    pallas_call x6, Pallas kernels, call(): pl.pallas_call(kernel, out_shape=[jax.ShapeDtypeStruct(shape, dtype) for...  16.6 us
    unnamed x43, local copies, waits for them, and re-layouts  6.65 us
  transfers between devices with their start and end apart: 39, of which 24 were waited for; matrix products, arithmetic and copies ran while one was open for 6% of the time, Pallas kernels for 9%

profile of v16, /device:TPU:0, one launch (start us, length us, event | category | flops | bytes accessed | tf_op | source)
XLA Modules:
  0.0 148.9 jit_solution(5033764751548104899)
XLA Ops:
  3.9 3.1 %collective-permute-start.4 = (bf16[64,2176]{1,0:T(8,128)(2,1)S(1)}, bf16[64,2176]{1,0:T(8,128)(2,1)}, u32[]{:S(2)}, u32[]{:S(2)}) collective-permute-start(bf16[64,2176]{1,0:T(8,128)(2,1)S(1)} %mark.1), channel_id=1, source_target_pairs={{0,8},{2,10},{4,12},{6,14},{8,0},{10,2},{12,4},{14,6},{16,24},{18,... | collective-permute-start | bytes 835592 | tf_op jit(solution)/shard_map/ppermute | solution.py:106
  7.0 2.6 %collective-permute-start.5 = (bf16[64,2176]{1,0:T(8,128)(2,1)S(1)}, bf16[64,2176]{1,0:T(8,128)(2,1)S(1)}, u32[]{:S(2)}, u32[]{:S(2)}) collective-permute-start(bf16[64,2176]{1,0:T(8,128)(2,1)S(1)} %mark.1), channel_id=1, source_target_pairs={{0,16},{2,18},{4,20},{6,22},{8,24},{10,26},{12,28},{14,30},{16,0},... | collective-permute-start | bytes 835592 | tf_op jit(solution)/shard_map/ppermute | solution.py:106
  12.0 1.8 %collective-permute-start = (bf16[2,128,512]{2,1,0:T(8,128)(2,1)S(1)}, bf16[2,128,512]{2,1,0:T(8,128)(2,1)S(1)}, u32[]{:S(2)}, u32[]{:S(2)}) collective-permute-start(bf16[2,128,512]{2,1,0:T(8,128)(2,1)S(1)} %get-tuple-element.34), channel_id=1, source_target_pairs={{0,2},{2,0},{4,6},{6,4},{8,10},{10,8},{12,14},{14,12},{16,18},{18,... | collective-permute-start | bytes 786440 | tf_op jit(solution)/shard_map/ppermute | solution.py:106
  17.2 2.4 %collective-permute-done = bf16[2,128,512]{2,1,0:T(8,128)(2,1)S(1)} collective-permute-done((bf16[2,128,512]{2,1,0:T(8,128)(2,1)S(1)}, bf16[2,128,512]{2,1,0:T(8,128)(2,1)S(1)}, u32[]{:S(2)}, u32[]{:S(2)}) %collective-permute-start) | collective-permute-done | bytes 262176 | tf_op jit(solution)/shard_map/ppermute | solution.py:106
  24.1 4.1 %collective-permute-done.2 = bf16[2,128,512]{2,1,0:T(8,128)(2,1)S(1)} collective-permute-done((bf16[2,128,512]{2,1,0:T(8,128)(2,1)S(1)}, bf16[2,128,512]{2,1,0:T(8,128)(2,1)S(1)}, u32[]{:S(2)}, u32[]{:S(2)}) %collective-permute-start.2) | collective-permute-done | bytes 262176 | tf_op jit(solution)/shard_map/ppermute | solution.py:106
  28.2 6.0 %collective-permute-done.3 = bf16[1,1024,128]{2,1,0:T(8,128)(2,1)S(1)} collective-permute-done((bf16[1,1024,128]{2,1,0:T(8,128)(2,1)}, bf16[1,1024,128]{2,1,0:T(8,128)(2,1)S(1)}, u32[]{:S(2)}, u32[]{:S(2)}) %collective-permute-start.3) | collective-permute-done | bytes 262176 | tf_op jit(solution)/shard_map/ppermute | solution.py:106
  40.4 22.4 %collective-permute-done.10.refs_1_.refs_10_ = bf16[256,2176]{1,0:T(8,128)(2,1)S(1)} collective-permute-done((bf16[256,2176]{1,0:T(8,128)(2,1)S(1)}, bf16[256,2176]{1,0:T(8,128)(2,1)S(1)}, u32[]{:S(2)}, u32[]{:S(2)}) %collective-permute-start.10) | collective-permute-done | bytes 1114144 | tf_op jit(solution)/shard_map/ppermute | solution.py:106
  65.5 3.3 %collective-permute-start.9 = (bf16[2,1024,128]{2,1,0:T(8,128)(2,1)S(1)}, bf16[2,1024,128]{2,1,0:T(8,128)(2,1)S(1)}, u32[]{:S(2)}, u32[]{:S(2)}) collective-permute-start(bf16[2,1024,128]{2,1,0:T(8,128)(2,1)S(1)} %pad_maximum_fusion.2.refs_5_), channel_id=1, source_target_pairs={{0,16},{2,18},{4,20},{6,22},{8,24},{10,26},{12,28},{14,30},{16,0},... | collective-permute-start | bytes 1572872 | tf_op jit(solution)/shard_map/ppermute | solution.py:106
  68.8 7.8 %collective-permute-done.12.refs_3_.refs_12_ = bf16[128,2176]{1,0:T(8,128)(2,1)S(1)} collective-permute-done((bf16[128,2176]{1,0:T(8,128)(2,1)S(1)}, bf16[128,2176]{1,0:T(8,128)(2,1)S(1)}, u32[]{:S(2)}, u32[]{:S(2)}) %collective-permute-start.12) | collective-permute-done | bytes 557088 | tf_op jit(solution)/shard_map/ppermute | solution.py:106
  77.4 6.9 %project.1 = (bf16[1024,256]{1,0:T(8,128)(2,1)S(1)}, bf16[1024,128]{1,0:T(8,128)(2,1)S(1)}, bf16[1024,128]{1,0:T(8,128)(2,1)S(1)}, bf16[1024,128]{1,0:T(8,128)(2,1)S(1)}) custom-call(s32[4]{0:T(128)S(1)} %pad_add_fusion.where, bf16[256,2176]{1,0:T(8,128)(2,1)S(1)} %constant_dynamic-update-slice_fusion.refs_0_.refs_9_, ...), custom_call_target="tpu_custom_call" | custom-call | bytes 6553616 | tf_op jit(solution)/shard_map/project/pallas_call | solution.py:363
  87.1 3.4 %attend.1 = bf16[4,4,64,128]{3,2,1,0:T(8,128)(2,1)S(1)} custom-call(bf16[1024,256]{1,0:T(8,128)(2,1)S(1)} %get-tuple-element.48.refs_0_, bf16[1024,128]{1,0:T(8,128)(2,1)S(1)} %get-tuple-element.49.refs_1_, bf16[1024,128]{1,0:T(8,128)(2,1)S(1)} %get-tuple-element.46.refs_2_, bf16[1024,128]{1,0:T(8,128)(2,1)S(1)} %collective-permute-done.17.refs_3_, ...), custom_call_target="tpu_custom_call" | custom-call | bytes 1835008 | tf_op jit(solution)/shard_map/attend/pallas_call | solution.py:363
  90.5 2.0 %collective-permute-done.9.refs_6_ = bf16[2,1024,128]{2,1,0:T(8,128)(2,1)S(1)} collective-permute-done((bf16[2,1024,128]{2,1,0:T(8,128)(2,1)S(1)}, bf16[2,1024,128]{2,1,0:T(8,128)(2,1)S(1)}, u32[]{:S(2)}, u32[]{:S(2)}) %collective-permute-start.9) | collective-permute-done | bytes 524320 | tf_op jit(solution)/shard_map/ppermute | solution.py:106
  93.5 2.1 %collective-permute-start.21 = (bf16[4,64,128]{2,1,0:T(8,128)(2,1)S(1)}, bf16[4,64,128]{2,1,0:T(8,128)(2,1)S(1)}, u32[]{:S(2)}, u32[]{:S(2)}) collective-permute-start(bf16[4,64,128]{2,1,0:T(8,128)(2,1)S(1)} %get-tuple-element.76), channel_id=1, source_target_pairs={{0,24},{2,26},{4,28},{6,30},{8,16},{10,18},{12,20},{14,22},{16,8},... | collective-permute-start | bytes 196616 | tf_op jit(solution)/shard_map/ppermute | solution.py:106
  95.6 2.3 %collective-permute-start.19 = (bf16[4,64,128]{2,1,0:T(8,128)(2,1)S(1)}, bf16[4,64,128]{2,1,0:T(8,128)(2,1)S(1)}, u32[]{:S(2)}, u32[]{:S(2)}) collective-permute-start(bf16[4,64,128]{2,1,0:T(8,128)(2,1)S(1)} %get-tuple-element.78), channel_id=1, source_target_pairs={{0,8},{2,10},{4,12},{6,14},{8,0},{10,2},{12,4},{14,6},{16,24},{18,... | collective-permute-start | bytes 196616 | tf_op jit(solution)/shard_map/ppermute | solution.py:106
  97.9 2.4 %collective-permute-done.21 = bf16[4,64,128]{2,1,0:T(8,128)(2,1)S(1)} collective-permute-done((bf16[4,64,128]{2,1,0:T(8,128)(2,1)S(1)}, bf16[4,64,128]{2,1,0:T(8,128)(2,1)S(1)}, u32[]{:S(2)}, u32[]{:S(2)}) %collective-permute-start.21) | collective-permute-done | bytes 65568 | tf_op jit(solution)/shard_map/ppermute | solution.py:106
  100.3 1.9 %collective-permute-done.20 = bf16[4,64,128]{2,1,0:T(8,128)(2,1)S(1)} collective-permute-done((bf16[4,64,128]{2,1,0:T(8,128)(2,1)S(1)}, bf16[4,64,128]{2,1,0:T(8,128)(2,1)S(1)}, u32[]{:S(2)}, u32[]{:S(2)}) %collective-permute-start.20) | collective-permute-done | bytes 65568 | tf_op jit(solution)/shard_map/ppermute | solution.py:106
  105.4 3.5 %collective-permute-done.31 = bf16[64,1152]{1,0:T(8,128)(2,1)} collective-permute-done((bf16[64,1152]{1,0:T(8,128)(2,1)S(1)}, bf16[64,1152]{1,0:T(8,128)(2,1)}, u32[]{:S(2)}, u32[]{:S(2)}) %collective-permute-start.31) | collective-permute-done | bytes 147488 | tf_op jit(solution)/shard_map/ppermute | solution.py:106
  109.9 3.2 %collective-permute-done.22.refs_1_ = bf16[4,4,64,128]{3,2,1,0:T(8,128)(2,1)S(1)} collective-permute-done((bf16[4,4,64,128]{3,2,1,0:T(8,128)(2,1)}, bf16[4,4,64,128]{3,2,1,0:T(8,128)(2,1)S(1)}, u32[]{:S(2)}, u32[]{:S(2)}) %collective-permute-start.22) | collective-permute-done | bytes 262176 | tf_op jit(solution)/shard_map/ppermute | solution.py:106
  115.9 2.4 %collective-permute-done.24.refs_3_ = bf16[2,4,64,128]{3,2,1,0:T(8,128)(2,1)S(1)} collective-permute-done((bf16[2,4,64,128]{3,2,1,0:T(8,128)(2,1)S(1)}, bf16[2,4,64,128]{3,2,1,0:T(8,128)(2,1)S(1)}, u32[]{:S(2)}, u32[]{:S(2)}) %collective-permute-start.24) | collective-permute-done | bytes 131104 | tf_op jit(solution)/shard_map/ppermute | solution.py:106
  119.9 2.7 %hidden.1.refs_0_ = bf16[4,64,512]{2,1,0:T(8,128)(2,1)S(1)} custom-call(s32[4]{0:T(128)S(1)} %pad_add_fusion.where, bf16[4,4,64,128]{3,2,1,0:T(8,128)(2,1)S(1)} %copy-done.6, bf16[4,4,64,128]{3,2,1,0:T(8,128)(2,1)S(1)} %collective-permute-done.22.refs_1_, bf16[4,4,64,128]{3,2,1,0:T(8,128)(2,1)S(1)} %collective-permute-done.23.refs_2_, ...), custom_call_target="tpu_custom_call" | custom-call | flops 536870912 | bytes 7045136 | tf_op jit(solution)/shard_map/hidden/pallas_call | solution.py:363
  122.6 2.6 %collective-permute-done.32 = bf16[128,1152]{1,0:T(8,128)(2,1)S(1)} collective-permute-done((bf16[128,1152]{1,0:T(8,128)(2,1)S(1)}, bf16[128,1152]{1,0:T(8,128)(2,1)S(1)}, u32[]{:S(2)}, u32[]{:S(2)}) %collective-permute-start.32) | collective-permute-done | bytes 294944 | tf_op jit(solution)/shard_map/ppermute | solution.py:106
  126.1 7.8 %collective-permute-done.27.refs_1_ = bf16[4,64,512]{2,1,0:T(8,128)(2,1)S(1)} collective-permute-done((bf16[4,64,512]{2,1,0:T(8,128)(2,1)S(1)}, bf16[4,64,512]{2,1,0:T(8,128)(2,1)S(1)}, u32[]{:S(2)}, u32[]{:S(2)}) %collective-permute-start.27) | collective-permute-done | bytes 262176 | tf_op jit(solution)/shard_map/ppermute | solution.py:106
  134.1 1.7 %collective-permute-start.30 = (bf16[2,64,512]{2,1,0:T(8,128)(2,1)S(1)}, bf16[2,64,512]{2,1,0:T(8,128)(2,1)S(1)}, u32[]{:S(2)}, u32[]{:S(2)}) collective-permute-start(bf16[2,64,512]{2,1,0:T(8,128)(2,1)S(1)} %slice.61), channel_id=1, source_target_pairs={{0,2},{2,0},{4,6},{6,4},{8,10},{10,8},{12,14},{14,12},{16,18},{18,... | collective-permute-start | bytes 393224 | tf_op jit(solution)/shard_map/ppermute | solution.py:106
  135.8 3.3 %collective-permute-done.29.refs_3_ = bf16[2,64,512]{2,1,0:T(8,128)(2,1)S(1)} collective-permute-done((bf16[2,64,512]{2,1,0:T(8,128)(2,1)S(1)}, bf16[2,64,512]{2,1,0:T(8,128)(2,1)S(1)}, u32[]{:S(2)}, u32[]{:S(2)}) %collective-permute-start.29) | collective-permute-done | bytes 131104 | tf_op jit(solution)/shard_map/ppermute | solution.py:106
  (135 shorter events, 46.1 us)
Async XLA Ops:
  3.9 30.4 %collective-permute-start.4 = (bf16[64,2176]{1,0:T(8,128)(2,1)S(1)}, bf16[64,2176]{1,0:T(8,128)(2,1)}, u32[]{:S(2)}, u32[]{:S(2)}) collective-permute-start(bf16[64,2176]{1,0:T(8,128)(2,1)S(1)} %mark.1), channel_id=1, source_target_pairs={{0,8},{2,10},{4,12},{6,14},{8,0},{10,2},{12,4},{14,6},{16,24},{18,... | collective-permute-start | bytes 835592 | tf_op jit(solution)/shard_map/ppermute | solution.py:106
  7.0 27.4 %collective-permute-start.5 = (bf16[64,2176]{1,0:T(8,128)(2,1)S(1)}, bf16[64,2176]{1,0:T(8,128)(2,1)S(1)}, u32[]{:S(2)}, u32[]{:S(2)}) collective-permute-start(bf16[64,2176]{1,0:T(8,128)(2,1)S(1)} %mark.1), channel_id=1, source_target_pairs={{0,16},{2,18},{4,20},{6,22},{8,24},{10,26},{12,28},{14,30},{16,0},... | collective-permute-start | bytes 835592 | tf_op jit(solution)/shard_map/ppermute | solution.py:106
  9.5 24.8 %collective-permute-start.6 = (bf16[64,2176]{1,0:T(8,128)(2,1)S(1)}, bf16[64,2176]{1,0:T(8,128)(2,1)S(1)}, u32[]{:S(2)}, u32[]{:S(2)}) collective-permute-start(bf16[64,2176]{1,0:T(8,128)(2,1)S(1)} %mark.1), channel_id=1, source_target_pairs={{0,24},{2,26},{4,28},{6,30},{8,16},{10,18},{12,20},{14,22},{16,8},... | collective-permute-start | bytes 835592 | tf_op jit(solution)/shard_map/ppermute | solution.py:106
  12.0 7.6 %collective-permute-start = (bf16[2,128,512]{2,1,0:T(8,128)(2,1)S(1)}, bf16[2,128,512]{2,1,0:T(8,128)(2,1)S(1)}, u32[]{:S(2)}, u32[]{:S(2)}) collective-permute-start(bf16[2,128,512]{2,1,0:T(8,128)(2,1)S(1)} %get-tuple-element.34), channel_id=1, source_target_pairs={{0,2},{2,0},{4,6},{6,4},{8,10},{10,8},{12,14},{14,12},{16,18},{18,... | collective-permute-start | bytes 786440 | tf_op jit(solution)/shard_map/ppermute | solution.py:106
  13.8 7.1 %collective-permute-start.1 = (bf16[2,128,512]{2,1,0:T(8,128)(2,1)S(1)}, bf16[2,128,512]{2,1,0:T(8,128)(2,1)}, u32[]{:S(2)}, u32[]{:S(2)}) collective-permute-start(bf16[2,128,512]{2,1,0:T(8,128)(2,1)S(1)} %get-tuple-element.35), channel_id=1, source_target_pairs={{0,4},{2,6},{4,0},{6,2},{8,12},{10,14},{12,8},{14,10},{16,20},{18,... | collective-permute-start | bytes 786440 | tf_op jit(solution)/shard_map/ppermute | solution.py:106
  20.9 7.3 %collective-permute-start.2 = (bf16[2,128,512]{2,1,0:T(8,128)(2,1)S(1)}, bf16[2,128,512]{2,1,0:T(8,128)(2,1)S(1)}, u32[]{:S(2)}, u32[]{:S(2)}) collective-permute-start(bf16[2,128,512]{2,1,0:T(8,128)(2,1)S(1)} %get-tuple-element.36), channel_id=1, source_target_pairs={{0,6},{2,4},{4,2},{6,0},{8,14},{10,12},{12,10},{14,8},{16,22},{18,... | collective-permute-start | bytes 786440 | tf_op jit(solution)/shard_map/ppermute | solution.py:106
  22.4 11.8 %collective-permute-start.3 = (bf16[1,1024,128]{2,1,0:T(8,128)(2,1)}, bf16[1,1024,128]{2,1,0:T(8,128)(2,1)S(1)}, u32[]{:S(2)}, u32[]{:S(2)}) collective-permute-start(bf16[1,1024,128]{2,1,0:T(8,128)(2,1)} %bitcast.66), channel_id=1, source_target_pairs={{0,8},{2,10},{4,12},{6,14},{8,0},{10,2},{12,4},{14,6},{16,24},{18,... | collective-permute-start | bytes 786440 | tf_op jit(solution)/shard_map/ppermute | solution.py:106
  36.4 26.5 %collective-permute-start.10 = (bf16[256,2176]{1,0:T(8,128)(2,1)S(1)}, bf16[256,2176]{1,0:T(8,128)(2,1)S(1)}, u32[]{:S(2)}, u32[]{:S(2)}) collective-permute-start(bf16[256,2176]{1,0:T(8,128)(2,1)S(1)} %constant_dynamic-update-slice_fusion.refs_0_.refs_9_), channel_id=1, source_target_pairs={{0,2},{2,0},{4,6},{6,4},{8,10},{10,8},{12,14},{14,12},{16,18},{18,... | collective-permute-start | bytes 3342344 | tf_op jit(solution)/shard_map/ppermute | solution.py:106
  37.9 26.1 %collective-permute-start.11 = (bf16[256,2176]{1,0:T(8,128)(2,1)S(1)}, bf16[256,2176]{1,0:T(8,128)(2,1)S(1)}, u32[]{:S(2)}, u32[]{:S(2)}) collective-permute-start(bf16[256,2176]{1,0:T(8,128)(2,1)S(1)} %constant_dynamic-update-slice_fusion.refs_0_.refs_9_), channel_id=1, source_target_pairs={{0,4},{2,6},{4,0},{6,2},{8,12},{10,14},{12,8},{14,10},{16,20},{18,... | collective-permute-start | bytes 3342344 | tf_op jit(solution)/shard_map/ppermute | solution.py:106
  38.9 26.0 %collective-permute-start.7 = (bf16[512,512]{1,0:T(8,128)(2,1)S(1)}, bf16[512,512]{1,0:T(8,128)(2,1)S(1)}, u32[]{:S(2)}, u32[]{:S(2)}) collective-permute-start(bf16[512,512]{1,0:T(8,128)(2,1)S(1)} %get-tuple-element.39), channel_id=1, source_target_pairs={{0,0},{1,16},{2,2},{3,18},{4,4},{5,20},{6,6},{7,22},{8,8},{9,24},{... | collective-permute-start | bytes 1572872 | tf_op jit(solution)/shard_map/ppermute | solution.py:152
  39.8 25.2 %collective-permute-start.8 = (bf16[512,512]{1,0:T(8,128)(2,1)S(1)}, bf16[512,512]{1,0:T(8,128)(2,1)S(1)}, u32[]{:S(2)}, u32[]{:S(2)}) collective-permute-start(bf16[512,512]{1,0:T(8,128)(2,1)S(1)} %get-tuple-element.40), channel_id=1, source_target_pairs={{0,8},{1,24},{2,10},{3,26},{4,12},{5,28},{6,14},{7,30},{8,0},{9,16... | collective-permute-start | bytes 1572872 | tf_op jit(solution)/shard_map/ppermute | solution.py:152
  62.9 13.7 %collective-permute-start.12 = (bf16[128,2176]{1,0:T(8,128)(2,1)S(1)}, bf16[128,2176]{1,0:T(8,128)(2,1)S(1)}, u32[]{:S(2)}, u32[]{:S(2)}) collective-permute-start(bf16[128,2176]{1,0:T(8,128)(2,1)S(1)} %slice.56), channel_id=1, source_target_pairs={{0,4},{2,6},{4,0},{6,2},{8,12},{10,14},{12,8},{14,10},{16,20},{18,... | collective-permute-start | bytes 1671176 | tf_op jit(solution)/shard_map/ppermute | solution.py:106
  64.0 13.3 %collective-permute-start.13 = (bf16[128,2176]{1,0:T(8,128)(2,1)S(1)}, bf16[128,2176]{1,0:T(8,128)(2,1)S(1)}, u32[]{:S(2)}, u32[]{:S(2)}) collective-permute-start(bf16[128,2176]{1,0:T(8,128)(2,1)S(1)} %slice.57), channel_id=1, source_target_pairs={{0,2},{2,0},{4,6},{6,4},{8,10},{10,8},{12,14},{14,12},{16,18},{18,... | collective-permute-start | bytes 1671176 | tf_op jit(solution)/shard_map/ppermute | solution.py:106
  65.5 27.0 %collective-permute-start.9 = (bf16[2,1024,128]{2,1,0:T(8,128)(2,1)S(1)}, bf16[2,1024,128]{2,1,0:T(8,128)(2,1)S(1)}, u32[]{:S(2)}, u32[]{:S(2)}) collective-permute-start(bf16[2,1024,128]{2,1,0:T(8,128)(2,1)S(1)} %pad_maximum_fusion.2.refs_5_), channel_id=1, source_target_pairs={{0,16},{2,18},{4,20},{6,22},{8,24},{10,26},{12,28},{14,30},{16,0},... | collective-permute-start | bytes 1572872 | tf_op jit(solution)/shard_map/ppermute | solution.py:106
  84.4 8.2 %collective-permute-start.16 = (bf16[2,1024,128]{2,1,0:T(8,128)(2,1)S(1)}, bf16[2,1024,128]{2,1,0:T(8,128)(2,1)S(1)}, u32[]{:S(2)}, u32[]{:S(2)}) collective-permute-start(bf16[2,1024,128]{2,1,0:T(8,128)(2,1)S(1)} %pad_maximum_fusion.2.refs_5_), channel_id=1, source_target_pairs={{0,1},{1,0},{2,3},{3,2},{4,5},{5,4},{6,7},{7,6},{8,9},{9,8},{10,11... | collective-permute-start | bytes 1572872 | tf_op jit(solution)/shard_map/ppermute | solution.py:110
  93.5 6.8 %collective-permute-start.21 = (bf16[4,64,128]{2,1,0:T(8,128)(2,1)S(1)}, bf16[4,64,128]{2,1,0:T(8,128)(2,1)S(1)}, u32[]{:S(2)}, u32[]{:S(2)}) collective-permute-start(bf16[4,64,128]{2,1,0:T(8,128)(2,1)S(1)} %get-tuple-element.76), channel_id=1, source_target_pairs={{0,24},{2,26},{4,28},{6,30},{8,16},{10,18},{12,20},{14,22},{16,8},... | collective-permute-start | bytes 196616 | tf_op jit(solution)/shard_map/ppermute | solution.py:106
  104.1 18.5 %collective-permute-start.33 = (bf16[64,1024]{1,0:T(8,128)(2,1)S(1)}, bf16[64,1024]{1,0:T(8,128)(2,1)S(1)}, u32[]{:S(2)}, u32[]{:S(2)}) collective-permute-start(bf16[64,1024]{1,0:T(8,128)(2,1)S(1)} %get-tuple-element.74), channel_id=1, source_target_pairs={{0,1},{1,0},{2,3},{3,2},{4,5},{5,4},{6,7},{7,6},{8,9},{9,8},{10,11... | collective-permute-start | bytes 393224 | tf_op jit(solution)/shard_map/ppermute | solution.py:110
  104.2 8.9 %collective-permute-start.22 = (bf16[4,4,64,128]{3,2,1,0:T(8,128)(2,1)}, bf16[4,4,64,128]{3,2,1,0:T(8,128)(2,1)S(1)}, u32[]{:S(2)}, u32[]{:S(2)}) collective-permute-start(bf16[4,4,64,128]{3,2,1,0:T(8,128)(2,1)} %pad_maximum_fusion.4.refs_0_), channel_id=1, source_target_pairs={{0,2},{2,0},{4,6},{6,4},{8,10},{10,8},{12,14},{14,12},{16,18},{18,... | collective-permute-start | bytes 786440 | tf_op jit(solution)/shard_map/ppermute | solution.py:106
  104.6 9.1 %collective-permute-start.23 = (bf16[4,4,64,128]{3,2,1,0:T(8,128)(2,1)}, bf16[4,4,64,128]{3,2,1,0:T(8,128)(2,1)S(1)}, u32[]{:S(2)}, u32[]{:S(2)}) collective-permute-start(bf16[4,4,64,128]{3,2,1,0:T(8,128)(2,1)} %pad_maximum_fusion.4.refs_0_), channel_id=1, source_target_pairs={{0,4},{2,6},{4,0},{6,2},{8,12},{10,14},{12,8},{14,10},{16,20},{18,... | collective-permute-start | bytes 786440 | tf_op jit(solution)/shard_map/ppermute | solution.py:106
  105.4 13.4 %collective-permute-start.26 = (bf16[2,1024,128]{2,1,0:T(8,128)(2,1)}, bf16[2,1024,128]{2,1,0:T(8,128)(2,1)S(1)}, u32[]{:S(2)}, u32[]{:S(2)}) collective-permute-start(bf16[2,1024,128]{2,1,0:T(8,128)(2,1)} %copy-done.8), channel_id=1, source_target_pairs={{0,1},{1,0},{2,3},{3,2},{4,5},{5,4},{6,7},{7,6},{8,9},{9,8},{10,11... | collective-permute-start | bytes 1572872 | tf_op jit(solution)/shard_map/ppermute | solution.py:110
  109.8 15.4 %collective-permute-start.32 = (bf16[128,1152]{1,0:T(8,128)(2,1)S(1)}, bf16[128,1152]{1,0:T(8,128)(2,1)S(1)}, u32[]{:S(2)}, u32[]{:S(2)}) collective-permute-start(bf16[128,1152]{1,0:T(8,128)(2,1)S(1)} %pad_maximum_fusion.3), channel_id=1, source_target_pairs={{0,16},{2,18},{4,20},{6,22},{8,24},{10,26},{12,28},{14,30},{16,0},... | collective-permute-start | bytes 884744 | tf_op jit(solution)/shard_map/ppermute | solution.py:106
  125.2 14.1 %collective-permute-start.34 = (bf16[256,1152]{1,0:T(8,128)(2,1)S(1)}, bf16[256,1152]{1,0:T(8,128)(2,1)S(1)}, u32[]{:S(2)}, u32[]{:S(2)}) collective-permute-start(bf16[256,1152]{1,0:T(8,128)(2,1)S(1)} %constant_dynamic-update-slice_fusion.4.refs_5_), channel_id=1, source_target_pairs={{0,1},{1,0},{2,3},{3,2},{4,5},{5,4},{6,7},{7,6},{8,9},{9,8},{10,11... | collective-permute-start | bytes 1769480 | tf_op jit(solution)/shard_map/ppermute | solution.py:110
  125.3 8.7 %collective-permute-start.27 = (bf16[4,64,512]{2,1,0:T(8,128)(2,1)S(1)}, bf16[4,64,512]{2,1,0:T(8,128)(2,1)S(1)}, u32[]{:S(2)}, u32[]{:S(2)}) collective-permute-start(bf16[4,64,512]{2,1,0:T(8,128)(2,1)S(1)} %hidden.1.refs_0_), channel_id=1, source_target_pairs={{0,2},{2,0},{4,6},{6,4},{8,10},{10,8},{12,14},{14,12},{16,18},{18,... | collective-permute-start | bytes 786440 | tf_op jit(solution)/shard_map/ppermute | solution.py:106
  125.6 8.5 %collective-permute-start.28 = (bf16[4,64,512]{2,1,0:T(8,128)(2,1)S(1)}, bf16[4,64,512]{2,1,0:T(8,128)(2,1)S(1)}, u32[]{:S(2)}, u32[]{:S(2)}) collective-permute-start(bf16[4,64,512]{2,1,0:T(8,128)(2,1)S(1)} %hidden.1.refs_0_), channel_id=1, source_target_pairs={{0,4},{2,6},{4,0},{6,2},{8,12},{10,14},{12,8},{14,10},{16,20},{18,... | collective-permute-start | bytes 786440 | tf_op jit(solution)/shard_map/ppermute | solution.py:106
  (34 other events, 245.8 us)

commit v17 on v16

--- a/solution.py
+++ b/solution.py
@@ -6,7 +6,7 @@
 from jax.sharding import PartitionSpec as P
 
 HEAD_DIM = 128
-VMEM_LIMIT = 24 * 1024 * 1024
+VMEM_LIMIT = 14 * 1024 * 1024
 BF16 = jnp.bfloat16
 F32 = jnp.float32
 
@@ -164,42 +164,49 @@
         copy.wait()
 
 
-def mark_kernel(where, tokens, positions, ids, mine):
+def mark_kernel(where, tokens, positions, ids, mine, events, sem):
     u = where[3]
-    rows, model = mine.shape[0], tokens.shape[1]
-    mine[:, :model] = tokens[pl.ds(pl.multiple_of(u * rows, rows), rows), :]
-    line = lax.broadcasted_iota(jnp.int32, (rows, rows), 0)
-    across = lax.broadcasted_iota(jnp.int32, (rows, rows), 1)
+    rows, model = events.shape
+    own = tokens.at[pl.ds(pl.multiple_of(u * rows, rows), rows), :]
+    copy = pltpu.make_async_copy(own, events, sem)
+    copy.start()
     lane = lax.broadcasted_iota(jnp.int32, (rows, W), 1)
     marks = jnp.zeros((rows, W), F32)
-    values = (positions[pl.ds(u, 1)], positions[pl.ds(1 - u, 1)], ids[...])
-    for i, (value, bits) in enumerate(zip(values, (7, 7, 8))):
-        column = jnp.sum(jnp.where(line == across, value, 0), axis=1, keepdims=True)
+    values = ((positions, u * rows, 7), (positions, (1 - u) * rows, 7), (ids, 0, 8))
+    for i, (ref, first, bits) in enumerate(values):
+        line = lax.broadcasted_iota(jnp.int32, (rows, ref.shape[1]), 0)
+        across = lax.broadcasted_iota(jnp.int32, (rows, ref.shape[1]), 1)
+        picked = jnp.where(across == line + first, ref[...], 0)
+        column = jnp.sum(picked, axis=1, keepdims=True)
         high = lax.shift_right_logical(column, bits)
         marks = jnp.where(lane == 2 * i, high.astype(F32), marks)
         marks = jnp.where(lane == 2 * i + 1, (column - high * 2**bits).astype(F32), marks)
     mine[:, model:] = marks.astype(BF16)
+    copy.wait()
+    mine[:, :model] = events[...]
 
 
 def proj_kernel(where, *refs):
-    count = len(refs) - 12
+    count = len(refs) - 11
     tok, w_own, w_other = refs[:count], refs[count : count + 2], refs[count + 2 : count + 4]
-    gate_query, value, key, marks, x_all, w_all, tok_sem, w_sem = refs[count + 4 :]
+    gate_query, value, key, marks, x_all, w_all, tok_sem = refs[count + 4 :]
     z, y, x, u = (where[i] for i in range(4))
     copies, base = [], 0
-    for side, (at, srcs) in enumerate(((u, w_own), (1 - u, w_other))):
+    for i, ref in enumerate(tok):
+        rows = pl.ds(base, ref.shape[0])
+        copies.append(pltpu.make_async_copy(ref, x_all.at[rows, :], tok_sem.at[i]))
+        base += ref.shape[0]
+    for copy in copies:
+        copy.start()
+    for at, srcs in ((u, w_own), (1 - u, w_other)):
         for e, src in enumerate(srcs):
             size = src.shape[0] // len(PLANE)
             for j, (by, bx) in enumerate(PLANE):
                 start = chip_at(2 * at + (e ^ (z & 1)), y ^ by, x ^ bx) * size
-                to = w_all.at[pl.ds(pl.multiple_of(start, size), size), :]
-                sem = w_sem.at[(2 * side + e) * len(PLANE) + j]
-                copies.append(pltpu.make_async_copy(src.at[pl.ds(j * size, size), :], to, sem))
-    for i, ref in enumerate(tok):
-        rows = pl.ds(base, ref.shape[0])
-        copies.append(pltpu.make_async_copy(ref, x_all.at[rows, :], tok_sem.at[i]))
-        base += ref.shape[0]
-    run_copies(copies)
+                part = src[j * size : (j + 1) * size, :]
+                w_all[pl.ds(pl.multiple_of(start, size), size), :] = part
+    for copy in copies:
+        copy.wait()
     model = w_all.shape[0]
     total = jnp.dot(x_all[:, :model], w_all[...], preferred_element_type=F32)
     proj = silu(total).astype(BF16)
@@ -407,9 +414,9 @@
         mark_kernel,
         "mark",
         [((rows, model + W), BF16)],
-        [],
-        [where, tokens, positions.reshape(2, rows), target_ids.reshape(1, rows)],
-        "svvv",
+        [pltpu.VMEM((rows, model), BF16), pltpu.SemaphoreType.DMA],
+        [where, tokens, positions.reshape(1, 2 * rows), target_ids.reshape(1, rows)],
+        "shvv",
         0,
     )
     line = [mine] + [hop(mine, flip(0, 0, s)) for s in range(1, NZ)]
@@ -426,16 +433,17 @@
     neg = with_marks(neg_emb, float_parts(norms) + whole_parts(own_ids, 256))
 
     out_pair = pair_up(after(w_out[None], w_rows[1:3]))
-    w_pieces, neg, out_pair, line = lax.optimization_barrier((w_pieces, neg, out_pair, line))
+    t_rows = target_emb.reshape(2, rows, -1)
+    t_keep, t_mine = pick_row(t_rows, u), pick_row(t_rows, 1 - u)
+    early = (w_pieces, neg, out_pair, t_keep, t_mine, line)
+    w_pieces, neg, out_pair, t_keep, t_mine, line = lax.optimization_barrier(early)
     near = jnp.concatenate(line)
     near_x, near_y = hop(near, to_x), hop(near, to_y)
     tok = [near, near_x, near_y, *across(near_x, near_y)]
     w_mine = heads_along_z(w_pieces)
     w_theirs = [swap_cores(w) for w in w_mine]
     out_own = [out_pair, hop(after(out_pair, w_mine), flip(0, 0, 2))]
-    t_rows = after(target_emb.reshape(2, rows, -1), w_theirs)
-    t_keep = pick_row(t_rows, u)
-    t_send = swap_cores(pick_row(t_rows, 1 - u))
+    t_send = swap_cores(after(t_mine, w_theirs))
 
     def project(pieces):
         count = sum(p.shape[0] for p in pieces)
@@ -447,10 +455,9 @@
                 pltpu.VMEM((count, model + W), BF16),
                 pltpu.VMEM((model, 4 * W), BF16),
                 pltpu.SemaphoreType.DMA((len(pieces),)),
-                pltpu.SemaphoreType.DMA((16,)),
             ],
             [where, *pieces, *w_mine, *w_theirs],
-            "s" + (len(pieces) + 4) * "h",
+            "s" + len(pieces) * "h" + 4 * "v",
             0,
         )
 
@@ -490,9 +497,9 @@
         "s" + 13 * "h",
         2 * plane * rows * model * NZ * W,
     )
-    neg_own = jnp.concatenate([neg_pair, after(neg_far, hidden, t_send)])
+    pieces = [hidden, hop(hidden, to_x), hop(hidden, to_y)]
+    neg_own = jnp.concatenate([neg_pair, after(neg_far, pieces, t_send)])
     neg_other = swap_cores(neg_own)
-    pieces = [hidden, hop(hidden, to_x), hop(hidden, to_y)]
     pieces += across(pieces[1], pieces[2])
     h_keep, h_send, positive, mass = call(
         mass_kernel,

time: 149 us -> 142 us (0.953)
  starting transfers between devices: 35.1 us -> 40.4 us
  local copies, waits for them, and re-layouts: 12.3 us -> 8.21 us
  waiting for transfers between devices: 80.2 us -> 76.3 us
  Pallas kernels: 16.6 us -> 13.5 us
  other arithmetic: 3.56 us -> 1.95 us
    ppermute x28, starting transfers between devices: 32.2 us -> 37.9 us  [hop(): return lax.ppermute(value, 'ctx', perm)]
    unnamed x43 -> x15, local copies, waits for them, and re-layouts: 6.65 us -> 2.47 us
    ppermute x28, waiting for transfers between devices: 78.1 us -> 74.2 us  [hop(): return lax.ppermute(value, 'ctx', perm)]
    pallas_call x6, Pallas kernels: 16.6 us -> 13.5 us  [call(): pl.pallas_call(kernel, out_shape=[jax.ShapeDtypeStruct(shape, dtype) for...]
  transfers between devices with their start and end apart: 39 -> 39, of which waited for: 24 -> 21; matrix products, arithmetic and copies ran while one was open for 6% -> 5% of each run, Pallas kernels for 9% -> 7%
where the time goes in v17:
time: 142 us; the launch traced here: 141 us
  waiting for transfers between devices  76.3 us (54%)
  starting transfers between devices  40.4 us (28%)
  Pallas kernels  13.5 us (10%)
  local copies, waits for them, and re-layouts  8.21 us (6%)
  other arithmetic  1.95 us (1%)
    ppermute x28, waiting for transfers between devices, hop(): return lax.ppermute(value, 'ctx', perm)  74.2 us
    ppermute x28, starting transfers between devices, hop(): return lax.ppermute(value, 'ctx', perm)  37.9 us
    pallas_call x6, Pallas kernels, call(): pl.pallas_call(kernel, out_shape=[jax.ShapeDtypeStruct(shape, dtype) for...  13.5 us
    squeeze x6, local copies, waits for them, and re-layouts, pick_row(): return lax.dynamic_index_in_dim(value, at, 0, keepdims=False)  3.08 us
  transfers between devices with their start and end apart: 39, of which 21 were waited for; matrix products, arithmetic and copies ran while one was open for 5% of the time, Pallas kernels for 7%

profile of v17, /device:TPU:0, one launch (start us, length us, event | category | flops | bytes accessed | tf_op | source)
XLA Modules:
  0.0 141.4 jit_solution(11038939591978948739)
XLA Ops:
  3.8 3.1 %collective-permute-start.4 = (bf16[64,2176]{1,0:T(8,128)(2,1)S(1)}, bf16[64,2176]{1,0:T(8,128)(2,1)S(1)}, u32[]{:S(2)}, u32[]{:S(2)}) collective-permute-start(bf16[64,2176]{1,0:T(8,128)(2,1)S(1)} %mark.1), channel_id=1, source_target_pairs={{0,8},{2,10},{4,12},{6,14},{8,0},{10,2},{12,4},{14,6},{16,24},{18,... | collective-permute-start | bytes 835592 | tf_op jit(solution)/shard_map/ppermute | solution.py:106
  6.9 2.6 %collective-permute-start.5 = (bf16[64,2176]{1,0:T(8,128)(2,1)S(1)}, bf16[64,2176]{1,0:T(8,128)(2,1)S(1)}, u32[]{:S(2)}, u32[]{:S(2)}) collective-permute-start(bf16[64,2176]{1,0:T(8,128)(2,1)S(1)} %mark.1), channel_id=1, source_target_pairs={{0,16},{2,18},{4,20},{6,22},{8,24},{10,26},{12,28},{14,30},{16,0},... | collective-permute-start | bytes 835592 | tf_op jit(solution)/shard_map/ppermute | solution.py:106
  12.0 1.8 %collective-permute-start.1 = (bf16[2,128,512]{2,1,0:T(8,128)(2,1)S(1)}, bf16[2,128,512]{2,1,0:T(8,128)(2,1)}, u32[]{:S(2)}, u32[]{:S(2)}) collective-permute-start(bf16[2,128,512]{2,1,0:T(8,128)(2,1)S(1)} %get-tuple-element.37), channel_id=1, source_target_pairs={{0,4},{2,6},{4,0},{6,2},{8,12},{10,14},{12,8},{14,10},{16,20},{18,... | collective-permute-start | bytes 786440 | tf_op jit(solution)/shard_map/ppermute | solution.py:106
  17.2 2.5 %collective-permute-done.1 = bf16[2,128,512]{2,1,0:T(8,128)(2,1)} collective-permute-done((bf16[2,128,512]{2,1,0:T(8,128)(2,1)S(1)}, bf16[2,128,512]{2,1,0:T(8,128)(2,1)}, u32[]{:S(2)}, u32[]{:S(2)}) %collective-permute-start.1) | collective-permute-done | bytes 262176 | tf_op jit(solution)/shard_map/ppermute | solution.py:106
  26.0 2.2 %collective-permute-done.2 = bf16[2,128,512]{2,1,0:T(8,128)(2,1)S(1)} collective-permute-done((bf16[2,128,512]{2,1,0:T(8,128)(2,1)S(1)}, bf16[2,128,512]{2,1,0:T(8,128)(2,1)S(1)}, u32[]{:S(2)}, u32[]{:S(2)}) %collective-permute-start.2) | collective-permute-done | bytes 262176 | tf_op jit(solution)/shard_map/ppermute | solution.py:106
  28.2 6.0 %collective-permute-done.3 = bf16[1,1024,128]{2,1,0:T(8,128)(2,1)S(1)} collective-permute-done((bf16[1,1024,128]{2,1,0:T(8,128)(2,1)}, bf16[1,1024,128]{2,1,0:T(8,128)(2,1)S(1)}, u32[]{:S(2)}, u32[]{:S(2)}) %collective-permute-start.3) | collective-permute-done | bytes 262176 | tf_op jit(solution)/shard_map/ppermute | solution.py:106
  38.6 22.4 %collective-permute-done.10.refs_1_.refs_10_ = bf16[256,2176]{1,0:T(8,128)(2,1)S(1)} collective-permute-done((bf16[256,2176]{1,0:T(8,128)(2,1)S(1)}, bf16[256,2176]{1,0:T(8,128)(2,1)S(1)}, u32[]{:S(2)}, u32[]{:S(2)}) %collective-permute-start.10) | collective-permute-done | bytes 1114144 | tf_op jit(solution)/shard_map/ppermute | solution.py:106
  64.6 2.3 %collective-permute-start.9 = (bf16[2,1024,128]{2,1,0:T(8,128)(2,1)S(1)}, bf16[2,1024,128]{2,1,0:T(8,128)(2,1)S(1)}, u32[]{:S(2)}, u32[]{:S(2)}) collective-permute-start(bf16[2,1024,128]{2,1,0:T(8,128)(2,1)S(1)} %pad_maximum_fusion.2.refs_5_), channel_id=1, source_target_pairs={{0,16},{2,18},{4,20},{6,22},{8,24},{10,26},{12,28},{14,30},{16,0},... | collective-permute-start | bytes 1572872 | tf_op jit(solution)/shard_map/ppermute | solution.py:106
  66.8 8.0 %collective-permute-done.12.refs_3_.refs_12_ = bf16[128,2176]{1,0:T(8,128)(2,1)S(1)} collective-permute-done((bf16[128,2176]{1,0:T(8,128)(2,1)S(1)}, bf16[128,2176]{1,0:T(8,128)(2,1)S(1)}, u32[]{:S(2)}, u32[]{:S(2)}) %collective-permute-start.12) | collective-permute-done | bytes 557088 | tf_op jit(solution)/shard_map/ppermute | solution.py:106
  76.2 3.8 %project.1 = (bf16[1024,256]{1,0:T(8,128)(2,1)S(1)}, bf16[1024,128]{1,0:T(8,128)(2,1)S(1)}, bf16[1024,128]{1,0:T(8,128)(2,1)S(1)}, bf16[1024,128]{1,0:T(8,128)(2,1)S(1)}) custom-call(s32[4]{0:T(128)S(1)} %pad_add_fusion.where, bf16[256,2176]{1,0:T(8,128)(2,1)S(1)} %constant_dynamic-update-slice_fusion.refs_0_.refs_9_, ...), custom_call_target="tpu_custom_call" | custom-call | bytes 6553616 | tf_op jit(solution)/shard_map/project/pallas_call | solution.py:370
  80.6 1.7 %collective-permute-done.17.refs_3_ = bf16[1024,128]{1,0:T(8,128)(2,1)S(1)} collective-permute-done((bf16[1024,128]{1,0:T(8,128)(2,1)S(1)}, bf16[1024,128]{1,0:T(8,128)(2,1)S(1)}, u32[]{:S(2)}, u32[]{:S(2)}) %collective-permute-start.17) | collective-permute-done | bytes 262176 | tf_op jit(solution)/shard_map/ppermute | solution.py:110
  82.7 3.4 %attend.1 = bf16[4,4,64,128]{3,2,1,0:T(8,128)(2,1)S(1)} custom-call(bf16[1024,256]{1,0:T(8,128)(2,1)S(1)} %get-tuple-element.50.refs_0_, bf16[1024,128]{1,0:T(8,128)(2,1)S(1)} %get-tuple-element.51.refs_1_, bf16[1024,128]{1,0:T(8,128)(2,1)S(1)} %get-tuple-element.48.refs_2_, bf16[1024,128]{1,0:T(8,128)(2,1)S(1)} %collective-permute-done.17.refs_3_, ...), custom_call_target="tpu_custom_call" | custom-call | bytes 1835008 | tf_op jit(solution)/shard_map/attend/pallas_call | solution.py:370
  86.1 4.5 %collective-permute-done.9.refs_6_ = bf16[2,1024,128]{2,1,0:T(8,128)(2,1)S(1)} collective-permute-done((bf16[2,1024,128]{2,1,0:T(8,128)(2,1)S(1)}, bf16[2,1024,128]{2,1,0:T(8,128)(2,1)S(1)}, u32[]{:S(2)}, u32[]{:S(2)}) %collective-permute-start.9) | collective-permute-done | bytes 524320 | tf_op jit(solution)/shard_map/ppermute | solution.py:106
  90.8 2.2 %collective-permute-start.20 = (bf16[4,64,128]{2,1,0:T(8,128)(2,1)S(1)}, bf16[4,64,128]{2,1,0:T(8,128)(2,1)S(1)}, u32[]{:S(2)}, u32[]{:S(2)}) collective-permute-start(bf16[4,64,128]{2,1,0:T(8,128)(2,1)S(1)} %get-tuple-element.79), channel_id=1, source_target_pairs={{0,16},{2,18},{4,20},{6,22},{8,24},{10,26},{12,28},{14,30},{16,0},... | collective-permute-start | bytes 196616 | tf_op jit(solution)/shard_map/ppermute | solution.py:106
  93.0 2.1 %collective-permute-start.21 = (bf16[4,64,128]{2,1,0:T(8,128)(2,1)S(1)}, bf16[4,64,128]{2,1,0:T(8,128)(2,1)S(1)}, u32[]{:S(2)}, u32[]{:S(2)}) collective-permute-start(bf16[4,64,128]{2,1,0:T(8,128)(2,1)S(1)} %get-tuple-element.78), channel_id=1, source_target_pairs={{0,24},{2,26},{4,28},{6,30},{8,16},{10,18},{12,20},{14,22},{16,8},... | collective-permute-start | bytes 196616 | tf_op jit(solution)/shard_map/ppermute | solution.py:106
  95.2 2.8 %collective-permute-done.20 = bf16[4,64,128]{2,1,0:T(8,128)(2,1)S(1)} collective-permute-done((bf16[4,64,128]{2,1,0:T(8,128)(2,1)S(1)}, bf16[4,64,128]{2,1,0:T(8,128)(2,1)S(1)}, u32[]{:S(2)}, u32[]{:S(2)}) %collective-permute-start.20) | collective-permute-done | bytes 65568 | tf_op jit(solution)/shard_map/ppermute | solution.py:106
  102.3 5.7 %collective-permute-done.22.refs_1_ = bf16[4,4,64,128]{3,2,1,0:T(8,128)(2,1)S(1)} collective-permute-done((bf16[4,4,64,128]{3,2,1,0:T(8,128)(2,1)S(1)}, bf16[4,4,64,128]{3,2,1,0:T(8,128)(2,1)S(1)}, u32[]{:S(2)}, u32[]{:S(2)}) %collective-permute-start.22) | collective-permute-done | bytes 262176 | tf_op jit(solution)/shard_map/ppermute | solution.py:106
  111.5 1.7 %collective-permute-done.24.refs_3_ = bf16[2,4,64,128]{3,2,1,0:T(8,128)(2,1)S(1)} collective-permute-done((bf16[2,4,64,128]{3,2,1,0:T(8,128)(2,1)S(1)}, bf16[2,4,64,128]{3,2,1,0:T(8,128)(2,1)S(1)}, u32[]{:S(2)}, u32[]{:S(2)}) %collective-permute-start.24) | collective-permute-done | bytes 131104 | tf_op jit(solution)/shard_map/ppermute | solution.py:106
  113.7 2.7 %hidden.1.refs_0_ = bf16[4,64,512]{2,1,0:T(8,128)(2,1)S(1)} custom-call(s32[4]{0:T(128)S(1)} %pad_add_fusion.where, bf16[4,4,64,128]{3,2,1,0:T(8,128)(2,1)S(1)} %pad_maximum_fusion.4.refs_0_, bf16[4,4,64,128]{3,2,1,0:T(8,128)(2,1)S(1)} %collective-permute-done.22.refs_1_, bf16[4,4,64,128]{3,2,1,0:T(8,128)(2,1)S(1)} %collective-permute-done.23.refs_2_, ...), custom_call_target="tpu_custom_call" | custom-call | flops 536870912 | bytes 7045136 | tf_op jit(solution)/shard_map/hidden/pallas_call | solution.py:370
  118.4 7.0 %collective-permute-done.32 = bf16[128,1152]{1,0:T(8,128)(2,1)S(1)} collective-permute-done((bf16[128,1152]{1,0:T(8,128)(2,1)S(1)}, bf16[128,1152]{1,0:T(8,128)(2,1)S(1)}, u32[]{:S(2)}, u32[]{:S(2)}) %collective-permute-start.32) | collective-permute-done | bytes 294944 | tf_op jit(solution)/shard_map/ppermute | solution.py:106
  126.1 1.7 %collective-permute-start.30 = (bf16[2,64,512]{2,1,0:T(8,128)(2,1)S(1)}, bf16[2,64,512]{2,1,0:T(8,128)(2,1)S(1)}, u32[]{:S(2)}, u32[]{:S(2)}) collective-permute-start(bf16[2,64,512]{2,1,0:T(8,128)(2,1)S(1)} %slice.61), channel_id=1, source_target_pairs={{0,2},{2,0},{4,6},{6,4},{8,10},{10,8},{12,14},{14,12},{16,18},{18,... | collective-permute-start | bytes 393224 | tf_op jit(solution)/shard_map/ppermute | solution.py:106
  127.8 3.6 %collective-permute-done.29.refs_3_ = bf16[2,64,512]{2,1,0:T(8,128)(2,1)S(1)} collective-permute-done((bf16[2,64,512]{2,1,0:T(8,128)(2,1)S(1)}, bf16[2,64,512]{2,1,0:T(8,128)(2,1)S(1)}, u32[]{:S(2)}, u32[]{:S(2)}) %collective-permute-start.29) | collective-permute-done | bytes 131104 | tf_op jit(solution)/shard_map/ppermute | solution.py:106
  133.5 1.7 %collective-permute-start.36 = (f32[1,64]{1,0:T(1,128)S(1)}, f32[1,64]{1,0:T(1,128)S(1)}, u32[]{:S(2)}, u32[]{:S(2)}) collective-permute-start(f32[1,64]{1,0:T(1,128)S(1)} %get-tuple-element.91), channel_id=1, source_target_pairs={{0,2},{2,0},{4,6},{6,4},{8,10},{10,8},{12,14},{14,12},{16,18},{18,... | collective-permute-start | bytes 776 | tf_op jit(solution)/shard_map/ppermute | solution.py:106
  137.1 1.7 %collective-permute-done.37.refs_2_ = f32[1,64]{1,0:T(1,128)S(1)} collective-permute-done((f32[1,64]{1,0:T(1,128)S(1)}, f32[1,64]{1,0:T(1,128)S(1)}, u32[]{:S(2)}, u32[]{:S(2)}) %collective-permute-start.37) | collective-permute-done | bytes 288 | tf_op jit(solution)/shard_map/ppermute | solution.py:106
  (106 shorter events, 43.2 us)
Async XLA Ops:
  3.8 30.5 %collective-permute-start.4 = (bf16[64,2176]{1,0:T(8,128)(2,1)S(1)}, bf16[64,2176]{1,0:T(8,128)(2,1)S(1)}, u32[]{:S(2)}, u32[]{:S(2)}) collective-permute-start(bf16[64,2176]{1,0:T(8,128)(2,1)S(1)} %mark.1), channel_id=1, source_target_pairs={{0,8},{2,10},{4,12},{6,14},{8,0},{10,2},{12,4},{14,6},{16,24},{18,... | collective-permute-start | bytes 835592 | tf_op jit(solution)/shard_map/ppermute | solution.py:106
  6.9 27.4 %collective-permute-start.5 = (bf16[64,2176]{1,0:T(8,128)(2,1)S(1)}, bf16[64,2176]{1,0:T(8,128)(2,1)S(1)}, u32[]{:S(2)}, u32[]{:S(2)}) collective-permute-start(bf16[64,2176]{1,0:T(8,128)(2,1)S(1)} %mark.1), channel_id=1, source_target_pairs={{0,16},{2,18},{4,20},{6,22},{8,24},{10,26},{12,28},{14,30},{16,0},... | collective-permute-start | bytes 835592 | tf_op jit(solution)/shard_map/ppermute | solution.py:106
  9.5 24.8 %collective-permute-start.6 = (bf16[64,2176]{1,0:T(8,128)(2,1)S(1)}, bf16[64,2176]{1,0:T(8,128)(2,1)S(1)}, u32[]{:S(2)}, u32[]{:S(2)}) collective-permute-start(bf16[64,2176]{1,0:T(8,128)(2,1)S(1)} %mark.1), channel_id=1, source_target_pairs={{0,24},{2,26},{4,28},{6,30},{8,16},{10,18},{12,20},{14,22},{16,8},... | collective-permute-start | bytes 835592 | tf_op jit(solution)/shard_map/ppermute | solution.py:106
  12.0 7.7 %collective-permute-start.1 = (bf16[2,128,512]{2,1,0:T(8,128)(2,1)S(1)}, bf16[2,128,512]{2,1,0:T(8,128)(2,1)}, u32[]{:S(2)}, u32[]{:S(2)}) collective-permute-start(bf16[2,128,512]{2,1,0:T(8,128)(2,1)S(1)} %get-tuple-element.37), channel_id=1, source_target_pairs={{0,4},{2,6},{4,0},{6,2},{8,12},{10,14},{12,8},{14,10},{16,20},{18,... | collective-permute-start | bytes 786440 | tf_op jit(solution)/shard_map/ppermute | solution.py:106
  13.8 7.1 %collective-permute-start = (bf16[2,128,512]{2,1,0:T(8,128)(2,1)S(1)}, bf16[2,128,512]{2,1,0:T(8,128)(2,1)}, u32[]{:S(2)}, u32[]{:S(2)}) collective-permute-start(bf16[2,128,512]{2,1,0:T(8,128)(2,1)S(1)} %get-tuple-element.36), channel_id=1, source_target_pairs={{0,2},{2,0},{4,6},{6,4},{8,10},{10,8},{12,14},{14,12},{16,18},{18,... | collective-permute-start | bytes 786440 | tf_op jit(solution)/shard_map/ppermute | solution.py:106
  20.9 7.3 %collective-permute-start.2 = (bf16[2,128,512]{2,1,0:T(8,128)(2,1)S(1)}, bf16[2,128,512]{2,1,0:T(8,128)(2,1)S(1)}, u32[]{:S(2)}, u32[]{:S(2)}) collective-permute-start(bf16[2,128,512]{2,1,0:T(8,128)(2,1)S(1)} %get-tuple-element.38), channel_id=1, source_target_pairs={{0,6},{2,4},{4,2},{6,0},{8,14},{10,12},{12,10},{14,8},{16,22},{18,... | collective-permute-start | bytes 786440 | tf_op jit(solution)/shard_map/ppermute | solution.py:106
  23.3 10.9 %collective-permute-start.3 = (bf16[1,1024,128]{2,1,0:T(8,128)(2,1)}, bf16[1,1024,128]{2,1,0:T(8,128)(2,1)S(1)}, u32[]{:S(2)}, u32[]{:S(2)}) collective-permute-start(bf16[1,1024,128]{2,1,0:T(8,128)(2,1)} %bitcast.68), channel_id=1, source_target_pairs={{0,8},{2,10},{4,12},{6,14},{8,0},{10,2},{12,4},{14,6},{16,24},{18,... | collective-permute-start | bytes 786440 | tf_op jit(solution)/shard_map/ppermute | solution.py:106
  34.5 26.5 %collective-permute-start.10 = (bf16[256,2176]{1,0:T(8,128)(2,1)S(1)}, bf16[256,2176]{1,0:T(8,128)(2,1)S(1)}, u32[]{:S(2)}, u32[]{:S(2)}) collective-permute-start(bf16[256,2176]{1,0:T(8,128)(2,1)S(1)} %constant_dynamic-update-slice_fusion.refs_0_.refs_9_), channel_id=1, source_target_pairs={{0,2},{2,0},{4,6},{6,4},{8,10},{10,8},{12,14},{14,12},{16,18},{18,... | collective-permute-start | bytes 3342344 | tf_op jit(solution)/shard_map/ppermute | solution.py:106
  36.1 26.6 %collective-permute-start.11 = (bf16[256,2176]{1,0:T(8,128)(2,1)S(1)}, bf16[256,2176]{1,0:T(8,128)(2,1)S(1)}, u32[]{:S(2)}, u32[]{:S(2)}) collective-permute-start(bf16[256,2176]{1,0:T(8,128)(2,1)S(1)} %constant_dynamic-update-slice_fusion.refs_0_.refs_9_), channel_id=1, source_target_pairs={{0,4},{2,6},{4,0},{6,2},{8,12},{10,14},{12,8},{14,10},{16,20},{18,... | collective-permute-start | bytes 3342344 | tf_op jit(solution)/shard_map/ppermute | solution.py:106
  37.5 26.6 %collective-permute-start.7 = (bf16[512,512]{1,0:T(8,128)(2,1)S(1)}, bf16[512,512]{1,0:T(8,128)(2,1)S(1)}, u32[]{:S(2)}, u32[]{:S(2)}) collective-permute-start(bf16[512,512]{1,0:T(8,128)(2,1)S(1)} %get-tuple-element.41), channel_id=1, source_target_pairs={{0,0},{1,16},{2,2},{3,18},{4,4},{5,20},{6,6},{7,22},{8,8},{9,24},{... | collective-permute-start | bytes 1572872 | tf_op jit(solution)/shard_map/ppermute | solution.py:152
  38.3 25.7 %collective-permute-start.8 = (bf16[512,512]{1,0:T(8,128)(2,1)S(1)}, bf16[512,512]{1,0:T(8,128)(2,1)S(1)}, u32[]{:S(2)}, u32[]{:S(2)}) collective-permute-start(bf16[512,512]{1,0:T(8,128)(2,1)S(1)} %get-tuple-element.42), channel_id=1, source_target_pairs={{0,8},{1,24},{2,10},{3,26},{4,12},{5,28},{6,14},{7,30},{8,0},{9,16... | collective-permute-start | bytes 1572872 | tf_op jit(solution)/shard_map/ppermute | solution.py:152
  61.1 13.7 %collective-permute-start.12 = (bf16[128,2176]{1,0:T(8,128)(2,1)S(1)}, bf16[128,2176]{1,0:T(8,128)(2,1)S(1)}, u32[]{:S(2)}, u32[]{:S(2)}) collective-permute-start(bf16[128,2176]{1,0:T(8,128)(2,1)S(1)} %slice.56), channel_id=1, source_target_pairs={{0,4},{2,6},{4,0},{6,2},{8,12},{10,14},{12,8},{14,10},{16,20},{18,... | collective-permute-start | bytes 1671176 | tf_op jit(solution)/shard_map/ppermute | solution.py:106
  62.7 13.4 %collective-permute-start.13 = (bf16[128,2176]{1,0:T(8,128)(2,1)S(1)}, bf16[128,2176]{1,0:T(8,128)(2,1)S(1)}, u32[]{:S(2)}, u32[]{:S(2)}) collective-permute-start(bf16[128,2176]{1,0:T(8,128)(2,1)S(1)} %slice.57), channel_id=1, source_target_pairs={{0,2},{2,0},{4,6},{6,4},{8,10},{10,8},{12,14},{14,12},{16,18},{18,... | collective-permute-start | bytes 1671176 | tf_op jit(solution)/shard_map/ppermute | solution.py:106
  64.6 26.1 %collective-permute-start.9 = (bf16[2,1024,128]{2,1,0:T(8,128)(2,1)S(1)}, bf16[2,1024,128]{2,1,0:T(8,128)(2,1)S(1)}, u32[]{:S(2)}, u32[]{:S(2)}) collective-permute-start(bf16[2,1024,128]{2,1,0:T(8,128)(2,1)S(1)} %pad_maximum_fusion.2.refs_5_), channel_id=1, source_target_pairs={{0,16},{2,18},{4,20},{6,22},{8,24},{10,26},{12,28},{14,30},{16,0},... | collective-permute-start | bytes 1572872 | tf_op jit(solution)/shard_map/ppermute | solution.py:106
  80.0 10.7 %collective-permute-start.16 = (bf16[2,1024,128]{2,1,0:T(8,128)(2,1)S(1)}, bf16[2,1024,128]{2,1,0:T(8,128)(2,1)S(1)}, u32[]{:S(2)}, u32[]{:S(2)}) collective-permute-start(bf16[2,1024,128]{2,1,0:T(8,128)(2,1)S(1)} %pad_maximum_fusion.2.refs_5_), channel_id=1, source_target_pairs={{0,1},{1,0},{2,3},{3,2},{4,5},{5,4},{6,7},{7,6},{8,9},{9,8},{10,11... | collective-permute-start | bytes 1572872 | tf_op jit(solution)/shard_map/ppermute | solution.py:110
  90.8 7.2 %collective-permute-start.20 = (bf16[4,64,128]{2,1,0:T(8,128)(2,1)S(1)}, bf16[4,64,128]{2,1,0:T(8,128)(2,1)S(1)}, u32[]{:S(2)}, u32[]{:S(2)}) collective-permute-start(bf16[4,64,128]{2,1,0:T(8,128)(2,1)S(1)} %get-tuple-element.79), channel_id=1, source_target_pairs={{0,16},{2,18},{4,20},{6,22},{8,24},{10,26},{12,28},{14,30},{16,0},... | collective-permute-start | bytes 196616 | tf_op jit(solution)/shard_map/ppermute | solution.py:106
  99.2 14.4 %collective-permute-start.26 = (bf16[2,1024,128]{2,1,0:T(8,128)(2,1)S(1)}, bf16[2,1024,128]{2,1,0:T(8,128)(2,1)S(1)}, u32[]{:S(2)}, u32[]{:S(2)}) collective-permute-start(bf16[2,1024,128]{2,1,0:T(8,128)(2,1)S(1)} %collective-permute-done.9.refs_6_), channel_id=1, source_target_pairs={{0,1},{1,0},{2,3},{3,2},{4,5},{5,4},{6,7},{7,6},{8,9},{9,8},{10,11... | collective-permute-start | bytes 1572872 | tf_op jit(solution)/shard_map/ppermute | solution.py:110
  99.3 8.7 %collective-permute-start.22 = (bf16[4,4,64,128]{3,2,1,0:T(8,128)(2,1)S(1)}, bf16[4,4,64,128]{3,2,1,0:T(8,128)(2,1)S(1)}, u32[]{:S(2)}, u32[]{:S(2)}) collective-permute-start(bf16[4,4,64,128]{3,2,1,0:T(8,128)(2,1)S(1)} %pad_maximum_fusion.4.refs_0_), channel_id=1, source_target_pairs={{0,2},{2,0},{4,6},{6,4},{8,10},{10,8},{12,14},{14,12},{16,18},{18,... | collective-permute-start | bytes 786440 | tf_op jit(solution)/shard_map/ppermute | solution.py:106
  99.7 8.9 %collective-permute-start.23 = (bf16[4,4,64,128]{3,2,1,0:T(8,128)(2,1)S(1)}, bf16[4,4,64,128]{3,2,1,0:T(8,128)(2,1)S(1)}, u32[]{:S(2)}, u32[]{:S(2)}) collective-permute-start(bf16[4,4,64,128]{3,2,1,0:T(8,128)(2,1)S(1)} %pad_maximum_fusion.4.refs_0_), channel_id=1, source_target_pairs={{0,4},{2,6},{4,0},{6,2},{8,12},{10,14},{12,8},{14,10},{16,20},{18,... | collective-permute-start | bytes 786440 | tf_op jit(solution)/shard_map/ppermute | solution.py:106
  101.2 8.8 %collective-permute-start.31 = (bf16[64,1152]{1,0:T(8,128)(2,1)S(1)}, bf16[64,1152]{1,0:T(8,128)(2,1)S(1)}, u32[]{:S(2)}, u32[]{:S(2)}) collective-permute-start(bf16[64,1152]{1,0:T(8,128)(2,1)S(1)} %fusion.1), channel_id=1, source_target_pairs={{0,8},{2,10},{4,12},{6,14},{8,0},{10,2},{12,4},{14,6},{16,24},{18,... | collective-permute-start | bytes 442376 | tf_op jit(solution)/shard_map/ppermute | solution.py:106
  102.3 16.1 %collective-permute-start.33 = (bf16[64,1024]{1,0:T(8,128)(2,1)S(1)}, bf16[64,1024]{1,0:T(8,128)(2,1)S(1)}, u32[]{:S(2)}, u32[]{:S(2)}) collective-permute-start(bf16[64,1024]{1,0:T(8,128)(2,1)S(1)} %get-tuple-element.61), channel_id=1, source_target_pairs={{0,1},{1,0},{2,3},{3,2},{4,5},{5,4},{6,7},{7,6},{8,9},{9,8},{10,11... | collective-permute-start | bytes 393224 | tf_op jit(solution)/shard_map/ppermute | solution.py:110
  110.1 15.3 %collective-permute-start.32 = (bf16[128,1152]{1,0:T(8,128)(2,1)S(1)}, bf16[128,1152]{1,0:T(8,128)(2,1)S(1)}, u32[]{:S(2)}, u32[]{:S(2)}) collective-permute-start(bf16[128,1152]{1,0:T(8,128)(2,1)S(1)} %pad_maximum_fusion.3), channel_id=1, source_target_pairs={{0,16},{2,18},{4,20},{6,22},{8,24},{10,26},{12,28},{14,30},{16,0},... | collective-permute-start | bytes 884744 | tf_op jit(solution)/shard_map/ppermute | solution.py:106
  116.4 9.0 %collective-permute-start.27 = (bf16[4,64,512]{2,1,0:T(8,128)(2,1)S(1)}, bf16[4,64,512]{2,1,0:T(8,128)(2,1)S(1)}, u32[]{:S(2)}, u32[]{:S(2)}) collective-permute-start(bf16[4,64,512]{2,1,0:T(8,128)(2,1)S(1)} %hidden.1.refs_0_), channel_id=1, source_target_pairs={{0,2},{2,0},{4,6},{6,4},{8,10},{10,8},{12,14},{14,12},{16,18},{18,... | collective-permute-start | bytes 786440 | tf_op jit(solution)/shard_map/ppermute | solution.py:106
  117.8 7.6 %collective-permute-start.28 = (bf16[4,64,512]{2,1,0:T(8,128)(2,1)S(1)}, bf16[4,64,512]{2,1,0:T(8,128)(2,1)S(1)}, u32[]{:S(2)}, u32[]{:S(2)}) collective-permute-start(bf16[4,64,512]{2,1,0:T(8,128)(2,1)S(1)} %hidden.1.refs_0_), channel_id=1, source_target_pairs={{0,4},{2,6},{4,0},{6,2},{8,12},{10,14},{12,8},{14,10},{16,20},{18,... | collective-permute-start | bytes 786440 | tf_op jit(solution)/shard_map/ppermute | solution.py:106
  (20 other events, 91.5 us)

commit v18 on v17

--- a/solution.py
+++ b/solution.py
@@ -164,12 +164,16 @@
         copy.wait()
 
 
-def mark_kernel(where, tokens, positions, ids, mine, events, sem):
+def mark_kernel(where, tokens, p_hbm, i_hbm, mine, events, positions, ids, sems):
     u = where[3]
     rows, model = events.shape
     own = tokens.at[pl.ds(pl.multiple_of(u * rows, rows), rows), :]
-    copy = pltpu.make_async_copy(own, events, sem)
-    copy.start()
+    copies = [(p_hbm, positions), (i_hbm, ids), (own, events)]
+    copies = [pltpu.make_async_copy(a, b, sems.at[i]) for i, (a, b) in enumerate(copies)]
+    for copy in copies:
+        copy.start()
+    for copy in copies[:2]:
+        copy.wait()
     lane = lax.broadcasted_iota(jnp.int32, (rows, W), 1)
     marks = jnp.zeros((rows, W), F32)
     values = ((positions, u * rows, 7), (positions, (1 - u) * rows, 7), (ids, 0, 8))
@@ -182,7 +186,7 @@
         marks = jnp.where(lane == 2 * i, high.astype(F32), marks)
         marks = jnp.where(lane == 2 * i + 1, (column - high * 2**bits).astype(F32), marks)
     mine[:, model:] = marks.astype(BF16)
-    copy.wait()
+    copies[2].wait()
     mine[:, :model] = events[...]
 
 
@@ -365,7 +369,7 @@
 
 
 def call(kernel, name, outs, scratch, args, places, flops):
-    space = {"s": pltpu.SMEM, "v": pltpu.VMEM, "h": pl.ANY}
+    space = {"s": pltpu.SMEM, "v": pltpu.VMEM, "h": pl.ANY, "o": pltpu.HBM}
     moved = sum(a.size * a.dtype.itemsize for a in args)
     return pl.pallas_call(
         kernel,
@@ -414,9 +418,14 @@
         mark_kernel,
         "mark",
         [((rows, model + W), BF16)],
-        [pltpu.VMEM((rows, model), BF16), pltpu.SemaphoreType.DMA],
+        [
+            pltpu.VMEM((rows, model), BF16),
+            pltpu.VMEM((1, 2 * rows), jnp.int32),
+            pltpu.VMEM((1, rows), jnp.int32),
+            pltpu.SemaphoreType.DMA((3,)),
+        ],
         [where, tokens, positions.reshape(1, 2 * rows), target_ids.reshape(1, rows)],
-        "shvv",
+        "sooo",
         0,
     )
     line = [mine] + [hop(mine, flip(0, 0, s)) for s in range(1, NZ)]
@@ -475,8 +484,9 @@
         6 * "h",
         0,
     )
-    out_own, out_pair_theirs, gated = lax.optimization_barrier((out_own, out_pair_theirs, gated))
-    gated = jnp.stack([gated[0]] + [hop(gated[s], flip(0, 0, s)) for s in range(1, NZ)])
+    hops = [hop(gated[s], flip(0, 0, s)) for s in (1, 2)]
+    out_own, out_pair_theirs, last = lax.optimization_barrier((out_own, out_pair_theirs, gated[3]))
+    gated = jnp.stack([gated[0], *hops, hop(last, flip(0, 0, 3))])
     neg_pair = pair_up(after(neg, gated))
     neg_far = hop(neg_pair, flip(0, 0, 2))
     out_other = [out_pair_theirs, swap_cores(after(out_own[1], gated))]

time: 142 us -> 141 us (level)
  starting transfers between devices: 40.4 us -> 37.1 us
  waiting for transfers between devices: 76.3 us -> 78.4 us
    ppermute x28, starting transfers between devices: 37.9 us -> 34.4 us  [hop(): return lax.ppermute(value, 'ctx', perm)]
    ppermute x28, waiting for transfers between devices: 74.2 us -> 76.3 us  [hop(): return lax.ppermute(value, 'ctx', perm)]
where the time goes in v18:
time: 141 us; the launch traced here: 140 us
  waiting for transfers between devices  78.4 us (56%)
  starting transfers between devices  37.1 us (26%)
  Pallas kernels  13.6 us (10%)
  local copies, waits for them, and re-layouts  8.21 us (6%)
  other arithmetic  1.95 us (1%)
    ppermute x28, waiting for transfers between devices, hop(): return lax.ppermute(value, 'ctx', perm)  76.3 us
    ppermute x28, starting transfers between devices, hop(): return lax.ppermute(value, 'ctx', perm)  34.4 us
    pallas_call x6, Pallas kernels, call(): pl.pallas_call(kernel, out_shape=[jax.ShapeDtypeStruct(shape, dtype) for...  13.6 us
    squeeze x6, local copies, waits for them, and re-layouts, pick_row(): return lax.dynamic_index_in_dim(value, at, 0, keepdims=False)  3.08 us
  transfers between devices with their start and end apart: 39, of which 21 were waited for; matrix products, arithmetic and copies ran while one was open for 5% of the time, Pallas kernels for 7%

profile of v18, /device:TPU:0, one launch (start us, length us, event | category | flops | bytes accessed | tf_op | source)
XLA Modules:
  0.0 140.2 jit_solution(4358440426380532463)
XLA Ops:
  3.9 3.1 %collective-permute-start.4 = (bf16[64,2176]{1,0:T(8,128)(2,1)S(1)}, bf16[64,2176]{1,0:T(8,128)(2,1)S(1)}, u32[]{:S(2)}, u32[]{:S(2)}) collective-permute-start(bf16[64,2176]{1,0:T(8,128)(2,1)S(1)} %mark.1), channel_id=1, source_target_pairs={{0,8},{2,10},{4,12},{6,14},{8,0},{10,2},{12,4},{14,6},{16,24},{18,... | collective-permute-start | bytes 835592 | tf_op jit(solution)/shard_map/ppermute | solution.py:106
  7.0 2.6 %collective-permute-start.5 = (bf16[64,2176]{1,0:T(8,128)(2,1)S(1)}, bf16[64,2176]{1,0:T(8,128)(2,1)S(1)}, u32[]{:S(2)}, u32[]{:S(2)}) collective-permute-start(bf16[64,2176]{1,0:T(8,128)(2,1)S(1)} %mark.1), channel_id=1, source_target_pairs={{0,16},{2,18},{4,20},{6,22},{8,24},{10,26},{12,28},{14,30},{16,0},... | collective-permute-start | bytes 835592 | tf_op jit(solution)/shard_map/ppermute | solution.py:106
  12.0 1.8 %collective-permute-start.1 = (bf16[2,128,512]{2,1,0:T(8,128)(2,1)S(1)}, bf16[2,128,512]{2,1,0:T(8,128)(2,1)}, u32[]{:S(2)}, u32[]{:S(2)}) collective-permute-start(bf16[2,128,512]{2,1,0:T(8,128)(2,1)S(1)} %get-tuple-element.37), channel_id=1, source_target_pairs={{0,4},{2,6},{4,0},{6,2},{8,12},{10,14},{12,8},{14,10},{16,20},{18,... | collective-permute-start | bytes 786440 | tf_op jit(solution)/shard_map/ppermute | solution.py:106
  17.2 2.5 %collective-permute-done.1 = bf16[2,128,512]{2,1,0:T(8,128)(2,1)} collective-permute-done((bf16[2,128,512]{2,1,0:T(8,128)(2,1)S(1)}, bf16[2,128,512]{2,1,0:T(8,128)(2,1)}, u32[]{:S(2)}, u32[]{:S(2)}) %collective-permute-start.1) | collective-permute-done | bytes 262176 | tf_op jit(solution)/shard_map/ppermute | solution.py:106
  26.0 2.2 %collective-permute-done.2 = bf16[2,128,512]{2,1,0:T(8,128)(2,1)S(1)} collective-permute-done((bf16[2,128,512]{2,1,0:T(8,128)(2,1)S(1)}, bf16[2,128,512]{2,1,0:T(8,128)(2,1)S(1)}, u32[]{:S(2)}, u32[]{:S(2)}) %collective-permute-start.2) | collective-permute-done | bytes 262176 | tf_op jit(solution)/shard_map/ppermute | solution.py:106
  28.2 6.0 %collective-permute-done.3 = bf16[1,1024,128]{2,1,0:T(8,128)(2,1)S(1)} collective-permute-done((bf16[1,1024,128]{2,1,0:T(8,128)(2,1)}, bf16[1,1024,128]{2,1,0:T(8,128)(2,1)S(1)}, u32[]{:S(2)}, u32[]{:S(2)}) %collective-permute-start.3) | collective-permute-done | bytes 262176 | tf_op jit(solution)/shard_map/ppermute | solution.py:106
  38.7 22.4 %collective-permute-done.8.refs_2_.refs_11_ = bf16[256,2176]{1,0:T(8,128)(2,1)S(1)} collective-permute-done((bf16[256,2176]{1,0:T(8,128)(2,1)S(1)}, bf16[256,2176]{1,0:T(8,128)(2,1)S(1)}, u32[]{:S(2)}, u32[]{:S(2)}) %collective-permute-start.8) | collective-permute-done | bytes 1114144 | tf_op jit(solution)/shard_map/ppermute | solution.py:106
  64.6 2.3 %collective-permute-start.19 = (bf16[2,1024,128]{2,1,0:T(8,128)(2,1)S(1)}, bf16[2,1024,128]{2,1,0:T(8,128)(2,1)S(1)}, u32[]{:S(2)}, u32[]{:S(2)}) collective-permute-start(bf16[2,1024,128]{2,1,0:T(8,128)(2,1)S(1)} %pad_maximum_fusion.2.refs_5_), channel_id=1, source_target_pairs={{0,16},{2,18},{4,20},{6,22},{8,24},{10,26},{12,28},{14,30},{16,0},... | collective-permute-start | bytes 1572872 | tf_op jit(solution)/shard_map/ppermute | solution.py:106
  66.9 8.0 %collective-permute-done.10.refs_4_ = bf16[128,2176]{1,0:T(8,128)(2,1)S(1)} collective-permute-done((bf16[128,2176]{1,0:T(8,128)(2,1)S(1)}, bf16[128,2176]{1,0:T(8,128)(2,1)S(1)}, u32[]{:S(2)}, u32[]{:S(2)}) %collective-permute-start.10) | collective-permute-done | bytes 557088 | tf_op jit(solution)/shard_map/ppermute | solution.py:106
  76.2 3.8 %project.1 = (bf16[1024,256]{1,0:T(8,128)(2,1)S(1)}, bf16[1024,128]{1,0:T(8,128)(2,1)S(1)}, bf16[1024,128]{1,0:T(8,128)(2,1)S(1)}, bf16[1024,128]{1,0:T(8,128)(2,1)S(1)}) custom-call(s32[4]{0:T(128)S(1)} %pad_add_fusion.where, bf16[256,2176]{1,0:T(8,128)(2,1)S(1)} %constant_dynamic-update-slice_fusion.refs_0_.refs_9_, ...), custom_call_target="tpu_custom_call" | custom-call | bytes 6553616 | tf_op jit(solution)/shard_map/project/pallas_call | solution.py:374
  80.7 1.7 %collective-permute-done.15.refs_3_ = bf16[1024,128]{1,0:T(8,128)(2,1)S(1)} collective-permute-done((bf16[1024,128]{1,0:T(8,128)(2,1)S(1)}, bf16[1024,128]{1,0:T(8,128)(2,1)S(1)}, u32[]{:S(2)}, u32[]{:S(2)}) %collective-permute-start.15) | collective-permute-done | bytes 262176 | tf_op jit(solution)/shard_map/ppermute | solution.py:110
  82.8 3.4 %attend.1 = bf16[4,4,64,128]{3,2,1,0:T(8,128)(2,1)S(1)} custom-call(bf16[1024,256]{1,0:T(8,128)(2,1)S(1)} %get-tuple-element.46.refs_0_, bf16[1024,128]{1,0:T(8,128)(2,1)S(1)} %get-tuple-element.47.refs_1_, bf16[1024,128]{1,0:T(8,128)(2,1)S(1)} %get-tuple-element.48.refs_2_, bf16[1024,128]{1,0:T(8,128)(2,1)S(1)} %collective-permute-done.15.refs_3_, ...), custom_call_target="tpu_custom_call" | custom-call | bytes 1835008 | tf_op jit(solution)/shard_map/attend/pallas_call | solution.py:374
  86.3 1.6 %collective-permute-start.18 = (bf16[4,64,128]{2,1,0:T(8,128)(2,1)S(1)}, bf16[4,64,128]{2,1,0:T(8,128)(2,1)S(1)}, u32[]{:S(2)}, u32[]{:S(2)}) collective-permute-start(bf16[4,64,128]{2,1,0:T(8,128)(2,1)S(1)} %get-tuple-element.79), channel_id=1, source_target_pairs={{0,16},{2,18},{4,20},{6,22},{8,24},{10,26},{12,28},{14,30},{16,0},... | collective-permute-start | bytes 196616 | tf_op jit(solution)/shard_map/ppermute | solution.py:106
  87.9 4.2 %collective-permute-done.19.refs_6_ = bf16[2,1024,128]{2,1,0:T(8,128)(2,1)S(1)} collective-permute-done((bf16[2,1024,128]{2,1,0:T(8,128)(2,1)S(1)}, bf16[2,1024,128]{2,1,0:T(8,128)(2,1)S(1)}, u32[]{:S(2)}, u32[]{:S(2)}) %collective-permute-start.19) | collective-permute-done | bytes 524320 | tf_op jit(solution)/shard_map/ppermute | solution.py:106
  92.2 2.5 %collective-permute-start.21 = (bf16[4,64,128]{2,1,0:T(8,128)(2,1)S(1)}, bf16[4,64,128]{2,1,0:T(8,128)(2,1)S(1)}, u32[]{:S(2)}, u32[]{:S(2)}) collective-permute-start(bf16[4,64,128]{2,1,0:T(8,128)(2,1)S(1)} %get-tuple-element.53), channel_id=1, source_target_pairs={{0,24},{2,26},{4,28},{6,30},{8,16},{10,18},{12,20},{14,22},{16,8},... | collective-permute-start | bytes 196616 | tf_op jit(solution)/shard_map/ppermute | solution.py:106
  94.7 3.5 %collective-permute-done.21 = bf16[4,64,128]{2,1,0:T(8,128)(2,1)S(1)} collective-permute-done((bf16[4,64,128]{2,1,0:T(8,128)(2,1)S(1)}, bf16[4,64,128]{2,1,0:T(8,128)(2,1)S(1)}, u32[]{:S(2)}, u32[]{:S(2)}) %collective-permute-start.21) | collective-permute-done | bytes 65568 | tf_op jit(solution)/shard_map/ppermute | solution.py:106
  99.1 8.0 %collective-permute-done.22.refs_1_ = bf16[4,4,64,128]{3,2,1,0:T(8,128)(2,1)S(1)} collective-permute-done((bf16[4,4,64,128]{3,2,1,0:T(8,128)(2,1)S(1)}, bf16[4,4,64,128]{3,2,1,0:T(8,128)(2,1)S(1)}, u32[]{:S(2)}, u32[]{:S(2)}) %collective-permute-start.22) | collective-permute-done | bytes 262176 | tf_op jit(solution)/shard_map/ppermute | solution.py:106
  109.0 3.2 %collective-permute-done.24.refs_3_ = bf16[2,4,64,128]{3,2,1,0:T(8,128)(2,1)S(1)} collective-permute-done((bf16[2,4,64,128]{3,2,1,0:T(8,128)(2,1)S(1)}, bf16[2,4,64,128]{3,2,1,0:T(8,128)(2,1)S(1)}, u32[]{:S(2)}, u32[]{:S(2)}) %collective-permute-start.24) | collective-permute-done | bytes 131104 | tf_op jit(solution)/shard_map/ppermute | solution.py:106
  112.3 2.7 %hidden.1.refs_0_ = bf16[4,64,512]{2,1,0:T(8,128)(2,1)S(1)} custom-call(s32[4]{0:T(128)S(1)} %pad_add_fusion.where, bf16[4,4,64,128]{3,2,1,0:T(8,128)(2,1)S(1)} %pad_maximum_fusion.4.refs_0_, bf16[4,4,64,128]{3,2,1,0:T(8,128)(2,1)S(1)} %collective-permute-done.22.refs_1_, bf16[4,4,64,128]{3,2,1,0:T(8,128)(2,1)S(1)} %collective-permute-done.23.refs_2_, ...), custom_call_target="tpu_custom_call" | custom-call | flops 536870912 | bytes 7045136 | tf_op jit(solution)/shard_map/hidden/pallas_call | solution.py:374
  117.5 6.5 %collective-permute-done.32 = bf16[128,1152]{1,0:T(8,128)(2,1)S(1)} collective-permute-done((bf16[128,1152]{1,0:T(8,128)(2,1)S(1)}, bf16[128,1152]{1,0:T(8,128)(2,1)S(1)}, u32[]{:S(2)}, u32[]{:S(2)}) %collective-permute-start.32) | collective-permute-done | bytes 294944 | tf_op jit(solution)/shard_map/ppermute | solution.py:106
  125.2 1.6 %collective-permute-start.30 = (bf16[2,64,512]{2,1,0:T(8,128)(2,1)S(1)}, bf16[2,64,512]{2,1,0:T(8,128)(2,1)S(1)}, u32[]{:S(2)}, u32[]{:S(2)}) collective-permute-start(bf16[2,64,512]{2,1,0:T(8,128)(2,1)S(1)} %slice.65), channel_id=1, source_target_pairs={{0,2},{2,0},{4,6},{6,4},{8,10},{10,8},{12,14},{14,12},{16,18},{18,... | collective-permute-start | bytes 393224 | tf_op jit(solution)/shard_map/ppermute | solution.py:106
  126.8 3.4 %collective-permute-done.29.refs_3_ = bf16[2,64,512]{2,1,0:T(8,128)(2,1)S(1)} collective-permute-done((bf16[2,64,512]{2,1,0:T(8,128)(2,1)S(1)}, bf16[2,64,512]{2,1,0:T(8,128)(2,1)S(1)}, u32[]{:S(2)}, u32[]{:S(2)}) %collective-permute-start.29) | collective-permute-done | bytes 131104 | tf_op jit(solution)/shard_map/ppermute | solution.py:106
  132.5 1.6 %collective-permute-start.36 = (f32[1,64]{1,0:T(1,128)S(1)}, f32[1,64]{1,0:T(1,128)S(1)}, u32[]{:S(2)}, u32[]{:S(2)}) collective-permute-start(f32[1,64]{1,0:T(1,128)S(1)} %get-tuple-element.91), channel_id=1, source_target_pairs={{0,2},{2,0},{4,6},{6,4},{8,10},{10,8},{12,14},{14,12},{16,18},{18,... | collective-permute-start | bytes 776 | tf_op jit(solution)/shard_map/ppermute | solution.py:106
  134.5 1.6 %collective-permute-start.38 = (f32[1,64]{1,0:T(1,128)S(1)}, f32[1,64]{1,0:T(1,128)S(1)}, u32[]{:S(2)}, u32[]{:S(2)}) collective-permute-start(f32[1,64]{1,0:T(1,128)S(1)} %get-tuple-element.89), channel_id=1, source_target_pairs={{0,6},{2,4},{4,2},{6,0},{8,14},{10,12},{12,10},{14,8},{16,22},{18,... | collective-permute-start | bytes 776 | tf_op jit(solution)/shard_map/ppermute | solution.py:106
  (106 shorter events, 38.8 us)
Async XLA Ops:
  3.9 30.5 %collective-permute-start.4 = (bf16[64,2176]{1,0:T(8,128)(2,1)S(1)}, bf16[64,2176]{1,0:T(8,128)(2,1)S(1)}, u32[]{:S(2)}, u32[]{:S(2)}) collective-permute-start(bf16[64,2176]{1,0:T(8,128)(2,1)S(1)} %mark.1), channel_id=1, source_target_pairs={{0,8},{2,10},{4,12},{6,14},{8,0},{10,2},{12,4},{14,6},{16,24},{18,... | collective-permute-start | bytes 835592 | tf_op jit(solution)/shard_map/ppermute | solution.py:106
  7.0 27.4 %collective-permute-start.5 = (bf16[64,2176]{1,0:T(8,128)(2,1)S(1)}, bf16[64,2176]{1,0:T(8,128)(2,1)S(1)}, u32[]{:S(2)}, u32[]{:S(2)}) collective-permute-start(bf16[64,2176]{1,0:T(8,128)(2,1)S(1)} %mark.1), channel_id=1, source_target_pairs={{0,16},{2,18},{4,20},{6,22},{8,24},{10,26},{12,28},{14,30},{16,0},... | collective-permute-start | bytes 835592 | tf_op jit(solution)/shard_map/ppermute | solution.py:106
  9.6 24.8 %collective-permute-start.6 = (bf16[64,2176]{1,0:T(8,128)(2,1)S(1)}, bf16[64,2176]{1,0:T(8,128)(2,1)S(1)}, u32[]{:S(2)}, u32[]{:S(2)}) collective-permute-start(bf16[64,2176]{1,0:T(8,128)(2,1)S(1)} %mark.1), channel_id=1, source_target_pairs={{0,24},{2,26},{4,28},{6,30},{8,16},{10,18},{12,20},{14,22},{16,8},... | collective-permute-start | bytes 835592 | tf_op jit(solution)/shard_map/ppermute | solution.py:106
  12.0 7.7 %collective-permute-start.1 = (bf16[2,128,512]{2,1,0:T(8,128)(2,1)S(1)}, bf16[2,128,512]{2,1,0:T(8,128)(2,1)}, u32[]{:S(2)}, u32[]{:S(2)}) collective-permute-start(bf16[2,128,512]{2,1,0:T(8,128)(2,1)S(1)} %get-tuple-element.37), channel_id=1, source_target_pairs={{0,4},{2,6},{4,0},{6,2},{8,12},{10,14},{12,8},{14,10},{16,20},{18,... | collective-permute-start | bytes 786440 | tf_op jit(solution)/shard_map/ppermute | solution.py:106
  20.9 7.3 %collective-permute-start.2 = (bf16[2,128,512]{2,1,0:T(8,128)(2,1)S(1)}, bf16[2,128,512]{2,1,0:T(8,128)(2,1)S(1)}, u32[]{:S(2)}, u32[]{:S(2)}) collective-permute-start(bf16[2,128,512]{2,1,0:T(8,128)(2,1)S(1)} %get-tuple-element.38), channel_id=1, source_target_pairs={{0,6},{2,4},{4,2},{6,0},{8,14},{10,12},{12,10},{14,8},{16,22},{18,... | collective-permute-start | bytes 786440 | tf_op jit(solution)/shard_map/ppermute | solution.py:106
  23.3 10.9 %collective-permute-start.3 = (bf16[1,1024,128]{2,1,0:T(8,128)(2,1)}, bf16[1,1024,128]{2,1,0:T(8,128)(2,1)S(1)}, u32[]{:S(2)}, u32[]{:S(2)}) collective-permute-start(bf16[1,1024,128]{2,1,0:T(8,128)(2,1)} %bitcast.68), channel_id=1, source_target_pairs={{0,8},{2,10},{4,12},{6,14},{8,0},{10,2},{12,4},{14,6},{16,24},{18,... | collective-permute-start | bytes 786440 | tf_op jit(solution)/shard_map/ppermute | solution.py:106
  34.5 26.5 %collective-permute-start.8 = (bf16[256,2176]{1,0:T(8,128)(2,1)S(1)}, bf16[256,2176]{1,0:T(8,128)(2,1)S(1)}, u32[]{:S(2)}, u32[]{:S(2)}) collective-permute-start(bf16[256,2176]{1,0:T(8,128)(2,1)S(1)} %constant_dynamic-update-slice_fusion.refs_0_.refs_9_), channel_id=1, source_target_pairs={{0,4},{2,6},{4,0},{6,2},{8,12},{10,14},{12,8},{14,10},{16,20},{18,... | collective-permute-start | bytes 3342344 | tf_op jit(solution)/shard_map/ppermute | solution.py:106
  36.1 26.6 %collective-permute-start.7 = (bf16[256,2176]{1,0:T(8,128)(2,1)S(1)}, bf16[256,2176]{1,0:T(8,128)(2,1)S(1)}, u32[]{:S(2)}, u32[]{:S(2)}) collective-permute-start(bf16[256,2176]{1,0:T(8,128)(2,1)S(1)} %constant_dynamic-update-slice_fusion.refs_0_.refs_9_), channel_id=1, source_target_pairs={{0,2},{2,0},{4,6},{6,4},{8,10},{10,8},{12,14},{14,12},{16,18},{18,... | collective-permute-start | bytes 3342344 | tf_op jit(solution)/shard_map/ppermute | solution.py:106
  37.5 26.6 %collective-permute-start.11 = (bf16[512,512]{1,0:T(8,128)(2,1)S(1)}, bf16[512,512]{1,0:T(8,128)(2,1)S(1)}, u32[]{:S(2)}, u32[]{:S(2)}) collective-permute-start(bf16[512,512]{1,0:T(8,128)(2,1)S(1)} %get-tuple-element.44), channel_id=1, source_target_pairs={{0,0},{1,16},{2,2},{3,18},{4,4},{5,20},{6,6},{7,22},{8,8},{9,24},{... | collective-permute-start | bytes 1572872 | tf_op jit(solution)/shard_map/ppermute | solution.py:152
  38.4 25.7 %collective-permute-start.12 = (bf16[512,512]{1,0:T(8,128)(2,1)S(1)}, bf16[512,512]{1,0:T(8,128)(2,1)S(1)}, u32[]{:S(2)}, u32[]{:S(2)}) collective-permute-start(bf16[512,512]{1,0:T(8,128)(2,1)S(1)} %get-tuple-element.45), channel_id=1, source_target_pairs={{0,8},{1,24},{2,10},{3,26},{4,12},{5,28},{6,14},{7,30},{8,0},{9,16... | collective-permute-start | bytes 1572872 | tf_op jit(solution)/shard_map/ppermute | solution.py:152
  61.1 13.7 %collective-permute-start.10 = (bf16[128,2176]{1,0:T(8,128)(2,1)S(1)}, bf16[128,2176]{1,0:T(8,128)(2,1)S(1)}, u32[]{:S(2)}, u32[]{:S(2)}) collective-permute-start(bf16[128,2176]{1,0:T(8,128)(2,1)S(1)} %slice.57), channel_id=1, source_target_pairs={{0,2},{2,0},{4,6},{6,4},{8,10},{10,8},{12,14},{14,12},{16,18},{18,... | collective-permute-start | bytes 1671176 | tf_op jit(solution)/shard_map/ppermute | solution.py:106
  62.7 13.5 %collective-permute-start.9 = (bf16[128,2176]{1,0:T(8,128)(2,1)S(1)}, bf16[128,2176]{1,0:T(8,128)(2,1)S(1)}, u32[]{:S(2)}, u32[]{:S(2)}) collective-permute-start(bf16[128,2176]{1,0:T(8,128)(2,1)S(1)} %slice.56), channel_id=1, source_target_pairs={{0,4},{2,6},{4,0},{6,2},{8,12},{10,14},{12,8},{14,10},{16,20},{18,... | collective-permute-start | bytes 1671176 | tf_op jit(solution)/shard_map/ppermute | solution.py:106
  64.6 27.6 %collective-permute-start.19 = (bf16[2,1024,128]{2,1,0:T(8,128)(2,1)S(1)}, bf16[2,1024,128]{2,1,0:T(8,128)(2,1)S(1)}, u32[]{:S(2)}, u32[]{:S(2)}) collective-permute-start(bf16[2,1024,128]{2,1,0:T(8,128)(2,1)S(1)} %pad_maximum_fusion.2.refs_5_), channel_id=1, source_target_pairs={{0,16},{2,18},{4,20},{6,22},{8,24},{10,26},{12,28},{14,30},{16,0},... | collective-permute-start | bytes 1572872 | tf_op jit(solution)/shard_map/ppermute | solution.py:106
  80.0 12.1 %collective-permute-start.20 = (bf16[2,1024,128]{2,1,0:T(8,128)(2,1)S(1)}, bf16[2,1024,128]{2,1,0:T(8,128)(2,1)S(1)}, u32[]{:S(2)}, u32[]{:S(2)}) collective-permute-start(bf16[2,1024,128]{2,1,0:T(8,128)(2,1)S(1)} %pad_maximum_fusion.2.refs_5_), channel_id=1, source_target_pairs={{0,1},{1,0},{2,3},{3,2},{4,5},{5,4},{6,7},{7,6},{8,9},{9,8},{10,11... | collective-permute-start | bytes 1572872 | tf_op jit(solution)/shard_map/ppermute | solution.py:110
  86.2 8.5 %collective-permute-start.17 = (bf16[4,64,128]{2,1,0:T(8,128)(2,1)S(1)}, bf16[4,64,128]{2,1,0:T(8,128)(2,1)S(1)}, u32[]{:S(2)}, u32[]{:S(2)}) collective-permute-start(bf16[4,64,128]{2,1,0:T(8,128)(2,1)S(1)} %get-tuple-element.80), channel_id=1, source_target_pairs={{0,8},{2,10},{4,12},{6,14},{8,0},{10,2},{12,4},{14,6},{16,24},{18,... | collective-permute-start | bytes 196616 | tf_op jit(solution)/shard_map/ppermute | solution.py:106
  86.3 8.4 %collective-permute-start.18 = (bf16[4,64,128]{2,1,0:T(8,128)(2,1)S(1)}, bf16[4,64,128]{2,1,0:T(8,128)(2,1)S(1)}, u32[]{:S(2)}, u32[]{:S(2)}) collective-permute-start(bf16[4,64,128]{2,1,0:T(8,128)(2,1)S(1)} %get-tuple-element.79), channel_id=1, source_target_pairs={{0,16},{2,18},{4,20},{6,22},{8,24},{10,26},{12,28},{14,30},{16,0},... | collective-permute-start | bytes 196616 | tf_op jit(solution)/shard_map/ppermute | solution.py:106
  98.3 14.1 %collective-permute-start.26 = (bf16[2,1024,128]{2,1,0:T(8,128)(2,1)S(1)}, bf16[2,1024,128]{2,1,0:T(8,128)(2,1)S(1)}, u32[]{:S(2)}, u32[]{:S(2)}) collective-permute-start(bf16[2,1024,128]{2,1,0:T(8,128)(2,1)S(1)} %collective-permute-done.19.refs_6_), channel_id=1, source_target_pairs={{0,1},{1,0},{2,3},{3,2},{4,5},{5,4},{6,7},{7,6},{8,9},{9,8},{10,11... | collective-permute-start | bytes 1572872 | tf_op jit(solution)/shard_map/ppermute | solution.py:110
  98.4 8.7 %collective-permute-start.22 = (bf16[4,4,64,128]{3,2,1,0:T(8,128)(2,1)S(1)}, bf16[4,4,64,128]{3,2,1,0:T(8,128)(2,1)S(1)}, u32[]{:S(2)}, u32[]{:S(2)}) collective-permute-start(bf16[4,4,64,128]{3,2,1,0:T(8,128)(2,1)S(1)} %pad_maximum_fusion.4.refs_0_), channel_id=1, source_target_pairs={{0,2},{2,0},{4,6},{6,4},{8,10},{10,8},{12,14},{14,12},{16,18},{18,... | collective-permute-start | bytes 786440 | tf_op jit(solution)/shard_map/ppermute | solution.py:106
  98.9 8.4 %collective-permute-start.23 = (bf16[4,4,64,128]{3,2,1,0:T(8,128)(2,1)S(1)}, bf16[4,4,64,128]{3,2,1,0:T(8,128)(2,1)S(1)}, u32[]{:S(2)}, u32[]{:S(2)}) collective-permute-start(bf16[4,4,64,128]{3,2,1,0:T(8,128)(2,1)S(1)} %pad_maximum_fusion.4.refs_0_), channel_id=1, source_target_pairs={{0,4},{2,6},{4,0},{6,2},{8,12},{10,14},{12,8},{14,10},{16,20},{18,... | collective-permute-start | bytes 786440 | tf_op jit(solution)/shard_map/ppermute | solution.py:106
  98.9 10.0 %collective-permute-start.31 = (bf16[64,1152]{1,0:T(8,128)(2,1)S(1)}, bf16[64,1152]{1,0:T(8,128)(2,1)S(1)}, u32[]{:S(2)}, u32[]{:S(2)}) collective-permute-start(bf16[64,1152]{1,0:T(8,128)(2,1)S(1)} %fusion.1), channel_id=1, source_target_pairs={{0,8},{2,10},{4,12},{6,14},{8,0},{10,2},{12,4},{14,6},{16,24},{18,... | collective-permute-start | bytes 442376 | tf_op jit(solution)/shard_map/ppermute | solution.py:106
  98.9 18.6 %collective-permute-start.33 = (bf16[64,1024]{1,0:T(8,128)(2,1)S(1)}, bf16[64,1024]{1,0:T(8,128)(2,1)S(1)}, u32[]{:S(2)}, u32[]{:S(2)}) collective-permute-start(bf16[64,1024]{1,0:T(8,128)(2,1)S(1)} %get-tuple-element.61), channel_id=1, source_target_pairs={{0,1},{1,0},{2,3},{3,2},{4,5},{5,4},{6,7},{7,6},{8,9},{9,8},{10,11... | collective-permute-start | bytes 393224 | tf_op jit(solution)/shard_map/ppermute | solution.py:110
  108.9 15.1 %collective-permute-start.32 = (bf16[128,1152]{1,0:T(8,128)(2,1)S(1)}, bf16[128,1152]{1,0:T(8,128)(2,1)S(1)}, u32[]{:S(2)}, u32[]{:S(2)}) collective-permute-start(bf16[128,1152]{1,0:T(8,128)(2,1)S(1)} %pad_maximum_fusion.3), channel_id=1, source_target_pairs={{0,16},{2,18},{4,20},{6,22},{8,24},{10,26},{12,28},{14,30},{16,0},... | collective-permute-start | bytes 884744 | tf_op jit(solution)/shard_map/ppermute | solution.py:106
  115.0 9.0 %collective-permute-start.27 = (bf16[4,64,512]{2,1,0:T(8,128)(2,1)S(1)}, bf16[4,64,512]{2,1,0:T(8,128)(2,1)S(1)}, u32[]{:S(2)}, u32[]{:S(2)}) collective-permute-start(bf16[4,64,512]{2,1,0:T(8,128)(2,1)S(1)} %hidden.1.refs_0_), channel_id=1, source_target_pairs={{0,2},{2,0},{4,6},{6,4},{8,10},{10,8},{12,14},{14,12},{16,18},{18,... | collective-permute-start | bytes 786440 | tf_op jit(solution)/shard_map/ppermute | solution.py:106
  116.6 7.4 %collective-permute-start.28 = (bf16[4,64,512]{2,1,0:T(8,128)(2,1)S(1)}, bf16[4,64,512]{2,1,0:T(8,128)(2,1)S(1)}, u32[]{:S(2)}, u32[]{:S(2)}) collective-permute-start(bf16[4,64,512]{2,1,0:T(8,128)(2,1)S(1)} %hidden.1.refs_0_), channel_id=1, source_target_pairs={{0,4},{2,6},{4,0},{6,2},{8,12},{10,14},{12,8},{14,10},{16,20},{18,... | collective-permute-start | bytes 786440 | tf_op jit(solution)/shard_map/ppermute | solution.py:106
  (20 other events, 94.0 us)

commit v19 on v18

--- a/solution.py
+++ b/solution.py
@@ -368,7 +368,7 @@
     loss[...] = jnp.log(total) - positive[...]
 
 
-def call(kernel, name, outs, scratch, args, places, flops):
+def call(kernel, name, outs, scratch, args, places, flops, vmem=VMEM_LIMIT):
     space = {"s": pltpu.SMEM, "v": pltpu.VMEM, "h": pl.ANY, "o": pltpu.HBM}
     moved = sum(a.size * a.dtype.itemsize for a in args)
     return pl.pallas_call(
@@ -377,7 +377,7 @@
         in_specs=[pl.BlockSpec(memory_space=space[p]) for p in places],
         out_specs=[pl.BlockSpec(memory_space=pltpu.VMEM)] * len(outs),
         scratch_shapes=scratch,
-        compiler_params=pltpu.CompilerParams(vmem_limit_bytes=VMEM_LIMIT),
+        compiler_params=pltpu.CompilerParams(vmem_limit_bytes=vmem),
         cost_estimate=pl.CostEstimate(flops=flops, bytes_accessed=moved, transcendentals=0),
         name=name,
     )(*args)
@@ -427,6 +427,7 @@
         [where, tokens, positions.reshape(1, 2 * rows), target_ids.reshape(1, rows)],
         "sooo",
         0,
+        4 * VMEM_LIMIT,
     )
     line = [mine] + [hop(mine, flip(0, 0, s)) for s in range(1, NZ)]
 

time: 141 us -> 141 us (level)
  starting transfers between devices: 37.1 us -> 39.9 us
  waiting for transfers between devices: 78.4 us -> 75.8 us
  local copies, waits for them, and re-layouts: 8.21 us -> 5.74 us
  Pallas kernels: 13.6 us -> 15.2 us
    ppermute x28, starting transfers between devices: 34.4 us -> 37.6 us  [hop(): return lax.ppermute(value, 'ctx', perm)]
    ppermute x28, waiting for transfers between devices: 76.3 us -> 73.7 us  [hop(): return lax.ppermute(value, 'ctx', perm)]
    pallas_call x6, Pallas kernels: 13.6 us -> 15.2 us  [call(): pl.pallas_call(kernel, out_shape=[jax.ShapeDtypeStruct(shape, dtype) for...]
    unnamed x15, local copies, waits for them, and re-layouts: 2.47 us -> 0.97 us
  transfers between devices with their start and end apart: 39 -> 39, of which waited for: 21 -> 22; matrix products, arithmetic and copies ran while one was open for 5% -> 5% of each run, Pallas kernels for 7% -> 7%
where the time goes in v19:
time: 141 us; the launch traced here: 140 us
  waiting for transfers between devices  75.8 us (54%)
  starting transfers between devices  39.9 us (28%)
  Pallas kernels  15.2 us (11%)
  local copies, waits for them, and re-layouts  5.74 us (4%)
  other arithmetic  2.53 us (2%)
    ppermute x28, waiting for transfers between devices, hop(): return lax.ppermute(value, 'ctx', perm)  73.7 us
    ppermute x28, starting transfers between devices, hop(): return lax.ppermute(value, 'ctx', perm)  37.6 us
    pallas_call x6, Pallas kernels, call(): pl.pallas_call(kernel, out_shape=[jax.ShapeDtypeStruct(shape, dtype) for...  15.2 us
  transfers between devices with their start and end apart: 39, of which 22 were waited for; matrix products, arithmetic and copies ran while one was open for 5% of the time, Pallas kernels for 7%

profile of v19, /device:TPU:0, one launch (start us, length us, event | category | flops | bytes accessed | tf_op | source)
XLA Modules:
  0.0 140.3 jit_solution(11230714848828928592)
XLA Ops:
  1.3 2.4 %mark.1 = bf16[64,2176]{1,0:T(8,128)(2,1)} custom-call(s32[4]{0:T(128)} %pad_add_fusion.where, bf16[128,2048]{1,0:T(8,128)(2,1)} %tokens.1, s32[1,128]{1,0:T(1,128)} %bitcast.71, s32[1,64]{1,0:T(1,128)} %bitcast.72), custom_call_target="tpu_custom_call" | custom-call | bytes 525072 | tf_op jit(solution)/shard_map/mark/pallas_call | solution.py:374
  3.7 3.1 %collective-permute-start.4 = (bf16[64,2176]{1,0:T(8,128)(2,1)}, bf16[64,2176]{1,0:T(8,128)(2,1)S(1)}, u32[]{:S(2)}, u32[]{:S(2)}) collective-permute-start(bf16[64,2176]{1,0:T(8,128)(2,1)} %mark.1), channel_id=1, source_target_pairs={{0,8},{2,10},{4,12},{6,14},{8,0},{10,2},{12,4},{14,6},{16,24},{18,... | collective-permute-start | bytes 835592 | tf_op jit(solution)/shard_map/ppermute | solution.py:106
  6.8 2.6 %collective-permute-start.5 = (bf16[64,2176]{1,0:T(8,128)(2,1)}, bf16[64,2176]{1,0:T(8,128)(2,1)S(1)}, u32[]{:S(2)}, u32[]{:S(2)}) collective-permute-start(bf16[64,2176]{1,0:T(8,128)(2,1)} %mark.1), channel_id=1, source_target_pairs={{0,16},{2,18},{4,20},{6,22},{8,24},{10,26},{12,28},{14,30},{16,0},... | collective-permute-start | bytes 835592 | tf_op jit(solution)/shard_map/ppermute | solution.py:106
  11.9 1.8 %collective-permute-start.1 = (bf16[2,128,512]{2,1,0:T(8,128)(2,1)S(1)}, bf16[2,128,512]{2,1,0:T(8,128)(2,1)}, u32[]{:S(2)}, u32[]{:S(2)}) collective-permute-start(bf16[2,128,512]{2,1,0:T(8,128)(2,1)S(1)} %get-tuple-element.37), channel_id=1, source_target_pairs={{0,4},{2,6},{4,0},{6,2},{8,12},{10,14},{12,8},{14,10},{16,20},{18,... | collective-permute-start | bytes 786440 | tf_op jit(solution)/shard_map/ppermute | solution.py:106
  17.1 2.5 %collective-permute-done.1 = bf16[2,128,512]{2,1,0:T(8,128)(2,1)} collective-permute-done((bf16[2,128,512]{2,1,0:T(8,128)(2,1)S(1)}, bf16[2,128,512]{2,1,0:T(8,128)(2,1)}, u32[]{:S(2)}, u32[]{:S(2)}) %collective-permute-start.1) | collective-permute-done | bytes 262176 | tf_op jit(solution)/shard_map/ppermute | solution.py:106
  24.9 3.1 %collective-permute-done.2 = bf16[2,128,512]{2,1,0:T(8,128)(2,1)S(1)} collective-permute-done((bf16[2,128,512]{2,1,0:T(8,128)(2,1)S(1)}, bf16[2,128,512]{2,1,0:T(8,128)(2,1)S(1)}, u32[]{:S(2)}, u32[]{:S(2)}) %collective-permute-start.2) | collective-permute-done | bytes 262176 | tf_op jit(solution)/shard_map/ppermute | solution.py:106
  28.1 6.1 %collective-permute-done.3 = bf16[1,1024,128]{2,1,0:T(8,128)(2,1)S(1)} collective-permute-done((bf16[1,1024,128]{2,1,0:T(8,128)(2,1)}, bf16[1,1024,128]{2,1,0:T(8,128)(2,1)S(1)}, u32[]{:S(2)}, u32[]{:S(2)}) %collective-permute-start.3) | collective-permute-done | bytes 262176 | tf_op jit(solution)/shard_map/ppermute | solution.py:106
  38.8 22.8 %collective-permute-done.8.refs_2_.refs_11_ = bf16[256,2176]{1,0:T(8,128)(2,1)S(1)} collective-permute-done((bf16[256,2176]{1,0:T(8,128)(2,1)S(1)}, bf16[256,2176]{1,0:T(8,128)(2,1)S(1)}, u32[]{:S(2)}, u32[]{:S(2)}) %collective-permute-start.8) | collective-permute-done | bytes 1114144 | tf_op jit(solution)/shard_map/ppermute | solution.py:106
  64.3 3.2 %collective-permute-start.19 = (bf16[2,1024,128]{2,1,0:T(8,128)(2,1)S(1)}, bf16[2,1024,128]{2,1,0:T(8,128)(2,1)S(1)}, u32[]{:S(2)}, u32[]{:S(2)}) collective-permute-start(bf16[2,1024,128]{2,1,0:T(8,128)(2,1)S(1)} %pad_maximum_fusion.2.refs_5_), channel_id=1, source_target_pairs={{0,16},{2,18},{4,20},{6,22},{8,24},{10,26},{12,28},{14,30},{16,0},... | collective-permute-start | bytes 1572872 | tf_op jit(solution)/shard_map/ppermute | solution.py:106
  67.5 7.8 %collective-permute-done.10.refs_4_ = bf16[128,2176]{1,0:T(8,128)(2,1)S(1)} collective-permute-done((bf16[128,2176]{1,0:T(8,128)(2,1)S(1)}, bf16[128,2176]{1,0:T(8,128)(2,1)S(1)}, u32[]{:S(2)}, u32[]{:S(2)}) %collective-permute-start.10) | collective-permute-done | bytes 557088 | tf_op jit(solution)/shard_map/ppermute | solution.py:106
  76.1 3.8 %project.1 = (bf16[1024,256]{1,0:T(8,128)(2,1)S(1)}, bf16[1024,128]{1,0:T(8,128)(2,1)S(1)}, bf16[1024,128]{1,0:T(8,128)(2,1)S(1)}, bf16[1024,128]{1,0:T(8,128)(2,1)S(1)}) custom-call(s32[4]{0:T(128)S(1)} %copy-done, bf16[256,2176]{1,0:T(8,128)(2,1)S(1)} %constant_dynamic-update-slice_fusion.refs_0_.refs_9_, ...), custom_call_target="tpu_custom_call" | custom-call | bytes 6553616 | tf_op jit(solution)/shard_map/project/pallas_call | solution.py:374
  80.6 1.7 %collective-permute-done.15.refs_3_ = bf16[1024,128]{1,0:T(8,128)(2,1)S(1)} collective-permute-done((bf16[1024,128]{1,0:T(8,128)(2,1)S(1)}, bf16[1024,128]{1,0:T(8,128)(2,1)S(1)}, u32[]{:S(2)}, u32[]{:S(2)}) %collective-permute-start.15) | collective-permute-done | bytes 262176 | tf_op jit(solution)/shard_map/ppermute | solution.py:110
  82.6 3.4 %attend.1 = bf16[4,4,64,128]{3,2,1,0:T(8,128)(2,1)S(1)} custom-call(bf16[1024,256]{1,0:T(8,128)(2,1)S(1)} %get-tuple-element.46.refs_0_, bf16[1024,128]{1,0:T(8,128)(2,1)S(1)} %get-tuple-element.47.refs_1_, bf16[1024,128]{1,0:T(8,128)(2,1)S(1)} %get-tuple-element.48.refs_2_, bf16[1024,128]{1,0:T(8,128)(2,1)S(1)} %collective-permute-done.15.refs_3_, ...), custom_call_target="tpu_custom_call" | custom-call | bytes 1835008 | tf_op jit(solution)/shard_map/attend/pallas_call | solution.py:374
  86.2 3.4 %collective-permute-start.18 = (bf16[4,64,128]{2,1,0:T(8,128)(2,1)S(1)}, bf16[4,64,128]{2,1,0:T(8,128)(2,1)S(1)}, u32[]{:S(2)}, u32[]{:S(2)}) collective-permute-start(bf16[4,64,128]{2,1,0:T(8,128)(2,1)S(1)} %get-tuple-element.79), channel_id=1, source_target_pairs={{0,16},{2,18},{4,20},{6,22},{8,24},{10,26},{12,28},{14,30},{16,0},... | collective-permute-start | bytes 196616 | tf_op jit(solution)/shard_map/ppermute | solution.py:106
  89.6 1.7 %collective-permute-done.19.refs_6_ = bf16[2,1024,128]{2,1,0:T(8,128)(2,1)S(1)} collective-permute-done((bf16[2,1024,128]{2,1,0:T(8,128)(2,1)S(1)}, bf16[2,1024,128]{2,1,0:T(8,128)(2,1)S(1)}, u32[]{:S(2)}, u32[]{:S(2)}) %collective-permute-start.19) | collective-permute-done | bytes 524320 | tf_op jit(solution)/shard_map/ppermute | solution.py:106
  91.3 4.7 %collective-permute-start.21 = (bf16[4,64,128]{2,1,0:T(8,128)(2,1)S(1)}, bf16[4,64,128]{2,1,0:T(8,128)(2,1)S(1)}, u32[]{:S(2)}, u32[]{:S(2)}) collective-permute-start(bf16[4,64,128]{2,1,0:T(8,128)(2,1)S(1)} %get-tuple-element.53), channel_id=1, source_target_pairs={{0,24},{2,26},{4,28},{6,30},{8,16},{10,18},{12,20},{14,22},{16,8},... | collective-permute-start | bytes 196616 | tf_op jit(solution)/shard_map/ppermute | solution.py:106
  96.0 2.2 %collective-permute-done.21 = bf16[4,64,128]{2,1,0:T(8,128)(2,1)S(1)} collective-permute-done((bf16[4,64,128]{2,1,0:T(8,128)(2,1)S(1)}, bf16[4,64,128]{2,1,0:T(8,128)(2,1)S(1)}, u32[]{:S(2)}, u32[]{:S(2)}) %collective-permute-start.21) | collective-permute-done | bytes 65568 | tf_op jit(solution)/shard_map/ppermute | solution.py:106
  99.2 7.9 %collective-permute-done.22.refs_1_ = bf16[4,4,64,128]{3,2,1,0:T(8,128)(2,1)S(1)} collective-permute-done((bf16[4,4,64,128]{3,2,1,0:T(8,128)(2,1)S(1)}, bf16[4,4,64,128]{3,2,1,0:T(8,128)(2,1)S(1)}, u32[]{:S(2)}, u32[]{:S(2)}) %collective-permute-start.22) | collective-permute-done | bytes 262176 | tf_op jit(solution)/shard_map/ppermute | solution.py:106
  109.0 3.2 %collective-permute-done.24.refs_3_ = bf16[2,4,64,128]{3,2,1,0:T(8,128)(2,1)S(1)} collective-permute-done((bf16[2,4,64,128]{3,2,1,0:T(8,128)(2,1)S(1)}, bf16[2,4,64,128]{3,2,1,0:T(8,128)(2,1)S(1)}, u32[]{:S(2)}, u32[]{:S(2)}) %collective-permute-start.24) | collective-permute-done | bytes 131104 | tf_op jit(solution)/shard_map/ppermute | solution.py:106
  112.4 2.7 %hidden.1.refs_0_ = bf16[4,64,512]{2,1,0:T(8,128)(2,1)S(1)} custom-call(s32[4]{0:T(128)S(1)} %copy-done, bf16[4,4,64,128]{3,2,1,0:T(8,128)(2,1)S(1)} %pad_maximum_fusion.4.refs_0_, bf16[4,4,64,128]{3,2,1,0:T(8,128)(2,1)S(1)} %collective-permute-done.22.refs_1_, bf16[4,4,64,128]{3,2,1,0:T(8,128)(2,1)S(1)} %collective-permute-done.23.refs_2_, ...), custom_call_target="tpu_custom_call" | custom-call | flops 536870912 | bytes 7045136 | tf_op jit(solution)/shard_map/hidden/pallas_call | solution.py:374
  117.6 6.5 %collective-permute-done.32 = bf16[128,1152]{1,0:T(8,128)(2,1)S(1)} collective-permute-done((bf16[128,1152]{1,0:T(8,128)(2,1)S(1)}, bf16[128,1152]{1,0:T(8,128)(2,1)S(1)}, u32[]{:S(2)}, u32[]{:S(2)}) %collective-permute-start.32) | collective-permute-done | bytes 294944 | tf_op jit(solution)/shard_map/ppermute | solution.py:106
  126.9 3.4 %collective-permute-done.29.refs_3_ = bf16[2,64,512]{2,1,0:T(8,128)(2,1)S(1)} collective-permute-done((bf16[2,64,512]{2,1,0:T(8,128)(2,1)S(1)}, bf16[2,64,512]{2,1,0:T(8,128)(2,1)S(1)}, u32[]{:S(2)}, u32[]{:S(2)}) %collective-permute-start.29) | collective-permute-done | bytes 131104 | tf_op jit(solution)/shard_map/ppermute | solution.py:106
  131.1 1.6 %mass.1 = (bf16[64,1024]{1,0:T(8,128)(2,1)S(1)}, bf16[64,1024]{1,0:T(8,128)(2,1)S(1)}, f32[1,64]{1,0:T(1,128)S(1)}, f32[4,1,64]{2,1,0:T(1,128)S(1)}) custom-call(s32[4]{0:T(128)S(1)} %copy-done, bf16[4,64,512]{2,1,0:T(8,128)(2,1)S(1)} %hidden.1.refs_0_, bf16[4,64,512]{2,1,0:T(8,128)(2,1)S(1)} %collective-permute-done.27.refs_1_, ...), custom_call_target="tpu_custom_call" | custom-call | flops 268435456 | bytes 2752528 | tf_op jit(solution)/shard_map/mass/pallas_call | solution.py:374
  134.6 1.8 %collective-permute-start.38 = (f32[1,64]{1,0:T(1,128)S(1)}, f32[1,64]{1,0:T(1,128)S(1)}, u32[]{:S(2)}, u32[]{:S(2)}) collective-permute-start(f32[1,64]{1,0:T(1,128)S(1)} %get-tuple-element.89), channel_id=1, source_target_pairs={{0,6},{2,4},{4,2},{6,0},{8,14},{10,12},{12,10},{14,8},{16,22},{18,... | collective-permute-start | bytes 776 | tf_op jit(solution)/shard_map/ppermute | solution.py:106
  (106 shorter events, 35.9 us)
Async XLA Ops:
  3.7 30.5 %collective-permute-start.4 = (bf16[64,2176]{1,0:T(8,128)(2,1)}, bf16[64,2176]{1,0:T(8,128)(2,1)S(1)}, u32[]{:S(2)}, u32[]{:S(2)}) collective-permute-start(bf16[64,2176]{1,0:T(8,128)(2,1)} %mark.1), channel_id=1, source_target_pairs={{0,8},{2,10},{4,12},{6,14},{8,0},{10,2},{12,4},{14,6},{16,24},{18,... | collective-permute-start | bytes 835592 | tf_op jit(solution)/shard_map/ppermute | solution.py:106
  6.8 27.5 %collective-permute-start.5 = (bf16[64,2176]{1,0:T(8,128)(2,1)}, bf16[64,2176]{1,0:T(8,128)(2,1)S(1)}, u32[]{:S(2)}, u32[]{:S(2)}) collective-permute-start(bf16[64,2176]{1,0:T(8,128)(2,1)} %mark.1), channel_id=1, source_target_pairs={{0,16},{2,18},{4,20},{6,22},{8,24},{10,26},{12,28},{14,30},{16,0},... | collective-permute-start | bytes 835592 | tf_op jit(solution)/shard_map/ppermute | solution.py:106
  9.4 24.9 %collective-permute-start.6 = (bf16[64,2176]{1,0:T(8,128)(2,1)}, bf16[64,2176]{1,0:T(8,128)(2,1)S(1)}, u32[]{:S(2)}, u32[]{:S(2)}) collective-permute-start(bf16[64,2176]{1,0:T(8,128)(2,1)} %mark.1), channel_id=1, source_target_pairs={{0,24},{2,26},{4,28},{6,30},{8,16},{10,18},{12,20},{14,22},{16,8},... | collective-permute-start | bytes 835592 | tf_op jit(solution)/shard_map/ppermute | solution.py:106
  11.9 7.7 %collective-permute-start.1 = (bf16[2,128,512]{2,1,0:T(8,128)(2,1)S(1)}, bf16[2,128,512]{2,1,0:T(8,128)(2,1)}, u32[]{:S(2)}, u32[]{:S(2)}) collective-permute-start(bf16[2,128,512]{2,1,0:T(8,128)(2,1)S(1)} %get-tuple-element.37), channel_id=1, source_target_pairs={{0,4},{2,6},{4,0},{6,2},{8,12},{10,14},{12,8},{14,10},{16,20},{18,... | collective-permute-start | bytes 786440 | tf_op jit(solution)/shard_map/ppermute | solution.py:106
  20.8 7.3 %collective-permute-start.2 = (bf16[2,128,512]{2,1,0:T(8,128)(2,1)S(1)}, bf16[2,128,512]{2,1,0:T(8,128)(2,1)S(1)}, u32[]{:S(2)}, u32[]{:S(2)}) collective-permute-start(bf16[2,128,512]{2,1,0:T(8,128)(2,1)S(1)} %get-tuple-element.38), channel_id=1, source_target_pairs={{0,6},{2,4},{4,2},{6,0},{8,14},{10,12},{12,10},{14,8},{16,22},{18,... | collective-permute-start | bytes 786440 | tf_op jit(solution)/shard_map/ppermute | solution.py:106
  22.2 11.9 %collective-permute-start.3 = (bf16[1,1024,128]{2,1,0:T(8,128)(2,1)}, bf16[1,1024,128]{2,1,0:T(8,128)(2,1)S(1)}, u32[]{:S(2)}, u32[]{:S(2)}) collective-permute-start(bf16[1,1024,128]{2,1,0:T(8,128)(2,1)} %bitcast.66), channel_id=1, source_target_pairs={{0,8},{2,10},{4,12},{6,14},{8,0},{10,2},{12,4},{14,6},{16,24},{18,... | collective-permute-start | bytes 786440 | tf_op jit(solution)/shard_map/ppermute | solution.py:106
  35.3 26.4 %collective-permute-start.8 = (bf16[256,2176]{1,0:T(8,128)(2,1)S(1)}, bf16[256,2176]{1,0:T(8,128)(2,1)S(1)}, u32[]{:S(2)}, u32[]{:S(2)}) collective-permute-start(bf16[256,2176]{1,0:T(8,128)(2,1)S(1)} %constant_dynamic-update-slice_fusion.refs_0_.refs_9_), channel_id=1, source_target_pairs={{0,4},{2,6},{4,0},{6,2},{8,12},{10,14},{12,8},{14,10},{16,20},{18,... | collective-permute-start | bytes 3342344 | tf_op jit(solution)/shard_map/ppermute | solution.py:106
  36.8 26.0 %collective-permute-start.7 = (bf16[256,2176]{1,0:T(8,128)(2,1)S(1)}, bf16[256,2176]{1,0:T(8,128)(2,1)S(1)}, u32[]{:S(2)}, u32[]{:S(2)}) collective-permute-start(bf16[256,2176]{1,0:T(8,128)(2,1)S(1)} %constant_dynamic-update-slice_fusion.refs_0_.refs_9_), channel_id=1, source_target_pairs={{0,2},{2,0},{4,6},{6,4},{8,10},{10,8},{12,14},{14,12},{16,18},{18,... | collective-permute-start | bytes 3342344 | tf_op jit(solution)/shard_map/ppermute | solution.py:106
  37.8 26.0 %collective-permute-start.11 = (bf16[512,512]{1,0:T(8,128)(2,1)S(1)}, bf16[512,512]{1,0:T(8,128)(2,1)S(1)}, u32[]{:S(2)}, u32[]{:S(2)}) collective-permute-start(bf16[512,512]{1,0:T(8,128)(2,1)S(1)} %get-tuple-element.44), channel_id=1, source_target_pairs={{0,0},{1,16},{2,2},{3,18},{4,4},{5,20},{6,6},{7,22},{8,8},{9,24},{... | collective-permute-start | bytes 1572872 | tf_op jit(solution)/shard_map/ppermute | solution.py:152
  38.7 25.1 %collective-permute-start.12 = (bf16[512,512]{1,0:T(8,128)(2,1)S(1)}, bf16[512,512]{1,0:T(8,128)(2,1)S(1)}, u32[]{:S(2)}, u32[]{:S(2)}) collective-permute-start(bf16[512,512]{1,0:T(8,128)(2,1)S(1)} %get-tuple-element.45), channel_id=1, source_target_pairs={{0,8},{1,24},{2,10},{3,26},{4,12},{5,28},{6,14},{7,30},{8,0},{9,16... | collective-permute-start | bytes 1572872 | tf_op jit(solution)/shard_map/ppermute | solution.py:152
  61.7 13.6 %collective-permute-start.10 = (bf16[128,2176]{1,0:T(8,128)(2,1)S(1)}, bf16[128,2176]{1,0:T(8,128)(2,1)S(1)}, u32[]{:S(2)}, u32[]{:S(2)}) collective-permute-start(bf16[128,2176]{1,0:T(8,128)(2,1)S(1)} %slice.57), channel_id=1, source_target_pairs={{0,2},{2,0},{4,6},{6,4},{8,10},{10,8},{12,14},{14,12},{16,18},{18,... | collective-permute-start | bytes 1671176 | tf_op jit(solution)/shard_map/ppermute | solution.py:106
  62.9 13.2 %collective-permute-start.9 = (bf16[128,2176]{1,0:T(8,128)(2,1)S(1)}, bf16[128,2176]{1,0:T(8,128)(2,1)S(1)}, u32[]{:S(2)}, u32[]{:S(2)}) collective-permute-start(bf16[128,2176]{1,0:T(8,128)(2,1)S(1)} %slice.56), channel_id=1, source_target_pairs={{0,4},{2,6},{4,0},{6,2},{8,12},{10,14},{12,8},{14,10},{16,20},{18,... | collective-permute-start | bytes 1671176 | tf_op jit(solution)/shard_map/ppermute | solution.py:106
  64.3 27.0 %collective-permute-start.19 = (bf16[2,1024,128]{2,1,0:T(8,128)(2,1)S(1)}, bf16[2,1024,128]{2,1,0:T(8,128)(2,1)S(1)}, u32[]{:S(2)}, u32[]{:S(2)}) collective-permute-start(bf16[2,1024,128]{2,1,0:T(8,128)(2,1)S(1)} %pad_maximum_fusion.2.refs_5_), channel_id=1, source_target_pairs={{0,16},{2,18},{4,20},{6,22},{8,24},{10,26},{12,28},{14,30},{16,0},... | collective-permute-start | bytes 1572872 | tf_op jit(solution)/shard_map/ppermute | solution.py:106
  79.9 11.4 %collective-permute-start.20 = (bf16[2,1024,128]{2,1,0:T(8,128)(2,1)S(1)}, bf16[2,1024,128]{2,1,0:T(8,128)(2,1)S(1)}, u32[]{:S(2)}, u32[]{:S(2)}) collective-permute-start(bf16[2,1024,128]{2,1,0:T(8,128)(2,1)S(1)} %pad_maximum_fusion.2.refs_5_), channel_id=1, source_target_pairs={{0,1},{1,0},{2,3},{3,2},{4,5},{5,4},{6,7},{7,6},{8,9},{9,8},{10,11... | collective-permute-start | bytes 1572872 | tf_op jit(solution)/shard_map/ppermute | solution.py:110
  86.1 9.9 %collective-permute-start.17 = (bf16[4,64,128]{2,1,0:T(8,128)(2,1)S(1)}, bf16[4,64,128]{2,1,0:T(8,128)(2,1)S(1)}, u32[]{:S(2)}, u32[]{:S(2)}) collective-permute-start(bf16[4,64,128]{2,1,0:T(8,128)(2,1)S(1)} %get-tuple-element.80), channel_id=1, source_target_pairs={{0,8},{2,10},{4,12},{6,14},{8,0},{10,2},{12,4},{14,6},{16,24},{18,... | collective-permute-start | bytes 196616 | tf_op jit(solution)/shard_map/ppermute | solution.py:106
  86.2 9.8 %collective-permute-start.18 = (bf16[4,64,128]{2,1,0:T(8,128)(2,1)S(1)}, bf16[4,64,128]{2,1,0:T(8,128)(2,1)S(1)}, u32[]{:S(2)}, u32[]{:S(2)}) collective-permute-start(bf16[4,64,128]{2,1,0:T(8,128)(2,1)S(1)} %get-tuple-element.79), channel_id=1, source_target_pairs={{0,16},{2,18},{4,20},{6,22},{8,24},{10,26},{12,28},{14,30},{16,0},... | collective-permute-start | bytes 196616 | tf_op jit(solution)/shard_map/ppermute | solution.py:106
  98.3 14.2 %collective-permute-start.26 = (bf16[2,1024,128]{2,1,0:T(8,128)(2,1)S(1)}, bf16[2,1024,128]{2,1,0:T(8,128)(2,1)S(1)}, u32[]{:S(2)}, u32[]{:S(2)}) collective-permute-start(bf16[2,1024,128]{2,1,0:T(8,128)(2,1)S(1)} %collective-permute-done.19.refs_6_), channel_id=1, source_target_pairs={{0,1},{1,0},{2,3},{3,2},{4,5},{5,4},{6,7},{7,6},{8,9},{9,8},{10,11... | collective-permute-start | bytes 1572872 | tf_op jit(solution)/shard_map/ppermute | solution.py:110
  98.3 8.7 %collective-permute-start.22 = (bf16[4,4,64,128]{3,2,1,0:T(8,128)(2,1)S(1)}, bf16[4,4,64,128]{3,2,1,0:T(8,128)(2,1)S(1)}, u32[]{:S(2)}, u32[]{:S(2)}) collective-permute-start(bf16[4,4,64,128]{3,2,1,0:T(8,128)(2,1)S(1)} %pad_maximum_fusion.4.refs_0_), channel_id=1, source_target_pairs={{0,2},{2,0},{4,6},{6,4},{8,10},{10,8},{12,14},{14,12},{16,18},{18,... | collective-permute-start | bytes 786440 | tf_op jit(solution)/shard_map/ppermute | solution.py:106
  99.0 8.4 %collective-permute-start.23 = (bf16[4,4,64,128]{3,2,1,0:T(8,128)(2,1)S(1)}, bf16[4,4,64,128]{3,2,1,0:T(8,128)(2,1)S(1)}, u32[]{:S(2)}, u32[]{:S(2)}) collective-permute-start(bf16[4,4,64,128]{3,2,1,0:T(8,128)(2,1)S(1)} %pad_maximum_fusion.4.refs_0_), channel_id=1, source_target_pairs={{0,4},{2,6},{4,0},{6,2},{8,12},{10,14},{12,8},{14,10},{16,20},{18,... | collective-permute-start | bytes 786440 | tf_op jit(solution)/shard_map/ppermute | solution.py:106
  99.2 9.7 %collective-permute-start.31 = (bf16[64,1152]{1,0:T(8,128)(2,1)S(1)}, bf16[64,1152]{1,0:T(8,128)(2,1)S(1)}, u32[]{:S(2)}, u32[]{:S(2)}) collective-permute-start(bf16[64,1152]{1,0:T(8,128)(2,1)S(1)} %fusion.1), channel_id=1, source_target_pairs={{0,8},{2,10},{4,12},{6,14},{8,0},{10,2},{12,4},{14,6},{16,24},{18,... | collective-permute-start | bytes 442376 | tf_op jit(solution)/shard_map/ppermute | solution.py:106
  99.2 18.4 %collective-permute-start.33 = (bf16[64,1024]{1,0:T(8,128)(2,1)S(1)}, bf16[64,1024]{1,0:T(8,128)(2,1)S(1)}, u32[]{:S(2)}, u32[]{:S(2)}) collective-permute-start(bf16[64,1024]{1,0:T(8,128)(2,1)S(1)} %get-tuple-element.61), channel_id=1, source_target_pairs={{0,1},{1,0},{2,3},{3,2},{4,5},{5,4},{6,7},{7,6},{8,9},{9,8},{10,11... | collective-permute-start | bytes 393224 | tf_op jit(solution)/shard_map/ppermute | solution.py:110
  108.9 15.3 %collective-permute-start.32 = (bf16[128,1152]{1,0:T(8,128)(2,1)S(1)}, bf16[128,1152]{1,0:T(8,128)(2,1)S(1)}, u32[]{:S(2)}, u32[]{:S(2)}) collective-permute-start(bf16[128,1152]{1,0:T(8,128)(2,1)S(1)} %pad_maximum_fusion.3), channel_id=1, source_target_pairs={{0,16},{2,18},{4,20},{6,22},{8,24},{10,26},{12,28},{14,30},{16,0},... | collective-permute-start | bytes 884744 | tf_op jit(solution)/shard_map/ppermute | solution.py:106
  115.1 9.0 %collective-permute-start.27 = (bf16[4,64,512]{2,1,0:T(8,128)(2,1)S(1)}, bf16[4,64,512]{2,1,0:T(8,128)(2,1)S(1)}, u32[]{:S(2)}, u32[]{:S(2)}) collective-permute-start(bf16[4,64,512]{2,1,0:T(8,128)(2,1)S(1)} %hidden.1.refs_0_), channel_id=1, source_target_pairs={{0,2},{2,0},{4,6},{6,4},{8,10},{10,8},{12,14},{14,12},{16,18},{18,... | collective-permute-start | bytes 786440 | tf_op jit(solution)/shard_map/ppermute | solution.py:106
  116.6 7.5 %collective-permute-start.28 = (bf16[4,64,512]{2,1,0:T(8,128)(2,1)S(1)}, bf16[4,64,512]{2,1,0:T(8,128)(2,1)S(1)}, u32[]{:S(2)}, u32[]{:S(2)}) collective-permute-start(bf16[4,64,512]{2,1,0:T(8,128)(2,1)S(1)} %hidden.1.refs_0_), channel_id=1, source_target_pairs={{0,4},{2,6},{4,0},{6,2},{8,12},{10,14},{12,8},{14,10},{16,20},{18,... | collective-permute-start | bytes 786440 | tf_op jit(solution)/shard_map/ppermute | solution.py:106
  (20 other events, 146.5 us)

commit v20 on v18

--- a/solution.py
+++ b/solution.py
@@ -120,6 +120,18 @@
 
 def pair_up(own):
     return jnp.concatenate([own, hop(own, flip(0, 0, 1))])
+
+
+def is_inner(z):
+    return ((z + 1) // 2) % 2 == 1
+
+
+def inner_hop(pair):
+    return hop(pair, [(c, relative_chip(c, 0, 0, 3)) for c in range(CHIPS) if is_inner(coords(c)[0])])
+
+
+def outer_hop(pair):
+    return hop(pair, [(c, relative_chip(c, 0, 0, 1)) for c in range(CHIPS) if is_inner(coords(c)[0])])
 
 
 def across(value_x, value_y):
@@ -270,12 +282,14 @@
     c = chip_at(z, y, x)
     rows = hidden.shape[1]
     half = w_all.shape[1]
+    flipped = ((z + 1) // 2) % 2
     copies = [(src, g_raw.at[k]) for k, src in enumerate(gated[:3])]
     copies += [(src, g_raw.at[3, pl.ds(2 * i, 2)]) for i, src in enumerate(gated[3:])]
     for s in range(NZ):
         cols = pl.ds(s * W, W)
         for side, src in enumerate((w_own, w_other)):
-            copies.append((src[s // 2].at[s % 2], w_all.at[side, :, cols]))
+            panel = src[0].at[s] if s < 2 else src[1].at[(s % 2) ^ flipped]
+            copies.append((panel, w_all.at[side, :, cols]))
         block = relative_chip(c, 0, 0, s)
         from_cols = pl.ds(pl.multiple_of(block * W, W), W)
         for k in range(n):
@@ -451,7 +465,7 @@
     tok = [near, near_x, near_y, *across(near_x, near_y)]
     w_mine = heads_along_z(w_pieces)
     w_theirs = [swap_cores(w) for w in w_mine]
-    out_own = [out_pair, hop(after(out_pair, w_mine), flip(0, 0, 2))]
+    out_met = inner_hop(after(out_pair, w_mine))
     t_send = swap_cores(after(t_mine, w_theirs))
 
     def project(pieces):
@@ -485,12 +499,15 @@
         0,
     )
     hops = [hop(gated[s], flip(0, 0, s)) for s in (1, 2)]
-    out_own, out_pair_theirs, last = lax.optimization_barrier((out_own, out_pair_theirs, gated[3]))
+    out_met, out_pair_theirs, last = lax.optimization_barrier((out_met, out_pair_theirs, gated[3]))
     gated = jnp.stack([gated[0], *hops, hop(last, flip(0, 0, 3))])
     neg_pair = pair_up(after(neg, gated))
     neg_far = hop(neg_pair, flip(0, 0, 2))
-    out_other = [out_pair_theirs, swap_cores(after(out_own[1], gated))]
+    out_passed = outer_hop(after(out_met, gated))
     gated = [gated, hop(gated, to_x), hop(gated, to_y)]
+    out_passed = after(out_passed, gated)
+    out_own = [out_pair, jnp.where(is_inner(z), out_met, out_passed)]
+    out_other = [out_pair_theirs, swap_cores(out_own[1])]
     gated += across(gated[1], gated[2])
     (hidden,) = call(
         hidden_kernel,

time: 141 us -> 151 us (1.071)
  local copies, waits for them, and re-layouts: 8.21 us -> 11.5 us
  starting transfers between devices: 37.1 us -> 39.9 us
  other arithmetic: 1.95 us -> 4.41 us
    ppermute x28 -> x29, starting transfers between devices: 34.4 us -> 37.3 us  [hop(): return lax.ppermute(value, 'ctx', perm)]
    slice x6, local copies, waits for them, and re-layouts: 0.12 us -> 1.92 us  [across(): return [hop(value_x[:half], flip(1, 0)), hop(value_y[half:], flip(0, 1))]]
    unnamed x15 -> x33, local copies, waits for them, and re-layouts: 2.47 us -> 3.3 us
    ppermute x28 -> x29, waiting for transfers between devices: 76.3 us -> 76.8 us  [hop(): return lax.ppermute(value, 'ctx', perm)]
  transfers between devices with their start and end apart: 39 -> 40, of which waited for: 21 -> 22; matrix products, arithmetic and copies ran while one was open for 5% -> 7% of each run, Pallas kernels for 7% -> 7%
where the time goes in v20:
time: 151 us; the launch traced here: 150 us
  waiting for transfers between devices  79.5 us (53%)
  starting transfers between devices  39.9 us (26%)
  Pallas kernels  13.9 us (9%)
  local copies, waits for them, and re-layouts  11.5 us (8%)
  other arithmetic  4.41 us (3%)
    ppermute x29, waiting for transfers between devices, hop(): return lax.ppermute(value, 'ctx', perm)  76.8 us
    ppermute x29, starting transfers between devices, hop(): return lax.ppermute(value, 'ctx', perm)  37.3 us
    pallas_call x6, Pallas kernels, call(): pl.pallas_call(kernel, out_shape=[jax.ShapeDtypeStruct(shape, dtype) for...  13.9 us
    squeeze x6, local copies, waits for them, and re-layouts, pick_row(): return lax.dynamic_index_in_dim(value, at, 0, keepdims=False)  3.72 us
    unnamed x33, local copies, waits for them, and re-layouts  3.3 us
  transfers between devices with their start and end apart: 40, of which 22 were waited for; matrix products, arithmetic and copies ran while one was open for 7% of the time, Pallas kernels for 7%

profile of v20, /device:TPU:0, one launch (start us, length us, event | category | flops | bytes accessed | tf_op | source)
XLA Modules:
  0.0 150.3 jit_solution(2719969125824470370)
XLA Ops:
  3.9 3.1 %collective-permute-start.4 = (bf16[64,2176]{1,0:T(8,128)(2,1)S(1)}, bf16[64,2176]{1,0:T(8,128)(2,1)S(1)}, u32[]{:S(2)}, u32[]{:S(2)}) collective-permute-start(bf16[64,2176]{1,0:T(8,128)(2,1)S(1)} %mark.1), channel_id=1, source_target_pairs={{0,8},{2,10},{4,12},{6,14},{8,0},{10,2},{12,4},{14,6},{16,24},{18,... | collective-permute-start | bytes 835592 | tf_op jit(solution)/shard_map/ppermute | solution.py:106
  7.0 2.6 %collective-permute-start.5 = (bf16[64,2176]{1,0:T(8,128)(2,1)S(1)}, bf16[64,2176]{1,0:T(8,128)(2,1)S(1)}, u32[]{:S(2)}, u32[]{:S(2)}) collective-permute-start(bf16[64,2176]{1,0:T(8,128)(2,1)S(1)} %mark.1), channel_id=1, source_target_pairs={{0,16},{2,18},{4,20},{6,22},{8,24},{10,26},{12,28},{14,30},{16,0},... | collective-permute-start | bytes 835592 | tf_op jit(solution)/shard_map/ppermute | solution.py:106
  12.0 1.8 %collective-permute-start.1 = (bf16[2,128,512]{2,1,0:T(8,128)(2,1)S(1)}, bf16[2,128,512]{2,1,0:T(8,128)(2,1)}, u32[]{:S(2)}, u32[]{:S(2)}) collective-permute-start(bf16[2,128,512]{2,1,0:T(8,128)(2,1)S(1)} %get-tuple-element.37), channel_id=1, source_target_pairs={{0,4},{2,6},{4,0},{6,2},{8,12},{10,14},{12,8},{14,10},{16,20},{18,... | collective-permute-start | bytes 786440 | tf_op jit(solution)/shard_map/ppermute | solution.py:106
  17.8 1.8 %collective-permute-done.1 = bf16[2,128,512]{2,1,0:T(8,128)(2,1)} collective-permute-done((bf16[2,128,512]{2,1,0:T(8,128)(2,1)S(1)}, bf16[2,128,512]{2,1,0:T(8,128)(2,1)}, u32[]{:S(2)}, u32[]{:S(2)}) %collective-permute-start.1) | collective-permute-done | bytes 262176 | tf_op jit(solution)/shard_map/ppermute | solution.py:106
  22.3 1.6 %dynamic-slice_bitcast_fusion.3 = (bf16[64,1024]{1,0:T(8,128)(2,1)}, bf16[64,1024]{1,0:T(8,128)(2,1)S(1)}) fusion(bf16[2,64,1024]{2,1,0:T(8,128)(2,1)} %bitcast.67, s32[]{:T(128)S(6)} %select_n.103, s32[]{:T(128)S(6)} %select_n.102), kind=kLoop, calls=%fused_computation.13 | loop fusion | bytes 524296 | tf_op jit(solution)/shard_map/jit(dynamic_index_in_dim)/squeeze | solution.py:114
  26.6 1.6 %collective-permute-done.2 = bf16[2,128,512]{2,1,0:T(8,128)(2,1)S(1)} collective-permute-done((bf16[2,128,512]{2,1,0:T(8,128)(2,1)S(1)}, bf16[2,128,512]{2,1,0:T(8,128)(2,1)S(1)}, u32[]{:S(2)}, u32[]{:S(2)}) %collective-permute-start.2) | collective-permute-done | bytes 262176 | tf_op jit(solution)/shard_map/ppermute | solution.py:106
  28.2 6.1 %collective-permute-done.3 = bf16[1,1024,128]{2,1,0:T(8,128)(2,1)S(1)} collective-permute-done((bf16[1,1024,128]{2,1,0:T(8,128)(2,1)}, bf16[1,1024,128]{2,1,0:T(8,128)(2,1)S(1)}, u32[]{:S(2)}, u32[]{:S(2)}) %collective-permute-start.3) | collective-permute-done | bytes 262176 | tf_op jit(solution)/shard_map/ppermute | solution.py:106
  38.5 22.4 %collective-permute-done.8.refs_2_.refs_11_ = bf16[256,2176]{1,0:T(8,128)(2,1)S(1)} collective-permute-done((bf16[256,2176]{1,0:T(8,128)(2,1)S(1)}, bf16[256,2176]{1,0:T(8,128)(2,1)S(1)}, u32[]{:S(2)}, u32[]{:S(2)}) %collective-permute-start.8) | collective-permute-done | bytes 1114144 | tf_op jit(solution)/shard_map/ppermute | solution.py:106
  61.0 1.7 %collective-permute-start.10 = (bf16[128,2176]{1,0:T(8,128)(2,1)S(1)}, bf16[128,2176]{1,0:T(8,128)(2,1)S(1)}, u32[]{:S(2)}, u32[]{:S(2)}) collective-permute-start(bf16[128,2176]{1,0:T(8,128)(2,1)S(1)} %slice.57), channel_id=1, source_target_pairs={{0,2},{2,0},{4,6},{6,4},{8,10},{10,8},{12,14},{14,12},{16,18},{18,... | collective-permute-start | bytes 1671176 | tf_op jit(solution)/shard_map/ppermute | solution.py:106
  67.0 7.7 %collective-permute-done.10.refs_4_ = bf16[128,2176]{1,0:T(8,128)(2,1)S(1)} collective-permute-done((bf16[128,2176]{1,0:T(8,128)(2,1)S(1)}, bf16[128,2176]{1,0:T(8,128)(2,1)S(1)}, u32[]{:S(2)}, u32[]{:S(2)}) %collective-permute-start.10) | collective-permute-done | bytes 557088 | tf_op jit(solution)/shard_map/ppermute | solution.py:106
  76.2 3.8 %project.1 = (bf16[1024,256]{1,0:T(8,128)(2,1)S(1)}, bf16[1024,128]{1,0:T(8,128)(2,1)S(1)}, bf16[1024,128]{1,0:T(8,128)(2,1)S(1)}, bf16[1024,128]{1,0:T(8,128)(2,1)S(1)}) custom-call(s32[4]{0:T(128)S(1)} %pad_add_fusion.where, bf16[256,2176]{1,0:T(8,128)(2,1)S(1)} %constant_dynamic-update-slice_fusion.refs_0_.refs_9_, ...), custom_call_target="tpu_custom_call" | custom-call | bytes 6553616 | tf_op jit(solution)/shard_map/project/pallas_call | solution.py:388
  80.8 1.7 %collective-permute-done.15.refs_3_ = bf16[1024,128]{1,0:T(8,128)(2,1)S(1)} collective-permute-done((bf16[1024,128]{1,0:T(8,128)(2,1)S(1)}, bf16[1024,128]{1,0:T(8,128)(2,1)S(1)}, u32[]{:S(2)}, u32[]{:S(2)}) %collective-permute-start.15) | collective-permute-done | bytes 262176 | tf_op jit(solution)/shard_map/ppermute | solution.py:110
  82.8 3.4 %attend.1 = bf16[4,4,64,128]{3,2,1,0:T(8,128)(2,1)S(1)} custom-call(bf16[1024,256]{1,0:T(8,128)(2,1)S(1)} %get-tuple-element.46.refs_0_, bf16[1024,128]{1,0:T(8,128)(2,1)S(1)} %get-tuple-element.47.refs_1_, bf16[1024,128]{1,0:T(8,128)(2,1)S(1)} %get-tuple-element.48.refs_2_, bf16[1024,128]{1,0:T(8,128)(2,1)S(1)} %collective-permute-done.15.refs_3_, ...), custom_call_target="tpu_custom_call" | custom-call | bytes 1835008 | tf_op jit(solution)/shard_map/attend/pallas_call | solution.py:388
  88.5 3.0 %collective-permute-start.21 = (bf16[4,64,128]{2,1,0:T(8,128)(2,1)S(1)}, bf16[4,64,128]{2,1,0:T(8,128)(2,1)S(1)}, u32[]{:S(2)}, u32[]{:S(2)}) collective-permute-start(bf16[4,64,128]{2,1,0:T(8,128)(2,1)S(1)} %get-tuple-element.53), channel_id=1, source_target_pairs={{0,24},{2,26},{4,28},{6,30},{8,16},{10,18},{12,20},{14,22},{16,8},... | collective-permute-start | bytes 196616 | tf_op jit(solution)/shard_map/ppermute | solution.py:106
  91.6 3.3 %collective-permute-done.18 = bf16[4,64,128]{2,1,0:T(8,128)(2,1)S(1)} collective-permute-done((bf16[4,64,128]{2,1,0:T(8,128)(2,1)S(1)}, bf16[4,64,128]{2,1,0:T(8,128)(2,1)S(1)}, u32[]{:S(2)}, u32[]{:S(2)}) %collective-permute-start.18) | collective-permute-done | bytes 65568 | tf_op jit(solution)/shard_map/ppermute | solution.py:106
  99.0 5.3 %collective-permute-done.22.refs_1_ = bf16[4,4,64,128]{3,2,1,0:T(8,128)(2,1)} collective-permute-done((bf16[4,4,64,128]{3,2,1,0:T(8,128)(2,1)}, bf16[4,4,64,128]{3,2,1,0:T(8,128)(2,1)}, u32[]{:S(2)}, u32[]{:S(2)}) %collective-permute-start.22) | collective-permute-done | bytes 262176 | tf_op jit(solution)/shard_map/ppermute | solution.py:106
  105.1 5.3 %collective-permute-done.26 = bf16[2,1024,128]{2,1,0:T(8,128)(2,1)} collective-permute-done((bf16[2,1024,128]{2,1,0:T(8,128)(2,1)}, bf16[2,1024,128]{2,1,0:T(8,128)(2,1)}, u32[]{:S(2)}, u32[]{:S(2)}) %collective-permute-start.26) | collective-permute-done | bytes 524320 | tf_op jit(solution)/shard_map/ppermute | solution.py:106
  115.8 2.2 %collective-permute-done.32 = bf16[64,1152]{1,0:T(8,128)(2,1)S(1)} collective-permute-done((bf16[64,1152]{1,0:T(8,128)(2,1)}, bf16[64,1152]{1,0:T(8,128)(2,1)S(1)}, u32[]{:S(2)}, u32[]{:S(2)}) %collective-permute-start.32) | collective-permute-done | bytes 147488 | tf_op jit(solution)/shard_map/ppermute | solution.py:106
  120.8 3.0 %hidden.1.refs_0_ = bf16[4,64,512]{2,1,0:T(8,128)(2,1)S(1)} custom-call(s32[4]{0:T(128)S(1)} %pad_add_fusion.where, bf16[4,4,64,128]{3,2,1,0:T(8,128)(2,1)} %pad_maximum_fusion.4.refs_0_, bf16[4,4,64,128]{3,2,1,0:T(8,128)(2,1)} %collective-permute-done.22.refs_1_, bf16[4,4,64,128]{3,2,1,0:T(8,128)(2,1)} %collective-permute-done.23.refs_2_, ...), custom_call_target="tpu_custom_call" | custom-call | flops 536870912 | bytes 7045136 | tf_op jit(solution)/shard_map/hidden/pallas_call | solution.py:388
  125.5 8.3 %collective-permute-done.33 = bf16[128,1152]{1,0:T(8,128)(2,1)S(1)} collective-permute-done((bf16[128,1152]{1,0:T(8,128)(2,1)S(1)}, bf16[128,1152]{1,0:T(8,128)(2,1)S(1)}, u32[]{:S(2)}, u32[]{:S(2)}) %collective-permute-start.33) | collective-permute-done | bytes 294944 | tf_op jit(solution)/shard_map/ppermute | solution.py:106
  135.9 4.0 %collective-permute-done.30.refs_3_ = bf16[2,64,512]{2,1,0:T(8,128)(2,1)S(1)} collective-permute-done((bf16[2,64,512]{2,1,0:T(8,128)(2,1)S(1)}, bf16[2,64,512]{2,1,0:T(8,128)(2,1)S(1)}, u32[]{:S(2)}, u32[]{:S(2)}) %collective-permute-start.30) | collective-permute-done | bytes 131104 | tf_op jit(solution)/shard_map/ppermute | solution.py:106
  141.2 1.6 %mass.1 = (bf16[64,1024]{1,0:T(8,128)(2,1)S(1)}, bf16[64,1024]{1,0:T(8,128)(2,1)S(1)}, f32[1,64]{1,0:T(1,128)S(1)}, f32[4,1,64]{2,1,0:T(1,128)S(1)}) custom-call(s32[4]{0:T(128)S(1)} %pad_add_fusion.where, bf16[4,64,512]{2,1,0:T(8,128)(2,1)S(1)} %hidden.1.refs_0_, bf16[4,64,512]{2,1,0:T(8,128)(2,1)S(1)} %collective-permute-done.28.refs_1_, ...), custom_call_target="tpu_custom_call" | custom-call | flops 268435456 | bytes 2752528 | tf_op jit(solution)/shard_map/mass/pallas_call | solution.py:388
  144.6 1.9 %collective-permute-start.39 = (f32[1,64]{1,0:T(1,128)S(1)}, f32[1,64]{1,0:T(1,128)S(1)}, u32[]{:S(2)}, u32[]{:S(2)}) collective-permute-start(f32[1,64]{1,0:T(1,128)S(1)} %get-tuple-element.89), channel_id=1, source_target_pairs={{0,6},{2,4},{4,2},{6,0},{8,14},{10,12},{12,10},{14,8},{16,22},{18,... | collective-permute-start | bytes 776 | tf_op jit(solution)/shard_map/ppermute | solution.py:106
  146.9 2.2 %collective-permute-done.39.refs_3_ = f32[1,64]{1,0:T(1,128)S(1)} collective-permute-done((f32[1,64]{1,0:T(1,128)S(1)}, f32[1,64]{1,0:T(1,128)S(1)}, u32[]{:S(2)}, u32[]{:S(2)}) %collective-permute-start.39) | collective-permute-done | bytes 288 | tf_op jit(solution)/shard_map/ppermute | solution.py:106
  (127 shorter events, 49.8 us)
Async XLA Ops:
  3.9 30.5 %collective-permute-start.4 = (bf16[64,2176]{1,0:T(8,128)(2,1)S(1)}, bf16[64,2176]{1,0:T(8,128)(2,1)S(1)}, u32[]{:S(2)}, u32[]{:S(2)}) collective-permute-start(bf16[64,2176]{1,0:T(8,128)(2,1)S(1)} %mark.1), channel_id=1, source_target_pairs={{0,8},{2,10},{4,12},{6,14},{8,0},{10,2},{12,4},{14,6},{16,24},{18,... | collective-permute-start | bytes 835592 | tf_op jit(solution)/shard_map/ppermute | solution.py:106
  7.0 27.4 %collective-permute-start.5 = (bf16[64,2176]{1,0:T(8,128)(2,1)S(1)}, bf16[64,2176]{1,0:T(8,128)(2,1)S(1)}, u32[]{:S(2)}, u32[]{:S(2)}) collective-permute-start(bf16[64,2176]{1,0:T(8,128)(2,1)S(1)} %mark.1), channel_id=1, source_target_pairs={{0,16},{2,18},{4,20},{6,22},{8,24},{10,26},{12,28},{14,30},{16,0},... | collective-permute-start | bytes 835592 | tf_op jit(solution)/shard_map/ppermute | solution.py:106
  9.6 24.9 %collective-permute-start.6 = (bf16[64,2176]{1,0:T(8,128)(2,1)S(1)}, bf16[64,2176]{1,0:T(8,128)(2,1)S(1)}, u32[]{:S(2)}, u32[]{:S(2)}) collective-permute-start(bf16[64,2176]{1,0:T(8,128)(2,1)S(1)} %mark.1), channel_id=1, source_target_pairs={{0,24},{2,26},{4,28},{6,30},{8,16},{10,18},{12,20},{14,22},{16,8},... | collective-permute-start | bytes 835592 | tf_op jit(solution)/shard_map/ppermute | solution.py:106
  12.0 7.7 %collective-permute-start.1 = (bf16[2,128,512]{2,1,0:T(8,128)(2,1)S(1)}, bf16[2,128,512]{2,1,0:T(8,128)(2,1)}, u32[]{:S(2)}, u32[]{:S(2)}) collective-permute-start(bf16[2,128,512]{2,1,0:T(8,128)(2,1)S(1)} %get-tuple-element.37), channel_id=1, source_target_pairs={{0,4},{2,6},{4,0},{6,2},{8,12},{10,14},{12,8},{14,10},{16,20},{18,... | collective-permute-start | bytes 786440 | tf_op jit(solution)/shard_map/ppermute | solution.py:106
  13.8 7.1 %collective-permute-start = (bf16[2,128,512]{2,1,0:T(8,128)(2,1)S(1)}, bf16[2,128,512]{2,1,0:T(8,128)(2,1)}, u32[]{:S(2)}, u32[]{:S(2)}) collective-permute-start(bf16[2,128,512]{2,1,0:T(8,128)(2,1)S(1)} %get-tuple-element.36), channel_id=1, source_target_pairs={{0,2},{2,0},{4,6},{6,4},{8,10},{10,8},{12,14},{14,12},{16,18},{18,... | collective-permute-start | bytes 786440 | tf_op jit(solution)/shard_map/ppermute | solution.py:106
  20.9 7.3 %collective-permute-start.2 = (bf16[2,128,512]{2,1,0:T(8,128)(2,1)S(1)}, bf16[2,128,512]{2,1,0:T(8,128)(2,1)S(1)}, u32[]{:S(2)}, u32[]{:S(2)}) collective-permute-start(bf16[2,128,512]{2,1,0:T(8,128)(2,1)S(1)} %get-tuple-element.38), channel_id=1, source_target_pairs={{0,6},{2,4},{4,2},{6,0},{8,14},{10,12},{12,10},{14,8},{16,22},{18,... | collective-permute-start | bytes 786440 | tf_op jit(solution)/shard_map/ppermute | solution.py:106
  24.0 10.3 %collective-permute-start.3 = (bf16[1,1024,128]{2,1,0:T(8,128)(2,1)}, bf16[1,1024,128]{2,1,0:T(8,128)(2,1)S(1)}, u32[]{:S(2)}, u32[]{:S(2)}) collective-permute-start(bf16[1,1024,128]{2,1,0:T(8,128)(2,1)} %bitcast.68), channel_id=1, source_target_pairs={{0,8},{2,10},{4,12},{6,14},{8,0},{10,2},{12,4},{14,6},{16,24},{18,... | collective-permute-start | bytes 786440 | tf_op jit(solution)/shard_map/ppermute | solution.py:106
  34.5 26.4 %collective-permute-start.8 = (bf16[256,2176]{1,0:T(8,128)(2,1)S(1)}, bf16[256,2176]{1,0:T(8,128)(2,1)S(1)}, u32[]{:S(2)}, u32[]{:S(2)}) collective-permute-start(bf16[256,2176]{1,0:T(8,128)(2,1)S(1)} %constant_dynamic-update-slice_fusion.refs_0_.refs_9_), channel_id=1, source_target_pairs={{0,4},{2,6},{4,0},{6,2},{8,12},{10,14},{12,8},{14,10},{16,20},{18,... | collective-permute-start | bytes 3342344 | tf_op jit(solution)/shard_map/ppermute | solution.py:106
  36.1 26.6 %collective-permute-start.7 = (bf16[256,2176]{1,0:T(8,128)(2,1)S(1)}, bf16[256,2176]{1,0:T(8,128)(2,1)S(1)}, u32[]{:S(2)}, u32[]{:S(2)}) collective-permute-start(bf16[256,2176]{1,0:T(8,128)(2,1)S(1)} %constant_dynamic-update-slice_fusion.refs_0_.refs_9_), channel_id=1, source_target_pairs={{0,2},{2,0},{4,6},{6,4},{8,10},{10,8},{12,14},{14,12},{16,18},{18,... | collective-permute-start | bytes 3342344 | tf_op jit(solution)/shard_map/ppermute | solution.py:106
  37.6 26.7 %collective-permute-start.11 = (bf16[512,512]{1,0:T(8,128)(2,1)S(1)}, bf16[512,512]{1,0:T(8,128)(2,1)S(1)}, u32[]{:S(2)}, u32[]{:S(2)}) collective-permute-start(bf16[512,512]{1,0:T(8,128)(2,1)S(1)} %get-tuple-element.44), channel_id=1, source_target_pairs={{0,0},{1,16},{2,2},{3,18},{4,4},{5,20},{6,6},{7,22},{8,8},{9,24},{... | collective-permute-start | bytes 1572872 | tf_op jit(solution)/shard_map/ppermute | solution.py:164
  38.3 26.0 %collective-permute-start.12 = (bf16[512,512]{1,0:T(8,128)(2,1)S(1)}, bf16[512,512]{1,0:T(8,128)(2,1)S(1)}, u32[]{:S(2)}, u32[]{:S(2)}) collective-permute-start(bf16[512,512]{1,0:T(8,128)(2,1)S(1)} %get-tuple-element.45), channel_id=1, source_target_pairs={{0,8},{1,24},{2,10},{3,26},{4,12},{5,28},{6,14},{7,30},{8,0},{9,16... | collective-permute-start | bytes 1572872 | tf_op jit(solution)/shard_map/ppermute | solution.py:164
  61.0 13.7 %collective-permute-start.10 = (bf16[128,2176]{1,0:T(8,128)(2,1)S(1)}, bf16[128,2176]{1,0:T(8,128)(2,1)S(1)}, u32[]{:S(2)}, u32[]{:S(2)}) collective-permute-start(bf16[128,2176]{1,0:T(8,128)(2,1)S(1)} %slice.57), channel_id=1, source_target_pairs={{0,2},{2,0},{4,6},{6,4},{8,10},{10,8},{12,14},{14,12},{16,18},{18,... | collective-permute-start | bytes 1671176 | tf_op jit(solution)/shard_map/ppermute | solution.py:106
  62.7 13.5 %collective-permute-start.9 = (bf16[128,2176]{1,0:T(8,128)(2,1)S(1)}, bf16[128,2176]{1,0:T(8,128)(2,1)S(1)}, u32[]{:S(2)}, u32[]{:S(2)}) collective-permute-start(bf16[128,2176]{1,0:T(8,128)(2,1)S(1)} %slice.56), channel_id=1, source_target_pairs={{0,4},{2,6},{4,0},{6,2},{8,12},{10,14},{12,8},{14,10},{16,20},{18,... | collective-permute-start | bytes 1671176 | tf_op jit(solution)/shard_map/ppermute | solution.py:106
  64.8 22.9 %collective-permute-start.19 = (bf16[2,1024,128]{2,1,0:T(8,128)(2,1)S(1)}, bf16[2,1024,128]{2,1,0:T(8,128)(2,1)}, u32[]{:S(2)}, u32[]{:S(2)}) collective-permute-start(bf16[2,1024,128]{2,1,0:T(8,128)(2,1)S(1)} %pad_maximum_fusion.2.refs_5_), channel_id=1, source_target_pairs={{8,16},{10,18},{12,20},{14,22},{16,8},{18,10},{20,12},{22,14},{9,1... | collective-permute-start | bytes 1572872 | tf_op jit(solution)/shard_map/ppermute | solution.py:106
  80.1 7.6 %collective-permute-start.20 = (bf16[2,1024,128]{2,1,0:T(8,128)(2,1)S(1)}, bf16[2,1024,128]{2,1,0:T(8,128)(2,1)S(1)}, u32[]{:S(2)}, u32[]{:S(2)}) collective-permute-start(bf16[2,1024,128]{2,1,0:T(8,128)(2,1)S(1)} %pad_maximum_fusion.2.refs_5_), channel_id=1, source_target_pairs={{0,1},{1,0},{2,3},{3,2},{4,5},{5,4},{6,7},{7,6},{8,9},{9,8},{10,11... | collective-permute-start | bytes 1572872 | tf_op jit(solution)/shard_map/ppermute | solution.py:110
  86.4 8.6 %collective-permute-start.18 = (bf16[4,64,128]{2,1,0:T(8,128)(2,1)S(1)}, bf16[4,64,128]{2,1,0:T(8,128)(2,1)S(1)}, u32[]{:S(2)}, u32[]{:S(2)}) collective-permute-start(bf16[4,64,128]{2,1,0:T(8,128)(2,1)S(1)} %get-tuple-element.79), channel_id=1, source_target_pairs={{0,16},{2,18},{4,20},{6,22},{8,24},{10,26},{12,28},{14,30},{16,0},... | collective-permute-start | bytes 196616 | tf_op jit(solution)/shard_map/ppermute | solution.py:106
  95.7 14.7 %collective-permute-start.26 = (bf16[2,1024,128]{2,1,0:T(8,128)(2,1)}, bf16[2,1024,128]{2,1,0:T(8,128)(2,1)}, u32[]{:S(2)}, u32[]{:S(2)}) collective-permute-start(bf16[2,1024,128]{2,1,0:T(8,128)(2,1)} %collective-permute-done.19), channel_id=1, source_target_pairs={{8,0},{10,2},{12,4},{14,6},{16,24},{18,26},{20,28},{22,30},{9,1},{... | collective-permute-start | bytes 1572872 | tf_op jit(solution)/shard_map/ppermute | solution.py:106
  97.1 7.2 %collective-permute-start.22 = (bf16[4,4,64,128]{3,2,1,0:T(8,128)(2,1)}, bf16[4,4,64,128]{3,2,1,0:T(8,128)(2,1)}, u32[]{:S(2)}, u32[]{:S(2)}) collective-permute-start(bf16[4,4,64,128]{3,2,1,0:T(8,128)(2,1)} %pad_maximum_fusion.4.refs_0_), channel_id=1, source_target_pairs={{0,2},{2,0},{4,6},{6,4},{8,10},{10,8},{12,14},{14,12},{16,18},{18,... | collective-permute-start | bytes 786440 | tf_op jit(solution)/shard_map/ppermute | solution.py:106
  111.5 9.3 %collective-permute-start.27 = (bf16[2,1024,128]{2,1,0:T(8,128)(2,1)S(1)}, bf16[2,1024,128]{2,1,0:T(8,128)(2,1)S(1)}, u32[]{:S(2)}, u32[]{:S(2)}) collective-permute-start(bf16[2,1024,128]{2,1,0:T(8,128)(2,1)S(1)} %broadcast_select_fusion.refs_6_), channel_id=1, source_target_pairs={{0,1},{1,0},{2,3},{3,2},{4,5},{5,4},{6,7},{7,6},{8,9},{9,8},{10,11... | collective-permute-start | bytes 1572872 | tf_op jit(solution)/shard_map/ppermute | solution.py:110
  111.6 13.9 %collective-permute-start.34 = (bf16[64,1024]{1,0:T(8,128)(2,1)}, bf16[64,1024]{1,0:T(8,128)(2,1)S(1)}, u32[]{:S(2)}, u32[]{:S(2)}) collective-permute-start(bf16[64,1024]{1,0:T(8,128)(2,1)} %get-tuple-element.61), channel_id=1, source_target_pairs={{0,1},{1,0},{2,3},{3,2},{4,5},{5,4},{6,7},{7,6},{8,9},{9,8},{10,11... | collective-permute-start | bytes 393224 | tf_op jit(solution)/shard_map/ppermute | solution.py:110
  118.1 15.8 %collective-permute-start.33 = (bf16[128,1152]{1,0:T(8,128)(2,1)S(1)}, bf16[128,1152]{1,0:T(8,128)(2,1)S(1)}, u32[]{:S(2)}, u32[]{:S(2)}) collective-permute-start(bf16[128,1152]{1,0:T(8,128)(2,1)S(1)} %pad_maximum_fusion.3), channel_id=1, source_target_pairs={{0,16},{2,18},{4,20},{6,22},{8,24},{10,26},{12,28},{14,30},{16,0},... | collective-permute-start | bytes 884744 | tf_op jit(solution)/shard_map/ppermute | solution.py:106
  123.8 10.0 %collective-permute-start.28 = (bf16[4,64,512]{2,1,0:T(8,128)(2,1)S(1)}, bf16[4,64,512]{2,1,0:T(8,128)(2,1)S(1)}, u32[]{:S(2)}, u32[]{:S(2)}) collective-permute-start(bf16[4,64,512]{2,1,0:T(8,128)(2,1)S(1)} %hidden.1.refs_0_), channel_id=1, source_target_pairs={{0,2},{2,0},{4,6},{6,4},{8,10},{10,8},{12,14},{14,12},{16,18},{18,... | collective-permute-start | bytes 786440 | tf_op jit(solution)/shard_map/ppermute | solution.py:106
  124.2 9.6 %collective-permute-start.29 = (bf16[4,64,512]{2,1,0:T(8,128)(2,1)S(1)}, bf16[4,64,512]{2,1,0:T(8,128)(2,1)S(1)}, u32[]{:S(2)}, u32[]{:S(2)}) collective-permute-start(bf16[4,64,512]{2,1,0:T(8,128)(2,1)S(1)} %hidden.1.refs_0_), channel_id=1, source_target_pairs={{0,4},{2,6},{4,0},{6,2},{8,12},{10,14},{12,8},{14,10},{16,20},{18,... | collective-permute-start | bytes 786440 | tf_op jit(solution)/shard_map/ppermute | solution.py:106
  133.9 7.4 %collective-permute-start.35 = (bf16[256,1152]{1,0:T(8,128)(2,1)S(1)}, bf16[256,1152]{1,0:T(8,128)(2,1)S(1)}, u32[]{:S(2)}, u32[]{:S(2)}) collective-permute-start(bf16[256,1152]{1,0:T(8,128)(2,1)S(1)} %constant_dynamic-update-slice_fusion.4.refs_5_), channel_id=1, source_target_pairs={{0,1},{1,0},{2,3},{3,2},{4,5},{5,4},{6,7},{7,6},{8,9},{9,8},{10,11... | collective-permute-start | bytes 1769480 | tf_op jit(solution)/shard_map/ppermute | solution.py:110
  (30 other events, 257.5 us)

commit v21 on v18

--- a/solution.py
+++ b/solution.py
@@ -450,7 +450,8 @@
     near_x, near_y = hop(near, to_x), hop(near, to_y)
     tok = [near, near_x, near_y, *across(near_x, near_y)]
     w_mine = heads_along_z(w_pieces)
-    w_theirs = [swap_cores(w) for w in w_mine]
+    neg_pair = pair_up(neg)
+    w_theirs = [swap_cores(w) for w in after(w_mine, neg_pair)]
     out_own = [out_pair, hop(after(out_pair, w_mine), flip(0, 0, 2))]
     t_send = swap_cores(after(t_mine, w_theirs))
 
@@ -487,8 +488,7 @@
     hops = [hop(gated[s], flip(0, 0, s)) for s in (1, 2)]
     out_own, out_pair_theirs, last = lax.optimization_barrier((out_own, out_pair_theirs, gated[3]))
     gated = jnp.stack([gated[0], *hops, hop(last, flip(0, 0, 3))])
-    neg_pair = pair_up(after(neg, gated))
-    neg_far = hop(neg_pair, flip(0, 0, 2))
+    neg_far = hop(after(neg_pair, gated), flip(0, 0, 2))
     out_other = [out_pair_theirs, swap_cores(after(out_own[1], gated))]
     gated = [gated, hop(gated, to_x), hop(gated, to_y)]
     gated += across(gated[1], gated[2])

time: 141 us -> 141 us (level)
    ppermute x28, waiting for transfers between devices: 76.3 us -> 74.1 us  [hop(): return lax.ppermute(value, 'ctx', perm)]
where the time goes in v21:
time: 141 us; the launch traced here: 140 us
  waiting for transfers between devices  77.5 us (55%)
  starting transfers between devices  37.9 us (27%)
  Pallas kernels  13.5 us (10%)
  local copies, waits for them, and re-layouts  8.23 us (6%)
  other arithmetic  1.93 us (1%)
    ppermute x28, waiting for transfers between devices, hop(): return lax.ppermute(value, 'ctx', perm)  74.1 us
    ppermute x28, starting transfers between devices, hop(): return lax.ppermute(value, 'ctx', perm)  35.3 us
    pallas_call x6, Pallas kernels, call(): pl.pallas_call(kernel, out_shape=[jax.ShapeDtypeStruct(shape, dtype) for...  13.5 us
    ppermute x9, waiting for transfers between devices, swap_cores(): return lax.ppermute(value, 'tp', SWAP)  3.43 us
    squeeze x6, local copies, waits for them, and re-layouts, pick_row(): return lax.dynamic_index_in_dim(value, at, 0, keepdims=False)  3.08 us
  transfers between devices with their start and end apart: 39, of which 21 were waited for; matrix products, arithmetic and copies ran while one was open for 5% of the time, Pallas kernels for 7%

profile of v21, /device:TPU:0, one launch (start us, length us, event | category | flops | bytes accessed | tf_op | source)
XLA Modules:
  0.0 140.2 jit_solution(14972742560360945683)
XLA Ops:
  3.9 3.1 %collective-permute-start.4 = (bf16[64,2176]{1,0:T(8,128)(2,1)S(1)}, bf16[64,2176]{1,0:T(8,128)(2,1)S(1)}, u32[]{:S(2)}, u32[]{:S(2)}) collective-permute-start(bf16[64,2176]{1,0:T(8,128)(2,1)S(1)} %mark.1), channel_id=1, source_target_pairs={{0,8},{2,10},{4,12},{6,14},{8,0},{10,2},{12,4},{14,6},{16,24},{18,... | collective-permute-start | bytes 835592 | tf_op jit(solution)/shard_map/ppermute | solution.py:106
  7.0 2.6 %collective-permute-start.5 = (bf16[64,2176]{1,0:T(8,128)(2,1)S(1)}, bf16[64,2176]{1,0:T(8,128)(2,1)S(1)}, u32[]{:S(2)}, u32[]{:S(2)}) collective-permute-start(bf16[64,2176]{1,0:T(8,128)(2,1)S(1)} %mark.1), channel_id=1, source_target_pairs={{0,16},{2,18},{4,20},{6,22},{8,24},{10,26},{12,28},{14,30},{16,0},... | collective-permute-start | bytes 835592 | tf_op jit(solution)/shard_map/ppermute | solution.py:106
  12.0 1.8 %collective-permute-start.1 = (bf16[2,128,512]{2,1,0:T(8,128)(2,1)S(1)}, bf16[2,128,512]{2,1,0:T(8,128)(2,1)}, u32[]{:S(2)}, u32[]{:S(2)}) collective-permute-start(bf16[2,128,512]{2,1,0:T(8,128)(2,1)S(1)} %get-tuple-element.39), channel_id=1, source_target_pairs={{0,4},{2,6},{4,0},{6,2},{8,12},{10,14},{12,8},{14,10},{16,20},{18,... | collective-permute-start | bytes 786440 | tf_op jit(solution)/shard_map/ppermute | solution.py:106
  17.2 2.5 %collective-permute-done.1 = bf16[2,128,512]{2,1,0:T(8,128)(2,1)} collective-permute-done((bf16[2,128,512]{2,1,0:T(8,128)(2,1)S(1)}, bf16[2,128,512]{2,1,0:T(8,128)(2,1)}, u32[]{:S(2)}, u32[]{:S(2)}) %collective-permute-start.1) | collective-permute-done | bytes 262176 | tf_op jit(solution)/shard_map/ppermute | solution.py:106
  26.0 2.2 %collective-permute-done.2 = bf16[2,128,512]{2,1,0:T(8,128)(2,1)S(1)} collective-permute-done((bf16[2,128,512]{2,1,0:T(8,128)(2,1)S(1)}, bf16[2,128,512]{2,1,0:T(8,128)(2,1)S(1)}, u32[]{:S(2)}, u32[]{:S(2)}) %collective-permute-start.2) | collective-permute-done | bytes 262176 | tf_op jit(solution)/shard_map/ppermute | solution.py:106
  28.2 6.0 %collective-permute-done.3 = bf16[1,1024,128]{2,1,0:T(8,128)(2,1)S(1)} collective-permute-done((bf16[1,1024,128]{2,1,0:T(8,128)(2,1)}, bf16[1,1024,128]{2,1,0:T(8,128)(2,1)S(1)}, u32[]{:S(2)}, u32[]{:S(2)}) %collective-permute-start.3) | collective-permute-done | bytes 262176 | tf_op jit(solution)/shard_map/ppermute | solution.py:106
  38.7 1.8 %collective-permute-start.13 = (bf16[64,1152]{1,0:T(8,128)(2,1)S(1)}, bf16[64,1152]{1,0:T(8,128)(2,1)S(1)}, u32[]{:S(2)}, u32[]{:S(2)}) collective-permute-start(bf16[64,1152]{1,0:T(8,128)(2,1)S(1)} %fusion.1), channel_id=1, source_target_pairs={{0,8},{2,10},{4,12},{6,14},{8,0},{10,2},{12,4},{14,6},{16,24},{18,... | collective-permute-start | bytes 442376 | tf_op jit(solution)/shard_map/ppermute | solution.py:106
  40.5 20.6 %collective-permute-done.8.refs_2_.refs_11_ = bf16[256,2176]{1,0:T(8,128)(2,1)S(1)} collective-permute-done((bf16[256,2176]{1,0:T(8,128)(2,1)S(1)}, bf16[256,2176]{1,0:T(8,128)(2,1)S(1)}, u32[]{:S(2)}, u32[]{:S(2)}) %collective-permute-start.8) | collective-permute-done | bytes 1114144 | tf_op jit(solution)/shard_map/ppermute | solution.py:106
  64.7 2.6 %collective-permute-start.20 = (bf16[2,1024,128]{2,1,0:T(8,128)(2,1)S(1)}, bf16[2,1024,128]{2,1,0:T(8,128)(2,1)S(1)}, u32[]{:S(2)}, u32[]{:S(2)}) collective-permute-start(bf16[2,1024,128]{2,1,0:T(8,128)(2,1)S(1)} %pad_maximum_fusion.2.refs_5_), channel_id=1, source_target_pairs={{0,16},{2,18},{4,20},{6,22},{8,24},{10,26},{12,28},{14,30},{16,0},... | collective-permute-start | bytes 1572872 | tf_op jit(solution)/shard_map/ppermute | solution.py:106
  67.4 7.4 %collective-permute-done.10.refs_4_ = bf16[128,2176]{1,0:T(8,128)(2,1)S(1)} collective-permute-done((bf16[128,2176]{1,0:T(8,128)(2,1)S(1)}, bf16[128,2176]{1,0:T(8,128)(2,1)S(1)}, u32[]{:S(2)}, u32[]{:S(2)}) %collective-permute-start.10) | collective-permute-done | bytes 557088 | tf_op jit(solution)/shard_map/ppermute | solution.py:106
  76.2 3.8 %project.1 = (bf16[1024,256]{1,0:T(8,128)(2,1)S(1)}, bf16[1024,128]{1,0:T(8,128)(2,1)S(1)}, bf16[1024,128]{1,0:T(8,128)(2,1)S(1)}, bf16[1024,128]{1,0:T(8,128)(2,1)S(1)}) custom-call(s32[4]{0:T(128)S(1)} %pad_add_fusion.where, bf16[256,2176]{1,0:T(8,128)(2,1)S(1)} %constant_dynamic-update-slice_fusion.refs_0_.refs_9_, ...), custom_call_target="tpu_custom_call" | custom-call | bytes 6553616 | tf_op jit(solution)/shard_map/project/pallas_call | solution.py:374
  80.7 1.7 %collective-permute-done.16.refs_3_ = bf16[1024,128]{1,0:T(8,128)(2,1)S(1)} collective-permute-done((bf16[1024,128]{1,0:T(8,128)(2,1)S(1)}, bf16[1024,128]{1,0:T(8,128)(2,1)S(1)}, u32[]{:S(2)}, u32[]{:S(2)}) %collective-permute-start.16) | collective-permute-done | bytes 262176 | tf_op jit(solution)/shard_map/ppermute | solution.py:110
  82.8 3.4 %attend.1 = bf16[4,4,64,128]{3,2,1,0:T(8,128)(2,1)S(1)} custom-call(bf16[1024,256]{1,0:T(8,128)(2,1)S(1)} %get-tuple-element.51.refs_0_, bf16[1024,128]{1,0:T(8,128)(2,1)S(1)} %get-tuple-element.52.refs_1_, bf16[1024,128]{1,0:T(8,128)(2,1)S(1)} %get-tuple-element.53.refs_2_, bf16[1024,128]{1,0:T(8,128)(2,1)S(1)} %collective-permute-done.16.refs_3_, ...), custom_call_target="tpu_custom_call" | custom-call | bytes 1835008 | tf_op jit(solution)/shard_map/attend/pallas_call | solution.py:374
  86.3 1.6 %collective-permute-start.19 = (bf16[4,64,128]{2,1,0:T(8,128)(2,1)S(1)}, bf16[4,64,128]{2,1,0:T(8,128)(2,1)S(1)}, u32[]{:S(2)}, u32[]{:S(2)}) collective-permute-start(bf16[4,64,128]{2,1,0:T(8,128)(2,1)S(1)} %get-tuple-element.83), channel_id=1, source_target_pairs={{0,16},{2,18},{4,20},{6,22},{8,24},{10,26},{12,28},{14,30},{16,0},... | collective-permute-start | bytes 196616 | tf_op jit(solution)/shard_map/ppermute | solution.py:106
  87.9 5.0 %collective-permute-done.20.refs_6_ = bf16[2,1024,128]{2,1,0:T(8,128)(2,1)S(1)} collective-permute-done((bf16[2,1024,128]{2,1,0:T(8,128)(2,1)S(1)}, bf16[2,1024,128]{2,1,0:T(8,128)(2,1)S(1)}, u32[]{:S(2)}, u32[]{:S(2)}) %collective-permute-start.20) | collective-permute-done | bytes 524320 | tf_op jit(solution)/shard_map/ppermute | solution.py:106
  92.9 1.9 %collective-permute-start.22 = (bf16[4,64,128]{2,1,0:T(8,128)(2,1)S(1)}, bf16[4,64,128]{2,1,0:T(8,128)(2,1)S(1)}, u32[]{:S(2)}, u32[]{:S(2)}) collective-permute-start(bf16[4,64,128]{2,1,0:T(8,128)(2,1)S(1)} %get-tuple-element.58), channel_id=1, source_target_pairs={{0,24},{2,26},{4,28},{6,30},{8,16},{10,18},{12,20},{14,22},{16,8},... | collective-permute-start | bytes 196616 | tf_op jit(solution)/shard_map/ppermute | solution.py:106
  94.8 4.2 %collective-permute-done.22 = bf16[4,64,128]{2,1,0:T(8,128)(2,1)S(1)} collective-permute-done((bf16[4,64,128]{2,1,0:T(8,128)(2,1)S(1)}, bf16[4,64,128]{2,1,0:T(8,128)(2,1)S(1)}, u32[]{:S(2)}, u32[]{:S(2)}) %collective-permute-start.22) | collective-permute-done | bytes 65568 | tf_op jit(solution)/shard_map/ppermute | solution.py:106
  99.3 8.6 %collective-permute-done.23.refs_1_ = bf16[4,4,64,128]{3,2,1,0:T(8,128)(2,1)S(1)} collective-permute-done((bf16[4,4,64,128]{3,2,1,0:T(8,128)(2,1)S(1)}, bf16[4,4,64,128]{3,2,1,0:T(8,128)(2,1)S(1)}, u32[]{:S(2)}, u32[]{:S(2)}) %collective-permute-start.23) | collective-permute-done | bytes 262176 | tf_op jit(solution)/shard_map/ppermute | solution.py:106
  108.0 1.7 %collective-permute-start.26 = (bf16[2,4,64,128]{3,2,1,0:T(8,128)(2,1)S(1)}, bf16[2,4,64,128]{3,2,1,0:T(8,128)(2,1)S(1)}, u32[]{:S(2)}, u32[]{:S(2)}) collective-permute-start(bf16[2,4,64,128]{3,2,1,0:T(8,128)(2,1)S(1)} %slice.63), channel_id=1, source_target_pairs={{0,2},{2,0},{4,6},{6,4},{8,10},{10,8},{12,14},{14,12},{16,18},{18,... | collective-permute-start | bytes 393224 | tf_op jit(solution)/shard_map/ppermute | solution.py:106
  109.7 3.3 %collective-permute-done.25.refs_3_ = bf16[2,4,64,128]{3,2,1,0:T(8,128)(2,1)S(1)} collective-permute-done((bf16[2,4,64,128]{3,2,1,0:T(8,128)(2,1)S(1)}, bf16[2,4,64,128]{3,2,1,0:T(8,128)(2,1)S(1)}, u32[]{:S(2)}, u32[]{:S(2)}) %collective-permute-start.25) | collective-permute-done | bytes 131104 | tf_op jit(solution)/shard_map/ppermute | solution.py:106
  113.1 2.7 %hidden.1.refs_0_ = bf16[4,64,512]{2,1,0:T(8,128)(2,1)S(1)} custom-call(s32[4]{0:T(128)S(1)} %pad_add_fusion.where, bf16[4,4,64,128]{3,2,1,0:T(8,128)(2,1)S(1)} %pad_maximum_fusion.3.refs_0_, bf16[4,4,64,128]{3,2,1,0:T(8,128)(2,1)S(1)} %collective-permute-done.23.refs_1_, bf16[4,4,64,128]{3,2,1,0:T(8,128)(2,1)S(1)} %collective-permute-done.24.refs_2_, ...), custom_call_target="tpu_custom_call" | custom-call | flops 536870912 | bytes 7045136 | tf_op jit(solution)/shard_map/hidden/pallas_call | solution.py:374
  119.4 4.7 %collective-permute-done.32 = bf16[128,1152]{1,0:T(8,128)(2,1)S(1)} collective-permute-done((bf16[128,1152]{1,0:T(8,128)(2,1)S(1)}, bf16[128,1152]{1,0:T(8,128)(2,1)S(1)}, u32[]{:S(2)}, u32[]{:S(2)}) %collective-permute-start.32) | collective-permute-done | bytes 294944 | tf_op jit(solution)/shard_map/ppermute | solution.py:106
  125.2 1.6 %collective-permute-start.31 = (bf16[2,64,512]{2,1,0:T(8,128)(2,1)S(1)}, bf16[2,64,512]{2,1,0:T(8,128)(2,1)S(1)}, u32[]{:S(2)}, u32[]{:S(2)}) collective-permute-start(bf16[2,64,512]{2,1,0:T(8,128)(2,1)S(1)} %slice.65), channel_id=1, source_target_pairs={{0,2},{2,0},{4,6},{6,4},{8,10},{10,8},{12,14},{14,12},{16,18},{18,... | collective-permute-start | bytes 393224 | tf_op jit(solution)/shard_map/ppermute | solution.py:106
  126.8 3.4 %collective-permute-done.30.refs_3_ = bf16[2,64,512]{2,1,0:T(8,128)(2,1)S(1)} collective-permute-done((bf16[2,64,512]{2,1,0:T(8,128)(2,1)S(1)}, bf16[2,64,512]{2,1,0:T(8,128)(2,1)S(1)}, u32[]{:S(2)}, u32[]{:S(2)}) %collective-permute-start.30) | collective-permute-done | bytes 131104 | tf_op jit(solution)/shard_map/ppermute | solution.py:106
  (105 shorter events, 40.9 us)
Async XLA Ops:
  3.9 30.5 %collective-permute-start.4 = (bf16[64,2176]{1,0:T(8,128)(2,1)S(1)}, bf16[64,2176]{1,0:T(8,128)(2,1)S(1)}, u32[]{:S(2)}, u32[]{:S(2)}) collective-permute-start(bf16[64,2176]{1,0:T(8,128)(2,1)S(1)} %mark.1), channel_id=1, source_target_pairs={{0,8},{2,10},{4,12},{6,14},{8,0},{10,2},{12,4},{14,6},{16,24},{18,... | collective-permute-start | bytes 835592 | tf_op jit(solution)/shard_map/ppermute | solution.py:106
  7.0 27.4 %collective-permute-start.5 = (bf16[64,2176]{1,0:T(8,128)(2,1)S(1)}, bf16[64,2176]{1,0:T(8,128)(2,1)S(1)}, u32[]{:S(2)}, u32[]{:S(2)}) collective-permute-start(bf16[64,2176]{1,0:T(8,128)(2,1)S(1)} %mark.1), channel_id=1, source_target_pairs={{0,16},{2,18},{4,20},{6,22},{8,24},{10,26},{12,28},{14,30},{16,0},... | collective-permute-start | bytes 835592 | tf_op jit(solution)/shard_map/ppermute | solution.py:106
  9.6 24.8 %collective-permute-start.6 = (bf16[64,2176]{1,0:T(8,128)(2,1)S(1)}, bf16[64,2176]{1,0:T(8,128)(2,1)S(1)}, u32[]{:S(2)}, u32[]{:S(2)}) collective-permute-start(bf16[64,2176]{1,0:T(8,128)(2,1)S(1)} %mark.1), channel_id=1, source_target_pairs={{0,24},{2,26},{4,28},{6,30},{8,16},{10,18},{12,20},{14,22},{16,8},... | collective-permute-start | bytes 835592 | tf_op jit(solution)/shard_map/ppermute | solution.py:106
  12.0 7.7 %collective-permute-start.1 = (bf16[2,128,512]{2,1,0:T(8,128)(2,1)S(1)}, bf16[2,128,512]{2,1,0:T(8,128)(2,1)}, u32[]{:S(2)}, u32[]{:S(2)}) collective-permute-start(bf16[2,128,512]{2,1,0:T(8,128)(2,1)S(1)} %get-tuple-element.39), channel_id=1, source_target_pairs={{0,4},{2,6},{4,0},{6,2},{8,12},{10,14},{12,8},{14,10},{16,20},{18,... | collective-permute-start | bytes 786440 | tf_op jit(solution)/shard_map/ppermute | solution.py:106
  13.8 7.1 %collective-permute-start = (bf16[2,128,512]{2,1,0:T(8,128)(2,1)S(1)}, bf16[2,128,512]{2,1,0:T(8,128)(2,1)}, u32[]{:S(2)}, u32[]{:S(2)}) collective-permute-start(bf16[2,128,512]{2,1,0:T(8,128)(2,1)S(1)} %get-tuple-element.38), channel_id=1, source_target_pairs={{0,2},{2,0},{4,6},{6,4},{8,10},{10,8},{12,14},{14,12},{16,18},{18,... | collective-permute-start | bytes 786440 | tf_op jit(solution)/shard_map/ppermute | solution.py:106
  20.9 7.3 %collective-permute-start.2 = (bf16[2,128,512]{2,1,0:T(8,128)(2,1)S(1)}, bf16[2,128,512]{2,1,0:T(8,128)(2,1)S(1)}, u32[]{:S(2)}, u32[]{:S(2)}) collective-permute-start(bf16[2,128,512]{2,1,0:T(8,128)(2,1)S(1)} %get-tuple-element.40), channel_id=1, source_target_pairs={{0,6},{2,4},{4,2},{6,0},{8,14},{10,12},{12,10},{14,8},{16,22},{18,... | collective-permute-start | bytes 786440 | tf_op jit(solution)/shard_map/ppermute | solution.py:106
  23.3 10.9 %collective-permute-start.3 = (bf16[1,1024,128]{2,1,0:T(8,128)(2,1)}, bf16[1,1024,128]{2,1,0:T(8,128)(2,1)S(1)}, u32[]{:S(2)}, u32[]{:S(2)}) collective-permute-start(bf16[1,1024,128]{2,1,0:T(8,128)(2,1)} %bitcast.68), channel_id=1, source_target_pairs={{0,8},{2,10},{4,12},{6,14},{8,0},{10,2},{12,4},{14,6},{16,24},{18,... | collective-permute-start | bytes 786440 | tf_op jit(solution)/shard_map/ppermute | solution.py:106
  34.5 26.5 %collective-permute-start.8 = (bf16[256,2176]{1,0:T(8,128)(2,1)S(1)}, bf16[256,2176]{1,0:T(8,128)(2,1)S(1)}, u32[]{:S(2)}, u32[]{:S(2)}) collective-permute-start(bf16[256,2176]{1,0:T(8,128)(2,1)S(1)} %constant_dynamic-update-slice_fusion.refs_0_.refs_9_), channel_id=1, source_target_pairs={{0,4},{2,6},{4,0},{6,2},{8,12},{10,14},{12,8},{14,10},{16,20},{18,... | collective-permute-start | bytes 3342344 | tf_op jit(solution)/shard_map/ppermute | solution.py:106
  36.1 26.6 %collective-permute-start.7 = (bf16[256,2176]{1,0:T(8,128)(2,1)S(1)}, bf16[256,2176]{1,0:T(8,128)(2,1)S(1)}, u32[]{:S(2)}, u32[]{:S(2)}) collective-permute-start(bf16[256,2176]{1,0:T(8,128)(2,1)S(1)} %constant_dynamic-update-slice_fusion.refs_0_.refs_9_), channel_id=1, source_target_pairs={{0,2},{2,0},{4,6},{6,4},{8,10},{10,8},{12,14},{14,12},{16,18},{18,... | collective-permute-start | bytes 3342344 | tf_op jit(solution)/shard_map/ppermute | solution.py:106
  37.5 26.6 %collective-permute-start.11 = (bf16[512,512]{1,0:T(8,128)(2,1)S(1)}, bf16[512,512]{1,0:T(8,128)(2,1)S(1)}, u32[]{:S(2)}, u32[]{:S(2)}) collective-permute-start(bf16[512,512]{1,0:T(8,128)(2,1)S(1)} %get-tuple-element.46), channel_id=1, source_target_pairs={{0,0},{1,16},{2,2},{3,18},{4,4},{5,20},{6,6},{7,22},{8,8},{9,24},{... | collective-permute-start | bytes 1572872 | tf_op jit(solution)/shard_map/ppermute | solution.py:152
  38.4 25.8 %collective-permute-start.12 = (bf16[512,512]{1,0:T(8,128)(2,1)S(1)}, bf16[512,512]{1,0:T(8,128)(2,1)S(1)}, u32[]{:S(2)}, u32[]{:S(2)}) collective-permute-start(bf16[512,512]{1,0:T(8,128)(2,1)S(1)} %get-tuple-element.47), channel_id=1, source_target_pairs={{0,8},{1,24},{2,10},{3,26},{4,12},{5,28},{6,14},{7,30},{8,0},{9,16... | collective-permute-start | bytes 1572872 | tf_op jit(solution)/shard_map/ppermute | solution.py:152
  38.7 25.4 %collective-permute-start.13 = (bf16[64,1152]{1,0:T(8,128)(2,1)S(1)}, bf16[64,1152]{1,0:T(8,128)(2,1)S(1)}, u32[]{:S(2)}, u32[]{:S(2)}) collective-permute-start(bf16[64,1152]{1,0:T(8,128)(2,1)S(1)} %fusion.1), channel_id=1, source_target_pairs={{0,8},{2,10},{4,12},{6,14},{8,0},{10,2},{12,4},{14,6},{16,24},{18,... | collective-permute-start | bytes 442376 | tf_op jit(solution)/shard_map/ppermute | solution.py:106
  61.1 13.7 %collective-permute-start.10 = (bf16[128,2176]{1,0:T(8,128)(2,1)S(1)}, bf16[128,2176]{1,0:T(8,128)(2,1)S(1)}, u32[]{:S(2)}, u32[]{:S(2)}) collective-permute-start(bf16[128,2176]{1,0:T(8,128)(2,1)S(1)} %slice.57), channel_id=1, source_target_pairs={{0,2},{2,0},{4,6},{6,4},{8,10},{10,8},{12,14},{14,12},{16,18},{18,... | collective-permute-start | bytes 1671176 | tf_op jit(solution)/shard_map/ppermute | solution.py:106
  62.7 13.5 %collective-permute-start.9 = (bf16[128,2176]{1,0:T(8,128)(2,1)S(1)}, bf16[128,2176]{1,0:T(8,128)(2,1)S(1)}, u32[]{:S(2)}, u32[]{:S(2)}) collective-permute-start(bf16[128,2176]{1,0:T(8,128)(2,1)S(1)} %slice.56), channel_id=1, source_target_pairs={{0,4},{2,6},{4,0},{6,2},{8,12},{10,14},{12,8},{14,10},{16,20},{18,... | collective-permute-start | bytes 1671176 | tf_op jit(solution)/shard_map/ppermute | solution.py:106
  64.7 28.2 %collective-permute-start.20 = (bf16[2,1024,128]{2,1,0:T(8,128)(2,1)S(1)}, bf16[2,1024,128]{2,1,0:T(8,128)(2,1)S(1)}, u32[]{:S(2)}, u32[]{:S(2)}) collective-permute-start(bf16[2,1024,128]{2,1,0:T(8,128)(2,1)S(1)} %pad_maximum_fusion.2.refs_5_), channel_id=1, source_target_pairs={{0,16},{2,18},{4,20},{6,22},{8,24},{10,26},{12,28},{14,30},{16,0},... | collective-permute-start | bytes 1572872 | tf_op jit(solution)/shard_map/ppermute | solution.py:106
  80.0 12.9 %collective-permute-start.21 = (bf16[2,1024,128]{2,1,0:T(8,128)(2,1)S(1)}, bf16[2,1024,128]{2,1,0:T(8,128)(2,1)S(1)}, u32[]{:S(2)}, u32[]{:S(2)}) collective-permute-start(bf16[2,1024,128]{2,1,0:T(8,128)(2,1)S(1)} %pad_maximum_fusion.2.refs_5_), channel_id=1, source_target_pairs={{0,1},{1,0},{2,3},{3,2},{4,5},{5,4},{6,7},{7,6},{8,9},{9,8},{10,11... | collective-permute-start | bytes 1572872 | tf_op jit(solution)/shard_map/ppermute | solution.py:110
  86.2 8.6 %collective-permute-start.18 = (bf16[4,64,128]{2,1,0:T(8,128)(2,1)S(1)}, bf16[4,64,128]{2,1,0:T(8,128)(2,1)S(1)}, u32[]{:S(2)}, u32[]{:S(2)}) collective-permute-start(bf16[4,64,128]{2,1,0:T(8,128)(2,1)S(1)} %get-tuple-element.84), channel_id=1, source_target_pairs={{0,8},{2,10},{4,12},{6,14},{8,0},{10,2},{12,4},{14,6},{16,24},{18,... | collective-permute-start | bytes 196616 | tf_op jit(solution)/shard_map/ppermute | solution.py:106
  86.3 8.5 %collective-permute-start.19 = (bf16[4,64,128]{2,1,0:T(8,128)(2,1)S(1)}, bf16[4,64,128]{2,1,0:T(8,128)(2,1)S(1)}, u32[]{:S(2)}, u32[]{:S(2)}) collective-permute-start(bf16[4,64,128]{2,1,0:T(8,128)(2,1)S(1)} %get-tuple-element.83), channel_id=1, source_target_pairs={{0,16},{2,18},{4,20},{6,22},{8,24},{10,26},{12,28},{14,30},{16,0},... | collective-permute-start | bytes 196616 | tf_op jit(solution)/shard_map/ppermute | solution.py:106
  99.0 14.1 %collective-permute-start.27 = (bf16[2,1024,128]{2,1,0:T(8,128)(2,1)S(1)}, bf16[2,1024,128]{2,1,0:T(8,128)(2,1)S(1)}, u32[]{:S(2)}, u32[]{:S(2)}) collective-permute-start(bf16[2,1024,128]{2,1,0:T(8,128)(2,1)S(1)} %collective-permute-done.20.refs_6_), channel_id=1, source_target_pairs={{0,1},{1,0},{2,3},{3,2},{4,5},{5,4},{6,7},{7,6},{8,9},{9,8},{10,11... | collective-permute-start | bytes 1572872 | tf_op jit(solution)/shard_map/ppermute | solution.py:110
  99.1 8.7 %collective-permute-start.23 = (bf16[4,4,64,128]{3,2,1,0:T(8,128)(2,1)S(1)}, bf16[4,4,64,128]{3,2,1,0:T(8,128)(2,1)S(1)}, u32[]{:S(2)}, u32[]{:S(2)}) collective-permute-start(bf16[4,4,64,128]{3,2,1,0:T(8,128)(2,1)S(1)} %pad_maximum_fusion.3.refs_0_), channel_id=1, source_target_pairs={{0,2},{2,0},{4,6},{6,4},{8,10},{10,8},{12,14},{14,12},{16,18},{18,... | collective-permute-start | bytes 786440 | tf_op jit(solution)/shard_map/ppermute | solution.py:106
  99.3 8.7 %collective-permute-start.24 = (bf16[4,4,64,128]{3,2,1,0:T(8,128)(2,1)S(1)}, bf16[4,4,64,128]{3,2,1,0:T(8,128)(2,1)S(1)}, u32[]{:S(2)}, u32[]{:S(2)}) collective-permute-start(bf16[4,4,64,128]{3,2,1,0:T(8,128)(2,1)S(1)} %pad_maximum_fusion.3.refs_0_), channel_id=1, source_target_pairs={{0,4},{2,6},{4,0},{6,2},{8,12},{10,14},{12,8},{14,10},{16,20},{18,... | collective-permute-start | bytes 786440 | tf_op jit(solution)/shard_map/ppermute | solution.py:106
  109.7 14.4 %collective-permute-start.32 = (bf16[128,1152]{1,0:T(8,128)(2,1)S(1)}, bf16[128,1152]{1,0:T(8,128)(2,1)S(1)}, u32[]{:S(2)}, u32[]{:S(2)}) collective-permute-start(bf16[128,1152]{1,0:T(8,128)(2,1)S(1)} %get-tuple-element.63), channel_id=1, source_target_pairs={{0,16},{2,18},{4,20},{6,22},{8,24},{10,26},{12,28},{14,30},{16,0},... | collective-permute-start | bytes 884744 | tf_op jit(solution)/shard_map/ppermute | solution.py:106
  115.8 8.3 %collective-permute-start.28 = (bf16[4,64,512]{2,1,0:T(8,128)(2,1)S(1)}, bf16[4,64,512]{2,1,0:T(8,128)(2,1)S(1)}, u32[]{:S(2)}, u32[]{:S(2)}) collective-permute-start(bf16[4,64,512]{2,1,0:T(8,128)(2,1)S(1)} %hidden.1.refs_0_), channel_id=1, source_target_pairs={{0,2},{2,0},{4,6},{6,4},{8,10},{10,8},{12,14},{14,12},{16,18},{18,... | collective-permute-start | bytes 786440 | tf_op jit(solution)/shard_map/ppermute | solution.py:106
  124.1 6.7 %collective-permute-start.34 = (bf16[256,1152]{1,0:T(8,128)(2,1)S(1)}, bf16[256,1152]{1,0:T(8,128)(2,1)S(1)}, u32[]{:S(2)}, u32[]{:S(2)}) collective-permute-start(bf16[256,1152]{1,0:T(8,128)(2,1)S(1)} %constant_dynamic-update-slice_fusion.6.refs_5_), channel_id=1, source_target_pairs={{0,1},{1,0},{2,3},{3,2},{4,5},{5,4},{6,7},{7,6},{8,9},{9,8},{10,11... | collective-permute-start | bytes 1769480 | tf_op jit(solution)/shard_map/ppermute | solution.py:110
  (20 other events, 89.2 us)
